TPU v7x, 32 devices: a whole 2x2x4 slice. The times are simulated.
32 devices in a mesh: grp: 2 (over y), sec: 16 (over z, x, core), op: 1.
Axes of the slice: x: 2, y: 2, z: 4, core: 2. Of those that a mesh axis runs over, the one named last changes fastest.
Arguments:
- psi: bfloat16 [256, 8, 64, 128], P(('grp', 'sec')), parts along dimension 0, may hold values from -6 to 6
- left_ops: bfloat16 [256, 64, 64], P(('grp', 'sec'), None, 'op'), parts along dimension 0, may hold values from -0.75 to 0.75
- right_ops: bfloat16 [512, 64, 64], P(('grp', 'sec'), None, 'op'), parts along dimension 0, may hold values from -0.75 to 0.75
- dims_left: int32 [256], P(('grp', 'sec')), parts along dimension 0, may hold values from 32 to 64
- dims_right: int32 [512], P(('grp', 'sec')), parts along dimension 0, may hold values from 32 to 64
- right_owner: int32 [256, 8], P(('grp', 'sec')), parts along dimension 0, may hold values from 0 to 15, all different within a row; in each aligned block of 8 rows (0 to 7, 8 to 15, ...) at most 8 rows name the same one
- right_slot: int32 [256, 8], P(('grp', 'sec')), parts along dimension 0, may hold values from 0 to 15
- term_active: int32 [256, 8, 1], P(('grp', 'sec'), None, 'op'), parts along dimension 0, may hold values 0 or 1
Outputs:
- sigma: bfloat16 [256, 8, 64, 128], P(('grp', 'sec'), None, None, 'op'), parts along dimension 0
There are 2 independent parts, one for each index of `grp`. A program takes and returns all parts, laid end to end along the dimension named above; each array names one. Nothing has to cross between parts.
Inputs may be any that keep to these rules, and one draw needn't show every extreme that they name: `right_owner`: each row names 8 different sec indices; within the rows of one device (aligned blocks of 8 rows) no index is named more than 8 times, a bound that some block reaches.
All inputs are finite; a program needn't handle non-finite values. No bound on the sum of `term_active` on one device may be relied on, other than what follows from the above.
Results may differ from a plain program's by a relative error of at most 0.0056.
Values may be sent and summed in bfloat16 or wider, within the bound.
No kernel may reach another device: no remote copies, remote signals or barrier semaphores. Data moves between devices by JAX's collectives and lax.ppermute only.
A program may use at most 64 MiB of HBM per device.

v0:
```python
import jax
import jax.numpy as jnp
from jax import lax
from jax.sharding import PartitionSpec as P


def contract_right(half_tiles, slot_code, right_ops, dims_right):
    sectors, capacity, tile_dim, width = half_tiles.shape
    term_count = right_ops.shape[2] // tile_dim
    vec_count = width // (term_count * tile_dim)
    right_index = jnp.maximum(slot_code.astype(jnp.int32) - 1, 0)
    right_sel = jnp.take(right_ops, right_index, axis=0)
    right_dims = jnp.take(dims_right, right_index)
    lanes = lax.iota(jnp.int32, tile_dim)
    col_keep = (lanes[None, None, :] < right_dims[:, :, None]).astype(jnp.bfloat16)
    right_sel = (
        right_sel.reshape(sectors, capacity, tile_dim, term_count, tile_dim)
        * col_keep[:, :, None, None, :]
    )
    half_split = half_tiles.reshape(sectors, capacity, tile_dim, term_count, vec_count, tile_dim)
    partial_sums = jnp.einsum(
        "ncitvj,ncstj->ncivs", half_split, right_sel, preferred_element_type=jnp.float32
    )
    partial_sums = partial_sums * col_keep.astype(jnp.float32)[:, :, None, None, :]
    partial_sums = partial_sums.astype(jnp.bfloat16).reshape(
        sectors, capacity, tile_dim, vec_count * tile_dim
    )
    return lax.all_to_all(partial_sums, "sec", split_axis=0, concat_axis=0, tiled=True)


def per_device(
    psi, left_ops, right_ops, dims_left, dims_right, right_owner, right_slot, term_active
):
    sectors = lax.axis_size("sec")
    left_count, block_count, tile_dim, vec_width = psi.shape
    term_count = left_ops.shape[2] // tile_dim
    item_count = left_count * block_count
    capacity = max(2, min(left_count, (2 * item_count + sectors - 1) // sectors))
    total_slots = sectors * capacity
    target = right_owner.reshape(item_count)
    position = lax.iota(jnp.int32, item_count)
    alike = target[:, None] == target[None, :]
    order_in = jnp.sum((alike & (position[None, :] < position[:, None])).astype(jnp.int32), axis=1)
    slot_item = target * capacity + order_in
    match = slot_item[None, :] == lax.iota(jnp.int32, total_slots)[:, None]
    source = jnp.sum(jnp.where(match, position[None, :] + 1, 0), axis=1) - 1
    filled = source >= 0
    source_safe = jnp.maximum(source, 0)

    def place_slots(values):
        taken = jnp.take(values, source_safe, axis=0)
        keep = filled.reshape((total_slots,) + (1,) * (values.ndim - 1))
        taken = jnp.where(keep, taken, jnp.zeros_like(taken))
        return taken.reshape((sectors, capacity) + values.shape[1:])

    lanes = lax.iota(jnp.int32, tile_dim)
    row_keep = (lanes[None, :] < dims_left[:, None]).astype(jnp.bfloat16)
    psi_kept = psi * row_keep[:, None, :, None]
    slot_code = place_slots((right_slot.reshape(item_count) + 1).astype(jnp.bfloat16))
    left_split = left_ops.reshape(left_count, tile_dim, term_count, tile_dim)
    half = jnp.einsum("aitl,ablw->abitw", left_split, psi_kept, preferred_element_type=jnp.float32)
    half = half * term_active.astype(jnp.float32)[:, :, None, :, None]
    half = half.astype(jnp.bfloat16).reshape(item_count, tile_dim, term_count * vec_width)
    half_slots = place_slots(half)
    half_part = lax.all_to_all(half_slots, "sec", split_axis=0, concat_axis=0, tiled=True)
    code_part = lax.all_to_all(slot_code, "sec", split_axis=0, concat_axis=0, tiled=True)
    returned = contract_right(half_part, code_part, right_ops, dims_right)
    flat = returned.reshape((total_slots,) + returned.shape[2:])
    mine = jnp.take(flat, slot_item, axis=0)
    summed = lax.psum_scatter(
        mine.astype(jnp.float32).astype(jnp.bfloat16), "op", scatter_dimension=2, tiled=True
    ).astype(jnp.float32)
    row_items = jnp.broadcast_to(row_keep[:, None, :], (left_count, block_count, tile_dim)).reshape(
        item_count, tile_dim
    )
    summed = summed * row_items.astype(jnp.float32)[:, :, None]
    return summed.astype(jnp.bfloat16).reshape(left_count, block_count, tile_dim, summed.shape[2])


def solution(mesh):
    placed = (
        P(("grp", "sec"), None, None, None),
        P(("grp", "sec"), None, "op"),
        P(("grp", "sec"), None, "op"),
        P(("grp", "sec")),
        P(("grp", "sec")),
        P(("grp", "sec"), None),
        P(("grp", "sec"), None),
        P(("grp", "sec"), None, "op"),
    )
    return jax.shard_map(
        per_device,
        mesh=mesh,
        in_specs=placed,
        out_specs=P(("grp", "sec"), None, None, "op"),
        check_vma=False,
    )
```

profile of v0, /device:TPU:15, one launch (start us, length us, event | category | flops | bytes accessed | tf_op | source)
XLA Modules:
  0.0 150.4 jit_solution(10164136876949800255)
XLA Ops:
  0.0 0.0 copy-start
  0.0 0.7 add_convert_fusion
  0.7 0.1 convert_element_type.90
  0.8 0.8 reshape.265
  1.6 0.2 convert_reduce_fusion
  1.8 0.1 select_reduce_fusion
  1.9 1.2 gather_fusion.1
  3.2 0.7 reshape.320
  3.9 6.6 %all-to-all-start.1 = ((bf16[16,1,8]{2,1,0:T(2,128)(2,1)}), bf16[16,1,8]{2,1,0:T(2,128)(2,1)S(1)}, u32[]{:S(2)}, u32[]{:S(2)}) async-start(bf16[16,1,8]{2,1,0:T(2,128)(2,1)} %reshape.320), calls=%async_computation.1 | async-start | bytes 16384 | tf_op jit(solution)/shard_map/all_to_all | solution.py:66
  10.4 0.7 fusion.17
  11.2 0.7 convert_bitcast_fusion
  11.9 1.8 %fusion.5 = bf16[8,8,128,64,1]{2,3,1,0,4:T(8,128)(2,1)S(1)} fusion(f32[8,8]{1,0:T(8,128)S(1)} %convert_bitcast_fusion, bf16[8,8,64,128]{3,2,1,0:T(8,128)(2,1)} %param.8, bf16[8,64]{1,0:T(8,128)(2,1)S(1)} %get-tuple-element.11, bf16[8,64,64]{2,1,0:T(8,128)(2,1)} %param.9), kind=kOutput, calls=%fused_computation.10 | convolution fusion | flops 70254592 | bytes 2163968 | tf_op jit(solution)/shard_map/aitl,ablw->abitw/dot_general | solution.py:61
  13.7 1.0 gather_fusion
  14.6 0.1 le.66
  14.7 0.1 ge.58
  14.8 1.6 %select_select_fusion = bf16[16,8,64,128]{3,2,1,0:T(8,128)(2,1)} fusion(bf16[16,8,64,128]{3,2,1,0:T(8,128)(2,1)S(1)} %bitcast.38, pred[16,8]{1,0:T(8,128)(4,1)S(1)} %le.66, pred[16,8]{1,0:T(8,128)(4,1)S(1)} %ge.58), kind=kLoop, calls=%fused_computation.14 | loop fusion | flops 2097152 | bytes 4194560 | tf_op jit(solution)/shard_map/jit(_where)/select_n | solution.py:53
  16.4 0.0 copy-start.1
  16.4 0.0 all-to-all-done.1
  16.4 6.2 %all-to-all-start = ((bf16[16,8,64,128]{3,2,1,0:T(8,128)(2,1)}), bf16[16,8,64,128]{3,2,1,0:T(8,128)(2,1)S(1)}, u32[]{:S(2)}, u32[]{:S(2)}) async-start(bf16[16,8,64,128]{3,2,1,0:T(8,128)(2,1)} %select_select_fusion), calls=%async_computation | async-start | bytes 4194304 | tf_op jit(solution)/shard_map/all_to_all | solution.py:65
  22.6 0.1 copy.32
  22.7 0.1 copy.34
  22.7 0.1 reshape.290
  22.8 0.0 copy-done.1
  22.8 1.2 gather_fusion.3
  24.1 0.1 reshape.297
  24.2 0.1 copy.35
  24.2 0.1 copy.36
  24.3 0.0 copy-done
  24.3 2.1 %gather_fusion.2 = bf16[128,64,64]{2,1,0:T(8,128)(2,1)} fusion(bf16[16,64,64]{2,1,0:T(8,128)(2,1)S(1)} %copy-done, s32[1024]{0:T(1024)S(1)} %pad_clamp_fusion.1), kind=kCustom, calls=%fused_computation.2 | custom fusion | bytes 2097664 | tf_op jit(solution)/shard_map/jit(_take)/gather | solution.py:12
  26.5 0.1 copy.33
  26.6 0.1 fusion.14
  26.6 43.3 %all-to-all-done = bf16[16,8,64,128]{3,2,1,0:T(8,128)(2,1)S(1)} async-done(((bf16[16,8,64,128]{3,2,1,0:T(8,128)(2,1)}), bf16[16,8,64,128]{3,2,1,0:T(8,128)(2,1)S(1)}, u32[]{:S(2)}, u32[]{:S(2)}) %all-to-all-start) | async-done | bytes 2097184 | tf_op jit(solution)/shard_map/all_to_all | solution.py:65
  70.0 3.3 %reshape.267 = bf16[16,8,64,2,64]{4,3,2,1,0:T(2,128)(2,1)} reshape(bf16[16,8,64,128]{3,2,1,0:T(8,128)(2,1)S(1)} %all-to-all-done) | data formatting | bytes 4194304 | tf_op jit(solution)/shard_map/reshape.7
  73.2 4.2 %multiply_convert_fusion = bf16[16,8,64,2,64]{4,2,3,1,0:T(8,128)(2,1)S(1)} fusion(f32[16,8,64]{2,1,0:T(8,128)S(1)} %get-tuple-element.8, bf16[16,8,64,2,64]{4,3,2,1,0:T(2,128)(2,1)} %reshape.267, bf16[16,8,64,64]{3,2,1,0:T(8,128)(2,1)} %bitcast.41, pred[16,8]{1,0:T(8,128)(4,1)S(1)} %copy.33, bf16[16,8,64]{2,1,0:T(8,128)(2,1)S(1)} %get-tuple-element.7), kind=kOutput, calls=%fused_computation.5 | convolution fusion | flops 137363456 | bytes 5292160 | tf_op jit(solution)/shard_map/ncitvj,ncstj->ncivs/dot_general | solution.py:21
  77.4 10.4 %copy.38 = bf16[16,8,64,2,64]{4,3,2,1,0:T(2,128)(2,1)} copy(bf16[16,8,64,2,64]{4,2,3,1,0:T(8,128)(2,1)S(1)} %multiply_convert_fusion) | data formatting | bytes 4194304 | tf_op jit(solution)/shard_map/convert_element_type | solution.py:25
  87.8 7.8 %reshape.268 = bf16[16,8,64,128]{3,2,1,0:T(8,128)(2,1)} reshape(bf16[16,8,64,2,64]{4,3,2,1,0:T(2,128)(2,1)} %copy.38) | data formatting | bytes 4194304 | tf_op jit(solution)/shard_map/reshape | solution.py:25
  95.6 0.0 copy-start.2
  95.6 5.0 %all-to-all-start.2 = ((bf16[16,8,64,128]{3,2,1,0:T(8,128)(2,1)}), bf16[16,8,64,128]{3,2,1,0:T(8,128)(2,1)S(1)}, u32[]{:S(2)}, u32[]{:S(2)}) async-start(bf16[16,8,64,128]{3,2,1,0:T(8,128)(2,1)} %reshape.268), calls=%async_computation.2 | async-start | bytes 4194304 | tf_op jit(solution)/shard_map/all_to_all | solution.py:28
  100.6 0.1 reduce_sum.23
  100.7 0.0 copy-done.2
  100.7 0.1 mul.87
  100.8 47.2 %all-to-all-done.2 = bf16[16,8,64,128]{3,2,1,0:T(8,128)(2,1)S(1)} async-done(((bf16[16,8,64,128]{3,2,1,0:T(8,128)(2,1)}), bf16[16,8,64,128]{3,2,1,0:T(8,128)(2,1)S(1)}, u32[]{:S(2)}, u32[]{:S(2)}) %all-to-all-start.2) | async-done | bytes 2097184 | tf_op jit(solution)/shard_map/all_to_all | solution.py:28
  148.1 0.7 gather_fusion.4
  148.8 1.6 %multiply_convert_fusion.1 = bf16[8,8,64,128]{3,2,1,0:T(8,128)(2,1)} fusion(f32[8,64]{1,0:T(8,128)S(1)} %get-tuple-element.12, bf16[8,8,64,128]{3,2,1,0:T(8,128)(2,1)S(1)} %bitcast.40, pred[8,8]{1,0:T(8,128)(4,1)S(1)} %compare_and_fusion), kind=kLoop, calls=%fused_computation.11 | loop fusion | flops 2097152 | bytes 2099264 | tf_op jit(solution)/shard_map/convert_element_type | solution.py:77
  (12 shorter events, 0.1 us)
Async XLA Ops:
  0.0 24.3 %copy-start = (bf16[16,64,64]{2,1,0:T(8,128)(2,1)S(1)}, bf16[16,64,64]{2,1,0:T(8,128)(2,1)}, u32[]{:S(2)}) copy-start(bf16[16,64,64]{2,1,0:T(8,128)(2,1)} %param.10) | copy-start | bytes 393220
  3.9 12.5 %all-to-all-start.1 = ((bf16[16,1,8]{2,1,0:T(2,128)(2,1)}), bf16[16,1,8]{2,1,0:T(2,128)(2,1)S(1)}, u32[]{:S(2)}, u32[]{:S(2)}) async-start(bf16[16,1,8]{2,1,0:T(2,128)(2,1)} %reshape.320), calls=%async_computation.1 | async-start | bytes 16384 | tf_op jit(solution)/shard_map/all_to_all | solution.py:66
  16.4 6.4 %copy-start.1 = (s32[16]{0:T(128)S(1)}, s32[16]{0:T(128)}, u32[]{:S(2)}) copy-start(s32[16]{0:T(128)} %param.12) | copy-start | bytes 196
  16.4 53.6 %all-to-all-start = ((bf16[16,8,64,128]{3,2,1,0:T(8,128)(2,1)}), bf16[16,8,64,128]{3,2,1,0:T(8,128)(2,1)S(1)}, u32[]{:S(2)}, u32[]{:S(2)}) async-start(bf16[16,8,64,128]{3,2,1,0:T(8,128)(2,1)} %select_select_fusion), calls=%async_computation | async-start | bytes 4194304 | tf_op jit(solution)/shard_map/all_to_all | solution.py:65
  95.6 5.1 %copy-start.2 = (s32[8,8]{1,0:T(8,128)S(1)}, s32[8,8]{1,0:T(8,128)}, u32[]{:S(2)}) copy-start(s32[8,8]{1,0:T(8,128)} %param.13) | copy-start | bytes 772
  95.6 52.5 %all-to-all-start.2 = ((bf16[16,8,64,128]{3,2,1,0:T(8,128)(2,1)}), bf16[16,8,64,128]{3,2,1,0:T(8,128)(2,1)S(1)}, u32[]{:S(2)}, u32[]{:S(2)}) async-start(bf16[16,8,64,128]{3,2,1,0:T(8,128)(2,1)} %reshape.268), calls=%async_computation.2 | async-start | bytes 4194304 | tf_op jit(solution)/shard_map/all_to_all | solution.py:28
where the time goes:
time: 151 us; the launch traced here: 150 us
  waiting for transfers between devices  90.5 us (60%)
  local copies, waits for them, and re-layouts  30.2 us (20%)
  starting transfers between devices  17.7 us (12%)
  matrix products  6 us (4%)
  other arithmetic  5.76 us (4%)
    all_to_all x1, waiting for transfers between devices, contract_right(): lax.all_to_all(partial_sums, 'sec', split_axis=0, concat_axis=0, tiled=True)  47.2 us
    all_to_all x1, waiting for transfers between devices, per_device(): lax.all_to_all(half_slots, 'sec', split_axis=0, concat_axis=0, tiled=True)  43.3 us
    convert_element_type x1, local copies, waits for them, and re-layouts, contract_right(): partial_sums.astype(jnp.bfloat16)  10.4 us
    reshape x1, local copies, waits for them, and re-layouts, contract_right(): partial_sums.astype(jnp.bfloat16)  7.78 us
    all_to_all x1, starting transfers between devices, per_device(): lax.all_to_all(slot_code, 'sec', split_axis=0, concat_axis=0, tiled=True)  6.55 us
    all_to_all x1, starting transfers between devices, per_device(): lax.all_to_all(half_slots, 'sec', split_axis=0, concat_axis=0, tiled=True)  6.15 us
    all_to_all x1, starting transfers between devices, contract_right(): lax.all_to_all(partial_sums, 'sec', split_axis=0, concat_axis=0, tiled=True)  5.04 us
    dot_general x1, matrix products, contract_right(): jnp.einsum('ncitvj,ncstj->ncivs', half_split, right_sel, preferred_elemen...  4.19 us
  transfers between devices with their start and end apart: 3, of which 2 were waited for; matrix products, arithmetic and copies ran while one was open for 7% of the time, Pallas kernels for 0%

commit v1 on v0

v1 whole, which is shorter than its diff:
```python
import functools

import jax
import jax.numpy as jnp
from jax import lax
from jax.experimental import pallas as pl
from jax.experimental.pallas import tpu as pltpu
from jax.sharding import PartitionSpec as P

VMEM_LIMIT = 48 * 1024 * 1024


def left_kernel(dims_ref, active_ref, left_ref, psi_ref, half_ref):
    sectors, blocks, tile, width = psi_ref.shape
    rows = lax.broadcasted_iota(jnp.int32, (tile, tile), 0)
    cols = lax.broadcasted_iota(jnp.int32, (tile, tile), 1)

    def one(a, carry):
        dim = dims_ref[a]
        keep = (rows < dim) & (cols < dim)
        op = jnp.where(keep, left_ref[a].astype(jnp.float32), 0.0).astype(jnp.bfloat16)
        for k in range(blocks):
            part = jnp.dot(op, psi_ref[a, k], preferred_element_type=jnp.float32)
            part = part * active_ref[a, k].astype(jnp.float32)
            half_ref[a, k] = part.astype(jnp.bfloat16)
        return carry

    lax.fori_loop(0, sectors, one, 0)


def right_kernel(owner_ref, slot_ref, half_ref, pairs_ref, out_ref):
    sectors, blocks, tile, width = half_ref.shape
    per_owner = pairs_ref.shape[1]
    lanes = lax.broadcasted_iota(jnp.int32, (tile, width), 1)

    def one(a, carry):
        for k in range(blocks):
            slot = slot_ref[a, k]
            second = (slot >= per_owner).astype(jnp.int32)
            pair = pairs_ref[owner_ref[a, k], slot - second * per_owner].astype(jnp.float32)
            swapped = pltpu.roll(pair, tile, 1)
            first_half = lanes < tile
            both = jnp.where((lanes >= tile).astype(jnp.int32) == second, pair, swapped)
            top = jnp.where(first_half, both, 0.0)
            low = jnp.where(first_half, 0.0, both)
            diag = jnp.concatenate([top, low], axis=0).astype(jnp.bfloat16)
            part = lax.dot_general(
                half_ref[a, k], diag, (((1,), (1,)), ((), ())), preferred_element_type=jnp.float32
            )
            out_ref[a, k] = part.astype(jnp.bfloat16)
        return carry

    lax.fori_loop(0, sectors, one, 0)


def per_device(
    psi, left_ops, right_ops, dims_left, dims_right, right_owner, right_slot, term_active
):
    left_count, block_count, tile, width = psi.shape
    right_count = right_ops.shape[0]
    pair_count = right_count // 2
    flops = 2 * psi.size * tile

    lanes = lax.iota(jnp.int32, tile)
    keep = lanes[None, :] < dims_right[:, None]
    kept = jnp.where(keep[:, :, None] & keep[:, None, :], right_ops, jnp.zeros_like(right_ops))
    pairs = jnp.concatenate([kept[:pair_count], kept[pair_count:]], axis=2)
    pairs_all = lax.all_gather(pairs, "sec", axis=0, tiled=False)

    smem = pl.BlockSpec(memory_space=pltpu.SMEM)
    vmem = pl.BlockSpec(memory_space=pltpu.VMEM)
    params = pltpu.CompilerParams(vmem_limit_bytes=VMEM_LIMIT)
    half = pl.pallas_call(
        left_kernel,
        out_shape=jax.ShapeDtypeStruct(psi.shape, jnp.bfloat16),
        in_specs=[smem, smem, vmem, vmem],
        out_specs=vmem,
        compiler_params=params,
        cost_estimate=pl.CostEstimate(flops=flops, bytes_accessed=4 * psi.size, transcendentals=0),
    )(dims_left, term_active.reshape(left_count, block_count), left_ops, psi)
    sigma = pl.pallas_call(
        right_kernel,
        out_shape=jax.ShapeDtypeStruct(psi.shape, jnp.bfloat16),
        in_specs=[smem, smem, vmem, vmem],
        out_specs=vmem,
        compiler_params=params,
        cost_estimate=pl.CostEstimate(flops=flops, bytes_accessed=8 * psi.size, transcendentals=0),
    )(right_owner, right_slot, half, pairs_all)
    if lax.axis_size("op") > 1:
        sigma = lax.psum_scatter(sigma, "op", scatter_dimension=3, tiled=True)
    return sigma


def solution(mesh):
    placed = (
        P(("grp", "sec"), None, None, None),
        P(("grp", "sec"), None, "op"),
        P(("grp", "sec"), None, "op"),
        P(("grp", "sec")),
        P(("grp", "sec")),
        P(("grp", "sec"), None),
        P(("grp", "sec"), None),
        P(("grp", "sec"), None, "op"),
    )
    return jax.shard_map(
        per_device,
        mesh=mesh,
        in_specs=placed,
        out_specs=P(("grp", "sec"), None, None, "op"),
        check_vma=False,
    )
```

time: 151 us -> 66.8 us (0.44)
  the two profiles are of different devices: /device:TPU:15 before, /device:TPU:0 now
where the time goes in v1:
time: 66.8 us; the launch traced here: 66.5 us
  waiting for transfers between devices  40.1 us (60%)
  between operations  13.4 us (20%)
  Pallas kernels  6.39 us (10%)
  local copies, waits for them, and re-layouts  3.86 us (6%)
  other arithmetic  2.73 us (4%)
    all_gather x1, waiting for transfers between devices, per_device(): pairs_all = lax.all_gather(pairs, 'sec', axis=0, tiled=False)  40.1 us
    pallas_call x1, Pallas kernels, per_device(): pl.pallas_call(right_kernel, out_shape=jax.ShapeDtypeStruct(psi.shape, jn...  4.43 us
    unnamed x14, local copies, waits for them, and re-layouts  3.84 us
    pallas_call x1, Pallas kernels, per_device(): pl.pallas_call(left_kernel, out_shape=jax.ShapeDtypeStruct(psi.shape, jnp...  1.96 us
  transfers between devices with their start and end apart: 1, of which 1 were waited for; matrix products, arithmetic and copies ran while one was open for 0% of the time, Pallas kernels for 3%

profile of v1, /device:TPU:0, one launch (start us, length us, event | category | flops | bytes accessed | tf_op | source)
XLA Modules:
  0.0 66.5 jit_solution(17278089279603907898)
XLA Ops:
  6.5 0.0 copy-start.1
  6.5 0.0 copy-start.5
  6.5 0.0 copy-start.4
  6.5 0.0 all-gather.3.cloned.1.call-start
  6.5 0.8 %iota_compare_fusion = pred[16,64]{1,0:T(8,128)(4,1)S(1)} fusion(s32[16]{0:T(128)} %param.12), kind=kLoop, calls=%fused_computation.2 | loop fusion | flops 1024 | bytes 1088 | tf_op jit(solution)/shard_map/lt | solution.py:65
  7.4 1.2 %and_select_fusion = bf16[16,64,64]{2,1,0:T(8,128)(2,1)S(1)} fusion(bf16[16,64,64]{2,1,0:T(8,128)(2,1)} %param.10, pred[16,64]{1,0:T(8,128)(4,1)S(1)} %iota_compare_fusion), kind=kLoop, calls=%fused_computation | loop fusion | flops 131072 | bytes 263168 | tf_op jit(solution)/shard_map/jit(_where)/select_n | solution.py:66
  8.5 0.8 %pad_maximum_fusion = bf16[8,64,128]{2,1,0:T(8,128)(2,1)} fusion(bf16[8,64,64]{2,1,0:T(8,128)(2,1)S(1)} %get-tuple-element.6, bf16[8,64,64]{2,1,0:T(8,128)(2,1)S(1)} %get-tuple-element.5), kind=kLoop, calls=%fused_computation.1 | loop fusion | flops 262144 | bytes 262144 | tf_op jit(solution)/shard_map/concatenate | solution.py:67
  9.3 0.0 all-gather.3.cloned.1.call-update
  9.3 0.0 copy-done.1
  9.3 0.0 copy-start.2
  9.4 0.9 %copy-done.2 = bf16[8,64,64]{2,1,0:T(8,128)(2,1)S(1)} copy-done((bf16[8,64,64]{2,1,0:T(8,128)(2,1)S(1)}, bf16[8,64,64]{2,1,0:T(8,128)(2,1)}, u32[]{:S(2)}) %copy-start.2) | copy-done | bytes 65560
  10.3 0.0 copy-start.3
  10.3 0.7 %copy-done.3 = s32[8,8,1]{1,2,0:T(1,128)S(1)} copy-done((s32[8,8,1]{1,2,0:T(1,128)S(1)}, s32[8,8,1]{1,2,0:T(1,128)}, u32[]{:S(2)}) %copy-start.3) | copy-done | bytes 280
  10.9 0.0 copy-start.6
  10.9 0.7 copy-done.6
  11.6 2.0 %shard_map.82.half_ref = bf16[8,8,64,128]{3,2,1,0:T(8,128)(2,1)S(1)} custom-call(s32[8]{0:T(128)S(1)} %copy-done.6, s32[8,8]{1,0:T(8,128)S(1)} %bitcast.3, bf16[8,64,64]{2,1,0:T(8,128)(2,1)S(1)} %copy-done.2, bf16[8,8,64,128]{3,2,1,0:T(8,128)(2,1)S(1)} %copy-done.1), custom_call_target="tpu_custom_call" | custom-call | flops 67108864 | bytes 2097152 | tf_op jit(solution)/shard_map/pallas_call | solution.py:73
  13.6 40.1 %all-gather.3.cloned.1.call-done = bf16[128,64,128]{2,1,0:T(8,128)(2,1)} async-done(((bf16[8,64,128]{2,1,0:T(8,128)(2,1)}), bf16[128,64,128]{2,1,0:T(8,128)(2,1)}) %all-gather.3.cloned.1.call-update) | async-done | bytes 2097168 | tf_op jit(solution)/shard_map/all_gather | solution.py:68
  53.7 0.0 copy-done.5
  53.7 0.0 copy-done.4
  53.7 0.0 copy-start
  53.7 1.6 %copy-done = bf16[128,64,128]{2,1,0:T(8,128)(2,1)S(1)} copy-done((bf16[128,64,128]{2,1,0:T(8,128)(2,1)S(1)}, bf16[128,64,128]{2,1,0:T(8,128)(2,1)}, u32[]{:S(2)}) %copy-start) | copy-done | bytes 2097176
  55.3 4.4 %shard_map.83 = bf16[8,8,64,128]{3,2,1,0:T(8,128)(2,1)} custom-call(s32[8,8]{1,0:T(8,128)S(1)} %copy-done.4, s32[8,8]{1,0:T(8,128)S(1)} %copy-done.5, bf16[8,8,64,128]{3,2,1,0:T(8,128)(2,1)S(1)} %shard_map.82.half_ref, bf16[16,8,64,128]{3,2,1,0:T(8,128)(2,1)S(1)} %bitcast.2), custom_call_target="tpu_custom_call" | custom-call | flops 67108864 | bytes 4194304 | tf_op jit(solution)/shard_map/pallas_call | solution.py:81
  (1 shorter events, 0.0 us)
Async XLA Ops:
  6.5 2.8 %copy-start.1 = (bf16[8,8,64,128]{3,2,1,0:T(8,128)(2,1)S(1)}, bf16[8,8,64,128]{3,2,1,0:T(8,128)(2,1)}, u32[]{:S(2)}) copy-start(bf16[8,8,64,128]{3,2,1,0:T(8,128)(2,1)} %psi_ref.1) | copy-start | bytes 3145732
  6.5 47.1 %copy-start.5 = (s32[8,8]{1,0:T(8,128)S(1)}, s32[8,8]{1,0:T(8,128)}, u32[]{:S(2)}) copy-start(s32[8,8]{1,0:T(8,128)} %slot_ref.1) | copy-start | bytes 772
  6.5 47.1 %copy-start.4 = (s32[8,8]{1,0:T(8,128)S(1)}, s32[8,8]{1,0:T(8,128)}, u32[]{:S(2)}) copy-start(s32[8,8]{1,0:T(8,128)} %owner_ref.1) | copy-start | bytes 772
  6.5 47.1 %all-gather.3.cloned.1.call-start = ((), (), s32[]{:S(2)}) async-start(), calls=%async_computation | async-start | bytes 2228224 | tf_op jit(solution)/shard_map/all_gather | solution.py:68
  9.3 0.9 %copy-start.2 = (bf16[8,64,64]{2,1,0:T(8,128)(2,1)S(1)}, bf16[8,64,64]{2,1,0:T(8,128)(2,1)}, u32[]{:S(2)}) copy-start(bf16[8,64,64]{2,1,0:T(8,128)(2,1)} %left_ref.1) | copy-start | bytes 196612
  10.3 0.7 %copy-start.3 = (s32[8,8,1]{1,2,0:T(1,128)S(1)}, s32[8,8,1]{1,2,0:T(1,128)}, u32[]{:S(2)}) copy-start(s32[8,8,1]{1,2,0:T(1,128)} %param.15) | copy-start | bytes 772
  10.9 0.7 copy-start.6
  53.7 1.6 %copy-start = (bf16[128,64,128]{2,1,0:T(8,128)(2,1)S(1)}, bf16[128,64,128]{2,1,0:T(8,128)(2,1)}, u32[]{:S(2)}) copy-start(bf16[128,64,128]{2,1,0:T(8,128)(2,1)} %all-gather.3.cloned.1.call-done) | copy-start | bytes 6291460
Sparse Core Ops, SparseCore 0:
  9.5 44.0 all-gather.2

commit v2 on v1

--- a/solution.py
+++ b/solution.py
@@ -28,21 +28,44 @@
     lax.fori_loop(0, sectors, one, 0)
 
 
-def right_kernel(owner_ref, slot_ref, half_ref, pairs_ref, out_ref):
+def pack_kernel(dims_ref, right_ref, pairs_ref):
+    count, tile, width = pairs_ref.shape
+    rows = lax.broadcasted_iota(jnp.int32, (tile, tile), 0)
+    cols = lax.broadcasted_iota(jnp.int32, (tile, tile), 1)
+    most = jnp.maximum(rows, cols)
+
+    def kept(b):
+        return jnp.where(most < dims_ref[b], right_ref[b].astype(jnp.float32), 0.0)
+
+    for p in range(count):
+        both = jnp.concatenate([kept(p), kept(p + count)], axis=1)
+        pairs_ref[p] = both.astype(jnp.bfloat16)
+
+
+def right_kernel(code_ref, half_ref, *refs):
+    piece_refs, out_ref, pairs_ref, sems = refs[:-3], refs[-3], refs[-2], refs[-1]
     sectors, blocks, tile, width = half_ref.shape
-    per_owner = pairs_ref.shape[1]
+    step = pairs_ref.shape[0] // len(piece_refs)
+    copies = [
+        pltpu.make_async_copy(piece, pairs_ref.at[pl.ds(i * step, step)], sems.at[i])
+        for i, piece in enumerate(piece_refs)
+    ]
+    for copy in copies:
+        copy.start()
+    for copy in copies:
+        copy.wait()
     lanes = lax.broadcasted_iota(jnp.int32, (tile, width), 1)
+    upper = (lanes >= tile).astype(jnp.int32)
 
     def one(a, carry):
         for k in range(blocks):
-            slot = slot_ref[a, k]
-            second = (slot >= per_owner).astype(jnp.int32)
-            pair = pairs_ref[owner_ref[a, k], slot - second * per_owner].astype(jnp.float32)
+            code = code_ref[a, k]
+            second = code & 1
+            pair = pairs_ref[code >> 1].astype(jnp.float32)
             swapped = pltpu.roll(pair, tile, 1)
-            first_half = lanes < tile
-            both = jnp.where((lanes >= tile).astype(jnp.int32) == second, pair, swapped)
-            top = jnp.where(first_half, both, 0.0)
-            low = jnp.where(first_half, 0.0, both)
+            both = jnp.where(upper == second, pair, swapped)
+            top = jnp.where(upper == 0, both, 0.0)
+            low = jnp.where(upper == 0, 0.0, both)
             diag = jnp.concatenate([top, low], axis=0).astype(jnp.bfloat16)
             part = lax.dot_general(
                 half_ref[a, k], diag, (((1,), (1,)), ((), ())), preferred_element_type=jnp.float32
@@ -53,23 +76,50 @@
     lax.fori_loop(0, sectors, one, 0)
 
 
+def gather_pieces(pairs):
+    count = lax.axis_size("sec")
+    me = lax.axis_index("sec")
+    if count % 4 or count > 32:
+        return [lax.all_gather(pairs, "sec", axis=0, tiled=True)], lambda owner: owner
+    lines = count // 4
+    pieces = [pairs]
+    for shift in range(1, lines):
+        route = [(i, (i + 4 * shift) % count) for i in range(count)]
+        pieces.append(lax.ppermute(pairs, "sec", route))
+    for bit in (2, 1):
+        route = [(i, i ^ bit) for i in range(count)]
+        pieces = pieces + [lax.ppermute(piece, "sec", route) for piece in pieces]
+
+    def order(owner):
+        shift = (me // 4 - owner // 4 + lines) % lines
+        flip = (me ^ owner) & 3
+        return ((flip & 1) * 2 + (flip >> 1)) * lines + shift
+
+    return pieces, order
+
+
 def per_device(
     psi, left_ops, right_ops, dims_left, dims_right, right_owner, right_slot, term_active
 ):
     left_count, block_count, tile, width = psi.shape
-    right_count = right_ops.shape[0]
-    pair_count = right_count // 2
+    pair_count = right_ops.shape[0] // 2
     flops = 2 * psi.size * tile
-
-    lanes = lax.iota(jnp.int32, tile)
-    keep = lanes[None, :] < dims_right[:, None]
-    kept = jnp.where(keep[:, :, None] & keep[:, None, :], right_ops, jnp.zeros_like(right_ops))
-    pairs = jnp.concatenate([kept[:pair_count], kept[pair_count:]], axis=2)
-    pairs_all = lax.all_gather(pairs, "sec", axis=0, tiled=False)
-
     smem = pl.BlockSpec(memory_space=pltpu.SMEM)
     vmem = pl.BlockSpec(memory_space=pltpu.VMEM)
     params = pltpu.CompilerParams(vmem_limit_bytes=VMEM_LIMIT)
+
+    pairs = pl.pallas_call(
+        pack_kernel,
+        out_shape=jax.ShapeDtypeStruct((pair_count, tile, 2 * tile), jnp.bfloat16),
+        in_specs=[smem, vmem],
+        out_specs=vmem,
+        compiler_params=params,
+        cost_estimate=pl.CostEstimate(flops=0, bytes_accessed=6 * right_ops.size, transcendentals=0),
+    )(dims_right, right_ops)
+    pieces, order = gather_pieces(pairs)
+    code = order(right_owner) * pair_count + right_slot % pair_count
+    code = code * 2 + right_slot // pair_count
+
     half = pl.pallas_call(
         left_kernel,
         out_shape=jax.ShapeDtypeStruct(psi.shape, jnp.bfloat16),
@@ -81,11 +131,15 @@
     sigma = pl.pallas_call(
         right_kernel,
         out_shape=jax.ShapeDtypeStruct(psi.shape, jnp.bfloat16),
-        in_specs=[smem, smem, vmem, vmem],
+        in_specs=[smem, vmem] + [pl.BlockSpec(memory_space=pl.ANY)] * len(pieces),
         out_specs=vmem,
+        scratch_shapes=[
+            pltpu.VMEM((lax.axis_size("sec") * pair_count, tile, 2 * tile), jnp.bfloat16),
+            pltpu.SemaphoreType.DMA((len(pieces),)),
+        ],
         compiler_params=params,
         cost_estimate=pl.CostEstimate(flops=flops, bytes_accessed=8 * psi.size, transcendentals=0),
-    )(right_owner, right_slot, half, pairs_all)
+    )(code, half, *pieces)
     if lax.axis_size("op") > 1:
         sigma = lax.psum_scatter(sigma, "op", scatter_dimension=3, tiled=True)
     return sigma

time: 66.8 us -> 37.3 us (0.56)
  waiting for transfers between devices: 40.1 us -> 12.2 us
  between operations: 13.4 us -> 0.09 us
  starting transfers between devices: 0.01 us -> 11.3 us
  Pallas kernels: 6.39 us -> 9.95 us
  other arithmetic: 2.73 us -> 0.02 us
    all_gather x1 -> x0, waiting for transfers between devices: 40.1 us -> none  [per_device(): pairs_all = lax.all_gather(pairs, 'sec', axis=0, tiled=False)]
    ppermute x0 -> x15, waiting for transfers between devices: none -> 12.2 us  [the longest x3 9.82 us: gather_pieces(): pieces.append(lax.ppermute(pairs, 'sec', route))]
    ppermute x0 -> x15, starting transfers between devices: none -> 11.3 us  [the longest x12 6.65 us: gather_pieces(): pieces = pieces + [lax.ppermute(piece, 'sec', route) for piece in pieces]]
    pallas_call x1, Pallas kernels: 4.43 us -> 7.34 us  [per_device(): pl.pallas_call(right_kernel, out_shape=jax.ShapeDtypeStruct(psi.shape, jn...]
    select_n x1 -> x0, other arithmetic: 1.15 us -> none  [per_device(): jnp.where(keep[:, :, None] & keep[:, None, :], right_ops, jnp.zeros_like(...]
    lt x1 -> x0, other arithmetic: 0.81 us -> none  [per_device(): keep = lanes[None, :] < dims_right[:, None]]
    concatenate x1 -> x0, other arithmetic: 0.77 us -> none  [per_device(): pairs = jnp.concatenate([kept[:pair_count], kept[pair_count:]], axis=2)]
    unnamed x14 -> x16, local copies, waits for them, and re-layouts: 3.84 us -> 3.53 us
  transfers between devices with their start and end apart: 1 -> 15, of which waited for: 1 -> 4; matrix products, arithmetic and copies ran while one was open for 0% -> 0% of each run, Pallas kernels for 3% -> 5%
where the time goes in v2:
time: 37.3 us; the launch traced here: 37 us
  waiting for transfers between devices  12.2 us (33%)
  starting transfers between devices  11.3 us (30%)
  Pallas kernels  9.95 us (27%)
  local copies, waits for them, and re-layouts  3.53 us (9%)
    ppermute x3, waiting for transfers between devices, gather_pieces(): pieces.append(lax.ppermute(pairs, 'sec', route))  9.82 us
    pallas_call x1, Pallas kernels, per_device(): pl.pallas_call(right_kernel, out_shape=jax.ShapeDtypeStruct(psi.shape, jn...  7.34 us
    ppermute x12, starting transfers between devices, gather_pieces(): pieces = pieces + [lax.ppermute(piece, 'sec', route) for piece in pieces]  6.65 us
    ppermute x3, starting transfers between devices, gather_pieces(): pieces.append(lax.ppermute(pairs, 'sec', route))  4.61 us
    unnamed x16, local copies, waits for them, and re-layouts  3.53 us
    ppermute x12, waiting for transfers between devices, gather_pieces(): pieces = pieces + [lax.ppermute(piece, 'sec', route) for piece in pieces]  2.36 us
    pallas_call x1, Pallas kernels, per_device(): pl.pallas_call(left_kernel, out_shape=jax.ShapeDtypeStruct(psi.shape, jnp...  1.96 us
  transfers between devices with their start and end apart: 15, of which 4 were waited for; matrix products, arithmetic and copies ran while one was open for 0% of the time, Pallas kernels for 5%

profile of v2, /device:TPU:0, one launch (start us, length us, event | category | flops | bytes accessed | tf_op | source)
XLA Modules:
  0.0 37.0 jit_solution(2851260610559655269)
XLA Ops:
  0.0 0.0 copy-start.1
  0.0 0.9 %copy-done.1 = bf16[16,64,64]{2,1,0:T(8,128)(2,1)S(1)} copy-done((bf16[16,64,64]{2,1,0:T(8,128)(2,1)S(1)}, bf16[16,64,64]{2,1,0:T(8,128)(2,1)}, u32[]{:S(2)}) %copy-start.1) | copy-done | bytes 131096
  1.0 0.0 copy-start.4
  1.0 0.7 %copy-done.4 = s32[16]{0:T(128)S(1)} copy-done((s32[16]{0:T(128)S(1)}, s32[16]{0:T(128)}, u32[]{:S(2)}) %copy-start.4) | copy-done | bytes 88
  1.6 0.0 copy-start.2
  1.6 0.6 %shard_map.83.refs_0_ = bf16[8,64,128]{2,1,0:T(8,128)(2,1)S(1)} custom-call(s32[16]{0:T(128)S(1)} %copy-done.4, bf16[16,64,64]{2,1,0:T(8,128)(2,1)S(1)} %copy-done.1), custom_call_target="tpu_custom_call" | custom-call | bytes 393216 | tf_op jit(solution)/shard_map/pallas_call | solution.py:111
  2.3 3.0 %collective-permute-start.3 = (bf16[8,64,128]{2,1,0:T(8,128)(2,1)S(1)}, bf16[8,64,128]{2,1,0:T(8,128)(2,1)S(1)}, u32[]{:S(2)}, u32[]{:S(2)}) collective-permute-start(bf16[8,64,128]{2,1,0:T(8,128)(2,1)S(1)} %shard_map.83.refs_0_), channel_id=1, source_target_pairs={{0,2},{1,3},{2,0},{3,1},{4,6},{5,7},{6,4},{7,5},{8,10},{9,11},{10,... | collective-permute-start | bytes 393224 | tf_op jit(solution)/shard_map/ppermute | solution.py:91
  5.3 3.6 %collective-permute-start.2 = (bf16[8,64,128]{2,1,0:T(8,128)(2,1)S(1)}, bf16[8,64,128]{2,1,0:T(8,128)(2,1)S(1)}, u32[]{:S(2)}, u32[]{:S(2)}) collective-permute-start(bf16[8,64,128]{2,1,0:T(8,128)(2,1)S(1)} %shard_map.83.refs_0_), channel_id=1, source_target_pairs={{0,12},{1,13},{2,14},{3,15},{4,0},{5,1},{6,2},{7,3},{8,4},{9,5},{1... | collective-permute-start | bytes 393224 | tf_op jit(solution)/shard_map/ppermute | solution.py:88
  8.9 0.0 collective-permute-start.7
  8.9 0.0 collective-permute-start.1
  8.9 1.0 %collective-permute-start = (bf16[8,64,128]{2,1,0:T(8,128)(2,1)S(1)}, bf16[8,64,128]{2,1,0:T(8,128)(2,1)S(1)}, u32[]{:S(2)}, u32[]{:S(2)}) collective-permute-start(bf16[8,64,128]{2,1,0:T(8,128)(2,1)S(1)} %shard_map.83.refs_0_), channel_id=1, source_target_pairs={{0,4},{1,5},{2,6},{3,7},{4,8},{5,9},{6,10},{7,11},{8,12},{9,13},{1... | collective-permute-start | bytes 393224 | tf_op jit(solution)/shard_map/ppermute | solution.py:88
  9.9 0.0 collective-permute-done.3.refs_4_
  9.9 0.0 collective-permute-start.11
  9.9 3.0 %collective-permute-done.2.refs_3_ = bf16[8,64,128]{2,1,0:T(8,128)(2,1)S(1)} collective-permute-done((bf16[8,64,128]{2,1,0:T(8,128)(2,1)S(1)}, bf16[8,64,128]{2,1,0:T(8,128)(2,1)S(1)}, u32[]{:S(2)}, u32[]{:S(2)}) %collective-permute-start.2) | collective-permute-done | bytes 131104 | tf_op jit(solution)/shard_map/ppermute | solution.py:88
  12.9 0.0 collective-permute-start.10
  12.9 0.0 collective-permute-done.7.refs_8_
  12.9 0.5 %collective-permute-start.6 = (bf16[8,64,128]{2,1,0:T(8,128)(2,1)S(1)}, bf16[8,64,128]{2,1,0:T(8,128)(2,1)S(1)}, u32[]{:S(2)}, u32[]{:S(2)}) collective-permute-start(bf16[8,64,128]{2,1,0:T(8,128)(2,1)S(1)} %collective-permute-done.2.refs_3_), channel_id=1, source_target_pairs={{0,2},{1,3},{2,0},{3,1},{4,6},{5,7},{6,4},{7,5},{8,10},{9,11},{10,... | collective-permute-start | bytes 393224 | tf_op jit(solution)/shard_map/ppermute | solution.py:91
  13.4 6.9 %collective-permute-done.1.refs_2_ = bf16[8,64,128]{2,1,0:T(8,128)(2,1)S(1)} collective-permute-done((bf16[8,64,128]{2,1,0:T(8,128)(2,1)S(1)}, bf16[8,64,128]{2,1,0:T(8,128)(2,1)S(1)}, u32[]{:S(2)}, u32[]{:S(2)}) %collective-permute-start.1) | collective-permute-done | bytes 131104 | tf_op jit(solution)/shard_map/ppermute | solution.py:88
  20.3 0.5 %collective-permute-start.5 = (bf16[8,64,128]{2,1,0:T(8,128)(2,1)S(1)}, bf16[8,64,128]{2,1,0:T(8,128)(2,1)S(1)}, u32[]{:S(2)}, u32[]{:S(2)}) collective-permute-start(bf16[8,64,128]{2,1,0:T(8,128)(2,1)S(1)} %collective-permute-done.1.refs_2_), channel_id=1, source_target_pairs={{0,2},{1,3},{2,0},{3,1},{4,6},{5,7},{6,4},{7,5},{8,10},{9,11},{10,... | collective-permute-start | bytes 393224 | tf_op jit(solution)/shard_map/ppermute | solution.py:91
  20.8 0.0 collective-permute-done.refs_1_
  20.8 1.5 %collective-permute-start.4 = (bf16[8,64,128]{2,1,0:T(8,128)(2,1)S(1)}, bf16[8,64,128]{2,1,0:T(8,128)(2,1)S(1)}, u32[]{:S(2)}, u32[]{:S(2)}) collective-permute-start(bf16[8,64,128]{2,1,0:T(8,128)(2,1)S(1)} %collective-permute-done.refs_1_), channel_id=1, source_target_pairs={{0,2},{1,3},{2,0},{3,1},{4,6},{5,7},{6,4},{7,5},{8,10},{9,11},{10,... | collective-permute-start | bytes 393224 | tf_op jit(solution)/shard_map/ppermute | solution.py:91
  22.3 0.0 copy-start.3
  22.3 0.0 copy-start.5
  22.3 0.0 copy-done.2
  22.3 0.7 %copy-done.3 = s32[8,8,1]{1,2,0:T(1,128)S(1)} copy-done((s32[8,8,1]{1,2,0:T(1,128)S(1)}, s32[8,8,1]{1,2,0:T(1,128)}, u32[]{:S(2)}) %copy-start.3) | copy-done | bytes 280
  23.0 0.0 copy-done.5
  23.0 0.0 copy-start
  23.0 1.2 %copy-done = bf16[8,8,64,128]{3,2,1,0:T(8,128)(2,1)S(1)} copy-done((bf16[8,8,64,128]{3,2,1,0:T(8,128)(2,1)S(1)}, bf16[8,8,64,128]{3,2,1,0:T(8,128)(2,1)}, u32[]{:S(2)}) %copy-start) | copy-done | bytes 1048600
  24.2 0.0 copy-start.6
  24.2 0.0 copy-start.7
  24.2 2.0 %shard_map.82.half_ref = bf16[8,8,64,128]{3,2,1,0:T(8,128)(2,1)S(1)} custom-call(s32[8]{0:T(128)S(1)} %copy-done.5, s32[8,8]{1,0:T(8,128)S(1)} %bitcast.1, bf16[8,64,64]{2,1,0:T(8,128)(2,1)S(1)} %copy-done.2, bf16[8,8,64,128]{3,2,1,0:T(8,128)(2,1)S(1)} %copy-done), custom_call_target="tpu_custom_call" | custom-call | flops 67108864 | bytes 2097152 | tf_op jit(solution)/shard_map/pallas_call | solution.py:123
  26.2 0.0 collective-permute-done.11.refs_12_
  26.2 0.1 collective-permute-start.9
  26.3 0.0 collective-permute-done.10.refs_11_
  26.3 0.5 %collective-permute-start.8 = (bf16[8,64,128]{2,1,0:T(8,128)(2,1)S(1)}, bf16[8,64,128]{2,1,0:T(8,128)(2,1)S(1)}, u32[]{:S(2)}, u32[]{:S(2)}) collective-permute-start(bf16[8,64,128]{2,1,0:T(8,128)(2,1)S(1)} %collective-permute-done.refs_1_), channel_id=1, source_target_pairs={{0,1},{1,0},{2,3},{3,2},{4,5},{5,4},{6,7},{7,6},{8,9},{9,8},{10,11... | collective-permute-start | bytes 393224 | tf_op jit(solution)/shard_map/ppermute | solution.py:91
  26.8 0.0 collective-permute-done.6.refs_7_
  26.8 0.1 collective-permute-start.14
  26.9 0.0 collective-permute-done.5.refs_6_
  26.9 0.4 %collective-permute-start.13 = (bf16[8,64,128]{2,1,0:T(8,128)(2,1)S(1)}, bf16[8,64,128]{2,1,0:T(8,128)(2,1)S(1)}, u32[]{:S(2)}, u32[]{:S(2)}) collective-permute-start(bf16[8,64,128]{2,1,0:T(8,128)(2,1)S(1)} %collective-permute-done.5.refs_6_), channel_id=1, source_target_pairs={{0,1},{1,0},{2,3},{3,2},{4,5},{5,4},{6,7},{7,6},{8,9},{9,8},{10,11... | collective-permute-start | bytes 393224 | tf_op jit(solution)/shard_map/ppermute | solution.py:91
  27.3 1.1 %collective-permute-done.4.refs_5_ = bf16[8,64,128]{2,1,0:T(8,128)(2,1)S(1)} collective-permute-done((bf16[8,64,128]{2,1,0:T(8,128)(2,1)S(1)}, bf16[8,64,128]{2,1,0:T(8,128)(2,1)S(1)}, u32[]{:S(2)}, u32[]{:S(2)}) %collective-permute-start.4) | collective-permute-done | bytes 131104 | tf_op jit(solution)/shard_map/ppermute | solution.py:91
  28.3 0.0 collective-permute-start.12
  28.4 0.0 copy-done.6
  28.4 0.0 copy-done.7
  28.4 0.0 collective-permute-done.9.refs_10_
  28.4 0.0 collective-permute-done.8.refs_9_
  28.4 0.0 collective-permute-done.14.refs_15_
  28.4 0.0 collective-permute-done.13.refs_14_
  28.4 1.3 %collective-permute-done.12.refs_13_ = bf16[8,64,128]{2,1,0:T(8,128)(2,1)S(1)} collective-permute-done((bf16[8,64,128]{2,1,0:T(8,128)(2,1)S(1)}, bf16[8,64,128]{2,1,0:T(8,128)(2,1)S(1)}, u32[]{:S(2)}, u32[]{:S(2)}) %collective-permute-start.12) | collective-permute-done | bytes 131104 | tf_op jit(solution)/shard_map/ppermute | solution.py:91
  29.7 7.3 %shard_map.84 = bf16[8,8,64,128]{3,2,1,0:T(8,128)(2,1)} custom-call(s32[8,8]{1,0:T(8,128)S(1)} %fusion.8.code_ref, bf16[8,8,64,128]{3,2,1,0:T(8,128)(2,1)S(1)} %shard_map.82.half_ref, bf16[8,64,128]{2,1,0:T(8,128)(2,1)S(1)} %shard_map.83.refs_0_, bf16[8,64,128]{2,1,0:T(8,128)(2,1)S(1)} %collective-permute-done.refs_1_, ...), custom_call_target="tpu_custom_call" | custom-call | flops 67108864 | bytes 4194304 | tf_op jit(solution)/shard_map/pallas_call | solution.py:131
  (1 shorter events, 0.0 us)
Async XLA Ops:
  0.0 0.9 %copy-start.1 = (bf16[16,64,64]{2,1,0:T(8,128)(2,1)S(1)}, bf16[16,64,64]{2,1,0:T(8,128)(2,1)}, u32[]{:S(2)}) copy-start(bf16[16,64,64]{2,1,0:T(8,128)(2,1)} %right_ref.1) | copy-start | bytes 393220
  1.0 0.7 %copy-start.4 = (s32[16]{0:T(128)S(1)}, s32[16]{0:T(128)}, u32[]{:S(2)}) copy-start(s32[16]{0:T(128)} %dims_ref.3) | copy-start | bytes 196
  1.6 20.7 %copy-start.2 = (bf16[8,64,64]{2,1,0:T(8,128)(2,1)S(1)}, bf16[8,64,64]{2,1,0:T(8,128)(2,1)}, u32[]{:S(2)}) copy-start(bf16[8,64,64]{2,1,0:T(8,128)(2,1)} %left_ref.1) | copy-start | bytes 196612
  2.3 7.6 %collective-permute-start.3 = (bf16[8,64,128]{2,1,0:T(8,128)(2,1)S(1)}, bf16[8,64,128]{2,1,0:T(8,128)(2,1)S(1)}, u32[]{:S(2)}, u32[]{:S(2)}) collective-permute-start(bf16[8,64,128]{2,1,0:T(8,128)(2,1)S(1)} %shard_map.83.refs_0_), channel_id=1, source_target_pairs={{0,2},{1,3},{2,0},{3,1},{4,6},{5,7},{6,4},{7,5},{8,10},{9,11},{10,... | collective-permute-start | bytes 393224 | tf_op jit(solution)/shard_map/ppermute | solution.py:91
  5.3 7.6 %collective-permute-start.2 = (bf16[8,64,128]{2,1,0:T(8,128)(2,1)S(1)}, bf16[8,64,128]{2,1,0:T(8,128)(2,1)S(1)}, u32[]{:S(2)}, u32[]{:S(2)}) collective-permute-start(bf16[8,64,128]{2,1,0:T(8,128)(2,1)S(1)} %shard_map.83.refs_0_), channel_id=1, source_target_pairs={{0,12},{1,13},{2,14},{3,15},{4,0},{5,1},{6,2},{7,3},{8,4},{9,5},{1... | collective-permute-start | bytes 393224 | tf_op jit(solution)/shard_map/ppermute | solution.py:88
  8.9 4.0 %collective-permute-start.7 = (bf16[8,64,128]{2,1,0:T(8,128)(2,1)S(1)}, bf16[8,64,128]{2,1,0:T(8,128)(2,1)S(1)}, u32[]{:S(2)}, u32[]{:S(2)}) collective-permute-start(bf16[8,64,128]{2,1,0:T(8,128)(2,1)S(1)} %shard_map.83.refs_0_), channel_id=1, source_target_pairs={{0,1},{1,0},{2,3},{3,2},{4,5},{5,4},{6,7},{7,6},{8,9},{9,8},{10,11... | collective-permute-start | bytes 393224 | tf_op jit(solution)/shard_map/ppermute | solution.py:91
  8.9 11.4 %collective-permute-start.1 = (bf16[8,64,128]{2,1,0:T(8,128)(2,1)S(1)}, bf16[8,64,128]{2,1,0:T(8,128)(2,1)S(1)}, u32[]{:S(2)}, u32[]{:S(2)}) collective-permute-start(bf16[8,64,128]{2,1,0:T(8,128)(2,1)S(1)} %shard_map.83.refs_0_), channel_id=1, source_target_pairs={{0,8},{1,9},{2,10},{3,11},{4,12},{5,13},{6,14},{7,15},{8,0},{9,1},... | collective-permute-start | bytes 393224 | tf_op jit(solution)/shard_map/ppermute | solution.py:88
  8.9 11.9 %collective-permute-start = (bf16[8,64,128]{2,1,0:T(8,128)(2,1)S(1)}, bf16[8,64,128]{2,1,0:T(8,128)(2,1)S(1)}, u32[]{:S(2)}, u32[]{:S(2)}) collective-permute-start(bf16[8,64,128]{2,1,0:T(8,128)(2,1)S(1)} %shard_map.83.refs_0_), channel_id=1, source_target_pairs={{0,4},{1,5},{2,6},{3,7},{4,8},{5,9},{6,10},{7,11},{8,12},{9,13},{1... | collective-permute-start | bytes 393224 | tf_op jit(solution)/shard_map/ppermute | solution.py:88
  9.9 16.3 %collective-permute-start.11 = (bf16[8,64,128]{2,1,0:T(8,128)(2,1)S(1)}, bf16[8,64,128]{2,1,0:T(8,128)(2,1)S(1)}, u32[]{:S(2)}, u32[]{:S(2)}) collective-permute-start(bf16[8,64,128]{2,1,0:T(8,128)(2,1)S(1)} %collective-permute-done.3.refs_4_), channel_id=1, source_target_pairs={{0,1},{1,0},{2,3},{3,2},{4,5},{5,4},{6,7},{7,6},{8,9},{9,8},{10,11... | collective-permute-start | bytes 393224 | tf_op jit(solution)/shard_map/ppermute | solution.py:91
  12.9 13.4 %collective-permute-start.10 = (bf16[8,64,128]{2,1,0:T(8,128)(2,1)S(1)}, bf16[8,64,128]{2,1,0:T(8,128)(2,1)S(1)}, u32[]{:S(2)}, u32[]{:S(2)}) collective-permute-start(bf16[8,64,128]{2,1,0:T(8,128)(2,1)S(1)} %collective-permute-done.2.refs_3_), channel_id=1, source_target_pairs={{0,1},{1,0},{2,3},{3,2},{4,5},{5,4},{6,7},{7,6},{8,9},{9,8},{10,11... | collective-permute-start | bytes 393224 | tf_op jit(solution)/shard_map/ppermute | solution.py:91
  12.9 13.9 %collective-permute-start.6 = (bf16[8,64,128]{2,1,0:T(8,128)(2,1)S(1)}, bf16[8,64,128]{2,1,0:T(8,128)(2,1)S(1)}, u32[]{:S(2)}, u32[]{:S(2)}) collective-permute-start(bf16[8,64,128]{2,1,0:T(8,128)(2,1)S(1)} %collective-permute-done.2.refs_3_), channel_id=1, source_target_pairs={{0,2},{1,3},{2,0},{3,1},{4,6},{5,7},{6,4},{7,5},{8,10},{9,11},{10,... | collective-permute-start | bytes 393224 | tf_op jit(solution)/shard_map/ppermute | solution.py:91
  20.3 6.6 %collective-permute-start.5 = (bf16[8,64,128]{2,1,0:T(8,128)(2,1)S(1)}, bf16[8,64,128]{2,1,0:T(8,128)(2,1)S(1)}, u32[]{:S(2)}, u32[]{:S(2)}) collective-permute-start(bf16[8,64,128]{2,1,0:T(8,128)(2,1)S(1)} %collective-permute-done.1.refs_2_), channel_id=1, source_target_pairs={{0,2},{1,3},{2,0},{3,1},{4,6},{5,7},{6,4},{7,5},{8,10},{9,11},{10,... | collective-permute-start | bytes 393224 | tf_op jit(solution)/shard_map/ppermute | solution.py:91
  20.8 7.6 %collective-permute-start.4 = (bf16[8,64,128]{2,1,0:T(8,128)(2,1)S(1)}, bf16[8,64,128]{2,1,0:T(8,128)(2,1)S(1)}, u32[]{:S(2)}, u32[]{:S(2)}) collective-permute-start(bf16[8,64,128]{2,1,0:T(8,128)(2,1)S(1)} %collective-permute-done.refs_1_), channel_id=1, source_target_pairs={{0,2},{1,3},{2,0},{3,1},{4,6},{5,7},{6,4},{7,5},{8,10},{9,11},{10,... | collective-permute-start | bytes 393224 | tf_op jit(solution)/shard_map/ppermute | solution.py:91
  22.3 0.7 %copy-start.3 = (s32[8,8,1]{1,2,0:T(1,128)S(1)}, s32[8,8,1]{1,2,0:T(1,128)}, u32[]{:S(2)}) copy-start(s32[8,8,1]{1,2,0:T(1,128)} %param.15) | copy-start | bytes 772
  22.3 0.7 %copy-start.5 = (s32[8]{0:T(128)S(1)}, s32[8]{0:T(128)}, u32[]{:S(2)}) copy-start(s32[8]{0:T(128)} %dims_ref.2) | copy-start | bytes 100
  23.0 1.2 %copy-start = (bf16[8,8,64,128]{3,2,1,0:T(8,128)(2,1)S(1)}, bf16[8,8,64,128]{3,2,1,0:T(8,128)(2,1)}, u32[]{:S(2)}) copy-start(bf16[8,8,64,128]{3,2,1,0:T(8,128)(2,1)} %psi_ref.1) | copy-start | bytes 3145732
  24.2 4.2 %copy-start.6 = (s32[8,8]{1,0:T(8,128)S(1)}, s32[8,8]{1,0:T(8,128)}, u32[]{:S(2)}) copy-start(s32[8,8]{1,0:T(8,128)} %param.13) | copy-start | bytes 772
  24.2 4.2 %copy-start.7 = (s32[8,8]{1,0:T(8,128)S(1)}, s32[8,8]{1,0:T(8,128)}, u32[]{:S(2)}) copy-start(s32[8,8]{1,0:T(8,128)} %param.14) | copy-start | bytes 772
  26.2 2.2 %collective-permute-start.9 = (bf16[8,64,128]{2,1,0:T(8,128)(2,1)S(1)}, bf16[8,64,128]{2,1,0:T(8,128)(2,1)S(1)}, u32[]{:S(2)}, u32[]{:S(2)}) collective-permute-start(bf16[8,64,128]{2,1,0:T(8,128)(2,1)S(1)} %collective-permute-done.1.refs_2_), channel_id=1, source_target_pairs={{0,1},{1,0},{2,3},{3,2},{4,5},{5,4},{6,7},{7,6},{8,9},{9,8},{10,11... | collective-permute-start | bytes 393224 | tf_op jit(solution)/shard_map/ppermute | solution.py:91
  26.3 2.1 %collective-permute-start.8 = (bf16[8,64,128]{2,1,0:T(8,128)(2,1)S(1)}, bf16[8,64,128]{2,1,0:T(8,128)(2,1)S(1)}, u32[]{:S(2)}, u32[]{:S(2)}) collective-permute-start(bf16[8,64,128]{2,1,0:T(8,128)(2,1)S(1)} %collective-permute-done.refs_1_), channel_id=1, source_target_pairs={{0,1},{1,0},{2,3},{3,2},{4,5},{5,4},{6,7},{7,6},{8,9},{9,8},{10,11... | collective-permute-start | bytes 393224 | tf_op jit(solution)/shard_map/ppermute | solution.py:91
  26.8 1.6 %collective-permute-start.14 = (bf16[8,64,128]{2,1,0:T(8,128)(2,1)S(1)}, bf16[8,64,128]{2,1,0:T(8,128)(2,1)S(1)}, u32[]{:S(2)}, u32[]{:S(2)}) collective-permute-start(bf16[8,64,128]{2,1,0:T(8,128)(2,1)S(1)} %collective-permute-done.6.refs_7_), channel_id=1, source_target_pairs={{0,1},{1,0},{2,3},{3,2},{4,5},{5,4},{6,7},{7,6},{8,9},{9,8},{10,11... | collective-permute-start | bytes 393224 | tf_op jit(solution)/shard_map/ppermute | solution.py:91
  26.9 1.6 %collective-permute-start.13 = (bf16[8,64,128]{2,1,0:T(8,128)(2,1)S(1)}, bf16[8,64,128]{2,1,0:T(8,128)(2,1)S(1)}, u32[]{:S(2)}, u32[]{:S(2)}) collective-permute-start(bf16[8,64,128]{2,1,0:T(8,128)(2,1)S(1)} %collective-permute-done.5.refs_6_), channel_id=1, source_target_pairs={{0,1},{1,0},{2,3},{3,2},{4,5},{5,4},{6,7},{7,6},{8,9},{9,8},{10,11... | collective-permute-start | bytes 393224 | tf_op jit(solution)/shard_map/ppermute | solution.py:91
  28.3 1.3 %collective-permute-start.12 = (bf16[8,64,128]{2,1,0:T(8,128)(2,1)S(1)}, bf16[8,64,128]{2,1,0:T(8,128)(2,1)S(1)}, u32[]{:S(2)}, u32[]{:S(2)}) collective-permute-start(bf16[8,64,128]{2,1,0:T(8,128)(2,1)S(1)} %collective-permute-done.4.refs_5_), channel_id=1, source_target_pairs={{0,1},{1,0},{2,3},{3,2},{4,5},{5,4},{6,7},{7,6},{8,9},{9,8},{10,11... | collective-permute-start | bytes 393224 | tf_op jit(solution)/shard_map/ppermute | solution.py:91

commit v3 on v1

v3 whole, which is shorter than its diff:
```python
import jax
import jax.numpy as jnp
from jax import lax
from jax.experimental import pallas as pl
from jax.experimental.pallas import tpu as pltpu
from jax.sharding import PartitionSpec as P

VMEM_LIMIT = 48 * 1024 * 1024
RING_MOST = 32


def pack_kernel(dims_hbm, right_hbm, pairs_ref, dims_ref, right_ref, sems):
    count, tile, width = pairs_ref.shape
    load_right = pltpu.make_async_copy(right_hbm, right_ref, sems.at[0])
    load_dims = pltpu.make_async_copy(dims_hbm, dims_ref, sems.at[1])
    load_right.start()
    load_dims.start()
    rows = lax.broadcasted_iota(jnp.int32, (tile, tile), 0)
    cols = lax.broadcasted_iota(jnp.int32, (tile, tile), 1)
    most = jnp.maximum(rows, cols)
    load_dims.wait()
    load_right.wait()

    def kept(b):
        return jnp.where(most < dims_ref[b], right_ref[b].astype(jnp.float32), 0.0)

    for p in range(count):
        both = jnp.concatenate([kept(p), kept(p + count)], axis=1)
        pairs_ref[p] = both.astype(jnp.bfloat16)


def left_kernel(dims_ref, active_ref, code_ref, left_ref, psi_ref, half_ref):
    sectors, blocks, tile, width = psi_ref.shape
    rows = lax.broadcasted_iota(jnp.int32, (tile, tile), 0)
    cols = lax.broadcasted_iota(jnp.int32, (tile, tile), 1)
    most = jnp.maximum(rows, cols)
    upper = (lax.broadcasted_iota(jnp.int32, (tile, width), 1) >= tile).astype(jnp.int32)

    def one(a, carry):
        op = jnp.where(most < dims_ref[a], left_ref[a].astype(jnp.float32), 0.0).astype(jnp.bfloat16)
        for k in range(blocks):
            part = jnp.dot(op, psi_ref[a, k], preferred_element_type=jnp.float32)
            part = part * active_ref[a, k].astype(jnp.float32)
            other = pltpu.roll(part, tile, 1)
            second = code_ref[a, k] & 1
            here = upper == second
            first = jnp.where(upper == 0, part, other)
            last = jnp.where(upper == 0, other, part)
            half_ref[a, k, :, :width] = jnp.where(here, first, 0.0).astype(jnp.bfloat16)
            half_ref[a, k, :, width:] = jnp.where(here, last, 0.0).astype(jnp.bfloat16)
        return carry

    lax.fori_loop(0, sectors, one, 0)


def right_kernel(code_ref, half_ref, *refs):
    piece_refs, (out_hbm, pairs_ref, out_ref, sems) = refs[:-4], refs[-4:]
    sectors, blocks, tile, width = out_ref.shape
    step = pairs_ref.shape[0] // len(piece_refs)
    for i, piece in enumerate(piece_refs):
        pairs_ref[i * step:(i + 1) * step] = piece[...]
    zero = jnp.zeros((tile, width), jnp.bfloat16)

    def store(a):
        return pltpu.make_async_copy(out_ref.at[a], out_hbm.at[a], sems.at[a])

    def one(a, carry):
        for k in range(blocks):
            pair = pairs_ref[code_ref[a, k] >> 1]
            top = jnp.concatenate([pair, zero], axis=1)
            low = jnp.concatenate([zero, pair], axis=1)
            diag = jnp.concatenate([top, low], axis=0)
            part = lax.dot_general(
                half_ref[a, k], diag, (((1,), (1,)), ((), ())), preferred_element_type=jnp.float32
            )
            out_ref[a, k] = part.astype(jnp.bfloat16)
        store(a).start()
        return carry

    lax.fori_loop(0, sectors, one, 0)
    for a in range(sectors):
        store(a).wait()


def gather_pieces(pairs):
    count = lax.axis_size("sec")
    if count % 4 or count > RING_MOST:
        return [lax.all_gather(pairs, "sec", axis=0, tiled=True)], lambda owner: owner
    lines, chips = count // 4, count // 2
    ring = [4 * z for z in range(lines)] + [4 * z + 2 for z in reversed(range(lines))]
    onward = [(ring[p], ring[(p + 1) % chips]) for p in range(chips)]
    onward += [(ring[p] + 1, ring[p - 1] + 1) for p in range(chips)]
    across = [(i, i ^ 1) for i in range(count)]

    def swap(piece):
        return lax.ppermute(piece, "sec", across)

    def send(piece):
        return lax.ppermute(piece, "sec", onward)

    mid = chips // 2
    own, partner = [pairs], [swap(pairs)]
    for hop in range(1, mid):
        own.append(send(own[-1]))
        partner.append(send(partner[-1]))
    own.append(send(own[-1]))
    pieces = []
    for hop in range(mid):
        pieces += [own[hop], partner[hop]]
    pieces += [own[mid], swap(own[mid])]
    for hop in reversed(range(1, mid)):
        pieces += [swap(partner[hop]), swap(own[hop])]

    def place(index):
        line, cross = index // 4, (index // 2) % 2
        return jnp.where(cross == 0, line, chips - 1 - line), index % 2

    def order(owner):
        me_at, me_core = place(lax.axis_index("sec"))
        at, core = place(owner)
        behind = jnp.where(me_core == 0, me_at - at, at - me_at)
        return ((behind + chips) % chips) * 2 + (core ^ me_core)

    return pieces, order


def per_device(
    psi, left_ops, right_ops, dims_left, dims_right, right_owner, right_slot, term_active
):
    left_count, block_count, tile, width = psi.shape
    pair_count = right_ops.shape[0] // 2
    flops = 2 * psi.size * tile
    smem = pl.BlockSpec(memory_space=pltpu.SMEM)
    vmem = pl.BlockSpec(memory_space=pltpu.VMEM)
    hbm = pl.BlockSpec(memory_space=pltpu.HBM)
    params = pltpu.CompilerParams(vmem_limit_bytes=VMEM_LIMIT)

    pairs = pl.pallas_call(
        pack_kernel,
        out_shape=jax.ShapeDtypeStruct((pair_count, tile, 2 * tile), jnp.bfloat16),
        in_specs=[hbm, hbm],
        out_specs=vmem,
        scratch_shapes=[
            pltpu.SMEM(dims_right.shape, jnp.int32),
            pltpu.VMEM(right_ops.shape, jnp.bfloat16),
            pltpu.SemaphoreType.DMA((2,)),
        ],
        compiler_params=params,
        cost_estimate=pl.CostEstimate(flops=0, bytes_accessed=6 * right_ops.size, transcendentals=0),
    )(dims_right, right_ops)
    pieces, order = gather_pieces(pairs)
    code = order(right_owner) * pair_count + right_slot % pair_count
    code = code * 2 + right_slot // pair_count

    half = pl.pallas_call(
        left_kernel,
        out_shape=jax.ShapeDtypeStruct((left_count, block_count, tile, 2 * width), jnp.bfloat16),
        in_specs=[smem, smem, smem, vmem, vmem],
        out_specs=vmem,
        compiler_params=params,
        cost_estimate=pl.CostEstimate(flops=flops, bytes_accessed=6 * psi.size, transcendentals=0),
    )(dims_left, term_active.reshape(left_count, block_count), code, left_ops, psi)
    sigma = pl.pallas_call(
        right_kernel,
        out_shape=jax.ShapeDtypeStruct(psi.shape, jnp.bfloat16),
        in_specs=[smem] + [vmem] * (1 + len(pieces)),
        out_specs=hbm,
        scratch_shapes=[
            pltpu.VMEM((lax.axis_size("sec") * pair_count, tile, 2 * tile), jnp.bfloat16),
            pltpu.VMEM(psi.shape, jnp.bfloat16),
            pltpu.SemaphoreType.DMA((left_count,)),
        ],
        compiler_params=params,
        cost_estimate=pl.CostEstimate(flops=flops, bytes_accessed=8 * psi.size, transcendentals=0),
    )(code, half, *pieces)
    if lax.axis_size("op") > 1:
        sigma = lax.psum_scatter(sigma, "op", scatter_dimension=3, tiled=True)
    return sigma


def solution(mesh):
    placed = (
        P(("grp", "sec"), None, None, None),
        P(("grp", "sec"), None, "op"),
        P(("grp", "sec"), None, "op"),
        P(("grp", "sec")),
        P(("grp", "sec")),
        P(("grp", "sec"), None),
        P(("grp", "sec"), None),
        P(("grp", "sec"), None, "op"),
    )
    return jax.shard_map(
        per_device,
        mesh=mesh,
        in_specs=placed,
        out_specs=P(("grp", "sec"), None, None, "op"),
        check_vma=False,
    )
```

time: 66.8 us -> 36.6 us (0.55)
  waiting for transfers between devices: 40.1 us -> 7.74 us
  starting transfers between devices: 0.01 us -> 15.2 us
  between operations: 13.4 us -> 0.08 us
  other arithmetic: 2.73 us -> 0.74 us
  local copies, waits for them, and re-layouts: 3.86 us -> 5.07 us
  Pallas kernels: 6.39 us -> 7.46 us
    all_gather x1 -> x0, waiting for transfers between devices: 40.1 us -> none  [per_device(): pairs_all = lax.all_gather(pairs, 'sec', axis=0, tiled=False)]
    ppermute x0 -> x15, starting transfers between devices: none -> 15.2 us  [the longest x7 14.1 us: send(): return lax.ppermute(piece, 'sec', onward)]
    ppermute x0 -> x15, waiting for transfers between devices: none -> 7.74 us  [the longest x7 7.71 us: send(): return lax.ppermute(piece, 'sec', onward)]
    pallas_call x1 -> x2, Pallas kernels: 1.96 us -> 3.49 us  [the longest x1 2.81 us: per_device(): pl.pallas_call(left_kernel, out_shape=jax.ShapeDtypeStruct((left_count, b...]
    unnamed x14 -> x12, local copies, waits for them, and re-layouts: 3.84 us -> 5.07 us
    select_n x1 -> x0, other arithmetic: 1.15 us -> none  [per_device(): jnp.where(keep[:, :, None] & keep[:, None, :], right_ops, jnp.zeros_like(...]
    lt x1 -> x0, other arithmetic: 0.81 us -> none  [per_device(): keep = lanes[None, :] < dims_right[:, None]]
    concatenate x1 -> x0, other arithmetic: 0.77 us -> none  [per_device(): pairs = jnp.concatenate([kept[:pair_count], kept[pair_count:]], axis=2)]
  transfers between devices with their start and end apart: 1 -> 15, of which waited for: 1 -> 5; matrix products, arithmetic and copies ran while one was open for 0% -> 2% of each run, Pallas kernels for 3% -> 8%
where the time goes in v3:
time: 36.6 us; the launch traced here: 36.3 us
  starting transfers between devices  15.2 us (42%)
  waiting for transfers between devices  7.74 us (21%)
  Pallas kernels  7.46 us (20%)
  local copies, waits for them, and re-layouts  5.07 us (14%)
  other arithmetic  0.74 us (2%)
    ppermute x7, starting transfers between devices, send(): return lax.ppermute(piece, 'sec', onward)  14.1 us
    ppermute x7, waiting for transfers between devices, send(): return lax.ppermute(piece, 'sec', onward)  7.71 us
    unnamed x12, local copies, waits for them, and re-layouts  5.07 us
    pallas_call x1, Pallas kernels, per_device(): pl.pallas_call(right_kernel, out_shape=jax.ShapeDtypeStruct(psi.shape, jn...  3.97 us
    pallas_call x1, Pallas kernels, per_device(): pl.pallas_call(left_kernel, out_shape=jax.ShapeDtypeStruct((left_count, b...  2.81 us
    ppermute x8, starting transfers between devices, swap(): return lax.ppermute(piece, 'sec', across)  1.1 us
    add x1, other arithmetic, per_device(): code = code * 2 + right_slot // pair_count  0.74 us
  transfers between devices with their start and end apart: 15, of which 5 were waited for; matrix products, arithmetic and copies ran while one was open for 2% of the time, Pallas kernels for 8%

profile of v3, /device:TPU:0, one launch (start us, length us, event | category | flops | bytes accessed | tf_op | source)
XLA Modules:
  0.0 36.3 jit_solution(18231077672653659656)
XLA Ops:
  0.0 0.0 copy-start.1
  0.0 0.9 %copy-done.1 = bf16[16,64,64]{2,1,0:T(8,128)(2,1)S(1)} copy-done((bf16[16,64,64]{2,1,0:T(8,128)(2,1)S(1)}, bf16[16,64,64]{2,1,0:T(8,128)(2,1)}, u32[]{:S(2)}) %copy-start.1) | copy-done | bytes 131096
  1.0 0.0 copy-start.4
  1.0 0.7 %copy-done.4 = s32[16]{0:T(128)S(1)} copy-done((s32[16]{0:T(128)S(1)}, s32[16]{0:T(128)}, u32[]{:S(2)}) %copy-start.4) | copy-done | bytes 88
  1.6 0.7 %shard_map.83.refs_0_ = bf16[8,64,128]{2,1,0:T(8,128)(2,1)S(1)} custom-call(s32[16]{0:T(128)S(1)} %copy-done.4, bf16[16,64,64]{2,1,0:T(8,128)(2,1)S(1)} %copy-done.1), custom_call_target="tpu_custom_call" | custom-call | bytes 393216 | tf_op jit(solution)/shard_map/pallas_call | solution.py:138
  2.3 3.1 %collective-permute-start.1 = (bf16[8,64,128]{2,1,0:T(8,128)(2,1)S(1)}, bf16[8,64,128]{2,1,0:T(8,128)(2,1)S(1)}, u32[]{:S(2)}, u32[]{:S(2)}) collective-permute-start(bf16[8,64,128]{2,1,0:T(8,128)(2,1)S(1)} %shard_map.83.refs_0_), channel_id=1, source_target_pairs={{0,4},{4,8},{8,12},{12,14},{14,10},{10,6},{6,2},{2,0},{1,3},{5,1},... | collective-permute-start | bytes 393224 | tf_op jit(solution)/shard_map/ppermute | solution.py:99
  5.4 0.0 collective-permute-start
  5.4 2.9 %collective-permute-done.1.refs_2_ = bf16[8,64,128]{2,1,0:T(8,128)(2,1)S(1)} collective-permute-done((bf16[8,64,128]{2,1,0:T(8,128)(2,1)S(1)}, bf16[8,64,128]{2,1,0:T(8,128)(2,1)S(1)}, u32[]{:S(2)}, u32[]{:S(2)}) %collective-permute-start.1) | collective-permute-done | bytes 131104 | tf_op jit(solution)/shard_map/ppermute | solution.py:99
  8.2 2.1 %collective-permute-start.3 = (bf16[8,64,128]{2,1,0:T(8,128)(2,1)S(1)}, bf16[8,64,128]{2,1,0:T(8,128)(2,1)S(1)}, u32[]{:S(2)}, u32[]{:S(2)}) collective-permute-start(bf16[8,64,128]{2,1,0:T(8,128)(2,1)S(1)} %collective-permute-done.1.refs_2_), channel_id=1, source_target_pairs={{0,4},{4,8},{8,12},{12,14},{14,10},{10,6},{6,2},{2,0},{1,3},{5,1},... | collective-permute-start | bytes 393224 | tf_op jit(solution)/shard_map/ppermute | solution.py:99
  10.3 0.0 collective-permute-done.refs_1_
  10.3 1.6 %collective-permute-start.2 = (bf16[8,64,128]{2,1,0:T(8,128)(2,1)S(1)}, bf16[8,64,128]{2,1,0:T(8,128)(2,1)S(1)}, u32[]{:S(2)}, u32[]{:S(2)}) collective-permute-start(bf16[8,64,128]{2,1,0:T(8,128)(2,1)S(1)} %collective-permute-done.refs_1_), channel_id=1, source_target_pairs={{0,4},{4,8},{8,12},{12,14},{14,10},{10,6},{6,2},{2,0},{1,3},{5,1},... | collective-permute-start | bytes 393224 | tf_op jit(solution)/shard_map/ppermute | solution.py:99
  11.9 1.3 %collective-permute-done.3.refs_4_ = bf16[8,64,128]{2,1,0:T(8,128)(2,1)S(1)} collective-permute-done((bf16[8,64,128]{2,1,0:T(8,128)(2,1)S(1)}, bf16[8,64,128]{2,1,0:T(8,128)(2,1)S(1)}, u32[]{:S(2)}, u32[]{:S(2)}) %collective-permute-start.3) | collective-permute-done | bytes 131104 | tf_op jit(solution)/shard_map/ppermute | solution.py:99
  13.2 2.1 %collective-permute-start.5 = (bf16[8,64,128]{2,1,0:T(8,128)(2,1)S(1)}, bf16[8,64,128]{2,1,0:T(8,128)(2,1)S(1)}, u32[]{:S(2)}, u32[]{:S(2)}) collective-permute-start(bf16[8,64,128]{2,1,0:T(8,128)(2,1)S(1)} %collective-permute-done.3.refs_4_), channel_id=1, source_target_pairs={{0,4},{4,8},{8,12},{12,14},{14,10},{10,6},{6,2},{2,0},{1,3},{5,1},... | collective-permute-start | bytes 393224 | tf_op jit(solution)/shard_map/ppermute | solution.py:99
  15.3 0.0 collective-permute-done.2.refs_3_
  15.3 1.6 %collective-permute-start.4 = (bf16[8,64,128]{2,1,0:T(8,128)(2,1)S(1)}, bf16[8,64,128]{2,1,0:T(8,128)(2,1)S(1)}, u32[]{:S(2)}, u32[]{:S(2)}) collective-permute-start(bf16[8,64,128]{2,1,0:T(8,128)(2,1)S(1)} %collective-permute-done.2.refs_3_), channel_id=1, source_target_pairs={{0,4},{4,8},{8,12},{12,14},{14,10},{10,6},{6,2},{2,0},{1,3},{5,1},... | collective-permute-start | bytes 393224 | tf_op jit(solution)/shard_map/ppermute | solution.py:99
  16.9 0.0 collective-permute-start.14
  16.9 0.5 %collective-permute-start.12 = (bf16[8,64,128]{2,1,0:T(8,128)(2,1)S(1)}, bf16[8,64,128]{2,1,0:T(8,128)(2,1)S(1)}, u32[]{:S(2)}, u32[]{:S(2)}) collective-permute-start(bf16[8,64,128]{2,1,0:T(8,128)(2,1)S(1)} %collective-permute-done.3.refs_4_), channel_id=1, source_target_pairs={{0,1},{1,0},{2,3},{3,2},{4,5},{5,4},{6,7},{7,6},{8,9},{9,8},{10,11... | collective-permute-start | bytes 393224 | tf_op jit(solution)/shard_map/ppermute | solution.py:96
  17.4 0.8 %collective-permute-done.5.refs_6_ = bf16[8,64,128]{2,1,0:T(8,128)(2,1)S(1)} collective-permute-done((bf16[8,64,128]{2,1,0:T(8,128)(2,1)S(1)}, bf16[8,64,128]{2,1,0:T(8,128)(2,1)S(1)}, u32[]{:S(2)}, u32[]{:S(2)}) %collective-permute-start.5) | collective-permute-done | bytes 131104 | tf_op jit(solution)/shard_map/ppermute | solution.py:99
  18.2 2.1 %collective-permute-start.7 = (bf16[8,64,128]{2,1,0:T(8,128)(2,1)S(1)}, bf16[8,64,128]{2,1,0:T(8,128)(2,1)S(1)}, u32[]{:S(2)}, u32[]{:S(2)}) collective-permute-start(bf16[8,64,128]{2,1,0:T(8,128)(2,1)S(1)} %collective-permute-done.5.refs_6_), channel_id=1, source_target_pairs={{0,4},{4,8},{8,12},{12,14},{14,10},{10,6},{6,2},{2,0},{1,3},{5,1},... | collective-permute-start | bytes 393224 | tf_op jit(solution)/shard_map/ppermute | solution.py:99
  20.3 0.0 collective-permute-done.4.refs_5_
  20.3 1.6 %collective-permute-start.6 = (bf16[8,64,128]{2,1,0:T(8,128)(2,1)S(1)}, bf16[8,64,128]{2,1,0:T(8,128)(2,1)S(1)}, u32[]{:S(2)}, u32[]{:S(2)}) collective-permute-start(bf16[8,64,128]{2,1,0:T(8,128)(2,1)S(1)} %collective-permute-done.4.refs_5_), channel_id=1, source_target_pairs={{0,4},{4,8},{8,12},{12,14},{14,10},{10,6},{6,2},{2,0},{1,3},{5,1},... | collective-permute-start | bytes 393224 | tf_op jit(solution)/shard_map/ppermute | solution.py:99
  21.9 0.0 collective-permute-start.13
  21.9 0.0 collective-permute-done.14.refs_15_
  21.9 0.5 %collective-permute-start.10 = (bf16[8,64,128]{2,1,0:T(8,128)(2,1)S(1)}, bf16[8,64,128]{2,1,0:T(8,128)(2,1)S(1)}, u32[]{:S(2)}, u32[]{:S(2)}) collective-permute-start(bf16[8,64,128]{2,1,0:T(8,128)(2,1)S(1)} %collective-permute-done.5.refs_6_), channel_id=1, source_target_pairs={{0,1},{1,0},{2,3},{3,2},{4,5},{5,4},{6,7},{7,6},{8,9},{9,8},{10,11... | collective-permute-start | bytes 393224 | tf_op jit(solution)/shard_map/ppermute | solution.py:96
  22.4 0.0 collective-permute-done.12.refs_13_
  22.4 0.1 collective-permute-start.11
  22.4 0.7 %collective-permute-done.7.refs_8_ = bf16[8,64,128]{2,1,0:T(8,128)(2,1)S(1)} collective-permute-done((bf16[8,64,128]{2,1,0:T(8,128)(2,1)S(1)}, bf16[8,64,128]{2,1,0:T(8,128)(2,1)S(1)}, u32[]{:S(2)}, u32[]{:S(2)}) %collective-permute-start.7) | collective-permute-done | bytes 131104 | tf_op jit(solution)/shard_map/ppermute | solution.py:99
  23.1 0.0 collective-permute-start.8
  23.1 2.1 %collective-permute-done.6.refs_7_ = bf16[8,64,128]{2,1,0:T(8,128)(2,1)S(1)} collective-permute-done((bf16[8,64,128]{2,1,0:T(8,128)(2,1)S(1)}, bf16[8,64,128]{2,1,0:T(8,128)(2,1)S(1)}, u32[]{:S(2)}, u32[]{:S(2)}) %collective-permute-start.6) | collective-permute-done | bytes 131104 | tf_op jit(solution)/shard_map/ppermute | solution.py:99
  25.3 0.0 collective-permute-start.9
  25.3 0.7 %fusion.9.code_ref = s32[8,8]{1,0:T(8,128)S(1)} fusion(s32[8,8]{1,0:T(8,128)} %param.14, s32[8,8]{1,0:T(8,128)} %param.13, s32[]{:T(128)S(6)} %select_n.61, s32[]{:T(128)S(6)} %select_n.66, pred[]{:T(512)S(6)} %eq.18), kind=kLoop, calls=%fused_computation.29 | loop fusion | flops 5376 | bytes 777 | tf_op jit(solution)/shard_map/add | solution.py:153
  26.0 0.0 copy-start
  26.0 1.2 %copy-done = bf16[8,8,64,128]{3,2,1,0:T(8,128)(2,1)S(1)} copy-done((bf16[8,8,64,128]{3,2,1,0:T(8,128)(2,1)S(1)}, bf16[8,8,64,128]{3,2,1,0:T(8,128)(2,1)}, u32[]{:S(2)}) %copy-start) | copy-done | bytes 1048600
  27.2 0.0 copy-start.2
  27.2 0.9 %copy-done.2 = bf16[8,64,64]{2,1,0:T(8,128)(2,1)S(1)} copy-done((bf16[8,64,64]{2,1,0:T(8,128)(2,1)S(1)}, bf16[8,64,64]{2,1,0:T(8,128)(2,1)}, u32[]{:S(2)}) %copy-start.2) | copy-done | bytes 65560
  28.1 0.0 copy-start.3
  28.1 0.7 %copy-done.3 = s32[8,8,1]{1,2,0:T(1,128)S(1)} copy-done((s32[8,8,1]{1,2,0:T(1,128)S(1)}, s32[8,8,1]{1,2,0:T(1,128)}, u32[]{:S(2)}) %copy-start.3) | copy-done | bytes 280
  28.8 0.0 copy-start.5
  28.8 0.7 %copy-done.5 = s32[8]{0:T(128)S(1)} copy-done((s32[8]{0:T(128)S(1)}, s32[8]{0:T(128)}, u32[]{:S(2)}) %copy-start.5) | copy-done | bytes 56
  29.5 2.8 %shard_map.82.half_ref = bf16[8,8,64,256]{3,2,1,0:T(8,128)(2,1)S(1)} custom-call(s32[8]{0:T(128)S(1)} %copy-done.5, s32[8,8]{1,0:T(8,128)S(1)} %bitcast.1, s32[8,8]{1,0:T(8,128)S(1)} %fusion.9.code_ref, bf16[8,64,64]{2,1,0:T(8,128)(2,1)S(1)} %copy-done.2, bf16[8,8,64,128]{3,2,1,0:T(8,128)(2,1)S(1)} %copy-done), custom_call_target="tpu_custom_call" | custom-call | flops 67108864 | bytes 3145728 | tf_op jit(solution)/shard_map/pallas_call | solution.py:155
  32.3 0.0 collective-permute-done.13.refs_14_
  32.3 0.0 collective-permute-done.10.refs_11_
  32.3 0.0 collective-permute-done.11.refs_12_
  32.3 0.0 collective-permute-done.8.refs_9_
  32.3 0.0 collective-permute-done.9.refs_10_
  32.3 4.0 %shard_map.84 = bf16[8,8,64,128]{3,2,1,0:T(8,128)(2,1)} custom-call(s32[8,8]{1,0:T(8,128)S(1)} %fusion.9.code_ref, bf16[8,8,64,256]{3,2,1,0:T(8,128)(2,1)S(1)} %shard_map.82.half_ref, bf16[8,64,128]{2,1,0:T(8,128)(2,1)S(1)} %shard_map.83.refs_0_, bf16[8,64,128]{2,1,0:T(8,128)(2,1)S(1)} %collective-permute-done.refs_1_, ...), custom_call_target="tpu_custom_call" | custom-call | flops 67108864 | bytes 4194304 | tf_op jit(solution)/shard_map/pallas_call | solution.py:163
Async XLA Ops:
  0.0 0.9 %copy-start.1 = (bf16[16,64,64]{2,1,0:T(8,128)(2,1)S(1)}, bf16[16,64,64]{2,1,0:T(8,128)(2,1)}, u32[]{:S(2)}) copy-start(bf16[16,64,64]{2,1,0:T(8,128)(2,1)} %right_hbm.1) | copy-start | bytes 393220
  1.0 0.7 %copy-start.4 = (s32[16]{0:T(128)S(1)}, s32[16]{0:T(128)}, u32[]{:S(2)}) copy-start(s32[16]{0:T(128)} %dims_hbm.1) | copy-start | bytes 196
  2.3 5.9 %collective-permute-start.1 = (bf16[8,64,128]{2,1,0:T(8,128)(2,1)S(1)}, bf16[8,64,128]{2,1,0:T(8,128)(2,1)S(1)}, u32[]{:S(2)}, u32[]{:S(2)}) collective-permute-start(bf16[8,64,128]{2,1,0:T(8,128)(2,1)S(1)} %shard_map.83.refs_0_), channel_id=1, source_target_pairs={{0,4},{4,8},{8,12},{12,14},{14,10},{10,6},{6,2},{2,0},{1,3},{5,1},... | collective-permute-start | bytes 393224 | tf_op jit(solution)/shard_map/ppermute | solution.py:99
  5.4 5.0 %collective-permute-start = (bf16[8,64,128]{2,1,0:T(8,128)(2,1)S(1)}, bf16[8,64,128]{2,1,0:T(8,128)(2,1)S(1)}, u32[]{:S(2)}, u32[]{:S(2)}) collective-permute-start(bf16[8,64,128]{2,1,0:T(8,128)(2,1)S(1)} %shard_map.83.refs_0_), channel_id=1, source_target_pairs={{0,1},{1,0},{2,3},{3,2},{4,5},{5,4},{6,7},{7,6},{8,9},{9,8},{10,11... | collective-permute-start | bytes 393224 | tf_op jit(solution)/shard_map/ppermute | solution.py:96
  8.2 5.0 %collective-permute-start.3 = (bf16[8,64,128]{2,1,0:T(8,128)(2,1)S(1)}, bf16[8,64,128]{2,1,0:T(8,128)(2,1)S(1)}, u32[]{:S(2)}, u32[]{:S(2)}) collective-permute-start(bf16[8,64,128]{2,1,0:T(8,128)(2,1)S(1)} %collective-permute-done.1.refs_2_), channel_id=1, source_target_pairs={{0,4},{4,8},{8,12},{12,14},{14,10},{10,6},{6,2},{2,0},{1,3},{5,1},... | collective-permute-start | bytes 393224 | tf_op jit(solution)/shard_map/ppermute | solution.py:99
  10.3 5.0 %collective-permute-start.2 = (bf16[8,64,128]{2,1,0:T(8,128)(2,1)S(1)}, bf16[8,64,128]{2,1,0:T(8,128)(2,1)S(1)}, u32[]{:S(2)}, u32[]{:S(2)}) collective-permute-start(bf16[8,64,128]{2,1,0:T(8,128)(2,1)S(1)} %collective-permute-done.refs_1_), channel_id=1, source_target_pairs={{0,4},{4,8},{8,12},{12,14},{14,10},{10,6},{6,2},{2,0},{1,3},{5,1},... | collective-permute-start | bytes 393224 | tf_op jit(solution)/shard_map/ppermute | solution.py:99
  13.2 5.0 %collective-permute-start.5 = (bf16[8,64,128]{2,1,0:T(8,128)(2,1)S(1)}, bf16[8,64,128]{2,1,0:T(8,128)(2,1)S(1)}, u32[]{:S(2)}, u32[]{:S(2)}) collective-permute-start(bf16[8,64,128]{2,1,0:T(8,128)(2,1)S(1)} %collective-permute-done.3.refs_4_), channel_id=1, source_target_pairs={{0,4},{4,8},{8,12},{12,14},{14,10},{10,6},{6,2},{2,0},{1,3},{5,1},... | collective-permute-start | bytes 393224 | tf_op jit(solution)/shard_map/ppermute | solution.py:99
  15.3 5.0 %collective-permute-start.4 = (bf16[8,64,128]{2,1,0:T(8,128)(2,1)S(1)}, bf16[8,64,128]{2,1,0:T(8,128)(2,1)S(1)}, u32[]{:S(2)}, u32[]{:S(2)}) collective-permute-start(bf16[8,64,128]{2,1,0:T(8,128)(2,1)S(1)} %collective-permute-done.2.refs_3_), channel_id=1, source_target_pairs={{0,4},{4,8},{8,12},{12,14},{14,10},{10,6},{6,2},{2,0},{1,3},{5,1},... | collective-permute-start | bytes 393224 | tf_op jit(solution)/shard_map/ppermute | solution.py:99
  16.9 5.0 %collective-permute-start.14 = (bf16[8,64,128]{2,1,0:T(8,128)(2,1)S(1)}, bf16[8,64,128]{2,1,0:T(8,128)(2,1)S(1)}, u32[]{:S(2)}, u32[]{:S(2)}) collective-permute-start(bf16[8,64,128]{2,1,0:T(8,128)(2,1)S(1)} %collective-permute-done.1.refs_2_), channel_id=1, source_target_pairs={{0,1},{1,0},{2,3},{3,2},{4,5},{5,4},{6,7},{7,6},{8,9},{9,8},{10,11... | collective-permute-start | bytes 393224 | tf_op jit(solution)/shard_map/ppermute | solution.py:96
  16.9 5.5 %collective-permute-start.12 = (bf16[8,64,128]{2,1,0:T(8,128)(2,1)S(1)}, bf16[8,64,128]{2,1,0:T(8,128)(2,1)S(1)}, u32[]{:S(2)}, u32[]{:S(2)}) collective-permute-start(bf16[8,64,128]{2,1,0:T(8,128)(2,1)S(1)} %collective-permute-done.3.refs_4_), channel_id=1, source_target_pairs={{0,1},{1,0},{2,3},{3,2},{4,5},{5,4},{6,7},{7,6},{8,9},{9,8},{10,11... | collective-permute-start | bytes 393224 | tf_op jit(solution)/shard_map/ppermute | solution.py:96
  18.2 5.0 %collective-permute-start.7 = (bf16[8,64,128]{2,1,0:T(8,128)(2,1)S(1)}, bf16[8,64,128]{2,1,0:T(8,128)(2,1)S(1)}, u32[]{:S(2)}, u32[]{:S(2)}) collective-permute-start(bf16[8,64,128]{2,1,0:T(8,128)(2,1)S(1)} %collective-permute-done.5.refs_6_), channel_id=1, source_target_pairs={{0,4},{4,8},{8,12},{12,14},{14,10},{10,6},{6,2},{2,0},{1,3},{5,1},... | collective-permute-start | bytes 393224 | tf_op jit(solution)/shard_map/ppermute | solution.py:99
  20.3 5.0 %collective-permute-start.6 = (bf16[8,64,128]{2,1,0:T(8,128)(2,1)S(1)}, bf16[8,64,128]{2,1,0:T(8,128)(2,1)S(1)}, u32[]{:S(2)}, u32[]{:S(2)}) collective-permute-start(bf16[8,64,128]{2,1,0:T(8,128)(2,1)S(1)} %collective-permute-done.4.refs_5_), channel_id=1, source_target_pairs={{0,4},{4,8},{8,12},{12,14},{14,10},{10,6},{6,2},{2,0},{1,3},{5,1},... | collective-permute-start | bytes 393224 | tf_op jit(solution)/shard_map/ppermute | solution.py:99
  21.9 10.4 %collective-permute-start.13 = (bf16[8,64,128]{2,1,0:T(8,128)(2,1)S(1)}, bf16[8,64,128]{2,1,0:T(8,128)(2,1)S(1)}, u32[]{:S(2)}, u32[]{:S(2)}) collective-permute-start(bf16[8,64,128]{2,1,0:T(8,128)(2,1)S(1)} %collective-permute-done.2.refs_3_), channel_id=1, source_target_pairs={{0,1},{1,0},{2,3},{3,2},{4,5},{5,4},{6,7},{7,6},{8,9},{9,8},{10,11... | collective-permute-start | bytes 393224 | tf_op jit(solution)/shard_map/ppermute | solution.py:96
  21.9 10.4 %collective-permute-start.10 = (bf16[8,64,128]{2,1,0:T(8,128)(2,1)S(1)}, bf16[8,64,128]{2,1,0:T(8,128)(2,1)S(1)}, u32[]{:S(2)}, u32[]{:S(2)}) collective-permute-start(bf16[8,64,128]{2,1,0:T(8,128)(2,1)S(1)} %collective-permute-done.5.refs_6_), channel_id=1, source_target_pairs={{0,1},{1,0},{2,3},{3,2},{4,5},{5,4},{6,7},{7,6},{8,9},{9,8},{10,11... | collective-permute-start | bytes 393224 | tf_op jit(solution)/shard_map/ppermute | solution.py:96
  22.4 9.9 %collective-permute-start.11 = (bf16[8,64,128]{2,1,0:T(8,128)(2,1)S(1)}, bf16[8,64,128]{2,1,0:T(8,128)(2,1)S(1)}, u32[]{:S(2)}, u32[]{:S(2)}) collective-permute-start(bf16[8,64,128]{2,1,0:T(8,128)(2,1)S(1)} %collective-permute-done.4.refs_5_), channel_id=1, source_target_pairs={{0,1},{1,0},{2,3},{3,2},{4,5},{5,4},{6,7},{7,6},{8,9},{9,8},{10,11... | collective-permute-start | bytes 393224 | tf_op jit(solution)/shard_map/ppermute | solution.py:96
  23.1 9.2 %collective-permute-start.8 = (bf16[8,64,128]{2,1,0:T(8,128)(2,1)S(1)}, bf16[8,64,128]{2,1,0:T(8,128)(2,1)S(1)}, u32[]{:S(2)}, u32[]{:S(2)}) collective-permute-start(bf16[8,64,128]{2,1,0:T(8,128)(2,1)S(1)} %collective-permute-done.7.refs_8_), channel_id=1, source_target_pairs={{0,1},{1,0},{2,3},{3,2},{4,5},{5,4},{6,7},{7,6},{8,9},{9,8},{10,11... | collective-permute-start | bytes 393224 | tf_op jit(solution)/shard_map/ppermute | solution.py:96
  25.3 7.1 %collective-permute-start.9 = (bf16[8,64,128]{2,1,0:T(8,128)(2,1)S(1)}, bf16[8,64,128]{2,1,0:T(8,128)(2,1)S(1)}, u32[]{:S(2)}, u32[]{:S(2)}) collective-permute-start(bf16[8,64,128]{2,1,0:T(8,128)(2,1)S(1)} %collective-permute-done.6.refs_7_), channel_id=1, source_target_pairs={{0,1},{1,0},{2,3},{3,2},{4,5},{5,4},{6,7},{7,6},{8,9},{9,8},{10,11... | collective-permute-start | bytes 393224 | tf_op jit(solution)/shard_map/ppermute | solution.py:96
  26.0 1.2 %copy-start = (bf16[8,8,64,128]{3,2,1,0:T(8,128)(2,1)S(1)}, bf16[8,8,64,128]{3,2,1,0:T(8,128)(2,1)}, u32[]{:S(2)}) copy-start(bf16[8,8,64,128]{3,2,1,0:T(8,128)(2,1)} %psi_ref.1) | copy-start | bytes 3145732
  27.2 0.9 %copy-start.2 = (bf16[8,64,64]{2,1,0:T(8,128)(2,1)S(1)}, bf16[8,64,64]{2,1,0:T(8,128)(2,1)}, u32[]{:S(2)}) copy-start(bf16[8,64,64]{2,1,0:T(8,128)(2,1)} %left_ref.1) | copy-start | bytes 196612
  28.1 0.7 %copy-start.3 = (s32[8,8,1]{1,2,0:T(1,128)S(1)}, s32[8,8,1]{1,2,0:T(1,128)}, u32[]{:S(2)}) copy-start(s32[8,8,1]{1,2,0:T(1,128)} %param.15) | copy-start | bytes 772
  28.8 0.7 %copy-start.5 = (s32[8]{0:T(128)S(1)}, s32[8]{0:T(128)}, u32[]{:S(2)}) copy-start(s32[8]{0:T(128)} %dims_ref.1) | copy-start | bytes 100

commit v4 on v3

v4 whole, which is shorter than its diff:
```python
import jax
import jax.numpy as jnp
from jax import lax
from jax.experimental import pallas as pl
from jax.experimental.pallas import tpu as pltpu
from jax.sharding import PartitionSpec as P

VMEM_LIMIT = 48 * 1024 * 1024
GROUP = 4


def pack_kernel(dims_hbm, right_hbm, pairs_ref, dims_ref, right_ref, sems):
    count, tile, width = pairs_ref.shape
    load_right = pltpu.make_async_copy(right_hbm, right_ref, sems.at[0])
    load_dims = pltpu.make_async_copy(dims_hbm, dims_ref, sems.at[1])
    load_right.start()
    load_dims.start()
    rows = lax.broadcasted_iota(jnp.int32, (tile, tile), 0)
    cols = lax.broadcasted_iota(jnp.int32, (tile, tile), 1)
    most = jnp.maximum(rows, cols)
    load_dims.wait()
    load_right.wait()

    def kept(b):
        return jnp.where(most < dims_ref[b], right_ref[b].astype(jnp.float32), 0.0)

    for p in range(count):
        both = jnp.concatenate([kept(p), kept(p + count)], axis=1)
        pairs_ref[p] = both.astype(jnp.bfloat16)


def left_kernel(dims_ref, active_ref, code_ref, left_ref, psi_ref, half_ref):
    sectors, blocks, tile, width = psi_ref.shape
    rows = lax.broadcasted_iota(jnp.int32, (tile, tile), 0)
    cols = lax.broadcasted_iota(jnp.int32, (tile, tile), 1)
    most = jnp.maximum(rows, cols)
    upper = (lax.broadcasted_iota(jnp.int32, (tile, width), 1) >= tile).astype(jnp.int32)

    def one(a, carry):
        op = jnp.where(most < dims_ref[a], left_ref[a].astype(jnp.float32), 0.0).astype(jnp.bfloat16)
        for k in range(blocks):
            part = jnp.dot(op, psi_ref[a, k], preferred_element_type=jnp.float32)
            part = part * active_ref[a, k].astype(jnp.float32)
            other = pltpu.roll(part, tile, 1)
            second = code_ref[a * blocks + k] & 1
            here = upper == second
            first = jnp.where(upper == 0, part, other)
            last = jnp.where(upper == 0, other, part)
            half_ref[a, k, :, :width] = jnp.where(here, first, 0.0).astype(jnp.bfloat16)
            half_ref[a, k, :, width:] = jnp.where(here, last, 0.0).astype(jnp.bfloat16)
        return carry

    lax.fori_loop(0, sectors, one, 0, unroll=2)


def times_operator(half, pair):
    zero = jnp.zeros_like(pair)
    top = jnp.concatenate([pair, zero], axis=1)
    low = jnp.concatenate([zero, pair], axis=1)
    both = jnp.concatenate([top, low], axis=0)
    part = lax.dot_general(half, both, (((1,), (1,)), ((), ())), preferred_element_type=jnp.float32)
    return part.astype(jnp.bfloat16)


def merge(piece_refs, pairs_ref):
    step = pairs_ref.shape[0] // len(piece_refs)
    for i, piece in enumerate(piece_refs):
        pairs_ref[i * step:(i + 1) * step] = piece[...]


def early_kernel(code_ref, half_ref, *refs):
    piece_refs, (out_hbm, late_ref, pairs_ref, out_ref, sems) = refs[:-5], refs[-5:]
    sectors, blocks, tile, width = out_ref.shape
    count = pairs_ref.shape[0]
    merge(piece_refs, pairs_ref)

    def store(a):
        return pltpu.make_async_copy(out_ref.at[a], out_hbm.at[a], sems.at[a])

    def one(a, listed):
        for k in range(blocks):
            item = a * blocks + k
            at = code_ref[item] >> 1
            late = at >= count
            pair = pairs_ref[jnp.where(late, 0, at)]
            out_ref[a, k] = times_operator(half_ref[a, k], pair)
            late_ref[listed] = item
            listed = listed + late.astype(jnp.int32)
        store(a).start()
        return listed

    listed = lax.fori_loop(0, sectors, one, 0)
    late_ref[sectors * blocks] = listed
    for a in range(sectors):
        store(a).wait()


def late_kernel(code_ref, late_ref, early_hbm, half_ref, *refs):
    piece_refs, (out_hbm, pairs_ref, out_ref, sems) = refs[:-4], refs[-4:]
    sectors, blocks, tile, width = half_ref.shape
    items = sectors * blocks
    skipped = early_count(len(piece_refs)) * (pairs_ref.shape[0] // len(piece_refs))
    listed = late_ref[items]
    merge(piece_refs, pairs_ref)

    def store(slot, item):
        return pltpu.make_async_copy(out_ref.at[slot], out_hbm.at[item // blocks, item % blocks], sems.at[slot])

    def group(g, carry):
        for u in range(GROUP):
            slot = g * GROUP + u
            item = late_ref[jnp.minimum(slot, listed - 1)]
            pair = pairs_ref[(code_ref[item] >> 1) - skipped]
            out_ref[slot] = times_operator(half_ref[item // blocks, item % blocks], pair)
        for u in range(GROUP):
            slot = g * GROUP + u

            @pl.when(slot < listed)
            def _():
                store(slot, late_ref[slot]).start()
        return carry

    def drain(slot, carry):
        store(slot, 0).wait()
        return carry

    lax.fori_loop(0, (listed + GROUP - 1) // GROUP, group, 0)
    lax.fori_loop(0, listed, drain, 0)


def early_count(late_count):
    return 3 * late_count


def swap(piece, bit):
    count = lax.axis_size("sec")
    return lax.ppermute(piece, "sec", [(i, i ^ bit) for i in range(count)])


def exchange(pairs, half_of):
    pieces = {0: pairs}
    half = None
    bit = lax.axis_size("sec") // 2
    while bit:
        if half is None and len(pieces) > 1:
            top = max(pieces)
            pieces[top], half = lax.optimization_barrier((pieces[top], half_of()))
        for r in list(pieces):
            if bit > 1 or r < max(pieces):
                pieces[r | bit] = swap(pieces[r], bit)
        bit //= 2
    return pieces, half


def per_device(
    psi, left_ops, right_ops, dims_left, dims_right, right_owner, right_slot, term_active
):
    left_count, block_count, tile, width = psi.shape
    items = left_count * block_count
    pair_count = right_ops.shape[0] // 2
    count = lax.axis_size("sec")
    flops = 2 * psi.size * tile
    smem = pl.BlockSpec(memory_space=pltpu.SMEM)
    vmem = pl.BlockSpec(memory_space=pltpu.VMEM)
    hbm = pl.BlockSpec(memory_space=pltpu.HBM)
    params = pltpu.CompilerParams(vmem_limit_bytes=VMEM_LIMIT)

    pairs = pl.pallas_call(
        pack_kernel,
        out_shape=jax.ShapeDtypeStruct((pair_count, tile, 2 * tile), jnp.bfloat16),
        in_specs=[hbm, hbm],
        out_specs=vmem,
        scratch_shapes=[
            pltpu.SMEM(dims_right.shape, jnp.int32),
            pltpu.VMEM(right_ops.shape, jnp.bfloat16),
            pltpu.SemaphoreType.DMA((2,)),
        ],
        compiler_params=params,
        cost_estimate=pl.CostEstimate(flops=0, bytes_accessed=6 * right_ops.size, transcendentals=0),
    )(dims_right, right_ops)

    by_swaps = count in (8, 16, 32)
    if by_swaps:
        last = count - 4
        order = [r for r in range(count) if r < last and r != last - 1] + [last]
        order += [r for r in range(count) if r not in order]
        where = [order.index(r) for r in range(count)]
        place = lax.axis_index("sec") ^ right_owner
        at = jnp.zeros_like(place)
        for r in range(count):
            at = at + jnp.where(place == r, where[r], 0)
    else:
        at = right_owner
    code = at * pair_count + right_slot % pair_count
    code = (code * 2 + right_slot // pair_count).reshape(items)

    def half_of():
        return pl.pallas_call(
            left_kernel,
            out_shape=jax.ShapeDtypeStruct((left_count, block_count, tile, 2 * width), jnp.bfloat16),
            in_specs=[smem, smem, smem, vmem, vmem],
            out_specs=vmem,
            compiler_params=params,
            cost_estimate=pl.CostEstimate(flops=flops, bytes_accessed=6 * psi.size, transcendentals=0),
        )(dims_left, term_active.reshape(left_count, block_count), code, left_ops, psi)

    if by_swaps:
        pieces, half = exchange(pairs, half_of)
        split = early_count(count // 4)
        early = [pieces[r] for r in order[:split]]
    else:
        half = half_of()
        early = [lax.all_gather(pairs, "sec", axis=0, tiled=True)]

    sigma, listed = pl.pallas_call(
        early_kernel,
        out_shape=(
            jax.ShapeDtypeStruct(psi.shape, jnp.bfloat16),
            jax.ShapeDtypeStruct((items + 1,), jnp.int32),
        ),
        in_specs=[smem] + [vmem] * (1 + len(early)),
        out_specs=(hbm, smem),
        scratch_shapes=[
            pltpu.VMEM((sum(piece.shape[0] for piece in early), tile, 2 * tile), jnp.bfloat16),
            pltpu.VMEM(psi.shape, jnp.bfloat16),
            pltpu.SemaphoreType.DMA((left_count,)),
        ],
        compiler_params=params,
        cost_estimate=pl.CostEstimate(flops=flops, bytes_accessed=8 * psi.size, transcendentals=0),
    )(code, half, *early)
    if by_swaps:
        top = count - 2
        pieces[top], sigma = lax.optimization_barrier((pieces[top], sigma))
        pieces[top + 1] = swap(pieces[top], 1)
        late = [pieces[r] for r in order[split:]]
        sigma = pl.pallas_call(
            late_kernel,
            out_shape=jax.ShapeDtypeStruct(psi.shape, jnp.bfloat16),
            in_specs=[smem, smem, hbm] + [vmem] * (1 + len(late)),
            out_specs=hbm,
            scratch_shapes=[
                pltpu.VMEM((len(late) * pair_count, tile, 2 * tile), jnp.bfloat16),
                pltpu.VMEM((items + GROUP, tile, width), jnp.bfloat16),
                pltpu.SemaphoreType.DMA((items,)),
            ],
            input_output_aliases={2: 0},
            compiler_params=params,
            cost_estimate=pl.CostEstimate(flops=flops // 4, bytes_accessed=2 * psi.size, transcendentals=0),
        )(code, listed, sigma, half, *late)
    if lax.axis_size("op") > 1:
        sigma = lax.psum_scatter(sigma, "op", scatter_dimension=3, tiled=True)
    return sigma


def solution(mesh):
    placed = (
        P(("grp", "sec"), None, None, None),
        P(("grp", "sec"), None, "op"),
        P(("grp", "sec"), None, "op"),
        P(("grp", "sec")),
        P(("grp", "sec")),
        P(("grp", "sec"), None),
        P(("grp", "sec"), None),
        P(("grp", "sec"), None, "op"),
    )
    return jax.shard_map(
        per_device,
        mesh=mesh,
        in_specs=placed,
        out_specs=P(("grp", "sec"), None, None, "op"),
        check_vma=False,
    )
```

time: 36.6 us -> 34.7 us (0.948)
  starting transfers between devices: 15.2 us -> 11.4 us
  Pallas kernels: 7.46 us -> 10 us
  waiting for transfers between devices: 7.74 us -> 7.18 us
    ppermute x15, starting transfers between devices: 15.2 us -> 11.4 us  [swap(): return lax.ppermute(piece, 'sec', [(i, i ^ bit) for i in range(count)])]
    pallas_call x2 -> x3, Pallas kernels: 6.78 us -> 9.33 us  [the longest x1 4.49 us: per_device(): pl.pallas_call(early_kernel, out_shape=(jax.ShapeDtypeStruct(psi.shape, j...]
    ppermute x15, waiting for transfers between devices: 7.74 us -> 7.18 us  [swap(): return lax.ppermute(piece, 'sec', [(i, i ^ bit) for i in range(count)])]
  transfers between devices with their start and end apart: 15 -> 15, of which waited for: 5 -> 4; matrix products, arithmetic and copies ran while one was open for 2% -> 2% of each run, Pallas kernels for 8% -> 19%
where the time goes in v4:
time: 34.7 us; the launch traced here: 34.5 us
  starting transfers between devices  11.4 us (33%)
  Pallas kernels  10 us (29%)
  waiting for transfers between devices  7.18 us (21%)
  local copies, waits for them, and re-layouts  5.16 us (15%)
  other arithmetic  0.73 us (2%)
    ppermute x15, starting transfers between devices, swap(): return lax.ppermute(piece, 'sec', [(i, i ^ bit) for i in range(count)])  11.4 us
    ppermute x15, waiting for transfers between devices, swap(): return lax.ppermute(piece, 'sec', [(i, i ^ bit) for i in range(count)])  7.18 us
    unnamed x12, local copies, waits for them, and re-layouts  5.08 us
    pallas_call x1, Pallas kernels, per_device(): pl.pallas_call(early_kernel, out_shape=(jax.ShapeDtypeStruct(psi.shape, j...  4.49 us
    pallas_call x1, Pallas kernels, per_device(): pl.pallas_call(late_kernel, out_shape=jax.ShapeDtypeStruct(psi.shape, jnp...  2.84 us
    pallas_call x1, Pallas kernels, half_of(): pl.pallas_call(left_kernel, out_shape=jax.ShapeDtypeStruct((left_count, b...  2 us
    add x1, other arithmetic, per_device(): code = (code * 2 + right_slot // pair_count).reshape(items)  0.73 us
  transfers between devices with their start and end apart: 15, of which 4 were waited for; matrix products, arithmetic and copies ran while one was open for 2% of the time, Pallas kernels for 19%

profile of v4, /device:TPU:0, one launch (start us, length us, event | category | flops | bytes accessed | tf_op | source)
XLA Modules:
  0.0 34.5 jit_solution(9632583686884956303)
XLA Ops:
  0.0 0.0 copy-start.1
  0.0 0.9 %copy-done.1 = bf16[16,64,64]{2,1,0:T(8,128)(2,1)S(1)} copy-done((bf16[16,64,64]{2,1,0:T(8,128)(2,1)S(1)}, bf16[16,64,64]{2,1,0:T(8,128)(2,1)}, u32[]{:S(2)}) %copy-start.1) | copy-done | bytes 131096
  1.0 0.0 copy-start.4
  1.0 0.7 %copy-done.4 = s32[16]{0:T(128)S(1)} copy-done((s32[16]{0:T(128)S(1)}, s32[16]{0:T(128)}, u32[]{:S(2)}) %copy-start.4) | copy-done | bytes 88
  1.6 0.7 %shard_map.82.refs_0_ = bf16[8,64,128]{2,1,0:T(8,128)(2,1)S(1)} custom-call(s32[16]{0:T(128)S(1)} %copy-done.4, bf16[16,64,64]{2,1,0:T(8,128)(2,1)S(1)} %copy-done.1), custom_call_target="tpu_custom_call" | custom-call | bytes 393216 | tf_op jit(solution)/shard_map/pallas_call | solution.py:168
  2.3 4.1 %collective-permute-start = (bf16[8,64,128]{2,1,0:T(8,128)(2,1)S(1)}, bf16[8,64,128]{2,1,0:T(8,128)(2,1)S(1)}, u32[]{:S(2)}, u32[]{:S(2)}) collective-permute-start(bf16[8,64,128]{2,1,0:T(8,128)(2,1)S(1)} %shard_map.82.refs_0_), channel_id=1, source_target_pairs={{0,8},{1,9},{2,10},{3,11},{4,12},{5,13},{6,14},{7,15},{8,0},{9,1},... | collective-permute-start | bytes 393224 | tf_op jit(solution)/shard_map/ppermute | solution.py:137
  6.4 1.6 %collective-permute-start.4 = (bf16[8,64,128]{2,1,0:T(8,128)(2,1)S(1)}, bf16[8,64,128]{2,1,0:T(8,128)(2,1)S(1)}, u32[]{:S(2)}, u32[]{:S(2)}) collective-permute-start(bf16[8,64,128]{2,1,0:T(8,128)(2,1)S(1)} %shard_map.82.refs_0_), channel_id=1, source_target_pairs={{0,4},{1,5},{2,6},{3,7},{4,0},{5,1},{6,2},{7,3},{8,12},{9,13},{10,... | collective-permute-start | bytes 393224 | tf_op jit(solution)/shard_map/ppermute | solution.py:137
  8.0 1.5 %collective-permute-start.2 = (bf16[8,64,128]{2,1,0:T(8,128)(2,1)S(1)}, bf16[8,64,128]{2,1,0:T(8,128)(2,1)S(1)}, u32[]{:S(2)}, u32[]{:S(2)}) collective-permute-start(bf16[8,64,128]{2,1,0:T(8,128)(2,1)S(1)} %shard_map.82.refs_0_), channel_id=1, source_target_pairs={{0,2},{1,3},{2,0},{3,1},{4,6},{5,7},{6,4},{7,5},{8,10},{9,11},{10,... | collective-permute-start | bytes 393224 | tf_op jit(solution)/shard_map/ppermute | solution.py:137
  9.5 0.0 collective-permute-start.1
  9.5 0.7 %fusion.2 = s32[8,8]{1,0:T(8,128)S(1)} fusion(s32[8,8]{1,0:T(8,128)} %param.14, s32[8,8]{1,0:T(8,128)} %param.13, s32[]{:T(128)S(6)} %axis_index.12), kind=kLoop, calls=%fused_computation.7 | loop fusion | flops 4352 | bytes 772 | tf_op jit(solution)/shard_map/add | solution.py:195
  10.2 0.1 reshape.6.code_ref
  10.3 0.0 copy-start
  10.3 1.2 %copy-done = bf16[8,8,64,128]{3,2,1,0:T(8,128)(2,1)S(1)} copy-done((bf16[8,8,64,128]{3,2,1,0:T(8,128)(2,1)S(1)}, bf16[8,8,64,128]{3,2,1,0:T(8,128)(2,1)}, u32[]{:S(2)}) %copy-start) | copy-done | bytes 1048600
  11.5 0.0 copy-start.2
  11.5 0.9 %copy-done.2 = bf16[8,64,64]{2,1,0:T(8,128)(2,1)S(1)} copy-done((bf16[8,64,64]{2,1,0:T(8,128)(2,1)S(1)}, bf16[8,64,64]{2,1,0:T(8,128)(2,1)}, u32[]{:S(2)}) %copy-start.2) | copy-done | bytes 65560
  12.4 0.0 copy-start.3
  12.4 0.7 %copy-done.3 = s32[8,8,1]{1,2,0:T(1,128)S(1)} copy-done((s32[8,8,1]{1,2,0:T(1,128)S(1)}, s32[8,8,1]{1,2,0:T(1,128)}, u32[]{:S(2)}) %copy-start.3) | copy-done | bytes 280
  13.1 0.0 copy-start.5
  13.1 0.7 %copy-done.5 = s32[8]{0:T(128)S(1)} copy-done((s32[8]{0:T(128)S(1)}, s32[8]{0:T(128)}, u32[]{:S(2)}) %copy-start.5) | copy-done | bytes 56
  13.8 2.0 %shard_map.83.half_ref = bf16[8,8,64,256]{3,2,1,0:T(8,128)(2,1)S(1)} custom-call(s32[8]{0:T(128)S(1)} %copy-done.5, s32[8,8]{1,0:T(8,128)S(1)} %bitcast.1, s32[64]{0:T(128)S(1)} %reshape.6.code_ref, bf16[8,64,64]{2,1,0:T(8,128)(2,1)S(1)} %copy-done.2, bf16[8,8,64,128]{3,2,1,0:T(8,128)(2,1)S(1)} %copy-done), custom_call_target="tpu_custom_call" | custom-call | flops 67108864 | bytes 3145728 | tf_op jit(solution)/shard_map/pallas_call | solution.py:198
  15.8 0.0 collective-permute-done.refs_8_
  15.8 0.5 %collective-permute-start.10 = (bf16[8,64,128]{2,1,0:T(8,128)(2,1)S(1)}, bf16[8,64,128]{2,1,0:T(8,128)(2,1)S(1)}, u32[]{:S(2)}, u32[]{:S(2)}) collective-permute-start(bf16[8,64,128]{2,1,0:T(8,128)(2,1)S(1)} %collective-permute-done.refs_8_), channel_id=1, source_target_pairs={{0,4},{1,5},{2,6},{3,7},{4,0},{5,1},{6,2},{7,3},{8,12},{9,13},{10,... | collective-permute-start | bytes 393224 | tf_op jit(solution)/shard_map/ppermute | solution.py:137
  16.3 0.0 collective-permute-done.4.refs_4_
  16.3 0.5 %collective-permute-start.6 = (bf16[8,64,128]{2,1,0:T(8,128)(2,1)S(1)}, bf16[8,64,128]{2,1,0:T(8,128)(2,1)S(1)}, u32[]{:S(2)}, u32[]{:S(2)}) collective-permute-start(bf16[8,64,128]{2,1,0:T(8,128)(2,1)S(1)} %collective-permute-done.4.refs_4_), channel_id=1, source_target_pairs={{0,2},{1,3},{2,0},{3,1},{4,6},{5,7},{6,4},{7,5},{8,10},{9,11},{10,... | collective-permute-start | bytes 393224 | tf_op jit(solution)/shard_map/ppermute | solution.py:137
  16.8 1.5 %collective-permute-start.9 = (bf16[8,64,128]{2,1,0:T(8,128)(2,1)S(1)}, bf16[8,64,128]{2,1,0:T(8,128)(2,1)S(1)}, u32[]{:S(2)}, u32[]{:S(2)}) collective-permute-start(bf16[8,64,128]{2,1,0:T(8,128)(2,1)S(1)} %collective-permute-done.refs_8_), channel_id=1, source_target_pairs={{0,2},{1,3},{2,0},{3,1},{4,6},{5,7},{6,4},{7,5},{8,10},{9,11},{10,... | collective-permute-start | bytes 393224 | tf_op jit(solution)/shard_map/ppermute | solution.py:137
  18.3 0.0 collective-permute-done.2.refs_2_
  18.3 0.0 collective-permute-start.8
  18.3 0.0 collective-permute-done.1.refs_1_
  18.3 0.5 %collective-permute-start.5 = (bf16[8,64,128]{2,1,0:T(8,128)(2,1)S(1)}, bf16[8,64,128]{2,1,0:T(8,128)(2,1)S(1)}, u32[]{:S(2)}, u32[]{:S(2)}) collective-permute-start(bf16[8,64,128]{2,1,0:T(8,128)(2,1)S(1)} %collective-permute-done.4.refs_4_), channel_id=1, source_target_pairs={{0,1},{1,0},{2,3},{3,2},{4,5},{5,4},{6,7},{7,6},{8,9},{9,8},{10,11... | collective-permute-start | bytes 393224 | tf_op jit(solution)/shard_map/ppermute | solution.py:137
  18.8 2.9 %collective-permute-done.10.refs_11_ = bf16[8,64,128]{2,1,0:T(8,128)(2,1)S(1)} collective-permute-done((bf16[8,64,128]{2,1,0:T(8,128)(2,1)S(1)}, bf16[8,64,128]{2,1,0:T(8,128)(2,1)S(1)}, u32[]{:S(2)}, u32[]{:S(2)}) %collective-permute-start.10) | collective-permute-done | bytes 131104 | tf_op jit(solution)/shard_map/ppermute | solution.py:137
  21.7 0.0 collective-permute-start.3
  21.7 0.9 %collective-permute-done.6.refs_6_ = bf16[8,64,128]{2,1,0:T(8,128)(2,1)S(1)} collective-permute-done((bf16[8,64,128]{2,1,0:T(8,128)(2,1)S(1)}, bf16[8,64,128]{2,1,0:T(8,128)(2,1)S(1)}, u32[]{:S(2)}, u32[]{:S(2)}) %collective-permute-start.6) | collective-permute-done | bytes 131104 | tf_op jit(solution)/shard_map/ppermute | solution.py:137
  22.6 0.0 collective-permute-start.7
  22.6 2.1 %collective-permute-done.9.refs_10_ = bf16[8,64,128]{2,1,0:T(8,128)(2,1)S(1)} collective-permute-done((bf16[8,64,128]{2,1,0:T(8,128)(2,1)S(1)}, bf16[8,64,128]{2,1,0:T(8,128)(2,1)S(1)}, u32[]{:S(2)}, u32[]{:S(2)}) %collective-permute-start.9) | collective-permute-done | bytes 131104 | tf_op jit(solution)/shard_map/ppermute | solution.py:137
  24.7 0.5 %collective-permute-start.11 = (bf16[8,64,128]{2,1,0:T(8,128)(2,1)S(1)}, bf16[8,64,128]{2,1,0:T(8,128)(2,1)S(1)}, u32[]{:S(2)}, u32[]{:S(2)}) collective-permute-start(bf16[8,64,128]{2,1,0:T(8,128)(2,1)S(1)} %collective-permute-done.10.refs_11_), channel_id=1, source_target_pairs={{0,2},{1,3},{2,0},{3,1},{4,6},{5,7},{6,4},{7,5},{8,10},{9,11},{10,... | collective-permute-start | bytes 393224 | tf_op jit(solution)/shard_map/ppermute | solution.py:137
  25.3 0.0 collective-permute-done.8.refs_9_
  25.3 0.0 collective-permute-start.13
  25.3 0.0 collective-permute-done.5.refs_5_
  25.3 0.5 %collective-permute-start.12 = (bf16[8,64,128]{2,1,0:T(8,128)(2,1)S(1)}, bf16[8,64,128]{2,1,0:T(8,128)(2,1)S(1)}, u32[]{:S(2)}, u32[]{:S(2)}) collective-permute-start(bf16[8,64,128]{2,1,0:T(8,128)(2,1)S(1)} %collective-permute-done.9.refs_10_), channel_id=1, source_target_pairs={{0,1},{1,0},{2,3},{3,2},{4,5},{5,4},{6,7},{7,6},{8,9},{9,8},{10,11... | collective-permute-start | bytes 393224 | tf_op jit(solution)/shard_map/ppermute | solution.py:137
  25.8 0.0 collective-permute-done.3.refs_3_
  25.8 0.0 collective-permute-done.7.refs_7_
  25.8 4.5 %shard_map.84 = (bf16[8,8,64,128]{3,2,1,0:T(8,128)(2,1)}, s32[65]{0:T(128)S(1)}) custom-call(s32[64]{0:T(128)S(1)} %reshape.6.code_ref, bf16[8,8,64,256]{3,2,1,0:T(8,128)(2,1)S(1)} %shard_map.83.half_ref, bf16[8,64,128]{2,1,0:T(8,128)(2,1)S(1)} %shard_map.82.refs_0_, bf16[8,64,128]{2,1,0:T(8,128)(2,1)S(1)} %collective-permute-done.1.refs_1_, ...), custom_call_target="tpu_custom_call" | custom-call | flops 67108864 | bytes 4194304 | tf_op jit(solution)/shard_map/pallas_call | solution.py:215
  30.3 0.0 collective-permute-done.11.refs_2_
  30.3 0.1 collective-permute-start.14
  30.4 0.0 collective-permute-done.13.refs_1_
  30.4 0.0 collective-permute-done.12.refs_0_
  30.4 1.3 %collective-permute-done.14.refs_3_ = bf16[8,64,128]{2,1,0:T(8,128)(2,1)S(1)} collective-permute-done((bf16[8,64,128]{2,1,0:T(8,128)(2,1)S(1)}, bf16[8,64,128]{2,1,0:T(8,128)(2,1)S(1)}, u32[]{:S(2)}, u32[]{:S(2)}) %collective-permute-start.14) | collective-permute-done | bytes 131104 | tf_op jit(solution)/shard_map/ppermute | solution.py:137
  31.7 2.8 %shard_map.85 = bf16[8,8,64,128]{3,2,1,0:T(8,128)(2,1)} custom-call(s32[64]{0:T(128)S(1)} %reshape.6.code_ref, s32[65]{0:T(128)S(1)} %get-tuple-element.13.late_ref, bf16[8,8,64,128]{3,2,1,0:T(8,128)(2,1)} %get-tuple-element.15.early_hbm, bf16[8,8,64,256]{3,2,1,0:T(8,128)(2,1)S(1)} %shard_map.83.half_ref, ...), custom_call_target="tpu_custom_call", output_to_operand_aliasing={{}: (2, {})} | custom-call | flops 16777216 | bytes 1048576 | tf_op jit(solution)/shard_map/pallas_call | solution.py:236
Async XLA Ops:
  0.0 0.9 %copy-start.1 = (bf16[16,64,64]{2,1,0:T(8,128)(2,1)S(1)}, bf16[16,64,64]{2,1,0:T(8,128)(2,1)}, u32[]{:S(2)}) copy-start(bf16[16,64,64]{2,1,0:T(8,128)(2,1)} %right_hbm.1) | copy-start | bytes 393220
  1.0 0.7 %copy-start.4 = (s32[16]{0:T(128)S(1)}, s32[16]{0:T(128)}, u32[]{:S(2)}) copy-start(s32[16]{0:T(128)} %dims_hbm.1) | copy-start | bytes 196
  2.3 13.5 %collective-permute-start = (bf16[8,64,128]{2,1,0:T(8,128)(2,1)S(1)}, bf16[8,64,128]{2,1,0:T(8,128)(2,1)S(1)}, u32[]{:S(2)}, u32[]{:S(2)}) collective-permute-start(bf16[8,64,128]{2,1,0:T(8,128)(2,1)S(1)} %shard_map.82.refs_0_), channel_id=1, source_target_pairs={{0,8},{1,9},{2,10},{3,11},{4,12},{5,13},{6,14},{7,15},{8,0},{9,1},... | collective-permute-start | bytes 393224 | tf_op jit(solution)/shard_map/ppermute | solution.py:137
  6.4 9.9 %collective-permute-start.4 = (bf16[8,64,128]{2,1,0:T(8,128)(2,1)S(1)}, bf16[8,64,128]{2,1,0:T(8,128)(2,1)S(1)}, u32[]{:S(2)}, u32[]{:S(2)}) collective-permute-start(bf16[8,64,128]{2,1,0:T(8,128)(2,1)S(1)} %shard_map.82.refs_0_), channel_id=1, source_target_pairs={{0,4},{1,5},{2,6},{3,7},{4,0},{5,1},{6,2},{7,3},{8,12},{9,13},{10,... | collective-permute-start | bytes 393224 | tf_op jit(solution)/shard_map/ppermute | solution.py:137
  8.0 10.3 %collective-permute-start.2 = (bf16[8,64,128]{2,1,0:T(8,128)(2,1)S(1)}, bf16[8,64,128]{2,1,0:T(8,128)(2,1)S(1)}, u32[]{:S(2)}, u32[]{:S(2)}) collective-permute-start(bf16[8,64,128]{2,1,0:T(8,128)(2,1)S(1)} %shard_map.82.refs_0_), channel_id=1, source_target_pairs={{0,2},{1,3},{2,0},{3,1},{4,6},{5,7},{6,4},{7,5},{8,10},{9,11},{10,... | collective-permute-start | bytes 393224 | tf_op jit(solution)/shard_map/ppermute | solution.py:137
  9.5 8.9 %collective-permute-start.1 = (bf16[8,64,128]{2,1,0:T(8,128)(2,1)S(1)}, bf16[8,64,128]{2,1,0:T(8,128)(2,1)S(1)}, u32[]{:S(2)}, u32[]{:S(2)}) collective-permute-start(bf16[8,64,128]{2,1,0:T(8,128)(2,1)S(1)} %shard_map.82.refs_0_), channel_id=1, source_target_pairs={{0,1},{1,0},{2,3},{3,2},{4,5},{5,4},{6,7},{7,6},{8,9},{9,8},{10,11... | collective-permute-start | bytes 393224 | tf_op jit(solution)/shard_map/ppermute | solution.py:137
  10.3 1.2 %copy-start = (bf16[8,8,64,128]{3,2,1,0:T(8,128)(2,1)S(1)}, bf16[8,8,64,128]{3,2,1,0:T(8,128)(2,1)}, u32[]{:S(2)}) copy-start(bf16[8,8,64,128]{3,2,1,0:T(8,128)(2,1)} %psi_ref.1) | copy-start | bytes 3145732
  11.5 0.9 %copy-start.2 = (bf16[8,64,64]{2,1,0:T(8,128)(2,1)S(1)}, bf16[8,64,64]{2,1,0:T(8,128)(2,1)}, u32[]{:S(2)}) copy-start(bf16[8,64,64]{2,1,0:T(8,128)(2,1)} %left_ref.1) | copy-start | bytes 196612
  12.4 0.7 %copy-start.3 = (s32[8,8,1]{1,2,0:T(1,128)S(1)}, s32[8,8,1]{1,2,0:T(1,128)}, u32[]{:S(2)}) copy-start(s32[8,8,1]{1,2,0:T(1,128)} %param.15) | copy-start | bytes 772
  13.1 0.7 %copy-start.5 = (s32[8]{0:T(128)S(1)}, s32[8]{0:T(128)}, u32[]{:S(2)}) copy-start(s32[8]{0:T(128)} %dims_ref.1) | copy-start | bytes 100
  15.8 6.0 %collective-permute-start.10 = (bf16[8,64,128]{2,1,0:T(8,128)(2,1)S(1)}, bf16[8,64,128]{2,1,0:T(8,128)(2,1)S(1)}, u32[]{:S(2)}, u32[]{:S(2)}) collective-permute-start(bf16[8,64,128]{2,1,0:T(8,128)(2,1)S(1)} %collective-permute-done.refs_8_), channel_id=1, source_target_pairs={{0,4},{1,5},{2,6},{3,7},{4,0},{5,1},{6,2},{7,3},{8,12},{9,13},{10,... | collective-permute-start | bytes 393224 | tf_op jit(solution)/shard_map/ppermute | solution.py:137
  16.3 6.3 %collective-permute-start.6 = (bf16[8,64,128]{2,1,0:T(8,128)(2,1)S(1)}, bf16[8,64,128]{2,1,0:T(8,128)(2,1)S(1)}, u32[]{:S(2)}, u32[]{:S(2)}) collective-permute-start(bf16[8,64,128]{2,1,0:T(8,128)(2,1)S(1)} %collective-permute-done.4.refs_4_), channel_id=1, source_target_pairs={{0,2},{1,3},{2,0},{3,1},{4,6},{5,7},{6,4},{7,5},{8,10},{9,11},{10,... | collective-permute-start | bytes 393224 | tf_op jit(solution)/shard_map/ppermute | solution.py:137
  16.8 7.9 %collective-permute-start.9 = (bf16[8,64,128]{2,1,0:T(8,128)(2,1)S(1)}, bf16[8,64,128]{2,1,0:T(8,128)(2,1)S(1)}, u32[]{:S(2)}, u32[]{:S(2)}) collective-permute-start(bf16[8,64,128]{2,1,0:T(8,128)(2,1)S(1)} %collective-permute-done.refs_8_), channel_id=1, source_target_pairs={{0,2},{1,3},{2,0},{3,1},{4,6},{5,7},{6,4},{7,5},{8,10},{9,11},{10,... | collective-permute-start | bytes 393224 | tf_op jit(solution)/shard_map/ppermute | solution.py:137
  18.3 6.9 %collective-permute-start.8 = (bf16[8,64,128]{2,1,0:T(8,128)(2,1)S(1)}, bf16[8,64,128]{2,1,0:T(8,128)(2,1)S(1)}, u32[]{:S(2)}, u32[]{:S(2)}) collective-permute-start(bf16[8,64,128]{2,1,0:T(8,128)(2,1)S(1)} %collective-permute-done.refs_8_), channel_id=1, source_target_pairs={{0,1},{1,0},{2,3},{3,2},{4,5},{5,4},{6,7},{7,6},{8,9},{9,8},{10,11... | collective-permute-start | bytes 393224 | tf_op jit(solution)/shard_map/ppermute | solution.py:137
  18.3 6.9 %collective-permute-start.5 = (bf16[8,64,128]{2,1,0:T(8,128)(2,1)S(1)}, bf16[8,64,128]{2,1,0:T(8,128)(2,1)S(1)}, u32[]{:S(2)}, u32[]{:S(2)}) collective-permute-start(bf16[8,64,128]{2,1,0:T(8,128)(2,1)S(1)} %collective-permute-done.4.refs_4_), channel_id=1, source_target_pairs={{0,1},{1,0},{2,3},{3,2},{4,5},{5,4},{6,7},{7,6},{8,9},{9,8},{10,11... | collective-permute-start | bytes 393224 | tf_op jit(solution)/shard_map/ppermute | solution.py:137
  21.7 4.1 %collective-permute-start.3 = (bf16[8,64,128]{2,1,0:T(8,128)(2,1)S(1)}, bf16[8,64,128]{2,1,0:T(8,128)(2,1)S(1)}, u32[]{:S(2)}, u32[]{:S(2)}) collective-permute-start(bf16[8,64,128]{2,1,0:T(8,128)(2,1)S(1)} %collective-permute-done.2.refs_2_), channel_id=1, source_target_pairs={{0,1},{1,0},{2,3},{3,2},{4,5},{5,4},{6,7},{7,6},{8,9},{9,8},{10,11... | collective-permute-start | bytes 393224 | tf_op jit(solution)/shard_map/ppermute | solution.py:137
  22.6 3.2 %collective-permute-start.7 = (bf16[8,64,128]{2,1,0:T(8,128)(2,1)S(1)}, bf16[8,64,128]{2,1,0:T(8,128)(2,1)S(1)}, u32[]{:S(2)}, u32[]{:S(2)}) collective-permute-start(bf16[8,64,128]{2,1,0:T(8,128)(2,1)S(1)} %collective-permute-done.6.refs_6_), channel_id=1, source_target_pairs={{0,1},{1,0},{2,3},{3,2},{4,5},{5,4},{6,7},{7,6},{8,9},{9,8},{10,11... | collective-permute-start | bytes 393224 | tf_op jit(solution)/shard_map/ppermute | solution.py:137
  24.7 5.6 %collective-permute-start.11 = (bf16[8,64,128]{2,1,0:T(8,128)(2,1)S(1)}, bf16[8,64,128]{2,1,0:T(8,128)(2,1)S(1)}, u32[]{:S(2)}, u32[]{:S(2)}) collective-permute-start(bf16[8,64,128]{2,1,0:T(8,128)(2,1)S(1)} %collective-permute-done.10.refs_11_), channel_id=1, source_target_pairs={{0,2},{1,3},{2,0},{3,1},{4,6},{5,7},{6,4},{7,5},{8,10},{9,11},{10,... | collective-permute-start | bytes 393224 | tf_op jit(solution)/shard_map/ppermute | solution.py:137
  25.3 5.2 %collective-permute-start.13 = (bf16[8,64,128]{2,1,0:T(8,128)(2,1)S(1)}, bf16[8,64,128]{2,1,0:T(8,128)(2,1)S(1)}, u32[]{:S(2)}, u32[]{:S(2)}) collective-permute-start(bf16[8,64,128]{2,1,0:T(8,128)(2,1)S(1)} %collective-permute-done.10.refs_11_), channel_id=1, source_target_pairs={{0,1},{1,0},{2,3},{3,2},{4,5},{5,4},{6,7},{7,6},{8,9},{9,8},{10,11... | collective-permute-start | bytes 393224 | tf_op jit(solution)/shard_map/ppermute | solution.py:137
  25.3 5.2 %collective-permute-start.12 = (bf16[8,64,128]{2,1,0:T(8,128)(2,1)S(1)}, bf16[8,64,128]{2,1,0:T(8,128)(2,1)S(1)}, u32[]{:S(2)}, u32[]{:S(2)}) collective-permute-start(bf16[8,64,128]{2,1,0:T(8,128)(2,1)S(1)} %collective-permute-done.9.refs_10_), channel_id=1, source_target_pairs={{0,1},{1,0},{2,3},{3,2},{4,5},{5,4},{6,7},{7,6},{8,9},{9,8},{10,11... | collective-permute-start | bytes 393224 | tf_op jit(solution)/shard_map/ppermute | solution.py:137
  30.3 1.4 %collective-permute-start.14 = (bf16[8,64,128]{2,1,0:T(8,128)(2,1)S(1)}, bf16[8,64,128]{2,1,0:T(8,128)(2,1)S(1)}, u32[]{:S(2)}, u32[]{:S(2)}) collective-permute-start(bf16[8,64,128]{2,1,0:T(8,128)(2,1)S(1)} %collective-permute-done.11.refs_2_), channel_id=1, source_target_pairs={{0,1},{1,0},{2,3},{3,2},{4,5},{5,4},{6,7},{7,6},{8,9},{9,8},{10,11... | collective-permute-start | bytes 393224 | tf_op jit(solution)/shard_map/ppermute | solution.py:137

commit v5 on v4

v5 whole, which is shorter than its diff:
```python
import functools

import jax
import jax.numpy as jnp
from jax import lax
from jax.experimental import pallas as pl
from jax.experimental.pallas import tpu as pltpu
from jax.sharding import PartitionSpec as P

VMEM_LIMIT = 48 * 1024 * 1024
GROUP = 4
FAR, NEAR, CROSS, CORE = 8, 4, 2, 1
EARLY = (0, CORE, NEAR, NEAR | CORE, CROSS, CROSS | CORE, FAR, NEAR | CROSS, NEAR | CROSS | CORE, FAR | NEAR)
LATE = tuple(r for r in range(16) if r not in EARLY)
ORDER = EARLY + LATE


def load_all(*copies):
    copies = [pltpu.make_async_copy(*copy) for copy in copies]
    for copy in copies:
        copy.start()
    return copies


def pack_kernel(dims_hbm, right_hbm, pairs_ref, dims_ref, right_ref, sems):
    count, tile, width = pairs_ref.shape
    copies = load_all((dims_hbm, dims_ref, sems.at[0]), (right_hbm, right_ref, sems.at[1]))
    rows = lax.broadcasted_iota(jnp.int32, (tile, tile), 0)
    cols = lax.broadcasted_iota(jnp.int32, (tile, tile), 1)
    most = jnp.maximum(rows, cols)
    for copy in copies:
        copy.wait()

    def kept(b):
        return jnp.where(most < dims_ref[b], right_ref[b].astype(jnp.float32), 0.0)

    for p in range(count):
        both = jnp.concatenate([kept(p), kept(p + count)], axis=1)
        pairs_ref[p] = both.astype(jnp.bfloat16)


def left_kernel(
    pair_count, dims_hbm, active_hbm, slot_hbm, left_hbm, psi_hbm,
    half_ref, dims_ref, active_ref, slot_ref, left_ref, psi_ref, sems, psi_sems,
):
    sectors, blocks, tile, width = psi_ref.shape
    copies = load_all(
        (dims_hbm, dims_ref, sems.at[0]),
        (active_hbm, active_ref, sems.at[1]),
        (slot_hbm, slot_ref, sems.at[2]),
        (left_hbm, left_ref, sems.at[3]),
    )
    psi_copies = load_all(*[(psi_hbm.at[a], psi_ref.at[a], psi_sems.at[a]) for a in range(sectors)])
    rows = lax.broadcasted_iota(jnp.int32, (tile, tile), 0)
    cols = lax.broadcasted_iota(jnp.int32, (tile, tile), 1)
    most = jnp.maximum(rows, cols)
    upper = (lax.broadcasted_iota(jnp.int32, (tile, width), 1) >= tile).astype(jnp.int32)
    for copy in copies:
        copy.wait()
    for a in range(sectors):
        psi_copies[a].wait()
        op = jnp.where(most < dims_ref[a], left_ref[a].astype(jnp.float32), 0.0).astype(jnp.bfloat16)
        for k in range(blocks):
            part = jnp.dot(op, psi_ref[a, k], preferred_element_type=jnp.float32)
            part = part * active_ref[a, k].astype(jnp.float32)
            other = pltpu.roll(part, tile, 1)
            here = upper == (slot_ref[a, k] >= pair_count).astype(jnp.int32)
            first = jnp.where(upper == 0, part, other)
            last = jnp.where(upper == 0, other, part)
            half_ref[a, k, :, :width] = jnp.where(here, first, 0.0).astype(jnp.bfloat16)
            half_ref[a, k, :, width:] = jnp.where(here, last, 0.0).astype(jnp.bfloat16)


def times_operator(half, pair):
    zero = jnp.zeros_like(pair)
    top = jnp.concatenate([pair, zero], axis=1)
    low = jnp.concatenate([zero, pair], axis=1)
    both = jnp.concatenate([top, low], axis=0)
    part = lax.dot_general(half, both, (((1,), (1,)), ((), ())), preferred_element_type=jnp.float32)
    return part.astype(jnp.bfloat16)


def merge(piece_refs, pairs_ref):
    at = 0
    for piece in piece_refs:
        pairs_ref[at:at + piece.shape[0]] = piece[...]
        at += piece.shape[0]


def piece_at(r):
    low = sum(ORDER.index(i) << (4 * i) for i in range(7))
    high = sum(ORDER.index(i + 8) << (4 * i) for i in range(7))
    packed = jnp.where(r < 8, low, high) >> (4 * (r & 7))
    end = jnp.where(r < 8, ORDER.index(7), ORDER.index(15))
    return jnp.where(r & 7 == 7, end, packed & 15)


def early_kernel(pair_count, owner_hbm, slot_hbm, half_ref, *refs):
    piece_refs = refs[:-7]
    out_hbm, late_ref, pairs_ref, out_ref, owner_ref, slot_ref, sems = refs[-7:]
    sectors, blocks, tile, width = out_ref.shape
    items, held = sectors * blocks, pairs_ref.shape[0]
    copies = load_all((owner_hbm, owner_ref, sems.at[0]), (slot_hbm, slot_ref, sems.at[1]))
    merge(piece_refs, pairs_ref)
    me = lax.axis_index("sec")
    for copy in copies:
        copy.wait()

    def store(a):
        return pltpu.make_async_copy(out_ref.at[a], out_hbm.at[a], sems.at[a])

    def one(a, listed):
        for k in range(blocks):
            owner, slot = owner_ref[a, k], slot_ref[a, k]
            at = piece_at(owner ^ me) if len(piece_refs) > 1 else owner
            at = at * pair_count + jnp.where(slot >= pair_count, slot - pair_count, slot)
            late = at >= held
            pair = pairs_ref[jnp.where(late, 0, at)]
            out_ref[a, k] = times_operator(half_ref[a, k], pair)
            late_ref[listed] = (at - held) * items + a * blocks + k
            listed = listed + late.astype(jnp.int32)
        store(a).start()
        return listed

    listed = lax.fori_loop(0, sectors, one, 0, unroll=2)
    late_ref[items] = listed
    for a in range(sectors):
        store(a).wait()


def late_kernel(late_ref, early_hbm, half_ref, *refs):
    piece_refs, (out_hbm, pairs_ref, out_ref, sems) = refs[:-4], refs[-4:]
    sectors, blocks, tile, width = half_ref.shape
    items = sectors * blocks
    listed = late_ref[items]
    merge(piece_refs, pairs_ref)

    def store(slot, item):
        return pltpu.make_async_copy(out_ref.at[slot], out_hbm.at[item // blocks, item % blocks], sems.at[slot])

    def group(g, carry):
        for u in range(GROUP):
            slot = g * GROUP + u
            entry = late_ref[jnp.minimum(slot, listed - 1)]
            item = entry % items
            out_ref[slot] = times_operator(half_ref[item // blocks, item % blocks], pairs_ref[entry // items])
        for u in range(GROUP):
            slot = g * GROUP + u

            @pl.when(slot < listed)
            def _():
                store(slot, late_ref[slot] % items).start()
        return carry

    def drain(slot, carry):
        store(slot, 0).wait()
        return carry

    lax.fori_loop(0, (listed + GROUP - 1) // GROUP, group, 0)
    lax.fori_loop(0, listed, drain, 0)


def swap(piece, bit):
    count = lax.axis_size("sec")
    return lax.ppermute(piece, "sec", [(i, i ^ bit) for i in range(count)])


def per_device(
    psi, left_ops, right_ops, dims_left, dims_right, right_owner, right_slot, term_active
):
    left_count, block_count, tile, width = psi.shape
    items = left_count * block_count
    pair_count = right_ops.shape[0] // 2
    count = lax.axis_size("sec")
    by_swaps = count == len(ORDER)
    flops = 2 * psi.size * tile
    smem = pl.BlockSpec(memory_space=pltpu.SMEM)
    vmem = pl.BlockSpec(memory_space=pltpu.VMEM)
    hbm = pl.BlockSpec(memory_space=pltpu.HBM)
    params = pltpu.CompilerParams(vmem_limit_bytes=VMEM_LIMIT)

    def in_hbm(*arrays):
        return [pltpu.with_memory_space_constraint(array, pltpu.HBM) for array in arrays]

    pairs = pl.pallas_call(
        pack_kernel,
        out_shape=jax.ShapeDtypeStruct((pair_count, tile, 2 * tile), jnp.bfloat16),
        in_specs=[hbm, hbm],
        out_specs=vmem,
        scratch_shapes=[
            pltpu.SMEM(dims_right.shape, jnp.int32),
            pltpu.VMEM(right_ops.shape, jnp.bfloat16),
            pltpu.SemaphoreType.DMA((2,)),
        ],
        compiler_params=params,
        cost_estimate=pl.CostEstimate(flops=0, bytes_accessed=2 * right_ops.size, transcendentals=0),
    )(*in_hbm(dims_right, right_ops))

    def half_of(dims_left):
        active = term_active.reshape(left_count, block_count)
        return pl.pallas_call(
            functools.partial(left_kernel, pair_count),
            out_shape=jax.ShapeDtypeStruct((left_count, block_count, tile, 2 * width), jnp.bfloat16),
            in_specs=[hbm] * 5,
            out_specs=vmem,
            scratch_shapes=[
                pltpu.SMEM(dims_left.shape, jnp.int32),
                pltpu.SMEM(active.shape, jnp.int32),
                pltpu.SMEM(right_slot.shape, jnp.int32),
                pltpu.VMEM(left_ops.shape, jnp.bfloat16),
                pltpu.VMEM(psi.shape, jnp.bfloat16),
                pltpu.SemaphoreType.DMA((4,)),
                pltpu.SemaphoreType.DMA((left_count,)),
            ],
            compiler_params=params,
            cost_estimate=pl.CostEstimate(flops=flops, bytes_accessed=2 * psi.size, transcendentals=0),
        )(*in_hbm(dims_left, active, right_slot, left_ops, psi))

    if by_swaps:
        pieces = {0: pairs}
        def pass_on(*pairs_of):
            for r, bit in pairs_of:
                pieces[r | bit] = swap(pieces[r], bit)

        pass_on((0, FAR), (0, NEAR))
        half, pieces[0] = lax.optimization_barrier((half_of(dims_left), pairs))
        pass_on((0, CROSS), (0, CORE), (NEAR, CORE), (CROSS, CORE), (NEAR, CROSS))
        pass_on((FAR, NEAR), (FAR, CROSS), (FAR | NEAR, CROSS), (NEAR | CROSS, CORE), (FAR | NEAR, CORE))
        early = [pieces[r] for r in EARLY]
    else:
        half = half_of(dims_left)
        early = [lax.all_gather(pairs, "sec", axis=0, tiled=True)]

    sigma, listed = pl.pallas_call(
        functools.partial(early_kernel, pair_count),
        out_shape=(
            jax.ShapeDtypeStruct(psi.shape, jnp.bfloat16),
            jax.ShapeDtypeStruct((items + 1,), jnp.int32),
        ),
        in_specs=[hbm, hbm] + [vmem] * (1 + len(early)),
        out_specs=(hbm, smem),
        scratch_shapes=[
            pltpu.VMEM((sum(piece.shape[0] for piece in early), tile, 2 * tile), jnp.bfloat16),
            pltpu.VMEM(psi.shape, jnp.bfloat16),
            pltpu.SMEM(right_owner.shape, jnp.int32),
            pltpu.SMEM(right_slot.shape, jnp.int32),
            pltpu.SemaphoreType.DMA((max(left_count, 2),)),
        ],
        compiler_params=params,
        cost_estimate=pl.CostEstimate(flops=flops, bytes_accessed=2 * psi.size, transcendentals=0),
    )(*in_hbm(right_owner, right_slot), half, *early)
    if by_swaps:
        ends = (FAR, FAR | CROSS, FAR | NEAR | CROSS)
        held, sigma = lax.optimization_barrier(([pieces[r] for r in ends], sigma))
        for r, piece in zip(ends, held):
            pieces[r], pieces[r | CORE] = piece, swap(piece, CORE)
        late = [pieces[r] for r in LATE]
        sigma = pl.pallas_call(
            late_kernel,
            out_shape=jax.ShapeDtypeStruct(psi.shape, jnp.bfloat16),
            in_specs=[smem, hbm] + [vmem] * (1 + len(late)),
            out_specs=hbm,
            scratch_shapes=[
                pltpu.VMEM((len(late) * pair_count, tile, 2 * tile), jnp.bfloat16),
                pltpu.VMEM((items + GROUP, tile, width), jnp.bfloat16),
                pltpu.SemaphoreType.DMA((items,)),
            ],
            input_output_aliases={1: 0},
            compiler_params=params,
            cost_estimate=pl.CostEstimate(flops=flops // 4, bytes_accessed=psi.size, transcendentals=0),
        )(listed, sigma, half, *late)
    if lax.axis_size("op") > 1:
        sigma = lax.psum_scatter(sigma, "op", scatter_dimension=3, tiled=True)
    return sigma


def solution(mesh):
    placed = (
        P(("grp", "sec"), None, None, None),
        P(("grp", "sec"), None, "op"),
        P(("grp", "sec"), None, "op"),
        P(("grp", "sec")),
        P(("grp", "sec")),
        P(("grp", "sec"), None),
        P(("grp", "sec"), None),
        P(("grp", "sec"), None, "op"),
    )
    return jax.shard_map(
        per_device,
        mesh=mesh,
        in_specs=placed,
        out_specs=P(("grp", "sec"), None, None, "op"),
        check_vma=False,
    )
```

time: 34.7 us -> 31.8 us (0.916)
  local copies, waits for them, and re-layouts: 5.16 us -> 0 us
  Pallas kernels: 10 us -> 12 us
  waiting for transfers between devices: 7.18 us -> 8.95 us
  other arithmetic: 0.73 us -> 0 us
  starting transfers between devices: 11.4 us -> 10.8 us
    unnamed x12 -> x0, local copies, waits for them, and re-layouts: 5.08 us -> none
    ppermute x15, waiting for transfers between devices: 7.18 us -> 8.95 us  [swap(): return lax.ppermute(piece, 'sec', [(i, i ^ bit) for i in range(count)])]
    pallas_call x2, Pallas kernels: 6.48 us -> 7.57 us  [the longest x1 4.06 us: per_device(): pl.pallas_call(functools.partial(early_kernel, pair_count), out_shape=(ja...]
    add x1 -> x0, other arithmetic: 0.73 us -> none  [per_device(): code = (code * 2 + right_slot // pair_count).reshape(items)]
    ppermute x15, starting transfers between devices: 11.4 us -> 10.8 us  [swap(): return lax.ppermute(piece, 'sec', [(i, i ^ bit) for i in range(count)])]
    pallas_call x1, Pallas kernels: 2.84 us -> 3.33 us  [per_device(): pl.pallas_call(late_kernel, out_shape=jax.ShapeDtypeStruct(psi.shape, jnp...]
    pallas_call x1, Pallas kernels: 0.68 us -> 1.08 us  [per_device(): pl.pallas_call(pack_kernel, out_shape=jax.ShapeDtypeStruct((pair_count, t...]
  transfers between devices with their start and end apart: 15 -> 15, of which waited for: 4 -> 8; matrix products, arithmetic and copies ran while one was open for 2% -> 0% of each run, Pallas kernels for 19% -> 24%
where the time goes in v5:
time: 31.8 us
  Pallas kernels  12 us (38%)
  starting transfers between devices  10.8 us (34%)
  waiting for transfers between devices  8.95 us (28%)
    ppermute x15, starting transfers between devices, swap(): return lax.ppermute(piece, 'sec', [(i, i ^ bit) for i in range(count)])  10.8 us
    ppermute x15, waiting for transfers between devices, swap(): return lax.ppermute(piece, 'sec', [(i, i ^ bit) for i in range(count)])  8.95 us
    pallas_call x1, Pallas kernels, per_device(): pl.pallas_call(functools.partial(early_kernel, pair_count), out_shape=(ja...  4.06 us
    pallas_call x1, Pallas kernels, half_of(): pl.pallas_call(functools.partial(left_kernel, pair_count), out_shape=jax....  3.52 us
    pallas_call x1, Pallas kernels, per_device(): pl.pallas_call(late_kernel, out_shape=jax.ShapeDtypeStruct(psi.shape, jnp...  3.33 us
    pallas_call x1, Pallas kernels, per_device(): pl.pallas_call(pack_kernel, out_shape=jax.ShapeDtypeStruct((pair_count, t...  1.08 us
  transfers between devices with their start and end apart: 15, of which 8 were waited for; matrix products, arithmetic and copies ran while one was open for 0% of the time, Pallas kernels for 24%

profile of v5, /device:TPU:0, one launch (start us, length us, event | category | flops | bytes accessed | tf_op | source)
XLA Modules:
  0.0 31.8 jit_solution(55181833501150823)
XLA Ops:
  0.0 1.1 %shard_map.83.refs_0_ = bf16[8,64,128]{2,1,0:T(8,128)(2,1)S(1)} custom-call(s32[16]{0:T(128)} %dims_hbm.3, bf16[16,64,64]{2,1,0:T(8,128)(2,1)} %right_hbm.1), custom_call_target="tpu_custom_call" | custom-call | bytes 131072 | tf_op jit(solution)/shard_map/pallas_call | solution.py:185
  1.1 3.1 %collective-permute-start.1 = (bf16[8,64,128]{2,1,0:T(8,128)(2,1)S(1)}, bf16[8,64,128]{2,1,0:T(8,128)(2,1)S(1)}, u32[]{:S(2)}, u32[]{:S(2)}) collective-permute-start(bf16[8,64,128]{2,1,0:T(8,128)(2,1)S(1)} %shard_map.83.refs_0_), channel_id=1, source_target_pairs={{0,4},{1,5},{2,6},{3,7},{4,0},{5,1},{6,2},{7,3},{8,12},{9,13},{10,... | collective-permute-start | bytes 393224 | tf_op jit(solution)/shard_map/ppermute | solution.py:165
  4.2 2.6 %collective-permute-start.5 = (bf16[8,64,128]{2,1,0:T(8,128)(2,1)S(1)}, bf16[8,64,128]{2,1,0:T(8,128)(2,1)S(1)}, u32[]{:S(2)}, u32[]{:S(2)}) collective-permute-start(bf16[8,64,128]{2,1,0:T(8,128)(2,1)S(1)} %shard_map.83.refs_0_), channel_id=1, source_target_pairs={{0,8},{1,9},{2,10},{3,11},{4,12},{5,13},{6,14},{7,15},{8,0},{9,1},... | collective-permute-start | bytes 393224 | tf_op jit(solution)/shard_map/ppermute | solution.py:165
  6.8 3.5 %shard_map.82.half_ref = bf16[8,8,64,256]{3,2,1,0:T(8,128)(2,1)S(1)} custom-call(s32[8]{0:T(128)} %dims_hbm.2, s32[8,8]{1,0:T(8,128)} %bitcast.1, s32[8,8]{1,0:T(8,128)} %slot_hbm.3, bf16[8,64,64]{2,1,0:T(8,128)(2,1)} %left_hbm.1, bf16[8,8,64,128]{3,2,1,0:T(8,128)(2,1)} %psi_hbm.1), custom_call_target="tpu_custom_call" | custom-call | flops 67108864 | bytes 1048576 | tf_op jit(solution)/shard_map/pallas_call | solution.py:201
  10.3 1.6 %collective-permute-start.3 = (bf16[8,64,128]{2,1,0:T(8,128)(2,1)S(1)}, bf16[8,64,128]{2,1,0:T(8,128)(2,1)S(1)}, u32[]{:S(2)}, u32[]{:S(2)}) collective-permute-start(bf16[8,64,128]{2,1,0:T(8,128)(2,1)S(1)} %shard_map.83.refs_0_), channel_id=1, source_target_pairs={{0,2},{1,3},{2,0},{3,1},{4,6},{5,7},{6,4},{7,5},{8,10},{9,11},{10,... | collective-permute-start | bytes 393224 | tf_op jit(solution)/shard_map/ppermute | solution.py:165
  11.8 0.0 collective-permute-done.1.refs_2_
  11.8 0.5 %collective-permute-start.6 = (bf16[8,64,128]{2,1,0:T(8,128)(2,1)S(1)}, bf16[8,64,128]{2,1,0:T(8,128)(2,1)S(1)}, u32[]{:S(2)}, u32[]{:S(2)}) collective-permute-start(bf16[8,64,128]{2,1,0:T(8,128)(2,1)S(1)} %collective-permute-done.1.refs_2_), channel_id=1, source_target_pairs={{0,2},{1,3},{2,0},{3,1},{4,6},{5,7},{6,4},{7,5},{8,10},{9,11},{10,... | collective-permute-start | bytes 393224 | tf_op jit(solution)/shard_map/ppermute | solution.py:165
  12.4 0.0 collective-permute-start
  12.4 0.5 %collective-permute-done.5.refs_6_ = bf16[8,64,128]{2,1,0:T(8,128)(2,1)S(1)} collective-permute-done((bf16[8,64,128]{2,1,0:T(8,128)(2,1)S(1)}, bf16[8,64,128]{2,1,0:T(8,128)(2,1)S(1)}, u32[]{:S(2)}, u32[]{:S(2)}) %collective-permute-start.5) | collective-permute-done | bytes 131104 | tf_op jit(solution)/shard_map/ppermute | solution.py:165
  12.9 0.4 %collective-permute-start.8 = (bf16[8,64,128]{2,1,0:T(8,128)(2,1)S(1)}, bf16[8,64,128]{2,1,0:T(8,128)(2,1)S(1)}, u32[]{:S(2)}, u32[]{:S(2)}) collective-permute-start(bf16[8,64,128]{2,1,0:T(8,128)(2,1)S(1)} %collective-permute-done.5.refs_6_), channel_id=1, source_target_pairs={{0,4},{1,5},{2,6},{3,7},{4,0},{5,1},{6,2},{7,3},{8,12},{9,13},{10,... | collective-permute-start | bytes 393224 | tf_op jit(solution)/shard_map/ppermute | solution.py:165
  13.3 0.0 collective-permute-start.2
  13.3 3.1 %collective-permute-done.3.refs_4_ = bf16[8,64,128]{2,1,0:T(8,128)(2,1)S(1)} collective-permute-done((bf16[8,64,128]{2,1,0:T(8,128)(2,1)S(1)}, bf16[8,64,128]{2,1,0:T(8,128)(2,1)S(1)}, u32[]{:S(2)}, u32[]{:S(2)}) %collective-permute-start.3) | collective-permute-done | bytes 131104 | tf_op jit(solution)/shard_map/ppermute | solution.py:165
  16.4 0.0 collective-permute-start.4
  16.4 1.4 %collective-permute-done.6.refs_7_ = bf16[8,64,128]{2,1,0:T(8,128)(2,1)S(1)} collective-permute-done((bf16[8,64,128]{2,1,0:T(8,128)(2,1)S(1)}, bf16[8,64,128]{2,1,0:T(8,128)(2,1)S(1)}, u32[]{:S(2)}, u32[]{:S(2)}) %collective-permute-start.6) | collective-permute-done | bytes 131104 | tf_op jit(solution)/shard_map/ppermute | solution.py:165
  17.8 0.0 collective-permute-start.7
  17.8 0.0 collective-permute-done.refs_1_
  17.8 1.5 %collective-permute-start.9 = (bf16[8,64,128]{2,1,0:T(8,128)(2,1)S(1)}, bf16[8,64,128]{2,1,0:T(8,128)(2,1)S(1)}, u32[]{:S(2)}, u32[]{:S(2)}) collective-permute-start(bf16[8,64,128]{2,1,0:T(8,128)(2,1)S(1)} %collective-permute-done.5.refs_6_), channel_id=1, source_target_pairs={{0,2},{1,3},{2,0},{3,1},{4,6},{5,7},{6,4},{7,5},{8,10},{9,11},{10,... | collective-permute-start | bytes 393224 | tf_op jit(solution)/shard_map/ppermute | solution.py:165
  19.3 0.0 collective-permute-done.8.refs_9_
  19.3 0.5 %collective-permute-start.10 = (bf16[8,64,128]{2,1,0:T(8,128)(2,1)S(1)}, bf16[8,64,128]{2,1,0:T(8,128)(2,1)S(1)}, u32[]{:S(2)}, u32[]{:S(2)}) collective-permute-start(bf16[8,64,128]{2,1,0:T(8,128)(2,1)S(1)} %collective-permute-done.8.refs_9_), channel_id=1, source_target_pairs={{0,2},{1,3},{2,0},{3,1},{4,6},{5,7},{6,4},{7,5},{8,10},{9,11},{10,... | collective-permute-start | bytes 393224 | tf_op jit(solution)/shard_map/ppermute | solution.py:165
  19.9 0.0 collective-permute-done.2.refs_3_
  19.9 0.0 collective-permute-start.13
  19.9 0.0 collective-permute-done.4.refs_5_
  19.9 0.0 collective-permute-done.7.refs_8_
  19.9 4.1 %shard_map.84 = (bf16[8,8,64,128]{3,2,1,0:T(8,128)(2,1)}, s32[65]{0:T(128)S(1)}) custom-call(s32[8,8]{1,0:T(8,128)} %owner_hbm.1, s32[8,8]{1,0:T(8,128)} %slot_hbm.3, bf16[8,8,64,256]{3,2,1,0:T(8,128)(2,1)S(1)} %shard_map.82.half_ref, bf16[8,64,128]{2,1,0:T(8,128)(2,1)S(1)} %shard_map.83.refs_0_, bf16[8,64,128]{2,1,0:T(8,128)(2,1)S(1)} %collective-permute-done.refs_1_, ...), custom_call_target="tpu_custom_call" | custom-call | flops 67108864 | bytes 1048576 | tf_op jit(solution)/shard_map/pallas_call | solution.py:234
  24.0 0.2 collective-permute-done.9.refs_1_
  24.1 2.4 %collective-permute-done.10.refs_4_ = bf16[8,64,128]{2,1,0:T(8,128)(2,1)S(1)} collective-permute-done((bf16[8,64,128]{2,1,0:T(8,128)(2,1)S(1)}, bf16[8,64,128]{2,1,0:T(8,128)(2,1)S(1)}, u32[]{:S(2)}, u32[]{:S(2)}) %collective-permute-start.10) | collective-permute-done | bytes 131104 | tf_op jit(solution)/shard_map/ppermute | solution.py:165
  26.6 0.0 collective-permute-start.11
  26.6 0.5 %collective-permute-start.12 = (bf16[8,64,128]{2,1,0:T(8,128)(2,1)S(1)}, bf16[8,64,128]{2,1,0:T(8,128)(2,1)S(1)}, u32[]{:S(2)}, u32[]{:S(2)}) collective-permute-start(bf16[8,64,128]{2,1,0:T(8,128)(2,1)S(1)} %collective-permute-done.9.refs_1_), channel_id=1, source_target_pairs={{0,1},{1,0},{2,3},{3,2},{4,5},{5,4},{6,7},{7,6},{8,9},{9,8},{10,11... | collective-permute-start | bytes 393224 | tf_op jit(solution)/shard_map/ppermute | solution.py:165
  27.1 0.0 collective-permute-start.14
  27.1 0.0 collective-permute-done.13.refs_3_
  27.1 0.8 %collective-permute-done.11.refs_0_ = bf16[8,64,128]{2,1,0:T(8,128)(2,1)S(1)} collective-permute-done((bf16[8,64,128]{2,1,0:T(8,128)(2,1)S(1)}, bf16[8,64,128]{2,1,0:T(8,128)(2,1)S(1)}, u32[]{:S(2)}, u32[]{:S(2)}) %collective-permute-start.11) | collective-permute-done | bytes 131104 | tf_op jit(solution)/shard_map/ppermute | solution.py:165
  27.9 0.2 collective-permute-done.12.refs_2_
  28.1 0.3 %collective-permute-done.14.refs_5_ = bf16[8,64,128]{2,1,0:T(8,128)(2,1)S(1)} collective-permute-done((bf16[8,64,128]{2,1,0:T(8,128)(2,1)S(1)}, bf16[8,64,128]{2,1,0:T(8,128)(2,1)S(1)}, u32[]{:S(2)}, u32[]{:S(2)}) %collective-permute-start.14) | collective-permute-done | bytes 131104 | tf_op jit(solution)/shard_map/ppermute | solution.py:165
  28.4 3.3 %shard_map.85 = bf16[8,8,64,128]{3,2,1,0:T(8,128)(2,1)} custom-call(s32[65]{0:T(128)S(1)} %get-tuple-element.15.late_ref, bf16[8,8,64,128]{3,2,1,0:T(8,128)(2,1)} %get-tuple-element.17.early_hbm, bf16[8,8,64,256]{3,2,1,0:T(8,128)(2,1)S(1)} %shard_map.82.half_ref, ...), custom_call_target="tpu_custom_call", output_to_operand_aliasing={{}: (1, {})} | custom-call | flops 16777216 | bytes 524288 | tf_op jit(solution)/shard_map/pallas_call | solution.py:258
Async XLA Ops:
  1.1 10.8 %collective-permute-start.1 = (bf16[8,64,128]{2,1,0:T(8,128)(2,1)S(1)}, bf16[8,64,128]{2,1,0:T(8,128)(2,1)S(1)}, u32[]{:S(2)}, u32[]{:S(2)}) collective-permute-start(bf16[8,64,128]{2,1,0:T(8,128)(2,1)S(1)} %shard_map.83.refs_0_), channel_id=1, source_target_pairs={{0,4},{1,5},{2,6},{3,7},{4,0},{5,1},{6,2},{7,3},{8,12},{9,13},{10,... | collective-permute-start | bytes 393224 | tf_op jit(solution)/shard_map/ppermute | solution.py:165
  4.2 8.7 %collective-permute-start.5 = (bf16[8,64,128]{2,1,0:T(8,128)(2,1)S(1)}, bf16[8,64,128]{2,1,0:T(8,128)(2,1)S(1)}, u32[]{:S(2)}, u32[]{:S(2)}) collective-permute-start(bf16[8,64,128]{2,1,0:T(8,128)(2,1)S(1)} %shard_map.83.refs_0_), channel_id=1, source_target_pairs={{0,8},{1,9},{2,10},{3,11},{4,12},{5,13},{6,14},{7,15},{8,0},{9,1},... | collective-permute-start | bytes 393224 | tf_op jit(solution)/shard_map/ppermute | solution.py:165
  10.3 6.1 %collective-permute-start.3 = (bf16[8,64,128]{2,1,0:T(8,128)(2,1)S(1)}, bf16[8,64,128]{2,1,0:T(8,128)(2,1)S(1)}, u32[]{:S(2)}, u32[]{:S(2)}) collective-permute-start(bf16[8,64,128]{2,1,0:T(8,128)(2,1)S(1)} %shard_map.83.refs_0_), channel_id=1, source_target_pairs={{0,2},{1,3},{2,0},{3,1},{4,6},{5,7},{6,4},{7,5},{8,10},{9,11},{10,... | collective-permute-start | bytes 393224 | tf_op jit(solution)/shard_map/ppermute | solution.py:165
  11.8 6.0 %collective-permute-start.6 = (bf16[8,64,128]{2,1,0:T(8,128)(2,1)S(1)}, bf16[8,64,128]{2,1,0:T(8,128)(2,1)S(1)}, u32[]{:S(2)}, u32[]{:S(2)}) collective-permute-start(bf16[8,64,128]{2,1,0:T(8,128)(2,1)S(1)} %collective-permute-done.1.refs_2_), channel_id=1, source_target_pairs={{0,2},{1,3},{2,0},{3,1},{4,6},{5,7},{6,4},{7,5},{8,10},{9,11},{10,... | collective-permute-start | bytes 393224 | tf_op jit(solution)/shard_map/ppermute | solution.py:165
  12.4 5.5 %collective-permute-start = (bf16[8,64,128]{2,1,0:T(8,128)(2,1)S(1)}, bf16[8,64,128]{2,1,0:T(8,128)(2,1)S(1)}, u32[]{:S(2)}, u32[]{:S(2)}) collective-permute-start(bf16[8,64,128]{2,1,0:T(8,128)(2,1)S(1)} %shard_map.83.refs_0_), channel_id=1, source_target_pairs={{0,1},{1,0},{2,3},{3,2},{4,5},{5,4},{6,7},{7,6},{8,9},{9,8},{10,11... | collective-permute-start | bytes 393224 | tf_op jit(solution)/shard_map/ppermute | solution.py:165
  12.9 6.5 %collective-permute-start.8 = (bf16[8,64,128]{2,1,0:T(8,128)(2,1)S(1)}, bf16[8,64,128]{2,1,0:T(8,128)(2,1)S(1)}, u32[]{:S(2)}, u32[]{:S(2)}) collective-permute-start(bf16[8,64,128]{2,1,0:T(8,128)(2,1)S(1)} %collective-permute-done.5.refs_6_), channel_id=1, source_target_pairs={{0,4},{1,5},{2,6},{3,7},{4,0},{5,1},{6,2},{7,3},{8,12},{9,13},{10,... | collective-permute-start | bytes 393224 | tf_op jit(solution)/shard_map/ppermute | solution.py:165
  13.3 6.5 %collective-permute-start.2 = (bf16[8,64,128]{2,1,0:T(8,128)(2,1)S(1)}, bf16[8,64,128]{2,1,0:T(8,128)(2,1)S(1)}, u32[]{:S(2)}, u32[]{:S(2)}) collective-permute-start(bf16[8,64,128]{2,1,0:T(8,128)(2,1)S(1)} %collective-permute-done.1.refs_2_), channel_id=1, source_target_pairs={{0,1},{1,0},{2,3},{3,2},{4,5},{5,4},{6,7},{7,6},{8,9},{9,8},{10,11... | collective-permute-start | bytes 393224 | tf_op jit(solution)/shard_map/ppermute | solution.py:165
  16.4 3.5 %collective-permute-start.4 = (bf16[8,64,128]{2,1,0:T(8,128)(2,1)S(1)}, bf16[8,64,128]{2,1,0:T(8,128)(2,1)S(1)}, u32[]{:S(2)}, u32[]{:S(2)}) collective-permute-start(bf16[8,64,128]{2,1,0:T(8,128)(2,1)S(1)} %collective-permute-done.3.refs_4_), channel_id=1, source_target_pairs={{0,1},{1,0},{2,3},{3,2},{4,5},{5,4},{6,7},{7,6},{8,9},{9,8},{10,11... | collective-permute-start | bytes 393224 | tf_op jit(solution)/shard_map/ppermute | solution.py:165
  17.8 2.1 %collective-permute-start.7 = (bf16[8,64,128]{2,1,0:T(8,128)(2,1)S(1)}, bf16[8,64,128]{2,1,0:T(8,128)(2,1)S(1)}, u32[]{:S(2)}, u32[]{:S(2)}) collective-permute-start(bf16[8,64,128]{2,1,0:T(8,128)(2,1)S(1)} %collective-permute-done.6.refs_7_), channel_id=1, source_target_pairs={{0,1},{1,0},{2,3},{3,2},{4,5},{5,4},{6,7},{7,6},{8,9},{9,8},{10,11... | collective-permute-start | bytes 393224 | tf_op jit(solution)/shard_map/ppermute | solution.py:165
  17.8 6.3 %collective-permute-start.9 = (bf16[8,64,128]{2,1,0:T(8,128)(2,1)S(1)}, bf16[8,64,128]{2,1,0:T(8,128)(2,1)S(1)}, u32[]{:S(2)}, u32[]{:S(2)}) collective-permute-start(bf16[8,64,128]{2,1,0:T(8,128)(2,1)S(1)} %collective-permute-done.5.refs_6_), channel_id=1, source_target_pairs={{0,2},{1,3},{2,0},{3,1},{4,6},{5,7},{6,4},{7,5},{8,10},{9,11},{10,... | collective-permute-start | bytes 393224 | tf_op jit(solution)/shard_map/ppermute | solution.py:165
  19.3 7.2 %collective-permute-start.10 = (bf16[8,64,128]{2,1,0:T(8,128)(2,1)S(1)}, bf16[8,64,128]{2,1,0:T(8,128)(2,1)S(1)}, u32[]{:S(2)}, u32[]{:S(2)}) collective-permute-start(bf16[8,64,128]{2,1,0:T(8,128)(2,1)S(1)} %collective-permute-done.8.refs_9_), channel_id=1, source_target_pairs={{0,2},{1,3},{2,0},{3,1},{4,6},{5,7},{6,4},{7,5},{8,10},{9,11},{10,... | collective-permute-start | bytes 393224 | tf_op jit(solution)/shard_map/ppermute | solution.py:165
  19.9 7.2 %collective-permute-start.13 = (bf16[8,64,128]{2,1,0:T(8,128)(2,1)S(1)}, bf16[8,64,128]{2,1,0:T(8,128)(2,1)S(1)}, u32[]{:S(2)}, u32[]{:S(2)}) collective-permute-start(bf16[8,64,128]{2,1,0:T(8,128)(2,1)S(1)} %collective-permute-done.8.refs_9_), channel_id=1, source_target_pairs={{0,1},{1,0},{2,3},{3,2},{4,5},{5,4},{6,7},{7,6},{8,9},{9,8},{10,11... | collective-permute-start | bytes 393224 | tf_op jit(solution)/shard_map/ppermute | solution.py:165
  26.6 1.3 %collective-permute-start.11 = (bf16[8,64,128]{2,1,0:T(8,128)(2,1)S(1)}, bf16[8,64,128]{2,1,0:T(8,128)(2,1)S(1)}, u32[]{:S(2)}, u32[]{:S(2)}) collective-permute-start(bf16[8,64,128]{2,1,0:T(8,128)(2,1)S(1)} %collective-permute-done.5.refs_6_), channel_id=1, source_target_pairs={{0,1},{1,0},{2,3},{3,2},{4,5},{5,4},{6,7},{7,6},{8,9},{9,8},{10,11... | collective-permute-start | bytes 393224 | tf_op jit(solution)/shard_map/ppermute | solution.py:165
  26.6 1.5 %collective-permute-start.12 = (bf16[8,64,128]{2,1,0:T(8,128)(2,1)S(1)}, bf16[8,64,128]{2,1,0:T(8,128)(2,1)S(1)}, u32[]{:S(2)}, u32[]{:S(2)}) collective-permute-start(bf16[8,64,128]{2,1,0:T(8,128)(2,1)S(1)} %collective-permute-done.9.refs_1_), channel_id=1, source_target_pairs={{0,1},{1,0},{2,3},{3,2},{4,5},{5,4},{6,7},{7,6},{8,9},{9,8},{10,11... | collective-permute-start | bytes 393224 | tf_op jit(solution)/shard_map/ppermute | solution.py:165
  27.1 1.3 %collective-permute-start.14 = (bf16[8,64,128]{2,1,0:T(8,128)(2,1)S(1)}, bf16[8,64,128]{2,1,0:T(8,128)(2,1)S(1)}, u32[]{:S(2)}, u32[]{:S(2)}) collective-permute-start(bf16[8,64,128]{2,1,0:T(8,128)(2,1)S(1)} %collective-permute-done.10.refs_4_), channel_id=1, source_target_pairs={{0,1},{1,0},{2,3},{3,2},{4,5},{5,4},{6,7},{7,6},{8,9},{9,8},{10,11... | collective-permute-start | bytes 393224 | tf_op jit(solution)/shard_map/ppermute | solution.py:165

commit v6 on v5

--- a/solution.py
+++ b/solution.py
@@ -222,9 +222,9 @@
             for r, bit in pairs_of:
                 pieces[r | bit] = swap(pieces[r], bit)
 
-        pass_on((0, FAR), (0, NEAR))
+        pass_on((0, FAR), (0, NEAR), (0, CROSS))
         half, pieces[0] = lax.optimization_barrier((half_of(dims_left), pairs))
-        pass_on((0, CROSS), (0, CORE), (NEAR, CORE), (CROSS, CORE), (NEAR, CROSS))
+        pass_on((0, CORE), (NEAR, CORE), (CROSS, CORE), (NEAR, CROSS))
         pass_on((FAR, NEAR), (FAR, CROSS), (FAR | NEAR, CROSS), (NEAR | CROSS, CORE), (FAR | NEAR, CORE))
         early = [pieces[r] for r in EARLY]
     else:

time: 31.8 us -> 31.1 us (0.978)
  waiting for transfers between devices: 8.95 us -> 7.99 us
    ppermute x15, waiting for transfers between devices: 8.95 us -> 7.99 us  [swap(): return lax.ppermute(piece, 'sec', [(i, i ^ bit) for i in range(count)])]
  transfers between devices with their start and end apart: 15 -> 15, of which waited for: 8 -> 7; matrix products, arithmetic and copies ran while one was open for 0% -> 0% of each run, Pallas kernels for 24% -> 24%
where the time goes in v6:
time: 31.1 us
  Pallas kernels  12 us (39%)
  starting transfers between devices  11.1 us (36%)
  waiting for transfers between devices  7.99 us (26%)
    ppermute x15, starting transfers between devices, swap(): return lax.ppermute(piece, 'sec', [(i, i ^ bit) for i in range(count)])  11.1 us
    ppermute x15, waiting for transfers between devices, swap(): return lax.ppermute(piece, 'sec', [(i, i ^ bit) for i in range(count)])  7.99 us
    pallas_call x1, Pallas kernels, per_device(): pl.pallas_call(functools.partial(early_kernel, pair_count), out_shape=(ja...  4.06 us
    pallas_call x1, Pallas kernels, half_of(): pl.pallas_call(functools.partial(left_kernel, pair_count), out_shape=jax....  3.52 us
    pallas_call x1, Pallas kernels, per_device(): pl.pallas_call(late_kernel, out_shape=jax.ShapeDtypeStruct(psi.shape, jnp...  3.33 us
    pallas_call x1, Pallas kernels, per_device(): pl.pallas_call(pack_kernel, out_shape=jax.ShapeDtypeStruct((pair_count, t...  1.08 us
  transfers between devices with their start and end apart: 15, of which 7 were waited for; matrix products, arithmetic and copies ran while one was open for 0% of the time, Pallas kernels for 24%

profile of v6, /device:TPU:0, one launch (start us, length us, event | category | flops | bytes accessed | tf_op | source)
XLA Modules:
  0.0 31.1 jit_solution(3991056493416346881)
XLA Ops:
  0.0 1.1 %shard_map.83.refs_0_ = bf16[8,64,128]{2,1,0:T(8,128)(2,1)S(1)} custom-call(s32[16]{0:T(128)} %dims_hbm.3, bf16[16,64,64]{2,1,0:T(8,128)(2,1)} %right_hbm.1), custom_call_target="tpu_custom_call" | custom-call | bytes 131072 | tf_op jit(solution)/shard_map/pallas_call | solution.py:185
  1.1 3.1 %collective-permute-start.1 = (bf16[8,64,128]{2,1,0:T(8,128)(2,1)S(1)}, bf16[8,64,128]{2,1,0:T(8,128)(2,1)S(1)}, u32[]{:S(2)}, u32[]{:S(2)}) collective-permute-start(bf16[8,64,128]{2,1,0:T(8,128)(2,1)S(1)} %shard_map.83.refs_0_), channel_id=1, source_target_pairs={{0,4},{1,5},{2,6},{3,7},{4,0},{5,1},{6,2},{7,3},{8,12},{9,13},{10,... | collective-permute-start | bytes 393224 | tf_op jit(solution)/shard_map/ppermute | solution.py:165
  4.2 2.6 %collective-permute-start.5 = (bf16[8,64,128]{2,1,0:T(8,128)(2,1)S(1)}, bf16[8,64,128]{2,1,0:T(8,128)(2,1)S(1)}, u32[]{:S(2)}, u32[]{:S(2)}) collective-permute-start(bf16[8,64,128]{2,1,0:T(8,128)(2,1)S(1)} %shard_map.83.refs_0_), channel_id=1, source_target_pairs={{0,8},{1,9},{2,10},{3,11},{4,12},{5,13},{6,14},{7,15},{8,0},{9,1},... | collective-permute-start | bytes 393224 | tf_op jit(solution)/shard_map/ppermute | solution.py:165
  6.8 1.5 %collective-permute-start.3 = (bf16[8,64,128]{2,1,0:T(8,128)(2,1)S(1)}, bf16[8,64,128]{2,1,0:T(8,128)(2,1)S(1)}, u32[]{:S(2)}, u32[]{:S(2)}) collective-permute-start(bf16[8,64,128]{2,1,0:T(8,128)(2,1)S(1)} %shard_map.83.refs_0_), channel_id=1, source_target_pairs={{0,2},{1,3},{2,0},{3,1},{4,6},{5,7},{6,4},{7,5},{8,10},{9,11},{10,... | collective-permute-start | bytes 393224 | tf_op jit(solution)/shard_map/ppermute | solution.py:165
  8.3 1.3 %collective-permute-done.1.refs_2_ = bf16[8,64,128]{2,1,0:T(8,128)(2,1)S(1)} collective-permute-done((bf16[8,64,128]{2,1,0:T(8,128)(2,1)S(1)}, bf16[8,64,128]{2,1,0:T(8,128)(2,1)S(1)}, u32[]{:S(2)}, u32[]{:S(2)}) %collective-permute-start.1) | collective-permute-done | bytes 131104 | tf_op jit(solution)/shard_map/ppermute | solution.py:165
  9.5 1.8 %collective-permute-start.6 = (bf16[8,64,128]{2,1,0:T(8,128)(2,1)S(1)}, bf16[8,64,128]{2,1,0:T(8,128)(2,1)S(1)}, u32[]{:S(2)}, u32[]{:S(2)}) collective-permute-start(bf16[8,64,128]{2,1,0:T(8,128)(2,1)S(1)} %collective-permute-done.1.refs_2_), channel_id=1, source_target_pairs={{0,2},{1,3},{2,0},{3,1},{4,6},{5,7},{6,4},{7,5},{8,10},{9,11},{10,... | collective-permute-start | bytes 393224 | tf_op jit(solution)/shard_map/ppermute | solution.py:165
  11.3 3.5 %shard_map.82.half_ref = bf16[8,8,64,256]{3,2,1,0:T(8,128)(2,1)S(1)} custom-call(s32[8]{0:T(128)} %dims_hbm.2, s32[8,8]{1,0:T(8,128)} %bitcast.1, s32[8,8]{1,0:T(8,128)} %slot_hbm.3, bf16[8,64,64]{2,1,0:T(8,128)(2,1)} %left_hbm.1, bf16[8,8,64,128]{3,2,1,0:T(8,128)(2,1)} %psi_hbm.1), custom_call_target="tpu_custom_call" | custom-call | flops 67108864 | bytes 1048576 | tf_op jit(solution)/shard_map/pallas_call | solution.py:201
  14.9 0.1 collective-permute-start
  14.9 0.0 collective-permute-done.5.refs_6_
  14.9 0.1 collective-permute-start.8
  15.1 0.0 collective-permute-done.3.refs_4_
  15.1 0.4 %collective-permute-start.4 = (bf16[8,64,128]{2,1,0:T(8,128)(2,1)S(1)}, bf16[8,64,128]{2,1,0:T(8,128)(2,1)S(1)}, u32[]{:S(2)}, u32[]{:S(2)}) collective-permute-start(bf16[8,64,128]{2,1,0:T(8,128)(2,1)S(1)} %collective-permute-done.3.refs_4_), channel_id=1, source_target_pairs={{0,1},{1,0},{2,3},{3,2},{4,5},{5,4},{6,7},{7,6},{8,9},{9,8},{10,11... | collective-permute-start | bytes 393224 | tf_op jit(solution)/shard_map/ppermute | solution.py:165
  15.5 0.1 collective-permute-start.2
  15.6 0.0 collective-permute-done.6.refs_7_
  15.6 0.4 %collective-permute-start.7 = (bf16[8,64,128]{2,1,0:T(8,128)(2,1)S(1)}, bf16[8,64,128]{2,1,0:T(8,128)(2,1)S(1)}, u32[]{:S(2)}, u32[]{:S(2)}) collective-permute-start(bf16[8,64,128]{2,1,0:T(8,128)(2,1)S(1)} %collective-permute-done.6.refs_7_), channel_id=1, source_target_pairs={{0,1},{1,0},{2,3},{3,2},{4,5},{5,4},{6,7},{7,6},{8,9},{9,8},{10,11... | collective-permute-start | bytes 393224 | tf_op jit(solution)/shard_map/ppermute | solution.py:165
  16.0 0.2 collective-permute-done.refs_1_
  16.3 0.2 collective-permute-start.9
  16.5 4.4 %collective-permute-done.8.refs_9_ = bf16[8,64,128]{2,1,0:T(8,128)(2,1)S(1)} collective-permute-done((bf16[8,64,128]{2,1,0:T(8,128)(2,1)S(1)}, bf16[8,64,128]{2,1,0:T(8,128)(2,1)S(1)}, u32[]{:S(2)}, u32[]{:S(2)}) %collective-permute-start.8) | collective-permute-done | bytes 131104 | tf_op jit(solution)/shard_map/ppermute | solution.py:165
  20.9 0.2 collective-permute-start.10
  21.1 0.0 collective-permute-done.4.refs_5_
  21.1 0.0 collective-permute-start.13
  21.1 0.0 collective-permute-done.2.refs_3_
  21.1 0.0 collective-permute-done.7.refs_8_
  21.1 4.1 %shard_map.84 = (bf16[8,8,64,128]{3,2,1,0:T(8,128)(2,1)}, s32[65]{0:T(128)S(1)}) custom-call(s32[8,8]{1,0:T(8,128)} %owner_hbm.1, s32[8,8]{1,0:T(8,128)} %slot_hbm.3, bf16[8,8,64,256]{3,2,1,0:T(8,128)(2,1)S(1)} %shard_map.82.half_ref, bf16[8,64,128]{2,1,0:T(8,128)(2,1)S(1)} %shard_map.83.refs_0_, bf16[8,64,128]{2,1,0:T(8,128)(2,1)S(1)} %collective-permute-done.refs_1_, ...), custom_call_target="tpu_custom_call" | custom-call | flops 67108864 | bytes 1048576 | tf_op jit(solution)/shard_map/pallas_call | solution.py:234
  25.1 0.0 collective-permute-done.9.refs_1_
  25.2 0.7 %collective-permute-done.10.refs_4_ = bf16[8,64,128]{2,1,0:T(8,128)(2,1)S(1)} collective-permute-done((bf16[8,64,128]{2,1,0:T(8,128)(2,1)S(1)}, bf16[8,64,128]{2,1,0:T(8,128)(2,1)S(1)}, u32[]{:S(2)}, u32[]{:S(2)}) %collective-permute-start.10) | collective-permute-done | bytes 131104 | tf_op jit(solution)/shard_map/ppermute | solution.py:165
  25.9 0.0 collective-permute-start.11
  25.9 0.5 %collective-permute-start.12 = (bf16[8,64,128]{2,1,0:T(8,128)(2,1)S(1)}, bf16[8,64,128]{2,1,0:T(8,128)(2,1)S(1)}, u32[]{:S(2)}, u32[]{:S(2)}) collective-permute-start(bf16[8,64,128]{2,1,0:T(8,128)(2,1)S(1)} %collective-permute-done.9.refs_1_), channel_id=1, source_target_pairs={{0,1},{1,0},{2,3},{3,2},{4,5},{5,4},{6,7},{7,6},{8,9},{9,8},{10,11... | collective-permute-start | bytes 393224 | tf_op jit(solution)/shard_map/ppermute | solution.py:165
  26.4 0.0 collective-permute-start.14
  26.4 0.0 collective-permute-done.13.refs_3_
  26.4 0.8 %collective-permute-done.11.refs_0_ = bf16[8,64,128]{2,1,0:T(8,128)(2,1)S(1)} collective-permute-done((bf16[8,64,128]{2,1,0:T(8,128)(2,1)S(1)}, bf16[8,64,128]{2,1,0:T(8,128)(2,1)S(1)}, u32[]{:S(2)}, u32[]{:S(2)}) %collective-permute-start.11) | collective-permute-done | bytes 131104 | tf_op jit(solution)/shard_map/ppermute | solution.py:165
  27.3 0.2 collective-permute-done.12.refs_2_
  27.4 0.3 %collective-permute-done.14.refs_5_ = bf16[8,64,128]{2,1,0:T(8,128)(2,1)S(1)} collective-permute-done((bf16[8,64,128]{2,1,0:T(8,128)(2,1)S(1)}, bf16[8,64,128]{2,1,0:T(8,128)(2,1)S(1)}, u32[]{:S(2)}, u32[]{:S(2)}) %collective-permute-start.14) | collective-permute-done | bytes 131104 | tf_op jit(solution)/shard_map/ppermute | solution.py:165
  27.8 3.3 %shard_map.85 = bf16[8,8,64,128]{3,2,1,0:T(8,128)(2,1)} custom-call(s32[65]{0:T(128)S(1)} %get-tuple-element.15.late_ref, bf16[8,8,64,128]{3,2,1,0:T(8,128)(2,1)} %get-tuple-element.17.early_hbm, bf16[8,8,64,256]{3,2,1,0:T(8,128)(2,1)S(1)} %shard_map.82.half_ref, ...), custom_call_target="tpu_custom_call", output_to_operand_aliasing={{}: (1, {})} | custom-call | flops 16777216 | bytes 524288 | tf_op jit(solution)/shard_map/pallas_call | solution.py:258
Async XLA Ops:
  1.1 8.4 %collective-permute-start.1 = (bf16[8,64,128]{2,1,0:T(8,128)(2,1)S(1)}, bf16[8,64,128]{2,1,0:T(8,128)(2,1)S(1)}, u32[]{:S(2)}, u32[]{:S(2)}) collective-permute-start(bf16[8,64,128]{2,1,0:T(8,128)(2,1)S(1)} %shard_map.83.refs_0_), channel_id=1, source_target_pairs={{0,4},{1,5},{2,6},{3,7},{4,0},{5,1},{6,2},{7,3},{8,12},{9,13},{10,... | collective-permute-start | bytes 393224 | tf_op jit(solution)/shard_map/ppermute | solution.py:165
  4.2 10.8 %collective-permute-start.5 = (bf16[8,64,128]{2,1,0:T(8,128)(2,1)S(1)}, bf16[8,64,128]{2,1,0:T(8,128)(2,1)S(1)}, u32[]{:S(2)}, u32[]{:S(2)}) collective-permute-start(bf16[8,64,128]{2,1,0:T(8,128)(2,1)S(1)} %shard_map.83.refs_0_), channel_id=1, source_target_pairs={{0,8},{1,9},{2,10},{3,11},{4,12},{5,13},{6,14},{7,15},{8,0},{9,1},... | collective-permute-start | bytes 393224 | tf_op jit(solution)/shard_map/ppermute | solution.py:165
  6.8 8.3 %collective-permute-start.3 = (bf16[8,64,128]{2,1,0:T(8,128)(2,1)S(1)}, bf16[8,64,128]{2,1,0:T(8,128)(2,1)S(1)}, u32[]{:S(2)}, u32[]{:S(2)}) collective-permute-start(bf16[8,64,128]{2,1,0:T(8,128)(2,1)S(1)} %shard_map.83.refs_0_), channel_id=1, source_target_pairs={{0,2},{1,3},{2,0},{3,1},{4,6},{5,7},{6,4},{7,5},{8,10},{9,11},{10,... | collective-permute-start | bytes 393224 | tf_op jit(solution)/shard_map/ppermute | solution.py:165
  9.5 6.1 %collective-permute-start.6 = (bf16[8,64,128]{2,1,0:T(8,128)(2,1)S(1)}, bf16[8,64,128]{2,1,0:T(8,128)(2,1)S(1)}, u32[]{:S(2)}, u32[]{:S(2)}) collective-permute-start(bf16[8,64,128]{2,1,0:T(8,128)(2,1)S(1)} %collective-permute-done.1.refs_2_), channel_id=1, source_target_pairs={{0,2},{1,3},{2,0},{3,1},{4,6},{5,7},{6,4},{7,5},{8,10},{9,11},{10,... | collective-permute-start | bytes 393224 | tf_op jit(solution)/shard_map/ppermute | solution.py:165
  14.9 1.4 %collective-permute-start = (bf16[8,64,128]{2,1,0:T(8,128)(2,1)S(1)}, bf16[8,64,128]{2,1,0:T(8,128)(2,1)S(1)}, u32[]{:S(2)}, u32[]{:S(2)}) collective-permute-start(bf16[8,64,128]{2,1,0:T(8,128)(2,1)S(1)} %shard_map.83.refs_0_), channel_id=1, source_target_pairs={{0,1},{1,0},{2,3},{3,2},{4,5},{5,4},{6,7},{7,6},{8,9},{9,8},{10,11... | collective-permute-start | bytes 393224 | tf_op jit(solution)/shard_map/ppermute | solution.py:165
  14.9 5.9 %collective-permute-start.8 = (bf16[8,64,128]{2,1,0:T(8,128)(2,1)S(1)}, bf16[8,64,128]{2,1,0:T(8,128)(2,1)S(1)}, u32[]{:S(2)}, u32[]{:S(2)}) collective-permute-start(bf16[8,64,128]{2,1,0:T(8,128)(2,1)S(1)} %collective-permute-done.5.refs_6_), channel_id=1, source_target_pairs={{0,4},{1,5},{2,6},{3,7},{4,0},{5,1},{6,2},{7,3},{8,12},{9,13},{10,... | collective-permute-start | bytes 393224 | tf_op jit(solution)/shard_map/ppermute | solution.py:165
  15.1 6.0 %collective-permute-start.4 = (bf16[8,64,128]{2,1,0:T(8,128)(2,1)S(1)}, bf16[8,64,128]{2,1,0:T(8,128)(2,1)S(1)}, u32[]{:S(2)}, u32[]{:S(2)}) collective-permute-start(bf16[8,64,128]{2,1,0:T(8,128)(2,1)S(1)} %collective-permute-done.3.refs_4_), channel_id=1, source_target_pairs={{0,1},{1,0},{2,3},{3,2},{4,5},{5,4},{6,7},{7,6},{8,9},{9,8},{10,11... | collective-permute-start | bytes 393224 | tf_op jit(solution)/shard_map/ppermute | solution.py:165
  15.5 5.6 %collective-permute-start.2 = (bf16[8,64,128]{2,1,0:T(8,128)(2,1)S(1)}, bf16[8,64,128]{2,1,0:T(8,128)(2,1)S(1)}, u32[]{:S(2)}, u32[]{:S(2)}) collective-permute-start(bf16[8,64,128]{2,1,0:T(8,128)(2,1)S(1)} %collective-permute-done.1.refs_2_), channel_id=1, source_target_pairs={{0,1},{1,0},{2,3},{3,2},{4,5},{5,4},{6,7},{7,6},{8,9},{9,8},{10,11... | collective-permute-start | bytes 393224 | tf_op jit(solution)/shard_map/ppermute | solution.py:165
  15.6 5.5 %collective-permute-start.7 = (bf16[8,64,128]{2,1,0:T(8,128)(2,1)S(1)}, bf16[8,64,128]{2,1,0:T(8,128)(2,1)S(1)}, u32[]{:S(2)}, u32[]{:S(2)}) collective-permute-start(bf16[8,64,128]{2,1,0:T(8,128)(2,1)S(1)} %collective-permute-done.6.refs_7_), channel_id=1, source_target_pairs={{0,1},{1,0},{2,3},{3,2},{4,5},{5,4},{6,7},{7,6},{8,9},{9,8},{10,11... | collective-permute-start | bytes 393224 | tf_op jit(solution)/shard_map/ppermute | solution.py:165
  16.3 8.9 %collective-permute-start.9 = (bf16[8,64,128]{2,1,0:T(8,128)(2,1)S(1)}, bf16[8,64,128]{2,1,0:T(8,128)(2,1)S(1)}, u32[]{:S(2)}, u32[]{:S(2)}) collective-permute-start(bf16[8,64,128]{2,1,0:T(8,128)(2,1)S(1)} %collective-permute-done.5.refs_6_), channel_id=1, source_target_pairs={{0,2},{1,3},{2,0},{3,1},{4,6},{5,7},{6,4},{7,5},{8,10},{9,11},{10,... | collective-permute-start | bytes 393224 | tf_op jit(solution)/shard_map/ppermute | solution.py:165
  20.9 5.1 %collective-permute-start.10 = (bf16[8,64,128]{2,1,0:T(8,128)(2,1)S(1)}, bf16[8,64,128]{2,1,0:T(8,128)(2,1)S(1)}, u32[]{:S(2)}, u32[]{:S(2)}) collective-permute-start(bf16[8,64,128]{2,1,0:T(8,128)(2,1)S(1)} %collective-permute-done.8.refs_9_), channel_id=1, source_target_pairs={{0,2},{1,3},{2,0},{3,1},{4,6},{5,7},{6,4},{7,5},{8,10},{9,11},{10,... | collective-permute-start | bytes 393224 | tf_op jit(solution)/shard_map/ppermute | solution.py:165
  21.1 5.4 %collective-permute-start.13 = (bf16[8,64,128]{2,1,0:T(8,128)(2,1)S(1)}, bf16[8,64,128]{2,1,0:T(8,128)(2,1)S(1)}, u32[]{:S(2)}, u32[]{:S(2)}) collective-permute-start(bf16[8,64,128]{2,1,0:T(8,128)(2,1)S(1)} %collective-permute-done.8.refs_9_), channel_id=1, source_target_pairs={{0,1},{1,0},{2,3},{3,2},{4,5},{5,4},{6,7},{7,6},{8,9},{9,8},{10,11... | collective-permute-start | bytes 393224 | tf_op jit(solution)/shard_map/ppermute | solution.py:165
  25.9 1.3 %collective-permute-start.11 = (bf16[8,64,128]{2,1,0:T(8,128)(2,1)S(1)}, bf16[8,64,128]{2,1,0:T(8,128)(2,1)S(1)}, u32[]{:S(2)}, u32[]{:S(2)}) collective-permute-start(bf16[8,64,128]{2,1,0:T(8,128)(2,1)S(1)} %collective-permute-done.5.refs_6_), channel_id=1, source_target_pairs={{0,1},{1,0},{2,3},{3,2},{4,5},{5,4},{6,7},{7,6},{8,9},{9,8},{10,11... | collective-permute-start | bytes 393224 | tf_op jit(solution)/shard_map/ppermute | solution.py:165
  25.9 1.5 %collective-permute-start.12 = (bf16[8,64,128]{2,1,0:T(8,128)(2,1)S(1)}, bf16[8,64,128]{2,1,0:T(8,128)(2,1)S(1)}, u32[]{:S(2)}, u32[]{:S(2)}) collective-permute-start(bf16[8,64,128]{2,1,0:T(8,128)(2,1)S(1)} %collective-permute-done.9.refs_1_), channel_id=1, source_target_pairs={{0,1},{1,0},{2,3},{3,2},{4,5},{5,4},{6,7},{7,6},{8,9},{9,8},{10,11... | collective-permute-start | bytes 393224 | tf_op jit(solution)/shard_map/ppermute | solution.py:165
  26.4 1.3 %collective-permute-start.14 = (bf16[8,64,128]{2,1,0:T(8,128)(2,1)S(1)}, bf16[8,64,128]{2,1,0:T(8,128)(2,1)S(1)}, u32[]{:S(2)}, u32[]{:S(2)}) collective-permute-start(bf16[8,64,128]{2,1,0:T(8,128)(2,1)S(1)} %collective-permute-done.10.refs_4_), channel_id=1, source_target_pairs={{0,1},{1,0},{2,3},{3,2},{4,5},{5,4},{6,7},{7,6},{8,9},{9,8},{10,11... | collective-permute-start | bytes 393224 | tf_op jit(solution)/shard_map/ppermute | solution.py:165

commit v7 on v6

--- a/solution.py
+++ b/solution.py
@@ -10,8 +10,8 @@
 VMEM_LIMIT = 48 * 1024 * 1024
 GROUP = 4
 FAR, NEAR, CROSS, CORE = 8, 4, 2, 1
-EARLY = (0, CORE, NEAR, NEAR | CORE, CROSS, CROSS | CORE, FAR, NEAR | CROSS, NEAR | CROSS | CORE, FAR | NEAR)
-LATE = tuple(r for r in range(16) if r not in EARLY)
+LATE = (FAR | CORE, FAR | NEAR | CORE, FAR | CROSS | CORE, FAR | NEAR | CROSS, FAR | NEAR | CROSS | CORE)
+EARLY = tuple(r for r in range(16) if r not in LATE)
 ORDER = EARLY + LATE
 
 
@@ -222,10 +222,13 @@
             for r, bit in pairs_of:
                 pieces[r | bit] = swap(pieces[r], bit)
 
-        pass_on((0, FAR), (0, NEAR), (0, CROSS))
-        half, pieces[0] = lax.optimization_barrier((half_of(dims_left), pairs))
-        pass_on((0, CORE), (NEAR, CORE), (CROSS, CORE), (NEAR, CROSS))
-        pass_on((FAR, NEAR), (FAR, CROSS), (FAR | NEAR, CROSS), (NEAR | CROSS, CORE), (FAR | NEAR, CORE))
+        pass_on((0, FAR), (0, NEAR), (0, CROSS), (0, CORE), (NEAR, CROSS), (FAR, NEAR), (FAR, CROSS), (FAR | NEAR, CROSS))
+        dims_left, pieces[FAR] = lax.optimization_barrier((dims_left, pieces[FAR]))
+        half = half_of(dims_left)
+        held = (NEAR, CROSS, NEAR | CROSS,)
+        half, ends = lax.optimization_barrier((half, [pieces[r] for r in held]))
+        pieces.update(zip(held, ends))
+        pass_on((NEAR, CORE), (CROSS, CORE), (NEAR | CROSS, CORE), (FAR | NEAR, CORE))
         early = [pieces[r] for r in EARLY]
     else:
         half = half_of(dims_left)
@@ -250,7 +253,7 @@
         cost_estimate=pl.CostEstimate(flops=flops, bytes_accessed=2 * psi.size, transcendentals=0),
     )(*in_hbm(right_owner, right_slot), half, *early)
     if by_swaps:
-        ends = (FAR, FAR | CROSS, FAR | NEAR | CROSS)
+        ends = (FAR, FAR | CROSS, FAR | NEAR | CROSS,)
         held, sigma = lax.optimization_barrier(([pieces[r] for r in ends], sigma))
         for r, piece in zip(ends, held):
             pieces[r], pieces[r | CORE] = piece, swap(piece, CORE)

time: 31.1 us -> 29.8 us (0.958); the launches traced: 31.1 us -> 29.4 us
  waiting for transfers between devices: 7.99 us -> 5.25 us
  starting transfers between devices: 11.1 us -> 12.8 us
  Pallas kernels: 12 us -> 11.3 us
    ppermute x15, waiting for transfers between devices: 7.99 us -> 5.25 us  [swap(): return lax.ppermute(piece, 'sec', [(i, i ^ bit) for i in range(count)])]
    ppermute x15, starting transfers between devices: 11.1 us -> 12.8 us  [swap(): return lax.ppermute(piece, 'sec', [(i, i ^ bit) for i in range(count)])]
    pallas_call x1, Pallas kernels: 3.33 us -> 2.67 us  [per_device(): pl.pallas_call(late_kernel, out_shape=jax.ShapeDtypeStruct(psi.shape, jnp...]
  transfers between devices with their start and end apart: 15 -> 15, of which waited for: 7 -> 8; matrix products, arithmetic and copies ran while one was open for 0% -> 0% of each run, Pallas kernels for 24% -> 26%
where the time goes in v7:
time: 29.8 us; the launch traced here: 29.4 us
  starting transfers between devices  12.8 us (43%)
  Pallas kernels  11.3 us (38%)
  waiting for transfers between devices  5.25 us (18%)
    ppermute x15, starting transfers between devices, swap(): return lax.ppermute(piece, 'sec', [(i, i ^ bit) for i in range(count)])  12.8 us
    ppermute x15, waiting for transfers between devices, swap(): return lax.ppermute(piece, 'sec', [(i, i ^ bit) for i in range(count)])  5.25 us
    pallas_call x1, Pallas kernels, per_device(): pl.pallas_call(functools.partial(early_kernel, pair_count), out_shape=(ja...  4.05 us
    pallas_call x1, Pallas kernels, half_of(): pl.pallas_call(functools.partial(left_kernel, pair_count), out_shape=jax....  3.52 us
    pallas_call x1, Pallas kernels, per_device(): pl.pallas_call(late_kernel, out_shape=jax.ShapeDtypeStruct(psi.shape, jnp...  2.67 us
    pallas_call x1, Pallas kernels, per_device(): pl.pallas_call(pack_kernel, out_shape=jax.ShapeDtypeStruct((pair_count, t...  1.08 us
  transfers between devices with their start and end apart: 15, of which 8 were waited for; matrix products, arithmetic and copies ran while one was open for 0% of the time, Pallas kernels for 26%

profile of v7, /device:TPU:0, one launch (start us, length us, event | category | flops | bytes accessed | tf_op | source)
XLA Modules:
  0.0 29.4 jit_solution(16283458294924761285)
XLA Ops:
  0.0 1.1 %shard_map.82.refs_0_ = bf16[8,64,128]{2,1,0:T(8,128)(2,1)S(1)} custom-call(s32[16]{0:T(128)} %dims_hbm.1, bf16[16,64,64]{2,1,0:T(8,128)(2,1)} %right_hbm.1), custom_call_target="tpu_custom_call" | custom-call | bytes 131072 | tf_op jit(solution)/shard_map/pallas_call | solution.py:185
  1.1 3.1 %collective-permute-start.1 = (bf16[8,64,128]{2,1,0:T(8,128)(2,1)S(1)}, bf16[8,64,128]{2,1,0:T(8,128)(2,1)S(1)}, u32[]{:S(2)}, u32[]{:S(2)}) collective-permute-start(bf16[8,64,128]{2,1,0:T(8,128)(2,1)S(1)} %shard_map.82.refs_0_), channel_id=1, source_target_pairs={{0,4},{1,5},{2,6},{3,7},{4,0},{5,1},{6,2},{7,3},{8,12},{9,13},{10,... | collective-permute-start | bytes 393224 | tf_op jit(solution)/shard_map/ppermute | solution.py:165
  4.2 2.6 %collective-permute-start = (bf16[8,64,128]{2,1,0:T(8,128)(2,1)S(1)}, bf16[8,64,128]{2,1,0:T(8,128)(2,1)S(1)}, u32[]{:S(2)}, u32[]{:S(2)}) collective-permute-start(bf16[8,64,128]{2,1,0:T(8,128)(2,1)S(1)} %shard_map.82.refs_0_), channel_id=1, source_target_pairs={{0,8},{1,9},{2,10},{3,11},{4,12},{5,13},{6,14},{7,15},{8,0},{9,1},... | collective-permute-start | bytes 393224 | tf_op jit(solution)/shard_map/ppermute | solution.py:165
  6.8 1.5 %collective-permute-start.2 = (bf16[8,64,128]{2,1,0:T(8,128)(2,1)S(1)}, bf16[8,64,128]{2,1,0:T(8,128)(2,1)S(1)}, u32[]{:S(2)}, u32[]{:S(2)}) collective-permute-start(bf16[8,64,128]{2,1,0:T(8,128)(2,1)S(1)} %shard_map.82.refs_0_), channel_id=1, source_target_pairs={{0,2},{1,3},{2,0},{3,1},{4,6},{5,7},{6,4},{7,5},{8,10},{9,11},{10,... | collective-permute-start | bytes 393224 | tf_op jit(solution)/shard_map/ppermute | solution.py:165
  8.3 1.3 %collective-permute-done.1.refs_4_ = bf16[8,64,128]{2,1,0:T(8,128)(2,1)S(1)} collective-permute-done((bf16[8,64,128]{2,1,0:T(8,128)(2,1)S(1)}, bf16[8,64,128]{2,1,0:T(8,128)(2,1)S(1)}, u32[]{:S(2)}, u32[]{:S(2)}) %collective-permute-start.1) | collective-permute-done | bytes 131104 | tf_op jit(solution)/shard_map/ppermute | solution.py:165
  9.5 1.8 %collective-permute-start.3 = (bf16[8,64,128]{2,1,0:T(8,128)(2,1)S(1)}, bf16[8,64,128]{2,1,0:T(8,128)(2,1)S(1)}, u32[]{:S(2)}, u32[]{:S(2)}) collective-permute-start(bf16[8,64,128]{2,1,0:T(8,128)(2,1)S(1)} %collective-permute-done.1.refs_4_), channel_id=1, source_target_pairs={{0,2},{1,3},{2,0},{3,1},{4,6},{5,7},{6,4},{7,5},{8,10},{9,11},{10,... | collective-permute-start | bytes 393224 | tf_op jit(solution)/shard_map/ppermute | solution.py:165
  11.3 0.0 collective-permute-start.4
  11.3 1.6 %collective-permute-done.refs_8_ = bf16[8,64,128]{2,1,0:T(8,128)(2,1)S(1)} collective-permute-done((bf16[8,64,128]{2,1,0:T(8,128)(2,1)S(1)}, bf16[8,64,128]{2,1,0:T(8,128)(2,1)S(1)}, u32[]{:S(2)}, u32[]{:S(2)}) %collective-permute-start) | collective-permute-done | bytes 131104 | tf_op jit(solution)/shard_map/ppermute | solution.py:165
  12.9 0.4 %collective-permute-start.9 = (bf16[8,64,128]{2,1,0:T(8,128)(2,1)S(1)}, bf16[8,64,128]{2,1,0:T(8,128)(2,1)S(1)}, u32[]{:S(2)}, u32[]{:S(2)}) collective-permute-start(bf16[8,64,128]{2,1,0:T(8,128)(2,1)S(1)} %collective-permute-done.refs_8_), channel_id=1, source_target_pairs={{0,4},{1,5},{2,6},{3,7},{4,0},{5,1},{6,2},{7,3},{8,12},{9,13},{10,... | collective-permute-start | bytes 393224 | tf_op jit(solution)/shard_map/ppermute | solution.py:165
  13.3 1.5 %collective-permute-start.8 = (bf16[8,64,128]{2,1,0:T(8,128)(2,1)S(1)}, bf16[8,64,128]{2,1,0:T(8,128)(2,1)S(1)}, u32[]{:S(2)}, u32[]{:S(2)}) collective-permute-start(bf16[8,64,128]{2,1,0:T(8,128)(2,1)S(1)} %collective-permute-done.refs_8_), channel_id=1, source_target_pairs={{0,2},{1,3},{2,0},{3,1},{4,6},{5,7},{6,4},{7,5},{8,10},{9,11},{10,... | collective-permute-start | bytes 393224 | tf_op jit(solution)/shard_map/ppermute | solution.py:165
  14.8 3.5 %shard_map.83.half_ref = bf16[8,8,64,256]{3,2,1,0:T(8,128)(2,1)S(1)} custom-call(s32[8]{0:T(128)} %dims_hbm.2, s32[8,8]{1,0:T(8,128)} %bitcast.1, s32[8,8]{1,0:T(8,128)} %slot_hbm.3, bf16[8,64,64]{2,1,0:T(8,128)(2,1)} %left_hbm.1, bf16[8,8,64,128]{3,2,1,0:T(8,128)(2,1)} %psi_hbm.1), custom_call_target="tpu_custom_call" | custom-call | flops 67108864 | bytes 1048576 | tf_op jit(solution)/shard_map/pallas_call | solution.py:201
  18.4 0.0 collective-permute-done.2.refs_2_
  18.4 0.0 collective-permute-done.3.refs_6_
  18.4 0.1 collective-permute-start.5
  18.4 0.5 %collective-permute-start.6 = (bf16[8,64,128]{2,1,0:T(8,128)(2,1)S(1)}, bf16[8,64,128]{2,1,0:T(8,128)(2,1)S(1)}, u32[]{:S(2)}, u32[]{:S(2)}) collective-permute-start(bf16[8,64,128]{2,1,0:T(8,128)(2,1)S(1)} %collective-permute-done.1.refs_4_), channel_id=1, source_target_pairs={{0,1},{1,0},{2,3},{3,2},{4,5},{5,4},{6,7},{7,6},{8,9},{9,8},{10,11... | collective-permute-start | bytes 393224 | tf_op jit(solution)/shard_map/ppermute | solution.py:165
  18.9 0.0 collective-permute-done.4.refs_1_
  19.0 0.1 collective-permute-start.7
  19.0 0.0 collective-permute-done.9.refs_10_
  19.0 0.5 %collective-permute-start.10 = (bf16[8,64,128]{2,1,0:T(8,128)(2,1)S(1)}, bf16[8,64,128]{2,1,0:T(8,128)(2,1)S(1)}, u32[]{:S(2)}, u32[]{:S(2)}) collective-permute-start(bf16[8,64,128]{2,1,0:T(8,128)(2,1)S(1)} %collective-permute-done.9.refs_10_), channel_id=1, source_target_pairs={{0,2},{1,3},{2,0},{3,1},{4,6},{5,7},{6,4},{7,5},{8,10},{9,11},{10,... | collective-permute-start | bytes 393224 | tf_op jit(solution)/shard_map/ppermute | solution.py:165
  19.6 0.0 collective-permute-done.8.refs_9_
  19.6 0.2 collective-permute-start.12
  19.7 0.0 collective-permute-done.5.refs_3_
  19.8 0.2 collective-permute-done.6.refs_5_
  20.0 0.3 %collective-permute-done.7.refs_7_ = bf16[8,64,128]{2,1,0:T(8,128)(2,1)S(1)} collective-permute-done((bf16[8,64,128]{2,1,0:T(8,128)(2,1)S(1)}, bf16[8,64,128]{2,1,0:T(8,128)(2,1)S(1)}, u32[]{:S(2)}, u32[]{:S(2)}) %collective-permute-start.7) | collective-permute-done | bytes 131104 | tf_op jit(solution)/shard_map/ppermute | solution.py:165
  20.3 4.0 %shard_map.84 = (bf16[8,8,64,128]{3,2,1,0:T(8,128)(2,1)}, s32[65]{0:T(128)S(1)}) custom-call(s32[8,8]{1,0:T(8,128)} %owner_hbm.1, s32[8,8]{1,0:T(8,128)} %slot_hbm.3, bf16[8,8,64,256]{3,2,1,0:T(8,128)(2,1)S(1)} %shard_map.83.half_ref, bf16[8,64,128]{2,1,0:T(8,128)(2,1)S(1)} %shard_map.82.refs_0_, bf16[8,64,128]{2,1,0:T(8,128)(2,1)S(1)} %collective-permute-done.4.refs_1_, ...), custom_call_target="tpu_custom_call" | custom-call | flops 67108864 | bytes 1048576 | tf_op jit(solution)/shard_map/pallas_call | solution.py:237
  24.4 0.5 %collective-permute-done.10.refs_3_ = bf16[8,64,128]{2,1,0:T(8,128)(2,1)S(1)} collective-permute-done((bf16[8,64,128]{2,1,0:T(8,128)(2,1)S(1)}, bf16[8,64,128]{2,1,0:T(8,128)(2,1)S(1)}, u32[]{:S(2)}, u32[]{:S(2)}) %collective-permute-start.10) | collective-permute-done | bytes 131104 | tf_op jit(solution)/shard_map/ppermute | solution.py:165
  24.9 0.0 collective-permute-start.11
  24.9 0.5 %collective-permute-start.13 = (bf16[8,64,128]{2,1,0:T(8,128)(2,1)S(1)}, bf16[8,64,128]{2,1,0:T(8,128)(2,1)S(1)}, u32[]{:S(2)}, u32[]{:S(2)}) collective-permute-start(bf16[8,64,128]{2,1,0:T(8,128)(2,1)S(1)} %collective-permute-done.8.refs_9_), channel_id=1, source_target_pairs={{0,1},{1,0},{2,3},{3,2},{4,5},{5,4},{6,7},{7,6},{8,9},{9,8},{10,11... | collective-permute-start | bytes 393224 | tf_op jit(solution)/shard_map/ppermute | solution.py:165
  25.4 0.0 collective-permute-start.14
  25.4 0.0 collective-permute-done.12.refs_1_
  25.4 0.8 %collective-permute-done.11.refs_0_ = bf16[8,64,128]{2,1,0:T(8,128)(2,1)S(1)} collective-permute-done((bf16[8,64,128]{2,1,0:T(8,128)(2,1)S(1)}, bf16[8,64,128]{2,1,0:T(8,128)(2,1)S(1)}, u32[]{:S(2)}, u32[]{:S(2)}) %collective-permute-start.11) | collective-permute-done | bytes 131104 | tf_op jit(solution)/shard_map/ppermute | solution.py:165
  26.2 0.2 collective-permute-done.13.refs_2_
  26.4 0.3 %collective-permute-done.14.refs_4_ = bf16[8,64,128]{2,1,0:T(8,128)(2,1)S(1)} collective-permute-done((bf16[8,64,128]{2,1,0:T(8,128)(2,1)S(1)}, bf16[8,64,128]{2,1,0:T(8,128)(2,1)S(1)}, u32[]{:S(2)}, u32[]{:S(2)}) %collective-permute-start.14) | collective-permute-done | bytes 131104 | tf_op jit(solution)/shard_map/ppermute | solution.py:165
  26.7 2.7 %shard_map.85 = bf16[8,8,64,128]{3,2,1,0:T(8,128)(2,1)} custom-call(s32[65]{0:T(128)S(1)} %get-tuple-element.23.late_ref, bf16[8,8,64,128]{3,2,1,0:T(8,128)(2,1)} %get-tuple-element.25.early_hbm, bf16[8,8,64,256]{3,2,1,0:T(8,128)(2,1)S(1)} %shard_map.83.half_ref, ...), custom_call_target="tpu_custom_call", output_to_operand_aliasing={{}: (1, {})} | custom-call | flops 16777216 | bytes 524288 | tf_op jit(solution)/shard_map/pallas_call | solution.py:261
Async XLA Ops:
  1.1 8.4 %collective-permute-start.1 = (bf16[8,64,128]{2,1,0:T(8,128)(2,1)S(1)}, bf16[8,64,128]{2,1,0:T(8,128)(2,1)S(1)}, u32[]{:S(2)}, u32[]{:S(2)}) collective-permute-start(bf16[8,64,128]{2,1,0:T(8,128)(2,1)S(1)} %shard_map.82.refs_0_), channel_id=1, source_target_pairs={{0,4},{1,5},{2,6},{3,7},{4,0},{5,1},{6,2},{7,3},{8,12},{9,13},{10,... | collective-permute-start | bytes 393224 | tf_op jit(solution)/shard_map/ppermute | solution.py:165
  4.2 8.7 %collective-permute-start = (bf16[8,64,128]{2,1,0:T(8,128)(2,1)S(1)}, bf16[8,64,128]{2,1,0:T(8,128)(2,1)S(1)}, u32[]{:S(2)}, u32[]{:S(2)}) collective-permute-start(bf16[8,64,128]{2,1,0:T(8,128)(2,1)S(1)} %shard_map.82.refs_0_), channel_id=1, source_target_pairs={{0,8},{1,9},{2,10},{3,11},{4,12},{5,13},{6,14},{7,15},{8,0},{9,1},... | collective-permute-start | bytes 393224 | tf_op jit(solution)/shard_map/ppermute | solution.py:165
  6.8 11.6 %collective-permute-start.2 = (bf16[8,64,128]{2,1,0:T(8,128)(2,1)S(1)}, bf16[8,64,128]{2,1,0:T(8,128)(2,1)S(1)}, u32[]{:S(2)}, u32[]{:S(2)}) collective-permute-start(bf16[8,64,128]{2,1,0:T(8,128)(2,1)S(1)} %shard_map.82.refs_0_), channel_id=1, source_target_pairs={{0,2},{1,3},{2,0},{3,1},{4,6},{5,7},{6,4},{7,5},{8,10},{9,11},{10,... | collective-permute-start | bytes 393224 | tf_op jit(solution)/shard_map/ppermute | solution.py:165
  9.5 8.8 %collective-permute-start.3 = (bf16[8,64,128]{2,1,0:T(8,128)(2,1)S(1)}, bf16[8,64,128]{2,1,0:T(8,128)(2,1)S(1)}, u32[]{:S(2)}, u32[]{:S(2)}) collective-permute-start(bf16[8,64,128]{2,1,0:T(8,128)(2,1)S(1)} %collective-permute-done.1.refs_4_), channel_id=1, source_target_pairs={{0,2},{1,3},{2,0},{3,1},{4,6},{5,7},{6,4},{7,5},{8,10},{9,11},{10,... | collective-permute-start | bytes 393224 | tf_op jit(solution)/shard_map/ppermute | solution.py:165
  11.3 7.6 %collective-permute-start.4 = (bf16[8,64,128]{2,1,0:T(8,128)(2,1)S(1)}, bf16[8,64,128]{2,1,0:T(8,128)(2,1)S(1)}, u32[]{:S(2)}, u32[]{:S(2)}) collective-permute-start(bf16[8,64,128]{2,1,0:T(8,128)(2,1)S(1)} %shard_map.82.refs_0_), channel_id=1, source_target_pairs={{0,1},{1,0},{2,3},{3,2},{4,5},{5,4},{6,7},{7,6},{8,9},{9,8},{10,11... | collective-permute-start | bytes 393224 | tf_op jit(solution)/shard_map/ppermute | solution.py:165
  12.9 6.1 %collective-permute-start.9 = (bf16[8,64,128]{2,1,0:T(8,128)(2,1)S(1)}, bf16[8,64,128]{2,1,0:T(8,128)(2,1)S(1)}, u32[]{:S(2)}, u32[]{:S(2)}) collective-permute-start(bf16[8,64,128]{2,1,0:T(8,128)(2,1)S(1)} %collective-permute-done.refs_8_), channel_id=1, source_target_pairs={{0,4},{1,5},{2,6},{3,7},{4,0},{5,1},{6,2},{7,3},{8,12},{9,13},{10,... | collective-permute-start | bytes 393224 | tf_op jit(solution)/shard_map/ppermute | solution.py:165
  13.3 6.2 %collective-permute-start.8 = (bf16[8,64,128]{2,1,0:T(8,128)(2,1)S(1)}, bf16[8,64,128]{2,1,0:T(8,128)(2,1)S(1)}, u32[]{:S(2)}, u32[]{:S(2)}) collective-permute-start(bf16[8,64,128]{2,1,0:T(8,128)(2,1)S(1)} %collective-permute-done.refs_8_), channel_id=1, source_target_pairs={{0,2},{1,3},{2,0},{3,1},{4,6},{5,7},{6,4},{7,5},{8,10},{9,11},{10,... | collective-permute-start | bytes 393224 | tf_op jit(solution)/shard_map/ppermute | solution.py:165
  18.4 1.4 %collective-permute-start.5 = (bf16[8,64,128]{2,1,0:T(8,128)(2,1)S(1)}, bf16[8,64,128]{2,1,0:T(8,128)(2,1)S(1)}, u32[]{:S(2)}, u32[]{:S(2)}) collective-permute-start(bf16[8,64,128]{2,1,0:T(8,128)(2,1)S(1)} %collective-permute-done.2.refs_2_), channel_id=1, source_target_pairs={{0,1},{1,0},{2,3},{3,2},{4,5},{5,4},{6,7},{7,6},{8,9},{9,8},{10,11... | collective-permute-start | bytes 393224 | tf_op jit(solution)/shard_map/ppermute | solution.py:165
  18.4 1.5 %collective-permute-start.6 = (bf16[8,64,128]{2,1,0:T(8,128)(2,1)S(1)}, bf16[8,64,128]{2,1,0:T(8,128)(2,1)S(1)}, u32[]{:S(2)}, u32[]{:S(2)}) collective-permute-start(bf16[8,64,128]{2,1,0:T(8,128)(2,1)S(1)} %collective-permute-done.1.refs_4_), channel_id=1, source_target_pairs={{0,1},{1,0},{2,3},{3,2},{4,5},{5,4},{6,7},{7,6},{8,9},{9,8},{10,11... | collective-permute-start | bytes 393224 | tf_op jit(solution)/shard_map/ppermute | solution.py:165
  19.0 1.3 %collective-permute-start.7 = (bf16[8,64,128]{2,1,0:T(8,128)(2,1)S(1)}, bf16[8,64,128]{2,1,0:T(8,128)(2,1)S(1)}, u32[]{:S(2)}, u32[]{:S(2)}) collective-permute-start(bf16[8,64,128]{2,1,0:T(8,128)(2,1)S(1)} %collective-permute-done.3.refs_6_), channel_id=1, source_target_pairs={{0,1},{1,0},{2,3},{3,2},{4,5},{5,4},{6,7},{7,6},{8,9},{9,8},{10,11... | collective-permute-start | bytes 393224 | tf_op jit(solution)/shard_map/ppermute | solution.py:165
  19.0 5.8 %collective-permute-start.10 = (bf16[8,64,128]{2,1,0:T(8,128)(2,1)S(1)}, bf16[8,64,128]{2,1,0:T(8,128)(2,1)S(1)}, u32[]{:S(2)}, u32[]{:S(2)}) collective-permute-start(bf16[8,64,128]{2,1,0:T(8,128)(2,1)S(1)} %collective-permute-done.9.refs_10_), channel_id=1, source_target_pairs={{0,2},{1,3},{2,0},{3,1},{4,6},{5,7},{6,4},{7,5},{8,10},{9,11},{10,... | collective-permute-start | bytes 393224 | tf_op jit(solution)/shard_map/ppermute | solution.py:165
  19.6 5.8 %collective-permute-start.12 = (bf16[8,64,128]{2,1,0:T(8,128)(2,1)S(1)}, bf16[8,64,128]{2,1,0:T(8,128)(2,1)S(1)}, u32[]{:S(2)}, u32[]{:S(2)}) collective-permute-start(bf16[8,64,128]{2,1,0:T(8,128)(2,1)S(1)} %collective-permute-done.9.refs_10_), channel_id=1, source_target_pairs={{0,1},{1,0},{2,3},{3,2},{4,5},{5,4},{6,7},{7,6},{8,9},{9,8},{10,11... | collective-permute-start | bytes 393224 | tf_op jit(solution)/shard_map/ppermute | solution.py:165
  24.9 1.3 %collective-permute-start.11 = (bf16[8,64,128]{2,1,0:T(8,128)(2,1)S(1)}, bf16[8,64,128]{2,1,0:T(8,128)(2,1)S(1)}, u32[]{:S(2)}, u32[]{:S(2)}) collective-permute-start(bf16[8,64,128]{2,1,0:T(8,128)(2,1)S(1)} %collective-permute-done.refs_8_), channel_id=1, source_target_pairs={{0,1},{1,0},{2,3},{3,2},{4,5},{5,4},{6,7},{7,6},{8,9},{9,8},{10,11... | collective-permute-start | bytes 393224 | tf_op jit(solution)/shard_map/ppermute | solution.py:165
  24.9 1.5 %collective-permute-start.13 = (bf16[8,64,128]{2,1,0:T(8,128)(2,1)S(1)}, bf16[8,64,128]{2,1,0:T(8,128)(2,1)S(1)}, u32[]{:S(2)}, u32[]{:S(2)}) collective-permute-start(bf16[8,64,128]{2,1,0:T(8,128)(2,1)S(1)} %collective-permute-done.8.refs_9_), channel_id=1, source_target_pairs={{0,1},{1,0},{2,3},{3,2},{4,5},{5,4},{6,7},{7,6},{8,9},{9,8},{10,11... | collective-permute-start | bytes 393224 | tf_op jit(solution)/shard_map/ppermute | solution.py:165
  25.4 1.3 %collective-permute-start.14 = (bf16[8,64,128]{2,1,0:T(8,128)(2,1)S(1)}, bf16[8,64,128]{2,1,0:T(8,128)(2,1)S(1)}, u32[]{:S(2)}, u32[]{:S(2)}) collective-permute-start(bf16[8,64,128]{2,1,0:T(8,128)(2,1)S(1)} %collective-permute-done.10.refs_3_), channel_id=1, source_target_pairs={{0,1},{1,0},{2,3},{3,2},{4,5},{5,4},{6,7},{7,6},{8,9},{9,8},{10,11... | collective-permute-start | bytes 393224 | tf_op jit(solution)/shard_map/ppermute | solution.py:165

commit v8 on v7

--- a/solution.py
+++ b/solution.py
@@ -8,7 +8,7 @@
 from jax.sharding import PartitionSpec as P
 
 VMEM_LIMIT = 48 * 1024 * 1024
-GROUP = 4
+GROUP = 8
 FAR, NEAR, CROSS, CORE = 8, 4, 2, 1
 LATE = (FAR | CORE, FAR | NEAR | CORE, FAR | CROSS | CORE, FAR | NEAR | CROSS, FAR | NEAR | CROSS | CORE)
 EARLY = tuple(r for r in range(16) if r not in LATE)
@@ -39,42 +39,36 @@
         pairs_ref[p] = both.astype(jnp.bfloat16)
 
 
-def left_kernel(
-    pair_count, dims_hbm, active_hbm, slot_hbm, left_hbm, psi_hbm,
-    half_ref, dims_ref, active_ref, slot_ref, left_ref, psi_ref, sems, psi_sems,
-):
+def left_kernel(dims_hbm, active_hbm, left_hbm, psi_hbm, half_ref, dims_ref, active_ref, left_ref, psi_ref, sems, psi_sems):
     sectors, blocks, tile, width = psi_ref.shape
     copies = load_all(
         (dims_hbm, dims_ref, sems.at[0]),
         (active_hbm, active_ref, sems.at[1]),
-        (slot_hbm, slot_ref, sems.at[2]),
-        (left_hbm, left_ref, sems.at[3]),
+        (left_hbm, left_ref, sems.at[2]),
     )
     psi_copies = load_all(*[(psi_hbm.at[a], psi_ref.at[a], psi_sems.at[a]) for a in range(sectors)])
     rows = lax.broadcasted_iota(jnp.int32, (tile, tile), 0)
     cols = lax.broadcasted_iota(jnp.int32, (tile, tile), 1)
     most = jnp.maximum(rows, cols)
-    upper = (lax.broadcasted_iota(jnp.int32, (tile, width), 1) >= tile).astype(jnp.int32)
     for copy in copies:
         copy.wait()
     for a in range(sectors):
         psi_copies[a].wait()
         op = jnp.where(most < dims_ref[a], left_ref[a].astype(jnp.float32), 0.0).astype(jnp.bfloat16)
-        for k in range(blocks):
-            part = jnp.dot(op, psi_ref[a, k], preferred_element_type=jnp.float32)
-            part = part * active_ref[a, k].astype(jnp.float32)
-            other = pltpu.roll(part, tile, 1)
-            here = upper == (slot_ref[a, k] >= pair_count).astype(jnp.int32)
-            first = jnp.where(upper == 0, part, other)
-            last = jnp.where(upper == 0, other, part)
-            half_ref[a, k, :, :width] = jnp.where(here, first, 0.0).astype(jnp.bfloat16)
-            half_ref[a, k, :, width:] = jnp.where(here, last, 0.0).astype(jnp.bfloat16)
-
-
-def times_operator(half, pair):
-    zero = jnp.zeros_like(pair)
-    top = jnp.concatenate([pair, zero], axis=1)
-    low = jnp.concatenate([zero, pair], axis=1)
+        for k in range(0, blocks, 2):
+            both = jnp.concatenate([psi_ref[a, k], psi_ref[a, k + 1]], axis=1)
+            part = jnp.dot(op, both, preferred_element_type=jnp.float32)
+            for u in range(2):
+                active = active_ref[a, k + u].astype(jnp.float32)
+                half_ref[a, k + u] = (part[:, u * width:(u + 1) * width] * active).astype(jnp.bfloat16)
+
+
+def times_operator(half, pair, second):
+    tile, width = pair.shape
+    lower = (lax.broadcasted_iota(jnp.int32, pair.shape, 1) < tile).astype(jnp.bfloat16)
+    other = pltpu.roll(pair, tile, 1)
+    top = jnp.where(second, other, pair) * lower
+    low = jnp.where(second, pair, other) * (1 - lower)
     both = jnp.concatenate([top, low], axis=0)
     part = lax.dot_general(half, both, (((1,), (1,)), ((), ())), preferred_element_type=jnp.float32)
     return part.astype(jnp.bfloat16)
@@ -113,11 +107,12 @@
         for k in range(blocks):
             owner, slot = owner_ref[a, k], slot_ref[a, k]
             at = piece_at(owner ^ me) if len(piece_refs) > 1 else owner
-            at = at * pair_count + jnp.where(slot >= pair_count, slot - pair_count, slot)
+            second = slot >= pair_count
+            at = at * pair_count + jnp.where(second, slot - pair_count, slot)
             late = at >= held
             pair = pairs_ref[jnp.where(late, 0, at)]
-            out_ref[a, k] = times_operator(half_ref[a, k], pair)
-            late_ref[listed] = (at - held) * items + a * blocks + k
+            out_ref[a, k] = times_operator(half_ref[a, k], pair, second)
+            late_ref[listed] = ((at - held) * 2 + second.astype(jnp.int32)) * items + a * blocks + k
             listed = listed + late.astype(jnp.int32)
         store(a).start()
         return listed
@@ -143,7 +138,9 @@
             slot = g * GROUP + u
             entry = late_ref[jnp.minimum(slot, listed - 1)]
             item = entry % items
-            out_ref[slot] = times_operator(half_ref[item // blocks, item % blocks], pairs_ref[entry // items])
+            at = entry // items
+            half = half_ref[item // blocks, item % blocks]
+            out_ref[slot] = times_operator(half, pairs_ref[at // 2], at % 2 == 1)
         for u in range(GROUP):
             slot = g * GROUP + u
 
@@ -199,22 +196,21 @@
     def half_of(dims_left):
         active = term_active.reshape(left_count, block_count)
         return pl.pallas_call(
-            functools.partial(left_kernel, pair_count),
-            out_shape=jax.ShapeDtypeStruct((left_count, block_count, tile, 2 * width), jnp.bfloat16),
-            in_specs=[hbm] * 5,
+            left_kernel,
+            out_shape=jax.ShapeDtypeStruct(psi.shape, jnp.bfloat16),
+            in_specs=[hbm] * 4,
             out_specs=vmem,
             scratch_shapes=[
                 pltpu.SMEM(dims_left.shape, jnp.int32),
                 pltpu.SMEM(active.shape, jnp.int32),
-                pltpu.SMEM(right_slot.shape, jnp.int32),
                 pltpu.VMEM(left_ops.shape, jnp.bfloat16),
                 pltpu.VMEM(psi.shape, jnp.bfloat16),
-                pltpu.SemaphoreType.DMA((4,)),
+                pltpu.SemaphoreType.DMA((3,)),
                 pltpu.SemaphoreType.DMA((left_count,)),
             ],
             compiler_params=params,
             cost_estimate=pl.CostEstimate(flops=flops, bytes_accessed=2 * psi.size, transcendentals=0),
-        )(*in_hbm(dims_left, active, right_slot, left_ops, psi))
+        )(*in_hbm(dims_left, active, left_ops, psi))
 
     if by_swaps:
         pieces = {0: pairs}

time: 29.8 us -> 29.1 us (0.977)
  waiting for transfers between devices: 5.25 us -> 4.59 us
  starting transfers between devices: 12.8 us -> 13.3 us
    pallas_call x1, Pallas kernels: 3.52 us -> 2.73 us  [half_of(): pl.pallas_call(left_kernel, out_shape=jax.ShapeDtypeStruct(psi.shape, jnp...]
    ppermute x15, waiting for transfers between devices: 5.25 us -> 4.59 us  [swap(): return lax.ppermute(piece, 'sec', [(i, i ^ bit) for i in range(count)])]
    ppermute x15, starting transfers between devices: 12.8 us -> 13.3 us  [swap(): return lax.ppermute(piece, 'sec', [(i, i ^ bit) for i in range(count)])]
    pallas_call x1, Pallas kernels: 2.67 us -> 3.03 us  [per_device(): pl.pallas_call(late_kernel, out_shape=jax.ShapeDtypeStruct(psi.shape, jnp...]
  transfers between devices with their start and end apart: 15 -> 15, of which waited for: 8 -> 7; matrix products, arithmetic and copies ran while one was open for 0% -> 0% of each run, Pallas kernels for 26% -> 24%
where the time goes in v8:
time: 29.1 us; the launch traced here: 29 us
  starting transfers between devices  13.3 us (46%)
  Pallas kernels  11.1 us (38%)
  waiting for transfers between devices  4.59 us (16%)
    ppermute x15, starting transfers between devices, swap(): return lax.ppermute(piece, 'sec', [(i, i ^ bit) for i in range(count)])  13.3 us
    ppermute x15, waiting for transfers between devices, swap(): return lax.ppermute(piece, 'sec', [(i, i ^ bit) for i in range(count)])  4.59 us
    pallas_call x1, Pallas kernels, per_device(): pl.pallas_call(functools.partial(early_kernel, pair_count), out_shape=(ja...  4.22 us
    pallas_call x1, Pallas kernels, per_device(): pl.pallas_call(late_kernel, out_shape=jax.ShapeDtypeStruct(psi.shape, jnp...  3.03 us
    pallas_call x1, Pallas kernels, half_of(): pl.pallas_call(left_kernel, out_shape=jax.ShapeDtypeStruct(psi.shape, jnp...  2.73 us
    pallas_call x1, Pallas kernels, per_device(): pl.pallas_call(pack_kernel, out_shape=jax.ShapeDtypeStruct((pair_count, t...  1.08 us
  transfers between devices with their start and end apart: 15, of which 7 were waited for; matrix products, arithmetic and copies ran while one was open for 0% of the time, Pallas kernels for 24%

profile of v8, /device:TPU:0, one launch (start us, length us, event | category | flops | bytes accessed | tf_op | source)
XLA Modules:
  0.0 29.0 jit_solution(13634418325673850342)
XLA Ops:
  0.0 1.1 %shard_map.82.refs_0_ = bf16[8,64,128]{2,1,0:T(8,128)(2,1)S(1)} custom-call(s32[16]{0:T(128)} %dims_hbm.1, bf16[16,64,64]{2,1,0:T(8,128)(2,1)} %right_hbm.1), custom_call_target="tpu_custom_call" | custom-call | bytes 131072 | tf_op jit(solution)/shard_map/pallas_call | solution.py:182
  1.1 3.1 %collective-permute-start.1 = (bf16[8,64,128]{2,1,0:T(8,128)(2,1)S(1)}, bf16[8,64,128]{2,1,0:T(8,128)(2,1)S(1)}, u32[]{:S(2)}, u32[]{:S(2)}) collective-permute-start(bf16[8,64,128]{2,1,0:T(8,128)(2,1)S(1)} %shard_map.82.refs_0_), channel_id=1, source_target_pairs={{0,4},{1,5},{2,6},{3,7},{4,0},{5,1},{6,2},{7,3},{8,12},{9,13},{10,... | collective-permute-start | bytes 393224 | tf_op jit(solution)/shard_map/ppermute | solution.py:162
  4.2 2.6 %collective-permute-start = (bf16[8,64,128]{2,1,0:T(8,128)(2,1)S(1)}, bf16[8,64,128]{2,1,0:T(8,128)(2,1)S(1)}, u32[]{:S(2)}, u32[]{:S(2)}) collective-permute-start(bf16[8,64,128]{2,1,0:T(8,128)(2,1)S(1)} %shard_map.82.refs_0_), channel_id=1, source_target_pairs={{0,8},{1,9},{2,10},{3,11},{4,12},{5,13},{6,14},{7,15},{8,0},{9,1},... | collective-permute-start | bytes 393224 | tf_op jit(solution)/shard_map/ppermute | solution.py:162
  6.8 1.5 %collective-permute-start.2 = (bf16[8,64,128]{2,1,0:T(8,128)(2,1)S(1)}, bf16[8,64,128]{2,1,0:T(8,128)(2,1)S(1)}, u32[]{:S(2)}, u32[]{:S(2)}) collective-permute-start(bf16[8,64,128]{2,1,0:T(8,128)(2,1)S(1)} %shard_map.82.refs_0_), channel_id=1, source_target_pairs={{0,2},{1,3},{2,0},{3,1},{4,6},{5,7},{6,4},{7,5},{8,10},{9,11},{10,... | collective-permute-start | bytes 393224 | tf_op jit(solution)/shard_map/ppermute | solution.py:162
  8.3 1.3 %collective-permute-done.1.refs_4_ = bf16[8,64,128]{2,1,0:T(8,128)(2,1)S(1)} collective-permute-done((bf16[8,64,128]{2,1,0:T(8,128)(2,1)S(1)}, bf16[8,64,128]{2,1,0:T(8,128)(2,1)S(1)}, u32[]{:S(2)}, u32[]{:S(2)}) %collective-permute-start.1) | collective-permute-done | bytes 131104 | tf_op jit(solution)/shard_map/ppermute | solution.py:162
  9.5 1.8 %collective-permute-start.3 = (bf16[8,64,128]{2,1,0:T(8,128)(2,1)S(1)}, bf16[8,64,128]{2,1,0:T(8,128)(2,1)S(1)}, u32[]{:S(2)}, u32[]{:S(2)}) collective-permute-start(bf16[8,64,128]{2,1,0:T(8,128)(2,1)S(1)} %collective-permute-done.1.refs_4_), channel_id=1, source_target_pairs={{0,2},{1,3},{2,0},{3,1},{4,6},{5,7},{6,4},{7,5},{8,10},{9,11},{10,... | collective-permute-start | bytes 393224 | tf_op jit(solution)/shard_map/ppermute | solution.py:162
  11.3 0.0 collective-permute-start.4
  11.3 1.6 %collective-permute-done.refs_8_ = bf16[8,64,128]{2,1,0:T(8,128)(2,1)S(1)} collective-permute-done((bf16[8,64,128]{2,1,0:T(8,128)(2,1)S(1)}, bf16[8,64,128]{2,1,0:T(8,128)(2,1)S(1)}, u32[]{:S(2)}, u32[]{:S(2)}) %collective-permute-start) | collective-permute-done | bytes 131104 | tf_op jit(solution)/shard_map/ppermute | solution.py:162
  12.9 0.4 %collective-permute-start.9 = (bf16[8,64,128]{2,1,0:T(8,128)(2,1)S(1)}, bf16[8,64,128]{2,1,0:T(8,128)(2,1)S(1)}, u32[]{:S(2)}, u32[]{:S(2)}) collective-permute-start(bf16[8,64,128]{2,1,0:T(8,128)(2,1)S(1)} %collective-permute-done.refs_8_), channel_id=1, source_target_pairs={{0,4},{1,5},{2,6},{3,7},{4,0},{5,1},{6,2},{7,3},{8,12},{9,13},{10,... | collective-permute-start | bytes 393224 | tf_op jit(solution)/shard_map/ppermute | solution.py:162
  13.3 1.5 %collective-permute-start.8 = (bf16[8,64,128]{2,1,0:T(8,128)(2,1)S(1)}, bf16[8,64,128]{2,1,0:T(8,128)(2,1)S(1)}, u32[]{:S(2)}, u32[]{:S(2)}) collective-permute-start(bf16[8,64,128]{2,1,0:T(8,128)(2,1)S(1)} %collective-permute-done.refs_8_), channel_id=1, source_target_pairs={{0,2},{1,3},{2,0},{3,1},{4,6},{5,7},{6,4},{7,5},{8,10},{9,11},{10,... | collective-permute-start | bytes 393224 | tf_op jit(solution)/shard_map/ppermute | solution.py:162
  14.8 2.7 %shard_map.83.half_ref = bf16[8,8,64,128]{3,2,1,0:T(8,128)(2,1)S(1)} custom-call(s32[8]{0:T(128)} %dims_hbm.2, s32[8,8]{1,0:T(8,128)} %bitcast.1, bf16[8,64,64]{2,1,0:T(8,128)(2,1)} %left_hbm.1, bf16[8,8,64,128]{3,2,1,0:T(8,128)(2,1)} %psi_hbm.1), custom_call_target="tpu_custom_call" | custom-call | flops 67108864 | bytes 1048576 | tf_op jit(solution)/shard_map/pallas_call | solution.py:198
  17.6 0.0 collective-permute-done.2.refs_2_
  17.6 0.0 collective-permute-done.3.refs_6_
  17.6 0.1 collective-permute-start.5
  17.7 0.5 %collective-permute-start.6 = (bf16[8,64,128]{2,1,0:T(8,128)(2,1)S(1)}, bf16[8,64,128]{2,1,0:T(8,128)(2,1)S(1)}, u32[]{:S(2)}, u32[]{:S(2)}) collective-permute-start(bf16[8,64,128]{2,1,0:T(8,128)(2,1)S(1)} %collective-permute-done.1.refs_4_), channel_id=1, source_target_pairs={{0,1},{1,0},{2,3},{3,2},{4,5},{5,4},{6,7},{7,6},{8,9},{9,8},{10,11... | collective-permute-start | bytes 393224 | tf_op jit(solution)/shard_map/ppermute | solution.py:162
  18.2 0.0 collective-permute-done.4.refs_1_
  18.2 0.1 collective-permute-start.7
  18.2 0.0 collective-permute-done.9.refs_10_
  18.2 1.1 %collective-permute-start.10 = (bf16[8,64,128]{2,1,0:T(8,128)(2,1)S(1)}, bf16[8,64,128]{2,1,0:T(8,128)(2,1)S(1)}, u32[]{:S(2)}, u32[]{:S(2)}) collective-permute-start(bf16[8,64,128]{2,1,0:T(8,128)(2,1)S(1)} %collective-permute-done.9.refs_10_), channel_id=1, source_target_pairs={{0,2},{1,3},{2,0},{3,1},{4,6},{5,7},{6,4},{7,5},{8,10},{9,11},{10,... | collective-permute-start | bytes 393224 | tf_op jit(solution)/shard_map/ppermute | solution.py:162
  19.3 0.0 collective-permute-done.8.refs_9_
  19.3 0.0 collective-permute-start.12
  19.4 0.0 collective-permute-done.5.refs_3_
  19.4 0.0 collective-permute-done.6.refs_5_
  19.4 0.1 collective-permute-done.7.refs_7_
  19.5 4.2 %shard_map.84 = (bf16[8,8,64,128]{3,2,1,0:T(8,128)(2,1)}, s32[65]{0:T(128)S(1)}) custom-call(s32[8,8]{1,0:T(8,128)} %owner_hbm.1, s32[8,8]{1,0:T(8,128)} %slot_hbm.1, bf16[8,8,64,128]{3,2,1,0:T(8,128)(2,1)S(1)} %shard_map.83.half_ref, bf16[8,64,128]{2,1,0:T(8,128)(2,1)S(1)} %shard_map.82.refs_0_, bf16[8,64,128]{2,1,0:T(8,128)(2,1)S(1)} %collective-permute-done.4.refs_1_, ...), custom_call_target="tpu_custom_call" | custom-call | flops 67108864 | bytes 1048576 | tf_op jit(solution)/shard_map/pallas_call | solution.py:233
  23.7 0.4 %collective-permute-done.10.refs_3_ = bf16[8,64,128]{2,1,0:T(8,128)(2,1)S(1)} collective-permute-done((bf16[8,64,128]{2,1,0:T(8,128)(2,1)S(1)}, bf16[8,64,128]{2,1,0:T(8,128)(2,1)S(1)}, u32[]{:S(2)}, u32[]{:S(2)}) %collective-permute-start.10) | collective-permute-done | bytes 131104 | tf_op jit(solution)/shard_map/ppermute | solution.py:162
  24.1 0.1 collective-permute-start.11
  24.2 0.4 %collective-permute-start.13 = (bf16[8,64,128]{2,1,0:T(8,128)(2,1)S(1)}, bf16[8,64,128]{2,1,0:T(8,128)(2,1)S(1)}, u32[]{:S(2)}, u32[]{:S(2)}) collective-permute-start(bf16[8,64,128]{2,1,0:T(8,128)(2,1)S(1)} %collective-permute-done.8.refs_9_), channel_id=1, source_target_pairs={{0,1},{1,0},{2,3},{3,2},{4,5},{5,4},{6,7},{7,6},{8,9},{9,8},{10,11... | collective-permute-start | bytes 393224 | tf_op jit(solution)/shard_map/ppermute | solution.py:162
  24.6 0.1 collective-permute-start.14
  24.7 0.0 collective-permute-done.12.refs_1_
  24.7 0.7 %collective-permute-done.11.refs_0_ = bf16[8,64,128]{2,1,0:T(8,128)(2,1)S(1)} collective-permute-done((bf16[8,64,128]{2,1,0:T(8,128)(2,1)S(1)}, bf16[8,64,128]{2,1,0:T(8,128)(2,1)S(1)}, u32[]{:S(2)}, u32[]{:S(2)}) %collective-permute-start.11) | collective-permute-done | bytes 131104 | tf_op jit(solution)/shard_map/ppermute | solution.py:162
  25.4 0.2 collective-permute-done.13.refs_2_
  25.6 0.3 %collective-permute-done.14.refs_4_ = bf16[8,64,128]{2,1,0:T(8,128)(2,1)S(1)} collective-permute-done((bf16[8,64,128]{2,1,0:T(8,128)(2,1)S(1)}, bf16[8,64,128]{2,1,0:T(8,128)(2,1)S(1)}, u32[]{:S(2)}, u32[]{:S(2)}) %collective-permute-start.14) | collective-permute-done | bytes 131104 | tf_op jit(solution)/shard_map/ppermute | solution.py:162
  26.0 3.0 %shard_map.85 = bf16[8,8,64,128]{3,2,1,0:T(8,128)(2,1)} custom-call(s32[65]{0:T(128)S(1)} %get-tuple-element.23.late_ref, bf16[8,8,64,128]{3,2,1,0:T(8,128)(2,1)} %get-tuple-element.25.early_hbm, bf16[8,8,64,128]{3,2,1,0:T(8,128)(2,1)S(1)} %shard_map.83.half_ref, ...), custom_call_target="tpu_custom_call", output_to_operand_aliasing={{}: (1, {})} | custom-call | flops 16777216 | bytes 524288 | tf_op jit(solution)/shard_map/pallas_call | solution.py:257
Async XLA Ops:
  1.1 8.4 %collective-permute-start.1 = (bf16[8,64,128]{2,1,0:T(8,128)(2,1)S(1)}, bf16[8,64,128]{2,1,0:T(8,128)(2,1)S(1)}, u32[]{:S(2)}, u32[]{:S(2)}) collective-permute-start(bf16[8,64,128]{2,1,0:T(8,128)(2,1)S(1)} %shard_map.82.refs_0_), channel_id=1, source_target_pairs={{0,4},{1,5},{2,6},{3,7},{4,0},{5,1},{6,2},{7,3},{8,12},{9,13},{10,... | collective-permute-start | bytes 393224 | tf_op jit(solution)/shard_map/ppermute | solution.py:162
  4.2 8.7 %collective-permute-start = (bf16[8,64,128]{2,1,0:T(8,128)(2,1)S(1)}, bf16[8,64,128]{2,1,0:T(8,128)(2,1)S(1)}, u32[]{:S(2)}, u32[]{:S(2)}) collective-permute-start(bf16[8,64,128]{2,1,0:T(8,128)(2,1)S(1)} %shard_map.82.refs_0_), channel_id=1, source_target_pairs={{0,8},{1,9},{2,10},{3,11},{4,12},{5,13},{6,14},{7,15},{8,0},{9,1},... | collective-permute-start | bytes 393224 | tf_op jit(solution)/shard_map/ppermute | solution.py:162
  6.8 10.8 %collective-permute-start.2 = (bf16[8,64,128]{2,1,0:T(8,128)(2,1)S(1)}, bf16[8,64,128]{2,1,0:T(8,128)(2,1)S(1)}, u32[]{:S(2)}, u32[]{:S(2)}) collective-permute-start(bf16[8,64,128]{2,1,0:T(8,128)(2,1)S(1)} %shard_map.82.refs_0_), channel_id=1, source_target_pairs={{0,2},{1,3},{2,0},{3,1},{4,6},{5,7},{6,4},{7,5},{8,10},{9,11},{10,... | collective-permute-start | bytes 393224 | tf_op jit(solution)/shard_map/ppermute | solution.py:162
  9.5 8.1 %collective-permute-start.3 = (bf16[8,64,128]{2,1,0:T(8,128)(2,1)S(1)}, bf16[8,64,128]{2,1,0:T(8,128)(2,1)S(1)}, u32[]{:S(2)}, u32[]{:S(2)}) collective-permute-start(bf16[8,64,128]{2,1,0:T(8,128)(2,1)S(1)} %collective-permute-done.1.refs_4_), channel_id=1, source_target_pairs={{0,2},{1,3},{2,0},{3,1},{4,6},{5,7},{6,4},{7,5},{8,10},{9,11},{10,... | collective-permute-start | bytes 393224 | tf_op jit(solution)/shard_map/ppermute | solution.py:162
  11.3 6.8 %collective-permute-start.4 = (bf16[8,64,128]{2,1,0:T(8,128)(2,1)S(1)}, bf16[8,64,128]{2,1,0:T(8,128)(2,1)S(1)}, u32[]{:S(2)}, u32[]{:S(2)}) collective-permute-start(bf16[8,64,128]{2,1,0:T(8,128)(2,1)S(1)} %shard_map.82.refs_0_), channel_id=1, source_target_pairs={{0,1},{1,0},{2,3},{3,2},{4,5},{5,4},{6,7},{7,6},{8,9},{9,8},{10,11... | collective-permute-start | bytes 393224 | tf_op jit(solution)/shard_map/ppermute | solution.py:162
  12.9 5.4 %collective-permute-start.9 = (bf16[8,64,128]{2,1,0:T(8,128)(2,1)S(1)}, bf16[8,64,128]{2,1,0:T(8,128)(2,1)S(1)}, u32[]{:S(2)}, u32[]{:S(2)}) collective-permute-start(bf16[8,64,128]{2,1,0:T(8,128)(2,1)S(1)} %collective-permute-done.refs_8_), channel_id=1, source_target_pairs={{0,4},{1,5},{2,6},{3,7},{4,0},{5,1},{6,2},{7,3},{8,12},{9,13},{10,... | collective-permute-start | bytes 393224 | tf_op jit(solution)/shard_map/ppermute | solution.py:162
  13.3 6.0 %collective-permute-start.8 = (bf16[8,64,128]{2,1,0:T(8,128)(2,1)S(1)}, bf16[8,64,128]{2,1,0:T(8,128)(2,1)S(1)}, u32[]{:S(2)}, u32[]{:S(2)}) collective-permute-start(bf16[8,64,128]{2,1,0:T(8,128)(2,1)S(1)} %collective-permute-done.refs_8_), channel_id=1, source_target_pairs={{0,2},{1,3},{2,0},{3,1},{4,6},{5,7},{6,4},{7,5},{8,10},{9,11},{10,... | collective-permute-start | bytes 393224 | tf_op jit(solution)/shard_map/ppermute | solution.py:162
  17.6 1.8 %collective-permute-start.5 = (bf16[8,64,128]{2,1,0:T(8,128)(2,1)S(1)}, bf16[8,64,128]{2,1,0:T(8,128)(2,1)S(1)}, u32[]{:S(2)}, u32[]{:S(2)}) collective-permute-start(bf16[8,64,128]{2,1,0:T(8,128)(2,1)S(1)} %collective-permute-done.2.refs_2_), channel_id=1, source_target_pairs={{0,1},{1,0},{2,3},{3,2},{4,5},{5,4},{6,7},{7,6},{8,9},{9,8},{10,11... | collective-permute-start | bytes 393224 | tf_op jit(solution)/shard_map/ppermute | solution.py:162
  17.7 1.7 %collective-permute-start.6 = (bf16[8,64,128]{2,1,0:T(8,128)(2,1)S(1)}, bf16[8,64,128]{2,1,0:T(8,128)(2,1)S(1)}, u32[]{:S(2)}, u32[]{:S(2)}) collective-permute-start(bf16[8,64,128]{2,1,0:T(8,128)(2,1)S(1)} %collective-permute-done.1.refs_4_), channel_id=1, source_target_pairs={{0,1},{1,0},{2,3},{3,2},{4,5},{5,4},{6,7},{7,6},{8,9},{9,8},{10,11... | collective-permute-start | bytes 393224 | tf_op jit(solution)/shard_map/ppermute | solution.py:162
  18.2 1.3 %collective-permute-start.7 = (bf16[8,64,128]{2,1,0:T(8,128)(2,1)S(1)}, bf16[8,64,128]{2,1,0:T(8,128)(2,1)S(1)}, u32[]{:S(2)}, u32[]{:S(2)}) collective-permute-start(bf16[8,64,128]{2,1,0:T(8,128)(2,1)S(1)} %collective-permute-done.3.refs_6_), channel_id=1, source_target_pairs={{0,1},{1,0},{2,3},{3,2},{4,5},{5,4},{6,7},{7,6},{8,9},{9,8},{10,11... | collective-permute-start | bytes 393224 | tf_op jit(solution)/shard_map/ppermute | solution.py:162
  18.2 5.8 %collective-permute-start.10 = (bf16[8,64,128]{2,1,0:T(8,128)(2,1)S(1)}, bf16[8,64,128]{2,1,0:T(8,128)(2,1)S(1)}, u32[]{:S(2)}, u32[]{:S(2)}) collective-permute-start(bf16[8,64,128]{2,1,0:T(8,128)(2,1)S(1)} %collective-permute-done.9.refs_10_), channel_id=1, source_target_pairs={{0,2},{1,3},{2,0},{3,1},{4,6},{5,7},{6,4},{7,5},{8,10},{9,11},{10,... | collective-permute-start | bytes 393224 | tf_op jit(solution)/shard_map/ppermute | solution.py:162
  19.3 5.3 %collective-permute-start.12 = (bf16[8,64,128]{2,1,0:T(8,128)(2,1)S(1)}, bf16[8,64,128]{2,1,0:T(8,128)(2,1)S(1)}, u32[]{:S(2)}, u32[]{:S(2)}) collective-permute-start(bf16[8,64,128]{2,1,0:T(8,128)(2,1)S(1)} %collective-permute-done.9.refs_10_), channel_id=1, source_target_pairs={{0,1},{1,0},{2,3},{3,2},{4,5},{5,4},{6,7},{7,6},{8,9},{9,8},{10,11... | collective-permute-start | bytes 393224 | tf_op jit(solution)/shard_map/ppermute | solution.py:162
  24.1 1.3 %collective-permute-start.11 = (bf16[8,64,128]{2,1,0:T(8,128)(2,1)S(1)}, bf16[8,64,128]{2,1,0:T(8,128)(2,1)S(1)}, u32[]{:S(2)}, u32[]{:S(2)}) collective-permute-start(bf16[8,64,128]{2,1,0:T(8,128)(2,1)S(1)} %collective-permute-done.refs_8_), channel_id=1, source_target_pairs={{0,1},{1,0},{2,3},{3,2},{4,5},{5,4},{6,7},{7,6},{8,9},{9,8},{10,11... | collective-permute-start | bytes 393224 | tf_op jit(solution)/shard_map/ppermute | solution.py:162
  24.2 1.4 %collective-permute-start.13 = (bf16[8,64,128]{2,1,0:T(8,128)(2,1)S(1)}, bf16[8,64,128]{2,1,0:T(8,128)(2,1)S(1)}, u32[]{:S(2)}, u32[]{:S(2)}) collective-permute-start(bf16[8,64,128]{2,1,0:T(8,128)(2,1)S(1)} %collective-permute-done.8.refs_9_), channel_id=1, source_target_pairs={{0,1},{1,0},{2,3},{3,2},{4,5},{5,4},{6,7},{7,6},{8,9},{9,8},{10,11... | collective-permute-start | bytes 393224 | tf_op jit(solution)/shard_map/ppermute | solution.py:162
  24.6 1.3 %collective-permute-start.14 = (bf16[8,64,128]{2,1,0:T(8,128)(2,1)S(1)}, bf16[8,64,128]{2,1,0:T(8,128)(2,1)S(1)}, u32[]{:S(2)}, u32[]{:S(2)}) collective-permute-start(bf16[8,64,128]{2,1,0:T(8,128)(2,1)S(1)} %collective-permute-done.10.refs_3_), channel_id=1, source_target_pairs={{0,1},{1,0},{2,3},{3,2},{4,5},{5,4},{6,7},{7,6},{8,9},{9,8},{10,11... | collective-permute-start | bytes 393224 | tf_op jit(solution)/shard_map/ppermute | solution.py:162

commit v9 on v8

--- a/solution.py
+++ b/solution.py
@@ -35,8 +35,8 @@
         return jnp.where(most < dims_ref[b], right_ref[b].astype(jnp.float32), 0.0)
 
     for p in range(count):
-        both = jnp.concatenate([kept(p), kept(p + count)], axis=1)
-        pairs_ref[p] = both.astype(jnp.bfloat16)
+        both = jnp.concatenate([kept(p), kept(p + count)], axis=0)
+        pairs_ref[p] = both.T.astype(jnp.bfloat16)
 
 
 def left_kernel(dims_hbm, active_hbm, left_hbm, psi_hbm, half_ref, dims_ref, active_ref, left_ref, psi_ref, sems, psi_sems):
@@ -63,15 +63,23 @@
                 half_ref[a, k + u] = (part[:, u * width:(u + 1) * width] * active).astype(jnp.bfloat16)
 
 
-def times_operator(half, pair, second):
+def block_form(pair, second):
     tile, width = pair.shape
     lower = (lax.broadcasted_iota(jnp.int32, pair.shape, 1) < tile).astype(jnp.bfloat16)
     other = pltpu.roll(pair, tile, 1)
     top = jnp.where(second, other, pair) * lower
     low = jnp.where(second, pair, other) * (1 - lower)
+    return jnp.concatenate([top, low], axis=0)
+
+
+def two_products(halves, forms):
+    zero = jnp.zeros_like(forms[0])
+    top = jnp.concatenate([forms[0], zero], axis=1)
+    low = jnp.concatenate([zero, forms[1]], axis=1)
     both = jnp.concatenate([top, low], axis=0)
-    part = lax.dot_general(half, both, (((1,), (1,)), ((), ())), preferred_element_type=jnp.float32)
-    return part.astype(jnp.bfloat16)
+    part = jnp.dot(jnp.concatenate(halves, axis=1), both, preferred_element_type=jnp.float32)
+    width = part.shape[1] // 2
+    return part[:, :width].astype(jnp.bfloat16), part[:, width:].astype(jnp.bfloat16)
 
 
 def merge(piece_refs, pairs_ref):
@@ -104,16 +112,18 @@
         return pltpu.make_async_copy(out_ref.at[a], out_hbm.at[a], sems.at[a])
 
     def one(a, listed):
-        for k in range(blocks):
-            owner, slot = owner_ref[a, k], slot_ref[a, k]
-            at = piece_at(owner ^ me) if len(piece_refs) > 1 else owner
-            second = slot >= pair_count
-            at = at * pair_count + jnp.where(second, slot - pair_count, slot)
-            late = at >= held
-            pair = pairs_ref[jnp.where(late, 0, at)]
-            out_ref[a, k] = times_operator(half_ref[a, k], pair, second)
-            late_ref[listed] = ((at - held) * 2 + second.astype(jnp.int32)) * items + a * blocks + k
-            listed = listed + late.astype(jnp.int32)
+        for k in range(0, blocks, 2):
+            forms = []
+            for u in range(2):
+                owner, slot = owner_ref[a, k + u], slot_ref[a, k + u]
+                at = piece_at(owner ^ me) if len(piece_refs) > 1 else owner
+                second = slot >= pair_count
+                at = at * pair_count + jnp.where(second, slot - pair_count, slot)
+                late = at >= held
+                forms.append(block_form(pairs_ref[jnp.where(late, 0, at)], second))
+                late_ref[listed] = ((at - held) * 2 + second.astype(jnp.int32)) * items + a * blocks + k + u
+                listed = listed + late.astype(jnp.int32)
+            out_ref[a, k], out_ref[a, k + 1] = two_products([half_ref[a, k], half_ref[a, k + 1]], forms)
         store(a).start()
         return listed
 
@@ -134,13 +144,15 @@
         return pltpu.make_async_copy(out_ref.at[slot], out_hbm.at[item // blocks, item % blocks], sems.at[slot])
 
     def group(g, carry):
-        for u in range(GROUP):
+        for u in range(0, GROUP, 2):
             slot = g * GROUP + u
-            entry = late_ref[jnp.minimum(slot, listed - 1)]
-            item = entry % items
-            at = entry // items
-            half = half_ref[item // blocks, item % blocks]
-            out_ref[slot] = times_operator(half, pairs_ref[at // 2], at % 2 == 1)
+            entries = [late_ref[jnp.minimum(slot + n, listed - 1)] for n in range(2)]
+            halves, forms = [], []
+            for entry in entries:
+                item, at = entry % items, entry // items
+                halves.append(half_ref[item // blocks, item % blocks])
+                forms.append(block_form(pairs_ref[at // 2], at % 2 == 1))
+            out_ref[slot], out_ref[slot + 1] = two_products(halves, forms)
         for u in range(GROUP):
             slot = g * GROUP + u
 
@@ -219,12 +231,14 @@
                 pieces[r | bit] = swap(pieces[r], bit)
 
         pass_on((0, FAR), (0, NEAR), (0, CROSS), (0, CORE), (NEAR, CROSS), (FAR, NEAR), (FAR, CROSS), (FAR | NEAR, CROSS))
-        dims_left, pieces[FAR] = lax.optimization_barrier((dims_left, pieces[FAR]))
+        held = (FAR,)
+        dims_left, ends = lax.optimization_barrier((dims_left, [pieces[r] for r in held]))
+        pieces.update(zip(held, ends))
         half = half_of(dims_left)
         held = (NEAR, CROSS, NEAR | CROSS,)
         half, ends = lax.optimization_barrier((half, [pieces[r] for r in held]))
         pieces.update(zip(held, ends))
-        pass_on((NEAR, CORE), (CROSS, CORE), (NEAR | CROSS, CORE), (FAR | NEAR, CORE))
+        pass_on((NEAR, CORE), (CROSS, CORE), (NEAR | CROSS, CORE), (FAR | NEAR, CORE), (FAR, CORE), (FAR | CROSS, CORE))
         early = [pieces[r] for r in EARLY]
     else:
         half = half_of(dims_left)
@@ -249,7 +263,7 @@
         cost_estimate=pl.CostEstimate(flops=flops, bytes_accessed=2 * psi.size, transcendentals=0),
     )(*in_hbm(right_owner, right_slot), half, *early)
     if by_swaps:
-        ends = (FAR, FAR | CROSS, FAR | NEAR | CROSS,)
+        ends = (FAR | NEAR | CROSS,)
         held, sigma = lax.optimization_barrier(([pieces[r] for r in ends], sigma))
         for r, piece in zip(ends, held):
             pieces[r], pieces[r | CORE] = piece, swap(piece, CORE)

time: 29.1 us -> 28.3 us (0.973)
  Pallas kernels: 11.1 us -> 10 us
    pallas_call x1, Pallas kernels: 3.03 us -> 2.47 us  [per_device(): pl.pallas_call(late_kernel, out_shape=jax.ShapeDtypeStruct(psi.shape, jnp...]
    pallas_call x1, Pallas kernels: 4.22 us -> 3.75 us  [per_device(): pl.pallas_call(functools.partial(early_kernel, pair_count), out_shape=(ja...]
  transfers between devices with their start and end apart: 15 -> 15, of which waited for: 7 -> 4; matrix products, arithmetic and copies ran while one was open for 0% -> 0% of each run, Pallas kernels for 24% -> 23%
where the time goes in v9:
time: 28.3 us; the launch traced here: 27.9 us
  starting transfers between devices  13.4 us (47%)
  Pallas kernels  10 us (35%)
  waiting for transfers between devices  4.43 us (16%)
    ppermute x15, starting transfers between devices, swap(): return lax.ppermute(piece, 'sec', [(i, i ^ bit) for i in range(count)])  13.4 us
    ppermute x15, waiting for transfers between devices, swap(): return lax.ppermute(piece, 'sec', [(i, i ^ bit) for i in range(count)])  4.43 us
    pallas_call x1, Pallas kernels, per_device(): pl.pallas_call(functools.partial(early_kernel, pair_count), out_shape=(ja...  3.75 us
    pallas_call x1, Pallas kernels, half_of(): pl.pallas_call(left_kernel, out_shape=jax.ShapeDtypeStruct(psi.shape, jnp...  2.72 us
    pallas_call x1, Pallas kernels, per_device(): pl.pallas_call(late_kernel, out_shape=jax.ShapeDtypeStruct(psi.shape, jnp...  2.47 us
    pallas_call x1, Pallas kernels, per_device(): pl.pallas_call(pack_kernel, out_shape=jax.ShapeDtypeStruct((pair_count, t...  1.09 us
  transfers between devices with their start and end apart: 15, of which 4 were waited for; matrix products, arithmetic and copies ran while one was open for 0% of the time, Pallas kernels for 23%

profile of v9, /device:TPU:0, one launch (start us, length us, event | category | flops | bytes accessed | tf_op | source)
XLA Modules:
  0.0 27.9 jit_solution(16926652883378716068)
XLA Ops:
  0.0 1.1 %shard_map.82.refs_0_ = bf16[8,64,128]{2,1,0:T(8,128)(2,1)S(1)} custom-call(s32[16]{0:T(128)} %dims_hbm.1, bf16[16,64,64]{2,1,0:T(8,128)(2,1)} %right_hbm.1), custom_call_target="tpu_custom_call" | custom-call | bytes 131072 | tf_op jit(solution)/shard_map/pallas_call | solution.py:194
  1.1 3.1 %collective-permute-start.1 = (bf16[8,64,128]{2,1,0:T(8,128)(2,1)S(1)}, bf16[8,64,128]{2,1,0:T(8,128)(2,1)S(1)}, u32[]{:S(2)}, u32[]{:S(2)}) collective-permute-start(bf16[8,64,128]{2,1,0:T(8,128)(2,1)S(1)} %shard_map.82.refs_0_), channel_id=1, source_target_pairs={{0,4},{1,5},{2,6},{3,7},{4,0},{5,1},{6,2},{7,3},{8,12},{9,13},{10,... | collective-permute-start | bytes 393224 | tf_op jit(solution)/shard_map/ppermute | solution.py:174
  4.2 2.6 %collective-permute-start = (bf16[8,64,128]{2,1,0:T(8,128)(2,1)S(1)}, bf16[8,64,128]{2,1,0:T(8,128)(2,1)S(1)}, u32[]{:S(2)}, u32[]{:S(2)}) collective-permute-start(bf16[8,64,128]{2,1,0:T(8,128)(2,1)S(1)} %shard_map.82.refs_0_), channel_id=1, source_target_pairs={{0,8},{1,9},{2,10},{3,11},{4,12},{5,13},{6,14},{7,15},{8,0},{9,1},... | collective-permute-start | bytes 393224 | tf_op jit(solution)/shard_map/ppermute | solution.py:174
  6.8 1.5 %collective-permute-start.2 = (bf16[8,64,128]{2,1,0:T(8,128)(2,1)S(1)}, bf16[8,64,128]{2,1,0:T(8,128)(2,1)S(1)}, u32[]{:S(2)}, u32[]{:S(2)}) collective-permute-start(bf16[8,64,128]{2,1,0:T(8,128)(2,1)S(1)} %shard_map.82.refs_0_), channel_id=1, source_target_pairs={{0,2},{1,3},{2,0},{3,1},{4,6},{5,7},{6,4},{7,5},{8,10},{9,11},{10,... | collective-permute-start | bytes 393224 | tf_op jit(solution)/shard_map/ppermute | solution.py:174
  8.3 1.3 %collective-permute-done.1.refs_4_ = bf16[8,64,128]{2,1,0:T(8,128)(2,1)S(1)} collective-permute-done((bf16[8,64,128]{2,1,0:T(8,128)(2,1)S(1)}, bf16[8,64,128]{2,1,0:T(8,128)(2,1)S(1)}, u32[]{:S(2)}, u32[]{:S(2)}) %collective-permute-start.1) | collective-permute-done | bytes 131104 | tf_op jit(solution)/shard_map/ppermute | solution.py:174
  9.5 1.8 %collective-permute-start.3 = (bf16[8,64,128]{2,1,0:T(8,128)(2,1)S(1)}, bf16[8,64,128]{2,1,0:T(8,128)(2,1)S(1)}, u32[]{:S(2)}, u32[]{:S(2)}) collective-permute-start(bf16[8,64,128]{2,1,0:T(8,128)(2,1)S(1)} %collective-permute-done.1.refs_4_), channel_id=1, source_target_pairs={{0,2},{1,3},{2,0},{3,1},{4,6},{5,7},{6,4},{7,5},{8,10},{9,11},{10,... | collective-permute-start | bytes 393224 | tf_op jit(solution)/shard_map/ppermute | solution.py:174
  11.3 0.0 collective-permute-start.4
  11.4 1.6 %collective-permute-done.refs_8_ = bf16[8,64,128]{2,1,0:T(8,128)(2,1)S(1)} collective-permute-done((bf16[8,64,128]{2,1,0:T(8,128)(2,1)S(1)}, bf16[8,64,128]{2,1,0:T(8,128)(2,1)S(1)}, u32[]{:S(2)}, u32[]{:S(2)}) %collective-permute-start) | collective-permute-done | bytes 131104 | tf_op jit(solution)/shard_map/ppermute | solution.py:174
  12.9 0.4 %collective-permute-start.9 = (bf16[8,64,128]{2,1,0:T(8,128)(2,1)S(1)}, bf16[8,64,128]{2,1,0:T(8,128)(2,1)S(1)}, u32[]{:S(2)}, u32[]{:S(2)}) collective-permute-start(bf16[8,64,128]{2,1,0:T(8,128)(2,1)S(1)} %collective-permute-done.refs_8_), channel_id=1, source_target_pairs={{0,4},{1,5},{2,6},{3,7},{4,0},{5,1},{6,2},{7,3},{8,12},{9,13},{10,... | collective-permute-start | bytes 393224 | tf_op jit(solution)/shard_map/ppermute | solution.py:174
  13.4 1.5 %collective-permute-start.8 = (bf16[8,64,128]{2,1,0:T(8,128)(2,1)S(1)}, bf16[8,64,128]{2,1,0:T(8,128)(2,1)S(1)}, u32[]{:S(2)}, u32[]{:S(2)}) collective-permute-start(bf16[8,64,128]{2,1,0:T(8,128)(2,1)S(1)} %collective-permute-done.refs_8_), channel_id=1, source_target_pairs={{0,2},{1,3},{2,0},{3,1},{4,6},{5,7},{6,4},{7,5},{8,10},{9,11},{10,... | collective-permute-start | bytes 393224 | tf_op jit(solution)/shard_map/ppermute | solution.py:174
  14.8 2.7 %shard_map.83.half_ref = bf16[8,8,64,128]{3,2,1,0:T(8,128)(2,1)S(1)} custom-call(s32[8]{0:T(128)} %dims_hbm.2, s32[8,8]{1,0:T(8,128)} %bitcast.1, bf16[8,64,64]{2,1,0:T(8,128)(2,1)} %left_hbm.1, bf16[8,8,64,128]{3,2,1,0:T(8,128)(2,1)} %psi_hbm.1), custom_call_target="tpu_custom_call" | custom-call | flops 67108864 | bytes 1048576 | tf_op jit(solution)/shard_map/pallas_call | solution.py:210
  17.6 0.0 collective-permute-done.2.refs_2_
  17.6 0.0 collective-permute-done.3.refs_6_
  17.6 0.1 collective-permute-start.5
  17.7 0.5 %collective-permute-start.6 = (bf16[8,64,128]{2,1,0:T(8,128)(2,1)S(1)}, bf16[8,64,128]{2,1,0:T(8,128)(2,1)S(1)}, u32[]{:S(2)}, u32[]{:S(2)}) collective-permute-start(bf16[8,64,128]{2,1,0:T(8,128)(2,1)S(1)} %collective-permute-done.1.refs_4_), channel_id=1, source_target_pairs={{0,1},{1,0},{2,3},{3,2},{4,5},{5,4},{6,7},{7,6},{8,9},{9,8},{10,11... | collective-permute-start | bytes 393224 | tf_op jit(solution)/shard_map/ppermute | solution.py:174
  18.2 0.0 collective-permute-done.4.refs_1_
  18.2 0.1 collective-permute-start.7
  18.3 0.0 collective-permute-done.9.refs_10_
  18.3 1.1 %collective-permute-start.10 = (bf16[8,64,128]{2,1,0:T(8,128)(2,1)S(1)}, bf16[8,64,128]{2,1,0:T(8,128)(2,1)S(1)}, u32[]{:S(2)}, u32[]{:S(2)}) collective-permute-start(bf16[8,64,128]{2,1,0:T(8,128)(2,1)S(1)} %collective-permute-done.9.refs_10_), channel_id=1, source_target_pairs={{0,2},{1,3},{2,0},{3,1},{4,6},{5,7},{6,4},{7,5},{8,10},{9,11},{10,... | collective-permute-start | bytes 393224 | tf_op jit(solution)/shard_map/ppermute | solution.py:174
  19.4 0.0 collective-permute-done.8.refs_9_
  19.4 0.0 collective-permute-start.11
  19.4 0.0 collective-permute-done.5.refs_3_
  19.4 0.5 %collective-permute-start.12 = (bf16[8,64,128]{2,1,0:T(8,128)(2,1)S(1)}, bf16[8,64,128]{2,1,0:T(8,128)(2,1)S(1)}, u32[]{:S(2)}, u32[]{:S(2)}) collective-permute-start(bf16[8,64,128]{2,1,0:T(8,128)(2,1)S(1)} %collective-permute-done.9.refs_10_), channel_id=1, source_target_pairs={{0,1},{1,0},{2,3},{3,2},{4,5},{5,4},{6,7},{7,6},{8,9},{9,8},{10,11... | collective-permute-start | bytes 393224 | tf_op jit(solution)/shard_map/ppermute | solution.py:174
  19.9 0.0 collective-permute-done.6.refs_5_
  19.9 0.1 collective-permute-start.13
  20.0 0.0 collective-permute-done.7.refs_7_
  20.0 3.8 %shard_map.84 = (bf16[8,8,64,128]{3,2,1,0:T(8,128)(2,1)}, s32[65]{0:T(128)S(1)}) custom-call(s32[8,8]{1,0:T(8,128)} %owner_hbm.1, s32[8,8]{1,0:T(8,128)} %slot_hbm.1, bf16[8,8,64,128]{3,2,1,0:T(8,128)(2,1)S(1)} %shard_map.83.half_ref, bf16[8,64,128]{2,1,0:T(8,128)(2,1)S(1)} %shard_map.82.refs_0_, bf16[8,64,128]{2,1,0:T(8,128)(2,1)S(1)} %collective-permute-done.4.refs_1_, ...), custom_call_target="tpu_custom_call" | custom-call | flops 67108864 | bytes 1048576 | tf_op jit(solution)/shard_map/pallas_call | solution.py:247
  23.7 0.4 %collective-permute-done.10.refs_3_ = bf16[8,64,128]{2,1,0:T(8,128)(2,1)S(1)} collective-permute-done((bf16[8,64,128]{2,1,0:T(8,128)(2,1)S(1)}, bf16[8,64,128]{2,1,0:T(8,128)(2,1)S(1)}, u32[]{:S(2)}, u32[]{:S(2)}) %collective-permute-start.10) | collective-permute-done | bytes 131104 | tf_op jit(solution)/shard_map/ppermute | solution.py:174
  24.1 0.1 collective-permute-start.14
  24.2 0.0 collective-permute-done.11.refs_0_
  24.2 0.0 collective-permute-done.12.refs_1_
  24.2 0.0 collective-permute-done.13.refs_2_
  24.2 1.2 %collective-permute-done.14.refs_4_ = bf16[8,64,128]{2,1,0:T(8,128)(2,1)S(1)} collective-permute-done((bf16[8,64,128]{2,1,0:T(8,128)(2,1)S(1)}, bf16[8,64,128]{2,1,0:T(8,128)(2,1)S(1)}, u32[]{:S(2)}, u32[]{:S(2)}) %collective-permute-start.14) | collective-permute-done | bytes 131104 | tf_op jit(solution)/shard_map/ppermute | solution.py:174
  25.5 2.5 %shard_map.85 = bf16[8,8,64,128]{3,2,1,0:T(8,128)(2,1)} custom-call(s32[65]{0:T(128)S(1)} %get-tuple-element.21.late_ref, bf16[8,8,64,128]{3,2,1,0:T(8,128)(2,1)} %get-tuple-element.23.early_hbm, bf16[8,8,64,128]{3,2,1,0:T(8,128)(2,1)S(1)} %shard_map.83.half_ref, ...), custom_call_target="tpu_custom_call", output_to_operand_aliasing={{}: (1, {})} | custom-call | flops 16777216 | bytes 524288 | tf_op jit(solution)/shard_map/pallas_call | solution.py:271
Async XLA Ops:
  1.1 8.4 %collective-permute-start.1 = (bf16[8,64,128]{2,1,0:T(8,128)(2,1)S(1)}, bf16[8,64,128]{2,1,0:T(8,128)(2,1)S(1)}, u32[]{:S(2)}, u32[]{:S(2)}) collective-permute-start(bf16[8,64,128]{2,1,0:T(8,128)(2,1)S(1)} %shard_map.82.refs_0_), channel_id=1, source_target_pairs={{0,4},{1,5},{2,6},{3,7},{4,0},{5,1},{6,2},{7,3},{8,12},{9,13},{10,... | collective-permute-start | bytes 393224 | tf_op jit(solution)/shard_map/ppermute | solution.py:174
  4.2 8.7 %collective-permute-start = (bf16[8,64,128]{2,1,0:T(8,128)(2,1)S(1)}, bf16[8,64,128]{2,1,0:T(8,128)(2,1)S(1)}, u32[]{:S(2)}, u32[]{:S(2)}) collective-permute-start(bf16[8,64,128]{2,1,0:T(8,128)(2,1)S(1)} %shard_map.82.refs_0_), channel_id=1, source_target_pairs={{0,8},{1,9},{2,10},{3,11},{4,12},{5,13},{6,14},{7,15},{8,0},{9,1},... | collective-permute-start | bytes 393224 | tf_op jit(solution)/shard_map/ppermute | solution.py:174
  6.8 10.8 %collective-permute-start.2 = (bf16[8,64,128]{2,1,0:T(8,128)(2,1)S(1)}, bf16[8,64,128]{2,1,0:T(8,128)(2,1)S(1)}, u32[]{:S(2)}, u32[]{:S(2)}) collective-permute-start(bf16[8,64,128]{2,1,0:T(8,128)(2,1)S(1)} %shard_map.82.refs_0_), channel_id=1, source_target_pairs={{0,2},{1,3},{2,0},{3,1},{4,6},{5,7},{6,4},{7,5},{8,10},{9,11},{10,... | collective-permute-start | bytes 393224 | tf_op jit(solution)/shard_map/ppermute | solution.py:174
  9.5 8.1 %collective-permute-start.3 = (bf16[8,64,128]{2,1,0:T(8,128)(2,1)S(1)}, bf16[8,64,128]{2,1,0:T(8,128)(2,1)S(1)}, u32[]{:S(2)}, u32[]{:S(2)}) collective-permute-start(bf16[8,64,128]{2,1,0:T(8,128)(2,1)S(1)} %collective-permute-done.1.refs_4_), channel_id=1, source_target_pairs={{0,2},{1,3},{2,0},{3,1},{4,6},{5,7},{6,4},{7,5},{8,10},{9,11},{10,... | collective-permute-start | bytes 393224 | tf_op jit(solution)/shard_map/ppermute | solution.py:174
  11.3 6.8 %collective-permute-start.4 = (bf16[8,64,128]{2,1,0:T(8,128)(2,1)S(1)}, bf16[8,64,128]{2,1,0:T(8,128)(2,1)S(1)}, u32[]{:S(2)}, u32[]{:S(2)}) collective-permute-start(bf16[8,64,128]{2,1,0:T(8,128)(2,1)S(1)} %shard_map.82.refs_0_), channel_id=1, source_target_pairs={{0,1},{1,0},{2,3},{3,2},{4,5},{5,4},{6,7},{7,6},{8,9},{9,8},{10,11... | collective-permute-start | bytes 393224 | tf_op jit(solution)/shard_map/ppermute | solution.py:174
  12.9 5.4 %collective-permute-start.9 = (bf16[8,64,128]{2,1,0:T(8,128)(2,1)S(1)}, bf16[8,64,128]{2,1,0:T(8,128)(2,1)S(1)}, u32[]{:S(2)}, u32[]{:S(2)}) collective-permute-start(bf16[8,64,128]{2,1,0:T(8,128)(2,1)S(1)} %collective-permute-done.refs_8_), channel_id=1, source_target_pairs={{0,4},{1,5},{2,6},{3,7},{4,0},{5,1},{6,2},{7,3},{8,12},{9,13},{10,... | collective-permute-start | bytes 393224 | tf_op jit(solution)/shard_map/ppermute | solution.py:174
  13.4 6.0 %collective-permute-start.8 = (bf16[8,64,128]{2,1,0:T(8,128)(2,1)S(1)}, bf16[8,64,128]{2,1,0:T(8,128)(2,1)S(1)}, u32[]{:S(2)}, u32[]{:S(2)}) collective-permute-start(bf16[8,64,128]{2,1,0:T(8,128)(2,1)S(1)} %collective-permute-done.refs_8_), channel_id=1, source_target_pairs={{0,2},{1,3},{2,0},{3,1},{4,6},{5,7},{6,4},{7,5},{8,10},{9,11},{10,... | collective-permute-start | bytes 393224 | tf_op jit(solution)/shard_map/ppermute | solution.py:174
  17.6 1.8 %collective-permute-start.5 = (bf16[8,64,128]{2,1,0:T(8,128)(2,1)S(1)}, bf16[8,64,128]{2,1,0:T(8,128)(2,1)S(1)}, u32[]{:S(2)}, u32[]{:S(2)}) collective-permute-start(bf16[8,64,128]{2,1,0:T(8,128)(2,1)S(1)} %collective-permute-done.2.refs_2_), channel_id=1, source_target_pairs={{0,1},{1,0},{2,3},{3,2},{4,5},{5,4},{6,7},{7,6},{8,9},{9,8},{10,11... | collective-permute-start | bytes 393224 | tf_op jit(solution)/shard_map/ppermute | solution.py:174
  17.7 2.2 %collective-permute-start.6 = (bf16[8,64,128]{2,1,0:T(8,128)(2,1)S(1)}, bf16[8,64,128]{2,1,0:T(8,128)(2,1)S(1)}, u32[]{:S(2)}, u32[]{:S(2)}) collective-permute-start(bf16[8,64,128]{2,1,0:T(8,128)(2,1)S(1)} %collective-permute-done.1.refs_4_), channel_id=1, source_target_pairs={{0,1},{1,0},{2,3},{3,2},{4,5},{5,4},{6,7},{7,6},{8,9},{9,8},{10,11... | collective-permute-start | bytes 393224 | tf_op jit(solution)/shard_map/ppermute | solution.py:174
  18.2 1.8 %collective-permute-start.7 = (bf16[8,64,128]{2,1,0:T(8,128)(2,1)S(1)}, bf16[8,64,128]{2,1,0:T(8,128)(2,1)S(1)}, u32[]{:S(2)}, u32[]{:S(2)}) collective-permute-start(bf16[8,64,128]{2,1,0:T(8,128)(2,1)S(1)} %collective-permute-done.3.refs_6_), channel_id=1, source_target_pairs={{0,1},{1,0},{2,3},{3,2},{4,5},{5,4},{6,7},{7,6},{8,9},{9,8},{10,11... | collective-permute-start | bytes 393224 | tf_op jit(solution)/shard_map/ppermute | solution.py:174
  18.3 5.8 %collective-permute-start.10 = (bf16[8,64,128]{2,1,0:T(8,128)(2,1)S(1)}, bf16[8,64,128]{2,1,0:T(8,128)(2,1)S(1)}, u32[]{:S(2)}, u32[]{:S(2)}) collective-permute-start(bf16[8,64,128]{2,1,0:T(8,128)(2,1)S(1)} %collective-permute-done.9.refs_10_), channel_id=1, source_target_pairs={{0,2},{1,3},{2,0},{3,1},{4,6},{5,7},{6,4},{7,5},{8,10},{9,11},{10,... | collective-permute-start | bytes 393224 | tf_op jit(solution)/shard_map/ppermute | solution.py:174
  19.4 4.9 %collective-permute-start.11 = (bf16[8,64,128]{2,1,0:T(8,128)(2,1)S(1)}, bf16[8,64,128]{2,1,0:T(8,128)(2,1)S(1)}, u32[]{:S(2)}, u32[]{:S(2)}) collective-permute-start(bf16[8,64,128]{2,1,0:T(8,128)(2,1)S(1)} %collective-permute-done.refs_8_), channel_id=1, source_target_pairs={{0,1},{1,0},{2,3},{3,2},{4,5},{5,4},{6,7},{7,6},{8,9},{9,8},{10,11... | collective-permute-start | bytes 393224 | tf_op jit(solution)/shard_map/ppermute | solution.py:174
  19.4 4.9 %collective-permute-start.12 = (bf16[8,64,128]{2,1,0:T(8,128)(2,1)S(1)}, bf16[8,64,128]{2,1,0:T(8,128)(2,1)S(1)}, u32[]{:S(2)}, u32[]{:S(2)}) collective-permute-start(bf16[8,64,128]{2,1,0:T(8,128)(2,1)S(1)} %collective-permute-done.9.refs_10_), channel_id=1, source_target_pairs={{0,1},{1,0},{2,3},{3,2},{4,5},{5,4},{6,7},{7,6},{8,9},{9,8},{10,11... | collective-permute-start | bytes 393224 | tf_op jit(solution)/shard_map/ppermute | solution.py:174
  19.9 4.4 %collective-permute-start.13 = (bf16[8,64,128]{2,1,0:T(8,128)(2,1)S(1)}, bf16[8,64,128]{2,1,0:T(8,128)(2,1)S(1)}, u32[]{:S(2)}, u32[]{:S(2)}) collective-permute-start(bf16[8,64,128]{2,1,0:T(8,128)(2,1)S(1)} %collective-permute-done.8.refs_9_), channel_id=1, source_target_pairs={{0,1},{1,0},{2,3},{3,2},{4,5},{5,4},{6,7},{7,6},{8,9},{9,8},{10,11... | collective-permute-start | bytes 393224 | tf_op jit(solution)/shard_map/ppermute | solution.py:174
  24.1 1.3 %collective-permute-start.14 = (bf16[8,64,128]{2,1,0:T(8,128)(2,1)S(1)}, bf16[8,64,128]{2,1,0:T(8,128)(2,1)S(1)}, u32[]{:S(2)}, u32[]{:S(2)}) collective-permute-start(bf16[8,64,128]{2,1,0:T(8,128)(2,1)S(1)} %collective-permute-done.10.refs_3_), channel_id=1, source_target_pairs={{0,1},{1,0},{2,3},{3,2},{4,5},{5,4},{6,7},{7,6},{8,9},{9,8},{10,11... | collective-permute-start | bytes 393224 | tf_op jit(solution)/shard_map/ppermute | solution.py:174

commit v10 on v9

--- a/solution.py
+++ b/solution.py
@@ -98,8 +98,8 @@
 
 
 def early_kernel(pair_count, owner_hbm, slot_hbm, half_ref, *refs):
-    piece_refs = refs[:-7]
-    out_hbm, late_ref, pairs_ref, out_ref, owner_ref, slot_ref, sems = refs[-7:]
+    piece_refs = refs[:-6]
+    out_ref, late_ref, pairs_ref, owner_ref, slot_ref, sems = refs[-6:]
     sectors, blocks, tile, width = out_ref.shape
     items, held = sectors * blocks, pairs_ref.shape[0]
     copies = load_all((owner_hbm, owner_ref, sems.at[0]), (slot_hbm, slot_ref, sems.at[1]))
@@ -107,9 +107,6 @@
     me = lax.axis_index("sec")
     for copy in copies:
         copy.wait()
-
-    def store(a):
-        return pltpu.make_async_copy(out_ref.at[a], out_hbm.at[a], sems.at[a])
 
     def one(a, listed):
         for k in range(0, blocks, 2):
@@ -124,19 +121,17 @@
                 late_ref[listed] = ((at - held) * 2 + second.astype(jnp.int32)) * items + a * blocks + k + u
                 listed = listed + late.astype(jnp.int32)
             out_ref[a, k], out_ref[a, k + 1] = two_products([half_ref[a, k], half_ref[a, k + 1]], forms)
-        store(a).start()
         return listed
 
     listed = lax.fori_loop(0, sectors, one, 0, unroll=2)
     late_ref[items] = listed
-    for a in range(sectors):
-        store(a).wait()
-
-
-def late_kernel(late_ref, early_hbm, half_ref, *refs):
-    piece_refs, (out_hbm, pairs_ref, out_ref, sems) = refs[:-4], refs[-4:]
+
+
+def late_kernel(late_ref, early_ref, half_ref, *refs):
+    piece_refs, (out_hbm, pairs_ref, out_ref, sems, early_sems) = refs[:-5], refs[-5:]
     sectors, blocks, tile, width = half_ref.shape
     items = sectors * blocks
+    early_stores = load_all(*[(early_ref.at[a], out_hbm.at[a], early_sems.at[a]) for a in range(sectors)])
     listed = late_ref[items]
     merge(piece_refs, pairs_ref)
 
@@ -153,12 +148,10 @@
                 halves.append(half_ref[item // blocks, item % blocks])
                 forms.append(block_form(pairs_ref[at // 2], at % 2 == 1))
             out_ref[slot], out_ref[slot + 1] = two_products(halves, forms)
-        for u in range(GROUP):
-            slot = g * GROUP + u
-
-            @pl.when(slot < listed)
-            def _():
-                store(slot, late_ref[slot] % items).start()
+        return carry
+
+    def place(slot, carry):
+        store(slot, late_ref[slot] % items).start()
         return carry
 
     def drain(slot, carry):
@@ -166,6 +159,9 @@
         return carry
 
     lax.fori_loop(0, (listed + GROUP - 1) // GROUP, group, 0)
+    for early_store in early_stores:
+        early_store.wait()
+    lax.fori_loop(0, listed, place, 0)
     lax.fori_loop(0, listed, drain, 0)
 
 
@@ -251,13 +247,12 @@
             jax.ShapeDtypeStruct((items + 1,), jnp.int32),
         ),
         in_specs=[hbm, hbm] + [vmem] * (1 + len(early)),
-        out_specs=(hbm, smem),
+        out_specs=(vmem, smem),
         scratch_shapes=[
             pltpu.VMEM((sum(piece.shape[0] for piece in early), tile, 2 * tile), jnp.bfloat16),
-            pltpu.VMEM(psi.shape, jnp.bfloat16),
             pltpu.SMEM(right_owner.shape, jnp.int32),
             pltpu.SMEM(right_slot.shape, jnp.int32),
-            pltpu.SemaphoreType.DMA((max(left_count, 2),)),
+            pltpu.SemaphoreType.DMA((2,)),
         ],
         compiler_params=params,
         cost_estimate=pl.CostEstimate(flops=flops, bytes_accessed=2 * psi.size, transcendentals=0),
@@ -271,14 +266,14 @@
         sigma = pl.pallas_call(
             late_kernel,
             out_shape=jax.ShapeDtypeStruct(psi.shape, jnp.bfloat16),
-            in_specs=[smem, hbm] + [vmem] * (1 + len(late)),
+            in_specs=[smem] + [vmem] * (2 + len(late)),
             out_specs=hbm,
             scratch_shapes=[
                 pltpu.VMEM((len(late) * pair_count, tile, 2 * tile), jnp.bfloat16),
                 pltpu.VMEM((items + GROUP, tile, width), jnp.bfloat16),
                 pltpu.SemaphoreType.DMA((items,)),
+                pltpu.SemaphoreType.DMA((left_count,)),
             ],
-            input_output_aliases={1: 0},
             compiler_params=params,
             cost_estimate=pl.CostEstimate(flops=flops // 4, bytes_accessed=psi.size, transcendentals=0),
         )(listed, sigma, half, *late)

time: 28.3 us -> 28.8 us (1.018)
  waiting for transfers between devices: 4.43 us -> 5.44 us
    ppermute x15, waiting for transfers between devices: 4.43 us -> 5.44 us  [swap(): return lax.ppermute(piece, 'sec', [(i, i ^ bit) for i in range(count)])]
    pallas_call x1, Pallas kernels: 3.75 us -> 2.86 us  [per_device(): pl.pallas_call(functools.partial(early_kernel, pair_count), out_shape=(ja...]
    pallas_call x1, Pallas kernels: 2.47 us -> 3.16 us  [per_device(): pl.pallas_call(late_kernel, out_shape=jax.ShapeDtypeStruct(psi.shape, jnp...]
  transfers between devices with their start and end apart: 15 -> 15, of which waited for: 4 -> 4; matrix products, arithmetic and copies ran while one was open for 0% -> 0% of each run, Pallas kernels for 23% -> 20%
where the time goes in v10:
time: 28.8 us; the launch traced here: 28.6 us
  starting transfers between devices  13.3 us (46%)
  Pallas kernels  9.83 us (34%)
  waiting for transfers between devices  5.44 us (19%)
    ppermute x15, starting transfers between devices, swap(): return lax.ppermute(piece, 'sec', [(i, i ^ bit) for i in range(count)])  13.3 us
    ppermute x15, waiting for transfers between devices, swap(): return lax.ppermute(piece, 'sec', [(i, i ^ bit) for i in range(count)])  5.44 us
    pallas_call x1, Pallas kernels, per_device(): pl.pallas_call(late_kernel, out_shape=jax.ShapeDtypeStruct(psi.shape, jnp...  3.16 us
    pallas_call x1, Pallas kernels, per_device(): pl.pallas_call(functools.partial(early_kernel, pair_count), out_shape=(ja...  2.86 us
    pallas_call x1, Pallas kernels, half_of(): pl.pallas_call(left_kernel, out_shape=jax.ShapeDtypeStruct(psi.shape, jnp...  2.72 us
    pallas_call x1, Pallas kernels, per_device(): pl.pallas_call(pack_kernel, out_shape=jax.ShapeDtypeStruct((pair_count, t...  1.09 us
  transfers between devices with their start and end apart: 15, of which 4 were waited for; matrix products, arithmetic and copies ran while one was open for 0% of the time, Pallas kernels for 20%

profile of v10, /device:TPU:0, one launch (start us, length us, event | category | flops | bytes accessed | tf_op | source)
XLA Modules:
  0.0 28.6 jit_solution(5421371003961196864)
XLA Ops:
  0.0 1.1 %shard_map.82.refs_0_ = bf16[8,64,128]{2,1,0:T(8,128)(2,1)S(1)} custom-call(s32[16]{0:T(128)} %dims_hbm.1, bf16[16,64,64]{2,1,0:T(8,128)(2,1)} %right_hbm.1), custom_call_target="tpu_custom_call" | custom-call | bytes 131072 | tf_op jit(solution)/shard_map/pallas_call | solution.py:190
  1.1 3.1 %collective-permute-start.1 = (bf16[8,64,128]{2,1,0:T(8,128)(2,1)S(1)}, bf16[8,64,128]{2,1,0:T(8,128)(2,1)S(1)}, u32[]{:S(2)}, u32[]{:S(2)}) collective-permute-start(bf16[8,64,128]{2,1,0:T(8,128)(2,1)S(1)} %shard_map.82.refs_0_), channel_id=1, source_target_pairs={{0,4},{1,5},{2,6},{3,7},{4,0},{5,1},{6,2},{7,3},{8,12},{9,13},{10,... | collective-permute-start | bytes 393224 | tf_op jit(solution)/shard_map/ppermute | solution.py:170
  4.2 2.6 %collective-permute-start = (bf16[8,64,128]{2,1,0:T(8,128)(2,1)S(1)}, bf16[8,64,128]{2,1,0:T(8,128)(2,1)S(1)}, u32[]{:S(2)}, u32[]{:S(2)}) collective-permute-start(bf16[8,64,128]{2,1,0:T(8,128)(2,1)S(1)} %shard_map.82.refs_0_), channel_id=1, source_target_pairs={{0,8},{1,9},{2,10},{3,11},{4,12},{5,13},{6,14},{7,15},{8,0},{9,1},... | collective-permute-start | bytes 393224 | tf_op jit(solution)/shard_map/ppermute | solution.py:170
  6.8 1.5 %collective-permute-start.2 = (bf16[8,64,128]{2,1,0:T(8,128)(2,1)S(1)}, bf16[8,64,128]{2,1,0:T(8,128)(2,1)S(1)}, u32[]{:S(2)}, u32[]{:S(2)}) collective-permute-start(bf16[8,64,128]{2,1,0:T(8,128)(2,1)S(1)} %shard_map.82.refs_0_), channel_id=1, source_target_pairs={{0,2},{1,3},{2,0},{3,1},{4,6},{5,7},{6,4},{7,5},{8,10},{9,11},{10,... | collective-permute-start | bytes 393224 | tf_op jit(solution)/shard_map/ppermute | solution.py:170
  8.3 1.3 %collective-permute-done.1.refs_4_ = bf16[8,64,128]{2,1,0:T(8,128)(2,1)S(1)} collective-permute-done((bf16[8,64,128]{2,1,0:T(8,128)(2,1)S(1)}, bf16[8,64,128]{2,1,0:T(8,128)(2,1)S(1)}, u32[]{:S(2)}, u32[]{:S(2)}) %collective-permute-start.1) | collective-permute-done | bytes 131104 | tf_op jit(solution)/shard_map/ppermute | solution.py:170
  9.5 1.8 %collective-permute-start.3 = (bf16[8,64,128]{2,1,0:T(8,128)(2,1)S(1)}, bf16[8,64,128]{2,1,0:T(8,128)(2,1)S(1)}, u32[]{:S(2)}, u32[]{:S(2)}) collective-permute-start(bf16[8,64,128]{2,1,0:T(8,128)(2,1)S(1)} %collective-permute-done.1.refs_4_), channel_id=1, source_target_pairs={{0,2},{1,3},{2,0},{3,1},{4,6},{5,7},{6,4},{7,5},{8,10},{9,11},{10,... | collective-permute-start | bytes 393224 | tf_op jit(solution)/shard_map/ppermute | solution.py:170
  11.3 0.0 collective-permute-start.4
  11.4 1.6 %collective-permute-done.refs_8_ = bf16[8,64,128]{2,1,0:T(8,128)(2,1)S(1)} collective-permute-done((bf16[8,64,128]{2,1,0:T(8,128)(2,1)S(1)}, bf16[8,64,128]{2,1,0:T(8,128)(2,1)S(1)}, u32[]{:S(2)}, u32[]{:S(2)}) %collective-permute-start) | collective-permute-done | bytes 131104 | tf_op jit(solution)/shard_map/ppermute | solution.py:170
  12.9 0.4 %collective-permute-start.9 = (bf16[8,64,128]{2,1,0:T(8,128)(2,1)S(1)}, bf16[8,64,128]{2,1,0:T(8,128)(2,1)S(1)}, u32[]{:S(2)}, u32[]{:S(2)}) collective-permute-start(bf16[8,64,128]{2,1,0:T(8,128)(2,1)S(1)} %collective-permute-done.refs_8_), channel_id=1, source_target_pairs={{0,4},{1,5},{2,6},{3,7},{4,0},{5,1},{6,2},{7,3},{8,12},{9,13},{10,... | collective-permute-start | bytes 393224 | tf_op jit(solution)/shard_map/ppermute | solution.py:170
  13.4 1.5 %collective-permute-start.8 = (bf16[8,64,128]{2,1,0:T(8,128)(2,1)S(1)}, bf16[8,64,128]{2,1,0:T(8,128)(2,1)S(1)}, u32[]{:S(2)}, u32[]{:S(2)}) collective-permute-start(bf16[8,64,128]{2,1,0:T(8,128)(2,1)S(1)} %collective-permute-done.refs_8_), channel_id=1, source_target_pairs={{0,2},{1,3},{2,0},{3,1},{4,6},{5,7},{6,4},{7,5},{8,10},{9,11},{10,... | collective-permute-start | bytes 393224 | tf_op jit(solution)/shard_map/ppermute | solution.py:170
  14.8 2.7 %shard_map.83.half_ref = bf16[8,8,64,128]{3,2,1,0:T(8,128)(2,1)S(1)} custom-call(s32[8]{0:T(128)} %dims_hbm.2, s32[8,8]{1,0:T(8,128)} %bitcast.1, bf16[8,64,64]{2,1,0:T(8,128)(2,1)} %left_hbm.1, bf16[8,8,64,128]{3,2,1,0:T(8,128)(2,1)} %psi_hbm.1), custom_call_target="tpu_custom_call" | custom-call | flops 67108864 | bytes 1048576 | tf_op jit(solution)/shard_map/pallas_call | solution.py:206
  17.6 0.0 collective-permute-done.2.refs_2_
  17.6 0.0 collective-permute-done.3.refs_6_
  17.6 0.1 collective-permute-start.5
  17.7 0.5 %collective-permute-start.6 = (bf16[8,64,128]{2,1,0:T(8,128)(2,1)S(1)}, bf16[8,64,128]{2,1,0:T(8,128)(2,1)S(1)}, u32[]{:S(2)}, u32[]{:S(2)}) collective-permute-start(bf16[8,64,128]{2,1,0:T(8,128)(2,1)S(1)} %collective-permute-done.1.refs_4_), channel_id=1, source_target_pairs={{0,1},{1,0},{2,3},{3,2},{4,5},{5,4},{6,7},{7,6},{8,9},{9,8},{10,11... | collective-permute-start | bytes 393224 | tf_op jit(solution)/shard_map/ppermute | solution.py:170
  18.2 0.0 collective-permute-done.4.refs_1_
  18.2 0.1 collective-permute-start.7
  18.3 0.0 collective-permute-done.9.refs_10_
  18.3 1.1 %collective-permute-start.10 = (bf16[8,64,128]{2,1,0:T(8,128)(2,1)S(1)}, bf16[8,64,128]{2,1,0:T(8,128)(2,1)S(1)}, u32[]{:S(2)}, u32[]{:S(2)}) collective-permute-start(bf16[8,64,128]{2,1,0:T(8,128)(2,1)S(1)} %collective-permute-done.9.refs_10_), channel_id=1, source_target_pairs={{0,2},{1,3},{2,0},{3,1},{4,6},{5,7},{6,4},{7,5},{8,10},{9,11},{10,... | collective-permute-start | bytes 393224 | tf_op jit(solution)/shard_map/ppermute | solution.py:170
  19.4 0.0 collective-permute-done.8.refs_9_
  19.4 0.0 collective-permute-start.11
  19.4 0.0 collective-permute-done.5.refs_3_
  19.4 0.5 %collective-permute-start.12 = (bf16[8,64,128]{2,1,0:T(8,128)(2,1)S(1)}, bf16[8,64,128]{2,1,0:T(8,128)(2,1)S(1)}, u32[]{:S(2)}, u32[]{:S(2)}) collective-permute-start(bf16[8,64,128]{2,1,0:T(8,128)(2,1)S(1)} %collective-permute-done.9.refs_10_), channel_id=1, source_target_pairs={{0,1},{1,0},{2,3},{3,2},{4,5},{5,4},{6,7},{7,6},{8,9},{9,8},{10,11... | collective-permute-start | bytes 393224 | tf_op jit(solution)/shard_map/ppermute | solution.py:170
  19.9 0.0 collective-permute-done.6.refs_5_
  19.9 0.1 collective-permute-start.13
  20.0 0.0 collective-permute-done.7.refs_7_
  20.0 2.9 %shard_map.84 = (bf16[8,8,64,128]{3,2,1,0:T(8,128)(2,1)S(1)}, s32[65]{0:T(128)S(1)}) custom-call(s32[8,8]{1,0:T(8,128)} %owner_hbm.1, s32[8,8]{1,0:T(8,128)} %slot_hbm.1, bf16[8,8,64,128]{3,2,1,0:T(8,128)(2,1)S(1)} %shard_map.83.half_ref, bf16[8,64,128]{2,1,0:T(8,128)(2,1)S(1)} %shard_map.82.refs_0_, bf16[8,64,128]{2,1,0:T(8,128)(2,1)S(1)} %collective-permute-done.4.refs_1_, ...), custom_call_target="tpu_custom_call" | custom-call | flops 67108864 | bytes 1048576 | tf_op jit(solution)/shard_map/pallas_call | solution.py:243
  22.8 1.3 %collective-permute-done.10.refs_3_ = bf16[8,64,128]{2,1,0:T(8,128)(2,1)S(1)} collective-permute-done((bf16[8,64,128]{2,1,0:T(8,128)(2,1)S(1)}, bf16[8,64,128]{2,1,0:T(8,128)(2,1)S(1)}, u32[]{:S(2)}, u32[]{:S(2)}) %collective-permute-start.10) | collective-permute-done | bytes 131104 | tf_op jit(solution)/shard_map/ppermute | solution.py:170
  24.1 0.0 collective-permute-start.14
  24.1 0.0 collective-permute-done.11.refs_0_
  24.1 0.0 collective-permute-done.12.refs_1_
  24.1 0.0 collective-permute-done.13.refs_2_
  24.1 1.3 %collective-permute-done.14.refs_4_ = bf16[8,64,128]{2,1,0:T(8,128)(2,1)S(1)} collective-permute-done((bf16[8,64,128]{2,1,0:T(8,128)(2,1)S(1)}, bf16[8,64,128]{2,1,0:T(8,128)(2,1)S(1)}, u32[]{:S(2)}, u32[]{:S(2)}) %collective-permute-start.14) | collective-permute-done | bytes 131104 | tf_op jit(solution)/shard_map/ppermute | solution.py:170
  25.5 3.2 %shard_map.85 = bf16[8,8,64,128]{3,2,1,0:T(8,128)(2,1)} custom-call(s32[65]{0:T(128)S(1)} %get-tuple-element.21.late_ref, bf16[8,8,64,128]{3,2,1,0:T(8,128)(2,1)S(1)} %get-tuple-element.23.early_ref, bf16[8,8,64,128]{3,2,1,0:T(8,128)(2,1)S(1)} %shard_map.83.half_ref, bf16[8,64,128]{2,1,0:T(8,128)(2,1)S(1)} %collective-permute-done.11.refs_0_, ...), custom_call_target="tpu_custom_call" | custom-call | flops 16777216 | bytes 524288 | tf_op jit(solution)/shard_map/pallas_call | solution.py:266
Async XLA Ops:
  1.1 8.4 %collective-permute-start.1 = (bf16[8,64,128]{2,1,0:T(8,128)(2,1)S(1)}, bf16[8,64,128]{2,1,0:T(8,128)(2,1)S(1)}, u32[]{:S(2)}, u32[]{:S(2)}) collective-permute-start(bf16[8,64,128]{2,1,0:T(8,128)(2,1)S(1)} %shard_map.82.refs_0_), channel_id=1, source_target_pairs={{0,4},{1,5},{2,6},{3,7},{4,0},{5,1},{6,2},{7,3},{8,12},{9,13},{10,... | collective-permute-start | bytes 393224 | tf_op jit(solution)/shard_map/ppermute | solution.py:170
  4.2 8.7 %collective-permute-start = (bf16[8,64,128]{2,1,0:T(8,128)(2,1)S(1)}, bf16[8,64,128]{2,1,0:T(8,128)(2,1)S(1)}, u32[]{:S(2)}, u32[]{:S(2)}) collective-permute-start(bf16[8,64,128]{2,1,0:T(8,128)(2,1)S(1)} %shard_map.82.refs_0_), channel_id=1, source_target_pairs={{0,8},{1,9},{2,10},{3,11},{4,12},{5,13},{6,14},{7,15},{8,0},{9,1},... | collective-permute-start | bytes 393224 | tf_op jit(solution)/shard_map/ppermute | solution.py:170
  6.8 10.8 %collective-permute-start.2 = (bf16[8,64,128]{2,1,0:T(8,128)(2,1)S(1)}, bf16[8,64,128]{2,1,0:T(8,128)(2,1)S(1)}, u32[]{:S(2)}, u32[]{:S(2)}) collective-permute-start(bf16[8,64,128]{2,1,0:T(8,128)(2,1)S(1)} %shard_map.82.refs_0_), channel_id=1, source_target_pairs={{0,2},{1,3},{2,0},{3,1},{4,6},{5,7},{6,4},{7,5},{8,10},{9,11},{10,... | collective-permute-start | bytes 393224 | tf_op jit(solution)/shard_map/ppermute | solution.py:170
  9.5 8.1 %collective-permute-start.3 = (bf16[8,64,128]{2,1,0:T(8,128)(2,1)S(1)}, bf16[8,64,128]{2,1,0:T(8,128)(2,1)S(1)}, u32[]{:S(2)}, u32[]{:S(2)}) collective-permute-start(bf16[8,64,128]{2,1,0:T(8,128)(2,1)S(1)} %collective-permute-done.1.refs_4_), channel_id=1, source_target_pairs={{0,2},{1,3},{2,0},{3,1},{4,6},{5,7},{6,4},{7,5},{8,10},{9,11},{10,... | collective-permute-start | bytes 393224 | tf_op jit(solution)/shard_map/ppermute | solution.py:170
  11.3 6.8 %collective-permute-start.4 = (bf16[8,64,128]{2,1,0:T(8,128)(2,1)S(1)}, bf16[8,64,128]{2,1,0:T(8,128)(2,1)S(1)}, u32[]{:S(2)}, u32[]{:S(2)}) collective-permute-start(bf16[8,64,128]{2,1,0:T(8,128)(2,1)S(1)} %shard_map.82.refs_0_), channel_id=1, source_target_pairs={{0,1},{1,0},{2,3},{3,2},{4,5},{5,4},{6,7},{7,6},{8,9},{9,8},{10,11... | collective-permute-start | bytes 393224 | tf_op jit(solution)/shard_map/ppermute | solution.py:170
  12.9 5.4 %collective-permute-start.9 = (bf16[8,64,128]{2,1,0:T(8,128)(2,1)S(1)}, bf16[8,64,128]{2,1,0:T(8,128)(2,1)S(1)}, u32[]{:S(2)}, u32[]{:S(2)}) collective-permute-start(bf16[8,64,128]{2,1,0:T(8,128)(2,1)S(1)} %collective-permute-done.refs_8_), channel_id=1, source_target_pairs={{0,4},{1,5},{2,6},{3,7},{4,0},{5,1},{6,2},{7,3},{8,12},{9,13},{10,... | collective-permute-start | bytes 393224 | tf_op jit(solution)/shard_map/ppermute | solution.py:170
  13.4 6.0 %collective-permute-start.8 = (bf16[8,64,128]{2,1,0:T(8,128)(2,1)S(1)}, bf16[8,64,128]{2,1,0:T(8,128)(2,1)S(1)}, u32[]{:S(2)}, u32[]{:S(2)}) collective-permute-start(bf16[8,64,128]{2,1,0:T(8,128)(2,1)S(1)} %collective-permute-done.refs_8_), channel_id=1, source_target_pairs={{0,2},{1,3},{2,0},{3,1},{4,6},{5,7},{6,4},{7,5},{8,10},{9,11},{10,... | collective-permute-start | bytes 393224 | tf_op jit(solution)/shard_map/ppermute | solution.py:170
  17.6 1.8 %collective-permute-start.5 = (bf16[8,64,128]{2,1,0:T(8,128)(2,1)S(1)}, bf16[8,64,128]{2,1,0:T(8,128)(2,1)S(1)}, u32[]{:S(2)}, u32[]{:S(2)}) collective-permute-start(bf16[8,64,128]{2,1,0:T(8,128)(2,1)S(1)} %collective-permute-done.2.refs_2_), channel_id=1, source_target_pairs={{0,1},{1,0},{2,3},{3,2},{4,5},{5,4},{6,7},{7,6},{8,9},{9,8},{10,11... | collective-permute-start | bytes 393224 | tf_op jit(solution)/shard_map/ppermute | solution.py:170
  17.7 2.2 %collective-permute-start.6 = (bf16[8,64,128]{2,1,0:T(8,128)(2,1)S(1)}, bf16[8,64,128]{2,1,0:T(8,128)(2,1)S(1)}, u32[]{:S(2)}, u32[]{:S(2)}) collective-permute-start(bf16[8,64,128]{2,1,0:T(8,128)(2,1)S(1)} %collective-permute-done.1.refs_4_), channel_id=1, source_target_pairs={{0,1},{1,0},{2,3},{3,2},{4,5},{5,4},{6,7},{7,6},{8,9},{9,8},{10,11... | collective-permute-start | bytes 393224 | tf_op jit(solution)/shard_map/ppermute | solution.py:170
  18.2 1.8 %collective-permute-start.7 = (bf16[8,64,128]{2,1,0:T(8,128)(2,1)S(1)}, bf16[8,64,128]{2,1,0:T(8,128)(2,1)S(1)}, u32[]{:S(2)}, u32[]{:S(2)}) collective-permute-start(bf16[8,64,128]{2,1,0:T(8,128)(2,1)S(1)} %collective-permute-done.3.refs_6_), channel_id=1, source_target_pairs={{0,1},{1,0},{2,3},{3,2},{4,5},{5,4},{6,7},{7,6},{8,9},{9,8},{10,11... | collective-permute-start | bytes 393224 | tf_op jit(solution)/shard_map/ppermute | solution.py:170
  18.3 5.8 %collective-permute-start.10 = (bf16[8,64,128]{2,1,0:T(8,128)(2,1)S(1)}, bf16[8,64,128]{2,1,0:T(8,128)(2,1)S(1)}, u32[]{:S(2)}, u32[]{:S(2)}) collective-permute-start(bf16[8,64,128]{2,1,0:T(8,128)(2,1)S(1)} %collective-permute-done.9.refs_10_), channel_id=1, source_target_pairs={{0,2},{1,3},{2,0},{3,1},{4,6},{5,7},{6,4},{7,5},{8,10},{9,11},{10,... | collective-permute-start | bytes 393224 | tf_op jit(solution)/shard_map/ppermute | solution.py:170
  19.4 4.7 %collective-permute-start.11 = (bf16[8,64,128]{2,1,0:T(8,128)(2,1)S(1)}, bf16[8,64,128]{2,1,0:T(8,128)(2,1)S(1)}, u32[]{:S(2)}, u32[]{:S(2)}) collective-permute-start(bf16[8,64,128]{2,1,0:T(8,128)(2,1)S(1)} %collective-permute-done.refs_8_), channel_id=1, source_target_pairs={{0,1},{1,0},{2,3},{3,2},{4,5},{5,4},{6,7},{7,6},{8,9},{9,8},{10,11... | collective-permute-start | bytes 393224 | tf_op jit(solution)/shard_map/ppermute | solution.py:170
  19.4 4.7 %collective-permute-start.12 = (bf16[8,64,128]{2,1,0:T(8,128)(2,1)S(1)}, bf16[8,64,128]{2,1,0:T(8,128)(2,1)S(1)}, u32[]{:S(2)}, u32[]{:S(2)}) collective-permute-start(bf16[8,64,128]{2,1,0:T(8,128)(2,1)S(1)} %collective-permute-done.9.refs_10_), channel_id=1, source_target_pairs={{0,1},{1,0},{2,3},{3,2},{4,5},{5,4},{6,7},{7,6},{8,9},{9,8},{10,11... | collective-permute-start | bytes 393224 | tf_op jit(solution)/shard_map/ppermute | solution.py:170
  19.9 4.2 %collective-permute-start.13 = (bf16[8,64,128]{2,1,0:T(8,128)(2,1)S(1)}, bf16[8,64,128]{2,1,0:T(8,128)(2,1)S(1)}, u32[]{:S(2)}, u32[]{:S(2)}) collective-permute-start(bf16[8,64,128]{2,1,0:T(8,128)(2,1)S(1)} %collective-permute-done.8.refs_9_), channel_id=1, source_target_pairs={{0,1},{1,0},{2,3},{3,2},{4,5},{5,4},{6,7},{7,6},{8,9},{9,8},{10,11... | collective-permute-start | bytes 393224 | tf_op jit(solution)/shard_map/ppermute | solution.py:170
  24.1 1.3 %collective-permute-start.14 = (bf16[8,64,128]{2,1,0:T(8,128)(2,1)S(1)}, bf16[8,64,128]{2,1,0:T(8,128)(2,1)S(1)}, u32[]{:S(2)}, u32[]{:S(2)}) collective-permute-start(bf16[8,64,128]{2,1,0:T(8,128)(2,1)S(1)} %collective-permute-done.10.refs_3_), channel_id=1, source_target_pairs={{0,1},{1,0},{2,3},{3,2},{4,5},{5,4},{6,7},{7,6},{8,9},{9,8},{10,11... | collective-permute-start | bytes 393224 | tf_op jit(solution)/shard_map/ppermute | solution.py:170

commit v11 on v10

--- a/solution.py
+++ b/solution.py
@@ -10,7 +10,7 @@
 VMEM_LIMIT = 48 * 1024 * 1024
 GROUP = 8
 FAR, NEAR, CROSS, CORE = 8, 4, 2, 1
-LATE = (FAR | CORE, FAR | NEAR | CORE, FAR | CROSS | CORE, FAR | NEAR | CROSS, FAR | NEAR | CROSS | CORE)
+LATE = (FAR | CORE, FAR | CROSS | CORE, FAR | NEAR | CROSS, FAR | NEAR | CROSS | CORE)
 EARLY = tuple(r for r in range(16) if r not in LATE)
 ORDER = EARLY + LATE
 
@@ -226,15 +226,13 @@
             for r, bit in pairs_of:
                 pieces[r | bit] = swap(pieces[r], bit)
 
-        pass_on((0, FAR), (0, NEAR), (0, CROSS), (0, CORE), (NEAR, CROSS), (FAR, NEAR), (FAR, CROSS), (FAR | NEAR, CROSS))
-        held = (FAR,)
-        dims_left, ends = lax.optimization_barrier((dims_left, [pieces[r] for r in held]))
-        pieces.update(zip(held, ends))
+        pass_on((0, FAR), (0, NEAR), (0, CROSS))
         half = half_of(dims_left)
-        held = (NEAR, CROSS, NEAR | CROSS,)
+        held = (0, NEAR,)
         half, ends = lax.optimization_barrier((half, [pieces[r] for r in held]))
         pieces.update(zip(held, ends))
-        pass_on((NEAR, CORE), (CROSS, CORE), (NEAR | CROSS, CORE), (FAR | NEAR, CORE), (FAR, CORE), (FAR | CROSS, CORE))
+        pass_on((NEAR, CROSS), (FAR, NEAR), (FAR, CROSS), (FAR | NEAR, CROSS))
+        pass_on((0, CORE), (NEAR, CORE), (CROSS, CORE), (NEAR | CROSS, CORE), (FAR | NEAR, CORE), (FAR, CORE), (FAR | CROSS, CORE))
         early = [pieces[r] for r in EARLY]
     else:
         half = half_of(dims_left)
@@ -244,7 +242,7 @@
         functools.partial(early_kernel, pair_count),
         out_shape=(
             jax.ShapeDtypeStruct(psi.shape, jnp.bfloat16),
-            jax.ShapeDtypeStruct((items + 1,), jnp.int32),
+            pltpu.SMEM((items + 1,), jnp.int32),
         ),
         in_specs=[hbm, hbm] + [vmem] * (1 + len(early)),
         out_specs=(vmem, smem),
@@ -276,7 +274,7 @@
             ],
             compiler_params=params,
             cost_estimate=pl.CostEstimate(flops=flops // 4, bytes_accessed=psi.size, transcendentals=0),
-        )(listed, sigma, half, *late)
+        )(pltpu.with_memory_space_constraint(listed, pltpu.SMEM), sigma, half, *late)
     if lax.axis_size("op") > 1:
         sigma = lax.psum_scatter(sigma, "op", scatter_dimension=3, tiled=True)
     return sigma

time: 28.8 us -> 27.8 us (0.965)
  Pallas kernels: 9.83 us -> 8.54 us
  waiting for transfers between devices: 5.44 us -> 6.59 us
  starting transfers between devices: 13.3 us -> 12.2 us
    ppermute x15, waiting for transfers between devices: 5.44 us -> 6.59 us  [swap(): return lax.ppermute(piece, 'sec', [(i, i ^ bit) for i in range(count)])]
    ppermute x15, starting transfers between devices: 13.3 us -> 12.2 us  [swap(): return lax.ppermute(piece, 'sec', [(i, i ^ bit) for i in range(count)])]
    pallas_call x1, Pallas kernels: 3.16 us -> 2.27 us  [per_device(): pl.pallas_call(late_kernel, out_shape=jax.ShapeDtypeStruct(psi.shape, jnp...]
    pallas_call x1, Pallas kernels: 2.86 us -> 2.44 us  [per_device(): pl.pallas_call(functools.partial(early_kernel, pair_count), out_shape=(ja...]
  transfers between devices with their start and end apart: 15 -> 15, of which waited for: 4 -> 5; matrix products, arithmetic and copies ran while one was open for 0% -> 0% of each run, Pallas kernels for 20% -> 19%
where the time goes in v11:
time: 27.8 us; the launch traced here: 27.4 us
  starting transfers between devices  12.2 us (44%)
  Pallas kernels  8.54 us (31%)
  waiting for transfers between devices  6.59 us (24%)
    ppermute x15, starting transfers between devices, swap(): return lax.ppermute(piece, 'sec', [(i, i ^ bit) for i in range(count)])  12.2 us
    ppermute x15, waiting for transfers between devices, swap(): return lax.ppermute(piece, 'sec', [(i, i ^ bit) for i in range(count)])  6.59 us
    pallas_call x1, Pallas kernels, half_of(): pl.pallas_call(left_kernel, out_shape=jax.ShapeDtypeStruct(psi.shape, jnp...  2.73 us
    pallas_call x1, Pallas kernels, per_device(): pl.pallas_call(functools.partial(early_kernel, pair_count), out_shape=(ja...  2.44 us
    pallas_call x1, Pallas kernels, per_device(): pl.pallas_call(late_kernel, out_shape=jax.ShapeDtypeStruct(psi.shape, jnp...  2.27 us
    pallas_call x1, Pallas kernels, per_device(): pl.pallas_call(pack_kernel, out_shape=jax.ShapeDtypeStruct((pair_count, t...  1.09 us
  transfers between devices with their start and end apart: 15, of which 5 were waited for; matrix products, arithmetic and copies ran while one was open for 0% of the time, Pallas kernels for 19%

profile of v11, /device:TPU:0, one launch (start us, length us, event | category | flops | bytes accessed | tf_op | source)
XLA Modules:
  0.0 27.4 jit_solution(11661042596830441599)
XLA Ops:
  0.0 1.1 %shard_map.83.refs_0_ = bf16[8,64,128]{2,1,0:T(8,128)(2,1)S(1)} custom-call(s32[16]{0:T(128)} %dims_hbm.3, bf16[16,64,64]{2,1,0:T(8,128)(2,1)} %right_hbm.1), custom_call_target="tpu_custom_call" | custom-call | bytes 131072 | tf_op jit(solution)/shard_map/pallas_call | solution.py:190
  1.1 3.1 %collective-permute-start = (bf16[8,64,128]{2,1,0:T(8,128)(2,1)S(1)}, bf16[8,64,128]{2,1,0:T(8,128)(2,1)S(1)}, u32[]{:S(2)}, u32[]{:S(2)}) collective-permute-start(bf16[8,64,128]{2,1,0:T(8,128)(2,1)S(1)} %shard_map.83.refs_0_), channel_id=1, source_target_pairs={{0,4},{1,5},{2,6},{3,7},{4,0},{5,1},{6,2},{7,3},{8,12},{9,13},{10,... | collective-permute-start | bytes 393224 | tf_op jit(solution)/shard_map/ppermute | solution.py:170
  4.2 2.6 %collective-permute-start.7 = (bf16[8,64,128]{2,1,0:T(8,128)(2,1)S(1)}, bf16[8,64,128]{2,1,0:T(8,128)(2,1)S(1)}, u32[]{:S(2)}, u32[]{:S(2)}) collective-permute-start(bf16[8,64,128]{2,1,0:T(8,128)(2,1)S(1)} %shard_map.83.refs_0_), channel_id=1, source_target_pairs={{0,8},{1,9},{2,10},{3,11},{4,12},{5,13},{6,14},{7,15},{8,0},{9,1},... | collective-permute-start | bytes 393224 | tf_op jit(solution)/shard_map/ppermute | solution.py:170
  6.8 1.5 %collective-permute-start.2 = (bf16[8,64,128]{2,1,0:T(8,128)(2,1)S(1)}, bf16[8,64,128]{2,1,0:T(8,128)(2,1)S(1)}, u32[]{:S(2)}, u32[]{:S(2)}) collective-permute-start(bf16[8,64,128]{2,1,0:T(8,128)(2,1)S(1)} %shard_map.83.refs_0_), channel_id=1, source_target_pairs={{0,2},{1,3},{2,0},{3,1},{4,6},{5,7},{6,4},{7,5},{8,10},{9,11},{10,... | collective-permute-start | bytes 393224 | tf_op jit(solution)/shard_map/ppermute | solution.py:170
  8.3 2.7 %shard_map.82.half_ref = bf16[8,8,64,128]{3,2,1,0:T(8,128)(2,1)S(1)} custom-call(s32[8]{0:T(128)} %dims_hbm.2, s32[8,8]{1,0:T(8,128)} %bitcast.1, bf16[8,64,64]{2,1,0:T(8,128)(2,1)} %left_hbm.1, bf16[8,8,64,128]{3,2,1,0:T(8,128)(2,1)} %psi_hbm.1), custom_call_target="tpu_custom_call" | custom-call | flops 67108864 | bytes 1048576 | tf_op jit(solution)/shard_map/pallas_call | solution.py:206
  11.0 0.0 collective-permute-done.refs_4_
  11.0 0.6 %collective-permute-start.5 = (bf16[8,64,128]{2,1,0:T(8,128)(2,1)S(1)}, bf16[8,64,128]{2,1,0:T(8,128)(2,1)S(1)}, u32[]{:S(2)}, u32[]{:S(2)}) collective-permute-start(bf16[8,64,128]{2,1,0:T(8,128)(2,1)S(1)} %collective-permute-done.refs_4_), channel_id=1, source_target_pairs={{0,2},{1,3},{2,0},{3,1},{4,6},{5,7},{6,4},{7,5},{8,10},{9,11},{10,... | collective-permute-start | bytes 393224 | tf_op jit(solution)/shard_map/ppermute | solution.py:170
  11.6 0.0 collective-permute-start.4
  11.6 1.3 %collective-permute-done.7.refs_8_ = bf16[8,64,128]{2,1,0:T(8,128)(2,1)S(1)} collective-permute-done((bf16[8,64,128]{2,1,0:T(8,128)(2,1)S(1)}, bf16[8,64,128]{2,1,0:T(8,128)(2,1)S(1)}, u32[]{:S(2)}, u32[]{:S(2)}) %collective-permute-start.7) | collective-permute-done | bytes 131104 | tf_op jit(solution)/shard_map/ppermute | solution.py:170
  12.9 0.4 %collective-permute-start.9 = (bf16[8,64,128]{2,1,0:T(8,128)(2,1)S(1)}, bf16[8,64,128]{2,1,0:T(8,128)(2,1)S(1)}, u32[]{:S(2)}, u32[]{:S(2)}) collective-permute-start(bf16[8,64,128]{2,1,0:T(8,128)(2,1)S(1)} %collective-permute-done.7.refs_8_), channel_id=1, source_target_pairs={{0,4},{1,5},{2,6},{3,7},{4,0},{5,1},{6,2},{7,3},{8,12},{9,13},{10,... | collective-permute-start | bytes 393224 | tf_op jit(solution)/shard_map/ppermute | solution.py:170
  13.4 0.0 collective-permute-start.1
  13.4 0.0 collective-permute-done.2.refs_2_
  13.4 1.5 %collective-permute-start.8 = (bf16[8,64,128]{2,1,0:T(8,128)(2,1)S(1)}, bf16[8,64,128]{2,1,0:T(8,128)(2,1)S(1)}, u32[]{:S(2)}, u32[]{:S(2)}) collective-permute-start(bf16[8,64,128]{2,1,0:T(8,128)(2,1)S(1)} %collective-permute-done.7.refs_8_), channel_id=1, source_target_pairs={{0,2},{1,3},{2,0},{3,1},{4,6},{5,7},{6,4},{7,5},{8,10},{9,11},{10,... | collective-permute-start | bytes 393224 | tf_op jit(solution)/shard_map/ppermute | solution.py:170
  14.9 1.2 %collective-permute-done.5.refs_6_ = bf16[8,64,128]{2,1,0:T(8,128)(2,1)S(1)} collective-permute-done((bf16[8,64,128]{2,1,0:T(8,128)(2,1)S(1)}, bf16[8,64,128]{2,1,0:T(8,128)(2,1)S(1)}, u32[]{:S(2)}, u32[]{:S(2)}) %collective-permute-start.5) | collective-permute-done | bytes 131104 | tf_op jit(solution)/shard_map/ppermute | solution.py:170
  16.0 0.0 collective-permute-start.3
  16.1 0.0 collective-permute-done.4.refs_5_
  16.1 0.5 %collective-permute-start.6 = (bf16[8,64,128]{2,1,0:T(8,128)(2,1)S(1)}, bf16[8,64,128]{2,1,0:T(8,128)(2,1)S(1)}, u32[]{:S(2)}, u32[]{:S(2)}) collective-permute-start(bf16[8,64,128]{2,1,0:T(8,128)(2,1)S(1)} %collective-permute-done.5.refs_6_), channel_id=1, source_target_pairs={{0,1},{1,0},{2,3},{3,2},{4,5},{5,4},{6,7},{7,6},{8,9},{9,8},{10,11... | collective-permute-start | bytes 393224 | tf_op jit(solution)/shard_map/ppermute | solution.py:170
  16.6 1.3 %collective-permute-done.9.refs_10_ = bf16[8,64,128]{2,1,0:T(8,128)(2,1)S(1)} collective-permute-done((bf16[8,64,128]{2,1,0:T(8,128)(2,1)S(1)}, bf16[8,64,128]{2,1,0:T(8,128)(2,1)S(1)}, u32[]{:S(2)}, u32[]{:S(2)}) %collective-permute-start.9) | collective-permute-done | bytes 131104 | tf_op jit(solution)/shard_map/ppermute | solution.py:170
  17.9 0.0 collective-permute-start.10
  17.9 0.0 collective-permute-done.1.refs_1_
  17.9 1.5 %collective-permute-start.11 = (bf16[8,64,128]{2,1,0:T(8,128)(2,1)S(1)}, bf16[8,64,128]{2,1,0:T(8,128)(2,1)S(1)}, u32[]{:S(2)}, u32[]{:S(2)}) collective-permute-start(bf16[8,64,128]{2,1,0:T(8,128)(2,1)S(1)} %collective-permute-done.9.refs_10_), channel_id=1, source_target_pairs={{0,2},{1,3},{2,0},{3,1},{4,6},{5,7},{6,4},{7,5},{8,10},{9,11},{10,... | collective-permute-start | bytes 393224 | tf_op jit(solution)/shard_map/ppermute | solution.py:170
  19.4 0.0 collective-permute-done.8.refs_9_
  19.4 0.2 collective-permute-start.12
  19.6 0.0 collective-permute-done.3.refs_3_
  19.6 0.3 %collective-permute-start.13 = (bf16[8,64,128]{2,1,0:T(8,128)(2,1)S(1)}, bf16[8,64,128]{2,1,0:T(8,128)(2,1)S(1)}, u32[]{:S(2)}, u32[]{:S(2)}) collective-permute-start(bf16[8,64,128]{2,1,0:T(8,128)(2,1)S(1)} %collective-permute-done.8.refs_9_), channel_id=1, source_target_pairs={{0,1},{1,0},{2,3},{3,2},{4,5},{5,4},{6,7},{7,6},{8,9},{9,8},{10,11... | collective-permute-start | bytes 393224 | tf_op jit(solution)/shard_map/ppermute | solution.py:170
  19.9 0.0 collective-permute-done.6.refs_7_
  19.9 0.0 collective-permute-done.10.refs_11_
  19.9 2.4 %shard_map.84 = (bf16[8,8,64,128]{3,2,1,0:T(8,128)(2,1)S(1)}, s32[65]{0:T(128)S(4)}) custom-call(s32[8,8]{1,0:T(8,128)} %owner_hbm.1, s32[8,8]{1,0:T(8,128)} %slot_hbm.1, bf16[8,8,64,128]{3,2,1,0:T(8,128)(2,1)S(1)} %shard_map.82.half_ref, bf16[8,64,128]{2,1,0:T(8,128)(2,1)S(1)} %shard_map.83.refs_0_, bf16[8,64,128]{2,1,0:T(8,128)(2,1)S(1)} %collective-permute-done.1.refs_1_, ...), custom_call_target="tpu_custom_call" | custom-call | flops 67108864 | bytes 1048576 | tf_op jit(solution)/shard_map/pallas_call | solution.py:241
  22.3 1.4 %collective-permute-done.11.refs_2_ = bf16[8,64,128]{2,1,0:T(8,128)(2,1)S(1)} collective-permute-done((bf16[8,64,128]{2,1,0:T(8,128)(2,1)S(1)}, bf16[8,64,128]{2,1,0:T(8,128)(2,1)S(1)}, u32[]{:S(2)}, u32[]{:S(2)}) %collective-permute-start.11) | collective-permute-done | bytes 131104 | tf_op jit(solution)/shard_map/ppermute | solution.py:170
  23.8 0.0 collective-permute-start.14
  23.8 0.0 collective-permute-done.12.refs_0_
  23.8 0.0 collective-permute-done.13.refs_1_
  23.8 1.3 %collective-permute-done.14.refs_3_ = bf16[8,64,128]{2,1,0:T(8,128)(2,1)S(1)} collective-permute-done((bf16[8,64,128]{2,1,0:T(8,128)(2,1)S(1)}, bf16[8,64,128]{2,1,0:T(8,128)(2,1)S(1)}, u32[]{:S(2)}, u32[]{:S(2)}) %collective-permute-start.14) | collective-permute-done | bytes 131104 | tf_op jit(solution)/shard_map/ppermute | solution.py:170
  25.1 2.3 %shard_map.85 = bf16[8,8,64,128]{3,2,1,0:T(8,128)(2,1)} custom-call(s32[65]{0:T(128)S(4)} %get-tuple-element.15.late_ref, bf16[8,8,64,128]{3,2,1,0:T(8,128)(2,1)S(1)} %get-tuple-element.17.early_ref, bf16[8,8,64,128]{3,2,1,0:T(8,128)(2,1)S(1)} %shard_map.82.half_ref, bf16[8,64,128]{2,1,0:T(8,128)(2,1)S(1)} %collective-permute-done.12.refs_0_, ...), custom_call_target="tpu_custom_call" | custom-call | flops 16777216 | bytes 524288 | tf_op jit(solution)/shard_map/pallas_call | solution.py:264
Async XLA Ops:
  1.1 9.9 %collective-permute-start = (bf16[8,64,128]{2,1,0:T(8,128)(2,1)S(1)}, bf16[8,64,128]{2,1,0:T(8,128)(2,1)S(1)}, u32[]{:S(2)}, u32[]{:S(2)}) collective-permute-start(bf16[8,64,128]{2,1,0:T(8,128)(2,1)S(1)} %shard_map.83.refs_0_), channel_id=1, source_target_pairs={{0,4},{1,5},{2,6},{3,7},{4,0},{5,1},{6,2},{7,3},{8,12},{9,13},{10,... | collective-permute-start | bytes 393224 | tf_op jit(solution)/shard_map/ppermute | solution.py:170
  4.2 8.7 %collective-permute-start.7 = (bf16[8,64,128]{2,1,0:T(8,128)(2,1)S(1)}, bf16[8,64,128]{2,1,0:T(8,128)(2,1)S(1)}, u32[]{:S(2)}, u32[]{:S(2)}) collective-permute-start(bf16[8,64,128]{2,1,0:T(8,128)(2,1)S(1)} %shard_map.83.refs_0_), channel_id=1, source_target_pairs={{0,8},{1,9},{2,10},{3,11},{4,12},{5,13},{6,14},{7,15},{8,0},{9,1},... | collective-permute-start | bytes 393224 | tf_op jit(solution)/shard_map/ppermute | solution.py:170
  6.8 6.6 %collective-permute-start.2 = (bf16[8,64,128]{2,1,0:T(8,128)(2,1)S(1)}, bf16[8,64,128]{2,1,0:T(8,128)(2,1)S(1)}, u32[]{:S(2)}, u32[]{:S(2)}) collective-permute-start(bf16[8,64,128]{2,1,0:T(8,128)(2,1)S(1)} %shard_map.83.refs_0_), channel_id=1, source_target_pairs={{0,2},{1,3},{2,0},{3,1},{4,6},{5,7},{6,4},{7,5},{8,10},{9,11},{10,... | collective-permute-start | bytes 393224 | tf_op jit(solution)/shard_map/ppermute | solution.py:170
  11.0 5.0 %collective-permute-start.5 = (bf16[8,64,128]{2,1,0:T(8,128)(2,1)S(1)}, bf16[8,64,128]{2,1,0:T(8,128)(2,1)S(1)}, u32[]{:S(2)}, u32[]{:S(2)}) collective-permute-start(bf16[8,64,128]{2,1,0:T(8,128)(2,1)S(1)} %collective-permute-done.refs_4_), channel_id=1, source_target_pairs={{0,2},{1,3},{2,0},{3,1},{4,6},{5,7},{6,4},{7,5},{8,10},{9,11},{10,... | collective-permute-start | bytes 393224 | tf_op jit(solution)/shard_map/ppermute | solution.py:170
  11.6 4.4 %collective-permute-start.4 = (bf16[8,64,128]{2,1,0:T(8,128)(2,1)S(1)}, bf16[8,64,128]{2,1,0:T(8,128)(2,1)S(1)}, u32[]{:S(2)}, u32[]{:S(2)}) collective-permute-start(bf16[8,64,128]{2,1,0:T(8,128)(2,1)S(1)} %collective-permute-done.refs_4_), channel_id=1, source_target_pairs={{0,1},{1,0},{2,3},{3,2},{4,5},{5,4},{6,7},{7,6},{8,9},{9,8},{10,11... | collective-permute-start | bytes 393224 | tf_op jit(solution)/shard_map/ppermute | solution.py:170
  12.9 5.0 %collective-permute-start.9 = (bf16[8,64,128]{2,1,0:T(8,128)(2,1)S(1)}, bf16[8,64,128]{2,1,0:T(8,128)(2,1)S(1)}, u32[]{:S(2)}, u32[]{:S(2)}) collective-permute-start(bf16[8,64,128]{2,1,0:T(8,128)(2,1)S(1)} %collective-permute-done.7.refs_8_), channel_id=1, source_target_pairs={{0,4},{1,5},{2,6},{3,7},{4,0},{5,1},{6,2},{7,3},{8,12},{9,13},{10,... | collective-permute-start | bytes 393224 | tf_op jit(solution)/shard_map/ppermute | solution.py:170
  13.4 4.5 %collective-permute-start.1 = (bf16[8,64,128]{2,1,0:T(8,128)(2,1)S(1)}, bf16[8,64,128]{2,1,0:T(8,128)(2,1)S(1)}, u32[]{:S(2)}, u32[]{:S(2)}) collective-permute-start(bf16[8,64,128]{2,1,0:T(8,128)(2,1)S(1)} %shard_map.83.refs_0_), channel_id=1, source_target_pairs={{0,1},{1,0},{2,3},{3,2},{4,5},{5,4},{6,7},{7,6},{8,9},{9,8},{10,11... | collective-permute-start | bytes 393224 | tf_op jit(solution)/shard_map/ppermute | solution.py:170
  13.4 6.0 %collective-permute-start.8 = (bf16[8,64,128]{2,1,0:T(8,128)(2,1)S(1)}, bf16[8,64,128]{2,1,0:T(8,128)(2,1)S(1)}, u32[]{:S(2)}, u32[]{:S(2)}) collective-permute-start(bf16[8,64,128]{2,1,0:T(8,128)(2,1)S(1)} %collective-permute-done.7.refs_8_), channel_id=1, source_target_pairs={{0,2},{1,3},{2,0},{3,1},{4,6},{5,7},{6,4},{7,5},{8,10},{9,11},{10,... | collective-permute-start | bytes 393224 | tf_op jit(solution)/shard_map/ppermute | solution.py:170
  16.0 3.6 %collective-permute-start.3 = (bf16[8,64,128]{2,1,0:T(8,128)(2,1)S(1)}, bf16[8,64,128]{2,1,0:T(8,128)(2,1)S(1)}, u32[]{:S(2)}, u32[]{:S(2)}) collective-permute-start(bf16[8,64,128]{2,1,0:T(8,128)(2,1)S(1)} %collective-permute-done.2.refs_2_), channel_id=1, source_target_pairs={{0,1},{1,0},{2,3},{3,2},{4,5},{5,4},{6,7},{7,6},{8,9},{9,8},{10,11... | collective-permute-start | bytes 393224 | tf_op jit(solution)/shard_map/ppermute | solution.py:170
  16.1 3.8 %collective-permute-start.6 = (bf16[8,64,128]{2,1,0:T(8,128)(2,1)S(1)}, bf16[8,64,128]{2,1,0:T(8,128)(2,1)S(1)}, u32[]{:S(2)}, u32[]{:S(2)}) collective-permute-start(bf16[8,64,128]{2,1,0:T(8,128)(2,1)S(1)} %collective-permute-done.5.refs_6_), channel_id=1, source_target_pairs={{0,1},{1,0},{2,3},{3,2},{4,5},{5,4},{6,7},{7,6},{8,9},{9,8},{10,11... | collective-permute-start | bytes 393224 | tf_op jit(solution)/shard_map/ppermute | solution.py:170
  17.9 2.0 %collective-permute-start.10 = (bf16[8,64,128]{2,1,0:T(8,128)(2,1)S(1)}, bf16[8,64,128]{2,1,0:T(8,128)(2,1)S(1)}, u32[]{:S(2)}, u32[]{:S(2)}) collective-permute-start(bf16[8,64,128]{2,1,0:T(8,128)(2,1)S(1)} %collective-permute-done.9.refs_10_), channel_id=1, source_target_pairs={{0,1},{1,0},{2,3},{3,2},{4,5},{5,4},{6,7},{7,6},{8,9},{9,8},{10,11... | collective-permute-start | bytes 393224 | tf_op jit(solution)/shard_map/ppermute | solution.py:170
  17.9 5.9 %collective-permute-start.11 = (bf16[8,64,128]{2,1,0:T(8,128)(2,1)S(1)}, bf16[8,64,128]{2,1,0:T(8,128)(2,1)S(1)}, u32[]{:S(2)}, u32[]{:S(2)}) collective-permute-start(bf16[8,64,128]{2,1,0:T(8,128)(2,1)S(1)} %collective-permute-done.9.refs_10_), channel_id=1, source_target_pairs={{0,2},{1,3},{2,0},{3,1},{4,6},{5,7},{6,4},{7,5},{8,10},{9,11},{10,... | collective-permute-start | bytes 393224 | tf_op jit(solution)/shard_map/ppermute | solution.py:170
  19.4 4.4 %collective-permute-start.12 = (bf16[8,64,128]{2,1,0:T(8,128)(2,1)S(1)}, bf16[8,64,128]{2,1,0:T(8,128)(2,1)S(1)}, u32[]{:S(2)}, u32[]{:S(2)}) collective-permute-start(bf16[8,64,128]{2,1,0:T(8,128)(2,1)S(1)} %collective-permute-done.7.refs_8_), channel_id=1, source_target_pairs={{0,1},{1,0},{2,3},{3,2},{4,5},{5,4},{6,7},{7,6},{8,9},{9,8},{10,11... | collective-permute-start | bytes 393224 | tf_op jit(solution)/shard_map/ppermute | solution.py:170
  19.6 4.2 %collective-permute-start.13 = (bf16[8,64,128]{2,1,0:T(8,128)(2,1)S(1)}, bf16[8,64,128]{2,1,0:T(8,128)(2,1)S(1)}, u32[]{:S(2)}, u32[]{:S(2)}) collective-permute-start(bf16[8,64,128]{2,1,0:T(8,128)(2,1)S(1)} %collective-permute-done.8.refs_9_), channel_id=1, source_target_pairs={{0,1},{1,0},{2,3},{3,2},{4,5},{5,4},{6,7},{7,6},{8,9},{9,8},{10,11... | collective-permute-start | bytes 393224 | tf_op jit(solution)/shard_map/ppermute | solution.py:170
  23.8 1.3 %collective-permute-start.14 = (bf16[8,64,128]{2,1,0:T(8,128)(2,1)S(1)}, bf16[8,64,128]{2,1,0:T(8,128)(2,1)S(1)}, u32[]{:S(2)}, u32[]{:S(2)}) collective-permute-start(bf16[8,64,128]{2,1,0:T(8,128)(2,1)S(1)} %collective-permute-done.11.refs_2_), channel_id=1, source_target_pairs={{0,1},{1,0},{2,3},{3,2},{4,5},{5,4},{6,7},{7,6},{8,9},{9,8},{10,11... | collective-permute-start | bytes 393224 | tf_op jit(solution)/shard_map/ppermute | solution.py:170

commit v12 on v11

--- a/solution.py
+++ b/solution.py
@@ -10,7 +10,7 @@
 VMEM_LIMIT = 48 * 1024 * 1024
 GROUP = 8
 FAR, NEAR, CROSS, CORE = 8, 4, 2, 1
-LATE = (FAR | CORE, FAR | CROSS | CORE, FAR | NEAR | CROSS, FAR | NEAR | CROSS | CORE)
+LATE = (NEAR | CROSS | CORE, FAR | CORE, FAR | CROSS | CORE, FAR | NEAR | CROSS, FAR | NEAR | CROSS | CORE)
 EARLY = tuple(r for r in range(16) if r not in LATE)
 ORDER = EARLY + LATE
 
@@ -226,13 +226,17 @@
             for r, bit in pairs_of:
                 pieces[r | bit] = swap(pieces[r], bit)
 
-        pass_on((0, FAR), (0, NEAR), (0, CROSS))
+        pass_on((0, FAR), (0, CORE), (0, CROSS))
+        held = (CORE,)
+        pieces[0], ends = lax.optimization_barrier((pieces[0], [pieces[r] for r in held]))
+        pieces.update(zip(held, ends))
+        pieces[NEAR] = swap(pieces[0], NEAR)
         half = half_of(dims_left)
-        held = (0, NEAR,)
+        held = (FAR, NEAR,)
         half, ends = lax.optimization_barrier((half, [pieces[r] for r in held]))
         pieces.update(zip(held, ends))
         pass_on((NEAR, CROSS), (FAR, NEAR), (FAR, CROSS), (FAR | NEAR, CROSS))
-        pass_on((0, CORE), (NEAR, CORE), (CROSS, CORE), (NEAR | CROSS, CORE), (FAR | NEAR, CORE), (FAR, CORE), (FAR | CROSS, CORE))
+        pass_on((NEAR, CORE), (CROSS, CORE), (NEAR | CROSS, CORE), (FAR | NEAR, CORE), (FAR, CORE), (FAR | CROSS, CORE))
         early = [pieces[r] for r in EARLY]
     else:
         half = half_of(dims_left)

time: 27.8 us -> 30.3 us (1.090); the launches traced: 27.4 us -> 30.5 us
  waiting for transfers between devices: 6.59 us -> 8.25 us
  Pallas kernels: 8.54 us -> 9.3 us
  starting transfers between devices: 12.2 us -> 12.9 us
    ppermute x15, waiting for transfers between devices: 6.59 us -> 8.25 us  [swap(): return lax.ppermute(piece, 'sec', [(i, i ^ bit) for i in range(count)])]
    pallas_call x1, Pallas kernels: 2.27 us -> 3.04 us  [per_device(): pl.pallas_call(late_kernel, out_shape=jax.ShapeDtypeStruct(psi.shape, jnp...]
    ppermute x15, starting transfers between devices: 12.2 us -> 12.9 us  [swap(): return lax.ppermute(piece, 'sec', [(i, i ^ bit) for i in range(count)])]
  transfers between devices with their start and end apart: 15 -> 15, of which waited for: 5 -> 6; matrix products, arithmetic and copies ran while one was open for 0% -> 0% of each run, Pallas kernels for 19% -> 17%
where the time goes in v12:
time: 30.3 us; the launch traced here: 30.5 us
  starting transfers between devices  12.9 us (43%)
  Pallas kernels  9.3 us (31%)
  waiting for transfers between devices  8.25 us (27%)
    ppermute x15, starting transfers between devices, swap(): return lax.ppermute(piece, 'sec', [(i, i ^ bit) for i in range(count)])  12.9 us
    ppermute x15, waiting for transfers between devices, swap(): return lax.ppermute(piece, 'sec', [(i, i ^ bit) for i in range(count)])  8.25 us
    pallas_call x1, Pallas kernels, per_device(): pl.pallas_call(late_kernel, out_shape=jax.ShapeDtypeStruct(psi.shape, jnp...  3.04 us
    pallas_call x1, Pallas kernels, half_of(): pl.pallas_call(left_kernel, out_shape=jax.ShapeDtypeStruct(psi.shape, jnp...  2.73 us
    pallas_call x1, Pallas kernels, per_device(): pl.pallas_call(functools.partial(early_kernel, pair_count), out_shape=(ja...  2.44 us
    pallas_call x1, Pallas kernels, per_device(): pl.pallas_call(pack_kernel, out_shape=jax.ShapeDtypeStruct((pair_count, t...  1.09 us
  transfers between devices with their start and end apart: 15, of which 6 were waited for; matrix products, arithmetic and copies ran while one was open for 0% of the time, Pallas kernels for 17%

profile of v12, /device:TPU:0, one launch (start us, length us, event | category | flops | bytes accessed | tf_op | source)
XLA Modules:
  0.0 30.5 jit_solution(1988460169186071127)
XLA Ops:
  0.0 1.1 %shard_map.83.refs_0_ = bf16[8,64,128]{2,1,0:T(8,128)(2,1)S(1)} custom-call(s32[16]{0:T(128)} %dims_hbm.3, bf16[16,64,64]{2,1,0:T(8,128)(2,1)} %right_hbm.1), custom_call_target="tpu_custom_call" | custom-call | bytes 131072 | tf_op jit(solution)/shard_map/pallas_call | solution.py:190
  1.1 0.5 %collective-permute-start.1 = (bf16[8,64,128]{2,1,0:T(8,128)(2,1)S(1)}, bf16[8,64,128]{2,1,0:T(8,128)(2,1)S(1)}, u32[]{:S(2)}, u32[]{:S(2)}) collective-permute-start(bf16[8,64,128]{2,1,0:T(8,128)(2,1)S(1)} %shard_map.83.refs_0_), channel_id=1, source_target_pairs={{0,1},{1,0},{2,3},{3,2},{4,5},{5,4},{6,7},{7,6},{8,9},{9,8},{10,11... | collective-permute-start | bytes 393224 | tf_op jit(solution)/shard_map/ppermute | solution.py:170
  1.6 3.7 %collective-permute-start = (bf16[8,64,128]{2,1,0:T(8,128)(2,1)S(1)}, bf16[8,64,128]{2,1,0:T(8,128)(2,1)S(1)}, u32[]{:S(2)}, u32[]{:S(2)}) collective-permute-start(bf16[8,64,128]{2,1,0:T(8,128)(2,1)S(1)} %shard_map.83.refs_0_), channel_id=1, source_target_pairs={{0,8},{1,9},{2,10},{3,11},{4,12},{5,13},{6,14},{7,15},{8,0},{9,1},... | collective-permute-start | bytes 393224 | tf_op jit(solution)/shard_map/ppermute | solution.py:170
  5.3 0.0 collective-permute-done.1.refs_1_
  5.3 1.6 %collective-permute-start.2 = (bf16[8,64,128]{2,1,0:T(8,128)(2,1)S(1)}, bf16[8,64,128]{2,1,0:T(8,128)(2,1)S(1)}, u32[]{:S(2)}, u32[]{:S(2)}) collective-permute-start(bf16[8,64,128]{2,1,0:T(8,128)(2,1)S(1)} %shard_map.83.refs_0_), channel_id=1, source_target_pairs={{0,4},{1,5},{2,6},{3,7},{4,0},{5,1},{6,2},{7,3},{8,12},{9,13},{10,... | collective-permute-start | bytes 393224 | tf_op jit(solution)/shard_map/ppermute | solution.py:170
  6.9 1.5 %collective-permute-start.3 = (bf16[8,64,128]{2,1,0:T(8,128)(2,1)S(1)}, bf16[8,64,128]{2,1,0:T(8,128)(2,1)S(1)}, u32[]{:S(2)}, u32[]{:S(2)}) collective-permute-start(bf16[8,64,128]{2,1,0:T(8,128)(2,1)S(1)} %shard_map.83.refs_0_), channel_id=1, source_target_pairs={{0,2},{1,3},{2,0},{3,1},{4,6},{5,7},{6,4},{7,5},{8,10},{9,11},{10,... | collective-permute-start | bytes 393224 | tf_op jit(solution)/shard_map/ppermute | solution.py:170
  8.4 2.7 %shard_map.82.half_ref = bf16[8,8,64,128]{3,2,1,0:T(8,128)(2,1)S(1)} custom-call(s32[8]{0:T(128)} %dims_hbm.2, s32[8,8]{1,0:T(8,128)} %bitcast.1, bf16[8,64,64]{2,1,0:T(8,128)(2,1)} %left_hbm.1, bf16[8,8,64,128]{3,2,1,0:T(8,128)(2,1)} %psi_hbm.1), custom_call_target="tpu_custom_call" | custom-call | flops 67108864 | bytes 1048576 | tf_op jit(solution)/shard_map/pallas_call | solution.py:206
  11.1 1.2 %collective-permute-done.refs_7_ = bf16[8,64,128]{2,1,0:T(8,128)(2,1)S(1)} collective-permute-done((bf16[8,64,128]{2,1,0:T(8,128)(2,1)S(1)}, bf16[8,64,128]{2,1,0:T(8,128)(2,1)S(1)}, u32[]{:S(2)}, u32[]{:S(2)}) %collective-permute-start) | collective-permute-done | bytes 131104 | tf_op jit(solution)/shard_map/ppermute | solution.py:170
  12.3 0.2 collective-permute-done.2.refs_4_
  12.5 1.5 %collective-permute-start.8 = (bf16[8,64,128]{2,1,0:T(8,128)(2,1)S(1)}, bf16[8,64,128]{2,1,0:T(8,128)(2,1)S(1)}, u32[]{:S(2)}, u32[]{:S(2)}) collective-permute-start(bf16[8,64,128]{2,1,0:T(8,128)(2,1)S(1)} %collective-permute-done.refs_7_), channel_id=1, source_target_pairs={{0,4},{1,5},{2,6},{3,7},{4,0},{5,1},{6,2},{7,3},{8,12},{9,13},{10,... | collective-permute-start | bytes 393224 | tf_op jit(solution)/shard_map/ppermute | solution.py:170
  14.0 0.0 collective-permute-done.3.refs_2_
  14.0 0.0 collective-permute-start.4
  14.0 1.5 %collective-permute-start.7 = (bf16[8,64,128]{2,1,0:T(8,128)(2,1)S(1)}, bf16[8,64,128]{2,1,0:T(8,128)(2,1)S(1)}, u32[]{:S(2)}, u32[]{:S(2)}) collective-permute-start(bf16[8,64,128]{2,1,0:T(8,128)(2,1)S(1)} %collective-permute-done.refs_7_), channel_id=1, source_target_pairs={{0,2},{1,3},{2,0},{3,1},{4,6},{5,7},{6,4},{7,5},{8,10},{9,11},{10,... | collective-permute-start | bytes 393224 | tf_op jit(solution)/shard_map/ppermute | solution.py:170
  15.5 0.5 %collective-permute-start.6 = (bf16[8,64,128]{2,1,0:T(8,128)(2,1)S(1)}, bf16[8,64,128]{2,1,0:T(8,128)(2,1)S(1)}, u32[]{:S(2)}, u32[]{:S(2)}) collective-permute-start(bf16[8,64,128]{2,1,0:T(8,128)(2,1)S(1)} %collective-permute-done.2.refs_4_), channel_id=1, source_target_pairs={{0,2},{1,3},{2,0},{3,1},{4,6},{5,7},{6,4},{7,5},{8,10},{9,11},{10,... | collective-permute-start | bytes 393224 | tf_op jit(solution)/shard_map/ppermute | solution.py:170
  16.0 0.0 collective-permute-start.5
  16.0 1.5 %collective-permute-done.8.refs_9_ = bf16[8,64,128]{2,1,0:T(8,128)(2,1)S(1)} collective-permute-done((bf16[8,64,128]{2,1,0:T(8,128)(2,1)S(1)}, bf16[8,64,128]{2,1,0:T(8,128)(2,1)S(1)}, u32[]{:S(2)}, u32[]{:S(2)}) %collective-permute-start.8) | collective-permute-done | bytes 131104 | tf_op jit(solution)/shard_map/ppermute | solution.py:170
  17.5 0.0 collective-permute-start.9
  17.5 0.0 collective-permute-done.4.refs_3_
  17.5 1.5 %collective-permute-start.10 = (bf16[8,64,128]{2,1,0:T(8,128)(2,1)S(1)}, bf16[8,64,128]{2,1,0:T(8,128)(2,1)S(1)}, u32[]{:S(2)}, u32[]{:S(2)}) collective-permute-start(bf16[8,64,128]{2,1,0:T(8,128)(2,1)S(1)} %collective-permute-done.8.refs_9_), channel_id=1, source_target_pairs={{0,2},{1,3},{2,0},{3,1},{4,6},{5,7},{6,4},{7,5},{8,10},{9,11},{10,... | collective-permute-start | bytes 393224 | tf_op jit(solution)/shard_map/ppermute | solution.py:170
  19.0 1.3 %collective-permute-done.7.refs_8_ = bf16[8,64,128]{2,1,0:T(8,128)(2,1)S(1)} collective-permute-done((bf16[8,64,128]{2,1,0:T(8,128)(2,1)S(1)}, bf16[8,64,128]{2,1,0:T(8,128)(2,1)S(1)}, u32[]{:S(2)}, u32[]{:S(2)}) %collective-permute-start.7) | collective-permute-done | bytes 131104 | tf_op jit(solution)/shard_map/ppermute | solution.py:170
  20.3 0.0 collective-permute-start.12
  20.3 2.8 %collective-permute-done.6.refs_6_ = bf16[8,64,128]{2,1,0:T(8,128)(2,1)S(1)} collective-permute-done((bf16[8,64,128]{2,1,0:T(8,128)(2,1)S(1)}, bf16[8,64,128]{2,1,0:T(8,128)(2,1)S(1)}, u32[]{:S(2)}, u32[]{:S(2)}) %collective-permute-start.6) | collective-permute-done | bytes 131104 | tf_op jit(solution)/shard_map/ppermute | solution.py:170
  23.1 0.0 collective-permute-start.13
  23.1 0.0 collective-permute-done.5.refs_5_
  23.1 0.5 %collective-permute-start.11 = (bf16[8,64,128]{2,1,0:T(8,128)(2,1)S(1)}, bf16[8,64,128]{2,1,0:T(8,128)(2,1)S(1)}, u32[]{:S(2)}, u32[]{:S(2)}) collective-permute-start(bf16[8,64,128]{2,1,0:T(8,128)(2,1)S(1)} %collective-permute-done.6.refs_6_), channel_id=1, source_target_pairs={{0,1},{1,0},{2,3},{3,2},{4,5},{5,4},{6,7},{7,6},{8,9},{9,8},{10,11... | collective-permute-start | bytes 393224 | tf_op jit(solution)/shard_map/ppermute | solution.py:170
  23.6 0.0 collective-permute-done.9.refs_10_
  23.6 2.4 %shard_map.84 = (bf16[8,8,64,128]{3,2,1,0:T(8,128)(2,1)S(1)}, s32[65]{0:T(128)S(4)}) custom-call(s32[8,8]{1,0:T(8,128)} %owner_hbm.1, s32[8,8]{1,0:T(8,128)} %slot_hbm.1, bf16[8,8,64,128]{3,2,1,0:T(8,128)(2,1)S(1)} %shard_map.82.half_ref, bf16[8,64,128]{2,1,0:T(8,128)(2,1)S(1)} %shard_map.83.refs_0_, bf16[8,64,128]{2,1,0:T(8,128)(2,1)S(1)} %collective-permute-done.1.refs_1_, ...), custom_call_target="tpu_custom_call" | custom-call | flops 67108864 | bytes 1048576 | tf_op jit(solution)/shard_map/pallas_call | solution.py:245
  26.1 0.0 collective-permute-done.10.refs_3_
  26.1 0.1 collective-permute-start.14
  26.1 0.0 collective-permute-done.12.refs_1_
  26.2 0.0 collective-permute-done.13.refs_2_
  26.2 0.0 collective-permute-done.11.refs_0_
  26.2 1.3 %collective-permute-done.14.refs_4_ = bf16[8,64,128]{2,1,0:T(8,128)(2,1)S(1)} collective-permute-done((bf16[8,64,128]{2,1,0:T(8,128)(2,1)S(1)}, bf16[8,64,128]{2,1,0:T(8,128)(2,1)S(1)}, u32[]{:S(2)}, u32[]{:S(2)}) %collective-permute-start.14) | collective-permute-done | bytes 131104 | tf_op jit(solution)/shard_map/ppermute | solution.py:170
  27.5 3.0 %shard_map.85 = bf16[8,8,64,128]{3,2,1,0:T(8,128)(2,1)} custom-call(s32[65]{0:T(128)S(4)} %get-tuple-element.19.late_ref, bf16[8,8,64,128]{3,2,1,0:T(8,128)(2,1)S(1)} %get-tuple-element.21.early_ref, bf16[8,8,64,128]{3,2,1,0:T(8,128)(2,1)S(1)} %shard_map.82.half_ref, bf16[8,64,128]{2,1,0:T(8,128)(2,1)S(1)} %collective-permute-done.11.refs_0_, ...), custom_call_target="tpu_custom_call" | custom-call | flops 16777216 | bytes 524288 | tf_op jit(solution)/shard_map/pallas_call | solution.py:268
Async XLA Ops:
  1.1 4.2 %collective-permute-start.1 = (bf16[8,64,128]{2,1,0:T(8,128)(2,1)S(1)}, bf16[8,64,128]{2,1,0:T(8,128)(2,1)S(1)}, u32[]{:S(2)}, u32[]{:S(2)}) collective-permute-start(bf16[8,64,128]{2,1,0:T(8,128)(2,1)S(1)} %shard_map.83.refs_0_), channel_id=1, source_target_pairs={{0,1},{1,0},{2,3},{3,2},{4,5},{5,4},{6,7},{7,6},{8,9},{9,8},{10,11... | collective-permute-start | bytes 393224 | tf_op jit(solution)/shard_map/ppermute | solution.py:170
  1.6 10.7 %collective-permute-start = (bf16[8,64,128]{2,1,0:T(8,128)(2,1)S(1)}, bf16[8,64,128]{2,1,0:T(8,128)(2,1)S(1)}, u32[]{:S(2)}, u32[]{:S(2)}) collective-permute-start(bf16[8,64,128]{2,1,0:T(8,128)(2,1)S(1)} %shard_map.83.refs_0_), channel_id=1, source_target_pairs={{0,8},{1,9},{2,10},{3,11},{4,12},{5,13},{6,14},{7,15},{8,0},{9,1},... | collective-permute-start | bytes 393224 | tf_op jit(solution)/shard_map/ppermute | solution.py:170
  5.3 7.2 %collective-permute-start.2 = (bf16[8,64,128]{2,1,0:T(8,128)(2,1)S(1)}, bf16[8,64,128]{2,1,0:T(8,128)(2,1)S(1)}, u32[]{:S(2)}, u32[]{:S(2)}) collective-permute-start(bf16[8,64,128]{2,1,0:T(8,128)(2,1)S(1)} %shard_map.83.refs_0_), channel_id=1, source_target_pairs={{0,4},{1,5},{2,6},{3,7},{4,0},{5,1},{6,2},{7,3},{8,12},{9,13},{10,... | collective-permute-start | bytes 393224 | tf_op jit(solution)/shard_map/ppermute | solution.py:170
  6.9 7.1 %collective-permute-start.3 = (bf16[8,64,128]{2,1,0:T(8,128)(2,1)S(1)}, bf16[8,64,128]{2,1,0:T(8,128)(2,1)S(1)}, u32[]{:S(2)}, u32[]{:S(2)}) collective-permute-start(bf16[8,64,128]{2,1,0:T(8,128)(2,1)S(1)} %shard_map.83.refs_0_), channel_id=1, source_target_pairs={{0,2},{1,3},{2,0},{3,1},{4,6},{5,7},{6,4},{7,5},{8,10},{9,11},{10,... | collective-permute-start | bytes 393224 | tf_op jit(solution)/shard_map/ppermute | solution.py:170
  12.5 5.0 %collective-permute-start.8 = (bf16[8,64,128]{2,1,0:T(8,128)(2,1)S(1)}, bf16[8,64,128]{2,1,0:T(8,128)(2,1)S(1)}, u32[]{:S(2)}, u32[]{:S(2)}) collective-permute-start(bf16[8,64,128]{2,1,0:T(8,128)(2,1)S(1)} %collective-permute-done.refs_7_), channel_id=1, source_target_pairs={{0,4},{1,5},{2,6},{3,7},{4,0},{5,1},{6,2},{7,3},{8,12},{9,13},{10,... | collective-permute-start | bytes 393224 | tf_op jit(solution)/shard_map/ppermute | solution.py:170
  14.0 3.5 %collective-permute-start.4 = (bf16[8,64,128]{2,1,0:T(8,128)(2,1)S(1)}, bf16[8,64,128]{2,1,0:T(8,128)(2,1)S(1)}, u32[]{:S(2)}, u32[]{:S(2)}) collective-permute-start(bf16[8,64,128]{2,1,0:T(8,128)(2,1)S(1)} %collective-permute-done.3.refs_2_), channel_id=1, source_target_pairs={{0,1},{1,0},{2,3},{3,2},{4,5},{5,4},{6,7},{7,6},{8,9},{9,8},{10,11... | collective-permute-start | bytes 393224 | tf_op jit(solution)/shard_map/ppermute | solution.py:170
  14.0 6.3 %collective-permute-start.7 = (bf16[8,64,128]{2,1,0:T(8,128)(2,1)S(1)}, bf16[8,64,128]{2,1,0:T(8,128)(2,1)S(1)}, u32[]{:S(2)}, u32[]{:S(2)}) collective-permute-start(bf16[8,64,128]{2,1,0:T(8,128)(2,1)S(1)} %collective-permute-done.refs_7_), channel_id=1, source_target_pairs={{0,2},{1,3},{2,0},{3,1},{4,6},{5,7},{6,4},{7,5},{8,10},{9,11},{10,... | collective-permute-start | bytes 393224 | tf_op jit(solution)/shard_map/ppermute | solution.py:170
  15.5 7.6 %collective-permute-start.6 = (bf16[8,64,128]{2,1,0:T(8,128)(2,1)S(1)}, bf16[8,64,128]{2,1,0:T(8,128)(2,1)S(1)}, u32[]{:S(2)}, u32[]{:S(2)}) collective-permute-start(bf16[8,64,128]{2,1,0:T(8,128)(2,1)S(1)} %collective-permute-done.2.refs_4_), channel_id=1, source_target_pairs={{0,2},{1,3},{2,0},{3,1},{4,6},{5,7},{6,4},{7,5},{8,10},{9,11},{10,... | collective-permute-start | bytes 393224 | tf_op jit(solution)/shard_map/ppermute | solution.py:170
  16.0 7.1 %collective-permute-start.5 = (bf16[8,64,128]{2,1,0:T(8,128)(2,1)S(1)}, bf16[8,64,128]{2,1,0:T(8,128)(2,1)S(1)}, u32[]{:S(2)}, u32[]{:S(2)}) collective-permute-start(bf16[8,64,128]{2,1,0:T(8,128)(2,1)S(1)} %collective-permute-done.2.refs_4_), channel_id=1, source_target_pairs={{0,1},{1,0},{2,3},{3,2},{4,5},{5,4},{6,7},{7,6},{8,9},{9,8},{10,11... | collective-permute-start | bytes 393224 | tf_op jit(solution)/shard_map/ppermute | solution.py:170
  17.5 6.1 %collective-permute-start.9 = (bf16[8,64,128]{2,1,0:T(8,128)(2,1)S(1)}, bf16[8,64,128]{2,1,0:T(8,128)(2,1)S(1)}, u32[]{:S(2)}, u32[]{:S(2)}) collective-permute-start(bf16[8,64,128]{2,1,0:T(8,128)(2,1)S(1)} %collective-permute-done.8.refs_9_), channel_id=1, source_target_pairs={{0,1},{1,0},{2,3},{3,2},{4,5},{5,4},{6,7},{7,6},{8,9},{9,8},{10,11... | collective-permute-start | bytes 393224 | tf_op jit(solution)/shard_map/ppermute | solution.py:170
  17.5 8.6 %collective-permute-start.10 = (bf16[8,64,128]{2,1,0:T(8,128)(2,1)S(1)}, bf16[8,64,128]{2,1,0:T(8,128)(2,1)S(1)}, u32[]{:S(2)}, u32[]{:S(2)}) collective-permute-start(bf16[8,64,128]{2,1,0:T(8,128)(2,1)S(1)} %collective-permute-done.8.refs_9_), channel_id=1, source_target_pairs={{0,2},{1,3},{2,0},{3,1},{4,6},{5,7},{6,4},{7,5},{8,10},{9,11},{10,... | collective-permute-start | bytes 393224 | tf_op jit(solution)/shard_map/ppermute | solution.py:170
  20.3 5.9 %collective-permute-start.12 = (bf16[8,64,128]{2,1,0:T(8,128)(2,1)S(1)}, bf16[8,64,128]{2,1,0:T(8,128)(2,1)S(1)}, u32[]{:S(2)}, u32[]{:S(2)}) collective-permute-start(bf16[8,64,128]{2,1,0:T(8,128)(2,1)S(1)} %collective-permute-done.refs_7_), channel_id=1, source_target_pairs={{0,1},{1,0},{2,3},{3,2},{4,5},{5,4},{6,7},{7,6},{8,9},{9,8},{10,11... | collective-permute-start | bytes 393224 | tf_op jit(solution)/shard_map/ppermute | solution.py:170
  23.1 3.1 %collective-permute-start.13 = (bf16[8,64,128]{2,1,0:T(8,128)(2,1)S(1)}, bf16[8,64,128]{2,1,0:T(8,128)(2,1)S(1)}, u32[]{:S(2)}, u32[]{:S(2)}) collective-permute-start(bf16[8,64,128]{2,1,0:T(8,128)(2,1)S(1)} %collective-permute-done.7.refs_8_), channel_id=1, source_target_pairs={{0,1},{1,0},{2,3},{3,2},{4,5},{5,4},{6,7},{7,6},{8,9},{9,8},{10,11... | collective-permute-start | bytes 393224 | tf_op jit(solution)/shard_map/ppermute | solution.py:170
  23.1 3.1 %collective-permute-start.11 = (bf16[8,64,128]{2,1,0:T(8,128)(2,1)S(1)}, bf16[8,64,128]{2,1,0:T(8,128)(2,1)S(1)}, u32[]{:S(2)}, u32[]{:S(2)}) collective-permute-start(bf16[8,64,128]{2,1,0:T(8,128)(2,1)S(1)} %collective-permute-done.6.refs_6_), channel_id=1, source_target_pairs={{0,1},{1,0},{2,3},{3,2},{4,5},{5,4},{6,7},{7,6},{8,9},{9,8},{10,11... | collective-permute-start | bytes 393224 | tf_op jit(solution)/shard_map/ppermute | solution.py:170
  26.1 1.4 %collective-permute-start.14 = (bf16[8,64,128]{2,1,0:T(8,128)(2,1)S(1)}, bf16[8,64,128]{2,1,0:T(8,128)(2,1)S(1)}, u32[]{:S(2)}, u32[]{:S(2)}) collective-permute-start(bf16[8,64,128]{2,1,0:T(8,128)(2,1)S(1)} %collective-permute-done.10.refs_3_), channel_id=1, source_target_pairs={{0,1},{1,0},{2,3},{3,2},{4,5},{5,4},{6,7},{7,6},{8,9},{9,8},{10,11... | collective-permute-start | bytes 393224 | tf_op jit(solution)/shard_map/ppermute | solution.py:170

commit v13 on v11

--- a/solution.py
+++ b/solution.py
@@ -10,8 +10,21 @@
 VMEM_LIMIT = 48 * 1024 * 1024
 GROUP = 8
 FAR, NEAR, CROSS, CORE = 8, 4, 2, 1
-LATE = (FAR | CORE, FAR | CROSS | CORE, FAR | NEAR | CROSS, FAR | NEAR | CROSS | CORE)
-EARLY = tuple(r for r in range(16) if r not in LATE)
+OWN, SIDE = (0, 0), (CROSS, CROSS)
+FIRST, SECOND = (FAR, NEAR), (NEAR, FAR)
+THIRD, FOURTH, FIFTH = (FAR | NEAR, NEAR | CROSS), (NEAR | CROSS, FAR | CROSS), (FAR | CROSS, FAR | NEAR)
+LAST = (FAR | NEAR | CROSS, FAR | NEAR | CROSS)
+
+
+def partner(name):
+    return name[1] | CORE, name[0] | CORE
+
+
+LATE = (partner(SIDE), partner(THIRD), partner(FOURTH), partner(FIFTH), LAST, partner(LAST))
+EARLY = tuple(name for name in (
+    OWN, SIDE, FIRST, SECOND, THIRD, FOURTH, FIFTH,
+    partner(OWN), partner(SIDE), partner(FIRST), partner(SECOND), partner(THIRD), partner(FOURTH), partner(FIFTH),
+) if name not in LATE)
 ORDER = EARLY + LATE
 
 
@@ -89,12 +102,17 @@
         at += piece.shape[0]
 
 
-def piece_at(r):
-    low = sum(ORDER.index(i) << (4 * i) for i in range(7))
-    high = sum(ORDER.index(i + 8) << (4 * i) for i in range(7))
-    packed = jnp.where(r < 8, low, high) >> (4 * (r & 7))
-    end = jnp.where(r < 8, ORDER.index(7), ORDER.index(15))
-    return jnp.where(r & 7 == 7, end, packed & 15)
+def piece_at(r, me):
+    places = [[0] * len(ORDER), [0] * len(ORDER)]
+    for at, name in enumerate(ORDER):
+        places[0][name[0]], places[1][name[1]] = at, at
+    at = jnp.int32(0)
+    for parity in range(2):
+        for half in range(2):
+            packed = sum(place << (4 * i) for i, place in enumerate(places[parity][8 * half:8 * half + 7]))
+            mine = jnp.where(r & 7 == 7, places[parity][8 * half + 7], (packed >> (4 * (r & 7))) & 15)
+            at = jnp.where((me & 1 == parity) & (r >> 3 == half), mine, at)
+    return at
 
 
 def early_kernel(pair_count, owner_hbm, slot_hbm, half_ref, *refs):
@@ -113,7 +131,7 @@
             forms = []
             for u in range(2):
                 owner, slot = owner_ref[a, k + u], slot_ref[a, k + u]
-                at = piece_at(owner ^ me) if len(piece_refs) > 1 else owner
+                at = piece_at(owner ^ me, me) if len(piece_refs) > 1 else owner
                 second = slot >= pair_count
                 at = at * pair_count + jnp.where(second, slot - pair_count, slot)
                 late = at >= held
@@ -165,9 +183,9 @@
     lax.fori_loop(0, listed, drain, 0)
 
 
-def swap(piece, bit):
+def swap(piece, even_bit, odd_bit):
     count = lax.axis_size("sec")
-    return lax.ppermute(piece, "sec", [(i, i ^ bit) for i in range(count)])
+    return lax.ppermute(piece, "sec", [(i, i ^ (odd_bit if i & CORE else even_bit)) for i in range(count)])
 
 
 def per_device(
@@ -221,19 +239,24 @@
         )(*in_hbm(dims_left, active, left_ops, psi))
 
     if by_swaps:
-        pieces = {0: pairs}
-        def pass_on(*pairs_of):
-            for r, bit in pairs_of:
-                pieces[r | bit] = swap(pieces[r], bit)
-
-        pass_on((0, FAR), (0, NEAR), (0, CROSS))
+        pieces = {OWN: pairs}
+
+        def pass_on(*routes):
+            for name, target in routes:
+                pieces[target] = swap(pieces[name], name[0] ^ target[0], name[1] ^ target[1])
+
+        def share(*names):
+            for name in names:
+                pieces[partner(name)] = swap(pieces[name], CORE, CORE)
+
+        pass_on((OWN, FIRST), (OWN, SECOND), (OWN, SIDE))
         half = half_of(dims_left)
-        held = (0, NEAR,)
+        held = (SECOND,)
         half, ends = lax.optimization_barrier((half, [pieces[r] for r in held]))
         pieces.update(zip(held, ends))
-        pass_on((NEAR, CROSS), (FAR, NEAR), (FAR, CROSS), (FAR | NEAR, CROSS))
-        pass_on((0, CORE), (NEAR, CORE), (CROSS, CORE), (NEAR | CROSS, CORE), (FAR | NEAR, CORE), (FAR, CORE), (FAR | CROSS, CORE))
-        early = [pieces[r] for r in EARLY]
+        pass_on((FIRST, THIRD), (SECOND, FOURTH), (FIRST, FIFTH), (THIRD, LAST))
+        share(OWN, SIDE, FIRST, SECOND, THIRD, FOURTH, FIFTH)
+        early = [pieces[name] for name in EARLY]
     else:
         half = half_of(dims_left)
         early = [lax.all_gather(pairs, "sec", axis=0, tiled=True)]
@@ -256,11 +279,11 @@
         cost_estimate=pl.CostEstimate(flops=flops, bytes_accessed=2 * psi.size, transcendentals=0),
     )(*in_hbm(right_owner, right_slot), half, *early)
     if by_swaps:
-        ends = (FAR | NEAR | CROSS,)
-        held, sigma = lax.optimization_barrier(([pieces[r] for r in ends], sigma))
-        for r, piece in zip(ends, held):
-            pieces[r], pieces[r | CORE] = piece, swap(piece, CORE)
-        late = [pieces[r] for r in LATE]
+        ends = (LAST,)
+        held, sigma = lax.optimization_barrier(([pieces[name] for name in ends], sigma))
+        pieces.update(zip(ends, held))
+        share(*ends)
+        late = [pieces[name] for name in LATE]
         sigma = pl.pallas_call(
             late_kernel,
             out_shape=jax.ShapeDtypeStruct(psi.shape, jnp.bfloat16),

time: 27.8 us -> 29.8 us (1.072); the launches traced: 27.4 us -> 29.7 us
  starting transfers between devices: 12.2 us -> 14.6 us
  waiting for transfers between devices: 6.59 us -> 5.46 us
  Pallas kernels: 8.54 us -> 9.63 us
    ppermute x15, starting transfers between devices: 12.2 us -> 14.6 us  [swap(): lax.ppermute(piece, 'sec', [(i, i ^ (odd_bit if i & CORE else even_bit))...]
    ppermute x15, waiting for transfers between devices: 6.59 us -> 5.46 us  [swap(): lax.ppermute(piece, 'sec', [(i, i ^ (odd_bit if i & CORE else even_bit))...]
    pallas_call x1, Pallas kernels: 2.27 us -> 3.08 us  [per_device(): pl.pallas_call(late_kernel, out_shape=jax.ShapeDtypeStruct(psi.shape, jnp...]
  transfers between devices with their start and end apart: 15 -> 15, of which waited for: 5 -> 3; matrix products, arithmetic and copies ran while one was open for 0% -> 0% of each run, Pallas kernels for 19% -> 18%
where the time goes in v13:
time: 29.8 us; the launch traced here: 29.7 us
  starting transfers between devices  14.6 us (49%)
  Pallas kernels  9.63 us (32%)
  waiting for transfers between devices  5.46 us (18%)
    ppermute x15, starting transfers between devices, swap(): lax.ppermute(piece, 'sec', [(i, i ^ (odd_bit if i & CORE else even_bit))...  14.6 us
    ppermute x15, waiting for transfers between devices, swap(): lax.ppermute(piece, 'sec', [(i, i ^ (odd_bit if i & CORE else even_bit))...  5.46 us
    pallas_call x1, Pallas kernels, per_device(): pl.pallas_call(late_kernel, out_shape=jax.ShapeDtypeStruct(psi.shape, jnp...  3.08 us
    pallas_call x1, Pallas kernels, per_device(): pl.pallas_call(functools.partial(early_kernel, pair_count), out_shape=(ja...  2.73 us
    pallas_call x1, Pallas kernels, half_of(): pl.pallas_call(left_kernel, out_shape=jax.ShapeDtypeStruct(psi.shape, jnp...  2.73 us
    pallas_call x1, Pallas kernels, per_device(): pl.pallas_call(pack_kernel, out_shape=jax.ShapeDtypeStruct((pair_count, t...  1.09 us
  transfers between devices with their start and end apart: 15, of which 3 were waited for; matrix products, arithmetic and copies ran while one was open for 0% of the time, Pallas kernels for 18%

profile of v13, /device:TPU:0, one launch (start us, length us, event | category | flops | bytes accessed | tf_op | source)
XLA Modules:
  0.0 29.7 jit_solution(12781028594357470801)
XLA Ops:
  0.0 1.1 %shard_map.83.refs_0_ = bf16[8,64,128]{2,1,0:T(8,128)(2,1)S(1)} custom-call(s32[16]{0:T(128)} %dims_hbm.3, bf16[16,64,64]{2,1,0:T(8,128)(2,1)} %right_hbm.1), custom_call_target="tpu_custom_call" | custom-call | bytes 131072 | tf_op jit(solution)/shard_map/pallas_call | solution.py:208
  1.1 4.1 %collective-permute-start.2 = (bf16[8,64,128]{2,1,0:T(8,128)(2,1)S(1)}, bf16[8,64,128]{2,1,0:T(8,128)(2,1)S(1)}, u32[]{:S(2)}, u32[]{:S(2)}) collective-permute-start(bf16[8,64,128]{2,1,0:T(8,128)(2,1)S(1)} %shard_map.83.refs_0_), channel_id=1, source_target_pairs={{0,8},{1,5},{2,10},{3,7},{4,12},{5,1},{6,14},{7,3},{8,0},{9,13},{1... | collective-permute-start | bytes 393224 | tf_op jit(solution)/shard_map/ppermute | solution.py:188
  5.2 1.6 %collective-permute-start = (bf16[8,64,128]{2,1,0:T(8,128)(2,1)S(1)}, bf16[8,64,128]{2,1,0:T(8,128)(2,1)S(1)}, u32[]{:S(2)}, u32[]{:S(2)}) collective-permute-start(bf16[8,64,128]{2,1,0:T(8,128)(2,1)S(1)} %shard_map.83.refs_0_), channel_id=1, source_target_pairs={{0,4},{1,9},{2,6},{3,11},{4,0},{5,13},{6,2},{7,15},{8,12},{9,1},{1... | collective-permute-start | bytes 393224 | tf_op jit(solution)/shard_map/ppermute | solution.py:188
  6.8 1.5 %collective-permute-start.1 = (bf16[8,64,128]{2,1,0:T(8,128)(2,1)S(1)}, bf16[8,64,128]{2,1,0:T(8,128)(2,1)S(1)}, u32[]{:S(2)}, u32[]{:S(2)}) collective-permute-start(bf16[8,64,128]{2,1,0:T(8,128)(2,1)S(1)} %shard_map.83.refs_0_), channel_id=1, source_target_pairs={{0,2},{1,3},{2,0},{3,1},{4,6},{5,7},{6,4},{7,5},{8,10},{9,11},{10,... | collective-permute-start | bytes 393224 | tf_op jit(solution)/shard_map/ppermute | solution.py:188
  8.3 0.0 collective-permute-start.6
  8.3 3.7 %collective-permute-done.2.refs_2_ = bf16[8,64,128]{2,1,0:T(8,128)(2,1)S(1)} collective-permute-done((bf16[8,64,128]{2,1,0:T(8,128)(2,1)S(1)}, bf16[8,64,128]{2,1,0:T(8,128)(2,1)S(1)}, u32[]{:S(2)}, u32[]{:S(2)}) %collective-permute-start.2) | collective-permute-done | bytes 131104 | tf_op jit(solution)/shard_map/ppermute | solution.py:188
  11.9 0.6 %collective-permute-start.3 = (bf16[8,64,128]{2,1,0:T(8,128)(2,1)S(1)}, bf16[8,64,128]{2,1,0:T(8,128)(2,1)S(1)}, u32[]{:S(2)}, u32[]{:S(2)}) collective-permute-start(bf16[8,64,128]{2,1,0:T(8,128)(2,1)S(1)} %collective-permute-done.2.refs_2_), channel_id=1, source_target_pairs={{0,4},{1,3},{2,6},{3,1},{4,0},{5,7},{6,2},{7,5},{8,12},{9,11},{10,... | collective-permute-start | bytes 393224 | tf_op jit(solution)/shard_map/ppermute | solution.py:188
  12.5 2.7 %shard_map.82.half_ref = bf16[8,8,64,128]{3,2,1,0:T(8,128)(2,1)S(1)} custom-call(s32[8]{0:T(128)} %dims_hbm.2, s32[8,8]{1,0:T(8,128)} %bitcast.1, bf16[8,64,64]{2,1,0:T(8,128)(2,1)} %left_hbm.1, bf16[8,8,64,128]{3,2,1,0:T(8,128)(2,1)} %psi_hbm.1), custom_call_target="tpu_custom_call" | custom-call | flops 67108864 | bytes 1048576 | tf_op jit(solution)/shard_map/pallas_call | solution.py:224
  15.2 0.0 collective-permute-done.refs_3_
  15.3 1.6 %collective-permute-start.4 = (bf16[8,64,128]{2,1,0:T(8,128)(2,1)S(1)}, bf16[8,64,128]{2,1,0:T(8,128)(2,1)S(1)}, u32[]{:S(2)}, u32[]{:S(2)}) collective-permute-start(bf16[8,64,128]{2,1,0:T(8,128)(2,1)S(1)} %collective-permute-done.refs_3_), channel_id=1, source_target_pairs={{0,2},{1,3},{2,0},{3,1},{4,6},{5,7},{6,4},{7,5},{8,10},{9,11},{10,... | collective-permute-start | bytes 393224 | tf_op jit(solution)/shard_map/ppermute | solution.py:188
  16.8 0.5 %collective-permute-start.5 = (bf16[8,64,128]{2,1,0:T(8,128)(2,1)S(1)}, bf16[8,64,128]{2,1,0:T(8,128)(2,1)S(1)}, u32[]{:S(2)}, u32[]{:S(2)}) collective-permute-start(bf16[8,64,128]{2,1,0:T(8,128)(2,1)S(1)} %collective-permute-done.2.refs_2_), channel_id=1, source_target_pairs={{0,2},{1,9},{2,0},{3,11},{4,6},{5,13},{6,4},{7,15},{8,10},{9,1},{1... | collective-permute-start | bytes 393224 | tf_op jit(solution)/shard_map/ppermute | solution.py:188
  17.4 0.0 collective-permute-done.1.refs_1_
  17.4 0.0 collective-permute-start.8
  17.4 0.0 collective-permute-done.6.refs_7_
  17.4 0.5 %collective-permute-start.7 = (bf16[8,64,128]{2,1,0:T(8,128)(2,1)S(1)}, bf16[8,64,128]{2,1,0:T(8,128)(2,1)S(1)}, u32[]{:S(2)}, u32[]{:S(2)}) collective-permute-start(bf16[8,64,128]{2,1,0:T(8,128)(2,1)S(1)} %collective-permute-done.2.refs_2_), channel_id=1, source_target_pairs={{0,1},{1,0},{2,3},{3,2},{4,5},{5,4},{6,7},{7,6},{8,9},{9,8},{10,11... | collective-permute-start | bytes 393224 | tf_op jit(solution)/shard_map/ppermute | solution.py:188
  17.9 0.0 collective-permute-done.3.refs_4_
  17.9 2.4 %collective-permute-start.9 = (bf16[8,64,128]{2,1,0:T(8,128)(2,1)S(1)}, bf16[8,64,128]{2,1,0:T(8,128)(2,1)S(1)}, u32[]{:S(2)}, u32[]{:S(2)}) collective-permute-start(bf16[8,64,128]{2,1,0:T(8,128)(2,1)S(1)} %collective-permute-done.3.refs_4_), channel_id=1, source_target_pairs={{0,2},{1,9},{2,0},{3,11},{4,6},{5,13},{6,4},{7,15},{8,10},{9,1},{1... | collective-permute-start | bytes 393224 | tf_op jit(solution)/shard_map/ppermute | solution.py:188
  20.2 0.0 collective-permute-done.4.refs_5_
  20.3 0.8 %collective-permute-start.10 = (bf16[8,64,128]{2,1,0:T(8,128)(2,1)S(1)}, bf16[8,64,128]{2,1,0:T(8,128)(2,1)S(1)}, u32[]{:S(2)}, u32[]{:S(2)}) collective-permute-start(bf16[8,64,128]{2,1,0:T(8,128)(2,1)S(1)} %collective-permute-done.1.refs_1_), channel_id=1, source_target_pairs={{0,1},{1,0},{2,3},{3,2},{4,5},{5,4},{6,7},{7,6},{8,9},{9,8},{10,11... | collective-permute-start | bytes 393224 | tf_op jit(solution)/shard_map/ppermute | solution.py:188
  21.1 0.7 %collective-permute-done.5.refs_6_ = bf16[8,64,128]{2,1,0:T(8,128)(2,1)S(1)} collective-permute-done((bf16[8,64,128]{2,1,0:T(8,128)(2,1)S(1)}, bf16[8,64,128]{2,1,0:T(8,128)(2,1)S(1)}, u32[]{:S(2)}, u32[]{:S(2)}) %collective-permute-start.5) | collective-permute-done | bytes 131104 | tf_op jit(solution)/shard_map/ppermute | solution.py:188
  21.8 0.0 collective-permute-start.11
  21.8 0.0 collective-permute-done.8.refs_9_
  21.8 0.5 %collective-permute-start.12 = (bf16[8,64,128]{2,1,0:T(8,128)(2,1)S(1)}, bf16[8,64,128]{2,1,0:T(8,128)(2,1)S(1)}, u32[]{:S(2)}, u32[]{:S(2)}) collective-permute-start(bf16[8,64,128]{2,1,0:T(8,128)(2,1)S(1)} %collective-permute-done.4.refs_5_), channel_id=1, source_target_pairs={{0,1},{1,0},{2,3},{3,2},{4,5},{5,4},{6,7},{7,6},{8,9},{9,8},{10,11... | collective-permute-start | bytes 393224 | tf_op jit(solution)/shard_map/ppermute | solution.py:188
  22.3 0.0 collective-permute-done.7.refs_8_
  22.3 0.1 collective-permute-start.13
  22.4 2.7 %shard_map.84 = (bf16[8,8,64,128]{3,2,1,0:T(8,128)(2,1)S(1)}, s32[65]{0:T(128)S(4)}) custom-call(s32[8,8]{1,0:T(8,128)} %owner_hbm.1, s32[8,8]{1,0:T(8,128)} %slot_hbm.1, bf16[8,8,64,128]{3,2,1,0:T(8,128)(2,1)S(1)} %shard_map.82.half_ref, bf16[8,64,128]{2,1,0:T(8,128)(2,1)S(1)} %shard_map.83.refs_0_, bf16[8,64,128]{2,1,0:T(8,128)(2,1)S(1)} %collective-permute-done.1.refs_1_, ...), custom_call_target="tpu_custom_call" | custom-call | flops 67108864 | bytes 1048576 | tf_op jit(solution)/shard_map/pallas_call | solution.py:264
  25.1 0.0 collective-permute-done.9.refs_4_
  25.1 0.5 %collective-permute-start.14 = (bf16[8,64,128]{2,1,0:T(8,128)(2,1)S(1)}, bf16[8,64,128]{2,1,0:T(8,128)(2,1)S(1)}, u32[]{:S(2)}, u32[]{:S(2)}) collective-permute-start(bf16[8,64,128]{2,1,0:T(8,128)(2,1)S(1)} %collective-permute-done.9.refs_4_), channel_id=1, source_target_pairs={{0,1},{1,0},{2,3},{3,2},{4,5},{5,4},{6,7},{7,6},{8,9},{9,8},{10,11... | collective-permute-start | bytes 393224 | tf_op jit(solution)/shard_map/ppermute | solution.py:188
  25.6 0.0 collective-permute-done.10.refs_0_
  25.6 0.0 collective-permute-done.11.refs_1_
  25.6 0.0 collective-permute-done.12.refs_2_
  25.7 0.0 collective-permute-done.13.refs_3_
  25.7 1.0 %collective-permute-done.14.refs_5_ = bf16[8,64,128]{2,1,0:T(8,128)(2,1)S(1)} collective-permute-done((bf16[8,64,128]{2,1,0:T(8,128)(2,1)S(1)}, bf16[8,64,128]{2,1,0:T(8,128)(2,1)S(1)}, u32[]{:S(2)}, u32[]{:S(2)}) %collective-permute-start.14) | collective-permute-done | bytes 131104 | tf_op jit(solution)/shard_map/ppermute | solution.py:188
  26.6 3.1 %shard_map.85 = bf16[8,8,64,128]{3,2,1,0:T(8,128)(2,1)} custom-call(s32[65]{0:T(128)S(4)} %get-tuple-element.13.late_ref, bf16[8,8,64,128]{3,2,1,0:T(8,128)(2,1)S(1)} %get-tuple-element.15.early_ref, bf16[8,8,64,128]{3,2,1,0:T(8,128)(2,1)S(1)} %shard_map.82.half_ref, bf16[8,64,128]{2,1,0:T(8,128)(2,1)S(1)} %collective-permute-done.10.refs_0_, ...), custom_call_target="tpu_custom_call" | custom-call | flops 16777216 | bytes 524288 | tf_op jit(solution)/shard_map/pallas_call | solution.py:287
Async XLA Ops:
  1.1 10.8 %collective-permute-start.2 = (bf16[8,64,128]{2,1,0:T(8,128)(2,1)S(1)}, bf16[8,64,128]{2,1,0:T(8,128)(2,1)S(1)}, u32[]{:S(2)}, u32[]{:S(2)}) collective-permute-start(bf16[8,64,128]{2,1,0:T(8,128)(2,1)S(1)} %shard_map.83.refs_0_), channel_id=1, source_target_pairs={{0,8},{1,5},{2,10},{3,7},{4,12},{5,1},{6,14},{7,3},{8,0},{9,13},{1... | collective-permute-start | bytes 393224 | tf_op jit(solution)/shard_map/ppermute | solution.py:188
  5.2 10.0 %collective-permute-start = (bf16[8,64,128]{2,1,0:T(8,128)(2,1)S(1)}, bf16[8,64,128]{2,1,0:T(8,128)(2,1)S(1)}, u32[]{:S(2)}, u32[]{:S(2)}) collective-permute-start(bf16[8,64,128]{2,1,0:T(8,128)(2,1)S(1)} %shard_map.83.refs_0_), channel_id=1, source_target_pairs={{0,4},{1,9},{2,6},{3,11},{4,0},{5,13},{6,2},{7,15},{8,12},{9,1},{1... | collective-permute-start | bytes 393224 | tf_op jit(solution)/shard_map/ppermute | solution.py:188
  6.8 10.6 %collective-permute-start.1 = (bf16[8,64,128]{2,1,0:T(8,128)(2,1)S(1)}, bf16[8,64,128]{2,1,0:T(8,128)(2,1)S(1)}, u32[]{:S(2)}, u32[]{:S(2)}) collective-permute-start(bf16[8,64,128]{2,1,0:T(8,128)(2,1)S(1)} %shard_map.83.refs_0_), channel_id=1, source_target_pairs={{0,2},{1,3},{2,0},{3,1},{4,6},{5,7},{6,4},{7,5},{8,10},{9,11},{10,... | collective-permute-start | bytes 393224 | tf_op jit(solution)/shard_map/ppermute | solution.py:188
  8.3 9.1 %collective-permute-start.6 = (bf16[8,64,128]{2,1,0:T(8,128)(2,1)S(1)}, bf16[8,64,128]{2,1,0:T(8,128)(2,1)S(1)}, u32[]{:S(2)}, u32[]{:S(2)}) collective-permute-start(bf16[8,64,128]{2,1,0:T(8,128)(2,1)S(1)} %shard_map.83.refs_0_), channel_id=1, source_target_pairs={{0,1},{1,0},{2,3},{3,2},{4,5},{5,4},{6,7},{7,6},{8,9},{9,8},{10,11... | collective-permute-start | bytes 393224 | tf_op jit(solution)/shard_map/ppermute | solution.py:188
  11.9 5.9 %collective-permute-start.3 = (bf16[8,64,128]{2,1,0:T(8,128)(2,1)S(1)}, bf16[8,64,128]{2,1,0:T(8,128)(2,1)S(1)}, u32[]{:S(2)}, u32[]{:S(2)}) collective-permute-start(bf16[8,64,128]{2,1,0:T(8,128)(2,1)S(1)} %collective-permute-done.2.refs_2_), channel_id=1, source_target_pairs={{0,4},{1,3},{2,6},{3,1},{4,0},{5,7},{6,2},{7,5},{8,12},{9,11},{10,... | collective-permute-start | bytes 393224 | tf_op jit(solution)/shard_map/ppermute | solution.py:188
  15.3 5.0 %collective-permute-start.4 = (bf16[8,64,128]{2,1,0:T(8,128)(2,1)S(1)}, bf16[8,64,128]{2,1,0:T(8,128)(2,1)S(1)}, u32[]{:S(2)}, u32[]{:S(2)}) collective-permute-start(bf16[8,64,128]{2,1,0:T(8,128)(2,1)S(1)} %collective-permute-done.refs_3_), channel_id=1, source_target_pairs={{0,2},{1,3},{2,0},{3,1},{4,6},{5,7},{6,4},{7,5},{8,10},{9,11},{10,... | collective-permute-start | bytes 393224 | tf_op jit(solution)/shard_map/ppermute | solution.py:188
  16.8 5.0 %collective-permute-start.5 = (bf16[8,64,128]{2,1,0:T(8,128)(2,1)S(1)}, bf16[8,64,128]{2,1,0:T(8,128)(2,1)S(1)}, u32[]{:S(2)}, u32[]{:S(2)}) collective-permute-start(bf16[8,64,128]{2,1,0:T(8,128)(2,1)S(1)} %collective-permute-done.2.refs_2_), channel_id=1, source_target_pairs={{0,2},{1,9},{2,0},{3,11},{4,6},{5,13},{6,4},{7,15},{8,10},{9,1},{1... | collective-permute-start | bytes 393224 | tf_op jit(solution)/shard_map/ppermute | solution.py:188
  17.4 4.5 %collective-permute-start.8 = (bf16[8,64,128]{2,1,0:T(8,128)(2,1)S(1)}, bf16[8,64,128]{2,1,0:T(8,128)(2,1)S(1)}, u32[]{:S(2)}, u32[]{:S(2)}) collective-permute-start(bf16[8,64,128]{2,1,0:T(8,128)(2,1)S(1)} %collective-permute-done.refs_3_), channel_id=1, source_target_pairs={{0,1},{1,0},{2,3},{3,2},{4,5},{5,4},{6,7},{7,6},{8,9},{9,8},{10,11... | collective-permute-start | bytes 393224 | tf_op jit(solution)/shard_map/ppermute | solution.py:188
  17.4 5.0 %collective-permute-start.7 = (bf16[8,64,128]{2,1,0:T(8,128)(2,1)S(1)}, bf16[8,64,128]{2,1,0:T(8,128)(2,1)S(1)}, u32[]{:S(2)}, u32[]{:S(2)}) collective-permute-start(bf16[8,64,128]{2,1,0:T(8,128)(2,1)S(1)} %collective-permute-done.2.refs_2_), channel_id=1, source_target_pairs={{0,1},{1,0},{2,3},{3,2},{4,5},{5,4},{6,7},{7,6},{8,9},{9,8},{10,11... | collective-permute-start | bytes 393224 | tf_op jit(solution)/shard_map/ppermute | solution.py:188
  17.9 7.3 %collective-permute-start.9 = (bf16[8,64,128]{2,1,0:T(8,128)(2,1)S(1)}, bf16[8,64,128]{2,1,0:T(8,128)(2,1)S(1)}, u32[]{:S(2)}, u32[]{:S(2)}) collective-permute-start(bf16[8,64,128]{2,1,0:T(8,128)(2,1)S(1)} %collective-permute-done.3.refs_4_), channel_id=1, source_target_pairs={{0,2},{1,9},{2,0},{3,11},{4,6},{5,13},{6,4},{7,15},{8,10},{9,1},{1... | collective-permute-start | bytes 393224 | tf_op jit(solution)/shard_map/ppermute | solution.py:188
  20.3 5.4 %collective-permute-start.10 = (bf16[8,64,128]{2,1,0:T(8,128)(2,1)S(1)}, bf16[8,64,128]{2,1,0:T(8,128)(2,1)S(1)}, u32[]{:S(2)}, u32[]{:S(2)}) collective-permute-start(bf16[8,64,128]{2,1,0:T(8,128)(2,1)S(1)} %collective-permute-done.1.refs_1_), channel_id=1, source_target_pairs={{0,1},{1,0},{2,3},{3,2},{4,5},{5,4},{6,7},{7,6},{8,9},{9,8},{10,11... | collective-permute-start | bytes 393224 | tf_op jit(solution)/shard_map/ppermute | solution.py:188
  21.8 3.8 %collective-permute-start.11 = (bf16[8,64,128]{2,1,0:T(8,128)(2,1)S(1)}, bf16[8,64,128]{2,1,0:T(8,128)(2,1)S(1)}, u32[]{:S(2)}, u32[]{:S(2)}) collective-permute-start(bf16[8,64,128]{2,1,0:T(8,128)(2,1)S(1)} %collective-permute-done.3.refs_4_), channel_id=1, source_target_pairs={{0,1},{1,0},{2,3},{3,2},{4,5},{5,4},{6,7},{7,6},{8,9},{9,8},{10,11... | collective-permute-start | bytes 393224 | tf_op jit(solution)/shard_map/ppermute | solution.py:188
  21.8 3.8 %collective-permute-start.12 = (bf16[8,64,128]{2,1,0:T(8,128)(2,1)S(1)}, bf16[8,64,128]{2,1,0:T(8,128)(2,1)S(1)}, u32[]{:S(2)}, u32[]{:S(2)}) collective-permute-start(bf16[8,64,128]{2,1,0:T(8,128)(2,1)S(1)} %collective-permute-done.4.refs_5_), channel_id=1, source_target_pairs={{0,1},{1,0},{2,3},{3,2},{4,5},{5,4},{6,7},{7,6},{8,9},{9,8},{10,11... | collective-permute-start | bytes 393224 | tf_op jit(solution)/shard_map/ppermute | solution.py:188
  22.3 3.3 %collective-permute-start.13 = (bf16[8,64,128]{2,1,0:T(8,128)(2,1)S(1)}, bf16[8,64,128]{2,1,0:T(8,128)(2,1)S(1)}, u32[]{:S(2)}, u32[]{:S(2)}) collective-permute-start(bf16[8,64,128]{2,1,0:T(8,128)(2,1)S(1)} %collective-permute-done.5.refs_6_), channel_id=1, source_target_pairs={{0,1},{1,0},{2,3},{3,2},{4,5},{5,4},{6,7},{7,6},{8,9},{9,8},{10,11... | collective-permute-start | bytes 393224 | tf_op jit(solution)/shard_map/ppermute | solution.py:188
  25.1 1.5 %collective-permute-start.14 = (bf16[8,64,128]{2,1,0:T(8,128)(2,1)S(1)}, bf16[8,64,128]{2,1,0:T(8,128)(2,1)S(1)}, u32[]{:S(2)}, u32[]{:S(2)}) collective-permute-start(bf16[8,64,128]{2,1,0:T(8,128)(2,1)S(1)} %collective-permute-done.9.refs_4_), channel_id=1, source_target_pairs={{0,1},{1,0},{2,3},{3,2},{4,5},{5,4},{6,7},{7,6},{8,9},{9,8},{10,11... | collective-permute-start | bytes 393224 | tf_op jit(solution)/shard_map/ppermute | solution.py:188

commit v14 on v13

--- a/solution.py
+++ b/solution.py
@@ -20,7 +20,7 @@
     return name[1] | CORE, name[0] | CORE
 
 
-LATE = (partner(SIDE), partner(THIRD), partner(FOURTH), partner(FIFTH), LAST, partner(LAST))
+LATE = (partner(SECOND), partner(THIRD), partner(FOURTH), partner(FIFTH), LAST, partner(LAST))
 EARLY = tuple(name for name in (
     OWN, SIDE, FIRST, SECOND, THIRD, FOURTH, FIFTH,
     partner(OWN), partner(SIDE), partner(FIRST), partner(SECOND), partner(THIRD), partner(FOURTH), partner(FIFTH),
@@ -251,7 +251,7 @@
 
         pass_on((OWN, FIRST), (OWN, SECOND), (OWN, SIDE))
         half = half_of(dims_left)
-        held = (SECOND,)
+        held = (FIRST,)
         half, ends = lax.optimization_barrier((half, [pieces[r] for r in held]))
         pieces.update(zip(held, ends))
         pass_on((FIRST, THIRD), (SECOND, FOURTH), (FIRST, FIFTH), (THIRD, LAST))

time: 29.8 us -> 30.4 us (1.020)
  starting transfers between devices: 14.6 us -> 17.2 us
  waiting for transfers between devices: 5.46 us -> 3.51 us
    ppermute x15, starting transfers between devices: 14.6 us -> 17.2 us  [swap(): lax.ppermute(piece, 'sec', [(i, i ^ (odd_bit if i & CORE else even_bit))...]
    ppermute x15, waiting for transfers between devices: 5.46 us -> 3.51 us  [swap(): lax.ppermute(piece, 'sec', [(i, i ^ (odd_bit if i & CORE else even_bit))...]
  transfers between devices with their start and end apart: 15 -> 15, of which waited for: 3 -> 4; matrix products, arithmetic and copies ran while one was open for 0% -> 0% of each run, Pallas kernels for 18% -> 18%
where the time goes in v14:
time: 30.4 us
  starting transfers between devices  17.2 us (57%)
  Pallas kernels  9.61 us (32%)
  waiting for transfers between devices  3.51 us (12%)
    ppermute x15, starting transfers between devices, swap(): lax.ppermute(piece, 'sec', [(i, i ^ (odd_bit if i & CORE else even_bit))...  17.2 us
    ppermute x15, waiting for transfers between devices, swap(): lax.ppermute(piece, 'sec', [(i, i ^ (odd_bit if i & CORE else even_bit))...  3.51 us
    pallas_call x1, Pallas kernels, per_device(): pl.pallas_call(late_kernel, out_shape=jax.ShapeDtypeStruct(psi.shape, jnp...  3.06 us
    pallas_call x1, Pallas kernels, per_device(): pl.pallas_call(functools.partial(early_kernel, pair_count), out_shape=(ja...  2.73 us
    pallas_call x1, Pallas kernels, half_of(): pl.pallas_call(left_kernel, out_shape=jax.ShapeDtypeStruct(psi.shape, jnp...  2.72 us
    pallas_call x1, Pallas kernels, per_device(): pl.pallas_call(pack_kernel, out_shape=jax.ShapeDtypeStruct((pair_count, t...  1.09 us
  transfers between devices with their start and end apart: 15, of which 4 were waited for; matrix products, arithmetic and copies ran while one was open for 0% of the time, Pallas kernels for 18%

profile of v14, /device:TPU:0, one launch (start us, length us, event | category | flops | bytes accessed | tf_op | source)
XLA Modules:
  0.0 30.4 jit_solution(17063992779077014827)
XLA Ops:
  0.0 1.1 %shard_map.83.refs_0_ = bf16[8,64,128]{2,1,0:T(8,128)(2,1)S(1)} custom-call(s32[16]{0:T(128)} %dims_hbm.3, bf16[16,64,64]{2,1,0:T(8,128)(2,1)} %right_hbm.1), custom_call_target="tpu_custom_call" | custom-call | bytes 131072 | tf_op jit(solution)/shard_map/pallas_call | solution.py:208
  1.1 4.1 %collective-permute-start = (bf16[8,64,128]{2,1,0:T(8,128)(2,1)S(1)}, bf16[8,64,128]{2,1,0:T(8,128)(2,1)S(1)}, u32[]{:S(2)}, u32[]{:S(2)}) collective-permute-start(bf16[8,64,128]{2,1,0:T(8,128)(2,1)S(1)} %shard_map.83.refs_0_), channel_id=1, source_target_pairs={{0,8},{1,5},{2,10},{3,7},{4,12},{5,1},{6,14},{7,3},{8,0},{9,13},{1... | collective-permute-start | bytes 393224 | tf_op jit(solution)/shard_map/ppermute | solution.py:188
  5.2 0.0 collective-permute-start.6
  5.2 1.6 %collective-permute-start.2 = (bf16[8,64,128]{2,1,0:T(8,128)(2,1)S(1)}, bf16[8,64,128]{2,1,0:T(8,128)(2,1)S(1)}, u32[]{:S(2)}, u32[]{:S(2)}) collective-permute-start(bf16[8,64,128]{2,1,0:T(8,128)(2,1)S(1)} %shard_map.83.refs_0_), channel_id=1, source_target_pairs={{0,4},{1,9},{2,6},{3,11},{4,0},{5,13},{6,2},{7,15},{8,12},{9,1},{1... | collective-permute-start | bytes 393224 | tf_op jit(solution)/shard_map/ppermute | solution.py:188
  6.8 1.5 %collective-permute-start.1 = (bf16[8,64,128]{2,1,0:T(8,128)(2,1)S(1)}, bf16[8,64,128]{2,1,0:T(8,128)(2,1)S(1)}, u32[]{:S(2)}, u32[]{:S(2)}) collective-permute-start(bf16[8,64,128]{2,1,0:T(8,128)(2,1)S(1)} %shard_map.83.refs_0_), channel_id=1, source_target_pairs={{0,2},{1,3},{2,0},{3,1},{4,6},{5,7},{6,4},{7,5},{8,10},{9,11},{10,... | collective-permute-start | bytes 393224 | tf_op jit(solution)/shard_map/ppermute | solution.py:188
  8.3 2.7 %shard_map.82.half_ref = bf16[8,8,64,128]{3,2,1,0:T(8,128)(2,1)S(1)} custom-call(s32[8]{0:T(128)} %dims_hbm.2, s32[8,8]{1,0:T(8,128)} %bitcast.1, bf16[8,64,64]{2,1,0:T(8,128)(2,1)} %left_hbm.1, bf16[8,8,64,128]{3,2,1,0:T(8,128)(2,1)} %psi_hbm.1), custom_call_target="tpu_custom_call" | custom-call | flops 67108864 | bytes 1048576 | tf_op jit(solution)/shard_map/pallas_call | solution.py:224
  11.0 0.0 collective-permute-done.refs_2_
  11.0 2.3 %collective-permute-start.3 = (bf16[8,64,128]{2,1,0:T(8,128)(2,1)S(1)}, bf16[8,64,128]{2,1,0:T(8,128)(2,1)S(1)}, u32[]{:S(2)}, u32[]{:S(2)}) collective-permute-start(bf16[8,64,128]{2,1,0:T(8,128)(2,1)S(1)} %collective-permute-done.refs_2_), channel_id=1, source_target_pairs={{0,4},{1,3},{2,6},{3,1},{4,0},{5,7},{6,2},{7,5},{8,12},{9,11},{10,... | collective-permute-start | bytes 393224 | tf_op jit(solution)/shard_map/ppermute | solution.py:188
  13.4 0.0 collective-permute-done.2.refs_3_
  13.4 1.5 %collective-permute-start.4 = (bf16[8,64,128]{2,1,0:T(8,128)(2,1)S(1)}, bf16[8,64,128]{2,1,0:T(8,128)(2,1)S(1)}, u32[]{:S(2)}, u32[]{:S(2)}) collective-permute-start(bf16[8,64,128]{2,1,0:T(8,128)(2,1)S(1)} %collective-permute-done.2.refs_3_), channel_id=1, source_target_pairs={{0,2},{1,3},{2,0},{3,1},{4,6},{5,7},{6,4},{7,5},{8,10},{9,11},{10,... | collective-permute-start | bytes 393224 | tf_op jit(solution)/shard_map/ppermute | solution.py:188
  14.9 0.0 collective-permute-done.1.refs_1_
  14.9 0.0 collective-permute-start.7
  14.9 0.5 %collective-permute-start.8 = (bf16[8,64,128]{2,1,0:T(8,128)(2,1)S(1)}, bf16[8,64,128]{2,1,0:T(8,128)(2,1)S(1)}, u32[]{:S(2)}, u32[]{:S(2)}) collective-permute-start(bf16[8,64,128]{2,1,0:T(8,128)(2,1)S(1)} %collective-permute-done.refs_2_), channel_id=1, source_target_pairs={{0,1},{1,0},{2,3},{3,2},{4,5},{5,4},{6,7},{7,6},{8,9},{9,8},{10,11... | collective-permute-start | bytes 393224 | tf_op jit(solution)/shard_map/ppermute | solution.py:188
  15.4 0.0 collective-permute-done.6.refs_7_
  15.4 0.5 %collective-permute-start.5 = (bf16[8,64,128]{2,1,0:T(8,128)(2,1)S(1)}, bf16[8,64,128]{2,1,0:T(8,128)(2,1)S(1)}, u32[]{:S(2)}, u32[]{:S(2)}) collective-permute-start(bf16[8,64,128]{2,1,0:T(8,128)(2,1)S(1)} %collective-permute-done.refs_2_), channel_id=1, source_target_pairs={{0,2},{1,9},{2,0},{3,11},{4,6},{5,13},{6,4},{7,15},{8,10},{9,1},{1... | collective-permute-start | bytes 393224 | tf_op jit(solution)/shard_map/ppermute | solution.py:188
  15.9 0.4 %collective-permute-done.3.refs_4_ = bf16[8,64,128]{2,1,0:T(8,128)(2,1)S(1)} collective-permute-done((bf16[8,64,128]{2,1,0:T(8,128)(2,1)S(1)}, bf16[8,64,128]{2,1,0:T(8,128)(2,1)S(1)}, u32[]{:S(2)}, u32[]{:S(2)}) %collective-permute-start.3) | collective-permute-done | bytes 131104 | tf_op jit(solution)/shard_map/ppermute | solution.py:188
  16.3 1.5 %collective-permute-start.9 = (bf16[8,64,128]{2,1,0:T(8,128)(2,1)S(1)}, bf16[8,64,128]{2,1,0:T(8,128)(2,1)S(1)}, u32[]{:S(2)}, u32[]{:S(2)}) collective-permute-start(bf16[8,64,128]{2,1,0:T(8,128)(2,1)S(1)} %collective-permute-done.3.refs_4_), channel_id=1, source_target_pairs={{0,2},{1,9},{2,0},{3,11},{4,6},{5,13},{6,4},{7,15},{8,10},{9,1},{1... | collective-permute-start | bytes 393224 | tf_op jit(solution)/shard_map/ppermute | solution.py:188
  17.8 0.5 %collective-permute-done.4.refs_5_ = bf16[8,64,128]{2,1,0:T(8,128)(2,1)S(1)} collective-permute-done((bf16[8,64,128]{2,1,0:T(8,128)(2,1)S(1)}, bf16[8,64,128]{2,1,0:T(8,128)(2,1)S(1)}, u32[]{:S(2)}, u32[]{:S(2)}) %collective-permute-start.4) | collective-permute-done | bytes 131104 | tf_op jit(solution)/shard_map/ppermute | solution.py:188
  18.3 0.2 collective-permute-start.10
  18.6 0.0 collective-permute-done.7.refs_8_
  18.6 0.3 collective-permute-start.11
  18.8 0.0 collective-permute-done.8.refs_9_
  18.8 0.2 collective-permute-start.12
  19.1 1.3 %collective-permute-done.5.refs_6_ = bf16[8,64,128]{2,1,0:T(8,128)(2,1)S(1)} collective-permute-done((bf16[8,64,128]{2,1,0:T(8,128)(2,1)S(1)}, bf16[8,64,128]{2,1,0:T(8,128)(2,1)S(1)}, u32[]{:S(2)}, u32[]{:S(2)}) %collective-permute-start.5) | collective-permute-done | bytes 131104 | tf_op jit(solution)/shard_map/ppermute | solution.py:188
  20.3 2.8 %collective-permute-start.13 = (bf16[8,64,128]{2,1,0:T(8,128)(2,1)S(1)}, bf16[8,64,128]{2,1,0:T(8,128)(2,1)S(1)}, u32[]{:S(2)}, u32[]{:S(2)}) collective-permute-start(bf16[8,64,128]{2,1,0:T(8,128)(2,1)S(1)} %collective-permute-done.5.refs_6_), channel_id=1, source_target_pairs={{0,1},{1,0},{2,3},{3,2},{4,5},{5,4},{6,7},{7,6},{8,9},{9,8},{10,11... | collective-permute-start | bytes 393224 | tf_op jit(solution)/shard_map/ppermute | solution.py:188
  23.2 2.7 %shard_map.84 = (bf16[8,8,64,128]{3,2,1,0:T(8,128)(2,1)S(1)}, s32[65]{0:T(128)S(4)}) custom-call(s32[8,8]{1,0:T(8,128)} %owner_hbm.1, s32[8,8]{1,0:T(8,128)} %slot_hbm.1, bf16[8,8,64,128]{3,2,1,0:T(8,128)(2,1)S(1)} %shard_map.82.half_ref, bf16[8,64,128]{2,1,0:T(8,128)(2,1)S(1)} %shard_map.83.refs_0_, bf16[8,64,128]{2,1,0:T(8,128)(2,1)S(1)} %collective-permute-done.1.refs_1_, ...), custom_call_target="tpu_custom_call" | custom-call | flops 67108864 | bytes 1048576 | tf_op jit(solution)/shard_map/pallas_call | solution.py:264
  25.9 0.0 collective-permute-done.9.refs_4_
  25.9 0.1 collective-permute-start.14
  26.0 0.0 collective-permute-done.10.refs_0_
  26.0 0.0 collective-permute-done.12.refs_2_
  26.0 0.0 collective-permute-done.13.refs_3_
  26.0 0.0 collective-permute-done.11.refs_1_
  26.0 1.3 %collective-permute-done.14.refs_5_ = bf16[8,64,128]{2,1,0:T(8,128)(2,1)S(1)} collective-permute-done((bf16[8,64,128]{2,1,0:T(8,128)(2,1)S(1)}, bf16[8,64,128]{2,1,0:T(8,128)(2,1)S(1)}, u32[]{:S(2)}, u32[]{:S(2)}) %collective-permute-start.14) | collective-permute-done | bytes 131104 | tf_op jit(solution)/shard_map/ppermute | solution.py:188
  27.3 3.1 %shard_map.85 = bf16[8,8,64,128]{3,2,1,0:T(8,128)(2,1)} custom-call(s32[65]{0:T(128)S(4)} %get-tuple-element.13.late_ref, bf16[8,8,64,128]{3,2,1,0:T(8,128)(2,1)S(1)} %get-tuple-element.15.early_ref, bf16[8,8,64,128]{3,2,1,0:T(8,128)(2,1)S(1)} %shard_map.82.half_ref, bf16[8,64,128]{2,1,0:T(8,128)(2,1)S(1)} %collective-permute-done.10.refs_0_, ...), custom_call_target="tpu_custom_call" | custom-call | flops 16777216 | bytes 524288 | tf_op jit(solution)/shard_map/pallas_call | solution.py:287
Async XLA Ops:
  1.1 9.9 %collective-permute-start = (bf16[8,64,128]{2,1,0:T(8,128)(2,1)S(1)}, bf16[8,64,128]{2,1,0:T(8,128)(2,1)S(1)}, u32[]{:S(2)}, u32[]{:S(2)}) collective-permute-start(bf16[8,64,128]{2,1,0:T(8,128)(2,1)S(1)} %shard_map.83.refs_0_), channel_id=1, source_target_pairs={{0,8},{1,5},{2,10},{3,7},{4,12},{5,1},{6,14},{7,3},{8,0},{9,13},{1... | collective-permute-start | bytes 393224 | tf_op jit(solution)/shard_map/ppermute | solution.py:188
  5.2 10.2 %collective-permute-start.6 = (bf16[8,64,128]{2,1,0:T(8,128)(2,1)S(1)}, bf16[8,64,128]{2,1,0:T(8,128)(2,1)S(1)}, u32[]{:S(2)}, u32[]{:S(2)}) collective-permute-start(bf16[8,64,128]{2,1,0:T(8,128)(2,1)S(1)} %shard_map.83.refs_0_), channel_id=1, source_target_pairs={{0,1},{1,0},{2,3},{3,2},{4,5},{5,4},{6,7},{7,6},{8,9},{9,8},{10,11... | collective-permute-start | bytes 393224 | tf_op jit(solution)/shard_map/ppermute | solution.py:188
  5.2 8.2 %collective-permute-start.2 = (bf16[8,64,128]{2,1,0:T(8,128)(2,1)S(1)}, bf16[8,64,128]{2,1,0:T(8,128)(2,1)S(1)}, u32[]{:S(2)}, u32[]{:S(2)}) collective-permute-start(bf16[8,64,128]{2,1,0:T(8,128)(2,1)S(1)} %shard_map.83.refs_0_), channel_id=1, source_target_pairs={{0,4},{1,9},{2,6},{3,11},{4,0},{5,13},{6,2},{7,15},{8,12},{9,1},{1... | collective-permute-start | bytes 393224 | tf_op jit(solution)/shard_map/ppermute | solution.py:188
  6.8 8.1 %collective-permute-start.1 = (bf16[8,64,128]{2,1,0:T(8,128)(2,1)S(1)}, bf16[8,64,128]{2,1,0:T(8,128)(2,1)S(1)}, u32[]{:S(2)}, u32[]{:S(2)}) collective-permute-start(bf16[8,64,128]{2,1,0:T(8,128)(2,1)S(1)} %shard_map.83.refs_0_), channel_id=1, source_target_pairs={{0,2},{1,3},{2,0},{3,1},{4,6},{5,7},{6,4},{7,5},{8,10},{9,11},{10,... | collective-permute-start | bytes 393224 | tf_op jit(solution)/shard_map/ppermute | solution.py:188
  11.0 5.3 %collective-permute-start.3 = (bf16[8,64,128]{2,1,0:T(8,128)(2,1)S(1)}, bf16[8,64,128]{2,1,0:T(8,128)(2,1)S(1)}, u32[]{:S(2)}, u32[]{:S(2)}) collective-permute-start(bf16[8,64,128]{2,1,0:T(8,128)(2,1)S(1)} %collective-permute-done.refs_2_), channel_id=1, source_target_pairs={{0,4},{1,3},{2,6},{3,1},{4,0},{5,7},{6,2},{7,5},{8,12},{9,11},{10,... | collective-permute-start | bytes 393224 | tf_op jit(solution)/shard_map/ppermute | solution.py:188
  13.4 5.0 %collective-permute-start.4 = (bf16[8,64,128]{2,1,0:T(8,128)(2,1)S(1)}, bf16[8,64,128]{2,1,0:T(8,128)(2,1)S(1)}, u32[]{:S(2)}, u32[]{:S(2)}) collective-permute-start(bf16[8,64,128]{2,1,0:T(8,128)(2,1)S(1)} %collective-permute-done.2.refs_3_), channel_id=1, source_target_pairs={{0,2},{1,3},{2,0},{3,1},{4,6},{5,7},{6,4},{7,5},{8,10},{9,11},{10,... | collective-permute-start | bytes 393224 | tf_op jit(solution)/shard_map/ppermute | solution.py:188
  14.9 3.7 %collective-permute-start.7 = (bf16[8,64,128]{2,1,0:T(8,128)(2,1)S(1)}, bf16[8,64,128]{2,1,0:T(8,128)(2,1)S(1)}, u32[]{:S(2)}, u32[]{:S(2)}) collective-permute-start(bf16[8,64,128]{2,1,0:T(8,128)(2,1)S(1)} %collective-permute-done.1.refs_1_), channel_id=1, source_target_pairs={{0,1},{1,0},{2,3},{3,2},{4,5},{5,4},{6,7},{7,6},{8,9},{9,8},{10,11... | collective-permute-start | bytes 393224 | tf_op jit(solution)/shard_map/ppermute | solution.py:188
  14.9 4.0 %collective-permute-start.8 = (bf16[8,64,128]{2,1,0:T(8,128)(2,1)S(1)}, bf16[8,64,128]{2,1,0:T(8,128)(2,1)S(1)}, u32[]{:S(2)}, u32[]{:S(2)}) collective-permute-start(bf16[8,64,128]{2,1,0:T(8,128)(2,1)S(1)} %collective-permute-done.refs_2_), channel_id=1, source_target_pairs={{0,1},{1,0},{2,3},{3,2},{4,5},{5,4},{6,7},{7,6},{8,9},{9,8},{10,11... | collective-permute-start | bytes 393224 | tf_op jit(solution)/shard_map/ppermute | solution.py:188
  15.4 5.0 %collective-permute-start.5 = (bf16[8,64,128]{2,1,0:T(8,128)(2,1)S(1)}, bf16[8,64,128]{2,1,0:T(8,128)(2,1)S(1)}, u32[]{:S(2)}, u32[]{:S(2)}) collective-permute-start(bf16[8,64,128]{2,1,0:T(8,128)(2,1)S(1)} %collective-permute-done.refs_2_), channel_id=1, source_target_pairs={{0,2},{1,9},{2,0},{3,11},{4,6},{5,13},{6,4},{7,15},{8,10},{9,1},{1... | collective-permute-start | bytes 393224 | tf_op jit(solution)/shard_map/ppermute | solution.py:188
  16.3 9.6 %collective-permute-start.9 = (bf16[8,64,128]{2,1,0:T(8,128)(2,1)S(1)}, bf16[8,64,128]{2,1,0:T(8,128)(2,1)S(1)}, u32[]{:S(2)}, u32[]{:S(2)}) collective-permute-start(bf16[8,64,128]{2,1,0:T(8,128)(2,1)S(1)} %collective-permute-done.3.refs_4_), channel_id=1, source_target_pairs={{0,2},{1,9},{2,0},{3,11},{4,6},{5,13},{6,4},{7,15},{8,10},{9,1},{1... | collective-permute-start | bytes 393224 | tf_op jit(solution)/shard_map/ppermute | solution.py:188
  18.3 7.7 %collective-permute-start.10 = (bf16[8,64,128]{2,1,0:T(8,128)(2,1)S(1)}, bf16[8,64,128]{2,1,0:T(8,128)(2,1)S(1)}, u32[]{:S(2)}, u32[]{:S(2)}) collective-permute-start(bf16[8,64,128]{2,1,0:T(8,128)(2,1)S(1)} %collective-permute-done.2.refs_3_), channel_id=1, source_target_pairs={{0,1},{1,0},{2,3},{3,2},{4,5},{5,4},{6,7},{7,6},{8,9},{9,8},{10,11... | collective-permute-start | bytes 393224 | tf_op jit(solution)/shard_map/ppermute | solution.py:188
  18.6 7.4 %collective-permute-start.11 = (bf16[8,64,128]{2,1,0:T(8,128)(2,1)S(1)}, bf16[8,64,128]{2,1,0:T(8,128)(2,1)S(1)}, u32[]{:S(2)}, u32[]{:S(2)}) collective-permute-start(bf16[8,64,128]{2,1,0:T(8,128)(2,1)S(1)} %collective-permute-done.3.refs_4_), channel_id=1, source_target_pairs={{0,1},{1,0},{2,3},{3,2},{4,5},{5,4},{6,7},{7,6},{8,9},{9,8},{10,11... | collective-permute-start | bytes 393224 | tf_op jit(solution)/shard_map/ppermute | solution.py:188
  18.8 7.1 %collective-permute-start.12 = (bf16[8,64,128]{2,1,0:T(8,128)(2,1)S(1)}, bf16[8,64,128]{2,1,0:T(8,128)(2,1)S(1)}, u32[]{:S(2)}, u32[]{:S(2)}) collective-permute-start(bf16[8,64,128]{2,1,0:T(8,128)(2,1)S(1)} %collective-permute-done.4.refs_5_), channel_id=1, source_target_pairs={{0,1},{1,0},{2,3},{3,2},{4,5},{5,4},{6,7},{7,6},{8,9},{9,8},{10,11... | collective-permute-start | bytes 393224 | tf_op jit(solution)/shard_map/ppermute | solution.py:188
  20.3 5.7 %collective-permute-start.13 = (bf16[8,64,128]{2,1,0:T(8,128)(2,1)S(1)}, bf16[8,64,128]{2,1,0:T(8,128)(2,1)S(1)}, u32[]{:S(2)}, u32[]{:S(2)}) collective-permute-start(bf16[8,64,128]{2,1,0:T(8,128)(2,1)S(1)} %collective-permute-done.5.refs_6_), channel_id=1, source_target_pairs={{0,1},{1,0},{2,3},{3,2},{4,5},{5,4},{6,7},{7,6},{8,9},{9,8},{10,11... | collective-permute-start | bytes 393224 | tf_op jit(solution)/shard_map/ppermute | solution.py:188
  25.9 1.4 %collective-permute-start.14 = (bf16[8,64,128]{2,1,0:T(8,128)(2,1)S(1)}, bf16[8,64,128]{2,1,0:T(8,128)(2,1)S(1)}, u32[]{:S(2)}, u32[]{:S(2)}) collective-permute-start(bf16[8,64,128]{2,1,0:T(8,128)(2,1)S(1)} %collective-permute-done.9.refs_4_), channel_id=1, source_target_pairs={{0,1},{1,0},{2,3},{3,2},{4,5},{5,4},{6,7},{7,6},{8,9},{9,8},{10,11... | collective-permute-start | bytes 393224 | tf_op jit(solution)/shard_map/ppermute | solution.py:188

commit v15 on v9

--- a/solution.py
+++ b/solution.py
@@ -8,11 +8,11 @@
 from jax.sharding import PartitionSpec as P
 
 VMEM_LIMIT = 48 * 1024 * 1024
-GROUP = 8
 FAR, NEAR, CROSS, CORE = 8, 4, 2, 1
-LATE = (FAR | CORE, FAR | NEAR | CORE, FAR | CROSS | CORE, FAR | NEAR | CROSS, FAR | NEAR | CROSS | CORE)
-EARLY = tuple(r for r in range(16) if r not in LATE)
-ORDER = EARLY + LATE
+MIDDLE = (FAR | CORE, FAR | NEAR | CORE, FAR | CROSS | CORE, FAR | NEAR | CROSS)
+LAST = (FAR | NEAR | CROSS | CORE,)
+EARLY = tuple(r for r in range(16) if r not in MIDDLE + LAST)
+ORDER = EARLY + MIDDLE + LAST
 
 
 def load_all(*copies):
@@ -99,9 +99,10 @@
 
 def early_kernel(pair_count, owner_hbm, slot_hbm, half_ref, *refs):
     piece_refs = refs[:-7]
-    out_hbm, late_ref, pairs_ref, out_ref, owner_ref, slot_ref, sems = refs[-7:]
+    out_hbm, list_ref, pairs_ref, out_ref, owner_ref, slot_ref, sems = refs[-7:]
     sectors, blocks, tile, width = out_ref.shape
     items, held = sectors * blocks, pairs_ref.shape[0]
+    last = held + len(MIDDLE) * pair_count
     copies = load_all((owner_hbm, owner_ref, sems.at[0]), (slot_hbm, slot_ref, sems.at[1]))
     merge(piece_refs, pairs_ref)
     me = lax.axis_index("sec")
@@ -119,53 +120,57 @@
                 at = piece_at(owner ^ me) if len(piece_refs) > 1 else owner
                 second = slot >= pair_count
                 at = at * pair_count + jnp.where(second, slot - pair_count, slot)
-                late = at >= held
-                forms.append(block_form(pairs_ref[jnp.where(late, 0, at)], second))
-                late_ref[listed] = ((at - held) * 2 + second.astype(jnp.int32)) * items + a * blocks + k + u
-                listed = listed + late.astype(jnp.int32)
+                forms.append(block_form(pairs_ref[jnp.where(at >= held, 0, at)], second))
+                in_last = at >= last
+                entry = (at - jnp.where(in_last, last, held)) * 2 + second.astype(jnp.int32)
+                entry = entry * items + a * blocks + k + u
+                list_ref[jnp.where(in_last, items + 1 + listed[1], listed[0])] = entry
+                in_middle = (at >= held) & (at < last)
+                listed = listed[0] + in_middle.astype(jnp.int32), listed[1] + in_last.astype(jnp.int32)
             out_ref[a, k], out_ref[a, k + 1] = two_products([half_ref[a, k], half_ref[a, k + 1]], forms)
         store(a).start()
         return listed
 
-    listed = lax.fori_loop(0, sectors, one, 0, unroll=2)
-    late_ref[items] = listed
+    listed = lax.fori_loop(0, sectors, one, (0, 0), unroll=2)
+    list_ref[items] = listed[0]
+    list_ref[2 * items + 1] = listed[1]
     for a in range(sectors):
         store(a).wait()
 
 
-def late_kernel(late_ref, early_hbm, half_ref, *refs):
+def late_kernel(group_size, first, list_ref, early_hbm, half_ref, *refs):
     piece_refs, (out_hbm, pairs_ref, out_ref, sems) = refs[:-4], refs[-4:]
     sectors, blocks, tile, width = half_ref.shape
     items = sectors * blocks
-    listed = late_ref[items]
+    listed = list_ref[first + items]
     merge(piece_refs, pairs_ref)
 
     def store(slot, item):
         return pltpu.make_async_copy(out_ref.at[slot], out_hbm.at[item // blocks, item % blocks], sems.at[slot])
 
     def group(g, carry):
-        for u in range(0, GROUP, 2):
-            slot = g * GROUP + u
-            entries = [late_ref[jnp.minimum(slot + n, listed - 1)] for n in range(2)]
+        for u in range(0, group_size, 2):
+            slot = g * group_size + u
+            entries = [list_ref[first + jnp.minimum(slot + n, listed - 1)] for n in range(2)]
             halves, forms = [], []
             for entry in entries:
                 item, at = entry % items, entry // items
                 halves.append(half_ref[item // blocks, item % blocks])
                 forms.append(block_form(pairs_ref[at // 2], at % 2 == 1))
             out_ref[slot], out_ref[slot + 1] = two_products(halves, forms)
-        for u in range(GROUP):
-            slot = g * GROUP + u
+        for u in range(group_size):
+            slot = g * group_size + u
 
             @pl.when(slot < listed)
             def _():
-                store(slot, late_ref[slot] % items).start()
+                store(slot, list_ref[first + slot] % items).start()
         return carry
 
     def drain(slot, carry):
         store(slot, 0).wait()
         return carry
 
-    lax.fori_loop(0, (listed + GROUP - 1) // GROUP, group, 0)
+    lax.fori_loop(0, (listed + group_size - 1) // group_size, group, 0)
     lax.fori_loop(0, listed, drain, 0)
 
 
@@ -230,15 +235,13 @@
             for r, bit in pairs_of:
                 pieces[r | bit] = swap(pieces[r], bit)
 
-        pass_on((0, FAR), (0, NEAR), (0, CROSS), (0, CORE), (NEAR, CROSS), (FAR, NEAR), (FAR, CROSS), (FAR | NEAR, CROSS))
-        held = (FAR,)
-        dims_left, ends = lax.optimization_barrier((dims_left, [pieces[r] for r in held]))
-        pieces.update(zip(held, ends))
+        pass_on((0, FAR), (0, NEAR), (0, CROSS))
         half = half_of(dims_left)
-        held = (NEAR, CROSS, NEAR | CROSS,)
+        held = (0, NEAR,)
         half, ends = lax.optimization_barrier((half, [pieces[r] for r in held]))
         pieces.update(zip(held, ends))
-        pass_on((NEAR, CORE), (CROSS, CORE), (NEAR | CROSS, CORE), (FAR | NEAR, CORE), (FAR, CORE), (FAR | CROSS, CORE))
+        pass_on((NEAR, CROSS), (FAR, NEAR), (FAR, CROSS), (FAR | NEAR, CROSS))
+        pass_on((0, CORE), (NEAR, CORE), (CROSS, CORE), (NEAR | CROSS, CORE), (FAR | NEAR, CORE), (FAR, CORE), (FAR | CROSS, CORE))
         early = [pieces[r] for r in EARLY]
     else:
         half = half_of(dims_left)
@@ -248,7 +251,7 @@
         functools.partial(early_kernel, pair_count),
         out_shape=(
             jax.ShapeDtypeStruct(psi.shape, jnp.bfloat16),
-            jax.ShapeDtypeStruct((items + 1,), jnp.int32),
+            pltpu.SMEM((2 * items + 2,), jnp.int32),
         ),
         in_specs=[hbm, hbm] + [vmem] * (1 + len(early)),
         out_specs=(hbm, smem),
@@ -262,26 +265,29 @@
         compiler_params=params,
         cost_estimate=pl.CostEstimate(flops=flops, bytes_accessed=2 * psi.size, transcendentals=0),
     )(*in_hbm(right_owner, right_slot), half, *early)
-    if by_swaps:
-        ends = (FAR | NEAR | CROSS,)
-        held, sigma = lax.optimization_barrier(([pieces[r] for r in ends], sigma))
-        for r, piece in zip(ends, held):
-            pieces[r], pieces[r | CORE] = piece, swap(piece, CORE)
-        late = [pieces[r] for r in LATE]
-        sigma = pl.pallas_call(
-            late_kernel,
+
+    def late(group_size, first, sigma, names):
+        return pl.pallas_call(
+            functools.partial(late_kernel, group_size, first),
             out_shape=jax.ShapeDtypeStruct(psi.shape, jnp.bfloat16),
-            in_specs=[smem, hbm] + [vmem] * (1 + len(late)),
+            in_specs=[smem, hbm] + [vmem] * (1 + len(names)),
             out_specs=hbm,
             scratch_shapes=[
-                pltpu.VMEM((len(late) * pair_count, tile, 2 * tile), jnp.bfloat16),
-                pltpu.VMEM((items + GROUP, tile, width), jnp.bfloat16),
+                pltpu.VMEM((len(names) * pair_count, tile, 2 * tile), jnp.bfloat16),
+                pltpu.VMEM((items + group_size, tile, width), jnp.bfloat16),
                 pltpu.SemaphoreType.DMA((items,)),
             ],
             input_output_aliases={1: 0},
             compiler_params=params,
-            cost_estimate=pl.CostEstimate(flops=flops // 4, bytes_accessed=psi.size, transcendentals=0),
-        )(listed, sigma, half, *late)
+            cost_estimate=pl.CostEstimate(flops=flops // 4, bytes_accessed=psi.size // 2, transcendentals=0),
+        )(pltpu.with_memory_space_constraint(listed, pltpu.SMEM), sigma, half, *[pieces[r] for r in names])
+
+    if by_swaps:
+        top = FAR | NEAR | CROSS
+        pieces[top], sigma = lax.optimization_barrier((pieces[top], sigma))
+        pieces[top | CORE] = swap(pieces[top], CORE)
+        sigma = late(8, 0, sigma, MIDDLE)
+        sigma = late(4, items + 1, sigma, LAST)
     if lax.axis_size("op") > 1:
         sigma = lax.psum_scatter(sigma, "op", scatter_dimension=3, tiled=True)
     return sigma

time: 28.3 us -> 27.6 us (0.975); the launches traced: 27.9 us -> 27.5 us
  Pallas kernels: 10 us -> 10.8 us
  waiting for transfers between devices: 4.43 us -> 3.82 us
  starting transfers between devices: 13.4 us -> 12.8 us
    pallas_call x1 -> x2, Pallas kernels: 2.47 us -> 3.74 us  [late(): pl.pallas_call(functools.partial(late_kernel, group_size, first), out_sha...]
    ppermute x15, waiting for transfers between devices: 4.43 us -> 3.82 us  [swap(): return lax.ppermute(piece, 'sec', [(i, i ^ bit) for i in range(count)])]
    ppermute x15, starting transfers between devices: 13.4 us -> 12.8 us  [swap(): return lax.ppermute(piece, 'sec', [(i, i ^ bit) for i in range(count)])]
    pallas_call x1, Pallas kernels: 3.75 us -> 3.27 us  [per_device(): pl.pallas_call(functools.partial(early_kernel, pair_count), out_shape=(ja...]
  transfers between devices with their start and end apart: 15 -> 15, of which waited for: 4 -> 3; matrix products, arithmetic and copies ran while one was open for 0% -> 0% of each run, Pallas kernels for 23% -> 30%
where the time goes in v15:
time: 27.6 us; the launch traced here: 27.5 us
  starting transfers between devices  12.8 us (46%)
  Pallas kernels  10.8 us (39%)
  waiting for transfers between devices  3.82 us (14%)
    ppermute x15, starting transfers between devices, swap(): return lax.ppermute(piece, 'sec', [(i, i ^ bit) for i in range(count)])  12.8 us
    ppermute x15, waiting for transfers between devices, swap(): return lax.ppermute(piece, 'sec', [(i, i ^ bit) for i in range(count)])  3.82 us
    pallas_call x2, Pallas kernels, late(): pl.pallas_call(functools.partial(late_kernel, group_size, first), out_sha...  3.74 us
    pallas_call x1, Pallas kernels, per_device(): pl.pallas_call(functools.partial(early_kernel, pair_count), out_shape=(ja...  3.27 us
    pallas_call x1, Pallas kernels, half_of(): pl.pallas_call(left_kernel, out_shape=jax.ShapeDtypeStruct(psi.shape, jnp...  2.73 us
    pallas_call x1, Pallas kernels, per_device(): pl.pallas_call(pack_kernel, out_shape=jax.ShapeDtypeStruct((pair_count, t...  1.09 us
  transfers between devices with their start and end apart: 15, of which 3 were waited for; matrix products, arithmetic and copies ran while one was open for 0% of the time, Pallas kernels for 30%

profile of v15, /device:TPU:0, one launch (start us, length us, event | category | flops | bytes accessed | tf_op | source)
XLA Modules:
  0.0 27.5 jit_solution(521990806513376268)
XLA Ops:
  0.0 1.1 %shard_map.83.refs_0_ = bf16[8,64,128]{2,1,0:T(8,128)(2,1)S(1)} custom-call(s32[16]{0:T(128)} %dims_hbm.3, bf16[16,64,64]{2,1,0:T(8,128)(2,1)} %right_hbm.1), custom_call_target="tpu_custom_call" | custom-call | bytes 131072 | tf_op jit(solution)/shard_map/pallas_call | solution.py:199
  1.1 3.1 %collective-permute-start = (bf16[8,64,128]{2,1,0:T(8,128)(2,1)S(1)}, bf16[8,64,128]{2,1,0:T(8,128)(2,1)S(1)}, u32[]{:S(2)}, u32[]{:S(2)}) collective-permute-start(bf16[8,64,128]{2,1,0:T(8,128)(2,1)S(1)} %shard_map.83.refs_0_), channel_id=1, source_target_pairs={{0,4},{1,5},{2,6},{3,7},{4,0},{5,1},{6,2},{7,3},{8,12},{9,13},{10,... | collective-permute-start | bytes 393224 | tf_op jit(solution)/shard_map/ppermute | solution.py:179
  4.2 2.6 %collective-permute-start.7 = (bf16[8,64,128]{2,1,0:T(8,128)(2,1)S(1)}, bf16[8,64,128]{2,1,0:T(8,128)(2,1)S(1)}, u32[]{:S(2)}, u32[]{:S(2)}) collective-permute-start(bf16[8,64,128]{2,1,0:T(8,128)(2,1)S(1)} %shard_map.83.refs_0_), channel_id=1, source_target_pairs={{0,8},{1,9},{2,10},{3,11},{4,12},{5,13},{6,14},{7,15},{8,0},{9,1},... | collective-permute-start | bytes 393224 | tf_op jit(solution)/shard_map/ppermute | solution.py:179
  6.8 1.5 %collective-permute-start.2 = (bf16[8,64,128]{2,1,0:T(8,128)(2,1)S(1)}, bf16[8,64,128]{2,1,0:T(8,128)(2,1)S(1)}, u32[]{:S(2)}, u32[]{:S(2)}) collective-permute-start(bf16[8,64,128]{2,1,0:T(8,128)(2,1)S(1)} %shard_map.83.refs_0_), channel_id=1, source_target_pairs={{0,2},{1,3},{2,0},{3,1},{4,6},{5,7},{6,4},{7,5},{8,10},{9,11},{10,... | collective-permute-start | bytes 393224 | tf_op jit(solution)/shard_map/ppermute | solution.py:179
  8.3 2.7 %shard_map.82.half_ref = bf16[8,8,64,128]{3,2,1,0:T(8,128)(2,1)S(1)} custom-call(s32[8]{0:T(128)} %dims_hbm.2, s32[8,8]{1,0:T(8,128)} %bitcast.1, bf16[8,64,64]{2,1,0:T(8,128)(2,1)} %left_hbm.1, bf16[8,8,64,128]{3,2,1,0:T(8,128)(2,1)} %psi_hbm.1), custom_call_target="tpu_custom_call" | custom-call | flops 67108864 | bytes 1048576 | tf_op jit(solution)/shard_map/pallas_call | solution.py:215
  11.0 0.0 collective-permute-done.refs_4_
  11.0 0.6 %collective-permute-start.5 = (bf16[8,64,128]{2,1,0:T(8,128)(2,1)S(1)}, bf16[8,64,128]{2,1,0:T(8,128)(2,1)S(1)}, u32[]{:S(2)}, u32[]{:S(2)}) collective-permute-start(bf16[8,64,128]{2,1,0:T(8,128)(2,1)S(1)} %collective-permute-done.refs_4_), channel_id=1, source_target_pairs={{0,2},{1,3},{2,0},{3,1},{4,6},{5,7},{6,4},{7,5},{8,10},{9,11},{10,... | collective-permute-start | bytes 393224 | tf_op jit(solution)/shard_map/ppermute | solution.py:179
  11.6 0.0 collective-permute-start.4
  11.6 1.3 %collective-permute-done.7.refs_8_ = bf16[8,64,128]{2,1,0:T(8,128)(2,1)S(1)} collective-permute-done((bf16[8,64,128]{2,1,0:T(8,128)(2,1)S(1)}, bf16[8,64,128]{2,1,0:T(8,128)(2,1)S(1)}, u32[]{:S(2)}, u32[]{:S(2)}) %collective-permute-start.7) | collective-permute-done | bytes 131104 | tf_op jit(solution)/shard_map/ppermute | solution.py:179
  12.9 0.4 %collective-permute-start.9 = (bf16[8,64,128]{2,1,0:T(8,128)(2,1)S(1)}, bf16[8,64,128]{2,1,0:T(8,128)(2,1)S(1)}, u32[]{:S(2)}, u32[]{:S(2)}) collective-permute-start(bf16[8,64,128]{2,1,0:T(8,128)(2,1)S(1)} %collective-permute-done.7.refs_8_), channel_id=1, source_target_pairs={{0,4},{1,5},{2,6},{3,7},{4,0},{5,1},{6,2},{7,3},{8,12},{9,13},{10,... | collective-permute-start | bytes 393224 | tf_op jit(solution)/shard_map/ppermute | solution.py:179
  13.4 0.0 collective-permute-start.1
  13.4 0.0 collective-permute-done.2.refs_2_
  13.4 1.5 %collective-permute-start.8 = (bf16[8,64,128]{2,1,0:T(8,128)(2,1)S(1)}, bf16[8,64,128]{2,1,0:T(8,128)(2,1)S(1)}, u32[]{:S(2)}, u32[]{:S(2)}) collective-permute-start(bf16[8,64,128]{2,1,0:T(8,128)(2,1)S(1)} %collective-permute-done.7.refs_8_), channel_id=1, source_target_pairs={{0,2},{1,3},{2,0},{3,1},{4,6},{5,7},{6,4},{7,5},{8,10},{9,11},{10,... | collective-permute-start | bytes 393224 | tf_op jit(solution)/shard_map/ppermute | solution.py:179
  14.9 1.2 %collective-permute-done.5.refs_6_ = bf16[8,64,128]{2,1,0:T(8,128)(2,1)S(1)} collective-permute-done((bf16[8,64,128]{2,1,0:T(8,128)(2,1)S(1)}, bf16[8,64,128]{2,1,0:T(8,128)(2,1)S(1)}, u32[]{:S(2)}, u32[]{:S(2)}) %collective-permute-start.5) | collective-permute-done | bytes 131104 | tf_op jit(solution)/shard_map/ppermute | solution.py:179
  16.0 0.0 collective-permute-start.3
  16.1 0.0 collective-permute-done.4.refs_5_
  16.1 0.5 %collective-permute-start.6 = (bf16[8,64,128]{2,1,0:T(8,128)(2,1)S(1)}, bf16[8,64,128]{2,1,0:T(8,128)(2,1)S(1)}, u32[]{:S(2)}, u32[]{:S(2)}) collective-permute-start(bf16[8,64,128]{2,1,0:T(8,128)(2,1)S(1)} %collective-permute-done.5.refs_6_), channel_id=1, source_target_pairs={{0,1},{1,0},{2,3},{3,2},{4,5},{5,4},{6,7},{7,6},{8,9},{9,8},{10,11... | collective-permute-start | bytes 393224 | tf_op jit(solution)/shard_map/ppermute | solution.py:179
  16.6 1.3 %collective-permute-done.9.refs_10_ = bf16[8,64,128]{2,1,0:T(8,128)(2,1)S(1)} collective-permute-done((bf16[8,64,128]{2,1,0:T(8,128)(2,1)S(1)}, bf16[8,64,128]{2,1,0:T(8,128)(2,1)S(1)}, u32[]{:S(2)}, u32[]{:S(2)}) %collective-permute-start.9) | collective-permute-done | bytes 131104 | tf_op jit(solution)/shard_map/ppermute | solution.py:179
  17.9 1.5 %collective-permute-start.10 = (bf16[8,64,128]{2,1,0:T(8,128)(2,1)S(1)}, bf16[8,64,128]{2,1,0:T(8,128)(2,1)S(1)}, u32[]{:S(2)}, u32[]{:S(2)}) collective-permute-start(bf16[8,64,128]{2,1,0:T(8,128)(2,1)S(1)} %collective-permute-done.9.refs_10_), channel_id=1, source_target_pairs={{0,2},{1,3},{2,0},{3,1},{4,6},{5,7},{6,4},{7,5},{8,10},{9,11},{10,... | collective-permute-start | bytes 393224 | tf_op jit(solution)/shard_map/ppermute | solution.py:179
  19.4 0.0 collective-permute-done.1.refs_1_
  19.4 0.0 collective-permute-start.11
  19.4 0.0 collective-permute-done.8.refs_9_
  19.4 0.5 %collective-permute-start.12 = (bf16[8,64,128]{2,1,0:T(8,128)(2,1)S(1)}, bf16[8,64,128]{2,1,0:T(8,128)(2,1)S(1)}, u32[]{:S(2)}, u32[]{:S(2)}) collective-permute-start(bf16[8,64,128]{2,1,0:T(8,128)(2,1)S(1)} %collective-permute-done.9.refs_10_), channel_id=1, source_target_pairs={{0,1},{1,0},{2,3},{3,2},{4,5},{5,4},{6,7},{7,6},{8,9},{9,8},{10,11... | collective-permute-start | bytes 393224 | tf_op jit(solution)/shard_map/ppermute | solution.py:179
  19.9 0.0 collective-permute-done.3.refs_3_
  19.9 0.1 collective-permute-start.13
  20.0 0.0 collective-permute-done.6.refs_7_
  20.0 3.3 %shard_map.84 = (bf16[8,8,64,128]{3,2,1,0:T(8,128)(2,1)}, s32[130]{0:T(256)S(4)}) custom-call(s32[8,8]{1,0:T(8,128)} %owner_hbm.1, s32[8,8]{1,0:T(8,128)} %slot_hbm.1, bf16[8,8,64,128]{3,2,1,0:T(8,128)(2,1)S(1)} %shard_map.82.half_ref, bf16[8,64,128]{2,1,0:T(8,128)(2,1)S(1)} %shard_map.83.refs_0_, bf16[8,64,128]{2,1,0:T(8,128)(2,1)S(1)} %collective-permute-done.1.refs_1_, ...), custom_call_target="tpu_custom_call" | custom-call | flops 67108864 | bytes 1048576 | tf_op jit(solution)/shard_map/pallas_call | solution.py:250
  23.2 0.0 collective-permute-done.10.refs_3_
  23.2 0.5 %collective-permute-start.14 = (bf16[8,64,128]{2,1,0:T(8,128)(2,1)S(1)}, bf16[8,64,128]{2,1,0:T(8,128)(2,1)S(1)}, u32[]{:S(2)}, u32[]{:S(2)}) collective-permute-start(bf16[8,64,128]{2,1,0:T(8,128)(2,1)S(1)} %collective-permute-done.10.refs_3_), channel_id=1, source_target_pairs={{0,1},{1,0},{2,3},{3,2},{4,5},{5,4},{6,7},{7,6},{8,9},{9,8},{10,11... | collective-permute-start | bytes 393224 | tf_op jit(solution)/shard_map/ppermute | solution.py:179
  23.8 0.0 collective-permute-done.11.refs_0_
  23.8 0.0 collective-permute-done.12.refs_1_
  23.8 0.0 collective-permute-done.13.refs_2_
  23.8 2.3 %shard_map.85.early_hbm = bf16[8,8,64,128]{3,2,1,0:T(8,128)(2,1)} custom-call(s32[130]{0:T(256)S(4)} %get-tuple-element.15.list_ref, bf16[8,8,64,128]{3,2,1,0:T(8,128)(2,1)} %get-tuple-element.17.early_hbm, bf16[8,8,64,128]{3,2,1,0:T(8,128)(2,1)S(1)} %shard_map.82.half_ref, ...), custom_call_target="tpu_custom_call", output_to_operand_aliasing={{}: (1, {})} | custom-call | flops 16777216 | bytes 262144 | tf_op jit(solution)/shard_map/pallas_call | solution.py:270
  26.0 0.0 collective-permute-done.14.refs_0_
  26.0 1.5 %shard_map.86 = bf16[8,8,64,128]{3,2,1,0:T(8,128)(2,1)} custom-call(s32[130]{0:T(256)S(4)} %get-tuple-element.15.list_ref, bf16[8,8,64,128]{3,2,1,0:T(8,128)(2,1)} %shard_map.85.early_hbm, bf16[8,8,64,128]{3,2,1,0:T(8,128)(2,1)S(1)} %shard_map.82.half_ref, bf16[8,64,128]{2,1,0:T(8,128)(2,1)S(1)} %collective-permute-done.14.refs_0_), custom_call_target="tpu_custom_call", output_to_operand_aliasing={{}: (1, {})} | custom-call | flops 16777216 | bytes 262144 | tf_op jit(solution)/shard_map/pallas_call | solution.py:270
Async XLA Ops:
  1.1 9.9 %collective-permute-start = (bf16[8,64,128]{2,1,0:T(8,128)(2,1)S(1)}, bf16[8,64,128]{2,1,0:T(8,128)(2,1)S(1)}, u32[]{:S(2)}, u32[]{:S(2)}) collective-permute-start(bf16[8,64,128]{2,1,0:T(8,128)(2,1)S(1)} %shard_map.83.refs_0_), channel_id=1, source_target_pairs={{0,4},{1,5},{2,6},{3,7},{4,0},{5,1},{6,2},{7,3},{8,12},{9,13},{10,... | collective-permute-start | bytes 393224 | tf_op jit(solution)/shard_map/ppermute | solution.py:179
  4.2 8.7 %collective-permute-start.7 = (bf16[8,64,128]{2,1,0:T(8,128)(2,1)S(1)}, bf16[8,64,128]{2,1,0:T(8,128)(2,1)S(1)}, u32[]{:S(2)}, u32[]{:S(2)}) collective-permute-start(bf16[8,64,128]{2,1,0:T(8,128)(2,1)S(1)} %shard_map.83.refs_0_), channel_id=1, source_target_pairs={{0,8},{1,9},{2,10},{3,11},{4,12},{5,13},{6,14},{7,15},{8,0},{9,1},... | collective-permute-start | bytes 393224 | tf_op jit(solution)/shard_map/ppermute | solution.py:179
  6.8 6.6 %collective-permute-start.2 = (bf16[8,64,128]{2,1,0:T(8,128)(2,1)S(1)}, bf16[8,64,128]{2,1,0:T(8,128)(2,1)S(1)}, u32[]{:S(2)}, u32[]{:S(2)}) collective-permute-start(bf16[8,64,128]{2,1,0:T(8,128)(2,1)S(1)} %shard_map.83.refs_0_), channel_id=1, source_target_pairs={{0,2},{1,3},{2,0},{3,1},{4,6},{5,7},{6,4},{7,5},{8,10},{9,11},{10,... | collective-permute-start | bytes 393224 | tf_op jit(solution)/shard_map/ppermute | solution.py:179
  11.0 5.0 %collective-permute-start.5 = (bf16[8,64,128]{2,1,0:T(8,128)(2,1)S(1)}, bf16[8,64,128]{2,1,0:T(8,128)(2,1)S(1)}, u32[]{:S(2)}, u32[]{:S(2)}) collective-permute-start(bf16[8,64,128]{2,1,0:T(8,128)(2,1)S(1)} %collective-permute-done.refs_4_), channel_id=1, source_target_pairs={{0,2},{1,3},{2,0},{3,1},{4,6},{5,7},{6,4},{7,5},{8,10},{9,11},{10,... | collective-permute-start | bytes 393224 | tf_op jit(solution)/shard_map/ppermute | solution.py:179
  11.6 4.4 %collective-permute-start.4 = (bf16[8,64,128]{2,1,0:T(8,128)(2,1)S(1)}, bf16[8,64,128]{2,1,0:T(8,128)(2,1)S(1)}, u32[]{:S(2)}, u32[]{:S(2)}) collective-permute-start(bf16[8,64,128]{2,1,0:T(8,128)(2,1)S(1)} %collective-permute-done.refs_4_), channel_id=1, source_target_pairs={{0,1},{1,0},{2,3},{3,2},{4,5},{5,4},{6,7},{7,6},{8,9},{9,8},{10,11... | collective-permute-start | bytes 393224 | tf_op jit(solution)/shard_map/ppermute | solution.py:179
  12.9 5.0 %collective-permute-start.9 = (bf16[8,64,128]{2,1,0:T(8,128)(2,1)S(1)}, bf16[8,64,128]{2,1,0:T(8,128)(2,1)S(1)}, u32[]{:S(2)}, u32[]{:S(2)}) collective-permute-start(bf16[8,64,128]{2,1,0:T(8,128)(2,1)S(1)} %collective-permute-done.7.refs_8_), channel_id=1, source_target_pairs={{0,4},{1,5},{2,6},{3,7},{4,0},{5,1},{6,2},{7,3},{8,12},{9,13},{10,... | collective-permute-start | bytes 393224 | tf_op jit(solution)/shard_map/ppermute | solution.py:179
  13.4 6.0 %collective-permute-start.1 = (bf16[8,64,128]{2,1,0:T(8,128)(2,1)S(1)}, bf16[8,64,128]{2,1,0:T(8,128)(2,1)S(1)}, u32[]{:S(2)}, u32[]{:S(2)}) collective-permute-start(bf16[8,64,128]{2,1,0:T(8,128)(2,1)S(1)} %shard_map.83.refs_0_), channel_id=1, source_target_pairs={{0,1},{1,0},{2,3},{3,2},{4,5},{5,4},{6,7},{7,6},{8,9},{9,8},{10,11... | collective-permute-start | bytes 393224 | tf_op jit(solution)/shard_map/ppermute | solution.py:179
  13.4 6.0 %collective-permute-start.8 = (bf16[8,64,128]{2,1,0:T(8,128)(2,1)S(1)}, bf16[8,64,128]{2,1,0:T(8,128)(2,1)S(1)}, u32[]{:S(2)}, u32[]{:S(2)}) collective-permute-start(bf16[8,64,128]{2,1,0:T(8,128)(2,1)S(1)} %collective-permute-done.7.refs_8_), channel_id=1, source_target_pairs={{0,2},{1,3},{2,0},{3,1},{4,6},{5,7},{6,4},{7,5},{8,10},{9,11},{10,... | collective-permute-start | bytes 393224 | tf_op jit(solution)/shard_map/ppermute | solution.py:179
  16.0 3.8 %collective-permute-start.3 = (bf16[8,64,128]{2,1,0:T(8,128)(2,1)S(1)}, bf16[8,64,128]{2,1,0:T(8,128)(2,1)S(1)}, u32[]{:S(2)}, u32[]{:S(2)}) collective-permute-start(bf16[8,64,128]{2,1,0:T(8,128)(2,1)S(1)} %collective-permute-done.2.refs_2_), channel_id=1, source_target_pairs={{0,1},{1,0},{2,3},{3,2},{4,5},{5,4},{6,7},{7,6},{8,9},{9,8},{10,11... | collective-permute-start | bytes 393224 | tf_op jit(solution)/shard_map/ppermute | solution.py:179
  16.1 3.9 %collective-permute-start.6 = (bf16[8,64,128]{2,1,0:T(8,128)(2,1)S(1)}, bf16[8,64,128]{2,1,0:T(8,128)(2,1)S(1)}, u32[]{:S(2)}, u32[]{:S(2)}) collective-permute-start(bf16[8,64,128]{2,1,0:T(8,128)(2,1)S(1)} %collective-permute-done.5.refs_6_), channel_id=1, source_target_pairs={{0,1},{1,0},{2,3},{3,2},{4,5},{5,4},{6,7},{7,6},{8,9},{9,8},{10,11... | collective-permute-start | bytes 393224 | tf_op jit(solution)/shard_map/ppermute | solution.py:179
  17.9 5.4 %collective-permute-start.10 = (bf16[8,64,128]{2,1,0:T(8,128)(2,1)S(1)}, bf16[8,64,128]{2,1,0:T(8,128)(2,1)S(1)}, u32[]{:S(2)}, u32[]{:S(2)}) collective-permute-start(bf16[8,64,128]{2,1,0:T(8,128)(2,1)S(1)} %collective-permute-done.9.refs_10_), channel_id=1, source_target_pairs={{0,2},{1,3},{2,0},{3,1},{4,6},{5,7},{6,4},{7,5},{8,10},{9,11},{10,... | collective-permute-start | bytes 393224 | tf_op jit(solution)/shard_map/ppermute | solution.py:179
  19.4 4.4 %collective-permute-start.11 = (bf16[8,64,128]{2,1,0:T(8,128)(2,1)S(1)}, bf16[8,64,128]{2,1,0:T(8,128)(2,1)S(1)}, u32[]{:S(2)}, u32[]{:S(2)}) collective-permute-start(bf16[8,64,128]{2,1,0:T(8,128)(2,1)S(1)} %collective-permute-done.7.refs_8_), channel_id=1, source_target_pairs={{0,1},{1,0},{2,3},{3,2},{4,5},{5,4},{6,7},{7,6},{8,9},{9,8},{10,11... | collective-permute-start | bytes 393224 | tf_op jit(solution)/shard_map/ppermute | solution.py:179
  19.4 4.4 %collective-permute-start.12 = (bf16[8,64,128]{2,1,0:T(8,128)(2,1)S(1)}, bf16[8,64,128]{2,1,0:T(8,128)(2,1)S(1)}, u32[]{:S(2)}, u32[]{:S(2)}) collective-permute-start(bf16[8,64,128]{2,1,0:T(8,128)(2,1)S(1)} %collective-permute-done.9.refs_10_), channel_id=1, source_target_pairs={{0,1},{1,0},{2,3},{3,2},{4,5},{5,4},{6,7},{7,6},{8,9},{9,8},{10,11... | collective-permute-start | bytes 393224 | tf_op jit(solution)/shard_map/ppermute | solution.py:179
  19.9 3.9 %collective-permute-start.13 = (bf16[8,64,128]{2,1,0:T(8,128)(2,1)S(1)}, bf16[8,64,128]{2,1,0:T(8,128)(2,1)S(1)}, u32[]{:S(2)}, u32[]{:S(2)}) collective-permute-start(bf16[8,64,128]{2,1,0:T(8,128)(2,1)S(1)} %collective-permute-done.8.refs_9_), channel_id=1, source_target_pairs={{0,1},{1,0},{2,3},{3,2},{4,5},{5,4},{6,7},{7,6},{8,9},{9,8},{10,11... | collective-permute-start | bytes 393224 | tf_op jit(solution)/shard_map/ppermute | solution.py:179
  23.2 2.8 %collective-permute-start.14 = (bf16[8,64,128]{2,1,0:T(8,128)(2,1)S(1)}, bf16[8,64,128]{2,1,0:T(8,128)(2,1)S(1)}, u32[]{:S(2)}, u32[]{:S(2)}) collective-permute-start(bf16[8,64,128]{2,1,0:T(8,128)(2,1)S(1)} %collective-permute-done.10.refs_3_), channel_id=1, source_target_pairs={{0,1},{1,0},{2,3},{3,2},{4,5},{5,4},{6,7},{7,6},{8,9},{9,8},{10,11... | collective-permute-start | bytes 393224 | tf_op jit(solution)/shard_map/ppermute | solution.py:179

commit v16 on v15

--- a/solution.py
+++ b/solution.py
@@ -98,8 +98,8 @@
 
 
 def early_kernel(pair_count, owner_hbm, slot_hbm, half_ref, *refs):
-    piece_refs = refs[:-7]
-    out_hbm, list_ref, pairs_ref, out_ref, owner_ref, slot_ref, sems = refs[-7:]
+    piece_refs = refs[:-6]
+    out_ref, list_ref, pairs_ref, owner_ref, slot_ref, sems = refs[-6:]
     sectors, blocks, tile, width = out_ref.shape
     items, held = sectors * blocks, pairs_ref.shape[0]
     last = held + len(MIDDLE) * pair_count
@@ -109,10 +109,8 @@
     for copy in copies:
         copy.wait()
 
-    def store(a):
-        return pltpu.make_async_copy(out_ref.at[a], out_hbm.at[a], sems.at[a])
-
     def one(a, listed):
+        before = listed[1]
         for k in range(0, blocks, 2):
             forms = []
             for u in range(2):
@@ -128,50 +126,68 @@
                 in_middle = (at >= held) & (at < last)
                 listed = listed[0] + in_middle.astype(jnp.int32), listed[1] + in_last.astype(jnp.int32)
             out_ref[a, k], out_ref[a, k + 1] = two_products([half_ref[a, k], half_ref[a, k + 1]], forms)
-        store(a).start()
+        list_ref[2 * items + 2 + a] = listed[1] - before
         return listed
 
     listed = lax.fori_loop(0, sectors, one, (0, 0), unroll=2)
     list_ref[items] = listed[0]
     list_ref[2 * items + 1] = listed[1]
-    for a in range(sectors):
-        store(a).wait()
-
-
-def late_kernel(group_size, first, list_ref, early_hbm, half_ref, *refs):
-    piece_refs, (out_hbm, pairs_ref, out_ref, sems) = refs[:-4], refs[-4:]
+
+
+def listed_products(group_size, first, list_ref, half_ref, pairs_ref, out_ref):
     sectors, blocks, tile, width = half_ref.shape
     items = sectors * blocks
     listed = list_ref[first + items]
-    merge(piece_refs, pairs_ref)
-
-    def store(slot, item):
-        return pltpu.make_async_copy(out_ref.at[slot], out_hbm.at[item // blocks, item % blocks], sems.at[slot])
 
     def group(g, carry):
         for u in range(0, group_size, 2):
-            slot = g * group_size + u
-            entries = [list_ref[first + jnp.minimum(slot + n, listed - 1)] for n in range(2)]
-            halves, forms = [], []
+            entries = [list_ref[first + jnp.minimum(g * group_size + u + n, listed - 1)] for n in range(2)]
+            places, halves, forms = [], [], []
             for entry in entries:
                 item, at = entry % items, entry // items
-                halves.append(half_ref[item // blocks, item % blocks])
+                places.append((item // blocks, item % blocks))
+                halves.append(half_ref[places[-1]])
                 forms.append(block_form(pairs_ref[at // 2], at % 2 == 1))
-            out_ref[slot], out_ref[slot + 1] = two_products(halves, forms)
-        for u in range(group_size):
-            slot = g * group_size + u
-
-            @pl.when(slot < listed)
-            def _():
-                store(slot, list_ref[first + slot] % items).start()
+            out_ref[places[0]], out_ref[places[1]] = two_products(halves, forms)
         return carry
 
-    def drain(slot, carry):
-        store(slot, 0).wait()
-        return carry
-
     lax.fori_loop(0, (listed + group_size - 1) // group_size, group, 0)
-    lax.fori_loop(0, listed, drain, 0)
+
+
+def middle_kernel(list_ref, early_ref, half_ref, *refs):
+    piece_refs, (out_ref, pairs_ref) = refs[:-2], refs[-2:]
+    out_ref[...] = early_ref[...]
+    merge(piece_refs, pairs_ref)
+    listed_products(8, 0, list_ref, half_ref, pairs_ref, out_ref)
+
+
+def last_kernel(list_ref, middle_ref, half_ref, pairs_ref, out_hbm, out_ref, sems):
+    sectors, blocks, tile, width = half_ref.shape
+    items = sectors * blocks
+
+    def store(a, ref):
+        return pltpu.make_async_copy(ref.at[a], out_hbm.at[a], sems.at[a])
+
+    for a in range(sectors):
+        changed = list_ref[2 * items + 2 + a] > 0
+
+        @pl.when(changed)
+        def _():
+            out_ref[a] = middle_ref[a]
+
+        @pl.when(jnp.logical_not(changed))
+        def _():
+            store(a, middle_ref).start()
+
+    listed_products(4, items + 1, list_ref, half_ref, pairs_ref, out_ref)
+    for a in range(sectors):
+
+        @pl.when(list_ref[2 * items + 2 + a] > 0)
+        def _():
+            store(a, out_ref).start()
+
+    for a in range(sectors):
+        store(a, out_ref).wait()
 
 
 def swap(piece, bit):
@@ -251,43 +267,43 @@
         functools.partial(early_kernel, pair_count),
         out_shape=(
             jax.ShapeDtypeStruct(psi.shape, jnp.bfloat16),
-            pltpu.SMEM((2 * items + 2,), jnp.int32),
+            pltpu.SMEM((2 * items + 2 + left_count,), jnp.int32),
         ),
         in_specs=[hbm, hbm] + [vmem] * (1 + len(early)),
-        out_specs=(hbm, smem),
+        out_specs=(vmem, smem),
         scratch_shapes=[
             pltpu.VMEM((sum(piece.shape[0] for piece in early), tile, 2 * tile), jnp.bfloat16),
-            pltpu.VMEM(psi.shape, jnp.bfloat16),
             pltpu.SMEM(right_owner.shape, jnp.int32),
             pltpu.SMEM(right_slot.shape, jnp.int32),
-            pltpu.SemaphoreType.DMA((max(left_count, 2),)),
+            pltpu.SemaphoreType.DMA((2,)),
         ],
         compiler_params=params,
         cost_estimate=pl.CostEstimate(flops=flops, bytes_accessed=2 * psi.size, transcendentals=0),
     )(*in_hbm(right_owner, right_slot), half, *early)
 
-    def late(group_size, first, sigma, names):
-        return pl.pallas_call(
-            functools.partial(late_kernel, group_size, first),
-            out_shape=jax.ShapeDtypeStruct(psi.shape, jnp.bfloat16),
-            in_specs=[smem, hbm] + [vmem] * (1 + len(names)),
-            out_specs=hbm,
-            scratch_shapes=[
-                pltpu.VMEM((len(names) * pair_count, tile, 2 * tile), jnp.bfloat16),
-                pltpu.VMEM((items + group_size, tile, width), jnp.bfloat16),
-                pltpu.SemaphoreType.DMA((items,)),
-            ],
-            input_output_aliases={1: 0},
-            compiler_params=params,
-            cost_estimate=pl.CostEstimate(flops=flops // 4, bytes_accessed=psi.size // 2, transcendentals=0),
-        )(pltpu.with_memory_space_constraint(listed, pltpu.SMEM), sigma, half, *[pieces[r] for r in names])
-
     if by_swaps:
         top = FAR | NEAR | CROSS
         pieces[top], sigma = lax.optimization_barrier((pieces[top], sigma))
         pieces[top | CORE] = swap(pieces[top], CORE)
-        sigma = late(8, 0, sigma, MIDDLE)
-        sigma = late(4, items + 1, sigma, LAST)
+        listed = pltpu.with_memory_space_constraint(listed, pltpu.SMEM)
+        sigma = pl.pallas_call(
+            middle_kernel,
+            out_shape=jax.ShapeDtypeStruct(psi.shape, jnp.bfloat16),
+            in_specs=[smem] + [vmem] * (2 + len(MIDDLE)),
+            out_specs=vmem,
+            scratch_shapes=[pltpu.VMEM((len(MIDDLE) * pair_count, tile, 2 * tile), jnp.bfloat16)],
+            compiler_params=params,
+            cost_estimate=pl.CostEstimate(flops=flops // 4, bytes_accessed=psi.size // 2, transcendentals=0),
+        )(listed, sigma, half, *[pieces[r] for r in MIDDLE])
+        sigma = pl.pallas_call(
+            last_kernel,
+            out_shape=jax.ShapeDtypeStruct(psi.shape, jnp.bfloat16),
+            in_specs=[smem] + [vmem] * 3,
+            out_specs=hbm,
+            scratch_shapes=[pltpu.VMEM(psi.shape, jnp.bfloat16), pltpu.SemaphoreType.DMA((left_count,))],
+            compiler_params=params,
+            cost_estimate=pl.CostEstimate(flops=flops // 16, bytes_accessed=2 * psi.size, transcendentals=0),
+        )(listed, sigma, half, pieces[LAST[0]])
     if lax.axis_size("op") > 1:
         sigma = lax.psum_scatter(sigma, "op", scatter_dimension=3, tiled=True)
     return sigma

time: 27.6 us -> 25.6 us (0.928)
  Pallas kernels: 10.8 us -> 8.33 us
  waiting for transfers between devices: 3.82 us -> 4.45 us
  starting transfers between devices: 12.8 us -> 12.5 us
    pallas_call x2, Pallas kernels: 3.74 us -> 1.94 us  [the longest x1 1.17 us: per_device(): pl.pallas_call(last_kernel, out_shape=jax.ShapeDtypeStruct(psi.shape, jnp...]
    pallas_call x1, Pallas kernels: 3.27 us -> 2.58 us  [per_device(): pl.pallas_call(functools.partial(early_kernel, pair_count), out_shape=(ja...]
    ppermute x15, waiting for transfers between devices: 3.82 us -> 4.45 us  [swap(): return lax.ppermute(piece, 'sec', [(i, i ^ bit) for i in range(count)])]
    ppermute x15, starting transfers between devices: 12.8 us -> 12.5 us  [swap(): return lax.ppermute(piece, 'sec', [(i, i ^ bit) for i in range(count)])]
  transfers between devices with their start and end apart: 15 -> 15, of which waited for: 3 -> 5; matrix products, arithmetic and copies ran while one was open for 0% -> 0% of each run, Pallas kernels for 30% -> 24%
where the time goes in v16:
time: 25.6 us; the launch traced here: 25.4 us
  starting transfers between devices  12.5 us (49%)
  Pallas kernels  8.33 us (33%)
  waiting for transfers between devices  4.45 us (17%)
    ppermute x15, starting transfers between devices, swap(): return lax.ppermute(piece, 'sec', [(i, i ^ bit) for i in range(count)])  12.5 us
    ppermute x15, waiting for transfers between devices, swap(): return lax.ppermute(piece, 'sec', [(i, i ^ bit) for i in range(count)])  4.45 us
    pallas_call x1, Pallas kernels, half_of(): pl.pallas_call(left_kernel, out_shape=jax.ShapeDtypeStruct(psi.shape, jnp...  2.73 us
    pallas_call x1, Pallas kernels, per_device(): pl.pallas_call(functools.partial(early_kernel, pair_count), out_shape=(ja...  2.58 us
    pallas_call x1, Pallas kernels, per_device(): pl.pallas_call(last_kernel, out_shape=jax.ShapeDtypeStruct(psi.shape, jnp...  1.17 us
    pallas_call x1, Pallas kernels, per_device(): pl.pallas_call(pack_kernel, out_shape=jax.ShapeDtypeStruct((pair_count, t...  1.09 us
    pallas_call x1, Pallas kernels, per_device(): pl.pallas_call(middle_kernel, out_shape=jax.ShapeDtypeStruct(psi.shape, j...  0.76 us
  transfers between devices with their start and end apart: 15, of which 5 were waited for; matrix products, arithmetic and copies ran while one was open for 0% of the time, Pallas kernels for 24%

profile of v16, /device:TPU:0, one launch (start us, length us, event | category | flops | bytes accessed | tf_op | source)
XLA Modules:
  0.0 25.4 jit_solution(13807507574782758063)
XLA Ops:
  0.0 1.1 %shard_map.83.refs_0_ = bf16[8,64,128]{2,1,0:T(8,128)(2,1)S(1)} custom-call(s32[16]{0:T(128)} %dims_hbm.3, bf16[16,64,64]{2,1,0:T(8,128)(2,1)} %right_hbm.1), custom_call_target="tpu_custom_call" | custom-call | bytes 131072 | tf_op jit(solution)/shard_map/pallas_call | solution.py:215
  1.1 3.1 %collective-permute-start = (bf16[8,64,128]{2,1,0:T(8,128)(2,1)S(1)}, bf16[8,64,128]{2,1,0:T(8,128)(2,1)S(1)}, u32[]{:S(2)}, u32[]{:S(2)}) collective-permute-start(bf16[8,64,128]{2,1,0:T(8,128)(2,1)S(1)} %shard_map.83.refs_0_), channel_id=1, source_target_pairs={{0,4},{1,5},{2,6},{3,7},{4,0},{5,1},{6,2},{7,3},{8,12},{9,13},{10,... | collective-permute-start | bytes 393224 | tf_op jit(solution)/shard_map/ppermute | solution.py:195
  4.2 2.6 %collective-permute-start.7 = (bf16[8,64,128]{2,1,0:T(8,128)(2,1)S(1)}, bf16[8,64,128]{2,1,0:T(8,128)(2,1)S(1)}, u32[]{:S(2)}, u32[]{:S(2)}) collective-permute-start(bf16[8,64,128]{2,1,0:T(8,128)(2,1)S(1)} %shard_map.83.refs_0_), channel_id=1, source_target_pairs={{0,8},{1,9},{2,10},{3,11},{4,12},{5,13},{6,14},{7,15},{8,0},{9,1},... | collective-permute-start | bytes 393224 | tf_op jit(solution)/shard_map/ppermute | solution.py:195
  6.8 1.5 %collective-permute-start.2 = (bf16[8,64,128]{2,1,0:T(8,128)(2,1)S(1)}, bf16[8,64,128]{2,1,0:T(8,128)(2,1)S(1)}, u32[]{:S(2)}, u32[]{:S(2)}) collective-permute-start(bf16[8,64,128]{2,1,0:T(8,128)(2,1)S(1)} %shard_map.83.refs_0_), channel_id=1, source_target_pairs={{0,2},{1,3},{2,0},{3,1},{4,6},{5,7},{6,4},{7,5},{8,10},{9,11},{10,... | collective-permute-start | bytes 393224 | tf_op jit(solution)/shard_map/ppermute | solution.py:195
  8.3 2.7 %shard_map.82.half_ref = bf16[8,8,64,128]{3,2,1,0:T(8,128)(2,1)S(1)} custom-call(s32[8]{0:T(128)} %dims_hbm.2, s32[8,8]{1,0:T(8,128)} %bitcast.1, bf16[8,64,64]{2,1,0:T(8,128)(2,1)} %left_hbm.1, bf16[8,8,64,128]{3,2,1,0:T(8,128)(2,1)} %psi_hbm.1), custom_call_target="tpu_custom_call" | custom-call | flops 67108864 | bytes 1048576 | tf_op jit(solution)/shard_map/pallas_call | solution.py:231
  11.0 0.0 collective-permute-done.refs_4_
  11.0 0.6 %collective-permute-start.5 = (bf16[8,64,128]{2,1,0:T(8,128)(2,1)S(1)}, bf16[8,64,128]{2,1,0:T(8,128)(2,1)S(1)}, u32[]{:S(2)}, u32[]{:S(2)}) collective-permute-start(bf16[8,64,128]{2,1,0:T(8,128)(2,1)S(1)} %collective-permute-done.refs_4_), channel_id=1, source_target_pairs={{0,2},{1,3},{2,0},{3,1},{4,6},{5,7},{6,4},{7,5},{8,10},{9,11},{10,... | collective-permute-start | bytes 393224 | tf_op jit(solution)/shard_map/ppermute | solution.py:195
  11.6 0.0 collective-permute-start.4
  11.6 1.3 %collective-permute-done.7.refs_8_ = bf16[8,64,128]{2,1,0:T(8,128)(2,1)S(1)} collective-permute-done((bf16[8,64,128]{2,1,0:T(8,128)(2,1)S(1)}, bf16[8,64,128]{2,1,0:T(8,128)(2,1)S(1)}, u32[]{:S(2)}, u32[]{:S(2)}) %collective-permute-start.7) | collective-permute-done | bytes 131104 | tf_op jit(solution)/shard_map/ppermute | solution.py:195
  12.9 0.4 %collective-permute-start.9 = (bf16[8,64,128]{2,1,0:T(8,128)(2,1)S(1)}, bf16[8,64,128]{2,1,0:T(8,128)(2,1)S(1)}, u32[]{:S(2)}, u32[]{:S(2)}) collective-permute-start(bf16[8,64,128]{2,1,0:T(8,128)(2,1)S(1)} %collective-permute-done.7.refs_8_), channel_id=1, source_target_pairs={{0,4},{1,5},{2,6},{3,7},{4,0},{5,1},{6,2},{7,3},{8,12},{9,13},{10,... | collective-permute-start | bytes 393224 | tf_op jit(solution)/shard_map/ppermute | solution.py:195
  13.4 0.0 collective-permute-start.1
  13.4 0.0 collective-permute-done.2.refs_2_
  13.4 1.5 %collective-permute-start.8 = (bf16[8,64,128]{2,1,0:T(8,128)(2,1)S(1)}, bf16[8,64,128]{2,1,0:T(8,128)(2,1)S(1)}, u32[]{:S(2)}, u32[]{:S(2)}) collective-permute-start(bf16[8,64,128]{2,1,0:T(8,128)(2,1)S(1)} %collective-permute-done.7.refs_8_), channel_id=1, source_target_pairs={{0,2},{1,3},{2,0},{3,1},{4,6},{5,7},{6,4},{7,5},{8,10},{9,11},{10,... | collective-permute-start | bytes 393224 | tf_op jit(solution)/shard_map/ppermute | solution.py:195
  14.9 1.2 %collective-permute-done.5.refs_6_ = bf16[8,64,128]{2,1,0:T(8,128)(2,1)S(1)} collective-permute-done((bf16[8,64,128]{2,1,0:T(8,128)(2,1)S(1)}, bf16[8,64,128]{2,1,0:T(8,128)(2,1)S(1)}, u32[]{:S(2)}, u32[]{:S(2)}) %collective-permute-start.5) | collective-permute-done | bytes 131104 | tf_op jit(solution)/shard_map/ppermute | solution.py:195
  16.0 0.0 collective-permute-start.3
  16.1 0.0 collective-permute-done.4.refs_5_
  16.1 0.5 %collective-permute-start.6 = (bf16[8,64,128]{2,1,0:T(8,128)(2,1)S(1)}, bf16[8,64,128]{2,1,0:T(8,128)(2,1)S(1)}, u32[]{:S(2)}, u32[]{:S(2)}) collective-permute-start(bf16[8,64,128]{2,1,0:T(8,128)(2,1)S(1)} %collective-permute-done.5.refs_6_), channel_id=1, source_target_pairs={{0,1},{1,0},{2,3},{3,2},{4,5},{5,4},{6,7},{7,6},{8,9},{9,8},{10,11... | collective-permute-start | bytes 393224 | tf_op jit(solution)/shard_map/ppermute | solution.py:195
  16.6 1.3 %collective-permute-done.9.refs_10_ = bf16[8,64,128]{2,1,0:T(8,128)(2,1)S(1)} collective-permute-done((bf16[8,64,128]{2,1,0:T(8,128)(2,1)S(1)}, bf16[8,64,128]{2,1,0:T(8,128)(2,1)S(1)}, u32[]{:S(2)}, u32[]{:S(2)}) %collective-permute-start.9) | collective-permute-done | bytes 131104 | tf_op jit(solution)/shard_map/ppermute | solution.py:195
  17.9 1.5 %collective-permute-start.10 = (bf16[8,64,128]{2,1,0:T(8,128)(2,1)S(1)}, bf16[8,64,128]{2,1,0:T(8,128)(2,1)S(1)}, u32[]{:S(2)}, u32[]{:S(2)}) collective-permute-start(bf16[8,64,128]{2,1,0:T(8,128)(2,1)S(1)} %collective-permute-done.9.refs_10_), channel_id=1, source_target_pairs={{0,2},{1,3},{2,0},{3,1},{4,6},{5,7},{6,4},{7,5},{8,10},{9,11},{10,... | collective-permute-start | bytes 393224 | tf_op jit(solution)/shard_map/ppermute | solution.py:195
  19.4 0.0 collective-permute-done.1.refs_1_
  19.4 0.0 collective-permute-start.11
  19.4 0.0 collective-permute-done.8.refs_9_
  19.4 0.5 %collective-permute-start.12 = (bf16[8,64,128]{2,1,0:T(8,128)(2,1)S(1)}, bf16[8,64,128]{2,1,0:T(8,128)(2,1)S(1)}, u32[]{:S(2)}, u32[]{:S(2)}) collective-permute-start(bf16[8,64,128]{2,1,0:T(8,128)(2,1)S(1)} %collective-permute-done.9.refs_10_), channel_id=1, source_target_pairs={{0,1},{1,0},{2,3},{3,2},{4,5},{5,4},{6,7},{7,6},{8,9},{9,8},{10,11... | collective-permute-start | bytes 393224 | tf_op jit(solution)/shard_map/ppermute | solution.py:195
  19.9 0.0 collective-permute-done.3.refs_3_
  19.9 0.1 collective-permute-start.13
  20.0 0.0 collective-permute-done.6.refs_7_
  20.0 2.6 %shard_map.84 = (bf16[8,8,64,128]{3,2,1,0:T(8,128)(2,1)S(1)}, s32[138]{0:T(256)S(4)}) custom-call(s32[8,8]{1,0:T(8,128)} %owner_hbm.1, s32[8,8]{1,0:T(8,128)} %slot_hbm.1, bf16[8,8,64,128]{3,2,1,0:T(8,128)(2,1)S(1)} %shard_map.82.half_ref, bf16[8,64,128]{2,1,0:T(8,128)(2,1)S(1)} %shard_map.83.refs_0_, ...), custom_call_target="tpu_custom_call" | custom-call | flops 67108864 | bytes 1048576 | tf_op jit(solution)/shard_map/pallas_call | solution.py:266
  22.5 0.3 %collective-permute-done.10.refs_3_ = bf16[8,64,128]{2,1,0:T(8,128)(2,1)S(1)} collective-permute-done((bf16[8,64,128]{2,1,0:T(8,128)(2,1)S(1)}, bf16[8,64,128]{2,1,0:T(8,128)(2,1)S(1)}, u32[]{:S(2)}, u32[]{:S(2)}) %collective-permute-start.10) | collective-permute-done | bytes 131104 | tf_op jit(solution)/shard_map/ppermute | solution.py:195
  22.8 0.2 collective-permute-start.14
  23.1 0.0 collective-permute-done.11.refs_0_
  23.1 0.0 collective-permute-done.12.refs_1_
  23.1 0.0 collective-permute-done.13.refs_2_
  23.1 0.8 %shard_map.85.middle_ref = bf16[8,8,64,128]{3,2,1,0:T(8,128)(2,1)S(1)} custom-call(s32[138]{0:T(256)S(4)} %get-tuple-element.15.list_ref, bf16[8,8,64,128]{3,2,1,0:T(8,128)(2,1)S(1)} %get-tuple-element.17.early_ref, bf16[8,8,64,128]{3,2,1,0:T(8,128)(2,1)S(1)} %shard_map.82.half_ref, bf16[8,64,128]{2,1,0:T(8,128)(2,1)S(1)} %collective-permute-done.11.refs_0_, ...), custom_call_target="tpu_custom_call" | custom-call | flops 16777216 | bytes 262144 | tf_op jit(solution)/shard_map/pallas_call | solution.py:289
  23.8 0.3 %collective-permute-done.14.pairs_ref = bf16[8,64,128]{2,1,0:T(8,128)(2,1)S(1)} collective-permute-done((bf16[8,64,128]{2,1,0:T(8,128)(2,1)S(1)}, bf16[8,64,128]{2,1,0:T(8,128)(2,1)S(1)}, u32[]{:S(2)}, u32[]{:S(2)}) %collective-permute-start.14) | collective-permute-done | bytes 131104 | tf_op jit(solution)/shard_map/ppermute | solution.py:195
  24.2 1.2 %shard_map.86 = bf16[8,8,64,128]{3,2,1,0:T(8,128)(2,1)} custom-call(s32[138]{0:T(256)S(4)} %get-tuple-element.15.list_ref, bf16[8,8,64,128]{3,2,1,0:T(8,128)(2,1)S(1)} %shard_map.85.middle_ref, bf16[8,8,64,128]{3,2,1,0:T(8,128)(2,1)S(1)} %shard_map.82.half_ref, bf16[8,64,128]{2,1,0:T(8,128)(2,1)S(1)} %collective-permute-done.14.pairs_ref), custom_call_target="tpu_custom_call" | custom-call | flops 4194304 | bytes 1048576 | tf_op jit(solution)/shard_map/pallas_call | solution.py:298
Async XLA Ops:
  1.1 9.9 %collective-permute-start = (bf16[8,64,128]{2,1,0:T(8,128)(2,1)S(1)}, bf16[8,64,128]{2,1,0:T(8,128)(2,1)S(1)}, u32[]{:S(2)}, u32[]{:S(2)}) collective-permute-start(bf16[8,64,128]{2,1,0:T(8,128)(2,1)S(1)} %shard_map.83.refs_0_), channel_id=1, source_target_pairs={{0,4},{1,5},{2,6},{3,7},{4,0},{5,1},{6,2},{7,3},{8,12},{9,13},{10,... | collective-permute-start | bytes 393224 | tf_op jit(solution)/shard_map/ppermute | solution.py:195
  4.2 8.7 %collective-permute-start.7 = (bf16[8,64,128]{2,1,0:T(8,128)(2,1)S(1)}, bf16[8,64,128]{2,1,0:T(8,128)(2,1)S(1)}, u32[]{:S(2)}, u32[]{:S(2)}) collective-permute-start(bf16[8,64,128]{2,1,0:T(8,128)(2,1)S(1)} %shard_map.83.refs_0_), channel_id=1, source_target_pairs={{0,8},{1,9},{2,10},{3,11},{4,12},{5,13},{6,14},{7,15},{8,0},{9,1},... | collective-permute-start | bytes 393224 | tf_op jit(solution)/shard_map/ppermute | solution.py:195
  6.8 6.6 %collective-permute-start.2 = (bf16[8,64,128]{2,1,0:T(8,128)(2,1)S(1)}, bf16[8,64,128]{2,1,0:T(8,128)(2,1)S(1)}, u32[]{:S(2)}, u32[]{:S(2)}) collective-permute-start(bf16[8,64,128]{2,1,0:T(8,128)(2,1)S(1)} %shard_map.83.refs_0_), channel_id=1, source_target_pairs={{0,2},{1,3},{2,0},{3,1},{4,6},{5,7},{6,4},{7,5},{8,10},{9,11},{10,... | collective-permute-start | bytes 393224 | tf_op jit(solution)/shard_map/ppermute | solution.py:195
  11.0 5.0 %collective-permute-start.5 = (bf16[8,64,128]{2,1,0:T(8,128)(2,1)S(1)}, bf16[8,64,128]{2,1,0:T(8,128)(2,1)S(1)}, u32[]{:S(2)}, u32[]{:S(2)}) collective-permute-start(bf16[8,64,128]{2,1,0:T(8,128)(2,1)S(1)} %collective-permute-done.refs_4_), channel_id=1, source_target_pairs={{0,2},{1,3},{2,0},{3,1},{4,6},{5,7},{6,4},{7,5},{8,10},{9,11},{10,... | collective-permute-start | bytes 393224 | tf_op jit(solution)/shard_map/ppermute | solution.py:195
  11.6 4.4 %collective-permute-start.4 = (bf16[8,64,128]{2,1,0:T(8,128)(2,1)S(1)}, bf16[8,64,128]{2,1,0:T(8,128)(2,1)S(1)}, u32[]{:S(2)}, u32[]{:S(2)}) collective-permute-start(bf16[8,64,128]{2,1,0:T(8,128)(2,1)S(1)} %collective-permute-done.refs_4_), channel_id=1, source_target_pairs={{0,1},{1,0},{2,3},{3,2},{4,5},{5,4},{6,7},{7,6},{8,9},{9,8},{10,11... | collective-permute-start | bytes 393224 | tf_op jit(solution)/shard_map/ppermute | solution.py:195
  12.9 5.0 %collective-permute-start.9 = (bf16[8,64,128]{2,1,0:T(8,128)(2,1)S(1)}, bf16[8,64,128]{2,1,0:T(8,128)(2,1)S(1)}, u32[]{:S(2)}, u32[]{:S(2)}) collective-permute-start(bf16[8,64,128]{2,1,0:T(8,128)(2,1)S(1)} %collective-permute-done.7.refs_8_), channel_id=1, source_target_pairs={{0,4},{1,5},{2,6},{3,7},{4,0},{5,1},{6,2},{7,3},{8,12},{9,13},{10,... | collective-permute-start | bytes 393224 | tf_op jit(solution)/shard_map/ppermute | solution.py:195
  13.4 6.0 %collective-permute-start.1 = (bf16[8,64,128]{2,1,0:T(8,128)(2,1)S(1)}, bf16[8,64,128]{2,1,0:T(8,128)(2,1)S(1)}, u32[]{:S(2)}, u32[]{:S(2)}) collective-permute-start(bf16[8,64,128]{2,1,0:T(8,128)(2,1)S(1)} %shard_map.83.refs_0_), channel_id=1, source_target_pairs={{0,1},{1,0},{2,3},{3,2},{4,5},{5,4},{6,7},{7,6},{8,9},{9,8},{10,11... | collective-permute-start | bytes 393224 | tf_op jit(solution)/shard_map/ppermute | solution.py:195
  13.4 6.0 %collective-permute-start.8 = (bf16[8,64,128]{2,1,0:T(8,128)(2,1)S(1)}, bf16[8,64,128]{2,1,0:T(8,128)(2,1)S(1)}, u32[]{:S(2)}, u32[]{:S(2)}) collective-permute-start(bf16[8,64,128]{2,1,0:T(8,128)(2,1)S(1)} %collective-permute-done.7.refs_8_), channel_id=1, source_target_pairs={{0,2},{1,3},{2,0},{3,1},{4,6},{5,7},{6,4},{7,5},{8,10},{9,11},{10,... | collective-permute-start | bytes 393224 | tf_op jit(solution)/shard_map/ppermute | solution.py:195
  16.0 3.8 %collective-permute-start.3 = (bf16[8,64,128]{2,1,0:T(8,128)(2,1)S(1)}, bf16[8,64,128]{2,1,0:T(8,128)(2,1)S(1)}, u32[]{:S(2)}, u32[]{:S(2)}) collective-permute-start(bf16[8,64,128]{2,1,0:T(8,128)(2,1)S(1)} %collective-permute-done.2.refs_2_), channel_id=1, source_target_pairs={{0,1},{1,0},{2,3},{3,2},{4,5},{5,4},{6,7},{7,6},{8,9},{9,8},{10,11... | collective-permute-start | bytes 393224 | tf_op jit(solution)/shard_map/ppermute | solution.py:195
  16.1 3.9 %collective-permute-start.6 = (bf16[8,64,128]{2,1,0:T(8,128)(2,1)S(1)}, bf16[8,64,128]{2,1,0:T(8,128)(2,1)S(1)}, u32[]{:S(2)}, u32[]{:S(2)}) collective-permute-start(bf16[8,64,128]{2,1,0:T(8,128)(2,1)S(1)} %collective-permute-done.5.refs_6_), channel_id=1, source_target_pairs={{0,1},{1,0},{2,3},{3,2},{4,5},{5,4},{6,7},{7,6},{8,9},{9,8},{10,11... | collective-permute-start | bytes 393224 | tf_op jit(solution)/shard_map/ppermute | solution.py:195
  17.9 5.0 %collective-permute-start.10 = (bf16[8,64,128]{2,1,0:T(8,128)(2,1)S(1)}, bf16[8,64,128]{2,1,0:T(8,128)(2,1)S(1)}, u32[]{:S(2)}, u32[]{:S(2)}) collective-permute-start(bf16[8,64,128]{2,1,0:T(8,128)(2,1)S(1)} %collective-permute-done.9.refs_10_), channel_id=1, source_target_pairs={{0,2},{1,3},{2,0},{3,1},{4,6},{5,7},{6,4},{7,5},{8,10},{9,11},{10,... | collective-permute-start | bytes 393224 | tf_op jit(solution)/shard_map/ppermute | solution.py:195
  19.4 3.7 %collective-permute-start.11 = (bf16[8,64,128]{2,1,0:T(8,128)(2,1)S(1)}, bf16[8,64,128]{2,1,0:T(8,128)(2,1)S(1)}, u32[]{:S(2)}, u32[]{:S(2)}) collective-permute-start(bf16[8,64,128]{2,1,0:T(8,128)(2,1)S(1)} %collective-permute-done.7.refs_8_), channel_id=1, source_target_pairs={{0,1},{1,0},{2,3},{3,2},{4,5},{5,4},{6,7},{7,6},{8,9},{9,8},{10,11... | collective-permute-start | bytes 393224 | tf_op jit(solution)/shard_map/ppermute | solution.py:195
  19.4 3.7 %collective-permute-start.12 = (bf16[8,64,128]{2,1,0:T(8,128)(2,1)S(1)}, bf16[8,64,128]{2,1,0:T(8,128)(2,1)S(1)}, u32[]{:S(2)}, u32[]{:S(2)}) collective-permute-start(bf16[8,64,128]{2,1,0:T(8,128)(2,1)S(1)} %collective-permute-done.9.refs_10_), channel_id=1, source_target_pairs={{0,1},{1,0},{2,3},{3,2},{4,5},{5,4},{6,7},{7,6},{8,9},{9,8},{10,11... | collective-permute-start | bytes 393224 | tf_op jit(solution)/shard_map/ppermute | solution.py:195
  19.9 3.2 %collective-permute-start.13 = (bf16[8,64,128]{2,1,0:T(8,128)(2,1)S(1)}, bf16[8,64,128]{2,1,0:T(8,128)(2,1)S(1)}, u32[]{:S(2)}, u32[]{:S(2)}) collective-permute-start(bf16[8,64,128]{2,1,0:T(8,128)(2,1)S(1)} %collective-permute-done.8.refs_9_), channel_id=1, source_target_pairs={{0,1},{1,0},{2,3},{3,2},{4,5},{5,4},{6,7},{7,6},{8,9},{9,8},{10,11... | collective-permute-start | bytes 393224 | tf_op jit(solution)/shard_map/ppermute | solution.py:195
  22.8 1.3 %collective-permute-start.14 = (bf16[8,64,128]{2,1,0:T(8,128)(2,1)S(1)}, bf16[8,64,128]{2,1,0:T(8,128)(2,1)S(1)}, u32[]{:S(2)}, u32[]{:S(2)}) collective-permute-start(bf16[8,64,128]{2,1,0:T(8,128)(2,1)S(1)} %collective-permute-done.10.refs_3_), channel_id=1, source_target_pairs={{0,1},{1,0},{2,3},{3,2},{4,5},{5,4},{6,7},{7,6},{8,9},{9,8},{10,11... | collective-permute-start | bytes 393224 | tf_op jit(solution)/shard_map/ppermute | solution.py:195

commit v17 on v16

--- a/solution.py
+++ b/solution.py
@@ -39,28 +39,53 @@
         pairs_ref[p] = both.T.astype(jnp.bfloat16)
 
 
-def left_kernel(dims_hbm, active_hbm, left_hbm, psi_hbm, half_ref, dims_ref, active_ref, left_ref, psi_ref, sems, psi_sems):
+def left_kernel(
+    pair_count, held, dims_hbm, active_hbm, owner_hbm, slot_hbm, left_hbm, psi_hbm,
+    half_ref, list_ref, dims_ref, active_ref, owner_ref, slot_ref, left_ref, psi_ref, sems, psi_sems,
+):
     sectors, blocks, tile, width = psi_ref.shape
+    items = sectors * blocks
+    last = held + len(MIDDLE) * pair_count
     copies = load_all(
         (dims_hbm, dims_ref, sems.at[0]),
         (active_hbm, active_ref, sems.at[1]),
-        (left_hbm, left_ref, sems.at[2]),
+        (owner_hbm, owner_ref, sems.at[2]),
+        (slot_hbm, slot_ref, sems.at[3]),
+        (left_hbm, left_ref, sems.at[4]),
     )
     psi_copies = load_all(*[(psi_hbm.at[a], psi_ref.at[a], psi_sems.at[a]) for a in range(sectors)])
     rows = lax.broadcasted_iota(jnp.int32, (tile, tile), 0)
     cols = lax.broadcasted_iota(jnp.int32, (tile, tile), 1)
     most = jnp.maximum(rows, cols)
+    me = lax.axis_index("sec")
+    by_swaps = lax.axis_size("sec") == len(ORDER)
     for copy in copies:
         copy.wait()
+    in_middle, in_last = jnp.int32(0), jnp.int32(0)
     for a in range(sectors):
         psi_copies[a].wait()
         op = jnp.where(most < dims_ref[a], left_ref[a].astype(jnp.float32), 0.0).astype(jnp.bfloat16)
+        before = in_last
         for k in range(0, blocks, 2):
             both = jnp.concatenate([psi_ref[a, k], psi_ref[a, k + 1]], axis=1)
             part = jnp.dot(op, both, preferred_element_type=jnp.float32)
             for u in range(2):
                 active = active_ref[a, k + u].astype(jnp.float32)
                 half_ref[a, k + u] = (part[:, u * width:(u + 1) * width] * active).astype(jnp.bfloat16)
+                item = a * blocks + k + u
+                owner, slot = owner_ref[a, k + u], slot_ref[a, k + u]
+                at = piece_at(owner ^ me) if by_swaps else owner
+                second = slot >= pair_count
+                at = at * pair_count + jnp.where(second, slot - pair_count, slot)
+                is_early, is_last = at < held, at >= last
+                at = (at - jnp.where(is_last, last, jnp.where(is_early, 0, held))) * 2 + second.astype(jnp.int32)
+                list_ref[jnp.where(is_last, items + 1 + in_last, in_middle)] = at * items + item
+                list_ref[2 * items + 2 + sectors + item] = jnp.where(is_early, at, 0)
+                in_last = in_last + is_last.astype(jnp.int32)
+                in_middle = in_middle + jnp.logical_not(is_early | is_last).astype(jnp.int32)
+        list_ref[2 * items + 2 + a] = in_last - before
+    list_ref[items] = in_middle
+    list_ref[2 * items + 1] = in_last
 
 
 def block_form(pair, second):
@@ -97,41 +122,20 @@
     return jnp.where(r & 7 == 7, end, packed & 15)
 
 
-def early_kernel(pair_count, owner_hbm, slot_hbm, half_ref, *refs):
-    piece_refs = refs[:-6]
-    out_ref, list_ref, pairs_ref, owner_ref, slot_ref, sems = refs[-6:]
+def early_kernel(list_ref, half_ref, *refs):
+    piece_refs, (out_ref, pairs_ref) = refs[:-2], refs[-2:]
     sectors, blocks, tile, width = out_ref.shape
-    items, held = sectors * blocks, pairs_ref.shape[0]
-    last = held + len(MIDDLE) * pair_count
-    copies = load_all((owner_hbm, owner_ref, sems.at[0]), (slot_hbm, slot_ref, sems.at[1]))
+    first = 2 * sectors * blocks + 2 + sectors
     merge(piece_refs, pairs_ref)
-    me = lax.axis_index("sec")
-    for copy in copies:
-        copy.wait()
-
-    def one(a, listed):
-        before = listed[1]
+
+    def one(a, carry):
         for k in range(0, blocks, 2):
-            forms = []
-            for u in range(2):
-                owner, slot = owner_ref[a, k + u], slot_ref[a, k + u]
-                at = piece_at(owner ^ me) if len(piece_refs) > 1 else owner
-                second = slot >= pair_count
-                at = at * pair_count + jnp.where(second, slot - pair_count, slot)
-                forms.append(block_form(pairs_ref[jnp.where(at >= held, 0, at)], second))
-                in_last = at >= last
-                entry = (at - jnp.where(in_last, last, held)) * 2 + second.astype(jnp.int32)
-                entry = entry * items + a * blocks + k + u
-                list_ref[jnp.where(in_last, items + 1 + listed[1], listed[0])] = entry
-                in_middle = (at >= held) & (at < last)
-                listed = listed[0] + in_middle.astype(jnp.int32), listed[1] + in_last.astype(jnp.int32)
+            ats = [list_ref[first + a * blocks + k + u] for u in range(2)]
+            forms = [block_form(pairs_ref[at // 2], at % 2 == 1) for at in ats]
             out_ref[a, k], out_ref[a, k + 1] = two_products([half_ref[a, k], half_ref[a, k + 1]], forms)
-        list_ref[2 * items + 2 + a] = listed[1] - before
-        return listed
-
-    listed = lax.fori_loop(0, sectors, one, (0, 0), unroll=2)
-    list_ref[items] = listed[0]
-    list_ref[2 * items + 1] = listed[1]
+        return carry
+
+    lax.fori_loop(0, sectors, one, 0, unroll=2)
 
 
 def listed_products(group_size, first, list_ref, half_ref, pairs_ref, out_ref):
@@ -226,24 +230,29 @@
         cost_estimate=pl.CostEstimate(flops=0, bytes_accessed=2 * right_ops.size, transcendentals=0),
     )(*in_hbm(dims_right, right_ops))
 
-    def half_of(dims_left):
-        active = term_active.reshape(left_count, block_count)
-        return pl.pallas_call(
-            left_kernel,
-            out_shape=jax.ShapeDtypeStruct(psi.shape, jnp.bfloat16),
-            in_specs=[hbm] * 4,
-            out_specs=vmem,
-            scratch_shapes=[
-                pltpu.SMEM(dims_left.shape, jnp.int32),
-                pltpu.SMEM(active.shape, jnp.int32),
-                pltpu.VMEM(left_ops.shape, jnp.bfloat16),
-                pltpu.VMEM(psi.shape, jnp.bfloat16),
-                pltpu.SemaphoreType.DMA((3,)),
-                pltpu.SemaphoreType.DMA((left_count,)),
-            ],
-            compiler_params=params,
-            cost_estimate=pl.CostEstimate(flops=flops, bytes_accessed=2 * psi.size, transcendentals=0),
-        )(*in_hbm(dims_left, active, left_ops, psi))
+    active = term_active.reshape(left_count, block_count)
+    half, listed = pl.pallas_call(
+        functools.partial(left_kernel, pair_count, len(EARLY if by_swaps else range(count)) * pair_count),
+        out_shape=(
+            jax.ShapeDtypeStruct(psi.shape, jnp.bfloat16),
+            pltpu.SMEM((3 * items + 2 + left_count,), jnp.int32),
+        ),
+        in_specs=[hbm] * 6,
+        out_specs=(vmem, smem),
+        scratch_shapes=[
+            pltpu.SMEM(dims_left.shape, jnp.int32),
+            pltpu.SMEM(active.shape, jnp.int32),
+            pltpu.SMEM(right_owner.shape, jnp.int32),
+            pltpu.SMEM(right_slot.shape, jnp.int32),
+            pltpu.VMEM(left_ops.shape, jnp.bfloat16),
+            pltpu.VMEM(psi.shape, jnp.bfloat16),
+            pltpu.SemaphoreType.DMA((5,)),
+            pltpu.SemaphoreType.DMA((left_count,)),
+        ],
+        compiler_params=params,
+        cost_estimate=pl.CostEstimate(flops=flops, bytes_accessed=2 * psi.size, transcendentals=0),
+    )(*in_hbm(dims_left, active, right_owner, right_slot, left_ops, psi))
+    listed = pltpu.with_memory_space_constraint(listed, pltpu.SMEM)
 
     if by_swaps:
         pieces = {0: pairs}
@@ -252,7 +261,6 @@
                 pieces[r | bit] = swap(pieces[r], bit)
 
         pass_on((0, FAR), (0, NEAR), (0, CROSS))
-        half = half_of(dims_left)
         held = (0, NEAR,)
         half, ends = lax.optimization_barrier((half, [pieces[r] for r in held]))
         pieces.update(zip(held, ends))
@@ -260,32 +268,21 @@
         pass_on((0, CORE), (NEAR, CORE), (CROSS, CORE), (NEAR | CROSS, CORE), (FAR | NEAR, CORE), (FAR, CORE), (FAR | CROSS, CORE))
         early = [pieces[r] for r in EARLY]
     else:
-        half = half_of(dims_left)
         early = [lax.all_gather(pairs, "sec", axis=0, tiled=True)]
 
-    sigma, listed = pl.pallas_call(
-        functools.partial(early_kernel, pair_count),
-        out_shape=(
-            jax.ShapeDtypeStruct(psi.shape, jnp.bfloat16),
-            pltpu.SMEM((2 * items + 2 + left_count,), jnp.int32),
-        ),
-        in_specs=[hbm, hbm] + [vmem] * (1 + len(early)),
-        out_specs=(vmem, smem),
-        scratch_shapes=[
-            pltpu.VMEM((sum(piece.shape[0] for piece in early), tile, 2 * tile), jnp.bfloat16),
-            pltpu.SMEM(right_owner.shape, jnp.int32),
-            pltpu.SMEM(right_slot.shape, jnp.int32),
-            pltpu.SemaphoreType.DMA((2,)),
-        ],
+    sigma = pl.pallas_call(
+        early_kernel,
+        out_shape=jax.ShapeDtypeStruct(psi.shape, jnp.bfloat16),
+        in_specs=[smem] + [vmem] * (1 + len(early)),
+        out_specs=vmem,
+        scratch_shapes=[pltpu.VMEM((sum(piece.shape[0] for piece in early), tile, 2 * tile), jnp.bfloat16)],
         compiler_params=params,
         cost_estimate=pl.CostEstimate(flops=flops, bytes_accessed=2 * psi.size, transcendentals=0),
-    )(*in_hbm(right_owner, right_slot), half, *early)
-
+    )(listed, half, *early)
     if by_swaps:
         top = FAR | NEAR | CROSS
         pieces[top], sigma = lax.optimization_barrier((pieces[top], sigma))
         pieces[top | CORE] = swap(pieces[top], CORE)
-        listed = pltpu.with_memory_space_constraint(listed, pltpu.SMEM)
         sigma = pl.pallas_call(
             middle_kernel,
             out_shape=jax.ShapeDtypeStruct(psi.shape, jnp.bfloat16),

time: 25.6 us -> 25.9 us (1.012)
  waiting for transfers between devices: 4.45 us -> 5.28 us
  Pallas kernels: 8.33 us -> 7.87 us
    ppermute x15, waiting for transfers between devices: 4.45 us -> 5.28 us  [swap(): return lax.ppermute(piece, 'sec', [(i, i ^ bit) for i in range(count)])]
    pallas_call x2, Pallas kernels: 5.3 us -> 4.81 us  [the longest x1 3.19 us: per_device(): pl.pallas_call(functools.partial(left_kernel, pair_count, len(EARLY if by...]
  transfers between devices with their start and end apart: 15 -> 15, of which waited for: 5 -> 5; matrix products, arithmetic and copies ran while one was open for 0% -> 0% of each run, Pallas kernels for 24% -> 22%
where the time goes in v17:
time: 25.9 us; the launch traced here: 25.5 us
  starting transfers between devices  12.3 us (47%)
  Pallas kernels  7.87 us (30%)
  waiting for transfers between devices  5.28 us (20%)
    ppermute x15, starting transfers between devices, swap(): return lax.ppermute(piece, 'sec', [(i, i ^ bit) for i in range(count)])  12.3 us
    ppermute x15, waiting for transfers between devices, swap(): return lax.ppermute(piece, 'sec', [(i, i ^ bit) for i in range(count)])  5.28 us
    pallas_call x1, Pallas kernels, per_device(): pl.pallas_call(functools.partial(left_kernel, pair_count, len(EARLY if by...  3.19 us
    pallas_call x1, Pallas kernels, per_device(): pl.pallas_call(early_kernel, out_shape=jax.ShapeDtypeStruct(psi.shape, jn...  1.62 us
    pallas_call x1, Pallas kernels, per_device(): pl.pallas_call(last_kernel, out_shape=jax.ShapeDtypeStruct(psi.shape, jnp...  1.21 us
    pallas_call x1, Pallas kernels, per_device(): pl.pallas_call(pack_kernel, out_shape=jax.ShapeDtypeStruct((pair_count, t...  1.09 us
    pallas_call x1, Pallas kernels, per_device(): pl.pallas_call(middle_kernel, out_shape=jax.ShapeDtypeStruct(psi.shape, j...  0.76 us
  transfers between devices with their start and end apart: 15, of which 5 were waited for; matrix products, arithmetic and copies ran while one was open for 0% of the time, Pallas kernels for 22%

profile of v17, /device:TPU:0, one launch (start us, length us, event | category | flops | bytes accessed | tf_op | source)
XLA Modules:
  0.0 25.5 jit_solution(8081622191234526829)
XLA Ops:
  0.0 1.1 %shard_map.83.refs_0_ = bf16[8,64,128]{2,1,0:T(8,128)(2,1)S(1)} custom-call(s32[16]{0:T(128)} %dims_hbm.3, bf16[16,64,64]{2,1,0:T(8,128)(2,1)} %right_hbm.1), custom_call_target="tpu_custom_call" | custom-call | bytes 131072 | tf_op jit(solution)/shard_map/pallas_call | solution.py:219
  1.1 3.1 %collective-permute-start.3 = (bf16[8,64,128]{2,1,0:T(8,128)(2,1)S(1)}, bf16[8,64,128]{2,1,0:T(8,128)(2,1)S(1)}, u32[]{:S(2)}, u32[]{:S(2)}) collective-permute-start(bf16[8,64,128]{2,1,0:T(8,128)(2,1)S(1)} %shard_map.83.refs_0_), channel_id=1, source_target_pairs={{0,4},{1,5},{2,6},{3,7},{4,0},{5,1},{6,2},{7,3},{8,12},{9,13},{10,... | collective-permute-start | bytes 393224 | tf_op jit(solution)/shard_map/ppermute | solution.py:199
  4.2 2.6 %collective-permute-start = (bf16[8,64,128]{2,1,0:T(8,128)(2,1)S(1)}, bf16[8,64,128]{2,1,0:T(8,128)(2,1)S(1)}, u32[]{:S(2)}, u32[]{:S(2)}) collective-permute-start(bf16[8,64,128]{2,1,0:T(8,128)(2,1)S(1)} %shard_map.83.refs_0_), channel_id=1, source_target_pairs={{0,8},{1,9},{2,10},{3,11},{4,12},{5,13},{6,14},{7,15},{8,0},{9,1},... | collective-permute-start | bytes 393224 | tf_op jit(solution)/shard_map/ppermute | solution.py:199
  6.8 1.5 %collective-permute-start.5 = (bf16[8,64,128]{2,1,0:T(8,128)(2,1)S(1)}, bf16[8,64,128]{2,1,0:T(8,128)(2,1)S(1)}, u32[]{:S(2)}, u32[]{:S(2)}) collective-permute-start(bf16[8,64,128]{2,1,0:T(8,128)(2,1)S(1)} %shard_map.83.refs_0_), channel_id=1, source_target_pairs={{0,2},{1,3},{2,0},{3,1},{4,6},{5,7},{6,4},{7,5},{8,10},{9,11},{10,... | collective-permute-start | bytes 393224 | tf_op jit(solution)/shard_map/ppermute | solution.py:199
  8.3 3.2 %shard_map.82 = (bf16[8,8,64,128]{3,2,1,0:T(8,128)(2,1)S(1)}, s32[202]{0:T(256)S(4)}) custom-call(s32[8]{0:T(128)} %dims_hbm.2, s32[8,8]{1,0:T(8,128)} %bitcast.1, s32[8,8]{1,0:T(8,128)} %owner_hbm.1, s32[8,8]{1,0:T(8,128)} %slot_hbm.1, bf16[8,64,64]{2,1,0:T(8,128)(2,1)} %left_hbm.1, bf16[8,8,64,128]{3,2,1,0:T(8,128)(2,1)} %psi_hbm.1), custom_call_target="tpu_custom_call" | custom-call | flops 67108864 | bytes 1048576 | tf_op jit(solution)/shard_map/pallas_call | solution.py:234
  11.5 0.0 collective-permute-done.3.refs_4_
  11.5 0.6 %collective-permute-start.8 = (bf16[8,64,128]{2,1,0:T(8,128)(2,1)S(1)}, bf16[8,64,128]{2,1,0:T(8,128)(2,1)S(1)}, u32[]{:S(2)}, u32[]{:S(2)}) collective-permute-start(bf16[8,64,128]{2,1,0:T(8,128)(2,1)S(1)} %collective-permute-done.3.refs_4_), channel_id=1, source_target_pairs={{0,2},{1,3},{2,0},{3,1},{4,6},{5,7},{6,4},{7,5},{8,10},{9,11},{10,... | collective-permute-start | bytes 393224 | tf_op jit(solution)/shard_map/ppermute | solution.py:199
  12.1 0.0 collective-permute-start.7
  12.1 0.8 %collective-permute-done.refs_8_ = bf16[8,64,128]{2,1,0:T(8,128)(2,1)S(1)} collective-permute-done((bf16[8,64,128]{2,1,0:T(8,128)(2,1)S(1)}, bf16[8,64,128]{2,1,0:T(8,128)(2,1)S(1)}, u32[]{:S(2)}, u32[]{:S(2)}) %collective-permute-start) | collective-permute-done | bytes 131104 | tf_op jit(solution)/shard_map/ppermute | solution.py:199
  12.9 0.4 %collective-permute-start.1 = (bf16[8,64,128]{2,1,0:T(8,128)(2,1)S(1)}, bf16[8,64,128]{2,1,0:T(8,128)(2,1)S(1)}, u32[]{:S(2)}, u32[]{:S(2)}) collective-permute-start(bf16[8,64,128]{2,1,0:T(8,128)(2,1)S(1)} %collective-permute-done.refs_8_), channel_id=1, source_target_pairs={{0,4},{1,5},{2,6},{3,7},{4,0},{5,1},{6,2},{7,3},{8,12},{9,13},{10,... | collective-permute-start | bytes 393224 | tf_op jit(solution)/shard_map/ppermute | solution.py:199
  13.4 0.0 collective-permute-start.4
  13.4 0.0 collective-permute-done.5.refs_2_
  13.4 1.5 %collective-permute-start.10 = (bf16[8,64,128]{2,1,0:T(8,128)(2,1)S(1)}, bf16[8,64,128]{2,1,0:T(8,128)(2,1)S(1)}, u32[]{:S(2)}, u32[]{:S(2)}) collective-permute-start(bf16[8,64,128]{2,1,0:T(8,128)(2,1)S(1)} %collective-permute-done.refs_8_), channel_id=1, source_target_pairs={{0,2},{1,3},{2,0},{3,1},{4,6},{5,7},{6,4},{7,5},{8,10},{9,11},{10,... | collective-permute-start | bytes 393224 | tf_op jit(solution)/shard_map/ppermute | solution.py:199
  14.9 1.7 %collective-permute-done.8.refs_6_ = bf16[8,64,128]{2,1,0:T(8,128)(2,1)S(1)} collective-permute-done((bf16[8,64,128]{2,1,0:T(8,128)(2,1)S(1)}, bf16[8,64,128]{2,1,0:T(8,128)(2,1)S(1)}, u32[]{:S(2)}, u32[]{:S(2)}) %collective-permute-start.8) | collective-permute-done | bytes 131104 | tf_op jit(solution)/shard_map/ppermute | solution.py:199
  16.5 0.0 collective-permute-start.6
  16.5 0.0 collective-permute-done.7.refs_5_
  16.5 0.5 %collective-permute-start.9 = (bf16[8,64,128]{2,1,0:T(8,128)(2,1)S(1)}, bf16[8,64,128]{2,1,0:T(8,128)(2,1)S(1)}, u32[]{:S(2)}, u32[]{:S(2)}) collective-permute-start(bf16[8,64,128]{2,1,0:T(8,128)(2,1)S(1)} %collective-permute-done.8.refs_6_), channel_id=1, source_target_pairs={{0,1},{1,0},{2,3},{3,2},{4,5},{5,4},{6,7},{7,6},{8,9},{9,8},{10,11... | collective-permute-start | bytes 393224 | tf_op jit(solution)/shard_map/ppermute | solution.py:199
  17.0 1.0 %collective-permute-done.1.refs_10_ = bf16[8,64,128]{2,1,0:T(8,128)(2,1)S(1)} collective-permute-done((bf16[8,64,128]{2,1,0:T(8,128)(2,1)S(1)}, bf16[8,64,128]{2,1,0:T(8,128)(2,1)S(1)}, u32[]{:S(2)}, u32[]{:S(2)}) %collective-permute-start.1) | collective-permute-done | bytes 131104 | tf_op jit(solution)/shard_map/ppermute | solution.py:199
  18.0 1.5 %collective-permute-start.2 = (bf16[8,64,128]{2,1,0:T(8,128)(2,1)S(1)}, bf16[8,64,128]{2,1,0:T(8,128)(2,1)S(1)}, u32[]{:S(2)}, u32[]{:S(2)}) collective-permute-start(bf16[8,64,128]{2,1,0:T(8,128)(2,1)S(1)} %collective-permute-done.1.refs_10_), channel_id=1, source_target_pairs={{0,2},{1,3},{2,0},{3,1},{4,6},{5,7},{6,4},{7,5},{8,10},{9,11},{10,... | collective-permute-start | bytes 393224 | tf_op jit(solution)/shard_map/ppermute | solution.py:199
  19.5 0.0 collective-permute-done.4.refs_1_
  19.5 0.0 collective-permute-start.11
  19.5 0.0 collective-permute-done.10.refs_9_
  19.5 0.5 %collective-permute-start.12 = (bf16[8,64,128]{2,1,0:T(8,128)(2,1)S(1)}, bf16[8,64,128]{2,1,0:T(8,128)(2,1)S(1)}, u32[]{:S(2)}, u32[]{:S(2)}) collective-permute-start(bf16[8,64,128]{2,1,0:T(8,128)(2,1)S(1)} %collective-permute-done.1.refs_10_), channel_id=1, source_target_pairs={{0,1},{1,0},{2,3},{3,2},{4,5},{5,4},{6,7},{7,6},{8,9},{9,8},{10,11... | collective-permute-start | bytes 393224 | tf_op jit(solution)/shard_map/ppermute | solution.py:199
  20.0 0.0 collective-permute-done.6.refs_3_
  20.0 0.1 collective-permute-start.13
  20.1 0.0 collective-permute-done.9.refs_7_
  20.1 1.6 %shard_map.84.early_ref = bf16[8,8,64,128]{3,2,1,0:T(8,128)(2,1)S(1)} custom-call(s32[202]{0:T(256)S(4)} %get-tuple-element.12.list_ref, bf16[8,8,64,128]{3,2,1,0:T(8,128)(2,1)S(1)} %get-tuple-element.14.half_ref, bf16[8,64,128]{2,1,0:T(8,128)(2,1)S(1)} %shard_map.83.refs_0_, bf16[8,64,128]{2,1,0:T(8,128)(2,1)S(1)} %collective-permute-done.4.refs_1_, ...), custom_call_target="tpu_custom_call" | custom-call | flops 67108864 | bytes 1048576 | tf_op jit(solution)/shard_map/pallas_call | solution.py:273
  21.7 1.3 %collective-permute-done.2.refs_3_ = bf16[8,64,128]{2,1,0:T(8,128)(2,1)S(1)} collective-permute-done((bf16[8,64,128]{2,1,0:T(8,128)(2,1)S(1)}, bf16[8,64,128]{2,1,0:T(8,128)(2,1)S(1)}, u32[]{:S(2)}, u32[]{:S(2)}) %collective-permute-start.2) | collective-permute-done | bytes 131104 | tf_op jit(solution)/shard_map/ppermute | solution.py:199
  23.0 0.0 collective-permute-start.14
  23.0 0.0 collective-permute-done.11.refs_0_
  23.0 0.0 collective-permute-done.12.refs_1_
  23.0 0.0 collective-permute-done.13.refs_2_
  23.0 0.8 %shard_map.85.middle_ref = bf16[8,8,64,128]{3,2,1,0:T(8,128)(2,1)S(1)} custom-call(s32[202]{0:T(256)S(4)} %get-tuple-element.12.list_ref, bf16[8,8,64,128]{3,2,1,0:T(8,128)(2,1)S(1)} %shard_map.84.early_ref, bf16[8,8,64,128]{3,2,1,0:T(8,128)(2,1)S(1)} %get-tuple-element.14.half_ref, bf16[8,64,128]{2,1,0:T(8,128)(2,1)S(1)} %collective-permute-done.11.refs_0_, ...), custom_call_target="tpu_custom_call" | custom-call | flops 16777216 | bytes 262144 | tf_op jit(solution)/shard_map/pallas_call | solution.py:286
  23.8 0.6 %collective-permute-done.14.pairs_ref = bf16[8,64,128]{2,1,0:T(8,128)(2,1)S(1)} collective-permute-done((bf16[8,64,128]{2,1,0:T(8,128)(2,1)S(1)}, bf16[8,64,128]{2,1,0:T(8,128)(2,1)S(1)}, u32[]{:S(2)}, u32[]{:S(2)}) %collective-permute-start.14) | collective-permute-done | bytes 131104 | tf_op jit(solution)/shard_map/ppermute | solution.py:199
  24.3 1.2 %shard_map.86 = bf16[8,8,64,128]{3,2,1,0:T(8,128)(2,1)} custom-call(s32[202]{0:T(256)S(4)} %get-tuple-element.12.list_ref, bf16[8,8,64,128]{3,2,1,0:T(8,128)(2,1)S(1)} %shard_map.85.middle_ref, bf16[8,8,64,128]{3,2,1,0:T(8,128)(2,1)S(1)} %get-tuple-element.14.half_ref, bf16[8,64,128]{2,1,0:T(8,128)(2,1)S(1)} %collective-permute-done.14.pairs_ref), custom_call_target="tpu_custom_call" | custom-call | flops 4194304 | bytes 1048576 | tf_op jit(solution)/shard_map/pallas_call | solution.py:295
Async XLA Ops:
  1.1 10.4 %collective-permute-start.3 = (bf16[8,64,128]{2,1,0:T(8,128)(2,1)S(1)}, bf16[8,64,128]{2,1,0:T(8,128)(2,1)S(1)}, u32[]{:S(2)}, u32[]{:S(2)}) collective-permute-start(bf16[8,64,128]{2,1,0:T(8,128)(2,1)S(1)} %shard_map.83.refs_0_), channel_id=1, source_target_pairs={{0,4},{1,5},{2,6},{3,7},{4,0},{5,1},{6,2},{7,3},{8,12},{9,13},{10,... | collective-permute-start | bytes 393224 | tf_op jit(solution)/shard_map/ppermute | solution.py:199
  4.2 8.7 %collective-permute-start = (bf16[8,64,128]{2,1,0:T(8,128)(2,1)S(1)}, bf16[8,64,128]{2,1,0:T(8,128)(2,1)S(1)}, u32[]{:S(2)}, u32[]{:S(2)}) collective-permute-start(bf16[8,64,128]{2,1,0:T(8,128)(2,1)S(1)} %shard_map.83.refs_0_), channel_id=1, source_target_pairs={{0,8},{1,9},{2,10},{3,11},{4,12},{5,13},{6,14},{7,15},{8,0},{9,1},... | collective-permute-start | bytes 393224 | tf_op jit(solution)/shard_map/ppermute | solution.py:199
  6.8 6.6 %collective-permute-start.5 = (bf16[8,64,128]{2,1,0:T(8,128)(2,1)S(1)}, bf16[8,64,128]{2,1,0:T(8,128)(2,1)S(1)}, u32[]{:S(2)}, u32[]{:S(2)}) collective-permute-start(bf16[8,64,128]{2,1,0:T(8,128)(2,1)S(1)} %shard_map.83.refs_0_), channel_id=1, source_target_pairs={{0,2},{1,3},{2,0},{3,1},{4,6},{5,7},{6,4},{7,5},{8,10},{9,11},{10,... | collective-permute-start | bytes 393224 | tf_op jit(solution)/shard_map/ppermute | solution.py:199
  11.5 5.0 %collective-permute-start.8 = (bf16[8,64,128]{2,1,0:T(8,128)(2,1)S(1)}, bf16[8,64,128]{2,1,0:T(8,128)(2,1)S(1)}, u32[]{:S(2)}, u32[]{:S(2)}) collective-permute-start(bf16[8,64,128]{2,1,0:T(8,128)(2,1)S(1)} %collective-permute-done.3.refs_4_), channel_id=1, source_target_pairs={{0,2},{1,3},{2,0},{3,1},{4,6},{5,7},{6,4},{7,5},{8,10},{9,11},{10,... | collective-permute-start | bytes 393224 | tf_op jit(solution)/shard_map/ppermute | solution.py:199
  12.1 4.4 %collective-permute-start.7 = (bf16[8,64,128]{2,1,0:T(8,128)(2,1)S(1)}, bf16[8,64,128]{2,1,0:T(8,128)(2,1)S(1)}, u32[]{:S(2)}, u32[]{:S(2)}) collective-permute-start(bf16[8,64,128]{2,1,0:T(8,128)(2,1)S(1)} %collective-permute-done.3.refs_4_), channel_id=1, source_target_pairs={{0,1},{1,0},{2,3},{3,2},{4,5},{5,4},{6,7},{7,6},{8,9},{9,8},{10,11... | collective-permute-start | bytes 393224 | tf_op jit(solution)/shard_map/ppermute | solution.py:199
  12.9 5.1 %collective-permute-start.1 = (bf16[8,64,128]{2,1,0:T(8,128)(2,1)S(1)}, bf16[8,64,128]{2,1,0:T(8,128)(2,1)S(1)}, u32[]{:S(2)}, u32[]{:S(2)}) collective-permute-start(bf16[8,64,128]{2,1,0:T(8,128)(2,1)S(1)} %collective-permute-done.refs_8_), channel_id=1, source_target_pairs={{0,4},{1,5},{2,6},{3,7},{4,0},{5,1},{6,2},{7,3},{8,12},{9,13},{10,... | collective-permute-start | bytes 393224 | tf_op jit(solution)/shard_map/ppermute | solution.py:199
  13.4 6.1 %collective-permute-start.4 = (bf16[8,64,128]{2,1,0:T(8,128)(2,1)S(1)}, bf16[8,64,128]{2,1,0:T(8,128)(2,1)S(1)}, u32[]{:S(2)}, u32[]{:S(2)}) collective-permute-start(bf16[8,64,128]{2,1,0:T(8,128)(2,1)S(1)} %shard_map.83.refs_0_), channel_id=1, source_target_pairs={{0,1},{1,0},{2,3},{3,2},{4,5},{5,4},{6,7},{7,6},{8,9},{9,8},{10,11... | collective-permute-start | bytes 393224 | tf_op jit(solution)/shard_map/ppermute | solution.py:199
  13.4 6.1 %collective-permute-start.10 = (bf16[8,64,128]{2,1,0:T(8,128)(2,1)S(1)}, bf16[8,64,128]{2,1,0:T(8,128)(2,1)S(1)}, u32[]{:S(2)}, u32[]{:S(2)}) collective-permute-start(bf16[8,64,128]{2,1,0:T(8,128)(2,1)S(1)} %collective-permute-done.refs_8_), channel_id=1, source_target_pairs={{0,2},{1,3},{2,0},{3,1},{4,6},{5,7},{6,4},{7,5},{8,10},{9,11},{10,... | collective-permute-start | bytes 393224 | tf_op jit(solution)/shard_map/ppermute | solution.py:199
  16.5 3.5 %collective-permute-start.6 = (bf16[8,64,128]{2,1,0:T(8,128)(2,1)S(1)}, bf16[8,64,128]{2,1,0:T(8,128)(2,1)S(1)}, u32[]{:S(2)}, u32[]{:S(2)}) collective-permute-start(bf16[8,64,128]{2,1,0:T(8,128)(2,1)S(1)} %collective-permute-done.5.refs_2_), channel_id=1, source_target_pairs={{0,1},{1,0},{2,3},{3,2},{4,5},{5,4},{6,7},{7,6},{8,9},{9,8},{10,11... | collective-permute-start | bytes 393224 | tf_op jit(solution)/shard_map/ppermute | solution.py:199
  16.5 3.6 %collective-permute-start.9 = (bf16[8,64,128]{2,1,0:T(8,128)(2,1)S(1)}, bf16[8,64,128]{2,1,0:T(8,128)(2,1)S(1)}, u32[]{:S(2)}, u32[]{:S(2)}) collective-permute-start(bf16[8,64,128]{2,1,0:T(8,128)(2,1)S(1)} %collective-permute-done.8.refs_6_), channel_id=1, source_target_pairs={{0,1},{1,0},{2,3},{3,2},{4,5},{5,4},{6,7},{7,6},{8,9},{9,8},{10,11... | collective-permute-start | bytes 393224 | tf_op jit(solution)/shard_map/ppermute | solution.py:199
  18.0 5.0 %collective-permute-start.2 = (bf16[8,64,128]{2,1,0:T(8,128)(2,1)S(1)}, bf16[8,64,128]{2,1,0:T(8,128)(2,1)S(1)}, u32[]{:S(2)}, u32[]{:S(2)}) collective-permute-start(bf16[8,64,128]{2,1,0:T(8,128)(2,1)S(1)} %collective-permute-done.1.refs_10_), channel_id=1, source_target_pairs={{0,2},{1,3},{2,0},{3,1},{4,6},{5,7},{6,4},{7,5},{8,10},{9,11},{10,... | collective-permute-start | bytes 393224 | tf_op jit(solution)/shard_map/ppermute | solution.py:199
  19.5 3.5 %collective-permute-start.11 = (bf16[8,64,128]{2,1,0:T(8,128)(2,1)S(1)}, bf16[8,64,128]{2,1,0:T(8,128)(2,1)S(1)}, u32[]{:S(2)}, u32[]{:S(2)}) collective-permute-start(bf16[8,64,128]{2,1,0:T(8,128)(2,1)S(1)} %collective-permute-done.refs_8_), channel_id=1, source_target_pairs={{0,1},{1,0},{2,3},{3,2},{4,5},{5,4},{6,7},{7,6},{8,9},{9,8},{10,11... | collective-permute-start | bytes 393224 | tf_op jit(solution)/shard_map/ppermute | solution.py:199
  19.5 3.5 %collective-permute-start.12 = (bf16[8,64,128]{2,1,0:T(8,128)(2,1)S(1)}, bf16[8,64,128]{2,1,0:T(8,128)(2,1)S(1)}, u32[]{:S(2)}, u32[]{:S(2)}) collective-permute-start(bf16[8,64,128]{2,1,0:T(8,128)(2,1)S(1)} %collective-permute-done.1.refs_10_), channel_id=1, source_target_pairs={{0,1},{1,0},{2,3},{3,2},{4,5},{5,4},{6,7},{7,6},{8,9},{9,8},{10,11... | collective-permute-start | bytes 393224 | tf_op jit(solution)/shard_map/ppermute | solution.py:199
  20.0 3.0 %collective-permute-start.13 = (bf16[8,64,128]{2,1,0:T(8,128)(2,1)S(1)}, bf16[8,64,128]{2,1,0:T(8,128)(2,1)S(1)}, u32[]{:S(2)}, u32[]{:S(2)}) collective-permute-start(bf16[8,64,128]{2,1,0:T(8,128)(2,1)S(1)} %collective-permute-done.10.refs_9_), channel_id=1, source_target_pairs={{0,1},{1,0},{2,3},{3,2},{4,5},{5,4},{6,7},{7,6},{8,9},{9,8},{10,11... | collective-permute-start | bytes 393224 | tf_op jit(solution)/shard_map/ppermute | solution.py:199
  23.0 1.3 %collective-permute-start.14 = (bf16[8,64,128]{2,1,0:T(8,128)(2,1)S(1)}, bf16[8,64,128]{2,1,0:T(8,128)(2,1)S(1)}, u32[]{:S(2)}, u32[]{:S(2)}) collective-permute-start(bf16[8,64,128]{2,1,0:T(8,128)(2,1)S(1)} %collective-permute-done.2.refs_3_), channel_id=1, source_target_pairs={{0,1},{1,0},{2,3},{3,2},{4,5},{5,4},{6,7},{7,6},{8,9},{9,8},{10,11... | collective-permute-start | bytes 393224 | tf_op jit(solution)/shard_map/ppermute | solution.py:199

commit v18 on v17

--- a/solution.py
+++ b/solution.py
@@ -9,9 +9,19 @@
 
 VMEM_LIMIT = 48 * 1024 * 1024
 FAR, NEAR, CROSS, CORE = 8, 4, 2, 1
-MIDDLE = (FAR | CORE, FAR | NEAR | CORE, FAR | CROSS | CORE, FAR | NEAR | CROSS)
-LAST = (FAR | NEAR | CROSS | CORE,)
-EARLY = tuple(r for r in range(16) if r not in MIDDLE + LAST)
+OWN, SIDE = (0, 0), (CROSS, CROSS)
+FIRST, SECOND = (FAR, NEAR), (NEAR, FAR)
+THIRD, FOURTH = (FAR | NEAR, NEAR | CROSS), (NEAR | CROSS, FAR | NEAR)
+FAR_SIDE, END = (FAR | CROSS, FAR | CROSS), (FAR | NEAR | CROSS, FAR | NEAR | CROSS)
+
+
+def partner(name):
+    return name[1] | CORE, name[0] | CORE
+
+
+EARLY = (OWN, SIDE, FIRST, SECOND, THIRD, FOURTH, FAR_SIDE, partner(OWN), partner(SIDE), partner(FIRST), partner(SECOND))
+MIDDLE = (partner(THIRD), partner(FOURTH), partner(FAR_SIDE), END)
+LAST = (partner(END),)
 ORDER = EARLY + MIDDLE + LAST
 
 
@@ -74,7 +84,7 @@
                 half_ref[a, k + u] = (part[:, u * width:(u + 1) * width] * active).astype(jnp.bfloat16)
                 item = a * blocks + k + u
                 owner, slot = owner_ref[a, k + u], slot_ref[a, k + u]
-                at = piece_at(owner ^ me) if by_swaps else owner
+                at = piece_at(owner ^ me, me) if by_swaps else owner
                 second = slot >= pair_count
                 at = at * pair_count + jnp.where(second, slot - pair_count, slot)
                 is_early, is_last = at < held, at >= last
@@ -114,12 +124,15 @@
         at += piece.shape[0]
 
 
-def piece_at(r):
-    low = sum(ORDER.index(i) << (4 * i) for i in range(7))
-    high = sum(ORDER.index(i + 8) << (4 * i) for i in range(7))
-    packed = jnp.where(r < 8, low, high) >> (4 * (r & 7))
-    end = jnp.where(r < 8, ORDER.index(7), ORDER.index(15))
-    return jnp.where(r & 7 == 7, end, packed & 15)
+def piece_at(r, me):
+    at = jnp.int32(0)
+    for parity in range(2):
+        places = [ORDER.index(next(name for name in ORDER if name[parity] == i)) for i in range(len(ORDER))]
+        for half in range(2):
+            packed = sum(place << (4 * i) for i, place in enumerate(places[8 * half:8 * half + 7]))
+            mine = jnp.where(r & 7 == 7, places[8 * half + 7], (packed >> (4 * (r & 7))) & 15)
+            at = jnp.where((me & 1 == parity) & (r >> 3 == half), mine, at)
+    return at
 
 
 def early_kernel(list_ref, half_ref, *refs):
@@ -194,9 +207,9 @@
         store(a, out_ref).wait()
 
 
-def swap(piece, bit):
+def swap(piece, even_bit, odd_bit):
     count = lax.axis_size("sec")
-    return lax.ppermute(piece, "sec", [(i, i ^ bit) for i in range(count)])
+    return lax.ppermute(piece, "sec", [(i, i ^ (odd_bit if i & CORE else even_bit)) for i in range(count)])
 
 
 def per_device(
@@ -255,18 +268,34 @@
     listed = pltpu.with_memory_space_constraint(listed, pltpu.SMEM)
 
     if by_swaps:
-        pieces = {0: pairs}
-        def pass_on(*pairs_of):
-            for r, bit in pairs_of:
-                pieces[r | bit] = swap(pieces[r], bit)
-
-        pass_on((0, FAR), (0, NEAR), (0, CROSS))
-        held = (0, NEAR,)
+        pieces = {OWN: pairs}
+        odd = lax.axis_index("sec") & CORE == 1
+
+        def pass_on(*routes):
+            for name, target in routes:
+                pieces[target] = swap(pieces[name], name[0] ^ target[0], name[1] ^ target[1])
+
+        def share(*names):
+            for name in names:
+                pieces[partner(name)] = swap(pieces[name], CORE, CORE)
+
+        def cross(even_name, odd_name, target):
+            pieces[target] = swap(jnp.where(odd, pieces[odd_name], pieces[even_name]), CROSS, CROSS)
+
+        pass_on((OWN, FIRST), (OWN, SIDE))
+        share(OWN)
+        held = (partner(OWN),)
+        pieces[OWN], ends = lax.optimization_barrier((pieces[OWN], [pieces[r] for r in held]))
+        pieces.update(zip(held, ends))
+        pass_on((OWN, SECOND), )
+        held = (FIRST,)
         half, ends = lax.optimization_barrier((half, [pieces[r] for r in held]))
         pieces.update(zip(held, ends))
-        pass_on((NEAR, CROSS), (FAR, NEAR), (FAR, CROSS), (FAR | NEAR, CROSS))
-        pass_on((0, CORE), (NEAR, CORE), (CROSS, CORE), (NEAR | CROSS, CORE), (FAR | NEAR, CORE), (FAR, CORE), (FAR | CROSS, CORE))
-        early = [pieces[r] for r in EARLY]
+        pass_on((FIRST, THIRD), (SECOND, FOURTH))
+        cross(FIRST, SECOND, FAR_SIDE)
+        cross(THIRD, FOURTH, END)
+        share(SIDE, FIRST, SECOND, THIRD, FOURTH, FAR_SIDE)
+        early = [pieces[name] for name in EARLY]
     else:
         early = [lax.all_gather(pairs, "sec", axis=0, tiled=True)]
 
@@ -280,9 +309,8 @@
         cost_estimate=pl.CostEstimate(flops=flops, bytes_accessed=2 * psi.size, transcendentals=0),
     )(listed, half, *early)
     if by_swaps:
-        top = FAR | NEAR | CROSS
-        pieces[top], sigma = lax.optimization_barrier((pieces[top], sigma))
-        pieces[top | CORE] = swap(pieces[top], CORE)
+        pieces[END], sigma = lax.optimization_barrier((pieces[END], sigma))
+        share(END)
         sigma = pl.pallas_call(
             middle_kernel,
             out_shape=jax.ShapeDtypeStruct(psi.shape, jnp.bfloat16),
@@ -291,7 +319,7 @@
             scratch_shapes=[pltpu.VMEM((len(MIDDLE) * pair_count, tile, 2 * tile), jnp.bfloat16)],
             compiler_params=params,
             cost_estimate=pl.CostEstimate(flops=flops // 4, bytes_accessed=psi.size // 2, transcendentals=0),
-        )(listed, sigma, half, *[pieces[r] for r in MIDDLE])
+        )(listed, sigma, half, *[pieces[name] for name in MIDDLE])
         sigma = pl.pallas_call(
             last_kernel,
             out_shape=jax.ShapeDtypeStruct(psi.shape, jnp.bfloat16),

time: 25.9 us -> 27.3 us (1.054)
  starting transfers between devices: 12.3 us -> 14.1 us
  waiting for transfers between devices: 5.28 us -> 4.93 us
    ppermute x15, starting transfers between devices: 12.3 us -> 14.1 us  [swap(): lax.ppermute(piece, 'sec', [(i, i ^ (odd_bit if i & CORE else even_bit))...]
    ppermute x15, waiting for transfers between devices: 5.28 us -> 4.93 us  [swap(): lax.ppermute(piece, 'sec', [(i, i ^ (odd_bit if i & CORE else even_bit))...]
    pallas_call x1, Pallas kernels: 0.76 us -> 1.09 us  [per_device(): pl.pallas_call(middle_kernel, out_shape=jax.ShapeDtypeStruct(psi.shape, j...]
    pallas_call x1, Pallas kernels: 3.19 us -> 2.91 us  [per_device(): pl.pallas_call(functools.partial(left_kernel, pair_count, len(EARLY if by...]
  transfers between devices with their start and end apart: 15 -> 15, of which waited for: 5 -> 4; matrix products, arithmetic and copies ran while one was open for 0% -> 0% of each run, Pallas kernels for 22% -> 21%
where the time goes in v18:
time: 27.3 us; the launch traced here: 27.1 us
  starting transfers between devices  14.1 us (52%)
  Pallas kernels  7.94 us (29%)
  waiting for transfers between devices  4.93 us (18%)
    ppermute x15, starting transfers between devices, swap(): lax.ppermute(piece, 'sec', [(i, i ^ (odd_bit if i & CORE else even_bit))...  14.1 us
    ppermute x15, waiting for transfers between devices, swap(): lax.ppermute(piece, 'sec', [(i, i ^ (odd_bit if i & CORE else even_bit))...  4.93 us
    pallas_call x1, Pallas kernels, per_device(): pl.pallas_call(functools.partial(left_kernel, pair_count, len(EARLY if by...  2.91 us
    pallas_call x1, Pallas kernels, per_device(): pl.pallas_call(early_kernel, out_shape=jax.ShapeDtypeStruct(psi.shape, jn...  1.62 us
    pallas_call x1, Pallas kernels, per_device(): pl.pallas_call(last_kernel, out_shape=jax.ShapeDtypeStruct(psi.shape, jnp...  1.23 us
    pallas_call x1, Pallas kernels, per_device(): pl.pallas_call(middle_kernel, out_shape=jax.ShapeDtypeStruct(psi.shape, j...  1.09 us
    pallas_call x1, Pallas kernels, per_device(): pl.pallas_call(pack_kernel, out_shape=jax.ShapeDtypeStruct((pair_count, t...  1.09 us
  transfers between devices with their start and end apart: 15, of which 4 were waited for; matrix products, arithmetic and copies ran while one was open for 0% of the time, Pallas kernels for 21%

profile of v18, /device:TPU:0, one launch (start us, length us, event | category | flops | bytes accessed | tf_op | source)
XLA Modules:
  0.0 27.1 jit_solution(13796094934098994932)
XLA Ops:
  0.0 1.1 %shard_map.83.refs_0_ = bf16[8,64,128]{2,1,0:T(8,128)(2,1)S(1)} custom-call(s32[16]{0:T(128)} %dims_hbm.3, bf16[16,64,64]{2,1,0:T(8,128)(2,1)} %right_hbm.1), custom_call_target="tpu_custom_call" | custom-call | bytes 131072 | tf_op jit(solution)/shard_map/pallas_call | solution.py:232
  1.1 0.5 %collective-permute-start = (bf16[8,64,128]{2,1,0:T(8,128)(2,1)S(1)}, bf16[8,64,128]{2,1,0:T(8,128)(2,1)S(1)}, u32[]{:S(2)}, u32[]{:S(2)}) collective-permute-start(bf16[8,64,128]{2,1,0:T(8,128)(2,1)S(1)} %shard_map.83.refs_0_), channel_id=1, source_target_pairs={{0,1},{1,0},{2,3},{3,2},{4,5},{5,4},{6,7},{7,6},{8,9},{9,8},{10,11... | collective-permute-start | bytes 393224 | tf_op jit(solution)/shard_map/ppermute | solution.py:212
  1.6 3.7 %collective-permute-start.3 = (bf16[8,64,128]{2,1,0:T(8,128)(2,1)S(1)}, bf16[8,64,128]{2,1,0:T(8,128)(2,1)S(1)}, u32[]{:S(2)}, u32[]{:S(2)}) collective-permute-start(bf16[8,64,128]{2,1,0:T(8,128)(2,1)S(1)} %shard_map.83.refs_0_), channel_id=1, source_target_pairs={{0,8},{1,5},{2,10},{3,7},{4,12},{5,1},{6,14},{7,3},{8,0},{9,13},{1... | collective-permute-start | bytes 393224 | tf_op jit(solution)/shard_map/ppermute | solution.py:212
  5.3 1.5 %collective-permute-start.6 = (bf16[8,64,128]{2,1,0:T(8,128)(2,1)S(1)}, bf16[8,64,128]{2,1,0:T(8,128)(2,1)S(1)}, u32[]{:S(2)}, u32[]{:S(2)}) collective-permute-start(bf16[8,64,128]{2,1,0:T(8,128)(2,1)S(1)} %shard_map.83.refs_0_), channel_id=1, source_target_pairs={{0,2},{1,3},{2,0},{3,1},{4,6},{5,7},{6,4},{7,5},{8,10},{9,11},{10,... | collective-permute-start | bytes 393224 | tf_op jit(solution)/shard_map/ppermute | solution.py:212
  6.8 0.0 collective-permute-done.refs_7_
  6.8 1.6 %collective-permute-start.1 = (bf16[8,64,128]{2,1,0:T(8,128)(2,1)S(1)}, bf16[8,64,128]{2,1,0:T(8,128)(2,1)S(1)}, u32[]{:S(2)}, u32[]{:S(2)}) collective-permute-start(bf16[8,64,128]{2,1,0:T(8,128)(2,1)S(1)} %shard_map.83.refs_0_), channel_id=1, source_target_pairs={{0,4},{1,9},{2,6},{3,11},{4,0},{5,13},{6,2},{7,15},{8,12},{9,1},{1... | collective-permute-start | bytes 393224 | tf_op jit(solution)/shard_map/ppermute | solution.py:212
  8.4 2.9 %shard_map.82 = (bf16[8,8,64,128]{3,2,1,0:T(8,128)(2,1)S(1)}, s32[202]{0:T(256)S(4)}) custom-call(s32[8]{0:T(128)} %dims_hbm.2, s32[8,8]{1,0:T(8,128)} %bitcast.1, s32[8,8]{1,0:T(8,128)} %owner_hbm.1, s32[8,8]{1,0:T(8,128)} %slot_hbm.1, bf16[8,64,64]{2,1,0:T(8,128)(2,1)} %left_hbm.1, bf16[8,8,64,128]{3,2,1,0:T(8,128)(2,1)} %psi_hbm.1), custom_call_target="tpu_custom_call" | custom-call | flops 67108864 | bytes 1048576 | tf_op jit(solution)/shard_map/pallas_call | solution.py:247
  11.3 0.0 collective-permute-done.3.refs_2_
  11.3 2.1 %collective-permute-start.4 = (bf16[8,64,128]{2,1,0:T(8,128)(2,1)S(1)}, bf16[8,64,128]{2,1,0:T(8,128)(2,1)S(1)}, u32[]{:S(2)}, u32[]{:S(2)}) collective-permute-start(bf16[8,64,128]{2,1,0:T(8,128)(2,1)S(1)} %collective-permute-done.3.refs_2_), channel_id=1, source_target_pairs={{0,4},{1,3},{2,6},{3,1},{4,0},{5,7},{6,2},{7,5},{8,12},{9,11},{10,... | collective-permute-start | bytes 393224 | tf_op jit(solution)/shard_map/ppermute | solution.py:212
  13.4 0.0 collective-permute-start.9
  13.4 0.0 collective-permute-done.6.refs_1_
  13.4 0.5 %collective-permute-start.8 = (bf16[8,64,128]{2,1,0:T(8,128)(2,1)S(1)}, bf16[8,64,128]{2,1,0:T(8,128)(2,1)S(1)}, u32[]{:S(2)}, u32[]{:S(2)}) collective-permute-start(bf16[8,64,128]{2,1,0:T(8,128)(2,1)S(1)} %collective-permute-done.6.refs_1_), channel_id=1, source_target_pairs={{0,1},{1,0},{2,3},{3,2},{4,5},{5,4},{6,7},{7,6},{8,9},{9,8},{10,11... | collective-permute-start | bytes 393224 | tf_op jit(solution)/shard_map/ppermute | solution.py:212
  13.9 0.0 collective-permute-done.1.refs_3_
  13.9 1.5 %collective-permute-start.2 = (bf16[8,64,128]{2,1,0:T(8,128)(2,1)S(1)}, bf16[8,64,128]{2,1,0:T(8,128)(2,1)S(1)}, u32[]{:S(2)}, u32[]{:S(2)}) collective-permute-start(bf16[8,64,128]{2,1,0:T(8,128)(2,1)S(1)} %collective-permute-done.1.refs_3_), channel_id=1, source_target_pairs={{0,2},{1,5},{2,0},{3,7},{4,6},{5,1},{6,4},{7,3},{8,10},{9,13},{10,... | collective-permute-start | bytes 393224 | tf_op jit(solution)/shard_map/ppermute | solution.py:212
  15.4 0.6 %collective-permute-start.7 = (bf16[8,64,128]{2,1,0:T(8,128)(2,1)S(1)}, bf16[8,64,128]{2,1,0:T(8,128)(2,1)S(1)}, u32[]{:S(2)}, u32[]{:S(2)}) collective-permute-start(bf16[8,64,128]{2,1,0:T(8,128)(2,1)S(1)} %broadcast_select_fusion), channel_id=1, source_target_pairs={{0,2},{1,3},{2,0},{3,1},{4,6},{5,7},{6,4},{7,5},{8,10},{9,11},{10,... | collective-permute-start | bytes 393224 | tf_op jit(solution)/shard_map/ppermute | solution.py:212
  16.0 1.2 %collective-permute-done.4.refs_4_ = bf16[8,64,128]{2,1,0:T(8,128)(2,1)S(1)} collective-permute-done((bf16[8,64,128]{2,1,0:T(8,128)(2,1)S(1)}, bf16[8,64,128]{2,1,0:T(8,128)(2,1)S(1)}, u32[]{:S(2)}, u32[]{:S(2)}) %collective-permute-start.4) | collective-permute-done | bytes 131104 | tf_op jit(solution)/shard_map/ppermute | solution.py:212
  17.2 0.0 collective-permute-start.10
  17.2 2.3 %collective-permute-done.2.refs_5_ = bf16[8,64,128]{2,1,0:T(8,128)(2,1)S(1)} collective-permute-done((bf16[8,64,128]{2,1,0:T(8,128)(2,1)S(1)}, bf16[8,64,128]{2,1,0:T(8,128)(2,1)S(1)}, u32[]{:S(2)}, u32[]{:S(2)}) %collective-permute-start.2) | collective-permute-done | bytes 131104 | tf_op jit(solution)/shard_map/ppermute | solution.py:212
  19.5 1.6 %collective-permute-start.5 = (bf16[8,64,128]{2,1,0:T(8,128)(2,1)S(1)}, bf16[8,64,128]{2,1,0:T(8,128)(2,1)S(1)}, u32[]{:S(2)}, u32[]{:S(2)}) collective-permute-start(bf16[8,64,128]{2,1,0:T(8,128)(2,1)S(1)} %broadcast_select_fusion.1), channel_id=1, source_target_pairs={{0,2},{1,3},{2,0},{3,1},{4,6},{5,7},{6,4},{7,5},{8,10},{9,11},{10,... | collective-permute-start | bytes 393224 | tf_op jit(solution)/shard_map/ppermute | solution.py:212
  21.1 0.0 collective-permute-done.9.refs_9_
  21.1 0.0 collective-permute-start.11
  21.1 0.0 collective-permute-done.8.refs_8_
  21.1 0.5 %collective-permute-start.12 = (bf16[8,64,128]{2,1,0:T(8,128)(2,1)S(1)}, bf16[8,64,128]{2,1,0:T(8,128)(2,1)S(1)}, u32[]{:S(2)}, u32[]{:S(2)}) collective-permute-start(bf16[8,64,128]{2,1,0:T(8,128)(2,1)S(1)} %collective-permute-done.2.refs_5_), channel_id=1, source_target_pairs={{0,1},{1,0},{2,3},{3,2},{4,5},{5,4},{6,7},{7,6},{8,9},{9,8},{10,11... | collective-permute-start | bytes 393224 | tf_op jit(solution)/shard_map/ppermute | solution.py:212
  21.6 0.0 collective-permute-done.7.refs_6_
  21.6 0.1 collective-permute-start.13
  21.7 0.0 collective-permute-done.10.refs_10_
  21.7 1.6 %shard_map.84.early_ref = bf16[8,8,64,128]{3,2,1,0:T(8,128)(2,1)S(1)} custom-call(s32[202]{0:T(256)S(4)} %get-tuple-element.13.list_ref, bf16[8,8,64,128]{3,2,1,0:T(8,128)(2,1)S(1)} %get-tuple-element.17.half_ref, bf16[8,64,128]{2,1,0:T(8,128)(2,1)S(1)} %shard_map.83.refs_0_, bf16[8,64,128]{2,1,0:T(8,128)(2,1)S(1)} %collective-permute-done.6.refs_1_, ...), custom_call_target="tpu_custom_call" | custom-call | flops 67108864 | bytes 1048576 | tf_op jit(solution)/shard_map/pallas_call | solution.py:302
  23.3 1.2 %collective-permute-done.5.refs_3_ = bf16[8,64,128]{2,1,0:T(8,128)(2,1)S(1)} collective-permute-done((bf16[8,64,128]{2,1,0:T(8,128)(2,1)S(1)}, bf16[8,64,128]{2,1,0:T(8,128)(2,1)S(1)}, u32[]{:S(2)}, u32[]{:S(2)}) %collective-permute-start.5) | collective-permute-done | bytes 131104 | tf_op jit(solution)/shard_map/ppermute | solution.py:212
  24.5 0.0 collective-permute-start.14
  24.5 0.0 collective-permute-done.11.refs_0_
  24.5 0.0 collective-permute-done.13.refs_2_
  24.5 0.0 collective-permute-done.12.refs_1_
  24.5 1.1 %shard_map.85.middle_ref = bf16[8,8,64,128]{3,2,1,0:T(8,128)(2,1)S(1)} custom-call(s32[202]{0:T(256)S(4)} %get-tuple-element.13.list_ref, bf16[8,8,64,128]{3,2,1,0:T(8,128)(2,1)S(1)} %shard_map.84.early_ref, bf16[8,8,64,128]{3,2,1,0:T(8,128)(2,1)S(1)} %get-tuple-element.17.half_ref, bf16[8,64,128]{2,1,0:T(8,128)(2,1)S(1)} %collective-permute-done.11.refs_0_, ...), custom_call_target="tpu_custom_call" | custom-call | flops 16777216 | bytes 262144 | tf_op jit(solution)/shard_map/pallas_call | solution.py:314
  25.6 0.2 collective-permute-done.14.pairs_ref
  25.9 1.2 %shard_map.86 = bf16[8,8,64,128]{3,2,1,0:T(8,128)(2,1)} custom-call(s32[202]{0:T(256)S(4)} %get-tuple-element.13.list_ref, bf16[8,8,64,128]{3,2,1,0:T(8,128)(2,1)S(1)} %shard_map.85.middle_ref, bf16[8,8,64,128]{3,2,1,0:T(8,128)(2,1)S(1)} %get-tuple-element.17.half_ref, bf16[8,64,128]{2,1,0:T(8,128)(2,1)S(1)} %collective-permute-done.14.pairs_ref), custom_call_target="tpu_custom_call" | custom-call | flops 4194304 | bytes 1048576 | tf_op jit(solution)/shard_map/pallas_call | solution.py:323
  (2 shorter events, 0.0 us)
Async XLA Ops:
  1.1 5.7 %collective-permute-start = (bf16[8,64,128]{2,1,0:T(8,128)(2,1)S(1)}, bf16[8,64,128]{2,1,0:T(8,128)(2,1)S(1)}, u32[]{:S(2)}, u32[]{:S(2)}) collective-permute-start(bf16[8,64,128]{2,1,0:T(8,128)(2,1)S(1)} %shard_map.83.refs_0_), channel_id=1, source_target_pairs={{0,1},{1,0},{2,3},{3,2},{4,5},{5,4},{6,7},{7,6},{8,9},{9,8},{10,11... | collective-permute-start | bytes 393224 | tf_op jit(solution)/shard_map/ppermute | solution.py:212
  1.6 9.7 %collective-permute-start.3 = (bf16[8,64,128]{2,1,0:T(8,128)(2,1)S(1)}, bf16[8,64,128]{2,1,0:T(8,128)(2,1)S(1)}, u32[]{:S(2)}, u32[]{:S(2)}) collective-permute-start(bf16[8,64,128]{2,1,0:T(8,128)(2,1)S(1)} %shard_map.83.refs_0_), channel_id=1, source_target_pairs={{0,8},{1,5},{2,10},{3,7},{4,12},{5,1},{6,14},{7,3},{8,0},{9,13},{1... | collective-permute-start | bytes 393224 | tf_op jit(solution)/shard_map/ppermute | solution.py:212
  5.3 8.1 %collective-permute-start.6 = (bf16[8,64,128]{2,1,0:T(8,128)(2,1)S(1)}, bf16[8,64,128]{2,1,0:T(8,128)(2,1)S(1)}, u32[]{:S(2)}, u32[]{:S(2)}) collective-permute-start(bf16[8,64,128]{2,1,0:T(8,128)(2,1)S(1)} %shard_map.83.refs_0_), channel_id=1, source_target_pairs={{0,2},{1,3},{2,0},{3,1},{4,6},{5,7},{6,4},{7,5},{8,10},{9,11},{10,... | collective-permute-start | bytes 393224 | tf_op jit(solution)/shard_map/ppermute | solution.py:212
  6.8 7.1 %collective-permute-start.1 = (bf16[8,64,128]{2,1,0:T(8,128)(2,1)S(1)}, bf16[8,64,128]{2,1,0:T(8,128)(2,1)S(1)}, u32[]{:S(2)}, u32[]{:S(2)}) collective-permute-start(bf16[8,64,128]{2,1,0:T(8,128)(2,1)S(1)} %shard_map.83.refs_0_), channel_id=1, source_target_pairs={{0,4},{1,9},{2,6},{3,11},{4,0},{5,13},{6,2},{7,15},{8,12},{9,1},{1... | collective-permute-start | bytes 393224 | tf_op jit(solution)/shard_map/ppermute | solution.py:212
  11.3 5.9 %collective-permute-start.4 = (bf16[8,64,128]{2,1,0:T(8,128)(2,1)S(1)}, bf16[8,64,128]{2,1,0:T(8,128)(2,1)S(1)}, u32[]{:S(2)}, u32[]{:S(2)}) collective-permute-start(bf16[8,64,128]{2,1,0:T(8,128)(2,1)S(1)} %collective-permute-done.3.refs_2_), channel_id=1, source_target_pairs={{0,4},{1,3},{2,6},{3,1},{4,0},{5,7},{6,2},{7,5},{8,12},{9,11},{10,... | collective-permute-start | bytes 393224 | tf_op jit(solution)/shard_map/ppermute | solution.py:212
  13.4 7.7 %collective-permute-start.9 = (bf16[8,64,128]{2,1,0:T(8,128)(2,1)S(1)}, bf16[8,64,128]{2,1,0:T(8,128)(2,1)S(1)}, u32[]{:S(2)}, u32[]{:S(2)}) collective-permute-start(bf16[8,64,128]{2,1,0:T(8,128)(2,1)S(1)} %collective-permute-done.3.refs_2_), channel_id=1, source_target_pairs={{0,1},{1,0},{2,3},{3,2},{4,5},{5,4},{6,7},{7,6},{8,9},{9,8},{10,11... | collective-permute-start | bytes 393224 | tf_op jit(solution)/shard_map/ppermute | solution.py:212
  13.4 7.7 %collective-permute-start.8 = (bf16[8,64,128]{2,1,0:T(8,128)(2,1)S(1)}, bf16[8,64,128]{2,1,0:T(8,128)(2,1)S(1)}, u32[]{:S(2)}, u32[]{:S(2)}) collective-permute-start(bf16[8,64,128]{2,1,0:T(8,128)(2,1)S(1)} %collective-permute-done.6.refs_1_), channel_id=1, source_target_pairs={{0,1},{1,0},{2,3},{3,2},{4,5},{5,4},{6,7},{7,6},{8,9},{9,8},{10,11... | collective-permute-start | bytes 393224 | tf_op jit(solution)/shard_map/ppermute | solution.py:212
  13.9 5.6 %collective-permute-start.2 = (bf16[8,64,128]{2,1,0:T(8,128)(2,1)S(1)}, bf16[8,64,128]{2,1,0:T(8,128)(2,1)S(1)}, u32[]{:S(2)}, u32[]{:S(2)}) collective-permute-start(bf16[8,64,128]{2,1,0:T(8,128)(2,1)S(1)} %collective-permute-done.1.refs_3_), channel_id=1, source_target_pairs={{0,2},{1,5},{2,0},{3,7},{4,6},{5,1},{6,4},{7,3},{8,10},{9,13},{10,... | collective-permute-start | bytes 393224 | tf_op jit(solution)/shard_map/ppermute | solution.py:212
  15.4 6.2 %collective-permute-start.7 = (bf16[8,64,128]{2,1,0:T(8,128)(2,1)S(1)}, bf16[8,64,128]{2,1,0:T(8,128)(2,1)S(1)}, u32[]{:S(2)}, u32[]{:S(2)}) collective-permute-start(bf16[8,64,128]{2,1,0:T(8,128)(2,1)S(1)} %broadcast_select_fusion), channel_id=1, source_target_pairs={{0,2},{1,3},{2,0},{3,1},{4,6},{5,7},{6,4},{7,5},{8,10},{9,11},{10,... | collective-permute-start | bytes 393224 | tf_op jit(solution)/shard_map/ppermute | solution.py:212
  17.2 4.5 %collective-permute-start.10 = (bf16[8,64,128]{2,1,0:T(8,128)(2,1)S(1)}, bf16[8,64,128]{2,1,0:T(8,128)(2,1)S(1)}, u32[]{:S(2)}, u32[]{:S(2)}) collective-permute-start(bf16[8,64,128]{2,1,0:T(8,128)(2,1)S(1)} %collective-permute-done.1.refs_3_), channel_id=1, source_target_pairs={{0,1},{1,0},{2,3},{3,2},{4,5},{5,4},{6,7},{7,6},{8,9},{9,8},{10,11... | collective-permute-start | bytes 393224 | tf_op jit(solution)/shard_map/ppermute | solution.py:212
  19.5 5.0 %collective-permute-start.5 = (bf16[8,64,128]{2,1,0:T(8,128)(2,1)S(1)}, bf16[8,64,128]{2,1,0:T(8,128)(2,1)S(1)}, u32[]{:S(2)}, u32[]{:S(2)}) collective-permute-start(bf16[8,64,128]{2,1,0:T(8,128)(2,1)S(1)} %broadcast_select_fusion.1), channel_id=1, source_target_pairs={{0,2},{1,3},{2,0},{3,1},{4,6},{5,7},{6,4},{7,5},{8,10},{9,11},{10,... | collective-permute-start | bytes 393224 | tf_op jit(solution)/shard_map/ppermute | solution.py:212
  21.1 3.4 %collective-permute-start.11 = (bf16[8,64,128]{2,1,0:T(8,128)(2,1)S(1)}, bf16[8,64,128]{2,1,0:T(8,128)(2,1)S(1)}, u32[]{:S(2)}, u32[]{:S(2)}) collective-permute-start(bf16[8,64,128]{2,1,0:T(8,128)(2,1)S(1)} %collective-permute-done.4.refs_4_), channel_id=1, source_target_pairs={{0,1},{1,0},{2,3},{3,2},{4,5},{5,4},{6,7},{7,6},{8,9},{9,8},{10,11... | collective-permute-start | bytes 393224 | tf_op jit(solution)/shard_map/ppermute | solution.py:212
  21.1 3.4 %collective-permute-start.12 = (bf16[8,64,128]{2,1,0:T(8,128)(2,1)S(1)}, bf16[8,64,128]{2,1,0:T(8,128)(2,1)S(1)}, u32[]{:S(2)}, u32[]{:S(2)}) collective-permute-start(bf16[8,64,128]{2,1,0:T(8,128)(2,1)S(1)} %collective-permute-done.2.refs_5_), channel_id=1, source_target_pairs={{0,1},{1,0},{2,3},{3,2},{4,5},{5,4},{6,7},{7,6},{8,9},{9,8},{10,11... | collective-permute-start | bytes 393224 | tf_op jit(solution)/shard_map/ppermute | solution.py:212
  21.6 2.9 %collective-permute-start.13 = (bf16[8,64,128]{2,1,0:T(8,128)(2,1)S(1)}, bf16[8,64,128]{2,1,0:T(8,128)(2,1)S(1)}, u32[]{:S(2)}, u32[]{:S(2)}) collective-permute-start(bf16[8,64,128]{2,1,0:T(8,128)(2,1)S(1)} %collective-permute-done.7.refs_6_), channel_id=1, source_target_pairs={{0,1},{1,0},{2,3},{3,2},{4,5},{5,4},{6,7},{7,6},{8,9},{9,8},{10,11... | collective-permute-start | bytes 393224 | tf_op jit(solution)/shard_map/ppermute | solution.py:212
  24.5 1.3 %collective-permute-start.14 = (bf16[8,64,128]{2,1,0:T(8,128)(2,1)S(1)}, bf16[8,64,128]{2,1,0:T(8,128)(2,1)S(1)}, u32[]{:S(2)}, u32[]{:S(2)}) collective-permute-start(bf16[8,64,128]{2,1,0:T(8,128)(2,1)S(1)} %collective-permute-done.5.refs_3_), channel_id=1, source_target_pairs={{0,1},{1,0},{2,3},{3,2},{4,5},{5,4},{6,7},{7,6},{8,9},{9,8},{10,11... | collective-permute-start | bytes 393224 | tf_op jit(solution)/shard_map/ppermute | solution.py:212

commit v19 on v18

--- a/solution.py
+++ b/solution.py
@@ -9,18 +9,17 @@
 
 VMEM_LIMIT = 48 * 1024 * 1024
 FAR, NEAR, CROSS, CORE = 8, 4, 2, 1
-OWN, SIDE = (0, 0), (CROSS, CROSS)
-FIRST, SECOND = (FAR, NEAR), (NEAR, FAR)
-THIRD, FOURTH = (FAR | NEAR, NEAR | CROSS), (NEAR | CROSS, FAR | NEAR)
-FAR_SIDE, END = (FAR | CROSS, FAR | CROSS), (FAR | NEAR | CROSS, FAR | NEAR | CROSS)
+OWN, SIDE, BESIDE, BEYOND, CORNER = (0, 0), (CROSS, CROSS), (NEAR, NEAR), (FAR, FAR), (NEAR | CROSS, NEAR | CROSS)
+FIRST, SECOND = (FAR | NEAR, FAR | CROSS), (FAR | CROSS, FAR | NEAR)
+END = (FAR | NEAR | CROSS, FAR | NEAR | CROSS)
 
 
 def partner(name):
     return name[1] | CORE, name[0] | CORE
 
 
-EARLY = (OWN, SIDE, FIRST, SECOND, THIRD, FOURTH, FAR_SIDE, partner(OWN), partner(SIDE), partner(FIRST), partner(SECOND))
-MIDDLE = (partner(THIRD), partner(FOURTH), partner(FAR_SIDE), END)
+EARLY = (OWN, SIDE, BESIDE, BEYOND, CORNER, FIRST, SECOND, partner(OWN), partner(SIDE), partner(BESIDE), partner(CORNER))
+MIDDLE = (partner(BEYOND), partner(FIRST), partner(SECOND), END)
 LAST = (partner(END),)
 ORDER = EARLY + MIDDLE + LAST
 
@@ -269,7 +268,6 @@
 
     if by_swaps:
         pieces = {OWN: pairs}
-        odd = lax.axis_index("sec") & CORE == 1
 
         def pass_on(*routes):
             for name, target in routes:
@@ -279,22 +277,12 @@
             for name in names:
                 pieces[partner(name)] = swap(pieces[name], CORE, CORE)
 
-        def cross(even_name, odd_name, target):
-            pieces[target] = swap(jnp.where(odd, pieces[odd_name], pieces[even_name]), CROSS, CROSS)
-
-        pass_on((OWN, FIRST), (OWN, SIDE))
-        share(OWN)
-        held = (partner(OWN),)
-        pieces[OWN], ends = lax.optimization_barrier((pieces[OWN], [pieces[r] for r in held]))
+        pass_on((OWN, BEYOND), (OWN, BESIDE), (OWN, SIDE))
+        held = (OWN, BESIDE,)
+        half, ends = lax.optimization_barrier((half, [pieces[name] for name in held]))
         pieces.update(zip(held, ends))
-        pass_on((OWN, SECOND), )
-        held = (FIRST,)
-        half, ends = lax.optimization_barrier((half, [pieces[r] for r in held]))
-        pieces.update(zip(held, ends))
-        pass_on((FIRST, THIRD), (SECOND, FOURTH))
-        cross(FIRST, SECOND, FAR_SIDE)
-        cross(THIRD, FOURTH, END)
-        share(SIDE, FIRST, SECOND, THIRD, FOURTH, FAR_SIDE)
+        pass_on((BESIDE, CORNER), (BEYOND, FIRST), (BEYOND, SECOND), (FIRST, END))
+        share(OWN, BESIDE, SIDE, CORNER, BEYOND, FIRST, SECOND)
         early = [pieces[name] for name in EARLY]
     else:
         early = [lax.all_gather(pairs, "sec", axis=0, tiled=True)]

time: 27.3 us -> 26.9 us (0.985)
  starting transfers between devices: 14.1 us -> 12.3 us
  waiting for transfers between devices: 4.93 us -> 6.57 us
    ppermute x15, starting transfers between devices: 14.1 us -> 12.3 us  [swap(): lax.ppermute(piece, 'sec', [(i, i ^ (odd_bit if i & CORE else even_bit))...]
    ppermute x15, waiting for transfers between devices: 4.93 us -> 6.57 us  [swap(): lax.ppermute(piece, 'sec', [(i, i ^ (odd_bit if i & CORE else even_bit))...]
  transfers between devices with their start and end apart: 15 -> 15, of which waited for: 4 -> 5; matrix products, arithmetic and copies ran while one was open for 0% -> 0% of each run, Pallas kernels for 21% -> 21%
where the time goes in v19:
time: 26.9 us; the launch traced here: 26.7 us
  starting transfers between devices  12.3 us (46%)
  Pallas kernels  7.78 us (29%)
  waiting for transfers between devices  6.57 us (24%)
    ppermute x15, starting transfers between devices, swap(): lax.ppermute(piece, 'sec', [(i, i ^ (odd_bit if i & CORE else even_bit))...  12.3 us
    ppermute x15, waiting for transfers between devices, swap(): lax.ppermute(piece, 'sec', [(i, i ^ (odd_bit if i & CORE else even_bit))...  6.57 us
    pallas_call x1, Pallas kernels, per_device(): pl.pallas_call(functools.partial(left_kernel, pair_count, len(EARLY if by...  2.85 us
    pallas_call x1, Pallas kernels, per_device(): pl.pallas_call(early_kernel, out_shape=jax.ShapeDtypeStruct(psi.shape, jn...  1.62 us
    pallas_call x1, Pallas kernels, per_device(): pl.pallas_call(last_kernel, out_shape=jax.ShapeDtypeStruct(psi.shape, jnp...  1.13 us
    pallas_call x1, Pallas kernels, per_device(): pl.pallas_call(middle_kernel, out_shape=jax.ShapeDtypeStruct(psi.shape, j...  1.09 us
    pallas_call x1, Pallas kernels, per_device(): pl.pallas_call(pack_kernel, out_shape=jax.ShapeDtypeStruct((pair_count, t...  1.09 us
  transfers between devices with their start and end apart: 15, of which 5 were waited for; matrix products, arithmetic and copies ran while one was open for 0% of the time, Pallas kernels for 21%

profile of v19, /device:TPU:0, one launch (start us, length us, event | category | flops | bytes accessed | tf_op | source)
XLA Modules:
  0.0 26.7 jit_solution(14936026187665573700)
XLA Ops:
  0.0 1.1 %shard_map.83.refs_0_ = bf16[8,64,128]{2,1,0:T(8,128)(2,1)S(1)} custom-call(s32[16]{0:T(128)} %dims_hbm.3, bf16[16,64,64]{2,1,0:T(8,128)(2,1)} %right_hbm.1), custom_call_target="tpu_custom_call" | custom-call | bytes 131072 | tf_op jit(solution)/shard_map/pallas_call | solution.py:231
  1.1 3.1 %collective-permute-start.3 = (bf16[8,64,128]{2,1,0:T(8,128)(2,1)S(1)}, bf16[8,64,128]{2,1,0:T(8,128)(2,1)S(1)}, u32[]{:S(2)}, u32[]{:S(2)}) collective-permute-start(bf16[8,64,128]{2,1,0:T(8,128)(2,1)S(1)} %shard_map.83.refs_0_), channel_id=1, source_target_pairs={{0,4},{1,5},{2,6},{3,7},{4,0},{5,1},{6,2},{7,3},{8,12},{9,13},{10,... | collective-permute-start | bytes 393224 | tf_op jit(solution)/shard_map/ppermute | solution.py:211
  4.2 2.6 %collective-permute-start = (bf16[8,64,128]{2,1,0:T(8,128)(2,1)S(1)}, bf16[8,64,128]{2,1,0:T(8,128)(2,1)S(1)}, u32[]{:S(2)}, u32[]{:S(2)}) collective-permute-start(bf16[8,64,128]{2,1,0:T(8,128)(2,1)S(1)} %shard_map.83.refs_0_), channel_id=1, source_target_pairs={{0,8},{1,9},{2,10},{3,11},{4,12},{5,13},{6,14},{7,15},{8,0},{9,1},... | collective-permute-start | bytes 393224 | tf_op jit(solution)/shard_map/ppermute | solution.py:211
  6.8 1.5 %collective-permute-start.4 = (bf16[8,64,128]{2,1,0:T(8,128)(2,1)S(1)}, bf16[8,64,128]{2,1,0:T(8,128)(2,1)S(1)}, u32[]{:S(2)}, u32[]{:S(2)}) collective-permute-start(bf16[8,64,128]{2,1,0:T(8,128)(2,1)S(1)} %shard_map.83.refs_0_), channel_id=1, source_target_pairs={{0,2},{1,3},{2,0},{3,1},{4,6},{5,7},{6,4},{7,5},{8,10},{9,11},{10,... | collective-permute-start | bytes 393224 | tf_op jit(solution)/shard_map/ppermute | solution.py:211
  8.3 2.9 %shard_map.82 = (bf16[8,8,64,128]{3,2,1,0:T(8,128)(2,1)S(1)}, s32[202]{0:T(256)S(4)}) custom-call(s32[8]{0:T(128)} %dims_hbm.2, s32[8,8]{1,0:T(8,128)} %bitcast.1, s32[8,8]{1,0:T(8,128)} %owner_hbm.1, s32[8,8]{1,0:T(8,128)} %slot_hbm.1, bf16[8,64,64]{2,1,0:T(8,128)(2,1)} %left_hbm.1, bf16[8,8,64,128]{3,2,1,0:T(8,128)(2,1)} %psi_hbm.1), custom_call_target="tpu_custom_call" | custom-call | flops 67108864 | bytes 1048576 | tf_op jit(solution)/shard_map/pallas_call | solution.py:246
  11.1 0.0 collective-permute-done.3.refs_2_
  11.1 0.6 %collective-permute-start.5 = (bf16[8,64,128]{2,1,0:T(8,128)(2,1)S(1)}, bf16[8,64,128]{2,1,0:T(8,128)(2,1)S(1)}, u32[]{:S(2)}, u32[]{:S(2)}) collective-permute-start(bf16[8,64,128]{2,1,0:T(8,128)(2,1)S(1)} %collective-permute-done.3.refs_2_), channel_id=1, source_target_pairs={{0,2},{1,3},{2,0},{3,1},{4,6},{5,7},{6,4},{7,5},{8,10},{9,11},{10,... | collective-permute-start | bytes 393224 | tf_op jit(solution)/shard_map/ppermute | solution.py:211
  11.7 0.0 collective-permute-start.9
  11.7 1.2 %collective-permute-done.refs_3_ = bf16[8,64,128]{2,1,0:T(8,128)(2,1)S(1)} collective-permute-done((bf16[8,64,128]{2,1,0:T(8,128)(2,1)S(1)}, bf16[8,64,128]{2,1,0:T(8,128)(2,1)S(1)}, u32[]{:S(2)}, u32[]{:S(2)}) %collective-permute-start) | collective-permute-done | bytes 131104 | tf_op jit(solution)/shard_map/ppermute | solution.py:211
  12.9 0.4 %collective-permute-start.1 = (bf16[8,64,128]{2,1,0:T(8,128)(2,1)S(1)}, bf16[8,64,128]{2,1,0:T(8,128)(2,1)S(1)}, u32[]{:S(2)}, u32[]{:S(2)}) collective-permute-start(bf16[8,64,128]{2,1,0:T(8,128)(2,1)S(1)} %collective-permute-done.refs_3_), channel_id=1, source_target_pairs={{0,4},{1,3},{2,6},{3,1},{4,0},{5,7},{6,2},{7,5},{8,12},{9,11},{10,... | collective-permute-start | bytes 393224 | tf_op jit(solution)/shard_map/ppermute | solution.py:211
  13.4 0.1 collective-permute-start.7
  13.5 0.0 collective-permute-done.4.refs_1_
  13.5 1.4 %collective-permute-start.6 = (bf16[8,64,128]{2,1,0:T(8,128)(2,1)S(1)}, bf16[8,64,128]{2,1,0:T(8,128)(2,1)S(1)}, u32[]{:S(2)}, u32[]{:S(2)}) collective-permute-start(bf16[8,64,128]{2,1,0:T(8,128)(2,1)S(1)} %collective-permute-done.refs_3_), channel_id=1, source_target_pairs={{0,2},{1,5},{2,0},{3,7},{4,6},{5,1},{6,4},{7,3},{8,10},{9,13},{10,... | collective-permute-start | bytes 393224 | tf_op jit(solution)/shard_map/ppermute | solution.py:211
  14.9 2.7 %collective-permute-done.5.refs_4_ = bf16[8,64,128]{2,1,0:T(8,128)(2,1)S(1)} collective-permute-done((bf16[8,64,128]{2,1,0:T(8,128)(2,1)S(1)}, bf16[8,64,128]{2,1,0:T(8,128)(2,1)S(1)}, u32[]{:S(2)}, u32[]{:S(2)}) %collective-permute-start.5) | collective-permute-done | bytes 131104 | tf_op jit(solution)/shard_map/ppermute | solution.py:211
  17.5 0.0 collective-permute-start.8
  17.5 0.0 collective-permute-done.9.refs_9_
  17.5 0.5 %collective-permute-start.10 = (bf16[8,64,128]{2,1,0:T(8,128)(2,1)S(1)}, bf16[8,64,128]{2,1,0:T(8,128)(2,1)S(1)}, u32[]{:S(2)}, u32[]{:S(2)}) collective-permute-start(bf16[8,64,128]{2,1,0:T(8,128)(2,1)S(1)} %collective-permute-done.5.refs_4_), channel_id=1, source_target_pairs={{0,1},{1,0},{2,3},{3,2},{4,5},{5,4},{6,7},{7,6},{8,9},{9,8},{10,11... | collective-permute-start | bytes 393224 | tf_op jit(solution)/shard_map/ppermute | solution.py:211
  18.0 1.3 %collective-permute-done.1.refs_5_ = bf16[8,64,128]{2,1,0:T(8,128)(2,1)S(1)} collective-permute-done((bf16[8,64,128]{2,1,0:T(8,128)(2,1)S(1)}, bf16[8,64,128]{2,1,0:T(8,128)(2,1)S(1)}, u32[]{:S(2)}, u32[]{:S(2)}) %collective-permute-start.1) | collective-permute-done | bytes 131104 | tf_op jit(solution)/shard_map/ppermute | solution.py:211
  19.3 1.5 %collective-permute-start.2 = (bf16[8,64,128]{2,1,0:T(8,128)(2,1)S(1)}, bf16[8,64,128]{2,1,0:T(8,128)(2,1)S(1)}, u32[]{:S(2)}, u32[]{:S(2)}) collective-permute-start(bf16[8,64,128]{2,1,0:T(8,128)(2,1)S(1)} %collective-permute-done.1.refs_5_), channel_id=1, source_target_pairs={{0,2},{1,5},{2,0},{3,7},{4,6},{5,1},{6,4},{7,3},{8,10},{9,13},{10,... | collective-permute-start | bytes 393224 | tf_op jit(solution)/shard_map/ppermute | solution.py:211
  20.8 0.0 collective-permute-done.7.refs_7_
  20.8 0.0 collective-permute-start.11
  20.8 0.0 collective-permute-done.6.refs_6_
  20.8 0.5 %collective-permute-start.12 = (bf16[8,64,128]{2,1,0:T(8,128)(2,1)S(1)}, bf16[8,64,128]{2,1,0:T(8,128)(2,1)S(1)}, u32[]{:S(2)}, u32[]{:S(2)}) collective-permute-start(bf16[8,64,128]{2,1,0:T(8,128)(2,1)S(1)} %collective-permute-done.1.refs_5_), channel_id=1, source_target_pairs={{0,1},{1,0},{2,3},{3,2},{4,5},{5,4},{6,7},{7,6},{8,9},{9,8},{10,11... | collective-permute-start | bytes 393224 | tf_op jit(solution)/shard_map/ppermute | solution.py:211
  21.3 0.0 collective-permute-done.8.refs_8_
  21.3 0.1 collective-permute-start.13
  21.4 0.0 collective-permute-done.10.refs_10_
  21.4 1.6 %shard_map.84.early_ref = bf16[8,8,64,128]{3,2,1,0:T(8,128)(2,1)S(1)} custom-call(s32[202]{0:T(256)S(4)} %get-tuple-element.12.list_ref, bf16[8,8,64,128]{3,2,1,0:T(8,128)(2,1)S(1)} %get-tuple-element.14.half_ref, bf16[8,64,128]{2,1,0:T(8,128)(2,1)S(1)} %shard_map.83.refs_0_, bf16[8,64,128]{2,1,0:T(8,128)(2,1)S(1)} %collective-permute-done.4.refs_1_, ...), custom_call_target="tpu_custom_call" | custom-call | flops 67108864 | bytes 1048576 | tf_op jit(solution)/shard_map/pallas_call | solution.py:290
  23.0 1.3 %collective-permute-done.2.refs_3_ = bf16[8,64,128]{2,1,0:T(8,128)(2,1)S(1)} collective-permute-done((bf16[8,64,128]{2,1,0:T(8,128)(2,1)S(1)}, bf16[8,64,128]{2,1,0:T(8,128)(2,1)S(1)}, u32[]{:S(2)}, u32[]{:S(2)}) %collective-permute-start.2) | collective-permute-done | bytes 131104 | tf_op jit(solution)/shard_map/ppermute | solution.py:211
  24.2 0.0 collective-permute-start.14
  24.2 0.0 collective-permute-done.11.refs_0_
  24.2 0.0 collective-permute-done.12.refs_1_
  24.3 0.0 collective-permute-done.13.refs_2_
  24.3 1.1 %shard_map.85.middle_ref = bf16[8,8,64,128]{3,2,1,0:T(8,128)(2,1)S(1)} custom-call(s32[202]{0:T(256)S(4)} %get-tuple-element.12.list_ref, bf16[8,8,64,128]{3,2,1,0:T(8,128)(2,1)S(1)} %shard_map.84.early_ref, bf16[8,8,64,128]{3,2,1,0:T(8,128)(2,1)S(1)} %get-tuple-element.14.half_ref, bf16[8,64,128]{2,1,0:T(8,128)(2,1)S(1)} %collective-permute-done.11.refs_0_, ...), custom_call_target="tpu_custom_call" | custom-call | flops 16777216 | bytes 262144 | tf_op jit(solution)/shard_map/pallas_call | solution.py:302
  25.4 0.2 collective-permute-done.14.pairs_ref
  25.6 1.1 %shard_map.86 = bf16[8,8,64,128]{3,2,1,0:T(8,128)(2,1)} custom-call(s32[202]{0:T(256)S(4)} %get-tuple-element.12.list_ref, bf16[8,8,64,128]{3,2,1,0:T(8,128)(2,1)S(1)} %shard_map.85.middle_ref, bf16[8,8,64,128]{3,2,1,0:T(8,128)(2,1)S(1)} %get-tuple-element.14.half_ref, bf16[8,64,128]{2,1,0:T(8,128)(2,1)S(1)} %collective-permute-done.14.pairs_ref), custom_call_target="tpu_custom_call" | custom-call | flops 4194304 | bytes 1048576 | tf_op jit(solution)/shard_map/pallas_call | solution.py:311
Async XLA Ops:
  1.1 10.0 %collective-permute-start.3 = (bf16[8,64,128]{2,1,0:T(8,128)(2,1)S(1)}, bf16[8,64,128]{2,1,0:T(8,128)(2,1)S(1)}, u32[]{:S(2)}, u32[]{:S(2)}) collective-permute-start(bf16[8,64,128]{2,1,0:T(8,128)(2,1)S(1)} %shard_map.83.refs_0_), channel_id=1, source_target_pairs={{0,4},{1,5},{2,6},{3,7},{4,0},{5,1},{6,2},{7,3},{8,12},{9,13},{10,... | collective-permute-start | bytes 393224 | tf_op jit(solution)/shard_map/ppermute | solution.py:211
  4.2 8.7 %collective-permute-start = (bf16[8,64,128]{2,1,0:T(8,128)(2,1)S(1)}, bf16[8,64,128]{2,1,0:T(8,128)(2,1)S(1)}, u32[]{:S(2)}, u32[]{:S(2)}) collective-permute-start(bf16[8,64,128]{2,1,0:T(8,128)(2,1)S(1)} %shard_map.83.refs_0_), channel_id=1, source_target_pairs={{0,8},{1,9},{2,10},{3,11},{4,12},{5,13},{6,14},{7,15},{8,0},{9,1},... | collective-permute-start | bytes 393224 | tf_op jit(solution)/shard_map/ppermute | solution.py:211
  6.8 6.7 %collective-permute-start.4 = (bf16[8,64,128]{2,1,0:T(8,128)(2,1)S(1)}, bf16[8,64,128]{2,1,0:T(8,128)(2,1)S(1)}, u32[]{:S(2)}, u32[]{:S(2)}) collective-permute-start(bf16[8,64,128]{2,1,0:T(8,128)(2,1)S(1)} %shard_map.83.refs_0_), channel_id=1, source_target_pairs={{0,2},{1,3},{2,0},{3,1},{4,6},{5,7},{6,4},{7,5},{8,10},{9,11},{10,... | collective-permute-start | bytes 393224 | tf_op jit(solution)/shard_map/ppermute | solution.py:211
  11.1 6.4 %collective-permute-start.5 = (bf16[8,64,128]{2,1,0:T(8,128)(2,1)S(1)}, bf16[8,64,128]{2,1,0:T(8,128)(2,1)S(1)}, u32[]{:S(2)}, u32[]{:S(2)}) collective-permute-start(bf16[8,64,128]{2,1,0:T(8,128)(2,1)S(1)} %collective-permute-done.3.refs_2_), channel_id=1, source_target_pairs={{0,2},{1,3},{2,0},{3,1},{4,6},{5,7},{6,4},{7,5},{8,10},{9,11},{10,... | collective-permute-start | bytes 393224 | tf_op jit(solution)/shard_map/ppermute | solution.py:211
  11.7 5.8 %collective-permute-start.9 = (bf16[8,64,128]{2,1,0:T(8,128)(2,1)S(1)}, bf16[8,64,128]{2,1,0:T(8,128)(2,1)S(1)}, u32[]{:S(2)}, u32[]{:S(2)}) collective-permute-start(bf16[8,64,128]{2,1,0:T(8,128)(2,1)S(1)} %collective-permute-done.3.refs_2_), channel_id=1, source_target_pairs={{0,1},{1,0},{2,3},{3,2},{4,5},{5,4},{6,7},{7,6},{8,9},{9,8},{10,11... | collective-permute-start | bytes 393224 | tf_op jit(solution)/shard_map/ppermute | solution.py:211
  12.9 6.4 %collective-permute-start.1 = (bf16[8,64,128]{2,1,0:T(8,128)(2,1)S(1)}, bf16[8,64,128]{2,1,0:T(8,128)(2,1)S(1)}, u32[]{:S(2)}, u32[]{:S(2)}) collective-permute-start(bf16[8,64,128]{2,1,0:T(8,128)(2,1)S(1)} %collective-permute-done.refs_3_), channel_id=1, source_target_pairs={{0,4},{1,3},{2,6},{3,1},{4,0},{5,7},{6,2},{7,5},{8,12},{9,11},{10,... | collective-permute-start | bytes 393224 | tf_op jit(solution)/shard_map/ppermute | solution.py:211
  13.4 7.4 %collective-permute-start.7 = (bf16[8,64,128]{2,1,0:T(8,128)(2,1)S(1)}, bf16[8,64,128]{2,1,0:T(8,128)(2,1)S(1)}, u32[]{:S(2)}, u32[]{:S(2)}) collective-permute-start(bf16[8,64,128]{2,1,0:T(8,128)(2,1)S(1)} %shard_map.83.refs_0_), channel_id=1, source_target_pairs={{0,1},{1,0},{2,3},{3,2},{4,5},{5,4},{6,7},{7,6},{8,9},{9,8},{10,11... | collective-permute-start | bytes 393224 | tf_op jit(solution)/shard_map/ppermute | solution.py:211
  13.5 7.3 %collective-permute-start.6 = (bf16[8,64,128]{2,1,0:T(8,128)(2,1)S(1)}, bf16[8,64,128]{2,1,0:T(8,128)(2,1)S(1)}, u32[]{:S(2)}, u32[]{:S(2)}) collective-permute-start(bf16[8,64,128]{2,1,0:T(8,128)(2,1)S(1)} %collective-permute-done.refs_3_), channel_id=1, source_target_pairs={{0,2},{1,5},{2,0},{3,7},{4,6},{5,1},{6,4},{7,3},{8,10},{9,13},{10,... | collective-permute-start | bytes 393224 | tf_op jit(solution)/shard_map/ppermute | solution.py:211
  17.5 3.8 %collective-permute-start.8 = (bf16[8,64,128]{2,1,0:T(8,128)(2,1)S(1)}, bf16[8,64,128]{2,1,0:T(8,128)(2,1)S(1)}, u32[]{:S(2)}, u32[]{:S(2)}) collective-permute-start(bf16[8,64,128]{2,1,0:T(8,128)(2,1)S(1)} %collective-permute-done.4.refs_1_), channel_id=1, source_target_pairs={{0,1},{1,0},{2,3},{3,2},{4,5},{5,4},{6,7},{7,6},{8,9},{9,8},{10,11... | collective-permute-start | bytes 393224 | tf_op jit(solution)/shard_map/ppermute | solution.py:211
  17.5 3.8 %collective-permute-start.10 = (bf16[8,64,128]{2,1,0:T(8,128)(2,1)S(1)}, bf16[8,64,128]{2,1,0:T(8,128)(2,1)S(1)}, u32[]{:S(2)}, u32[]{:S(2)}) collective-permute-start(bf16[8,64,128]{2,1,0:T(8,128)(2,1)S(1)} %collective-permute-done.5.refs_4_), channel_id=1, source_target_pairs={{0,1},{1,0},{2,3},{3,2},{4,5},{5,4},{6,7},{7,6},{8,9},{9,8},{10,11... | collective-permute-start | bytes 393224 | tf_op jit(solution)/shard_map/ppermute | solution.py:211
  19.3 5.0 %collective-permute-start.2 = (bf16[8,64,128]{2,1,0:T(8,128)(2,1)S(1)}, bf16[8,64,128]{2,1,0:T(8,128)(2,1)S(1)}, u32[]{:S(2)}, u32[]{:S(2)}) collective-permute-start(bf16[8,64,128]{2,1,0:T(8,128)(2,1)S(1)} %collective-permute-done.1.refs_5_), channel_id=1, source_target_pairs={{0,2},{1,5},{2,0},{3,7},{4,6},{5,1},{6,4},{7,3},{8,10},{9,13},{10,... | collective-permute-start | bytes 393224 | tf_op jit(solution)/shard_map/ppermute | solution.py:211
  20.8 3.5 %collective-permute-start.11 = (bf16[8,64,128]{2,1,0:T(8,128)(2,1)S(1)}, bf16[8,64,128]{2,1,0:T(8,128)(2,1)S(1)}, u32[]{:S(2)}, u32[]{:S(2)}) collective-permute-start(bf16[8,64,128]{2,1,0:T(8,128)(2,1)S(1)} %collective-permute-done.refs_3_), channel_id=1, source_target_pairs={{0,1},{1,0},{2,3},{3,2},{4,5},{5,4},{6,7},{7,6},{8,9},{9,8},{10,11... | collective-permute-start | bytes 393224 | tf_op jit(solution)/shard_map/ppermute | solution.py:211
  20.8 3.5 %collective-permute-start.12 = (bf16[8,64,128]{2,1,0:T(8,128)(2,1)S(1)}, bf16[8,64,128]{2,1,0:T(8,128)(2,1)S(1)}, u32[]{:S(2)}, u32[]{:S(2)}) collective-permute-start(bf16[8,64,128]{2,1,0:T(8,128)(2,1)S(1)} %collective-permute-done.1.refs_5_), channel_id=1, source_target_pairs={{0,1},{1,0},{2,3},{3,2},{4,5},{5,4},{6,7},{7,6},{8,9},{9,8},{10,11... | collective-permute-start | bytes 393224 | tf_op jit(solution)/shard_map/ppermute | solution.py:211
  21.3 3.0 %collective-permute-start.13 = (bf16[8,64,128]{2,1,0:T(8,128)(2,1)S(1)}, bf16[8,64,128]{2,1,0:T(8,128)(2,1)S(1)}, u32[]{:S(2)}, u32[]{:S(2)}) collective-permute-start(bf16[8,64,128]{2,1,0:T(8,128)(2,1)S(1)} %collective-permute-done.6.refs_6_), channel_id=1, source_target_pairs={{0,1},{1,0},{2,3},{3,2},{4,5},{5,4},{6,7},{7,6},{8,9},{9,8},{10,11... | collective-permute-start | bytes 393224 | tf_op jit(solution)/shard_map/ppermute | solution.py:211
  24.2 1.3 %collective-permute-start.14 = (bf16[8,64,128]{2,1,0:T(8,128)(2,1)S(1)}, bf16[8,64,128]{2,1,0:T(8,128)(2,1)S(1)}, u32[]{:S(2)}, u32[]{:S(2)}) collective-permute-start(bf16[8,64,128]{2,1,0:T(8,128)(2,1)S(1)} %collective-permute-done.2.refs_3_), channel_id=1, source_target_pairs={{0,1},{1,0},{2,3},{3,2},{4,5},{5,4},{6,7},{7,6},{8,9},{9,8},{10,11... | collective-permute-start | bytes 393224 | tf_op jit(solution)/shard_map/ppermute | solution.py:211

commit v20 on v19

--- a/solution.py
+++ b/solution.py
@@ -9,7 +9,7 @@
 
 VMEM_LIMIT = 48 * 1024 * 1024
 FAR, NEAR, CROSS, CORE = 8, 4, 2, 1
-OWN, SIDE, BESIDE, BEYOND, CORNER = (0, 0), (CROSS, CROSS), (NEAR, NEAR), (FAR, FAR), (NEAR | CROSS, NEAR | CROSS)
+OWN, SIDE, BESIDE, BEYOND, CORNER = (0, 0), (CROSS, NEAR), (NEAR, CROSS), (FAR, FAR), (NEAR | CROSS, NEAR | CROSS)
 FIRST, SECOND = (FAR | NEAR, FAR | CROSS), (FAR | CROSS, FAR | NEAR)
 END = (FAR | NEAR | CROSS, FAR | NEAR | CROSS)
 

time: 26.9 us -> 26.4 us (0.981)
  waiting for transfers between devices: 6.57 us -> 3.96 us
  starting transfers between devices: 12.3 us -> 14.3 us
    ppermute x15, waiting for transfers between devices: 6.57 us -> 3.96 us  [swap(): lax.ppermute(piece, 'sec', [(i, i ^ (odd_bit if i & CORE else even_bit))...]
    ppermute x15, starting transfers between devices: 12.3 us -> 14.3 us  [swap(): lax.ppermute(piece, 'sec', [(i, i ^ (odd_bit if i & CORE else even_bit))...]
    pallas_call x1, Pallas kernels: 1.13 us -> 1.63 us  [per_device(): pl.pallas_call(last_kernel, out_shape=jax.ShapeDtypeStruct(psi.shape, jnp...]
    pallas_call x1, Pallas kernels: 1.09 us -> 0.76 us  [per_device(): pl.pallas_call(middle_kernel, out_shape=jax.ShapeDtypeStruct(psi.shape, j...]
  transfers between devices with their start and end apart: 15 -> 15, of which waited for: 5 -> 4; matrix products, arithmetic and copies ran while one was open for 0% -> 0% of each run, Pallas kernels for 21% -> 20%
where the time goes in v20:
time: 26.4 us; the launch traced here: 26.3 us
  starting transfers between devices  14.3 us (54%)
  Pallas kernels  8.01 us (30%)
  waiting for transfers between devices  3.96 us (15%)
    ppermute x15, starting transfers between devices, swap(): lax.ppermute(piece, 'sec', [(i, i ^ (odd_bit if i & CORE else even_bit))...  14.3 us
    ppermute x15, waiting for transfers between devices, swap(): lax.ppermute(piece, 'sec', [(i, i ^ (odd_bit if i & CORE else even_bit))...  3.96 us
    pallas_call x1, Pallas kernels, per_device(): pl.pallas_call(functools.partial(left_kernel, pair_count, len(EARLY if by...  2.91 us
    pallas_call x1, Pallas kernels, per_device(): pl.pallas_call(last_kernel, out_shape=jax.ShapeDtypeStruct(psi.shape, jnp...  1.63 us
    pallas_call x1, Pallas kernels, per_device(): pl.pallas_call(early_kernel, out_shape=jax.ShapeDtypeStruct(psi.shape, jn...  1.62 us
    pallas_call x1, Pallas kernels, per_device(): pl.pallas_call(pack_kernel, out_shape=jax.ShapeDtypeStruct((pair_count, t...  1.09 us
    pallas_call x1, Pallas kernels, per_device(): pl.pallas_call(middle_kernel, out_shape=jax.ShapeDtypeStruct(psi.shape, j...  0.76 us
  transfers between devices with their start and end apart: 15, of which 4 were waited for; matrix products, arithmetic and copies ran while one was open for 0% of the time, Pallas kernels for 20%

profile of v20, /device:TPU:0, one launch (start us, length us, event | category | flops | bytes accessed | tf_op | source)
XLA Modules:
  0.0 26.3 jit_solution(9565680809779405360)
XLA Ops:
  0.0 1.1 %shard_map.83.refs_0_ = bf16[8,64,128]{2,1,0:T(8,128)(2,1)S(1)} custom-call(s32[16]{0:T(128)} %dims_hbm.3, bf16[16,64,64]{2,1,0:T(8,128)(2,1)} %right_hbm.1), custom_call_target="tpu_custom_call" | custom-call | bytes 131072 | tf_op jit(solution)/shard_map/pallas_call | solution.py:231
  1.1 3.1 %collective-permute-start.3 = (bf16[8,64,128]{2,1,0:T(8,128)(2,1)S(1)}, bf16[8,64,128]{2,1,0:T(8,128)(2,1)S(1)}, u32[]{:S(2)}, u32[]{:S(2)}) collective-permute-start(bf16[8,64,128]{2,1,0:T(8,128)(2,1)S(1)} %shard_map.83.refs_0_), channel_id=1, source_target_pairs={{0,4},{1,3},{2,6},{3,1},{4,0},{5,7},{6,2},{7,5},{8,12},{9,11},{10,... | collective-permute-start | bytes 393224 | tf_op jit(solution)/shard_map/ppermute | solution.py:211
  4.2 2.6 %collective-permute-start = (bf16[8,64,128]{2,1,0:T(8,128)(2,1)S(1)}, bf16[8,64,128]{2,1,0:T(8,128)(2,1)S(1)}, u32[]{:S(2)}, u32[]{:S(2)}) collective-permute-start(bf16[8,64,128]{2,1,0:T(8,128)(2,1)S(1)} %shard_map.83.refs_0_), channel_id=1, source_target_pairs={{0,8},{1,9},{2,10},{3,11},{4,12},{5,13},{6,14},{7,15},{8,0},{9,1},... | collective-permute-start | bytes 393224 | tf_op jit(solution)/shard_map/ppermute | solution.py:211
  6.8 1.5 %collective-permute-start.4 = (bf16[8,64,128]{2,1,0:T(8,128)(2,1)S(1)}, bf16[8,64,128]{2,1,0:T(8,128)(2,1)S(1)}, u32[]{:S(2)}, u32[]{:S(2)}) collective-permute-start(bf16[8,64,128]{2,1,0:T(8,128)(2,1)S(1)} %shard_map.83.refs_0_), channel_id=1, source_target_pairs={{0,2},{1,5},{2,0},{3,7},{4,6},{5,1},{6,4},{7,3},{8,10},{9,13},{10,... | collective-permute-start | bytes 393224 | tf_op jit(solution)/shard_map/ppermute | solution.py:211
  8.3 2.9 %shard_map.82 = (bf16[8,8,64,128]{3,2,1,0:T(8,128)(2,1)S(1)}, s32[202]{0:T(256)S(4)}) custom-call(s32[8]{0:T(128)} %dims_hbm.2, s32[8,8]{1,0:T(8,128)} %bitcast.1, s32[8,8]{1,0:T(8,128)} %owner_hbm.1, s32[8,8]{1,0:T(8,128)} %slot_hbm.1, bf16[8,64,64]{2,1,0:T(8,128)(2,1)} %left_hbm.1, bf16[8,8,64,128]{3,2,1,0:T(8,128)(2,1)} %psi_hbm.1), custom_call_target="tpu_custom_call" | custom-call | flops 67108864 | bytes 1048576 | tf_op jit(solution)/shard_map/pallas_call | solution.py:246
  11.2 0.0 collective-permute-done.3.refs_2_
  11.2 1.8 %collective-permute-start.5 = (bf16[8,64,128]{2,1,0:T(8,128)(2,1)S(1)}, bf16[8,64,128]{2,1,0:T(8,128)(2,1)S(1)}, u32[]{:S(2)}, u32[]{:S(2)}) collective-permute-start(bf16[8,64,128]{2,1,0:T(8,128)(2,1)S(1)} %collective-permute-done.3.refs_2_), channel_id=1, source_target_pairs={{0,2},{1,5},{2,0},{3,7},{4,6},{5,1},{6,4},{7,3},{8,10},{9,13},{10,... | collective-permute-start | bytes 393224 | tf_op jit(solution)/shard_map/ppermute | solution.py:211
  13.0 0.0 collective-permute-start.9
  13.0 0.0 collective-permute-done.refs_3_
  13.0 1.4 %collective-permute-start.1 = (bf16[8,64,128]{2,1,0:T(8,128)(2,1)S(1)}, bf16[8,64,128]{2,1,0:T(8,128)(2,1)S(1)}, u32[]{:S(2)}, u32[]{:S(2)}) collective-permute-start(bf16[8,64,128]{2,1,0:T(8,128)(2,1)S(1)} %collective-permute-done.refs_3_), channel_id=1, source_target_pairs={{0,4},{1,3},{2,6},{3,1},{4,0},{5,7},{6,2},{7,5},{8,12},{9,11},{10,... | collective-permute-start | bytes 393224 | tf_op jit(solution)/shard_map/ppermute | solution.py:211
  14.4 0.0 collective-permute-start.7
  14.4 0.0 collective-permute-done.4.refs_1_
  14.4 1.5 %collective-permute-start.6 = (bf16[8,64,128]{2,1,0:T(8,128)(2,1)S(1)}, bf16[8,64,128]{2,1,0:T(8,128)(2,1)S(1)}, u32[]{:S(2)}, u32[]{:S(2)}) collective-permute-start(bf16[8,64,128]{2,1,0:T(8,128)(2,1)S(1)} %collective-permute-done.refs_3_), channel_id=1, source_target_pairs={{0,2},{1,5},{2,0},{3,7},{4,6},{5,1},{6,4},{7,3},{8,10},{9,13},{10,... | collective-permute-start | bytes 393224 | tf_op jit(solution)/shard_map/ppermute | solution.py:211
  15.9 0.8 %collective-permute-done.5.refs_4_ = bf16[8,64,128]{2,1,0:T(8,128)(2,1)S(1)} collective-permute-done((bf16[8,64,128]{2,1,0:T(8,128)(2,1)S(1)}, bf16[8,64,128]{2,1,0:T(8,128)(2,1)S(1)}, u32[]{:S(2)}, u32[]{:S(2)}) %collective-permute-start.5) | collective-permute-done | bytes 131104 | tf_op jit(solution)/shard_map/ppermute | solution.py:211
  16.7 0.0 collective-permute-start.8
  16.7 0.0 collective-permute-done.9.refs_9_
  16.7 0.5 %collective-permute-start.10 = (bf16[8,64,128]{2,1,0:T(8,128)(2,1)S(1)}, bf16[8,64,128]{2,1,0:T(8,128)(2,1)S(1)}, u32[]{:S(2)}, u32[]{:S(2)}) collective-permute-start(bf16[8,64,128]{2,1,0:T(8,128)(2,1)S(1)} %collective-permute-done.5.refs_4_), channel_id=1, source_target_pairs={{0,1},{1,0},{2,3},{3,2},{4,5},{5,4},{6,7},{7,6},{8,9},{9,8},{10,11... | collective-permute-start | bytes 393224 | tf_op jit(solution)/shard_map/ppermute | solution.py:211
  17.2 1.1 %collective-permute-done.1.refs_5_ = bf16[8,64,128]{2,1,0:T(8,128)(2,1)S(1)} collective-permute-done((bf16[8,64,128]{2,1,0:T(8,128)(2,1)S(1)}, bf16[8,64,128]{2,1,0:T(8,128)(2,1)S(1)}, u32[]{:S(2)}, u32[]{:S(2)}) %collective-permute-start.1) | collective-permute-done | bytes 131104 | tf_op jit(solution)/shard_map/ppermute | solution.py:211
  18.4 1.4 %collective-permute-start.2 = (bf16[8,64,128]{2,1,0:T(8,128)(2,1)S(1)}, bf16[8,64,128]{2,1,0:T(8,128)(2,1)S(1)}, u32[]{:S(2)}, u32[]{:S(2)}) collective-permute-start(bf16[8,64,128]{2,1,0:T(8,128)(2,1)S(1)} %collective-permute-done.1.refs_5_), channel_id=1, source_target_pairs={{0,2},{1,5},{2,0},{3,7},{4,6},{5,1},{6,4},{7,3},{8,10},{9,13},{10,... | collective-permute-start | bytes 393224 | tf_op jit(solution)/shard_map/ppermute | solution.py:211
  19.7 0.0 collective-permute-done.7.refs_7_
  19.7 0.0 collective-permute-start.11
  19.7 0.0 collective-permute-done.6.refs_6_
  19.7 0.5 %collective-permute-start.12 = (bf16[8,64,128]{2,1,0:T(8,128)(2,1)S(1)}, bf16[8,64,128]{2,1,0:T(8,128)(2,1)S(1)}, u32[]{:S(2)}, u32[]{:S(2)}) collective-permute-start(bf16[8,64,128]{2,1,0:T(8,128)(2,1)S(1)} %collective-permute-done.1.refs_5_), channel_id=1, source_target_pairs={{0,1},{1,0},{2,3},{3,2},{4,5},{5,4},{6,7},{7,6},{8,9},{9,8},{10,11... | collective-permute-start | bytes 393224 | tf_op jit(solution)/shard_map/ppermute | solution.py:211
  20.2 0.0 collective-permute-done.8.refs_8_
  20.2 0.1 collective-permute-start.13
  20.3 0.0 collective-permute-done.10.refs_10_
  20.3 1.6 %shard_map.84.early_ref = bf16[8,8,64,128]{3,2,1,0:T(8,128)(2,1)S(1)} custom-call(s32[202]{0:T(256)S(4)} %get-tuple-element.12.list_ref, bf16[8,8,64,128]{3,2,1,0:T(8,128)(2,1)S(1)} %get-tuple-element.14.half_ref, bf16[8,64,128]{2,1,0:T(8,128)(2,1)S(1)} %shard_map.83.refs_0_, bf16[8,64,128]{2,1,0:T(8,128)(2,1)S(1)} %collective-permute-done.4.refs_1_, ...), custom_call_target="tpu_custom_call" | custom-call | flops 67108864 | bytes 1048576 | tf_op jit(solution)/shard_map/pallas_call | solution.py:290
  21.9 1.4 %collective-permute-done.2.refs_3_ = bf16[8,64,128]{2,1,0:T(8,128)(2,1)S(1)} collective-permute-done((bf16[8,64,128]{2,1,0:T(8,128)(2,1)S(1)}, bf16[8,64,128]{2,1,0:T(8,128)(2,1)S(1)}, u32[]{:S(2)}, u32[]{:S(2)}) %collective-permute-start.2) | collective-permute-done | bytes 131104 | tf_op jit(solution)/shard_map/ppermute | solution.py:211
  23.3 0.0 collective-permute-start.14
  23.3 0.0 collective-permute-done.11.refs_0_
  23.4 0.0 collective-permute-done.12.refs_1_
  23.4 0.0 collective-permute-done.13.refs_2_
  23.4 0.8 %shard_map.85.middle_ref = bf16[8,8,64,128]{3,2,1,0:T(8,128)(2,1)S(1)} custom-call(s32[202]{0:T(256)S(4)} %get-tuple-element.12.list_ref, bf16[8,8,64,128]{3,2,1,0:T(8,128)(2,1)S(1)} %shard_map.84.early_ref, bf16[8,8,64,128]{3,2,1,0:T(8,128)(2,1)S(1)} %get-tuple-element.14.half_ref, bf16[8,64,128]{2,1,0:T(8,128)(2,1)S(1)} %collective-permute-done.11.refs_0_, ...), custom_call_target="tpu_custom_call" | custom-call | flops 16777216 | bytes 262144 | tf_op jit(solution)/shard_map/pallas_call | solution.py:302
  24.1 0.6 %collective-permute-done.14.pairs_ref = bf16[8,64,128]{2,1,0:T(8,128)(2,1)S(1)} collective-permute-done((bf16[8,64,128]{2,1,0:T(8,128)(2,1)S(1)}, bf16[8,64,128]{2,1,0:T(8,128)(2,1)S(1)}, u32[]{:S(2)}, u32[]{:S(2)}) %collective-permute-start.14) | collective-permute-done | bytes 131104 | tf_op jit(solution)/shard_map/ppermute | solution.py:211
  24.7 1.6 %shard_map.86 = bf16[8,8,64,128]{3,2,1,0:T(8,128)(2,1)} custom-call(s32[202]{0:T(256)S(4)} %get-tuple-element.12.list_ref, bf16[8,8,64,128]{3,2,1,0:T(8,128)(2,1)S(1)} %shard_map.85.middle_ref, bf16[8,8,64,128]{3,2,1,0:T(8,128)(2,1)S(1)} %get-tuple-element.14.half_ref, bf16[8,64,128]{2,1,0:T(8,128)(2,1)S(1)} %collective-permute-done.14.pairs_ref), custom_call_target="tpu_custom_call" | custom-call | flops 4194304 | bytes 1048576 | tf_op jit(solution)/shard_map/pallas_call | solution.py:311
Async XLA Ops:
  1.1 10.1 %collective-permute-start.3 = (bf16[8,64,128]{2,1,0:T(8,128)(2,1)S(1)}, bf16[8,64,128]{2,1,0:T(8,128)(2,1)S(1)}, u32[]{:S(2)}, u32[]{:S(2)}) collective-permute-start(bf16[8,64,128]{2,1,0:T(8,128)(2,1)S(1)} %shard_map.83.refs_0_), channel_id=1, source_target_pairs={{0,4},{1,3},{2,6},{3,1},{4,0},{5,7},{6,2},{7,5},{8,12},{9,11},{10,... | collective-permute-start | bytes 393224 | tf_op jit(solution)/shard_map/ppermute | solution.py:211
  4.2 8.8 %collective-permute-start = (bf16[8,64,128]{2,1,0:T(8,128)(2,1)S(1)}, bf16[8,64,128]{2,1,0:T(8,128)(2,1)S(1)}, u32[]{:S(2)}, u32[]{:S(2)}) collective-permute-start(bf16[8,64,128]{2,1,0:T(8,128)(2,1)S(1)} %shard_map.83.refs_0_), channel_id=1, source_target_pairs={{0,8},{1,9},{2,10},{3,11},{4,12},{5,13},{6,14},{7,15},{8,0},{9,1},... | collective-permute-start | bytes 393224 | tf_op jit(solution)/shard_map/ppermute | solution.py:211
  6.8 7.6 %collective-permute-start.4 = (bf16[8,64,128]{2,1,0:T(8,128)(2,1)S(1)}, bf16[8,64,128]{2,1,0:T(8,128)(2,1)S(1)}, u32[]{:S(2)}, u32[]{:S(2)}) collective-permute-start(bf16[8,64,128]{2,1,0:T(8,128)(2,1)S(1)} %shard_map.83.refs_0_), channel_id=1, source_target_pairs={{0,2},{1,5},{2,0},{3,7},{4,6},{5,1},{6,4},{7,3},{8,10},{9,13},{10,... | collective-permute-start | bytes 393224 | tf_op jit(solution)/shard_map/ppermute | solution.py:211
  11.2 5.5 %collective-permute-start.5 = (bf16[8,64,128]{2,1,0:T(8,128)(2,1)S(1)}, bf16[8,64,128]{2,1,0:T(8,128)(2,1)S(1)}, u32[]{:S(2)}, u32[]{:S(2)}) collective-permute-start(bf16[8,64,128]{2,1,0:T(8,128)(2,1)S(1)} %collective-permute-done.3.refs_2_), channel_id=1, source_target_pairs={{0,2},{1,5},{2,0},{3,7},{4,6},{5,1},{6,4},{7,3},{8,10},{9,13},{10,... | collective-permute-start | bytes 393224 | tf_op jit(solution)/shard_map/ppermute | solution.py:211
  13.0 3.8 %collective-permute-start.9 = (bf16[8,64,128]{2,1,0:T(8,128)(2,1)S(1)}, bf16[8,64,128]{2,1,0:T(8,128)(2,1)S(1)}, u32[]{:S(2)}, u32[]{:S(2)}) collective-permute-start(bf16[8,64,128]{2,1,0:T(8,128)(2,1)S(1)} %collective-permute-done.3.refs_2_), channel_id=1, source_target_pairs={{0,1},{1,0},{2,3},{3,2},{4,5},{5,4},{6,7},{7,6},{8,9},{9,8},{10,11... | collective-permute-start | bytes 393224 | tf_op jit(solution)/shard_map/ppermute | solution.py:211
  13.0 5.4 %collective-permute-start.1 = (bf16[8,64,128]{2,1,0:T(8,128)(2,1)S(1)}, bf16[8,64,128]{2,1,0:T(8,128)(2,1)S(1)}, u32[]{:S(2)}, u32[]{:S(2)}) collective-permute-start(bf16[8,64,128]{2,1,0:T(8,128)(2,1)S(1)} %collective-permute-done.refs_3_), channel_id=1, source_target_pairs={{0,4},{1,3},{2,6},{3,1},{4,0},{5,7},{6,2},{7,5},{8,12},{9,11},{10,... | collective-permute-start | bytes 393224 | tf_op jit(solution)/shard_map/ppermute | solution.py:211
  14.4 5.3 %collective-permute-start.7 = (bf16[8,64,128]{2,1,0:T(8,128)(2,1)S(1)}, bf16[8,64,128]{2,1,0:T(8,128)(2,1)S(1)}, u32[]{:S(2)}, u32[]{:S(2)}) collective-permute-start(bf16[8,64,128]{2,1,0:T(8,128)(2,1)S(1)} %shard_map.83.refs_0_), channel_id=1, source_target_pairs={{0,1},{1,0},{2,3},{3,2},{4,5},{5,4},{6,7},{7,6},{8,9},{9,8},{10,11... | collective-permute-start | bytes 393224 | tf_op jit(solution)/shard_map/ppermute | solution.py:211
  14.4 5.3 %collective-permute-start.6 = (bf16[8,64,128]{2,1,0:T(8,128)(2,1)S(1)}, bf16[8,64,128]{2,1,0:T(8,128)(2,1)S(1)}, u32[]{:S(2)}, u32[]{:S(2)}) collective-permute-start(bf16[8,64,128]{2,1,0:T(8,128)(2,1)S(1)} %collective-permute-done.refs_3_), channel_id=1, source_target_pairs={{0,2},{1,5},{2,0},{3,7},{4,6},{5,1},{6,4},{7,3},{8,10},{9,13},{10,... | collective-permute-start | bytes 393224 | tf_op jit(solution)/shard_map/ppermute | solution.py:211
  16.7 3.5 %collective-permute-start.8 = (bf16[8,64,128]{2,1,0:T(8,128)(2,1)S(1)}, bf16[8,64,128]{2,1,0:T(8,128)(2,1)S(1)}, u32[]{:S(2)}, u32[]{:S(2)}) collective-permute-start(bf16[8,64,128]{2,1,0:T(8,128)(2,1)S(1)} %collective-permute-done.4.refs_1_), channel_id=1, source_target_pairs={{0,1},{1,0},{2,3},{3,2},{4,5},{5,4},{6,7},{7,6},{8,9},{9,8},{10,11... | collective-permute-start | bytes 393224 | tf_op jit(solution)/shard_map/ppermute | solution.py:211
  16.7 3.6 %collective-permute-start.10 = (bf16[8,64,128]{2,1,0:T(8,128)(2,1)S(1)}, bf16[8,64,128]{2,1,0:T(8,128)(2,1)S(1)}, u32[]{:S(2)}, u32[]{:S(2)}) collective-permute-start(bf16[8,64,128]{2,1,0:T(8,128)(2,1)S(1)} %collective-permute-done.5.refs_4_), channel_id=1, source_target_pairs={{0,1},{1,0},{2,3},{3,2},{4,5},{5,4},{6,7},{7,6},{8,9},{9,8},{10,11... | collective-permute-start | bytes 393224 | tf_op jit(solution)/shard_map/ppermute | solution.py:211
  18.4 5.0 %collective-permute-start.2 = (bf16[8,64,128]{2,1,0:T(8,128)(2,1)S(1)}, bf16[8,64,128]{2,1,0:T(8,128)(2,1)S(1)}, u32[]{:S(2)}, u32[]{:S(2)}) collective-permute-start(bf16[8,64,128]{2,1,0:T(8,128)(2,1)S(1)} %collective-permute-done.1.refs_5_), channel_id=1, source_target_pairs={{0,2},{1,5},{2,0},{3,7},{4,6},{5,1},{6,4},{7,3},{8,10},{9,13},{10,... | collective-permute-start | bytes 393224 | tf_op jit(solution)/shard_map/ppermute | solution.py:211
  19.7 3.6 %collective-permute-start.11 = (bf16[8,64,128]{2,1,0:T(8,128)(2,1)S(1)}, bf16[8,64,128]{2,1,0:T(8,128)(2,1)S(1)}, u32[]{:S(2)}, u32[]{:S(2)}) collective-permute-start(bf16[8,64,128]{2,1,0:T(8,128)(2,1)S(1)} %collective-permute-done.refs_3_), channel_id=1, source_target_pairs={{0,1},{1,0},{2,3},{3,2},{4,5},{5,4},{6,7},{7,6},{8,9},{9,8},{10,11... | collective-permute-start | bytes 393224 | tf_op jit(solution)/shard_map/ppermute | solution.py:211
  19.7 3.6 %collective-permute-start.12 = (bf16[8,64,128]{2,1,0:T(8,128)(2,1)S(1)}, bf16[8,64,128]{2,1,0:T(8,128)(2,1)S(1)}, u32[]{:S(2)}, u32[]{:S(2)}) collective-permute-start(bf16[8,64,128]{2,1,0:T(8,128)(2,1)S(1)} %collective-permute-done.1.refs_5_), channel_id=1, source_target_pairs={{0,1},{1,0},{2,3},{3,2},{4,5},{5,4},{6,7},{7,6},{8,9},{9,8},{10,11... | collective-permute-start | bytes 393224 | tf_op jit(solution)/shard_map/ppermute | solution.py:211
  20.2 3.1 %collective-permute-start.13 = (bf16[8,64,128]{2,1,0:T(8,128)(2,1)S(1)}, bf16[8,64,128]{2,1,0:T(8,128)(2,1)S(1)}, u32[]{:S(2)}, u32[]{:S(2)}) collective-permute-start(bf16[8,64,128]{2,1,0:T(8,128)(2,1)S(1)} %collective-permute-done.6.refs_6_), channel_id=1, source_target_pairs={{0,1},{1,0},{2,3},{3,2},{4,5},{5,4},{6,7},{7,6},{8,9},{9,8},{10,11... | collective-permute-start | bytes 393224 | tf_op jit(solution)/shard_map/ppermute | solution.py:211
  23.3 1.3 %collective-permute-start.14 = (bf16[8,64,128]{2,1,0:T(8,128)(2,1)S(1)}, bf16[8,64,128]{2,1,0:T(8,128)(2,1)S(1)}, u32[]{:S(2)}, u32[]{:S(2)}) collective-permute-start(bf16[8,64,128]{2,1,0:T(8,128)(2,1)S(1)} %collective-permute-done.2.refs_3_), channel_id=1, source_target_pairs={{0,1},{1,0},{2,3},{3,2},{4,5},{5,4},{6,7},{7,6},{8,9},{9,8},{10,11... | collective-permute-start | bytes 393224 | tf_op jit(solution)/shard_map/ppermute | solution.py:211

commit v21 on v17

--- a/solution.py
+++ b/solution.py
@@ -9,7 +9,7 @@
 
 VMEM_LIMIT = 48 * 1024 * 1024
 FAR, NEAR, CROSS, CORE = 8, 4, 2, 1
-MIDDLE = (FAR | CORE, FAR | NEAR | CORE, FAR | CROSS | CORE, FAR | NEAR | CROSS)
+MIDDLE = (NEAR | CROSS | CORE, FAR | CORE, FAR | NEAR | CORE, FAR | CROSS | CORE, FAR | NEAR | CROSS)
 LAST = (FAR | NEAR | CROSS | CORE,)
 EARLY = tuple(r for r in range(16) if r not in MIDDLE + LAST)
 ORDER = EARLY + MIDDLE + LAST
@@ -256,16 +256,16 @@
 
     if by_swaps:
         pieces = {0: pairs}
-        def pass_on(*pairs_of):
-            for r, bit in pairs_of:
+        def pass_on(*routes):
+            for r, bit in routes:
                 pieces[r | bit] = swap(pieces[r], bit)
 
-        pass_on((0, FAR), (0, NEAR), (0, CROSS))
-        held = (0, NEAR,)
+        pass_on((0, FAR), (0, NEAR), (0, CROSS), (0, CORE))
+        held = (FAR,)
         half, ends = lax.optimization_barrier((half, [pieces[r] for r in held]))
         pieces.update(zip(held, ends))
-        pass_on((NEAR, CROSS), (FAR, NEAR), (FAR, CROSS), (FAR | NEAR, CROSS))
-        pass_on((0, CORE), (NEAR, CORE), (CROSS, CORE), (NEAR | CROSS, CORE), (FAR | NEAR, CORE), (FAR, CORE), (FAR | CROSS, CORE))
+        pass_on((FAR, NEAR), (NEAR, CROSS), (FAR, CROSS), (FAR | NEAR, CROSS))
+        pass_on((NEAR, CORE), (CROSS, CORE), (NEAR | CROSS, CORE), (FAR | NEAR, CORE), (FAR, CORE), (FAR | CROSS, CORE))
         early = [pieces[r] for r in EARLY]
     else:
         early = [lax.all_gather(pairs, "sec", axis=0, tiled=True)]

time: 25.9 us -> 26 us (level)
  waiting for transfers between devices: 5.28 us -> 6.19 us
  starting transfers between devices: 12.3 us -> 11.7 us
    ppermute x15, waiting for transfers between devices: 5.28 us -> 6.19 us  [swap(): return lax.ppermute(piece, 'sec', [(i, i ^ bit) for i in range(count)])]
    ppermute x15, starting transfers between devices: 12.3 us -> 11.7 us  [swap(): return lax.ppermute(piece, 'sec', [(i, i ^ bit) for i in range(count)])]
  transfers between devices with their start and end apart: 15 -> 15, of which waited for: 5 -> 6; matrix products, arithmetic and copies ran while one was open for 0% -> 0% of each run, Pallas kernels for 22% -> 22%
where the time goes in v21:
time: 26 us; the launch traced here: 25.7 us
  starting transfers between devices  11.7 us (45%)
  Pallas kernels  7.77 us (30%)
  waiting for transfers between devices  6.19 us (24%)
    ppermute x15, starting transfers between devices, swap(): return lax.ppermute(piece, 'sec', [(i, i ^ bit) for i in range(count)])  11.7 us
    ppermute x15, waiting for transfers between devices, swap(): return lax.ppermute(piece, 'sec', [(i, i ^ bit) for i in range(count)])  6.19 us
    pallas_call x1, Pallas kernels, per_device(): pl.pallas_call(functools.partial(left_kernel, pair_count, len(EARLY if by...  3.2 us
    pallas_call x1, Pallas kernels, per_device(): pl.pallas_call(early_kernel, out_shape=jax.ShapeDtypeStruct(psi.shape, jn...  1.61 us
    pallas_call x1, Pallas kernels, per_device(): pl.pallas_call(last_kernel, out_shape=jax.ShapeDtypeStruct(psi.shape, jnp...  1.09 us
    pallas_call x1, Pallas kernels, per_device(): pl.pallas_call(pack_kernel, out_shape=jax.ShapeDtypeStruct((pair_count, t...  1.09 us
    pallas_call x1, Pallas kernels, per_device(): pl.pallas_call(middle_kernel, out_shape=jax.ShapeDtypeStruct(psi.shape, j...  0.77 us
  transfers between devices with their start and end apart: 15, of which 6 were waited for; matrix products, arithmetic and copies ran while one was open for 0% of the time, Pallas kernels for 22%

profile of v21, /device:TPU:0, one launch (start us, length us, event | category | flops | bytes accessed | tf_op | source)
XLA Modules:
  0.0 25.7 jit_solution(5525999486682587926)
XLA Ops:
  0.0 1.1 %shard_map.83.refs_0_ = bf16[8,64,128]{2,1,0:T(8,128)(2,1)S(1)} custom-call(s32[16]{0:T(128)} %dims_hbm.3, bf16[16,64,64]{2,1,0:T(8,128)(2,1)} %right_hbm.1), custom_call_target="tpu_custom_call" | custom-call | bytes 131072 | tf_op jit(solution)/shard_map/pallas_call | solution.py:219
  1.1 4.1 %collective-permute-start = (bf16[8,64,128]{2,1,0:T(8,128)(2,1)S(1)}, bf16[8,64,128]{2,1,0:T(8,128)(2,1)S(1)}, u32[]{:S(2)}, u32[]{:S(2)}) collective-permute-start(bf16[8,64,128]{2,1,0:T(8,128)(2,1)S(1)} %shard_map.83.refs_0_), channel_id=1, source_target_pairs={{0,8},{1,9},{2,10},{3,11},{4,12},{5,13},{6,14},{7,15},{8,0},{9,1},... | collective-permute-start | bytes 393224 | tf_op jit(solution)/shard_map/ppermute | solution.py:199
  5.2 1.6 %collective-permute-start.6 = (bf16[8,64,128]{2,1,0:T(8,128)(2,1)S(1)}, bf16[8,64,128]{2,1,0:T(8,128)(2,1)S(1)}, u32[]{:S(2)}, u32[]{:S(2)}) collective-permute-start(bf16[8,64,128]{2,1,0:T(8,128)(2,1)S(1)} %shard_map.83.refs_0_), channel_id=1, source_target_pairs={{0,4},{1,5},{2,6},{3,7},{4,0},{5,1},{6,2},{7,3},{8,12},{9,13},{10,... | collective-permute-start | bytes 393224 | tf_op jit(solution)/shard_map/ppermute | solution.py:199
  6.8 1.5 %collective-permute-start.4 = (bf16[8,64,128]{2,1,0:T(8,128)(2,1)S(1)}, bf16[8,64,128]{2,1,0:T(8,128)(2,1)S(1)}, u32[]{:S(2)}, u32[]{:S(2)}) collective-permute-start(bf16[8,64,128]{2,1,0:T(8,128)(2,1)S(1)} %shard_map.83.refs_0_), channel_id=1, source_target_pairs={{0,2},{1,3},{2,0},{3,1},{4,6},{5,7},{6,4},{7,5},{8,10},{9,11},{10,... | collective-permute-start | bytes 393224 | tf_op jit(solution)/shard_map/ppermute | solution.py:199
  8.3 0.0 collective-permute-start.3
  8.3 3.2 %shard_map.82 = (bf16[8,8,64,128]{3,2,1,0:T(8,128)(2,1)S(1)}, s32[202]{0:T(256)S(4)}) custom-call(s32[8]{0:T(128)} %dims_hbm.2, s32[8,8]{1,0:T(8,128)} %bitcast.1, s32[8,8]{1,0:T(8,128)} %owner_hbm.1, s32[8,8]{1,0:T(8,128)} %slot_hbm.1, bf16[8,64,64]{2,1,0:T(8,128)(2,1)} %left_hbm.1, bf16[8,8,64,128]{3,2,1,0:T(8,128)(2,1)} %psi_hbm.1), custom_call_target="tpu_custom_call" | custom-call | flops 67108864 | bytes 1048576 | tf_op jit(solution)/shard_map/pallas_call | solution.py:234
  11.5 0.1 collective-permute-done.refs_7_
  11.6 0.6 %collective-permute-start.1 = (bf16[8,64,128]{2,1,0:T(8,128)(2,1)S(1)}, bf16[8,64,128]{2,1,0:T(8,128)(2,1)S(1)}, u32[]{:S(2)}, u32[]{:S(2)}) collective-permute-start(bf16[8,64,128]{2,1,0:T(8,128)(2,1)S(1)} %collective-permute-done.refs_7_), channel_id=1, source_target_pairs={{0,4},{1,5},{2,6},{3,7},{4,0},{5,1},{6,2},{7,3},{8,12},{9,13},{10,... | collective-permute-start | bytes 393224 | tf_op jit(solution)/shard_map/ppermute | solution.py:199
  12.2 0.0 collective-permute-done.6.refs_4_
  12.2 1.5 %collective-permute-start.8 = (bf16[8,64,128]{2,1,0:T(8,128)(2,1)S(1)}, bf16[8,64,128]{2,1,0:T(8,128)(2,1)S(1)}, u32[]{:S(2)}, u32[]{:S(2)}) collective-permute-start(bf16[8,64,128]{2,1,0:T(8,128)(2,1)S(1)} %collective-permute-done.6.refs_4_), channel_id=1, source_target_pairs={{0,2},{1,3},{2,0},{3,1},{4,6},{5,7},{6,4},{7,5},{8,10},{9,11},{10,... | collective-permute-start | bytes 393224 | tf_op jit(solution)/shard_map/ppermute | solution.py:199
  13.7 0.0 collective-permute-start.7
  13.7 0.0 collective-permute-done.4.refs_2_
  13.7 0.5 %collective-permute-start.5 = (bf16[8,64,128]{2,1,0:T(8,128)(2,1)S(1)}, bf16[8,64,128]{2,1,0:T(8,128)(2,1)S(1)}, u32[]{:S(2)}, u32[]{:S(2)}) collective-permute-start(bf16[8,64,128]{2,1,0:T(8,128)(2,1)S(1)} %collective-permute-done.4.refs_2_), channel_id=1, source_target_pairs={{0,1},{1,0},{2,3},{3,2},{4,5},{5,4},{6,7},{7,6},{8,9},{9,8},{10,11... | collective-permute-start | bytes 393224 | tf_op jit(solution)/shard_map/ppermute | solution.py:199
  14.2 0.0 collective-permute-done.3.refs_1_
  14.2 0.5 %collective-permute-start.9 = (bf16[8,64,128]{2,1,0:T(8,128)(2,1)S(1)}, bf16[8,64,128]{2,1,0:T(8,128)(2,1)S(1)}, u32[]{:S(2)}, u32[]{:S(2)}) collective-permute-start(bf16[8,64,128]{2,1,0:T(8,128)(2,1)S(1)} %collective-permute-done.refs_7_), channel_id=1, source_target_pairs={{0,2},{1,3},{2,0},{3,1},{4,6},{5,7},{6,4},{7,5},{8,10},{9,11},{10,... | collective-permute-start | bytes 393224 | tf_op jit(solution)/shard_map/ppermute | solution.py:199
  14.8 2.7 %collective-permute-done.1.refs_9_ = bf16[8,64,128]{2,1,0:T(8,128)(2,1)S(1)} collective-permute-done((bf16[8,64,128]{2,1,0:T(8,128)(2,1)S(1)}, bf16[8,64,128]{2,1,0:T(8,128)(2,1)S(1)}, u32[]{:S(2)}, u32[]{:S(2)}) %collective-permute-start.1) | collective-permute-done | bytes 131104 | tf_op jit(solution)/shard_map/ppermute | solution.py:199
  17.5 0.7 %collective-permute-start.2 = (bf16[8,64,128]{2,1,0:T(8,128)(2,1)S(1)}, bf16[8,64,128]{2,1,0:T(8,128)(2,1)S(1)}, u32[]{:S(2)}, u32[]{:S(2)}) collective-permute-start(bf16[8,64,128]{2,1,0:T(8,128)(2,1)S(1)} %collective-permute-done.1.refs_9_), channel_id=1, source_target_pairs={{0,2},{1,3},{2,0},{3,1},{4,6},{5,7},{6,4},{7,5},{8,10},{9,11},{10,... | collective-permute-start | bytes 393224 | tf_op jit(solution)/shard_map/ppermute | solution.py:199
  18.1 0.2 collective-permute-done.8.refs_6_
  18.4 0.0 collective-permute-start.11
  18.4 0.0 collective-permute-done.7.refs_5_
  18.4 0.5 %collective-permute-start.12 = (bf16[8,64,128]{2,1,0:T(8,128)(2,1)S(1)}, bf16[8,64,128]{2,1,0:T(8,128)(2,1)S(1)}, u32[]{:S(2)}, u32[]{:S(2)}) collective-permute-start(bf16[8,64,128]{2,1,0:T(8,128)(2,1)S(1)} %collective-permute-done.1.refs_9_), channel_id=1, source_target_pairs={{0,1},{1,0},{2,3},{3,2},{4,5},{5,4},{6,7},{7,6},{8,9},{9,8},{10,11... | collective-permute-start | bytes 393224 | tf_op jit(solution)/shard_map/ppermute | solution.py:199
  18.9 0.0 collective-permute-done.5.refs_3_
  18.9 0.1 collective-permute-start.10
  18.9 2.2 %collective-permute-done.9.refs_8_ = bf16[8,64,128]{2,1,0:T(8,128)(2,1)S(1)} collective-permute-done((bf16[8,64,128]{2,1,0:T(8,128)(2,1)S(1)}, bf16[8,64,128]{2,1,0:T(8,128)(2,1)S(1)}, u32[]{:S(2)}, u32[]{:S(2)}) %collective-permute-start.9) | collective-permute-done | bytes 131104 | tf_op jit(solution)/shard_map/ppermute | solution.py:199
  21.2 0.0 collective-permute-start.13
  21.2 1.6 %shard_map.84.early_ref = bf16[8,8,64,128]{3,2,1,0:T(8,128)(2,1)S(1)} custom-call(s32[202]{0:T(256)S(4)} %get-tuple-element.11.list_ref, bf16[8,8,64,128]{3,2,1,0:T(8,128)(2,1)S(1)} %get-tuple-element.14.half_ref, bf16[8,64,128]{2,1,0:T(8,128)(2,1)S(1)} %shard_map.83.refs_0_, bf16[8,64,128]{2,1,0:T(8,128)(2,1)S(1)} %collective-permute-done.3.refs_1_, ...), custom_call_target="tpu_custom_call" | custom-call | flops 67108864 | bytes 1048576 | tf_op jit(solution)/shard_map/pallas_call | solution.py:273
  22.8 0.5 %collective-permute-done.2.refs_4_ = bf16[8,64,128]{2,1,0:T(8,128)(2,1)S(1)} collective-permute-done((bf16[8,64,128]{2,1,0:T(8,128)(2,1)S(1)}, bf16[8,64,128]{2,1,0:T(8,128)(2,1)S(1)}, u32[]{:S(2)}, u32[]{:S(2)}) %collective-permute-start.2) | collective-permute-done | bytes 131104 | tf_op jit(solution)/shard_map/ppermute | solution.py:199
  23.3 0.1 collective-permute-start.14
  23.4 0.0 collective-permute-done.11.refs_1_
  23.4 0.0 collective-permute-done.10.refs_0_
  23.4 0.0 collective-permute-done.13.refs_3_
  23.4 0.0 collective-permute-done.12.refs_2_
  23.4 0.8 %shard_map.85.middle_ref = bf16[8,8,64,128]{3,2,1,0:T(8,128)(2,1)S(1)} custom-call(s32[202]{0:T(256)S(4)} %get-tuple-element.11.list_ref, bf16[8,8,64,128]{3,2,1,0:T(8,128)(2,1)S(1)} %shard_map.84.early_ref, bf16[8,8,64,128]{3,2,1,0:T(8,128)(2,1)S(1)} %get-tuple-element.14.half_ref, bf16[8,64,128]{2,1,0:T(8,128)(2,1)S(1)} %collective-permute-done.10.refs_0_, ...), custom_call_target="tpu_custom_call" | custom-call | flops 16777216 | bytes 262144 | tf_op jit(solution)/shard_map/pallas_call | solution.py:286
  24.2 0.4 %collective-permute-done.14.pairs_ref = bf16[8,64,128]{2,1,0:T(8,128)(2,1)S(1)} collective-permute-done((bf16[8,64,128]{2,1,0:T(8,128)(2,1)S(1)}, bf16[8,64,128]{2,1,0:T(8,128)(2,1)S(1)}, u32[]{:S(2)}, u32[]{:S(2)}) %collective-permute-start.14) | collective-permute-done | bytes 131104 | tf_op jit(solution)/shard_map/ppermute | solution.py:199
  24.6 1.1 %shard_map.86 = bf16[8,8,64,128]{3,2,1,0:T(8,128)(2,1)} custom-call(s32[202]{0:T(256)S(4)} %get-tuple-element.11.list_ref, bf16[8,8,64,128]{3,2,1,0:T(8,128)(2,1)S(1)} %shard_map.85.middle_ref, bf16[8,8,64,128]{3,2,1,0:T(8,128)(2,1)S(1)} %get-tuple-element.14.half_ref, bf16[8,64,128]{2,1,0:T(8,128)(2,1)S(1)} %collective-permute-done.14.pairs_ref), custom_call_target="tpu_custom_call" | custom-call | flops 4194304 | bytes 1048576 | tf_op jit(solution)/shard_map/pallas_call | solution.py:295
Async XLA Ops:
  1.1 10.5 %collective-permute-start = (bf16[8,64,128]{2,1,0:T(8,128)(2,1)S(1)}, bf16[8,64,128]{2,1,0:T(8,128)(2,1)S(1)}, u32[]{:S(2)}, u32[]{:S(2)}) collective-permute-start(bf16[8,64,128]{2,1,0:T(8,128)(2,1)S(1)} %shard_map.83.refs_0_), channel_id=1, source_target_pairs={{0,8},{1,9},{2,10},{3,11},{4,12},{5,13},{6,14},{7,15},{8,0},{9,1},... | collective-permute-start | bytes 393224 | tf_op jit(solution)/shard_map/ppermute | solution.py:199
  5.2 7.0 %collective-permute-start.6 = (bf16[8,64,128]{2,1,0:T(8,128)(2,1)S(1)}, bf16[8,64,128]{2,1,0:T(8,128)(2,1)S(1)}, u32[]{:S(2)}, u32[]{:S(2)}) collective-permute-start(bf16[8,64,128]{2,1,0:T(8,128)(2,1)S(1)} %shard_map.83.refs_0_), channel_id=1, source_target_pairs={{0,4},{1,5},{2,6},{3,7},{4,0},{5,1},{6,2},{7,3},{8,12},{9,13},{10,... | collective-permute-start | bytes 393224 | tf_op jit(solution)/shard_map/ppermute | solution.py:199
  6.8 7.0 %collective-permute-start.4 = (bf16[8,64,128]{2,1,0:T(8,128)(2,1)S(1)}, bf16[8,64,128]{2,1,0:T(8,128)(2,1)S(1)}, u32[]{:S(2)}, u32[]{:S(2)}) collective-permute-start(bf16[8,64,128]{2,1,0:T(8,128)(2,1)S(1)} %shard_map.83.refs_0_), channel_id=1, source_target_pairs={{0,2},{1,3},{2,0},{3,1},{4,6},{5,7},{6,4},{7,5},{8,10},{9,11},{10,... | collective-permute-start | bytes 393224 | tf_op jit(solution)/shard_map/ppermute | solution.py:199
  8.3 6.0 %collective-permute-start.3 = (bf16[8,64,128]{2,1,0:T(8,128)(2,1)S(1)}, bf16[8,64,128]{2,1,0:T(8,128)(2,1)S(1)}, u32[]{:S(2)}, u32[]{:S(2)}) collective-permute-start(bf16[8,64,128]{2,1,0:T(8,128)(2,1)S(1)} %shard_map.83.refs_0_), channel_id=1, source_target_pairs={{0,1},{1,0},{2,3},{3,2},{4,5},{5,4},{6,7},{7,6},{8,9},{9,8},{10,11... | collective-permute-start | bytes 393224 | tf_op jit(solution)/shard_map/ppermute | solution.py:199
  11.6 5.8 %collective-permute-start.1 = (bf16[8,64,128]{2,1,0:T(8,128)(2,1)S(1)}, bf16[8,64,128]{2,1,0:T(8,128)(2,1)S(1)}, u32[]{:S(2)}, u32[]{:S(2)}) collective-permute-start(bf16[8,64,128]{2,1,0:T(8,128)(2,1)S(1)} %collective-permute-done.refs_7_), channel_id=1, source_target_pairs={{0,4},{1,5},{2,6},{3,7},{4,0},{5,1},{6,2},{7,3},{8,12},{9,13},{10,... | collective-permute-start | bytes 393224 | tf_op jit(solution)/shard_map/ppermute | solution.py:199
  12.2 6.1 %collective-permute-start.8 = (bf16[8,64,128]{2,1,0:T(8,128)(2,1)S(1)}, bf16[8,64,128]{2,1,0:T(8,128)(2,1)S(1)}, u32[]{:S(2)}, u32[]{:S(2)}) collective-permute-start(bf16[8,64,128]{2,1,0:T(8,128)(2,1)S(1)} %collective-permute-done.6.refs_4_), channel_id=1, source_target_pairs={{0,2},{1,3},{2,0},{3,1},{4,6},{5,7},{6,4},{7,5},{8,10},{9,11},{10,... | collective-permute-start | bytes 393224 | tf_op jit(solution)/shard_map/ppermute | solution.py:199
  13.7 4.6 %collective-permute-start.7 = (bf16[8,64,128]{2,1,0:T(8,128)(2,1)S(1)}, bf16[8,64,128]{2,1,0:T(8,128)(2,1)S(1)}, u32[]{:S(2)}, u32[]{:S(2)}) collective-permute-start(bf16[8,64,128]{2,1,0:T(8,128)(2,1)S(1)} %collective-permute-done.6.refs_4_), channel_id=1, source_target_pairs={{0,1},{1,0},{2,3},{3,2},{4,5},{5,4},{6,7},{7,6},{8,9},{9,8},{10,11... | collective-permute-start | bytes 393224 | tf_op jit(solution)/shard_map/ppermute | solution.py:199
  13.7 5.1 %collective-permute-start.5 = (bf16[8,64,128]{2,1,0:T(8,128)(2,1)S(1)}, bf16[8,64,128]{2,1,0:T(8,128)(2,1)S(1)}, u32[]{:S(2)}, u32[]{:S(2)}) collective-permute-start(bf16[8,64,128]{2,1,0:T(8,128)(2,1)S(1)} %collective-permute-done.4.refs_2_), channel_id=1, source_target_pairs={{0,1},{1,0},{2,3},{3,2},{4,5},{5,4},{6,7},{7,6},{8,9},{9,8},{10,11... | collective-permute-start | bytes 393224 | tf_op jit(solution)/shard_map/ppermute | solution.py:199
  14.2 6.9 %collective-permute-start.9 = (bf16[8,64,128]{2,1,0:T(8,128)(2,1)S(1)}, bf16[8,64,128]{2,1,0:T(8,128)(2,1)S(1)}, u32[]{:S(2)}, u32[]{:S(2)}) collective-permute-start(bf16[8,64,128]{2,1,0:T(8,128)(2,1)S(1)} %collective-permute-done.refs_7_), channel_id=1, source_target_pairs={{0,2},{1,3},{2,0},{3,1},{4,6},{5,7},{6,4},{7,5},{8,10},{9,11},{10,... | collective-permute-start | bytes 393224 | tf_op jit(solution)/shard_map/ppermute | solution.py:199
  17.5 5.8 %collective-permute-start.2 = (bf16[8,64,128]{2,1,0:T(8,128)(2,1)S(1)}, bf16[8,64,128]{2,1,0:T(8,128)(2,1)S(1)}, u32[]{:S(2)}, u32[]{:S(2)}) collective-permute-start(bf16[8,64,128]{2,1,0:T(8,128)(2,1)S(1)} %collective-permute-done.1.refs_9_), channel_id=1, source_target_pairs={{0,2},{1,3},{2,0},{3,1},{4,6},{5,7},{6,4},{7,5},{8,10},{9,11},{10,... | collective-permute-start | bytes 393224 | tf_op jit(solution)/shard_map/ppermute | solution.py:199
  18.4 5.0 %collective-permute-start.11 = (bf16[8,64,128]{2,1,0:T(8,128)(2,1)S(1)}, bf16[8,64,128]{2,1,0:T(8,128)(2,1)S(1)}, u32[]{:S(2)}, u32[]{:S(2)}) collective-permute-start(bf16[8,64,128]{2,1,0:T(8,128)(2,1)S(1)} %collective-permute-done.refs_7_), channel_id=1, source_target_pairs={{0,1},{1,0},{2,3},{3,2},{4,5},{5,4},{6,7},{7,6},{8,9},{9,8},{10,11... | collective-permute-start | bytes 393224 | tf_op jit(solution)/shard_map/ppermute | solution.py:199
  18.4 5.0 %collective-permute-start.12 = (bf16[8,64,128]{2,1,0:T(8,128)(2,1)S(1)}, bf16[8,64,128]{2,1,0:T(8,128)(2,1)S(1)}, u32[]{:S(2)}, u32[]{:S(2)}) collective-permute-start(bf16[8,64,128]{2,1,0:T(8,128)(2,1)S(1)} %collective-permute-done.1.refs_9_), channel_id=1, source_target_pairs={{0,1},{1,0},{2,3},{3,2},{4,5},{5,4},{6,7},{7,6},{8,9},{9,8},{10,11... | collective-permute-start | bytes 393224 | tf_op jit(solution)/shard_map/ppermute | solution.py:199
  18.9 4.5 %collective-permute-start.10 = (bf16[8,64,128]{2,1,0:T(8,128)(2,1)S(1)}, bf16[8,64,128]{2,1,0:T(8,128)(2,1)S(1)}, u32[]{:S(2)}, u32[]{:S(2)}) collective-permute-start(bf16[8,64,128]{2,1,0:T(8,128)(2,1)S(1)} %collective-permute-done.8.refs_6_), channel_id=1, source_target_pairs={{0,1},{1,0},{2,3},{3,2},{4,5},{5,4},{6,7},{7,6},{8,9},{9,8},{10,11... | collective-permute-start | bytes 393224 | tf_op jit(solution)/shard_map/ppermute | solution.py:199
  21.2 2.2 %collective-permute-start.13 = (bf16[8,64,128]{2,1,0:T(8,128)(2,1)S(1)}, bf16[8,64,128]{2,1,0:T(8,128)(2,1)S(1)}, u32[]{:S(2)}, u32[]{:S(2)}) collective-permute-start(bf16[8,64,128]{2,1,0:T(8,128)(2,1)S(1)} %collective-permute-done.9.refs_8_), channel_id=1, source_target_pairs={{0,1},{1,0},{2,3},{3,2},{4,5},{5,4},{6,7},{7,6},{8,9},{9,8},{10,11... | collective-permute-start | bytes 393224 | tf_op jit(solution)/shard_map/ppermute | solution.py:199
  23.3 1.3 %collective-permute-start.14 = (bf16[8,64,128]{2,1,0:T(8,128)(2,1)S(1)}, bf16[8,64,128]{2,1,0:T(8,128)(2,1)S(1)}, u32[]{:S(2)}, u32[]{:S(2)}) collective-permute-start(bf16[8,64,128]{2,1,0:T(8,128)(2,1)S(1)} %collective-permute-done.2.refs_4_), channel_id=1, source_target_pairs={{0,1},{1,0},{2,3},{3,2},{4,5},{5,4},{6,7},{7,6},{8,9},{9,8},{10,11... | collective-permute-start | bytes 393224 | tf_op jit(solution)/shard_map/ppermute | solution.py:199

commit v22 on v19

--- a/solution.py
+++ b/solution.py
@@ -18,9 +18,12 @@
     return name[1] | CORE, name[0] | CORE
 
 
-EARLY = (OWN, SIDE, BESIDE, BEYOND, CORNER, FIRST, SECOND, partner(OWN), partner(SIDE), partner(BESIDE), partner(CORNER))
-MIDDLE = (partner(BEYOND), partner(FIRST), partner(SECOND), END)
+MIDDLE = (CORNER, partner(CORNER), partner(BEYOND), partner(FIRST), partner(SECOND), END)
 LAST = (partner(END),)
+EARLY = tuple(name for name in (
+    OWN, SIDE, BESIDE, BEYOND, CORNER, FIRST, SECOND,
+    partner(OWN), partner(SIDE), partner(BESIDE), partner(BEYOND), partner(CORNER), partner(FIRST), partner(SECOND),
+) if name not in MIDDLE)
 ORDER = EARLY + MIDDLE + LAST
 
 
@@ -278,11 +281,12 @@
                 pieces[partner(name)] = swap(pieces[name], CORE, CORE)
 
         pass_on((OWN, BEYOND), (OWN, BESIDE), (OWN, SIDE))
-        held = (OWN, BESIDE,)
+        share(OWN)
+        held = (BEYOND,)
         half, ends = lax.optimization_barrier((half, [pieces[name] for name in held]))
         pieces.update(zip(held, ends))
-        pass_on((BESIDE, CORNER), (BEYOND, FIRST), (BEYOND, SECOND), (FIRST, END))
-        share(OWN, BESIDE, SIDE, CORNER, BEYOND, FIRST, SECOND)
+        pass_on((BEYOND, FIRST), (BESIDE, CORNER), (BEYOND, SECOND), (FIRST, END))
+        share(BESIDE, SIDE, CORNER, FIRST, BEYOND, SECOND)
         early = [pieces[name] for name in EARLY]
     else:
         early = [lax.all_gather(pairs, "sec", axis=0, tiled=True)]

time: 26.9 us -> 24.8 us (0.922); the launches traced: 26.7 us -> 25.1 us
  waiting for transfers between devices: 6.57 us -> 3.37 us
  Pallas kernels: 7.78 us -> 8.62 us
  starting transfers between devices: 12.3 us -> 13 us
    ppermute x15, waiting for transfers between devices: 6.57 us -> 3.37 us  [swap(): lax.ppermute(piece, 'sec', [(i, i ^ (odd_bit if i & CORE else even_bit))...]
    ppermute x15, starting transfers between devices: 12.3 us -> 13 us  [swap(): lax.ppermute(piece, 'sec', [(i, i ^ (odd_bit if i & CORE else even_bit))...]
    pallas_call x1, Pallas kernels: 1.13 us -> 1.64 us  [per_device(): pl.pallas_call(last_kernel, out_shape=jax.ShapeDtypeStruct(psi.shape, jnp...]
    pallas_call x1, Pallas kernels: 1.09 us -> 1.44 us  [per_device(): pl.pallas_call(middle_kernel, out_shape=jax.ShapeDtypeStruct(psi.shape, j...]
  transfers between devices with their start and end apart: 15 -> 15, of which waited for: 5 -> 5; matrix products, arithmetic and copies ran while one was open for 0% -> 0% of each run, Pallas kernels for 21% -> 23%
where the time goes in v22:
time: 24.8 us; the launch traced here: 25.1 us
  starting transfers between devices  13 us (52%)
  Pallas kernels  8.62 us (35%)
  waiting for transfers between devices  3.37 us (14%)
    ppermute x15, starting transfers between devices, swap(): lax.ppermute(piece, 'sec', [(i, i ^ (odd_bit if i & CORE else even_bit))...  13 us
    ppermute x15, waiting for transfers between devices, swap(): lax.ppermute(piece, 'sec', [(i, i ^ (odd_bit if i & CORE else even_bit))...  3.37 us
    pallas_call x1, Pallas kernels, per_device(): pl.pallas_call(functools.partial(left_kernel, pair_count, len(EARLY if by...  2.85 us
    pallas_call x1, Pallas kernels, per_device(): pl.pallas_call(last_kernel, out_shape=jax.ShapeDtypeStruct(psi.shape, jnp...  1.64 us
    pallas_call x1, Pallas kernels, per_device(): pl.pallas_call(early_kernel, out_shape=jax.ShapeDtypeStruct(psi.shape, jn...  1.6 us
    pallas_call x1, Pallas kernels, per_device(): pl.pallas_call(middle_kernel, out_shape=jax.ShapeDtypeStruct(psi.shape, j...  1.44 us
    pallas_call x1, Pallas kernels, per_device(): pl.pallas_call(pack_kernel, out_shape=jax.ShapeDtypeStruct((pair_count, t...  1.09 us
  transfers between devices with their start and end apart: 15, of which 5 were waited for; matrix products, arithmetic and copies ran while one was open for 0% of the time, Pallas kernels for 23%

profile of v22, /device:TPU:0, one launch (start us, length us, event | category | flops | bytes accessed | tf_op | source)
XLA Modules:
  0.0 25.1 jit_solution(1462849321226689881)
XLA Ops:
  0.0 1.1 %shard_map.83.refs_0_ = bf16[8,64,128]{2,1,0:T(8,128)(2,1)S(1)} custom-call(s32[16]{0:T(128)} %dims_hbm.3, bf16[16,64,64]{2,1,0:T(8,128)(2,1)} %right_hbm.1), custom_call_target="tpu_custom_call" | custom-call | bytes 131072 | tf_op jit(solution)/shard_map/pallas_call | solution.py:234
  1.1 4.1 %collective-permute-start = (bf16[8,64,128]{2,1,0:T(8,128)(2,1)S(1)}, bf16[8,64,128]{2,1,0:T(8,128)(2,1)S(1)}, u32[]{:S(2)}, u32[]{:S(2)}) collective-permute-start(bf16[8,64,128]{2,1,0:T(8,128)(2,1)S(1)} %shard_map.83.refs_0_), channel_id=1, source_target_pairs={{0,8},{1,9},{2,10},{3,11},{4,12},{5,13},{6,14},{7,15},{8,0},{9,1},... | collective-permute-start | bytes 393224 | tf_op jit(solution)/shard_map/ppermute | solution.py:214
  5.2 0.0 collective-permute-start.6
  5.2 1.6 %collective-permute-start.4 = (bf16[8,64,128]{2,1,0:T(8,128)(2,1)S(1)}, bf16[8,64,128]{2,1,0:T(8,128)(2,1)S(1)}, u32[]{:S(2)}, u32[]{:S(2)}) collective-permute-start(bf16[8,64,128]{2,1,0:T(8,128)(2,1)S(1)} %shard_map.83.refs_0_), channel_id=1, source_target_pairs={{0,4},{1,5},{2,6},{3,7},{4,0},{5,1},{6,2},{7,3},{8,12},{9,13},{10,... | collective-permute-start | bytes 393224 | tf_op jit(solution)/shard_map/ppermute | solution.py:214
  6.8 1.5 %collective-permute-start.3 = (bf16[8,64,128]{2,1,0:T(8,128)(2,1)S(1)}, bf16[8,64,128]{2,1,0:T(8,128)(2,1)S(1)}, u32[]{:S(2)}, u32[]{:S(2)}) collective-permute-start(bf16[8,64,128]{2,1,0:T(8,128)(2,1)S(1)} %shard_map.83.refs_0_), channel_id=1, source_target_pairs={{0,2},{1,3},{2,0},{3,1},{4,6},{5,7},{6,4},{7,5},{8,10},{9,11},{10,... | collective-permute-start | bytes 393224 | tf_op jit(solution)/shard_map/ppermute | solution.py:214
  8.3 2.9 %shard_map.82 = (bf16[8,8,64,128]{3,2,1,0:T(8,128)(2,1)S(1)}, s32[202]{0:T(256)S(4)}) custom-call(s32[8]{0:T(128)} %dims_hbm.2, s32[8,8]{1,0:T(8,128)} %bitcast.1, s32[8,8]{1,0:T(8,128)} %owner_hbm.1, s32[8,8]{1,0:T(8,128)} %slot_hbm.1, bf16[8,64,64]{2,1,0:T(8,128)(2,1)} %left_hbm.1, bf16[8,8,64,128]{3,2,1,0:T(8,128)(2,1)} %psi_hbm.1), custom_call_target="tpu_custom_call" | custom-call | flops 67108864 | bytes 1048576 | tf_op jit(solution)/shard_map/pallas_call | solution.py:249
  11.1 0.5 %collective-permute-done.refs_3_ = bf16[8,64,128]{2,1,0:T(8,128)(2,1)S(1)} collective-permute-done((bf16[8,64,128]{2,1,0:T(8,128)(2,1)S(1)}, bf16[8,64,128]{2,1,0:T(8,128)(2,1)S(1)}, u32[]{:S(2)}, u32[]{:S(2)}) %collective-permute-start) | collective-permute-done | bytes 131104 | tf_op jit(solution)/shard_map/ppermute | solution.py:214
  11.6 0.7 %collective-permute-start.1 = (bf16[8,64,128]{2,1,0:T(8,128)(2,1)S(1)}, bf16[8,64,128]{2,1,0:T(8,128)(2,1)S(1)}, u32[]{:S(2)}, u32[]{:S(2)}) collective-permute-start(bf16[8,64,128]{2,1,0:T(8,128)(2,1)S(1)} %collective-permute-done.refs_3_), channel_id=1, source_target_pairs={{0,4},{1,3},{2,6},{3,1},{4,0},{5,7},{6,2},{7,5},{8,12},{9,11},{10,... | collective-permute-start | bytes 393224 | tf_op jit(solution)/shard_map/ppermute | solution.py:214
  12.3 0.5 %collective-permute-done.4.refs_2_ = bf16[8,64,128]{2,1,0:T(8,128)(2,1)S(1)} collective-permute-done((bf16[8,64,128]{2,1,0:T(8,128)(2,1)S(1)}, bf16[8,64,128]{2,1,0:T(8,128)(2,1)S(1)}, u32[]{:S(2)}, u32[]{:S(2)}) %collective-permute-start.4) | collective-permute-done | bytes 131104 | tf_op jit(solution)/shard_map/ppermute | solution.py:214
  12.8 1.5 %collective-permute-start.9 = (bf16[8,64,128]{2,1,0:T(8,128)(2,1)S(1)}, bf16[8,64,128]{2,1,0:T(8,128)(2,1)S(1)}, u32[]{:S(2)}, u32[]{:S(2)}) collective-permute-start(bf16[8,64,128]{2,1,0:T(8,128)(2,1)S(1)} %collective-permute-done.4.refs_2_), channel_id=1, source_target_pairs={{0,2},{1,3},{2,0},{3,1},{4,6},{5,7},{6,4},{7,5},{8,10},{9,11},{10,... | collective-permute-start | bytes 393224 | tf_op jit(solution)/shard_map/ppermute | solution.py:214
  14.3 0.0 collective-permute-start.8
  14.3 0.0 collective-permute-done.3.refs_1_
  14.3 0.5 %collective-permute-start.7 = (bf16[8,64,128]{2,1,0:T(8,128)(2,1)S(1)}, bf16[8,64,128]{2,1,0:T(8,128)(2,1)S(1)}, u32[]{:S(2)}, u32[]{:S(2)}) collective-permute-start(bf16[8,64,128]{2,1,0:T(8,128)(2,1)S(1)} %collective-permute-done.3.refs_1_), channel_id=1, source_target_pairs={{0,1},{1,0},{2,3},{3,2},{4,5},{5,4},{6,7},{7,6},{8,9},{9,8},{10,11... | collective-permute-start | bytes 393224 | tf_op jit(solution)/shard_map/ppermute | solution.py:214
  14.8 0.0 collective-permute-done.6.refs_6_
  14.8 0.5 %collective-permute-start.5 = (bf16[8,64,128]{2,1,0:T(8,128)(2,1)S(1)}, bf16[8,64,128]{2,1,0:T(8,128)(2,1)S(1)}, u32[]{:S(2)}, u32[]{:S(2)}) collective-permute-start(bf16[8,64,128]{2,1,0:T(8,128)(2,1)S(1)} %collective-permute-done.refs_3_), channel_id=1, source_target_pairs={{0,2},{1,5},{2,0},{3,7},{4,6},{5,1},{6,4},{7,3},{8,10},{9,13},{10,... | collective-permute-start | bytes 393224 | tf_op jit(solution)/shard_map/ppermute | solution.py:214
  15.3 1.3 %collective-permute-done.1.refs_4_ = bf16[8,64,128]{2,1,0:T(8,128)(2,1)S(1)} collective-permute-done((bf16[8,64,128]{2,1,0:T(8,128)(2,1)S(1)}, bf16[8,64,128]{2,1,0:T(8,128)(2,1)S(1)}, u32[]{:S(2)}, u32[]{:S(2)}) %collective-permute-start.1) | collective-permute-done | bytes 131104 | tf_op jit(solution)/shard_map/ppermute | solution.py:214
  16.6 1.7 %collective-permute-start.2 = (bf16[8,64,128]{2,1,0:T(8,128)(2,1)S(1)}, bf16[8,64,128]{2,1,0:T(8,128)(2,1)S(1)}, u32[]{:S(2)}, u32[]{:S(2)}) collective-permute-start(bf16[8,64,128]{2,1,0:T(8,128)(2,1)S(1)} %collective-permute-done.1.refs_4_), channel_id=1, source_target_pairs={{0,2},{1,5},{2,0},{3,7},{4,6},{5,1},{6,4},{7,3},{8,10},{9,13},{10,... | collective-permute-start | bytes 393224 | tf_op jit(solution)/shard_map/ppermute | solution.py:214
  18.2 0.0 collective-permute-done.9.refs_0_
  18.2 0.0 collective-permute-start.11
  18.3 0.0 collective-permute-done.8.refs_8_
  18.3 0.5 %collective-permute-start.12 = (bf16[8,64,128]{2,1,0:T(8,128)(2,1)S(1)}, bf16[8,64,128]{2,1,0:T(8,128)(2,1)S(1)}, u32[]{:S(2)}, u32[]{:S(2)}) collective-permute-start(bf16[8,64,128]{2,1,0:T(8,128)(2,1)S(1)} %collective-permute-done.1.refs_4_), channel_id=1, source_target_pairs={{0,1},{1,0},{2,3},{3,2},{4,5},{5,4},{6,7},{7,6},{8,9},{9,8},{10,11... | collective-permute-start | bytes 393224 | tf_op jit(solution)/shard_map/ppermute | solution.py:214
  18.8 0.0 collective-permute-done.7.refs_7_
  18.8 0.1 collective-permute-start.10
  18.8 1.0 %collective-permute-done.5.refs_5_ = bf16[8,64,128]{2,1,0:T(8,128)(2,1)S(1)} collective-permute-done((bf16[8,64,128]{2,1,0:T(8,128)(2,1)S(1)}, bf16[8,64,128]{2,1,0:T(8,128)(2,1)S(1)}, u32[]{:S(2)}, u32[]{:S(2)}) %collective-permute-start.5) | collective-permute-done | bytes 131104 | tf_op jit(solution)/shard_map/ppermute | solution.py:214
  19.8 0.0 collective-permute-start.13
  19.8 1.6 %shard_map.84.early_ref = bf16[8,8,64,128]{3,2,1,0:T(8,128)(2,1)S(1)} custom-call(s32[202]{0:T(256)S(4)} %get-tuple-element.11.list_ref, bf16[8,8,64,128]{3,2,1,0:T(8,128)(2,1)S(1)} %get-tuple-element.14.half_ref, bf16[8,64,128]{2,1,0:T(8,128)(2,1)S(1)} %shard_map.83.refs_0_, bf16[8,64,128]{2,1,0:T(8,128)(2,1)S(1)} %collective-permute-done.3.refs_1_, ...), custom_call_target="tpu_custom_call" | custom-call | flops 67108864 | bytes 1048576 | tf_op jit(solution)/shard_map/pallas_call | solution.py:294
  21.4 0.1 collective-permute-done.2.refs_5_
  21.6 0.4 %collective-permute-start.14 = (bf16[8,64,128]{2,1,0:T(8,128)(2,1)S(1)}, bf16[8,64,128]{2,1,0:T(8,128)(2,1)S(1)}, u32[]{:S(2)}, u32[]{:S(2)}) collective-permute-start(bf16[8,64,128]{2,1,0:T(8,128)(2,1)S(1)} %collective-permute-done.2.refs_5_), channel_id=1, source_target_pairs={{0,1},{1,0},{2,3},{3,2},{4,5},{5,4},{6,7},{7,6},{8,9},{9,8},{10,11... | collective-permute-start | bytes 393224 | tf_op jit(solution)/shard_map/ppermute | solution.py:214
  22.0 0.0 collective-permute-done.11.refs_2_
  22.0 0.0 collective-permute-done.10.refs_1_
  22.0 0.0 collective-permute-done.13.refs_4_
  22.0 0.0 collective-permute-done.12.refs_3_
  22.0 1.4 %shard_map.85.middle_ref = bf16[8,8,64,128]{3,2,1,0:T(8,128)(2,1)S(1)} custom-call(s32[202]{0:T(256)S(4)} %get-tuple-element.11.list_ref, bf16[8,8,64,128]{3,2,1,0:T(8,128)(2,1)S(1)} %shard_map.84.early_ref, bf16[8,8,64,128]{3,2,1,0:T(8,128)(2,1)S(1)} %get-tuple-element.14.half_ref, bf16[8,64,128]{2,1,0:T(8,128)(2,1)S(1)} %collective-permute-done.9.refs_0_, ...), custom_call_target="tpu_custom_call" | custom-call | flops 16777216 | bytes 262144 | tf_op jit(solution)/shard_map/pallas_call | solution.py:306
  23.5 0.0 collective-permute-done.14.pairs_ref
  23.5 1.6 %shard_map.86 = bf16[8,8,64,128]{3,2,1,0:T(8,128)(2,1)} custom-call(s32[202]{0:T(256)S(4)} %get-tuple-element.11.list_ref, bf16[8,8,64,128]{3,2,1,0:T(8,128)(2,1)S(1)} %shard_map.85.middle_ref, bf16[8,8,64,128]{3,2,1,0:T(8,128)(2,1)S(1)} %get-tuple-element.14.half_ref, bf16[8,64,128]{2,1,0:T(8,128)(2,1)S(1)} %collective-permute-done.14.pairs_ref), custom_call_target="tpu_custom_call" | custom-call | flops 4194304 | bytes 1048576 | tf_op jit(solution)/shard_map/pallas_call | solution.py:315
Async XLA Ops:
  1.1 10.5 %collective-permute-start = (bf16[8,64,128]{2,1,0:T(8,128)(2,1)S(1)}, bf16[8,64,128]{2,1,0:T(8,128)(2,1)S(1)}, u32[]{:S(2)}, u32[]{:S(2)}) collective-permute-start(bf16[8,64,128]{2,1,0:T(8,128)(2,1)S(1)} %shard_map.83.refs_0_), channel_id=1, source_target_pairs={{0,8},{1,9},{2,10},{3,11},{4,12},{5,13},{6,14},{7,15},{8,0},{9,1},... | collective-permute-start | bytes 393224 | tf_op jit(solution)/shard_map/ppermute | solution.py:214
  5.2 9.6 %collective-permute-start.6 = (bf16[8,64,128]{2,1,0:T(8,128)(2,1)S(1)}, bf16[8,64,128]{2,1,0:T(8,128)(2,1)S(1)}, u32[]{:S(2)}, u32[]{:S(2)}) collective-permute-start(bf16[8,64,128]{2,1,0:T(8,128)(2,1)S(1)} %shard_map.83.refs_0_), channel_id=1, source_target_pairs={{0,1},{1,0},{2,3},{3,2},{4,5},{5,4},{6,7},{7,6},{8,9},{9,8},{10,11... | collective-permute-start | bytes 393224 | tf_op jit(solution)/shard_map/ppermute | solution.py:214
  5.2 7.6 %collective-permute-start.4 = (bf16[8,64,128]{2,1,0:T(8,128)(2,1)S(1)}, bf16[8,64,128]{2,1,0:T(8,128)(2,1)S(1)}, u32[]{:S(2)}, u32[]{:S(2)}) collective-permute-start(bf16[8,64,128]{2,1,0:T(8,128)(2,1)S(1)} %shard_map.83.refs_0_), channel_id=1, source_target_pairs={{0,4},{1,5},{2,6},{3,7},{4,0},{5,1},{6,2},{7,3},{8,12},{9,13},{10,... | collective-permute-start | bytes 393224 | tf_op jit(solution)/shard_map/ppermute | solution.py:214
  6.8 7.5 %collective-permute-start.3 = (bf16[8,64,128]{2,1,0:T(8,128)(2,1)S(1)}, bf16[8,64,128]{2,1,0:T(8,128)(2,1)S(1)}, u32[]{:S(2)}, u32[]{:S(2)}) collective-permute-start(bf16[8,64,128]{2,1,0:T(8,128)(2,1)S(1)} %shard_map.83.refs_0_), channel_id=1, source_target_pairs={{0,2},{1,3},{2,0},{3,1},{4,6},{5,7},{6,4},{7,5},{8,10},{9,11},{10,... | collective-permute-start | bytes 393224 | tf_op jit(solution)/shard_map/ppermute | solution.py:214
  11.6 5.0 %collective-permute-start.1 = (bf16[8,64,128]{2,1,0:T(8,128)(2,1)S(1)}, bf16[8,64,128]{2,1,0:T(8,128)(2,1)S(1)}, u32[]{:S(2)}, u32[]{:S(2)}) collective-permute-start(bf16[8,64,128]{2,1,0:T(8,128)(2,1)S(1)} %collective-permute-done.refs_3_), channel_id=1, source_target_pairs={{0,4},{1,3},{2,6},{3,1},{4,0},{5,7},{6,2},{7,5},{8,12},{9,11},{10,... | collective-permute-start | bytes 393224 | tf_op jit(solution)/shard_map/ppermute | solution.py:214
  12.8 5.5 %collective-permute-start.9 = (bf16[8,64,128]{2,1,0:T(8,128)(2,1)S(1)}, bf16[8,64,128]{2,1,0:T(8,128)(2,1)S(1)}, u32[]{:S(2)}, u32[]{:S(2)}) collective-permute-start(bf16[8,64,128]{2,1,0:T(8,128)(2,1)S(1)} %collective-permute-done.4.refs_2_), channel_id=1, source_target_pairs={{0,2},{1,3},{2,0},{3,1},{4,6},{5,7},{6,4},{7,5},{8,10},{9,11},{10,... | collective-permute-start | bytes 393224 | tf_op jit(solution)/shard_map/ppermute | solution.py:214
  14.3 4.0 %collective-permute-start.8 = (bf16[8,64,128]{2,1,0:T(8,128)(2,1)S(1)}, bf16[8,64,128]{2,1,0:T(8,128)(2,1)S(1)}, u32[]{:S(2)}, u32[]{:S(2)}) collective-permute-start(bf16[8,64,128]{2,1,0:T(8,128)(2,1)S(1)} %collective-permute-done.4.refs_2_), channel_id=1, source_target_pairs={{0,1},{1,0},{2,3},{3,2},{4,5},{5,4},{6,7},{7,6},{8,9},{9,8},{10,11... | collective-permute-start | bytes 393224 | tf_op jit(solution)/shard_map/ppermute | solution.py:214
  14.3 4.5 %collective-permute-start.7 = (bf16[8,64,128]{2,1,0:T(8,128)(2,1)S(1)}, bf16[8,64,128]{2,1,0:T(8,128)(2,1)S(1)}, u32[]{:S(2)}, u32[]{:S(2)}) collective-permute-start(bf16[8,64,128]{2,1,0:T(8,128)(2,1)S(1)} %collective-permute-done.3.refs_1_), channel_id=1, source_target_pairs={{0,1},{1,0},{2,3},{3,2},{4,5},{5,4},{6,7},{7,6},{8,9},{9,8},{10,11... | collective-permute-start | bytes 393224 | tf_op jit(solution)/shard_map/ppermute | solution.py:214
  14.8 5.0 %collective-permute-start.5 = (bf16[8,64,128]{2,1,0:T(8,128)(2,1)S(1)}, bf16[8,64,128]{2,1,0:T(8,128)(2,1)S(1)}, u32[]{:S(2)}, u32[]{:S(2)}) collective-permute-start(bf16[8,64,128]{2,1,0:T(8,128)(2,1)S(1)} %collective-permute-done.refs_3_), channel_id=1, source_target_pairs={{0,2},{1,5},{2,0},{3,7},{4,6},{5,1},{6,4},{7,3},{8,10},{9,13},{10,... | collective-permute-start | bytes 393224 | tf_op jit(solution)/shard_map/ppermute | solution.py:214
  16.6 5.0 %collective-permute-start.2 = (bf16[8,64,128]{2,1,0:T(8,128)(2,1)S(1)}, bf16[8,64,128]{2,1,0:T(8,128)(2,1)S(1)}, u32[]{:S(2)}, u32[]{:S(2)}) collective-permute-start(bf16[8,64,128]{2,1,0:T(8,128)(2,1)S(1)} %collective-permute-done.1.refs_4_), channel_id=1, source_target_pairs={{0,2},{1,5},{2,0},{3,7},{4,6},{5,1},{6,4},{7,3},{8,10},{9,13},{10,... | collective-permute-start | bytes 393224 | tf_op jit(solution)/shard_map/ppermute | solution.py:214
  18.2 3.7 %collective-permute-start.11 = (bf16[8,64,128]{2,1,0:T(8,128)(2,1)S(1)}, bf16[8,64,128]{2,1,0:T(8,128)(2,1)S(1)}, u32[]{:S(2)}, u32[]{:S(2)}) collective-permute-start(bf16[8,64,128]{2,1,0:T(8,128)(2,1)S(1)} %collective-permute-done.refs_3_), channel_id=1, source_target_pairs={{0,1},{1,0},{2,3},{3,2},{4,5},{5,4},{6,7},{7,6},{8,9},{9,8},{10,11... | collective-permute-start | bytes 393224 | tf_op jit(solution)/shard_map/ppermute | solution.py:214
  18.3 3.7 %collective-permute-start.12 = (bf16[8,64,128]{2,1,0:T(8,128)(2,1)S(1)}, bf16[8,64,128]{2,1,0:T(8,128)(2,1)S(1)}, u32[]{:S(2)}, u32[]{:S(2)}) collective-permute-start(bf16[8,64,128]{2,1,0:T(8,128)(2,1)S(1)} %collective-permute-done.1.refs_4_), channel_id=1, source_target_pairs={{0,1},{1,0},{2,3},{3,2},{4,5},{5,4},{6,7},{7,6},{8,9},{9,8},{10,11... | collective-permute-start | bytes 393224 | tf_op jit(solution)/shard_map/ppermute | solution.py:214
  18.8 3.2 %collective-permute-start.10 = (bf16[8,64,128]{2,1,0:T(8,128)(2,1)S(1)}, bf16[8,64,128]{2,1,0:T(8,128)(2,1)S(1)}, u32[]{:S(2)}, u32[]{:S(2)}) collective-permute-start(bf16[8,64,128]{2,1,0:T(8,128)(2,1)S(1)} %collective-permute-done.9.refs_0_), channel_id=1, source_target_pairs={{0,1},{1,0},{2,3},{3,2},{4,5},{5,4},{6,7},{7,6},{8,9},{9,8},{10,11... | collective-permute-start | bytes 393224 | tf_op jit(solution)/shard_map/ppermute | solution.py:214
  19.8 2.2 %collective-permute-start.13 = (bf16[8,64,128]{2,1,0:T(8,128)(2,1)S(1)}, bf16[8,64,128]{2,1,0:T(8,128)(2,1)S(1)}, u32[]{:S(2)}, u32[]{:S(2)}) collective-permute-start(bf16[8,64,128]{2,1,0:T(8,128)(2,1)S(1)} %collective-permute-done.5.refs_5_), channel_id=1, source_target_pairs={{0,1},{1,0},{2,3},{3,2},{4,5},{5,4},{6,7},{7,6},{8,9},{9,8},{10,11... | collective-permute-start | bytes 393224 | tf_op jit(solution)/shard_map/ppermute | solution.py:214
  21.6 1.9 %collective-permute-start.14 = (bf16[8,64,128]{2,1,0:T(8,128)(2,1)S(1)}, bf16[8,64,128]{2,1,0:T(8,128)(2,1)S(1)}, u32[]{:S(2)}, u32[]{:S(2)}) collective-permute-start(bf16[8,64,128]{2,1,0:T(8,128)(2,1)S(1)} %collective-permute-done.2.refs_5_), channel_id=1, source_target_pairs={{0,1},{1,0},{2,3},{3,2},{4,5},{5,4},{6,7},{7,6},{8,9},{9,8},{10,11... | collective-permute-start | bytes 393224 | tf_op jit(solution)/shard_map/ppermute | solution.py:214

commit v23 on v22

--- a/solution.py
+++ b/solution.py
@@ -18,7 +18,7 @@
     return name[1] | CORE, name[0] | CORE
 
 
-MIDDLE = (CORNER, partner(CORNER), partner(BEYOND), partner(FIRST), partner(SECOND), END)
+MIDDLE = (partner(CORNER), partner(BEYOND), partner(FIRST), partner(SECOND), END)
 LAST = (partner(END),)
 EARLY = tuple(name for name in (
     OWN, SIDE, BESIDE, BEYOND, CORNER, FIRST, SECOND,
@@ -177,7 +177,7 @@
     piece_refs, (out_ref, pairs_ref) = refs[:-2], refs[-2:]
     out_ref[...] = early_ref[...]
     merge(piece_refs, pairs_ref)
-    listed_products(8, 0, list_ref, half_ref, pairs_ref, out_ref)
+    listed_products(16, 0, list_ref, half_ref, pairs_ref, out_ref)
 
 
 def last_kernel(list_ref, middle_ref, half_ref, pairs_ref, out_hbm, out_ref, sems):
@@ -198,7 +198,7 @@
         def _():
             store(a, middle_ref).start()
 
-    listed_products(4, items + 1, list_ref, half_ref, pairs_ref, out_ref)
+    listed_products(8, items + 1, list_ref, half_ref, pairs_ref, out_ref)
     for a in range(sectors):
 
         @pl.when(list_ref[2 * items + 2 + a] > 0)

time: 24.8 us -> 24.9 us (level); the launches traced: 25.1 us -> 24.8 us
  Pallas kernels: 8.62 us -> 8.03 us
  waiting for transfers between devices: 3.37 us -> 3.79 us
    ppermute x15, waiting for transfers between devices: 3.37 us -> 3.79 us  [swap(): lax.ppermute(piece, 'sec', [(i, i ^ (odd_bit if i & CORE else even_bit))...]
    pallas_call x1, Pallas kernels: 1.44 us -> 1.04 us  [per_device(): pl.pallas_call(middle_kernel, out_shape=jax.ShapeDtypeStruct(psi.shape, j...]
  transfers between devices with their start and end apart: 15 -> 15, of which waited for: 5 -> 5; matrix products, arithmetic and copies ran while one was open for 0% -> 0% of each run, Pallas kernels for 23% -> 22%
where the time goes in v23:
time: 24.9 us; the launch traced here: 24.8 us
  starting transfers between devices  12.9 us (52%)
  Pallas kernels  8.03 us (32%)
  waiting for transfers between devices  3.79 us (15%)
    ppermute x15, starting transfers between devices, swap(): lax.ppermute(piece, 'sec', [(i, i ^ (odd_bit if i & CORE else even_bit))...  12.9 us
    ppermute x15, waiting for transfers between devices, swap(): lax.ppermute(piece, 'sec', [(i, i ^ (odd_bit if i & CORE else even_bit))...  3.79 us
    pallas_call x1, Pallas kernels, per_device(): pl.pallas_call(functools.partial(left_kernel, pair_count, len(EARLY if by...  2.85 us
    pallas_call x1, Pallas kernels, per_device(): pl.pallas_call(early_kernel, out_shape=jax.ShapeDtypeStruct(psi.shape, jn...  1.61 us
    pallas_call x1, Pallas kernels, per_device(): pl.pallas_call(last_kernel, out_shape=jax.ShapeDtypeStruct(psi.shape, jnp...  1.44 us
    pallas_call x1, Pallas kernels, per_device(): pl.pallas_call(pack_kernel, out_shape=jax.ShapeDtypeStruct((pair_count, t...  1.09 us
    pallas_call x1, Pallas kernels, per_device(): pl.pallas_call(middle_kernel, out_shape=jax.ShapeDtypeStruct(psi.shape, j...  1.04 us
  transfers between devices with their start and end apart: 15, of which 5 were waited for; matrix products, arithmetic and copies ran while one was open for 0% of the time, Pallas kernels for 22%

profile of v23, /device:TPU:0, one launch (start us, length us, event | category | flops | bytes accessed | tf_op | source)
XLA Modules:
  0.0 24.8 jit_solution(4986603512233694478)
XLA Ops:
  0.0 1.1 %shard_map.83.refs_0_ = bf16[8,64,128]{2,1,0:T(8,128)(2,1)S(1)} custom-call(s32[16]{0:T(128)} %dims_hbm.3, bf16[16,64,64]{2,1,0:T(8,128)(2,1)} %right_hbm.1), custom_call_target="tpu_custom_call" | custom-call | bytes 131072 | tf_op jit(solution)/shard_map/pallas_call | solution.py:234
  1.1 4.1 %collective-permute-start = (bf16[8,64,128]{2,1,0:T(8,128)(2,1)S(1)}, bf16[8,64,128]{2,1,0:T(8,128)(2,1)S(1)}, u32[]{:S(2)}, u32[]{:S(2)}) collective-permute-start(bf16[8,64,128]{2,1,0:T(8,128)(2,1)S(1)} %shard_map.83.refs_0_), channel_id=1, source_target_pairs={{0,8},{1,9},{2,10},{3,11},{4,12},{5,13},{6,14},{7,15},{8,0},{9,1},... | collective-permute-start | bytes 393224 | tf_op jit(solution)/shard_map/ppermute | solution.py:214
  5.2 0.0 collective-permute-start.7
  5.2 1.6 %collective-permute-start.4 = (bf16[8,64,128]{2,1,0:T(8,128)(2,1)S(1)}, bf16[8,64,128]{2,1,0:T(8,128)(2,1)S(1)}, u32[]{:S(2)}, u32[]{:S(2)}) collective-permute-start(bf16[8,64,128]{2,1,0:T(8,128)(2,1)S(1)} %shard_map.83.refs_0_), channel_id=1, source_target_pairs={{0,4},{1,5},{2,6},{3,7},{4,0},{5,1},{6,2},{7,3},{8,12},{9,13},{10,... | collective-permute-start | bytes 393224 | tf_op jit(solution)/shard_map/ppermute | solution.py:214
  6.8 1.5 %collective-permute-start.3 = (bf16[8,64,128]{2,1,0:T(8,128)(2,1)S(1)}, bf16[8,64,128]{2,1,0:T(8,128)(2,1)S(1)}, u32[]{:S(2)}, u32[]{:S(2)}) collective-permute-start(bf16[8,64,128]{2,1,0:T(8,128)(2,1)S(1)} %shard_map.83.refs_0_), channel_id=1, source_target_pairs={{0,2},{1,3},{2,0},{3,1},{4,6},{5,7},{6,4},{7,5},{8,10},{9,11},{10,... | collective-permute-start | bytes 393224 | tf_op jit(solution)/shard_map/ppermute | solution.py:214
  8.3 2.9 %shard_map.82 = (bf16[8,8,64,128]{3,2,1,0:T(8,128)(2,1)S(1)}, s32[202]{0:T(256)S(4)}) custom-call(s32[8]{0:T(128)} %dims_hbm.2, s32[8,8]{1,0:T(8,128)} %bitcast.1, s32[8,8]{1,0:T(8,128)} %owner_hbm.1, s32[8,8]{1,0:T(8,128)} %slot_hbm.1, bf16[8,64,64]{2,1,0:T(8,128)(2,1)} %left_hbm.1, bf16[8,8,64,128]{3,2,1,0:T(8,128)(2,1)} %psi_hbm.1), custom_call_target="tpu_custom_call" | custom-call | flops 67108864 | bytes 1048576 | tf_op jit(solution)/shard_map/pallas_call | solution.py:249
  11.1 0.5 %collective-permute-done.refs_3_ = bf16[8,64,128]{2,1,0:T(8,128)(2,1)S(1)} collective-permute-done((bf16[8,64,128]{2,1,0:T(8,128)(2,1)S(1)}, bf16[8,64,128]{2,1,0:T(8,128)(2,1)S(1)}, u32[]{:S(2)}, u32[]{:S(2)}) %collective-permute-start) | collective-permute-done | bytes 131104 | tf_op jit(solution)/shard_map/ppermute | solution.py:214
  11.6 0.7 %collective-permute-start.1 = (bf16[8,64,128]{2,1,0:T(8,128)(2,1)S(1)}, bf16[8,64,128]{2,1,0:T(8,128)(2,1)S(1)}, u32[]{:S(2)}, u32[]{:S(2)}) collective-permute-start(bf16[8,64,128]{2,1,0:T(8,128)(2,1)S(1)} %collective-permute-done.refs_3_), channel_id=1, source_target_pairs={{0,4},{1,3},{2,6},{3,1},{4,0},{5,7},{6,2},{7,5},{8,12},{9,11},{10,... | collective-permute-start | bytes 393224 | tf_op jit(solution)/shard_map/ppermute | solution.py:214
  12.3 0.5 %collective-permute-done.4.refs_2_ = bf16[8,64,128]{2,1,0:T(8,128)(2,1)S(1)} collective-permute-done((bf16[8,64,128]{2,1,0:T(8,128)(2,1)S(1)}, bf16[8,64,128]{2,1,0:T(8,128)(2,1)S(1)}, u32[]{:S(2)}, u32[]{:S(2)}) %collective-permute-start.4) | collective-permute-done | bytes 131104 | tf_op jit(solution)/shard_map/ppermute | solution.py:214
  12.8 0.0 collective-permute-start.9
  12.8 1.5 %collective-permute-start.5 = (bf16[8,64,128]{2,1,0:T(8,128)(2,1)S(1)}, bf16[8,64,128]{2,1,0:T(8,128)(2,1)S(1)}, u32[]{:S(2)}, u32[]{:S(2)}) collective-permute-start(bf16[8,64,128]{2,1,0:T(8,128)(2,1)S(1)} %collective-permute-done.4.refs_2_), channel_id=1, source_target_pairs={{0,2},{1,3},{2,0},{3,1},{4,6},{5,7},{6,4},{7,5},{8,10},{9,11},{10,... | collective-permute-start | bytes 393224 | tf_op jit(solution)/shard_map/ppermute | solution.py:214
  14.3 0.0 collective-permute-done.3.refs_1_
  14.3 0.2 collective-permute-start.8
  14.5 0.0 collective-permute-done.7.refs_7_
  14.5 0.5 %collective-permute-start.6 = (bf16[8,64,128]{2,1,0:T(8,128)(2,1)S(1)}, bf16[8,64,128]{2,1,0:T(8,128)(2,1)S(1)}, u32[]{:S(2)}, u32[]{:S(2)}) collective-permute-start(bf16[8,64,128]{2,1,0:T(8,128)(2,1)S(1)} %collective-permute-done.refs_3_), channel_id=1, source_target_pairs={{0,2},{1,5},{2,0},{3,7},{4,6},{5,1},{6,4},{7,3},{8,10},{9,13},{10,... | collective-permute-start | bytes 393224 | tf_op jit(solution)/shard_map/ppermute | solution.py:214
  15.0 1.6 %collective-permute-done.1.refs_5_ = bf16[8,64,128]{2,1,0:T(8,128)(2,1)S(1)} collective-permute-done((bf16[8,64,128]{2,1,0:T(8,128)(2,1)S(1)}, bf16[8,64,128]{2,1,0:T(8,128)(2,1)S(1)}, u32[]{:S(2)}, u32[]{:S(2)}) %collective-permute-start.1) | collective-permute-done | bytes 131104 | tf_op jit(solution)/shard_map/ppermute | solution.py:214
  16.6 1.7 %collective-permute-start.2 = (bf16[8,64,128]{2,1,0:T(8,128)(2,1)S(1)}, bf16[8,64,128]{2,1,0:T(8,128)(2,1)S(1)}, u32[]{:S(2)}, u32[]{:S(2)}) collective-permute-start(bf16[8,64,128]{2,1,0:T(8,128)(2,1)S(1)} %collective-permute-done.1.refs_5_), channel_id=1, source_target_pairs={{0,2},{1,5},{2,0},{3,7},{4,6},{5,1},{6,4},{7,3},{8,10},{9,13},{10,... | collective-permute-start | bytes 393224 | tf_op jit(solution)/shard_map/ppermute | solution.py:214
  18.3 0.0 collective-permute-done.9.refs_9_
  18.3 0.0 collective-permute-start.11
  18.3 0.3 %collective-permute-done.5.refs_4_ = bf16[8,64,128]{2,1,0:T(8,128)(2,1)S(1)} collective-permute-done((bf16[8,64,128]{2,1,0:T(8,128)(2,1)S(1)}, bf16[8,64,128]{2,1,0:T(8,128)(2,1)S(1)}, u32[]{:S(2)}, u32[]{:S(2)}) %collective-permute-start.5) | collective-permute-done | bytes 131104 | tf_op jit(solution)/shard_map/ppermute | solution.py:214
  18.7 0.2 collective-permute-start.12
  18.8 0.0 collective-permute-done.8.refs_8_
  18.8 0.3 %collective-permute-start.10 = (bf16[8,64,128]{2,1,0:T(8,128)(2,1)S(1)}, bf16[8,64,128]{2,1,0:T(8,128)(2,1)S(1)}, u32[]{:S(2)}, u32[]{:S(2)}) collective-permute-start(bf16[8,64,128]{2,1,0:T(8,128)(2,1)S(1)} %collective-permute-done.5.refs_4_), channel_id=1, source_target_pairs={{0,1},{1,0},{2,3},{3,2},{4,5},{5,4},{6,7},{7,6},{8,9},{9,8},{10,11... | collective-permute-start | bytes 393224 | tf_op jit(solution)/shard_map/ppermute | solution.py:214
  19.2 0.9 %collective-permute-done.6.refs_6_ = bf16[8,64,128]{2,1,0:T(8,128)(2,1)S(1)} collective-permute-done((bf16[8,64,128]{2,1,0:T(8,128)(2,1)S(1)}, bf16[8,64,128]{2,1,0:T(8,128)(2,1)S(1)}, u32[]{:S(2)}, u32[]{:S(2)}) %collective-permute-start.6) | collective-permute-done | bytes 131104 | tf_op jit(solution)/shard_map/ppermute | solution.py:214
  20.1 0.0 collective-permute-start.13
  20.1 1.6 %shard_map.84.early_ref = bf16[8,8,64,128]{3,2,1,0:T(8,128)(2,1)S(1)} custom-call(s32[202]{0:T(256)S(4)} %get-tuple-element.11.list_ref, bf16[8,8,64,128]{3,2,1,0:T(8,128)(2,1)S(1)} %get-tuple-element.14.half_ref, bf16[8,64,128]{2,1,0:T(8,128)(2,1)S(1)} %shard_map.83.refs_0_, bf16[8,64,128]{2,1,0:T(8,128)(2,1)S(1)} %collective-permute-done.3.refs_1_, ...), custom_call_target="tpu_custom_call" | custom-call | flops 67108864 | bytes 1048576 | tf_op jit(solution)/shard_map/pallas_call | solution.py:294
  21.7 0.0 collective-permute-done.2.refs_4_
  21.7 0.6 %collective-permute-start.14 = (bf16[8,64,128]{2,1,0:T(8,128)(2,1)S(1)}, bf16[8,64,128]{2,1,0:T(8,128)(2,1)S(1)}, u32[]{:S(2)}, u32[]{:S(2)}) collective-permute-start(bf16[8,64,128]{2,1,0:T(8,128)(2,1)S(1)} %collective-permute-done.2.refs_4_), channel_id=1, source_target_pairs={{0,1},{1,0},{2,3},{3,2},{4,5},{5,4},{6,7},{7,6},{8,9},{9,8},{10,11... | collective-permute-start | bytes 393224 | tf_op jit(solution)/shard_map/ppermute | solution.py:214
  22.3 0.0 collective-permute-done.11.refs_1_
  22.3 0.0 collective-permute-done.10.refs_0_
  22.3 0.0 collective-permute-done.13.refs_3_
  22.3 0.0 collective-permute-done.12.refs_2_
  22.3 1.0 %shard_map.85.middle_ref = bf16[8,8,64,128]{3,2,1,0:T(8,128)(2,1)S(1)} custom-call(s32[202]{0:T(256)S(4)} %get-tuple-element.11.list_ref, bf16[8,8,64,128]{3,2,1,0:T(8,128)(2,1)S(1)} %shard_map.84.early_ref, bf16[8,8,64,128]{3,2,1,0:T(8,128)(2,1)S(1)} %get-tuple-element.14.half_ref, bf16[8,64,128]{2,1,0:T(8,128)(2,1)S(1)} %collective-permute-done.10.refs_0_, ...), custom_call_target="tpu_custom_call" | custom-call | flops 16777216 | bytes 262144 | tf_op jit(solution)/shard_map/pallas_call | solution.py:306
  23.4 0.0 collective-permute-done.14.pairs_ref
  23.4 1.4 %shard_map.86 = bf16[8,8,64,128]{3,2,1,0:T(8,128)(2,1)} custom-call(s32[202]{0:T(256)S(4)} %get-tuple-element.11.list_ref, bf16[8,8,64,128]{3,2,1,0:T(8,128)(2,1)S(1)} %shard_map.85.middle_ref, bf16[8,8,64,128]{3,2,1,0:T(8,128)(2,1)S(1)} %get-tuple-element.14.half_ref, bf16[8,64,128]{2,1,0:T(8,128)(2,1)S(1)} %collective-permute-done.14.pairs_ref), custom_call_target="tpu_custom_call" | custom-call | flops 4194304 | bytes 1048576 | tf_op jit(solution)/shard_map/pallas_call | solution.py:315
Async XLA Ops:
  1.1 10.5 %collective-permute-start = (bf16[8,64,128]{2,1,0:T(8,128)(2,1)S(1)}, bf16[8,64,128]{2,1,0:T(8,128)(2,1)S(1)}, u32[]{:S(2)}, u32[]{:S(2)}) collective-permute-start(bf16[8,64,128]{2,1,0:T(8,128)(2,1)S(1)} %shard_map.83.refs_0_), channel_id=1, source_target_pairs={{0,8},{1,9},{2,10},{3,11},{4,12},{5,13},{6,14},{7,15},{8,0},{9,1},... | collective-permute-start | bytes 393224 | tf_op jit(solution)/shard_map/ppermute | solution.py:214
  5.2 9.3 %collective-permute-start.7 = (bf16[8,64,128]{2,1,0:T(8,128)(2,1)S(1)}, bf16[8,64,128]{2,1,0:T(8,128)(2,1)S(1)}, u32[]{:S(2)}, u32[]{:S(2)}) collective-permute-start(bf16[8,64,128]{2,1,0:T(8,128)(2,1)S(1)} %shard_map.83.refs_0_), channel_id=1, source_target_pairs={{0,1},{1,0},{2,3},{3,2},{4,5},{5,4},{6,7},{7,6},{8,9},{9,8},{10,11... | collective-permute-start | bytes 393224 | tf_op jit(solution)/shard_map/ppermute | solution.py:214
  5.2 7.6 %collective-permute-start.4 = (bf16[8,64,128]{2,1,0:T(8,128)(2,1)S(1)}, bf16[8,64,128]{2,1,0:T(8,128)(2,1)S(1)}, u32[]{:S(2)}, u32[]{:S(2)}) collective-permute-start(bf16[8,64,128]{2,1,0:T(8,128)(2,1)S(1)} %shard_map.83.refs_0_), channel_id=1, source_target_pairs={{0,4},{1,5},{2,6},{3,7},{4,0},{5,1},{6,2},{7,3},{8,12},{9,13},{10,... | collective-permute-start | bytes 393224 | tf_op jit(solution)/shard_map/ppermute | solution.py:214
  6.8 7.5 %collective-permute-start.3 = (bf16[8,64,128]{2,1,0:T(8,128)(2,1)S(1)}, bf16[8,64,128]{2,1,0:T(8,128)(2,1)S(1)}, u32[]{:S(2)}, u32[]{:S(2)}) collective-permute-start(bf16[8,64,128]{2,1,0:T(8,128)(2,1)S(1)} %shard_map.83.refs_0_), channel_id=1, source_target_pairs={{0,2},{1,3},{2,0},{3,1},{4,6},{5,7},{6,4},{7,5},{8,10},{9,11},{10,... | collective-permute-start | bytes 393224 | tf_op jit(solution)/shard_map/ppermute | solution.py:214
  11.6 5.0 %collective-permute-start.1 = (bf16[8,64,128]{2,1,0:T(8,128)(2,1)S(1)}, bf16[8,64,128]{2,1,0:T(8,128)(2,1)S(1)}, u32[]{:S(2)}, u32[]{:S(2)}) collective-permute-start(bf16[8,64,128]{2,1,0:T(8,128)(2,1)S(1)} %collective-permute-done.refs_3_), channel_id=1, source_target_pairs={{0,4},{1,3},{2,6},{3,1},{4,0},{5,7},{6,2},{7,5},{8,12},{9,11},{10,... | collective-permute-start | bytes 393224 | tf_op jit(solution)/shard_map/ppermute | solution.py:214
  12.8 5.6 %collective-permute-start.9 = (bf16[8,64,128]{2,1,0:T(8,128)(2,1)S(1)}, bf16[8,64,128]{2,1,0:T(8,128)(2,1)S(1)}, u32[]{:S(2)}, u32[]{:S(2)}) collective-permute-start(bf16[8,64,128]{2,1,0:T(8,128)(2,1)S(1)} %collective-permute-done.4.refs_2_), channel_id=1, source_target_pairs={{0,1},{1,0},{2,3},{3,2},{4,5},{5,4},{6,7},{7,6},{8,9},{9,8},{10,11... | collective-permute-start | bytes 393224 | tf_op jit(solution)/shard_map/ppermute | solution.py:214
  12.8 5.9 %collective-permute-start.5 = (bf16[8,64,128]{2,1,0:T(8,128)(2,1)S(1)}, bf16[8,64,128]{2,1,0:T(8,128)(2,1)S(1)}, u32[]{:S(2)}, u32[]{:S(2)}) collective-permute-start(bf16[8,64,128]{2,1,0:T(8,128)(2,1)S(1)} %collective-permute-done.4.refs_2_), channel_id=1, source_target_pairs={{0,2},{1,3},{2,0},{3,1},{4,6},{5,7},{6,4},{7,5},{8,10},{9,11},{10,... | collective-permute-start | bytes 393224 | tf_op jit(solution)/shard_map/ppermute | solution.py:214
  14.3 4.5 %collective-permute-start.8 = (bf16[8,64,128]{2,1,0:T(8,128)(2,1)S(1)}, bf16[8,64,128]{2,1,0:T(8,128)(2,1)S(1)}, u32[]{:S(2)}, u32[]{:S(2)}) collective-permute-start(bf16[8,64,128]{2,1,0:T(8,128)(2,1)S(1)} %collective-permute-done.3.refs_1_), channel_id=1, source_target_pairs={{0,1},{1,0},{2,3},{3,2},{4,5},{5,4},{6,7},{7,6},{8,9},{9,8},{10,11... | collective-permute-start | bytes 393224 | tf_op jit(solution)/shard_map/ppermute | solution.py:214
  14.5 5.5 %collective-permute-start.6 = (bf16[8,64,128]{2,1,0:T(8,128)(2,1)S(1)}, bf16[8,64,128]{2,1,0:T(8,128)(2,1)S(1)}, u32[]{:S(2)}, u32[]{:S(2)}) collective-permute-start(bf16[8,64,128]{2,1,0:T(8,128)(2,1)S(1)} %collective-permute-done.refs_3_), channel_id=1, source_target_pairs={{0,2},{1,5},{2,0},{3,7},{4,6},{5,1},{6,4},{7,3},{8,10},{9,13},{10,... | collective-permute-start | bytes 393224 | tf_op jit(solution)/shard_map/ppermute | solution.py:214
  16.6 5.1 %collective-permute-start.2 = (bf16[8,64,128]{2,1,0:T(8,128)(2,1)S(1)}, bf16[8,64,128]{2,1,0:T(8,128)(2,1)S(1)}, u32[]{:S(2)}, u32[]{:S(2)}) collective-permute-start(bf16[8,64,128]{2,1,0:T(8,128)(2,1)S(1)} %collective-permute-done.1.refs_5_), channel_id=1, source_target_pairs={{0,2},{1,5},{2,0},{3,7},{4,6},{5,1},{6,4},{7,3},{8,10},{9,13},{10,... | collective-permute-start | bytes 393224 | tf_op jit(solution)/shard_map/ppermute | solution.py:214
  18.3 4.0 %collective-permute-start.11 = (bf16[8,64,128]{2,1,0:T(8,128)(2,1)S(1)}, bf16[8,64,128]{2,1,0:T(8,128)(2,1)S(1)}, u32[]{:S(2)}, u32[]{:S(2)}) collective-permute-start(bf16[8,64,128]{2,1,0:T(8,128)(2,1)S(1)} %collective-permute-done.refs_3_), channel_id=1, source_target_pairs={{0,1},{1,0},{2,3},{3,2},{4,5},{5,4},{6,7},{7,6},{8,9},{9,8},{10,11... | collective-permute-start | bytes 393224 | tf_op jit(solution)/shard_map/ppermute | solution.py:214
  18.7 3.6 %collective-permute-start.12 = (bf16[8,64,128]{2,1,0:T(8,128)(2,1)S(1)}, bf16[8,64,128]{2,1,0:T(8,128)(2,1)S(1)}, u32[]{:S(2)}, u32[]{:S(2)}) collective-permute-start(bf16[8,64,128]{2,1,0:T(8,128)(2,1)S(1)} %collective-permute-done.1.refs_5_), channel_id=1, source_target_pairs={{0,1},{1,0},{2,3},{3,2},{4,5},{5,4},{6,7},{7,6},{8,9},{9,8},{10,11... | collective-permute-start | bytes 393224 | tf_op jit(solution)/shard_map/ppermute | solution.py:214
  18.8 3.4 %collective-permute-start.10 = (bf16[8,64,128]{2,1,0:T(8,128)(2,1)S(1)}, bf16[8,64,128]{2,1,0:T(8,128)(2,1)S(1)}, u32[]{:S(2)}, u32[]{:S(2)}) collective-permute-start(bf16[8,64,128]{2,1,0:T(8,128)(2,1)S(1)} %collective-permute-done.5.refs_4_), channel_id=1, source_target_pairs={{0,1},{1,0},{2,3},{3,2},{4,5},{5,4},{6,7},{7,6},{8,9},{9,8},{10,11... | collective-permute-start | bytes 393224 | tf_op jit(solution)/shard_map/ppermute | solution.py:214
  20.1 2.2 %collective-permute-start.13 = (bf16[8,64,128]{2,1,0:T(8,128)(2,1)S(1)}, bf16[8,64,128]{2,1,0:T(8,128)(2,1)S(1)}, u32[]{:S(2)}, u32[]{:S(2)}) collective-permute-start(bf16[8,64,128]{2,1,0:T(8,128)(2,1)S(1)} %collective-permute-done.6.refs_6_), channel_id=1, source_target_pairs={{0,1},{1,0},{2,3},{3,2},{4,5},{5,4},{6,7},{7,6},{8,9},{9,8},{10,11... | collective-permute-start | bytes 393224 | tf_op jit(solution)/shard_map/ppermute | solution.py:214
  21.7 1.6 %collective-permute-start.14 = (bf16[8,64,128]{2,1,0:T(8,128)(2,1)S(1)}, bf16[8,64,128]{2,1,0:T(8,128)(2,1)S(1)}, u32[]{:S(2)}, u32[]{:S(2)}) collective-permute-start(bf16[8,64,128]{2,1,0:T(8,128)(2,1)S(1)} %collective-permute-done.2.refs_4_), channel_id=1, source_target_pairs={{0,1},{1,0},{2,3},{3,2},{4,5},{5,4},{6,7},{7,6},{8,9},{9,8},{10,11... | collective-permute-start | bytes 393224 | tf_op jit(solution)/shard_map/ppermute | solution.py:214

commit v24 on v23

--- a/solution.py
+++ b/solution.py
@@ -18,7 +18,7 @@
     return name[1] | CORE, name[0] | CORE
 
 
-MIDDLE = (partner(CORNER), partner(BEYOND), partner(FIRST), partner(SECOND), END)
+MIDDLE = (CORNER, SECOND, partner(CORNER), partner(BEYOND), partner(FIRST), partner(SECOND), END)
 LAST = (partner(END),)
 EARLY = tuple(name for name in (
     OWN, SIDE, BESIDE, BEYOND, CORNER, FIRST, SECOND,
@@ -286,7 +286,7 @@
         half, ends = lax.optimization_barrier((half, [pieces[name] for name in held]))
         pieces.update(zip(held, ends))
         pass_on((BEYOND, FIRST), (BESIDE, CORNER), (BEYOND, SECOND), (FIRST, END))
-        share(BESIDE, SIDE, CORNER, FIRST, BEYOND, SECOND)
+        share(BESIDE, SIDE, CORNER, FIRST, BEYOND)
         early = [pieces[name] for name in EARLY]
     else:
         early = [lax.all_gather(pairs, "sec", axis=0, tiled=True)]
@@ -301,8 +301,8 @@
         cost_estimate=pl.CostEstimate(flops=flops, bytes_accessed=2 * psi.size, transcendentals=0),
     )(listed, half, *early)
     if by_swaps:
-        pieces[END], sigma = lax.optimization_barrier((pieces[END], sigma))
-        share(END)
+        pieces[END], pieces[SECOND], sigma = lax.optimization_barrier((pieces[END], pieces[SECOND], sigma))
+        share(END, SECOND)
         sigma = pl.pallas_call(
             middle_kernel,
             out_shape=jax.ShapeDtypeStruct(psi.shape, jnp.bfloat16),

time: 24.9 us -> 25.4 us (1.020)
  waiting for transfers between devices: 3.79 us -> 4.2 us
    ppermute x15, waiting for transfers between devices: 3.79 us -> 4.2 us  [swap(): lax.ppermute(piece, 'sec', [(i, i ^ (odd_bit if i & CORE else even_bit))...]
where the time goes in v24:
time: 25.4 us; the launch traced here: 25.3 us
  starting transfers between devices  13.1 us (52%)
  Pallas kernels  7.89 us (31%)
  waiting for transfers between devices  4.2 us (17%)
    ppermute x15, starting transfers between devices, swap(): lax.ppermute(piece, 'sec', [(i, i ^ (odd_bit if i & CORE else even_bit))...  13.1 us
    ppermute x15, waiting for transfers between devices, swap(): lax.ppermute(piece, 'sec', [(i, i ^ (odd_bit if i & CORE else even_bit))...  4.2 us
    pallas_call x1, Pallas kernels, per_device(): pl.pallas_call(functools.partial(left_kernel, pair_count, len(EARLY if by...  2.85 us
    pallas_call x1, Pallas kernels, per_device(): pl.pallas_call(early_kernel, out_shape=jax.ShapeDtypeStruct(psi.shape, jn...  1.59 us
    pallas_call x1, Pallas kernels, per_device(): pl.pallas_call(last_kernel, out_shape=jax.ShapeDtypeStruct(psi.shape, jnp...  1.3 us
    pallas_call x1, Pallas kernels, per_device(): pl.pallas_call(pack_kernel, out_shape=jax.ShapeDtypeStruct((pair_count, t...  1.09 us
    pallas_call x1, Pallas kernels, per_device(): pl.pallas_call(middle_kernel, out_shape=jax.ShapeDtypeStruct(psi.shape, j...  1.05 us
  transfers between devices with their start and end apart: 15, of which 5 were waited for; matrix products, arithmetic and copies ran while one was open for 0% of the time, Pallas kernels for 22%

profile of v24, /device:TPU:0, one launch (start us, length us, event | category | flops | bytes accessed | tf_op | source)
XLA Modules:
  0.0 25.3 jit_solution(4860315043946289407)
XLA Ops:
  0.0 1.1 %shard_map.83.refs_0_ = bf16[8,64,128]{2,1,0:T(8,128)(2,1)S(1)} custom-call(s32[16]{0:T(128)} %dims_hbm.3, bf16[16,64,64]{2,1,0:T(8,128)(2,1)} %right_hbm.1), custom_call_target="tpu_custom_call" | custom-call | bytes 131072 | tf_op jit(solution)/shard_map/pallas_call | solution.py:234
  1.1 4.1 %collective-permute-start = (bf16[8,64,128]{2,1,0:T(8,128)(2,1)S(1)}, bf16[8,64,128]{2,1,0:T(8,128)(2,1)S(1)}, u32[]{:S(2)}, u32[]{:S(2)}) collective-permute-start(bf16[8,64,128]{2,1,0:T(8,128)(2,1)S(1)} %shard_map.83.refs_0_), channel_id=1, source_target_pairs={{0,8},{1,9},{2,10},{3,11},{4,12},{5,13},{6,14},{7,15},{8,0},{9,1},... | collective-permute-start | bytes 393224 | tf_op jit(solution)/shard_map/ppermute | solution.py:214
  5.2 0.0 collective-permute-start.6
  5.2 1.6 %collective-permute-start.5 = (bf16[8,64,128]{2,1,0:T(8,128)(2,1)S(1)}, bf16[8,64,128]{2,1,0:T(8,128)(2,1)S(1)}, u32[]{:S(2)}, u32[]{:S(2)}) collective-permute-start(bf16[8,64,128]{2,1,0:T(8,128)(2,1)S(1)} %shard_map.83.refs_0_), channel_id=1, source_target_pairs={{0,4},{1,5},{2,6},{3,7},{4,0},{5,1},{6,2},{7,3},{8,12},{9,13},{10,... | collective-permute-start | bytes 393224 | tf_op jit(solution)/shard_map/ppermute | solution.py:214
  6.8 1.5 %collective-permute-start.4 = (bf16[8,64,128]{2,1,0:T(8,128)(2,1)S(1)}, bf16[8,64,128]{2,1,0:T(8,128)(2,1)S(1)}, u32[]{:S(2)}, u32[]{:S(2)}) collective-permute-start(bf16[8,64,128]{2,1,0:T(8,128)(2,1)S(1)} %shard_map.83.refs_0_), channel_id=1, source_target_pairs={{0,2},{1,3},{2,0},{3,1},{4,6},{5,7},{6,4},{7,5},{8,10},{9,11},{10,... | collective-permute-start | bytes 393224 | tf_op jit(solution)/shard_map/ppermute | solution.py:214
  8.3 2.9 %shard_map.82 = (bf16[8,8,64,128]{3,2,1,0:T(8,128)(2,1)S(1)}, s32[202]{0:T(256)S(4)}) custom-call(s32[8]{0:T(128)} %dims_hbm.2, s32[8,8]{1,0:T(8,128)} %bitcast.1, s32[8,8]{1,0:T(8,128)} %owner_hbm.1, s32[8,8]{1,0:T(8,128)} %slot_hbm.1, bf16[8,64,64]{2,1,0:T(8,128)(2,1)} %left_hbm.1, bf16[8,8,64,128]{3,2,1,0:T(8,128)(2,1)} %psi_hbm.1), custom_call_target="tpu_custom_call" | custom-call | flops 67108864 | bytes 1048576 | tf_op jit(solution)/shard_map/pallas_call | solution.py:249
  11.1 0.5 %collective-permute-done.refs_3_ = bf16[8,64,128]{2,1,0:T(8,128)(2,1)S(1)} collective-permute-done((bf16[8,64,128]{2,1,0:T(8,128)(2,1)S(1)}, bf16[8,64,128]{2,1,0:T(8,128)(2,1)S(1)}, u32[]{:S(2)}, u32[]{:S(2)}) %collective-permute-start) | collective-permute-done | bytes 131104 | tf_op jit(solution)/shard_map/ppermute | solution.py:214
  11.6 0.7 %collective-permute-start.1 = (bf16[8,64,128]{2,1,0:T(8,128)(2,1)S(1)}, bf16[8,64,128]{2,1,0:T(8,128)(2,1)S(1)}, u32[]{:S(2)}, u32[]{:S(2)}) collective-permute-start(bf16[8,64,128]{2,1,0:T(8,128)(2,1)S(1)} %collective-permute-done.refs_3_), channel_id=1, source_target_pairs={{0,4},{1,3},{2,6},{3,1},{4,0},{5,7},{6,2},{7,5},{8,12},{9,11},{10,... | collective-permute-start | bytes 393224 | tf_op jit(solution)/shard_map/ppermute | solution.py:214
  12.3 0.5 %collective-permute-done.5.refs_2_ = bf16[8,64,128]{2,1,0:T(8,128)(2,1)S(1)} collective-permute-done((bf16[8,64,128]{2,1,0:T(8,128)(2,1)S(1)}, bf16[8,64,128]{2,1,0:T(8,128)(2,1)S(1)}, u32[]{:S(2)}, u32[]{:S(2)}) %collective-permute-start.5) | collective-permute-done | bytes 131104 | tf_op jit(solution)/shard_map/ppermute | solution.py:214
  12.8 1.5 %collective-permute-start.9 = (bf16[8,64,128]{2,1,0:T(8,128)(2,1)S(1)}, bf16[8,64,128]{2,1,0:T(8,128)(2,1)S(1)}, u32[]{:S(2)}, u32[]{:S(2)}) collective-permute-start(bf16[8,64,128]{2,1,0:T(8,128)(2,1)S(1)} %collective-permute-done.5.refs_2_), channel_id=1, source_target_pairs={{0,2},{1,3},{2,0},{3,1},{4,6},{5,7},{6,4},{7,5},{8,10},{9,11},{10,... | collective-permute-start | bytes 393224 | tf_op jit(solution)/shard_map/ppermute | solution.py:214
  14.3 0.0 collective-permute-start.8
  14.3 0.0 collective-permute-done.4.refs_1_
  14.3 0.5 %collective-permute-start.7 = (bf16[8,64,128]{2,1,0:T(8,128)(2,1)S(1)}, bf16[8,64,128]{2,1,0:T(8,128)(2,1)S(1)}, u32[]{:S(2)}, u32[]{:S(2)}) collective-permute-start(bf16[8,64,128]{2,1,0:T(8,128)(2,1)S(1)} %collective-permute-done.4.refs_1_), channel_id=1, source_target_pairs={{0,1},{1,0},{2,3},{3,2},{4,5},{5,4},{6,7},{7,6},{8,9},{9,8},{10,11... | collective-permute-start | bytes 393224 | tf_op jit(solution)/shard_map/ppermute | solution.py:214
  14.8 0.0 collective-permute-done.6.refs_5_
  14.8 0.5 %collective-permute-start.3 = (bf16[8,64,128]{2,1,0:T(8,128)(2,1)S(1)}, bf16[8,64,128]{2,1,0:T(8,128)(2,1)S(1)}, u32[]{:S(2)}, u32[]{:S(2)}) collective-permute-start(bf16[8,64,128]{2,1,0:T(8,128)(2,1)S(1)} %collective-permute-done.refs_3_), channel_id=1, source_target_pairs={{0,2},{1,5},{2,0},{3,7},{4,6},{5,1},{6,4},{7,3},{8,10},{9,13},{10,... | collective-permute-start | bytes 393224 | tf_op jit(solution)/shard_map/ppermute | solution.py:214
  15.3 1.3 %collective-permute-done.1.refs_4_ = bf16[8,64,128]{2,1,0:T(8,128)(2,1)S(1)} collective-permute-done((bf16[8,64,128]{2,1,0:T(8,128)(2,1)S(1)}, bf16[8,64,128]{2,1,0:T(8,128)(2,1)S(1)}, u32[]{:S(2)}, u32[]{:S(2)}) %collective-permute-start.1) | collective-permute-done | bytes 131104 | tf_op jit(solution)/shard_map/ppermute | solution.py:214
  16.6 1.7 %collective-permute-start.2 = (bf16[8,64,128]{2,1,0:T(8,128)(2,1)S(1)}, bf16[8,64,128]{2,1,0:T(8,128)(2,1)S(1)}, u32[]{:S(2)}, u32[]{:S(2)}) collective-permute-start(bf16[8,64,128]{2,1,0:T(8,128)(2,1)S(1)} %collective-permute-done.1.refs_4_), channel_id=1, source_target_pairs={{0,2},{1,5},{2,0},{3,7},{4,6},{5,1},{6,4},{7,3},{8,10},{9,13},{10,... | collective-permute-start | bytes 393224 | tf_op jit(solution)/shard_map/ppermute | solution.py:214
  18.2 0.0 collective-permute-done.9.refs_0_
  18.2 0.0 collective-permute-start.11
  18.3 0.0 collective-permute-done.8.refs_7_
  18.3 0.5 %collective-permute-start.12 = (bf16[8,64,128]{2,1,0:T(8,128)(2,1)S(1)}, bf16[8,64,128]{2,1,0:T(8,128)(2,1)S(1)}, u32[]{:S(2)}, u32[]{:S(2)}) collective-permute-start(bf16[8,64,128]{2,1,0:T(8,128)(2,1)S(1)} %collective-permute-done.1.refs_4_), channel_id=1, source_target_pairs={{0,1},{1,0},{2,3},{3,2},{4,5},{5,4},{6,7},{7,6},{8,9},{9,8},{10,11... | collective-permute-start | bytes 393224 | tf_op jit(solution)/shard_map/ppermute | solution.py:214
  18.8 0.0 collective-permute-done.7.refs_6_
  18.8 0.1 collective-permute-start.10
  18.8 1.6 %shard_map.84.early_ref = bf16[8,8,64,128]{3,2,1,0:T(8,128)(2,1)S(1)} custom-call(s32[202]{0:T(256)S(4)} %get-tuple-element.12.list_ref, bf16[8,8,64,128]{3,2,1,0:T(8,128)(2,1)S(1)} %get-tuple-element.15.half_ref, bf16[8,64,128]{2,1,0:T(8,128)(2,1)S(1)} %shard_map.83.refs_0_, bf16[8,64,128]{2,1,0:T(8,128)(2,1)S(1)} %collective-permute-done.4.refs_1_, ...), custom_call_target="tpu_custom_call" | custom-call | flops 67108864 | bytes 1048576 | tf_op jit(solution)/shard_map/pallas_call | solution.py:294
  20.4 0.0 collective-permute-done.3.refs_1_
  20.4 1.1 %collective-permute-done.2.refs_6_ = bf16[8,64,128]{2,1,0:T(8,128)(2,1)S(1)} collective-permute-done((bf16[8,64,128]{2,1,0:T(8,128)(2,1)S(1)}, bf16[8,64,128]{2,1,0:T(8,128)(2,1)S(1)}, u32[]{:S(2)}, u32[]{:S(2)}) %collective-permute-start.2) | collective-permute-done | bytes 131104 | tf_op jit(solution)/shard_map/ppermute | solution.py:214
  21.6 0.0 collective-permute-start.13
  21.6 0.5 %collective-permute-start.14 = (bf16[8,64,128]{2,1,0:T(8,128)(2,1)S(1)}, bf16[8,64,128]{2,1,0:T(8,128)(2,1)S(1)}, u32[]{:S(2)}, u32[]{:S(2)}) collective-permute-start(bf16[8,64,128]{2,1,0:T(8,128)(2,1)S(1)} %collective-permute-done.2.refs_6_), channel_id=1, source_target_pairs={{0,1},{1,0},{2,3},{3,2},{4,5},{5,4},{6,7},{7,6},{8,9},{9,8},{10,11... | collective-permute-start | bytes 393224 | tf_op jit(solution)/shard_map/ppermute | solution.py:214
  22.1 0.0 collective-permute-done.11.refs_3_
  22.1 0.0 collective-permute-done.10.refs_2_
  22.1 0.0 collective-permute-done.12.refs_4_
  22.1 0.8 %collective-permute-done.13.refs_5_ = bf16[8,64,128]{2,1,0:T(8,128)(2,1)S(1)} collective-permute-done((bf16[8,64,128]{2,1,0:T(8,128)(2,1)S(1)}, bf16[8,64,128]{2,1,0:T(8,128)(2,1)S(1)}, u32[]{:S(2)}, u32[]{:S(2)}) %collective-permute-start.13) | collective-permute-done | bytes 131104 | tf_op jit(solution)/shard_map/ppermute | solution.py:214
  22.9 1.1 %shard_map.85.middle_ref = bf16[8,8,64,128]{3,2,1,0:T(8,128)(2,1)S(1)} custom-call(s32[202]{0:T(256)S(4)} %get-tuple-element.12.list_ref, bf16[8,8,64,128]{3,2,1,0:T(8,128)(2,1)S(1)} %shard_map.84.early_ref, bf16[8,8,64,128]{3,2,1,0:T(8,128)(2,1)S(1)} %get-tuple-element.15.half_ref, bf16[8,64,128]{2,1,0:T(8,128)(2,1)S(1)} %collective-permute-done.9.refs_0_, ...), custom_call_target="tpu_custom_call" | custom-call | flops 16777216 | bytes 262144 | tf_op jit(solution)/shard_map/pallas_call | solution.py:306
  24.0 0.0 collective-permute-done.14.pairs_ref
  24.0 1.3 %shard_map.86 = bf16[8,8,64,128]{3,2,1,0:T(8,128)(2,1)} custom-call(s32[202]{0:T(256)S(4)} %get-tuple-element.12.list_ref, bf16[8,8,64,128]{3,2,1,0:T(8,128)(2,1)S(1)} %shard_map.85.middle_ref, bf16[8,8,64,128]{3,2,1,0:T(8,128)(2,1)S(1)} %get-tuple-element.15.half_ref, bf16[8,64,128]{2,1,0:T(8,128)(2,1)S(1)} %collective-permute-done.14.pairs_ref), custom_call_target="tpu_custom_call" | custom-call | flops 4194304 | bytes 1048576 | tf_op jit(solution)/shard_map/pallas_call | solution.py:315
Async XLA Ops:
  1.1 10.5 %collective-permute-start = (bf16[8,64,128]{2,1,0:T(8,128)(2,1)S(1)}, bf16[8,64,128]{2,1,0:T(8,128)(2,1)S(1)}, u32[]{:S(2)}, u32[]{:S(2)}) collective-permute-start(bf16[8,64,128]{2,1,0:T(8,128)(2,1)S(1)} %shard_map.83.refs_0_), channel_id=1, source_target_pairs={{0,8},{1,9},{2,10},{3,11},{4,12},{5,13},{6,14},{7,15},{8,0},{9,1},... | collective-permute-start | bytes 393224 | tf_op jit(solution)/shard_map/ppermute | solution.py:214
  5.2 9.6 %collective-permute-start.6 = (bf16[8,64,128]{2,1,0:T(8,128)(2,1)S(1)}, bf16[8,64,128]{2,1,0:T(8,128)(2,1)S(1)}, u32[]{:S(2)}, u32[]{:S(2)}) collective-permute-start(bf16[8,64,128]{2,1,0:T(8,128)(2,1)S(1)} %shard_map.83.refs_0_), channel_id=1, source_target_pairs={{0,1},{1,0},{2,3},{3,2},{4,5},{5,4},{6,7},{7,6},{8,9},{9,8},{10,11... | collective-permute-start | bytes 393224 | tf_op jit(solution)/shard_map/ppermute | solution.py:214
  5.2 7.6 %collective-permute-start.5 = (bf16[8,64,128]{2,1,0:T(8,128)(2,1)S(1)}, bf16[8,64,128]{2,1,0:T(8,128)(2,1)S(1)}, u32[]{:S(2)}, u32[]{:S(2)}) collective-permute-start(bf16[8,64,128]{2,1,0:T(8,128)(2,1)S(1)} %shard_map.83.refs_0_), channel_id=1, source_target_pairs={{0,4},{1,5},{2,6},{3,7},{4,0},{5,1},{6,2},{7,3},{8,12},{9,13},{10,... | collective-permute-start | bytes 393224 | tf_op jit(solution)/shard_map/ppermute | solution.py:214
  6.8 7.5 %collective-permute-start.4 = (bf16[8,64,128]{2,1,0:T(8,128)(2,1)S(1)}, bf16[8,64,128]{2,1,0:T(8,128)(2,1)S(1)}, u32[]{:S(2)}, u32[]{:S(2)}) collective-permute-start(bf16[8,64,128]{2,1,0:T(8,128)(2,1)S(1)} %shard_map.83.refs_0_), channel_id=1, source_target_pairs={{0,2},{1,3},{2,0},{3,1},{4,6},{5,7},{6,4},{7,5},{8,10},{9,11},{10,... | collective-permute-start | bytes 393224 | tf_op jit(solution)/shard_map/ppermute | solution.py:214
  11.6 5.0 %collective-permute-start.1 = (bf16[8,64,128]{2,1,0:T(8,128)(2,1)S(1)}, bf16[8,64,128]{2,1,0:T(8,128)(2,1)S(1)}, u32[]{:S(2)}, u32[]{:S(2)}) collective-permute-start(bf16[8,64,128]{2,1,0:T(8,128)(2,1)S(1)} %collective-permute-done.refs_3_), channel_id=1, source_target_pairs={{0,4},{1,3},{2,6},{3,1},{4,0},{5,7},{6,2},{7,5},{8,12},{9,11},{10,... | collective-permute-start | bytes 393224 | tf_op jit(solution)/shard_map/ppermute | solution.py:214
  12.8 5.5 %collective-permute-start.9 = (bf16[8,64,128]{2,1,0:T(8,128)(2,1)S(1)}, bf16[8,64,128]{2,1,0:T(8,128)(2,1)S(1)}, u32[]{:S(2)}, u32[]{:S(2)}) collective-permute-start(bf16[8,64,128]{2,1,0:T(8,128)(2,1)S(1)} %collective-permute-done.5.refs_2_), channel_id=1, source_target_pairs={{0,2},{1,3},{2,0},{3,1},{4,6},{5,7},{6,4},{7,5},{8,10},{9,11},{10,... | collective-permute-start | bytes 393224 | tf_op jit(solution)/shard_map/ppermute | solution.py:214
  14.3 4.0 %collective-permute-start.8 = (bf16[8,64,128]{2,1,0:T(8,128)(2,1)S(1)}, bf16[8,64,128]{2,1,0:T(8,128)(2,1)S(1)}, u32[]{:S(2)}, u32[]{:S(2)}) collective-permute-start(bf16[8,64,128]{2,1,0:T(8,128)(2,1)S(1)} %collective-permute-done.5.refs_2_), channel_id=1, source_target_pairs={{0,1},{1,0},{2,3},{3,2},{4,5},{5,4},{6,7},{7,6},{8,9},{9,8},{10,11... | collective-permute-start | bytes 393224 | tf_op jit(solution)/shard_map/ppermute | solution.py:214
  14.3 4.5 %collective-permute-start.7 = (bf16[8,64,128]{2,1,0:T(8,128)(2,1)S(1)}, bf16[8,64,128]{2,1,0:T(8,128)(2,1)S(1)}, u32[]{:S(2)}, u32[]{:S(2)}) collective-permute-start(bf16[8,64,128]{2,1,0:T(8,128)(2,1)S(1)} %collective-permute-done.4.refs_1_), channel_id=1, source_target_pairs={{0,1},{1,0},{2,3},{3,2},{4,5},{5,4},{6,7},{7,6},{8,9},{9,8},{10,11... | collective-permute-start | bytes 393224 | tf_op jit(solution)/shard_map/ppermute | solution.py:214
  14.8 5.6 %collective-permute-start.3 = (bf16[8,64,128]{2,1,0:T(8,128)(2,1)S(1)}, bf16[8,64,128]{2,1,0:T(8,128)(2,1)S(1)}, u32[]{:S(2)}, u32[]{:S(2)}) collective-permute-start(bf16[8,64,128]{2,1,0:T(8,128)(2,1)S(1)} %collective-permute-done.refs_3_), channel_id=1, source_target_pairs={{0,2},{1,5},{2,0},{3,7},{4,6},{5,1},{6,4},{7,3},{8,10},{9,13},{10,... | collective-permute-start | bytes 393224 | tf_op jit(solution)/shard_map/ppermute | solution.py:214
  16.6 5.0 %collective-permute-start.2 = (bf16[8,64,128]{2,1,0:T(8,128)(2,1)S(1)}, bf16[8,64,128]{2,1,0:T(8,128)(2,1)S(1)}, u32[]{:S(2)}, u32[]{:S(2)}) collective-permute-start(bf16[8,64,128]{2,1,0:T(8,128)(2,1)S(1)} %collective-permute-done.1.refs_4_), channel_id=1, source_target_pairs={{0,2},{1,5},{2,0},{3,7},{4,6},{5,1},{6,4},{7,3},{8,10},{9,13},{10,... | collective-permute-start | bytes 393224 | tf_op jit(solution)/shard_map/ppermute | solution.py:214
  18.2 3.8 %collective-permute-start.11 = (bf16[8,64,128]{2,1,0:T(8,128)(2,1)S(1)}, bf16[8,64,128]{2,1,0:T(8,128)(2,1)S(1)}, u32[]{:S(2)}, u32[]{:S(2)}) collective-permute-start(bf16[8,64,128]{2,1,0:T(8,128)(2,1)S(1)} %collective-permute-done.refs_3_), channel_id=1, source_target_pairs={{0,1},{1,0},{2,3},{3,2},{4,5},{5,4},{6,7},{7,6},{8,9},{9,8},{10,11... | collective-permute-start | bytes 393224 | tf_op jit(solution)/shard_map/ppermute | solution.py:214
  18.3 3.8 %collective-permute-start.12 = (bf16[8,64,128]{2,1,0:T(8,128)(2,1)S(1)}, bf16[8,64,128]{2,1,0:T(8,128)(2,1)S(1)}, u32[]{:S(2)}, u32[]{:S(2)}) collective-permute-start(bf16[8,64,128]{2,1,0:T(8,128)(2,1)S(1)} %collective-permute-done.1.refs_4_), channel_id=1, source_target_pairs={{0,1},{1,0},{2,3},{3,2},{4,5},{5,4},{6,7},{7,6},{8,9},{9,8},{10,11... | collective-permute-start | bytes 393224 | tf_op jit(solution)/shard_map/ppermute | solution.py:214
  18.8 3.3 %collective-permute-start.10 = (bf16[8,64,128]{2,1,0:T(8,128)(2,1)S(1)}, bf16[8,64,128]{2,1,0:T(8,128)(2,1)S(1)}, u32[]{:S(2)}, u32[]{:S(2)}) collective-permute-start(bf16[8,64,128]{2,1,0:T(8,128)(2,1)S(1)} %collective-permute-done.9.refs_0_), channel_id=1, source_target_pairs={{0,1},{1,0},{2,3},{3,2},{4,5},{5,4},{6,7},{7,6},{8,9},{9,8},{10,11... | collective-permute-start | bytes 393224 | tf_op jit(solution)/shard_map/ppermute | solution.py:214
  21.6 1.3 %collective-permute-start.13 = (bf16[8,64,128]{2,1,0:T(8,128)(2,1)S(1)}, bf16[8,64,128]{2,1,0:T(8,128)(2,1)S(1)}, u32[]{:S(2)}, u32[]{:S(2)}) collective-permute-start(bf16[8,64,128]{2,1,0:T(8,128)(2,1)S(1)} %collective-permute-done.3.refs_1_), channel_id=1, source_target_pairs={{0,1},{1,0},{2,3},{3,2},{4,5},{5,4},{6,7},{7,6},{8,9},{9,8},{10,11... | collective-permute-start | bytes 393224 | tf_op jit(solution)/shard_map/ppermute | solution.py:214
  21.6 2.4 %collective-permute-start.14 = (bf16[8,64,128]{2,1,0:T(8,128)(2,1)S(1)}, bf16[8,64,128]{2,1,0:T(8,128)(2,1)S(1)}, u32[]{:S(2)}, u32[]{:S(2)}) collective-permute-start(bf16[8,64,128]{2,1,0:T(8,128)(2,1)S(1)} %collective-permute-done.2.refs_6_), channel_id=1, source_target_pairs={{0,1},{1,0},{2,3},{3,2},{4,5},{5,4},{6,7},{7,6},{8,9},{9,8},{10,11... | collective-permute-start | bytes 393224 | tf_op jit(solution)/shard_map/ppermute | solution.py:214

commit v25 on v24

--- a/solution.py
+++ b/solution.py
@@ -18,7 +18,7 @@
     return name[1] | CORE, name[0] | CORE
 
 
-MIDDLE = (CORNER, SECOND, partner(CORNER), partner(BEYOND), partner(FIRST), partner(SECOND), END)
+MIDDLE = (SECOND, partner(CORNER), partner(BEYOND), partner(FIRST), partner(SECOND), END)
 LAST = (partner(END),)
 EARLY = tuple(name for name in (
     OWN, SIDE, BESIDE, BEYOND, CORNER, FIRST, SECOND,
@@ -301,8 +301,9 @@
         cost_estimate=pl.CostEstimate(flops=flops, bytes_accessed=2 * psi.size, transcendentals=0),
     )(listed, half, *early)
     if by_swaps:
-        pieces[END], pieces[SECOND], sigma = lax.optimization_barrier((pieces[END], pieces[SECOND], sigma))
-        share(END, SECOND)
+        for name in (SECOND, END):
+            pieces[name], _ = lax.optimization_barrier((pieces[name], sigma))
+            share(name)
         sigma = pl.pallas_call(
             middle_kernel,
             out_shape=jax.ShapeDtypeStruct(psi.shape, jnp.bfloat16),

time: 25.4 us -> 25.1 us (0.988)
  waiting for transfers between devices: 4.2 us -> 3.32 us
  starting transfers between devices: 13.1 us -> 13.6 us
    ppermute x15, waiting for transfers between devices: 4.2 us -> 3.32 us  [swap(): lax.ppermute(piece, 'sec', [(i, i ^ (odd_bit if i & CORE else even_bit))...]
    ppermute x15, starting transfers between devices: 13.1 us -> 13.6 us  [swap(): lax.ppermute(piece, 'sec', [(i, i ^ (odd_bit if i & CORE else even_bit))...]
  transfers between devices with their start and end apart: 15 -> 15, of which waited for: 5 -> 6; matrix products, arithmetic and copies ran while one was open for 0% -> 0% of each run, Pallas kernels for 22% -> 22%
where the time goes in v25:
time: 25.1 us; the launch traced here: 25 us
  starting transfers between devices  13.6 us (54%)
  Pallas kernels  7.94 us (32%)
  waiting for transfers between devices  3.32 us (13%)
    ppermute x15, starting transfers between devices, swap(): lax.ppermute(piece, 'sec', [(i, i ^ (odd_bit if i & CORE else even_bit))...  13.6 us
    ppermute x15, waiting for transfers between devices, swap(): lax.ppermute(piece, 'sec', [(i, i ^ (odd_bit if i & CORE else even_bit))...  3.32 us
    pallas_call x1, Pallas kernels, per_device(): pl.pallas_call(functools.partial(left_kernel, pair_count, len(EARLY if by...  2.85 us
    pallas_call x1, Pallas kernels, per_device(): pl.pallas_call(early_kernel, out_shape=jax.ShapeDtypeStruct(psi.shape, jn...  1.61 us
    pallas_call x1, Pallas kernels, per_device(): pl.pallas_call(last_kernel, out_shape=jax.ShapeDtypeStruct(psi.shape, jnp...  1.34 us
    pallas_call x1, Pallas kernels, per_device(): pl.pallas_call(pack_kernel, out_shape=jax.ShapeDtypeStruct((pair_count, t...  1.09 us
    pallas_call x1, Pallas kernels, per_device(): pl.pallas_call(middle_kernel, out_shape=jax.ShapeDtypeStruct(psi.shape, j...  1.04 us
  transfers between devices with their start and end apart: 15, of which 6 were waited for; matrix products, arithmetic and copies ran while one was open for 0% of the time, Pallas kernels for 22%

profile of v25, /device:TPU:0, one launch (start us, length us, event | category | flops | bytes accessed | tf_op | source)
XLA Modules:
  0.0 25.0 jit_solution(17045955356250623888)
XLA Ops:
  0.0 1.1 %shard_map.83.refs_0_ = bf16[8,64,128]{2,1,0:T(8,128)(2,1)S(1)} custom-call(s32[16]{0:T(128)} %dims_hbm.3, bf16[16,64,64]{2,1,0:T(8,128)(2,1)} %right_hbm.1), custom_call_target="tpu_custom_call" | custom-call | bytes 131072 | tf_op jit(solution)/shard_map/pallas_call | solution.py:234
  1.1 4.1 %collective-permute-start = (bf16[8,64,128]{2,1,0:T(8,128)(2,1)S(1)}, bf16[8,64,128]{2,1,0:T(8,128)(2,1)S(1)}, u32[]{:S(2)}, u32[]{:S(2)}) collective-permute-start(bf16[8,64,128]{2,1,0:T(8,128)(2,1)S(1)} %shard_map.83.refs_0_), channel_id=1, source_target_pairs={{0,8},{1,9},{2,10},{3,11},{4,12},{5,13},{6,14},{7,15},{8,0},{9,1},... | collective-permute-start | bytes 393224 | tf_op jit(solution)/shard_map/ppermute | solution.py:214
  5.2 1.6 %collective-permute-start.2 = (bf16[8,64,128]{2,1,0:T(8,128)(2,1)S(1)}, bf16[8,64,128]{2,1,0:T(8,128)(2,1)S(1)}, u32[]{:S(2)}, u32[]{:S(2)}) collective-permute-start(bf16[8,64,128]{2,1,0:T(8,128)(2,1)S(1)} %shard_map.83.refs_0_), channel_id=1, source_target_pairs={{0,4},{1,5},{2,6},{3,7},{4,0},{5,1},{6,2},{7,3},{8,12},{9,13},{10,... | collective-permute-start | bytes 393224 | tf_op jit(solution)/shard_map/ppermute | solution.py:214
  6.8 1.5 %collective-permute-start.1 = (bf16[8,64,128]{2,1,0:T(8,128)(2,1)S(1)}, bf16[8,64,128]{2,1,0:T(8,128)(2,1)S(1)}, u32[]{:S(2)}, u32[]{:S(2)}) collective-permute-start(bf16[8,64,128]{2,1,0:T(8,128)(2,1)S(1)} %shard_map.83.refs_0_), channel_id=1, source_target_pairs={{0,2},{1,3},{2,0},{3,1},{4,6},{5,7},{6,4},{7,5},{8,10},{9,11},{10,... | collective-permute-start | bytes 393224 | tf_op jit(solution)/shard_map/ppermute | solution.py:214
  8.3 0.0 collective-permute-start.5
  8.3 2.9 %shard_map.82 = (bf16[8,8,64,128]{3,2,1,0:T(8,128)(2,1)S(1)}, s32[202]{0:T(256)S(4)}) custom-call(s32[8]{0:T(128)} %dims_hbm.2, s32[8,8]{1,0:T(8,128)} %bitcast.1, s32[8,8]{1,0:T(8,128)} %owner_hbm.1, s32[8,8]{1,0:T(8,128)} %slot_hbm.1, bf16[8,64,64]{2,1,0:T(8,128)(2,1)} %left_hbm.1, bf16[8,8,64,128]{3,2,1,0:T(8,128)(2,1)} %psi_hbm.1), custom_call_target="tpu_custom_call" | custom-call | flops 67108864 | bytes 1048576 | tf_op jit(solution)/shard_map/pallas_call | solution.py:249
  11.1 0.5 %collective-permute-done.refs_3_ = bf16[8,64,128]{2,1,0:T(8,128)(2,1)S(1)} collective-permute-done((bf16[8,64,128]{2,1,0:T(8,128)(2,1)S(1)}, bf16[8,64,128]{2,1,0:T(8,128)(2,1)S(1)}, u32[]{:S(2)}, u32[]{:S(2)}) %collective-permute-start) | collective-permute-done | bytes 131104 | tf_op jit(solution)/shard_map/ppermute | solution.py:214
  11.6 0.6 %collective-permute-start.4 = (bf16[8,64,128]{2,1,0:T(8,128)(2,1)S(1)}, bf16[8,64,128]{2,1,0:T(8,128)(2,1)S(1)}, u32[]{:S(2)}, u32[]{:S(2)}) collective-permute-start(bf16[8,64,128]{2,1,0:T(8,128)(2,1)S(1)} %collective-permute-done.refs_3_), channel_id=1, source_target_pairs={{0,4},{1,3},{2,6},{3,1},{4,0},{5,7},{6,2},{7,5},{8,12},{9,11},{10,... | collective-permute-start | bytes 393224 | tf_op jit(solution)/shard_map/ppermute | solution.py:214
  12.2 0.0 collective-permute-done.2.refs_2_
  12.2 1.5 %collective-permute-start.3 = (bf16[8,64,128]{2,1,0:T(8,128)(2,1)S(1)}, bf16[8,64,128]{2,1,0:T(8,128)(2,1)S(1)}, u32[]{:S(2)}, u32[]{:S(2)}) collective-permute-start(bf16[8,64,128]{2,1,0:T(8,128)(2,1)S(1)} %collective-permute-done.2.refs_2_), channel_id=1, source_target_pairs={{0,2},{1,3},{2,0},{3,1},{4,6},{5,7},{6,4},{7,5},{8,10},{9,11},{10,... | collective-permute-start | bytes 393224 | tf_op jit(solution)/shard_map/ppermute | solution.py:214
  13.7 0.0 collective-permute-start.7
  13.7 0.0 collective-permute-done.1.refs_1_
  13.7 0.5 %collective-permute-start.6 = (bf16[8,64,128]{2,1,0:T(8,128)(2,1)S(1)}, bf16[8,64,128]{2,1,0:T(8,128)(2,1)S(1)}, u32[]{:S(2)}, u32[]{:S(2)}) collective-permute-start(bf16[8,64,128]{2,1,0:T(8,128)(2,1)S(1)} %collective-permute-done.1.refs_1_), channel_id=1, source_target_pairs={{0,1},{1,0},{2,3},{3,2},{4,5},{5,4},{6,7},{7,6},{8,9},{9,8},{10,11... | collective-permute-start | bytes 393224 | tf_op jit(solution)/shard_map/ppermute | solution.py:214
  14.2 0.0 collective-permute-done.5.refs_6_
  14.2 0.5 %collective-permute-start.8 = (bf16[8,64,128]{2,1,0:T(8,128)(2,1)S(1)}, bf16[8,64,128]{2,1,0:T(8,128)(2,1)S(1)}, u32[]{:S(2)}, u32[]{:S(2)}) collective-permute-start(bf16[8,64,128]{2,1,0:T(8,128)(2,1)S(1)} %collective-permute-done.refs_3_), channel_id=1, source_target_pairs={{0,2},{1,5},{2,0},{3,7},{4,6},{5,1},{6,4},{7,3},{8,10},{9,13},{10,... | collective-permute-start | bytes 393224 | tf_op jit(solution)/shard_map/ppermute | solution.py:214
  14.8 1.8 %collective-permute-done.4.refs_5_ = bf16[8,64,128]{2,1,0:T(8,128)(2,1)S(1)} collective-permute-done((bf16[8,64,128]{2,1,0:T(8,128)(2,1)S(1)}, bf16[8,64,128]{2,1,0:T(8,128)(2,1)S(1)}, u32[]{:S(2)}, u32[]{:S(2)}) %collective-permute-start.4) | collective-permute-done | bytes 131104 | tf_op jit(solution)/shard_map/ppermute | solution.py:214
  16.6 2.3 %collective-permute-start.13 = (bf16[8,64,128]{2,1,0:T(8,128)(2,1)S(1)}, bf16[8,64,128]{2,1,0:T(8,128)(2,1)S(1)}, u32[]{:S(2)}, u32[]{:S(2)}) collective-permute-start(bf16[8,64,128]{2,1,0:T(8,128)(2,1)S(1)} %collective-permute-done.4.refs_5_), channel_id=1, source_target_pairs={{0,2},{1,5},{2,0},{3,7},{4,6},{5,1},{6,4},{7,3},{8,10},{9,13},{10,... | collective-permute-start | bytes 393224 | tf_op jit(solution)/shard_map/ppermute | solution.py:214
  18.8 0.0 collective-permute-done.3.refs_4_
  18.8 0.0 collective-permute-start.10
  18.8 0.0 collective-permute-done.7.refs_8_
  18.8 0.0 collective-permute-done.6.refs_7_
  18.9 1.6 %shard_map.84.early_ref = bf16[8,8,64,128]{3,2,1,0:T(8,128)(2,1)S(1)} custom-call(s32[202]{0:T(256)S(4)} %get-tuple-element.11.list_ref, bf16[8,8,64,128]{3,2,1,0:T(8,128)(2,1)S(1)} %get-tuple-element.13.half_ref, bf16[8,64,128]{2,1,0:T(8,128)(2,1)S(1)} %shard_map.83.refs_0_, bf16[8,64,128]{2,1,0:T(8,128)(2,1)S(1)} %collective-permute-done.1.refs_1_, ...), custom_call_target="tpu_custom_call" | custom-call | flops 67108864 | bytes 1048576 | tf_op jit(solution)/shard_map/pallas_call | solution.py:294
  20.5 0.0 collective-permute-done.8.refs_0_
  20.5 0.6 %collective-permute-start.12 = (bf16[8,64,128]{2,1,0:T(8,128)(2,1)S(1)}, bf16[8,64,128]{2,1,0:T(8,128)(2,1)S(1)}, u32[]{:S(2)}, u32[]{:S(2)}) collective-permute-start(bf16[8,64,128]{2,1,0:T(8,128)(2,1)S(1)} %collective-permute-done.8.refs_0_), channel_id=1, source_target_pairs={{0,1},{1,0},{2,3},{3,2},{4,5},{5,4},{6,7},{7,6},{8,9},{9,8},{10,11... | collective-permute-start | bytes 393224 | tf_op jit(solution)/shard_map/ppermute | solution.py:214
  21.0 0.1 collective-permute-start.11
  21.1 0.4 %collective-permute-start.9 = (bf16[8,64,128]{2,1,0:T(8,128)(2,1)S(1)}, bf16[8,64,128]{2,1,0:T(8,128)(2,1)S(1)}, u32[]{:S(2)}, u32[]{:S(2)}) collective-permute-start(bf16[8,64,128]{2,1,0:T(8,128)(2,1)S(1)} %collective-permute-done.3.refs_4_), channel_id=1, source_target_pairs={{0,1},{1,0},{2,3},{3,2},{4,5},{5,4},{6,7},{7,6},{8,9},{9,8},{10,11... | collective-permute-start | bytes 393224 | tf_op jit(solution)/shard_map/ppermute | solution.py:214
  21.6 0.2 collective-permute-done.13.refs_5_
  21.8 0.0 collective-permute-start.14
  21.8 0.0 collective-permute-done.10.refs_2_
  21.8 0.2 collective-permute-done.12.refs_4_
  22.0 0.4 %collective-permute-done.11.refs_3_ = bf16[8,64,128]{2,1,0:T(8,128)(2,1)S(1)} collective-permute-done((bf16[8,64,128]{2,1,0:T(8,128)(2,1)S(1)}, bf16[8,64,128]{2,1,0:T(8,128)(2,1)S(1)}, u32[]{:S(2)}, u32[]{:S(2)}) %collective-permute-start.11) | collective-permute-done | bytes 131104 | tf_op jit(solution)/shard_map/ppermute | solution.py:214
  22.4 0.2 collective-permute-done.9.refs_1_
  22.6 1.0 %shard_map.85.middle_ref = bf16[8,8,64,128]{3,2,1,0:T(8,128)(2,1)S(1)} custom-call(s32[202]{0:T(256)S(4)} %get-tuple-element.11.list_ref, bf16[8,8,64,128]{3,2,1,0:T(8,128)(2,1)S(1)} %shard_map.84.early_ref, bf16[8,8,64,128]{3,2,1,0:T(8,128)(2,1)S(1)} %get-tuple-element.13.half_ref, bf16[8,64,128]{2,1,0:T(8,128)(2,1)S(1)} %collective-permute-done.8.refs_0_, ...), custom_call_target="tpu_custom_call" | custom-call | flops 16777216 | bytes 262144 | tf_op jit(solution)/shard_map/pallas_call | solution.py:307
  23.6 0.0 collective-permute-done.14.pairs_ref
  23.6 1.3 %shard_map.86 = bf16[8,8,64,128]{3,2,1,0:T(8,128)(2,1)} custom-call(s32[202]{0:T(256)S(4)} %get-tuple-element.11.list_ref, bf16[8,8,64,128]{3,2,1,0:T(8,128)(2,1)S(1)} %shard_map.85.middle_ref, bf16[8,8,64,128]{3,2,1,0:T(8,128)(2,1)S(1)} %get-tuple-element.13.half_ref, bf16[8,64,128]{2,1,0:T(8,128)(2,1)S(1)} %collective-permute-done.14.pairs_ref), custom_call_target="tpu_custom_call" | custom-call | flops 4194304 | bytes 1048576 | tf_op jit(solution)/shard_map/pallas_call | solution.py:316
Async XLA Ops:
  1.1 10.5 %collective-permute-start = (bf16[8,64,128]{2,1,0:T(8,128)(2,1)S(1)}, bf16[8,64,128]{2,1,0:T(8,128)(2,1)S(1)}, u32[]{:S(2)}, u32[]{:S(2)}) collective-permute-start(bf16[8,64,128]{2,1,0:T(8,128)(2,1)S(1)} %shard_map.83.refs_0_), channel_id=1, source_target_pairs={{0,8},{1,9},{2,10},{3,11},{4,12},{5,13},{6,14},{7,15},{8,0},{9,1},... | collective-permute-start | bytes 393224 | tf_op jit(solution)/shard_map/ppermute | solution.py:214
  5.2 7.0 %collective-permute-start.2 = (bf16[8,64,128]{2,1,0:T(8,128)(2,1)S(1)}, bf16[8,64,128]{2,1,0:T(8,128)(2,1)S(1)}, u32[]{:S(2)}, u32[]{:S(2)}) collective-permute-start(bf16[8,64,128]{2,1,0:T(8,128)(2,1)S(1)} %shard_map.83.refs_0_), channel_id=1, source_target_pairs={{0,4},{1,5},{2,6},{3,7},{4,0},{5,1},{6,2},{7,3},{8,12},{9,13},{10,... | collective-permute-start | bytes 393224 | tf_op jit(solution)/shard_map/ppermute | solution.py:214
  6.8 7.0 %collective-permute-start.1 = (bf16[8,64,128]{2,1,0:T(8,128)(2,1)S(1)}, bf16[8,64,128]{2,1,0:T(8,128)(2,1)S(1)}, u32[]{:S(2)}, u32[]{:S(2)}) collective-permute-start(bf16[8,64,128]{2,1,0:T(8,128)(2,1)S(1)} %shard_map.83.refs_0_), channel_id=1, source_target_pairs={{0,2},{1,3},{2,0},{3,1},{4,6},{5,7},{6,4},{7,5},{8,10},{9,11},{10,... | collective-permute-start | bytes 393224 | tf_op jit(solution)/shard_map/ppermute | solution.py:214
  8.3 6.0 %collective-permute-start.5 = (bf16[8,64,128]{2,1,0:T(8,128)(2,1)S(1)}, bf16[8,64,128]{2,1,0:T(8,128)(2,1)S(1)}, u32[]{:S(2)}, u32[]{:S(2)}) collective-permute-start(bf16[8,64,128]{2,1,0:T(8,128)(2,1)S(1)} %shard_map.83.refs_0_), channel_id=1, source_target_pairs={{0,1},{1,0},{2,3},{3,2},{4,5},{5,4},{6,7},{7,6},{8,9},{9,8},{10,11... | collective-permute-start | bytes 393224 | tf_op jit(solution)/shard_map/ppermute | solution.py:214
  11.6 5.0 %collective-permute-start.4 = (bf16[8,64,128]{2,1,0:T(8,128)(2,1)S(1)}, bf16[8,64,128]{2,1,0:T(8,128)(2,1)S(1)}, u32[]{:S(2)}, u32[]{:S(2)}) collective-permute-start(bf16[8,64,128]{2,1,0:T(8,128)(2,1)S(1)} %collective-permute-done.refs_3_), channel_id=1, source_target_pairs={{0,4},{1,3},{2,6},{3,1},{4,0},{5,7},{6,2},{7,5},{8,12},{9,11},{10,... | collective-permute-start | bytes 393224 | tf_op jit(solution)/shard_map/ppermute | solution.py:214
  12.2 6.6 %collective-permute-start.3 = (bf16[8,64,128]{2,1,0:T(8,128)(2,1)S(1)}, bf16[8,64,128]{2,1,0:T(8,128)(2,1)S(1)}, u32[]{:S(2)}, u32[]{:S(2)}) collective-permute-start(bf16[8,64,128]{2,1,0:T(8,128)(2,1)S(1)} %collective-permute-done.2.refs_2_), channel_id=1, source_target_pairs={{0,2},{1,3},{2,0},{3,1},{4,6},{5,7},{6,4},{7,5},{8,10},{9,11},{10,... | collective-permute-start | bytes 393224 | tf_op jit(solution)/shard_map/ppermute | solution.py:214
  13.7 5.1 %collective-permute-start.7 = (bf16[8,64,128]{2,1,0:T(8,128)(2,1)S(1)}, bf16[8,64,128]{2,1,0:T(8,128)(2,1)S(1)}, u32[]{:S(2)}, u32[]{:S(2)}) collective-permute-start(bf16[8,64,128]{2,1,0:T(8,128)(2,1)S(1)} %collective-permute-done.2.refs_2_), channel_id=1, source_target_pairs={{0,1},{1,0},{2,3},{3,2},{4,5},{5,4},{6,7},{7,6},{8,9},{9,8},{10,11... | collective-permute-start | bytes 393224 | tf_op jit(solution)/shard_map/ppermute | solution.py:214
  13.7 5.1 %collective-permute-start.6 = (bf16[8,64,128]{2,1,0:T(8,128)(2,1)S(1)}, bf16[8,64,128]{2,1,0:T(8,128)(2,1)S(1)}, u32[]{:S(2)}, u32[]{:S(2)}) collective-permute-start(bf16[8,64,128]{2,1,0:T(8,128)(2,1)S(1)} %collective-permute-done.1.refs_1_), channel_id=1, source_target_pairs={{0,1},{1,0},{2,3},{3,2},{4,5},{5,4},{6,7},{7,6},{8,9},{9,8},{10,11... | collective-permute-start | bytes 393224 | tf_op jit(solution)/shard_map/ppermute | solution.py:214
  14.2 6.2 %collective-permute-start.8 = (bf16[8,64,128]{2,1,0:T(8,128)(2,1)S(1)}, bf16[8,64,128]{2,1,0:T(8,128)(2,1)S(1)}, u32[]{:S(2)}, u32[]{:S(2)}) collective-permute-start(bf16[8,64,128]{2,1,0:T(8,128)(2,1)S(1)} %collective-permute-done.refs_3_), channel_id=1, source_target_pairs={{0,2},{1,5},{2,0},{3,7},{4,6},{5,1},{6,4},{7,3},{8,10},{9,13},{10,... | collective-permute-start | bytes 393224 | tf_op jit(solution)/shard_map/ppermute | solution.py:214
  16.6 5.2 %collective-permute-start.13 = (bf16[8,64,128]{2,1,0:T(8,128)(2,1)S(1)}, bf16[8,64,128]{2,1,0:T(8,128)(2,1)S(1)}, u32[]{:S(2)}, u32[]{:S(2)}) collective-permute-start(bf16[8,64,128]{2,1,0:T(8,128)(2,1)S(1)} %collective-permute-done.4.refs_5_), channel_id=1, source_target_pairs={{0,2},{1,5},{2,0},{3,7},{4,6},{5,1},{6,4},{7,3},{8,10},{9,13},{10,... | collective-permute-start | bytes 393224 | tf_op jit(solution)/shard_map/ppermute | solution.py:214
  18.8 2.9 %collective-permute-start.10 = (bf16[8,64,128]{2,1,0:T(8,128)(2,1)S(1)}, bf16[8,64,128]{2,1,0:T(8,128)(2,1)S(1)}, u32[]{:S(2)}, u32[]{:S(2)}) collective-permute-start(bf16[8,64,128]{2,1,0:T(8,128)(2,1)S(1)} %collective-permute-done.refs_3_), channel_id=1, source_target_pairs={{0,1},{1,0},{2,3},{3,2},{4,5},{5,4},{6,7},{7,6},{8,9},{9,8},{10,11... | collective-permute-start | bytes 393224 | tf_op jit(solution)/shard_map/ppermute | solution.py:214
  20.5 1.5 %collective-permute-start.12 = (bf16[8,64,128]{2,1,0:T(8,128)(2,1)S(1)}, bf16[8,64,128]{2,1,0:T(8,128)(2,1)S(1)}, u32[]{:S(2)}, u32[]{:S(2)}) collective-permute-start(bf16[8,64,128]{2,1,0:T(8,128)(2,1)S(1)} %collective-permute-done.8.refs_0_), channel_id=1, source_target_pairs={{0,1},{1,0},{2,3},{3,2},{4,5},{5,4},{6,7},{7,6},{8,9},{9,8},{10,11... | collective-permute-start | bytes 393224 | tf_op jit(solution)/shard_map/ppermute | solution.py:214
  21.0 1.3 %collective-permute-start.11 = (bf16[8,64,128]{2,1,0:T(8,128)(2,1)S(1)}, bf16[8,64,128]{2,1,0:T(8,128)(2,1)S(1)}, u32[]{:S(2)}, u32[]{:S(2)}) collective-permute-start(bf16[8,64,128]{2,1,0:T(8,128)(2,1)S(1)} %collective-permute-done.4.refs_5_), channel_id=1, source_target_pairs={{0,1},{1,0},{2,3},{3,2},{4,5},{5,4},{6,7},{7,6},{8,9},{9,8},{10,11... | collective-permute-start | bytes 393224 | tf_op jit(solution)/shard_map/ppermute | solution.py:214
  21.1 1.5 %collective-permute-start.9 = (bf16[8,64,128]{2,1,0:T(8,128)(2,1)S(1)}, bf16[8,64,128]{2,1,0:T(8,128)(2,1)S(1)}, u32[]{:S(2)}, u32[]{:S(2)}) collective-permute-start(bf16[8,64,128]{2,1,0:T(8,128)(2,1)S(1)} %collective-permute-done.3.refs_4_), channel_id=1, source_target_pairs={{0,1},{1,0},{2,3},{3,2},{4,5},{5,4},{6,7},{7,6},{8,9},{9,8},{10,11... | collective-permute-start | bytes 393224 | tf_op jit(solution)/shard_map/ppermute | solution.py:214
  21.8 1.9 %collective-permute-start.14 = (bf16[8,64,128]{2,1,0:T(8,128)(2,1)S(1)}, bf16[8,64,128]{2,1,0:T(8,128)(2,1)S(1)}, u32[]{:S(2)}, u32[]{:S(2)}) collective-permute-start(bf16[8,64,128]{2,1,0:T(8,128)(2,1)S(1)} %collective-permute-done.13.refs_5_), channel_id=1, source_target_pairs={{0,1},{1,0},{2,3},{3,2},{4,5},{5,4},{6,7},{7,6},{8,9},{9,8},{10,11... | collective-permute-start | bytes 393224 | tf_op jit(solution)/shard_map/ppermute | solution.py:214

commit v26 on v24

--- a/solution.py
+++ b/solution.py
@@ -18,12 +18,12 @@
     return name[1] | CORE, name[0] | CORE
 
 
-MIDDLE = (CORNER, SECOND, partner(CORNER), partner(BEYOND), partner(FIRST), partner(SECOND), END)
-LAST = (partner(END),)
+MIDDLE = (CORNER, SECOND, partner(CORNER), partner(BEYOND), partner(FIRST), END)
+LAST = (partner(SECOND), partner(END))
 EARLY = tuple(name for name in (
     OWN, SIDE, BESIDE, BEYOND, CORNER, FIRST, SECOND,
     partner(OWN), partner(SIDE), partner(BESIDE), partner(BEYOND), partner(CORNER), partner(FIRST), partner(SECOND),
-) if name not in MIDDLE)
+) if name not in MIDDLE + LAST)
 ORDER = EARLY + MIDDLE + LAST
 
 
@@ -180,7 +180,8 @@
     listed_products(16, 0, list_ref, half_ref, pairs_ref, out_ref)
 
 
-def last_kernel(list_ref, middle_ref, half_ref, pairs_ref, out_hbm, out_ref, sems):
+def last_kernel(list_ref, middle_ref, half_ref, *refs):
+    piece_refs, (out_hbm, pairs_ref, out_ref, sems) = refs[:-4], refs[-4:]
     sectors, blocks, tile, width = half_ref.shape
     items = sectors * blocks
 
@@ -198,7 +199,8 @@
         def _():
             store(a, middle_ref).start()
 
-    listed_products(8, items + 1, list_ref, half_ref, pairs_ref, out_ref)
+    merge(piece_refs, pairs_ref)
+    listed_products(16, items + 1, list_ref, half_ref, pairs_ref, out_ref)
     for a in range(sectors):
 
         @pl.when(list_ref[2 * items + 2 + a] > 0)
@@ -315,12 +317,16 @@
         sigma = pl.pallas_call(
             last_kernel,
             out_shape=jax.ShapeDtypeStruct(psi.shape, jnp.bfloat16),
-            in_specs=[smem] + [vmem] * 3,
+            in_specs=[smem] + [vmem] * (2 + len(LAST)),
             out_specs=hbm,
-            scratch_shapes=[pltpu.VMEM(psi.shape, jnp.bfloat16), pltpu.SemaphoreType.DMA((left_count,))],
+            scratch_shapes=[
+                pltpu.VMEM((len(LAST) * pair_count, tile, 2 * tile), jnp.bfloat16),
+                pltpu.VMEM(psi.shape, jnp.bfloat16),
+                pltpu.SemaphoreType.DMA((left_count,)),
+            ],
             compiler_params=params,
             cost_estimate=pl.CostEstimate(flops=flops // 16, bytes_accessed=2 * psi.size, transcendentals=0),
-        )(listed, sigma, half, pieces[LAST[0]])
+        )(listed, sigma, half, *[pieces[name] for name in LAST])
     if lax.axis_size("op") > 1:
         sigma = lax.psum_scatter(sigma, "op", scatter_dimension=3, tiled=True)
     return sigma

time: 25.4 us -> 24.9 us (0.980)
  waiting for transfers between devices: 4.2 us -> 3.38 us
    ppermute x15, waiting for transfers between devices: 4.2 us -> 3.38 us  [swap(): lax.ppermute(piece, 'sec', [(i, i ^ (odd_bit if i & CORE else even_bit))...]
  transfers between devices with their start and end apart: 15 -> 15, of which waited for: 5 -> 4; matrix products, arithmetic and copies ran while one was open for 0% -> 0% of each run, Pallas kernels for 22% -> 22%
where the time goes in v26:
time: 24.9 us; the launch traced here: 24.6 us
  starting transfers between devices  13.1 us (53%)
  Pallas kernels  8.08 us (32%)
  waiting for transfers between devices  3.38 us (14%)
    ppermute x15, starting transfers between devices, swap(): lax.ppermute(piece, 'sec', [(i, i ^ (odd_bit if i & CORE else even_bit))...  13.1 us
    ppermute x15, waiting for transfers between devices, swap(): lax.ppermute(piece, 'sec', [(i, i ^ (odd_bit if i & CORE else even_bit))...  3.38 us
    pallas_call x1, Pallas kernels, per_device(): pl.pallas_call(functools.partial(left_kernel, pair_count, len(EARLY if by...  2.85 us
    pallas_call x1, Pallas kernels, per_device(): pl.pallas_call(early_kernel, out_shape=jax.ShapeDtypeStruct(psi.shape, jn...  1.59 us
    pallas_call x1, Pallas kernels, per_device(): pl.pallas_call(last_kernel, out_shape=jax.ShapeDtypeStruct(psi.shape, jnp...  1.49 us
    pallas_call x1, Pallas kernels, per_device(): pl.pallas_call(pack_kernel, out_shape=jax.ShapeDtypeStruct((pair_count, t...  1.09 us
    pallas_call x1, Pallas kernels, per_device(): pl.pallas_call(middle_kernel, out_shape=jax.ShapeDtypeStruct(psi.shape, j...  1.05 us
  transfers between devices with their start and end apart: 15, of which 4 were waited for; matrix products, arithmetic and copies ran while one was open for 0% of the time, Pallas kernels for 22%

profile of v26, /device:TPU:0, one launch (start us, length us, event | category | flops | bytes accessed | tf_op | source)
XLA Modules:
  0.0 24.6 jit_solution(5147117255329043147)
XLA Ops:
  0.0 1.1 %shard_map.83.refs_0_ = bf16[8,64,128]{2,1,0:T(8,128)(2,1)S(1)} custom-call(s32[16]{0:T(128)} %dims_hbm.3, bf16[16,64,64]{2,1,0:T(8,128)(2,1)} %right_hbm.1), custom_call_target="tpu_custom_call" | custom-call | bytes 131072 | tf_op jit(solution)/shard_map/pallas_call | solution.py:236
  1.1 4.1 %collective-permute-start = (bf16[8,64,128]{2,1,0:T(8,128)(2,1)S(1)}, bf16[8,64,128]{2,1,0:T(8,128)(2,1)S(1)}, u32[]{:S(2)}, u32[]{:S(2)}) collective-permute-start(bf16[8,64,128]{2,1,0:T(8,128)(2,1)S(1)} %shard_map.83.refs_0_), channel_id=1, source_target_pairs={{0,8},{1,9},{2,10},{3,11},{4,12},{5,13},{6,14},{7,15},{8,0},{9,1},... | collective-permute-start | bytes 393224 | tf_op jit(solution)/shard_map/ppermute | solution.py:216
  5.2 0.0 collective-permute-start.6
  5.2 1.6 %collective-permute-start.5 = (bf16[8,64,128]{2,1,0:T(8,128)(2,1)S(1)}, bf16[8,64,128]{2,1,0:T(8,128)(2,1)S(1)}, u32[]{:S(2)}, u32[]{:S(2)}) collective-permute-start(bf16[8,64,128]{2,1,0:T(8,128)(2,1)S(1)} %shard_map.83.refs_0_), channel_id=1, source_target_pairs={{0,4},{1,5},{2,6},{3,7},{4,0},{5,1},{6,2},{7,3},{8,12},{9,13},{10,... | collective-permute-start | bytes 393224 | tf_op jit(solution)/shard_map/ppermute | solution.py:216
  6.8 1.5 %collective-permute-start.4 = (bf16[8,64,128]{2,1,0:T(8,128)(2,1)S(1)}, bf16[8,64,128]{2,1,0:T(8,128)(2,1)S(1)}, u32[]{:S(2)}, u32[]{:S(2)}) collective-permute-start(bf16[8,64,128]{2,1,0:T(8,128)(2,1)S(1)} %shard_map.83.refs_0_), channel_id=1, source_target_pairs={{0,2},{1,3},{2,0},{3,1},{4,6},{5,7},{6,4},{7,5},{8,10},{9,11},{10,... | collective-permute-start | bytes 393224 | tf_op jit(solution)/shard_map/ppermute | solution.py:216
  8.3 2.9 %shard_map.82 = (bf16[8,8,64,128]{3,2,1,0:T(8,128)(2,1)S(1)}, s32[202]{0:T(256)S(4)}) custom-call(s32[8]{0:T(128)} %dims_hbm.2, s32[8,8]{1,0:T(8,128)} %bitcast.1, s32[8,8]{1,0:T(8,128)} %owner_hbm.1, s32[8,8]{1,0:T(8,128)} %slot_hbm.1, bf16[8,64,64]{2,1,0:T(8,128)(2,1)} %left_hbm.1, bf16[8,8,64,128]{3,2,1,0:T(8,128)(2,1)} %psi_hbm.1), custom_call_target="tpu_custom_call" | custom-call | flops 67108864 | bytes 1048576 | tf_op jit(solution)/shard_map/pallas_call | solution.py:251
  11.1 0.5 %collective-permute-done.refs_3_ = bf16[8,64,128]{2,1,0:T(8,128)(2,1)S(1)} collective-permute-done((bf16[8,64,128]{2,1,0:T(8,128)(2,1)S(1)}, bf16[8,64,128]{2,1,0:T(8,128)(2,1)S(1)}, u32[]{:S(2)}, u32[]{:S(2)}) %collective-permute-start) | collective-permute-done | bytes 131104 | tf_op jit(solution)/shard_map/ppermute | solution.py:216
  11.6 0.7 %collective-permute-start.1 = (bf16[8,64,128]{2,1,0:T(8,128)(2,1)S(1)}, bf16[8,64,128]{2,1,0:T(8,128)(2,1)S(1)}, u32[]{:S(2)}, u32[]{:S(2)}) collective-permute-start(bf16[8,64,128]{2,1,0:T(8,128)(2,1)S(1)} %collective-permute-done.refs_3_), channel_id=1, source_target_pairs={{0,4},{1,3},{2,6},{3,1},{4,0},{5,7},{6,2},{7,5},{8,12},{9,11},{10,... | collective-permute-start | bytes 393224 | tf_op jit(solution)/shard_map/ppermute | solution.py:216
  12.3 0.5 %collective-permute-done.5.refs_2_ = bf16[8,64,128]{2,1,0:T(8,128)(2,1)S(1)} collective-permute-done((bf16[8,64,128]{2,1,0:T(8,128)(2,1)S(1)}, bf16[8,64,128]{2,1,0:T(8,128)(2,1)S(1)}, u32[]{:S(2)}, u32[]{:S(2)}) %collective-permute-start.5) | collective-permute-done | bytes 131104 | tf_op jit(solution)/shard_map/ppermute | solution.py:216
  12.8 1.5 %collective-permute-start.9 = (bf16[8,64,128]{2,1,0:T(8,128)(2,1)S(1)}, bf16[8,64,128]{2,1,0:T(8,128)(2,1)S(1)}, u32[]{:S(2)}, u32[]{:S(2)}) collective-permute-start(bf16[8,64,128]{2,1,0:T(8,128)(2,1)S(1)} %collective-permute-done.5.refs_2_), channel_id=1, source_target_pairs={{0,2},{1,3},{2,0},{3,1},{4,6},{5,7},{6,4},{7,5},{8,10},{9,11},{10,... | collective-permute-start | bytes 393224 | tf_op jit(solution)/shard_map/ppermute | solution.py:216
  14.3 0.0 collective-permute-start.8
  14.3 0.0 collective-permute-done.4.refs_1_
  14.3 0.5 %collective-permute-start.7 = (bf16[8,64,128]{2,1,0:T(8,128)(2,1)S(1)}, bf16[8,64,128]{2,1,0:T(8,128)(2,1)S(1)}, u32[]{:S(2)}, u32[]{:S(2)}) collective-permute-start(bf16[8,64,128]{2,1,0:T(8,128)(2,1)S(1)} %collective-permute-done.4.refs_1_), channel_id=1, source_target_pairs={{0,1},{1,0},{2,3},{3,2},{4,5},{5,4},{6,7},{7,6},{8,9},{9,8},{10,11... | collective-permute-start | bytes 393224 | tf_op jit(solution)/shard_map/ppermute | solution.py:216
  14.8 0.0 collective-permute-done.6.refs_5_
  14.8 0.5 %collective-permute-start.3 = (bf16[8,64,128]{2,1,0:T(8,128)(2,1)S(1)}, bf16[8,64,128]{2,1,0:T(8,128)(2,1)S(1)}, u32[]{:S(2)}, u32[]{:S(2)}) collective-permute-start(bf16[8,64,128]{2,1,0:T(8,128)(2,1)S(1)} %collective-permute-done.refs_3_), channel_id=1, source_target_pairs={{0,2},{1,5},{2,0},{3,7},{4,6},{5,1},{6,4},{7,3},{8,10},{9,13},{10,... | collective-permute-start | bytes 393224 | tf_op jit(solution)/shard_map/ppermute | solution.py:216
  15.3 1.3 %collective-permute-done.1.refs_4_ = bf16[8,64,128]{2,1,0:T(8,128)(2,1)S(1)} collective-permute-done((bf16[8,64,128]{2,1,0:T(8,128)(2,1)S(1)}, bf16[8,64,128]{2,1,0:T(8,128)(2,1)S(1)}, u32[]{:S(2)}, u32[]{:S(2)}) %collective-permute-start.1) | collective-permute-done | bytes 131104 | tf_op jit(solution)/shard_map/ppermute | solution.py:216
  16.6 1.7 %collective-permute-start.2 = (bf16[8,64,128]{2,1,0:T(8,128)(2,1)S(1)}, bf16[8,64,128]{2,1,0:T(8,128)(2,1)S(1)}, u32[]{:S(2)}, u32[]{:S(2)}) collective-permute-start(bf16[8,64,128]{2,1,0:T(8,128)(2,1)S(1)} %collective-permute-done.1.refs_4_), channel_id=1, source_target_pairs={{0,2},{1,5},{2,0},{3,7},{4,6},{5,1},{6,4},{7,3},{8,10},{9,13},{10,... | collective-permute-start | bytes 393224 | tf_op jit(solution)/shard_map/ppermute | solution.py:216
  18.2 0.0 collective-permute-done.9.refs_0_
  18.2 0.0 collective-permute-start.11
  18.3 0.0 collective-permute-done.8.refs_7_
  18.3 0.5 %collective-permute-start.12 = (bf16[8,64,128]{2,1,0:T(8,128)(2,1)S(1)}, bf16[8,64,128]{2,1,0:T(8,128)(2,1)S(1)}, u32[]{:S(2)}, u32[]{:S(2)}) collective-permute-start(bf16[8,64,128]{2,1,0:T(8,128)(2,1)S(1)} %collective-permute-done.1.refs_4_), channel_id=1, source_target_pairs={{0,1},{1,0},{2,3},{3,2},{4,5},{5,4},{6,7},{7,6},{8,9},{9,8},{10,11... | collective-permute-start | bytes 393224 | tf_op jit(solution)/shard_map/ppermute | solution.py:216
  18.8 0.0 collective-permute-done.7.refs_6_
  18.8 0.1 collective-permute-start.10
  18.8 1.6 %shard_map.84.early_ref = bf16[8,8,64,128]{3,2,1,0:T(8,128)(2,1)S(1)} custom-call(s32[202]{0:T(256)S(4)} %get-tuple-element.12.list_ref, bf16[8,8,64,128]{3,2,1,0:T(8,128)(2,1)S(1)} %get-tuple-element.15.half_ref, bf16[8,64,128]{2,1,0:T(8,128)(2,1)S(1)} %shard_map.83.refs_0_, bf16[8,64,128]{2,1,0:T(8,128)(2,1)S(1)} %collective-permute-done.4.refs_1_, ...), custom_call_target="tpu_custom_call" | custom-call | flops 67108864 | bytes 1048576 | tf_op jit(solution)/shard_map/pallas_call | solution.py:296
  20.4 0.0 collective-permute-done.3.refs_1_
  20.4 1.1 %collective-permute-done.2.refs_5_ = bf16[8,64,128]{2,1,0:T(8,128)(2,1)S(1)} collective-permute-done((bf16[8,64,128]{2,1,0:T(8,128)(2,1)S(1)}, bf16[8,64,128]{2,1,0:T(8,128)(2,1)S(1)}, u32[]{:S(2)}, u32[]{:S(2)}) %collective-permute-start.2) | collective-permute-done | bytes 131104 | tf_op jit(solution)/shard_map/ppermute | solution.py:216
  21.6 0.0 collective-permute-start.13
  21.6 0.5 %collective-permute-start.14 = (bf16[8,64,128]{2,1,0:T(8,128)(2,1)S(1)}, bf16[8,64,128]{2,1,0:T(8,128)(2,1)S(1)}, u32[]{:S(2)}, u32[]{:S(2)}) collective-permute-start(bf16[8,64,128]{2,1,0:T(8,128)(2,1)S(1)} %collective-permute-done.2.refs_5_), channel_id=1, source_target_pairs={{0,1},{1,0},{2,3},{3,2},{4,5},{5,4},{6,7},{7,6},{8,9},{9,8},{10,11... | collective-permute-start | bytes 393224 | tf_op jit(solution)/shard_map/ppermute | solution.py:216
  22.1 0.0 collective-permute-done.11.refs_3_
  22.1 0.0 collective-permute-done.10.refs_2_
  22.1 0.0 collective-permute-done.12.refs_4_
  22.1 1.1 %shard_map.85.middle_ref = bf16[8,8,64,128]{3,2,1,0:T(8,128)(2,1)S(1)} custom-call(s32[202]{0:T(256)S(4)} %get-tuple-element.12.list_ref, bf16[8,8,64,128]{3,2,1,0:T(8,128)(2,1)S(1)} %shard_map.84.early_ref, bf16[8,8,64,128]{3,2,1,0:T(8,128)(2,1)S(1)} %get-tuple-element.15.half_ref, bf16[8,64,128]{2,1,0:T(8,128)(2,1)S(1)} %collective-permute-done.9.refs_0_, ...), custom_call_target="tpu_custom_call" | custom-call | flops 16777216 | bytes 262144 | tf_op jit(solution)/shard_map/pallas_call | solution.py:308
  23.1 0.0 collective-permute-done.13.refs_0_
  23.1 0.0 collective-permute-done.14.refs_1_
  23.2 1.5 %shard_map.86 = bf16[8,8,64,128]{3,2,1,0:T(8,128)(2,1)} custom-call(s32[202]{0:T(256)S(4)} %get-tuple-element.12.list_ref, bf16[8,8,64,128]{3,2,1,0:T(8,128)(2,1)S(1)} %shard_map.85.middle_ref, bf16[8,8,64,128]{3,2,1,0:T(8,128)(2,1)S(1)} %get-tuple-element.15.half_ref, bf16[8,64,128]{2,1,0:T(8,128)(2,1)S(1)} %collective-permute-done.13.refs_0_, ...), custom_call_target="tpu_custom_call" | custom-call | flops 4194304 | bytes 1048576 | tf_op jit(solution)/shard_map/pallas_call | solution.py:317
Async XLA Ops:
  1.1 10.5 %collective-permute-start = (bf16[8,64,128]{2,1,0:T(8,128)(2,1)S(1)}, bf16[8,64,128]{2,1,0:T(8,128)(2,1)S(1)}, u32[]{:S(2)}, u32[]{:S(2)}) collective-permute-start(bf16[8,64,128]{2,1,0:T(8,128)(2,1)S(1)} %shard_map.83.refs_0_), channel_id=1, source_target_pairs={{0,8},{1,9},{2,10},{3,11},{4,12},{5,13},{6,14},{7,15},{8,0},{9,1},... | collective-permute-start | bytes 393224 | tf_op jit(solution)/shard_map/ppermute | solution.py:216
  5.2 9.6 %collective-permute-start.6 = (bf16[8,64,128]{2,1,0:T(8,128)(2,1)S(1)}, bf16[8,64,128]{2,1,0:T(8,128)(2,1)S(1)}, u32[]{:S(2)}, u32[]{:S(2)}) collective-permute-start(bf16[8,64,128]{2,1,0:T(8,128)(2,1)S(1)} %shard_map.83.refs_0_), channel_id=1, source_target_pairs={{0,1},{1,0},{2,3},{3,2},{4,5},{5,4},{6,7},{7,6},{8,9},{9,8},{10,11... | collective-permute-start | bytes 393224 | tf_op jit(solution)/shard_map/ppermute | solution.py:216
  5.2 7.6 %collective-permute-start.5 = (bf16[8,64,128]{2,1,0:T(8,128)(2,1)S(1)}, bf16[8,64,128]{2,1,0:T(8,128)(2,1)S(1)}, u32[]{:S(2)}, u32[]{:S(2)}) collective-permute-start(bf16[8,64,128]{2,1,0:T(8,128)(2,1)S(1)} %shard_map.83.refs_0_), channel_id=1, source_target_pairs={{0,4},{1,5},{2,6},{3,7},{4,0},{5,1},{6,2},{7,3},{8,12},{9,13},{10,... | collective-permute-start | bytes 393224 | tf_op jit(solution)/shard_map/ppermute | solution.py:216
  6.8 7.5 %collective-permute-start.4 = (bf16[8,64,128]{2,1,0:T(8,128)(2,1)S(1)}, bf16[8,64,128]{2,1,0:T(8,128)(2,1)S(1)}, u32[]{:S(2)}, u32[]{:S(2)}) collective-permute-start(bf16[8,64,128]{2,1,0:T(8,128)(2,1)S(1)} %shard_map.83.refs_0_), channel_id=1, source_target_pairs={{0,2},{1,3},{2,0},{3,1},{4,6},{5,7},{6,4},{7,5},{8,10},{9,11},{10,... | collective-permute-start | bytes 393224 | tf_op jit(solution)/shard_map/ppermute | solution.py:216
  11.6 5.0 %collective-permute-start.1 = (bf16[8,64,128]{2,1,0:T(8,128)(2,1)S(1)}, bf16[8,64,128]{2,1,0:T(8,128)(2,1)S(1)}, u32[]{:S(2)}, u32[]{:S(2)}) collective-permute-start(bf16[8,64,128]{2,1,0:T(8,128)(2,1)S(1)} %collective-permute-done.refs_3_), channel_id=1, source_target_pairs={{0,4},{1,3},{2,6},{3,1},{4,0},{5,7},{6,2},{7,5},{8,12},{9,11},{10,... | collective-permute-start | bytes 393224 | tf_op jit(solution)/shard_map/ppermute | solution.py:216
  12.8 5.5 %collective-permute-start.9 = (bf16[8,64,128]{2,1,0:T(8,128)(2,1)S(1)}, bf16[8,64,128]{2,1,0:T(8,128)(2,1)S(1)}, u32[]{:S(2)}, u32[]{:S(2)}) collective-permute-start(bf16[8,64,128]{2,1,0:T(8,128)(2,1)S(1)} %collective-permute-done.5.refs_2_), channel_id=1, source_target_pairs={{0,2},{1,3},{2,0},{3,1},{4,6},{5,7},{6,4},{7,5},{8,10},{9,11},{10,... | collective-permute-start | bytes 393224 | tf_op jit(solution)/shard_map/ppermute | solution.py:216
  14.3 4.0 %collective-permute-start.8 = (bf16[8,64,128]{2,1,0:T(8,128)(2,1)S(1)}, bf16[8,64,128]{2,1,0:T(8,128)(2,1)S(1)}, u32[]{:S(2)}, u32[]{:S(2)}) collective-permute-start(bf16[8,64,128]{2,1,0:T(8,128)(2,1)S(1)} %collective-permute-done.5.refs_2_), channel_id=1, source_target_pairs={{0,1},{1,0},{2,3},{3,2},{4,5},{5,4},{6,7},{7,6},{8,9},{9,8},{10,11... | collective-permute-start | bytes 393224 | tf_op jit(solution)/shard_map/ppermute | solution.py:216
  14.3 4.5 %collective-permute-start.7 = (bf16[8,64,128]{2,1,0:T(8,128)(2,1)S(1)}, bf16[8,64,128]{2,1,0:T(8,128)(2,1)S(1)}, u32[]{:S(2)}, u32[]{:S(2)}) collective-permute-start(bf16[8,64,128]{2,1,0:T(8,128)(2,1)S(1)} %collective-permute-done.4.refs_1_), channel_id=1, source_target_pairs={{0,1},{1,0},{2,3},{3,2},{4,5},{5,4},{6,7},{7,6},{8,9},{9,8},{10,11... | collective-permute-start | bytes 393224 | tf_op jit(solution)/shard_map/ppermute | solution.py:216
  14.8 5.6 %collective-permute-start.3 = (bf16[8,64,128]{2,1,0:T(8,128)(2,1)S(1)}, bf16[8,64,128]{2,1,0:T(8,128)(2,1)S(1)}, u32[]{:S(2)}, u32[]{:S(2)}) collective-permute-start(bf16[8,64,128]{2,1,0:T(8,128)(2,1)S(1)} %collective-permute-done.refs_3_), channel_id=1, source_target_pairs={{0,2},{1,5},{2,0},{3,7},{4,6},{5,1},{6,4},{7,3},{8,10},{9,13},{10,... | collective-permute-start | bytes 393224 | tf_op jit(solution)/shard_map/ppermute | solution.py:216
  16.6 5.0 %collective-permute-start.2 = (bf16[8,64,128]{2,1,0:T(8,128)(2,1)S(1)}, bf16[8,64,128]{2,1,0:T(8,128)(2,1)S(1)}, u32[]{:S(2)}, u32[]{:S(2)}) collective-permute-start(bf16[8,64,128]{2,1,0:T(8,128)(2,1)S(1)} %collective-permute-done.1.refs_4_), channel_id=1, source_target_pairs={{0,2},{1,5},{2,0},{3,7},{4,6},{5,1},{6,4},{7,3},{8,10},{9,13},{10,... | collective-permute-start | bytes 393224 | tf_op jit(solution)/shard_map/ppermute | solution.py:216
  18.2 3.8 %collective-permute-start.11 = (bf16[8,64,128]{2,1,0:T(8,128)(2,1)S(1)}, bf16[8,64,128]{2,1,0:T(8,128)(2,1)S(1)}, u32[]{:S(2)}, u32[]{:S(2)}) collective-permute-start(bf16[8,64,128]{2,1,0:T(8,128)(2,1)S(1)} %collective-permute-done.refs_3_), channel_id=1, source_target_pairs={{0,1},{1,0},{2,3},{3,2},{4,5},{5,4},{6,7},{7,6},{8,9},{9,8},{10,11... | collective-permute-start | bytes 393224 | tf_op jit(solution)/shard_map/ppermute | solution.py:216
  18.3 3.8 %collective-permute-start.12 = (bf16[8,64,128]{2,1,0:T(8,128)(2,1)S(1)}, bf16[8,64,128]{2,1,0:T(8,128)(2,1)S(1)}, u32[]{:S(2)}, u32[]{:S(2)}) collective-permute-start(bf16[8,64,128]{2,1,0:T(8,128)(2,1)S(1)} %collective-permute-done.1.refs_4_), channel_id=1, source_target_pairs={{0,1},{1,0},{2,3},{3,2},{4,5},{5,4},{6,7},{7,6},{8,9},{9,8},{10,11... | collective-permute-start | bytes 393224 | tf_op jit(solution)/shard_map/ppermute | solution.py:216
  18.8 3.3 %collective-permute-start.10 = (bf16[8,64,128]{2,1,0:T(8,128)(2,1)S(1)}, bf16[8,64,128]{2,1,0:T(8,128)(2,1)S(1)}, u32[]{:S(2)}, u32[]{:S(2)}) collective-permute-start(bf16[8,64,128]{2,1,0:T(8,128)(2,1)S(1)} %collective-permute-done.9.refs_0_), channel_id=1, source_target_pairs={{0,1},{1,0},{2,3},{3,2},{4,5},{5,4},{6,7},{7,6},{8,9},{9,8},{10,11... | collective-permute-start | bytes 393224 | tf_op jit(solution)/shard_map/ppermute | solution.py:216
  21.6 1.6 %collective-permute-start.13 = (bf16[8,64,128]{2,1,0:T(8,128)(2,1)S(1)}, bf16[8,64,128]{2,1,0:T(8,128)(2,1)S(1)}, u32[]{:S(2)}, u32[]{:S(2)}) collective-permute-start(bf16[8,64,128]{2,1,0:T(8,128)(2,1)S(1)} %collective-permute-done.3.refs_1_), channel_id=1, source_target_pairs={{0,1},{1,0},{2,3},{3,2},{4,5},{5,4},{6,7},{7,6},{8,9},{9,8},{10,11... | collective-permute-start | bytes 393224 | tf_op jit(solution)/shard_map/ppermute | solution.py:216
  21.6 1.6 %collective-permute-start.14 = (bf16[8,64,128]{2,1,0:T(8,128)(2,1)S(1)}, bf16[8,64,128]{2,1,0:T(8,128)(2,1)S(1)}, u32[]{:S(2)}, u32[]{:S(2)}) collective-permute-start(bf16[8,64,128]{2,1,0:T(8,128)(2,1)S(1)} %collective-permute-done.2.refs_5_), channel_id=1, source_target_pairs={{0,1},{1,0},{2,3},{3,2},{4,5},{5,4},{6,7},{7,6},{8,9},{9,8},{10,11... | collective-permute-start | bytes 393224 | tf_op jit(solution)/shard_map/ppermute | solution.py:216

commit v27 on v24

--- a/solution.py
+++ b/solution.py
@@ -301,8 +301,12 @@
         cost_estimate=pl.CostEstimate(flops=flops, bytes_accessed=2 * psi.size, transcendentals=0),
     )(listed, half, *early)
     if by_swaps:
-        pieces[END], pieces[SECOND], sigma = lax.optimization_barrier((pieces[END], pieces[SECOND], sigma))
-        share(END, SECOND)
+        held = (partner(FIRST),)
+        sigma, pieces[SECOND], ends = lax.optimization_barrier((sigma, pieces[SECOND], [pieces[name] for name in held]))
+        pieces.update(zip(held, ends))
+        share(SECOND)
+        pieces[END], sigma = lax.optimization_barrier((pieces[END], sigma))
+        share(END)
         sigma = pl.pallas_call(
             middle_kernel,
             out_shape=jax.ShapeDtypeStruct(psi.shape, jnp.bfloat16),

time: 25.4 us -> 26.1 us (1.028)
  waiting for transfers between devices: 4.2 us -> 6.07 us
  starting transfers between devices: 13.1 us -> 11.6 us
  Pallas kernels: 7.89 us -> 8.31 us
    ppermute x15, waiting for transfers between devices: 4.2 us -> 6.07 us  [swap(): lax.ppermute(piece, 'sec', [(i, i ^ (odd_bit if i & CORE else even_bit))...]
    ppermute x15, starting transfers between devices: 13.1 us -> 11.6 us  [swap(): lax.ppermute(piece, 'sec', [(i, i ^ (odd_bit if i & CORE else even_bit))...]
    pallas_call x1, Pallas kernels: 1.05 us -> 1.52 us  [per_device(): pl.pallas_call(middle_kernel, out_shape=jax.ShapeDtypeStruct(psi.shape, j...]
  transfers between devices with their start and end apart: 15 -> 15, of which waited for: 5 -> 4; matrix products, arithmetic and copies ran while one was open for 0% -> 0% of each run, Pallas kernels for 22% -> 23%
where the time goes in v27:
time: 26.1 us; the launch traced here: 26 us
  starting transfers between devices  11.6 us (44%)
  Pallas kernels  8.31 us (32%)
  waiting for transfers between devices  6.07 us (23%)
    ppermute x15, starting transfers between devices, swap(): lax.ppermute(piece, 'sec', [(i, i ^ (odd_bit if i & CORE else even_bit))...  11.6 us
    ppermute x15, waiting for transfers between devices, swap(): lax.ppermute(piece, 'sec', [(i, i ^ (odd_bit if i & CORE else even_bit))...  6.07 us
    pallas_call x1, Pallas kernels, per_device(): pl.pallas_call(functools.partial(left_kernel, pair_count, len(EARLY if by...  2.85 us
    pallas_call x1, Pallas kernels, per_device(): pl.pallas_call(early_kernel, out_shape=jax.ShapeDtypeStruct(psi.shape, jn...  1.59 us
    pallas_call x1, Pallas kernels, per_device(): pl.pallas_call(middle_kernel, out_shape=jax.ShapeDtypeStruct(psi.shape, j...  1.52 us
    pallas_call x1, Pallas kernels, per_device(): pl.pallas_call(last_kernel, out_shape=jax.ShapeDtypeStruct(psi.shape, jnp...  1.26 us
    pallas_call x1, Pallas kernels, per_device(): pl.pallas_call(pack_kernel, out_shape=jax.ShapeDtypeStruct((pair_count, t...  1.09 us
  transfers between devices with their start and end apart: 15, of which 4 were waited for; matrix products, arithmetic and copies ran while one was open for 0% of the time, Pallas kernels for 23%

profile of v27, /device:TPU:0, one launch (start us, length us, event | category | flops | bytes accessed | tf_op | source)
XLA Modules:
  0.0 26.0 jit_solution(830213610574708130)
XLA Ops:
  0.0 1.1 %shard_map.83.refs_0_ = bf16[8,64,128]{2,1,0:T(8,128)(2,1)S(1)} custom-call(s32[16]{0:T(128)} %dims_hbm.3, bf16[16,64,64]{2,1,0:T(8,128)(2,1)} %right_hbm.1), custom_call_target="tpu_custom_call" | custom-call | bytes 131072 | tf_op jit(solution)/shard_map/pallas_call | solution.py:234
  1.1 4.1 %collective-permute-start = (bf16[8,64,128]{2,1,0:T(8,128)(2,1)S(1)}, bf16[8,64,128]{2,1,0:T(8,128)(2,1)S(1)}, u32[]{:S(2)}, u32[]{:S(2)}) collective-permute-start(bf16[8,64,128]{2,1,0:T(8,128)(2,1)S(1)} %shard_map.83.refs_0_), channel_id=1, source_target_pairs={{0,8},{1,9},{2,10},{3,11},{4,12},{5,13},{6,14},{7,15},{8,0},{9,1},... | collective-permute-start | bytes 393224 | tf_op jit(solution)/shard_map/ppermute | solution.py:214
  5.2 1.6 %collective-permute-start.4 = (bf16[8,64,128]{2,1,0:T(8,128)(2,1)S(1)}, bf16[8,64,128]{2,1,0:T(8,128)(2,1)S(1)}, u32[]{:S(2)}, u32[]{:S(2)}) collective-permute-start(bf16[8,64,128]{2,1,0:T(8,128)(2,1)S(1)} %shard_map.83.refs_0_), channel_id=1, source_target_pairs={{0,4},{1,5},{2,6},{3,7},{4,0},{5,1},{6,2},{7,3},{8,12},{9,13},{10,... | collective-permute-start | bytes 393224 | tf_op jit(solution)/shard_map/ppermute | solution.py:214
  6.8 0.0 collective-permute-start.5
  6.8 1.5 %collective-permute-start.3 = (bf16[8,64,128]{2,1,0:T(8,128)(2,1)S(1)}, bf16[8,64,128]{2,1,0:T(8,128)(2,1)S(1)}, u32[]{:S(2)}, u32[]{:S(2)}) collective-permute-start(bf16[8,64,128]{2,1,0:T(8,128)(2,1)S(1)} %shard_map.83.refs_0_), channel_id=1, source_target_pairs={{0,2},{1,3},{2,0},{3,1},{4,6},{5,7},{6,4},{7,5},{8,10},{9,11},{10,... | collective-permute-start | bytes 393224 | tf_op jit(solution)/shard_map/ppermute | solution.py:214
  8.3 2.9 %shard_map.82 = (bf16[8,8,64,128]{3,2,1,0:T(8,128)(2,1)S(1)}, s32[202]{0:T(256)S(4)}) custom-call(s32[8]{0:T(128)} %dims_hbm.2, s32[8,8]{1,0:T(8,128)} %bitcast.1, s32[8,8]{1,0:T(8,128)} %owner_hbm.1, s32[8,8]{1,0:T(8,128)} %slot_hbm.1, bf16[8,64,64]{2,1,0:T(8,128)(2,1)} %left_hbm.1, bf16[8,8,64,128]{3,2,1,0:T(8,128)(2,1)} %psi_hbm.1), custom_call_target="tpu_custom_call" | custom-call | flops 67108864 | bytes 1048576 | tf_op jit(solution)/shard_map/pallas_call | solution.py:249
  11.1 0.5 %collective-permute-done.refs_3_ = bf16[8,64,128]{2,1,0:T(8,128)(2,1)S(1)} collective-permute-done((bf16[8,64,128]{2,1,0:T(8,128)(2,1)S(1)}, bf16[8,64,128]{2,1,0:T(8,128)(2,1)S(1)}, u32[]{:S(2)}, u32[]{:S(2)}) %collective-permute-start) | collective-permute-done | bytes 131104 | tf_op jit(solution)/shard_map/ppermute | solution.py:214
  11.6 0.6 %collective-permute-start.1 = (bf16[8,64,128]{2,1,0:T(8,128)(2,1)S(1)}, bf16[8,64,128]{2,1,0:T(8,128)(2,1)S(1)}, u32[]{:S(2)}, u32[]{:S(2)}) collective-permute-start(bf16[8,64,128]{2,1,0:T(8,128)(2,1)S(1)} %collective-permute-done.refs_3_), channel_id=1, source_target_pairs={{0,4},{1,3},{2,6},{3,1},{4,0},{5,7},{6,2},{7,5},{8,12},{9,11},{10,... | collective-permute-start | bytes 393224 | tf_op jit(solution)/shard_map/ppermute | solution.py:214
  12.2 0.0 collective-permute-done.4.refs_2_
  12.2 1.5 %collective-permute-start.10 = (bf16[8,64,128]{2,1,0:T(8,128)(2,1)S(1)}, bf16[8,64,128]{2,1,0:T(8,128)(2,1)S(1)}, u32[]{:S(2)}, u32[]{:S(2)}) collective-permute-start(bf16[8,64,128]{2,1,0:T(8,128)(2,1)S(1)} %collective-permute-done.4.refs_2_), channel_id=1, source_target_pairs={{0,2},{1,3},{2,0},{3,1},{4,6},{5,7},{6,4},{7,5},{8,10},{9,11},{10,... | collective-permute-start | bytes 393224 | tf_op jit(solution)/shard_map/ppermute | solution.py:214
  13.7 0.0 collective-permute-start.7
  13.7 0.0 collective-permute-done.3.refs_1_
  13.7 0.5 %collective-permute-start.6 = (bf16[8,64,128]{2,1,0:T(8,128)(2,1)S(1)}, bf16[8,64,128]{2,1,0:T(8,128)(2,1)S(1)}, u32[]{:S(2)}, u32[]{:S(2)}) collective-permute-start(bf16[8,64,128]{2,1,0:T(8,128)(2,1)S(1)} %collective-permute-done.3.refs_1_), channel_id=1, source_target_pairs={{0,1},{1,0},{2,3},{3,2},{4,5},{5,4},{6,7},{7,6},{8,9},{9,8},{10,11... | collective-permute-start | bytes 393224 | tf_op jit(solution)/shard_map/ppermute | solution.py:214
  14.2 0.0 collective-permute-done.5.refs_5_
  14.2 0.5 %collective-permute-start.8 = (bf16[8,64,128]{2,1,0:T(8,128)(2,1)S(1)}, bf16[8,64,128]{2,1,0:T(8,128)(2,1)S(1)}, u32[]{:S(2)}, u32[]{:S(2)}) collective-permute-start(bf16[8,64,128]{2,1,0:T(8,128)(2,1)S(1)} %collective-permute-done.refs_3_), channel_id=1, source_target_pairs={{0,2},{1,5},{2,0},{3,7},{4,6},{5,1},{6,4},{7,3},{8,10},{9,13},{10,... | collective-permute-start | bytes 393224 | tf_op jit(solution)/shard_map/ppermute | solution.py:214
  14.8 1.8 %collective-permute-done.1.refs_4_ = bf16[8,64,128]{2,1,0:T(8,128)(2,1)S(1)} collective-permute-done((bf16[8,64,128]{2,1,0:T(8,128)(2,1)S(1)}, bf16[8,64,128]{2,1,0:T(8,128)(2,1)S(1)}, u32[]{:S(2)}, u32[]{:S(2)}) %collective-permute-start.1) | collective-permute-done | bytes 131104 | tf_op jit(solution)/shard_map/ppermute | solution.py:214
  16.6 0.0 collective-permute-start.9
  16.6 1.7 %collective-permute-done.10.refs_0_ = bf16[8,64,128]{2,1,0:T(8,128)(2,1)S(1)} collective-permute-done((bf16[8,64,128]{2,1,0:T(8,128)(2,1)S(1)}, bf16[8,64,128]{2,1,0:T(8,128)(2,1)S(1)}, u32[]{:S(2)}, u32[]{:S(2)}) %collective-permute-start.10) | collective-permute-done | bytes 131104 | tf_op jit(solution)/shard_map/ppermute | solution.py:214
  18.2 0.6 %collective-permute-start.2 = (bf16[8,64,128]{2,1,0:T(8,128)(2,1)S(1)}, bf16[8,64,128]{2,1,0:T(8,128)(2,1)S(1)}, u32[]{:S(2)}, u32[]{:S(2)}) collective-permute-start(bf16[8,64,128]{2,1,0:T(8,128)(2,1)S(1)} %collective-permute-done.1.refs_4_), channel_id=1, source_target_pairs={{0,2},{1,5},{2,0},{3,7},{4,6},{5,1},{6,4},{7,3},{8,10},{9,13},{10,... | collective-permute-start | bytes 393224 | tf_op jit(solution)/shard_map/ppermute | solution.py:214
  18.8 0.0 collective-permute-done.7.refs_7_
  18.8 0.0 collective-permute-start.12
  18.9 0.0 collective-permute-done.6.refs_6_
  18.9 0.5 %collective-permute-start.11 = (bf16[8,64,128]{2,1,0:T(8,128)(2,1)S(1)}, bf16[8,64,128]{2,1,0:T(8,128)(2,1)S(1)}, u32[]{:S(2)}, u32[]{:S(2)}) collective-permute-start(bf16[8,64,128]{2,1,0:T(8,128)(2,1)S(1)} %collective-permute-done.10.refs_0_), channel_id=1, source_target_pairs={{0,1},{1,0},{2,3},{3,2},{4,5},{5,4},{6,7},{7,6},{8,9},{9,8},{10,11... | collective-permute-start | bytes 393224 | tf_op jit(solution)/shard_map/ppermute | solution.py:214
  19.4 1.6 %shard_map.84.early_ref = bf16[8,8,64,128]{3,2,1,0:T(8,128)(2,1)S(1)} custom-call(s32[202]{0:T(256)S(4)} %get-tuple-element.14.list_ref, bf16[8,8,64,128]{3,2,1,0:T(8,128)(2,1)S(1)} %get-tuple-element.17.half_ref, bf16[8,64,128]{2,1,0:T(8,128)(2,1)S(1)} %shard_map.83.refs_0_, bf16[8,64,128]{2,1,0:T(8,128)(2,1)S(1)} %collective-permute-done.3.refs_1_, ...), custom_call_target="tpu_custom_call" | custom-call | flops 67108864 | bytes 1048576 | tf_op jit(solution)/shard_map/pallas_call | solution.py:294
  21.0 0.0 collective-permute-done.8.refs_1_
  21.0 0.0 collective-permute-done.9.refs_4_
  21.0 0.1 collective-permute-start.13
  21.1 2.1 %collective-permute-done.2.refs_6_ = bf16[8,64,128]{2,1,0:T(8,128)(2,1)S(1)} collective-permute-done((bf16[8,64,128]{2,1,0:T(8,128)(2,1)S(1)}, bf16[8,64,128]{2,1,0:T(8,128)(2,1)S(1)}, u32[]{:S(2)}, u32[]{:S(2)}) %collective-permute-start.2) | collective-permute-done | bytes 131104 | tf_op jit(solution)/shard_map/ppermute | solution.py:214
  23.2 0.0 collective-permute-start.14
  23.2 0.0 collective-permute-done.12.refs_3_
  23.2 0.0 collective-permute-done.11.refs_2_
  23.2 0.0 collective-permute-done.13.refs_5_
  23.2 1.5 %shard_map.85.middle_ref = bf16[8,8,64,128]{3,2,1,0:T(8,128)(2,1)S(1)} custom-call(s32[202]{0:T(256)S(4)} %get-tuple-element.14.list_ref, bf16[8,8,64,128]{3,2,1,0:T(8,128)(2,1)S(1)} %shard_map.84.early_ref, bf16[8,8,64,128]{3,2,1,0:T(8,128)(2,1)S(1)} %get-tuple-element.17.half_ref, bf16[8,64,128]{2,1,0:T(8,128)(2,1)S(1)} %collective-permute-done.10.refs_0_, ...), custom_call_target="tpu_custom_call" | custom-call | flops 16777216 | bytes 262144 | tf_op jit(solution)/shard_map/pallas_call | solution.py:310
  24.8 0.0 collective-permute-done.14.pairs_ref
  24.8 1.3 %shard_map.86 = bf16[8,8,64,128]{3,2,1,0:T(8,128)(2,1)} custom-call(s32[202]{0:T(256)S(4)} %get-tuple-element.14.list_ref, bf16[8,8,64,128]{3,2,1,0:T(8,128)(2,1)S(1)} %shard_map.85.middle_ref, bf16[8,8,64,128]{3,2,1,0:T(8,128)(2,1)S(1)} %get-tuple-element.17.half_ref, bf16[8,64,128]{2,1,0:T(8,128)(2,1)S(1)} %collective-permute-done.14.pairs_ref), custom_call_target="tpu_custom_call" | custom-call | flops 4194304 | bytes 1048576 | tf_op jit(solution)/shard_map/pallas_call | solution.py:319
Async XLA Ops:
  1.1 10.5 %collective-permute-start = (bf16[8,64,128]{2,1,0:T(8,128)(2,1)S(1)}, bf16[8,64,128]{2,1,0:T(8,128)(2,1)S(1)}, u32[]{:S(2)}, u32[]{:S(2)}) collective-permute-start(bf16[8,64,128]{2,1,0:T(8,128)(2,1)S(1)} %shard_map.83.refs_0_), channel_id=1, source_target_pairs={{0,8},{1,9},{2,10},{3,11},{4,12},{5,13},{6,14},{7,15},{8,0},{9,1},... | collective-permute-start | bytes 393224 | tf_op jit(solution)/shard_map/ppermute | solution.py:214
  5.2 7.0 %collective-permute-start.4 = (bf16[8,64,128]{2,1,0:T(8,128)(2,1)S(1)}, bf16[8,64,128]{2,1,0:T(8,128)(2,1)S(1)}, u32[]{:S(2)}, u32[]{:S(2)}) collective-permute-start(bf16[8,64,128]{2,1,0:T(8,128)(2,1)S(1)} %shard_map.83.refs_0_), channel_id=1, source_target_pairs={{0,4},{1,5},{2,6},{3,7},{4,0},{5,1},{6,2},{7,3},{8,12},{9,13},{10,... | collective-permute-start | bytes 393224 | tf_op jit(solution)/shard_map/ppermute | solution.py:214
  6.8 7.5 %collective-permute-start.5 = (bf16[8,64,128]{2,1,0:T(8,128)(2,1)S(1)}, bf16[8,64,128]{2,1,0:T(8,128)(2,1)S(1)}, u32[]{:S(2)}, u32[]{:S(2)}) collective-permute-start(bf16[8,64,128]{2,1,0:T(8,128)(2,1)S(1)} %shard_map.83.refs_0_), channel_id=1, source_target_pairs={{0,1},{1,0},{2,3},{3,2},{4,5},{5,4},{6,7},{7,6},{8,9},{9,8},{10,11... | collective-permute-start | bytes 393224 | tf_op jit(solution)/shard_map/ppermute | solution.py:214
  6.8 6.9 %collective-permute-start.3 = (bf16[8,64,128]{2,1,0:T(8,128)(2,1)S(1)}, bf16[8,64,128]{2,1,0:T(8,128)(2,1)S(1)}, u32[]{:S(2)}, u32[]{:S(2)}) collective-permute-start(bf16[8,64,128]{2,1,0:T(8,128)(2,1)S(1)} %shard_map.83.refs_0_), channel_id=1, source_target_pairs={{0,2},{1,3},{2,0},{3,1},{4,6},{5,7},{6,4},{7,5},{8,10},{9,11},{10,... | collective-permute-start | bytes 393224 | tf_op jit(solution)/shard_map/ppermute | solution.py:214
  11.6 5.0 %collective-permute-start.1 = (bf16[8,64,128]{2,1,0:T(8,128)(2,1)S(1)}, bf16[8,64,128]{2,1,0:T(8,128)(2,1)S(1)}, u32[]{:S(2)}, u32[]{:S(2)}) collective-permute-start(bf16[8,64,128]{2,1,0:T(8,128)(2,1)S(1)} %collective-permute-done.refs_3_), channel_id=1, source_target_pairs={{0,4},{1,3},{2,6},{3,1},{4,0},{5,7},{6,2},{7,5},{8,12},{9,11},{10,... | collective-permute-start | bytes 393224 | tf_op jit(solution)/shard_map/ppermute | solution.py:214
  12.2 6.0 %collective-permute-start.10 = (bf16[8,64,128]{2,1,0:T(8,128)(2,1)S(1)}, bf16[8,64,128]{2,1,0:T(8,128)(2,1)S(1)}, u32[]{:S(2)}, u32[]{:S(2)}) collective-permute-start(bf16[8,64,128]{2,1,0:T(8,128)(2,1)S(1)} %collective-permute-done.4.refs_2_), channel_id=1, source_target_pairs={{0,2},{1,3},{2,0},{3,1},{4,6},{5,7},{6,4},{7,5},{8,10},{9,11},{10,... | collective-permute-start | bytes 393224 | tf_op jit(solution)/shard_map/ppermute | solution.py:214
  13.7 5.1 %collective-permute-start.7 = (bf16[8,64,128]{2,1,0:T(8,128)(2,1)S(1)}, bf16[8,64,128]{2,1,0:T(8,128)(2,1)S(1)}, u32[]{:S(2)}, u32[]{:S(2)}) collective-permute-start(bf16[8,64,128]{2,1,0:T(8,128)(2,1)S(1)} %collective-permute-done.4.refs_2_), channel_id=1, source_target_pairs={{0,1},{1,0},{2,3},{3,2},{4,5},{5,4},{6,7},{7,6},{8,9},{9,8},{10,11... | collective-permute-start | bytes 393224 | tf_op jit(solution)/shard_map/ppermute | solution.py:214
  13.7 5.1 %collective-permute-start.6 = (bf16[8,64,128]{2,1,0:T(8,128)(2,1)S(1)}, bf16[8,64,128]{2,1,0:T(8,128)(2,1)S(1)}, u32[]{:S(2)}, u32[]{:S(2)}) collective-permute-start(bf16[8,64,128]{2,1,0:T(8,128)(2,1)S(1)} %collective-permute-done.3.refs_1_), channel_id=1, source_target_pairs={{0,1},{1,0},{2,3},{3,2},{4,5},{5,4},{6,7},{7,6},{8,9},{9,8},{10,11... | collective-permute-start | bytes 393224 | tf_op jit(solution)/shard_map/ppermute | solution.py:214
  14.2 6.7 %collective-permute-start.8 = (bf16[8,64,128]{2,1,0:T(8,128)(2,1)S(1)}, bf16[8,64,128]{2,1,0:T(8,128)(2,1)S(1)}, u32[]{:S(2)}, u32[]{:S(2)}) collective-permute-start(bf16[8,64,128]{2,1,0:T(8,128)(2,1)S(1)} %collective-permute-done.refs_3_), channel_id=1, source_target_pairs={{0,2},{1,5},{2,0},{3,7},{4,6},{5,1},{6,4},{7,3},{8,10},{9,13},{10,... | collective-permute-start | bytes 393224 | tf_op jit(solution)/shard_map/ppermute | solution.py:214
  16.6 4.4 %collective-permute-start.9 = (bf16[8,64,128]{2,1,0:T(8,128)(2,1)S(1)}, bf16[8,64,128]{2,1,0:T(8,128)(2,1)S(1)}, u32[]{:S(2)}, u32[]{:S(2)}) collective-permute-start(bf16[8,64,128]{2,1,0:T(8,128)(2,1)S(1)} %collective-permute-done.1.refs_4_), channel_id=1, source_target_pairs={{0,1},{1,0},{2,3},{3,2},{4,5},{5,4},{6,7},{7,6},{8,9},{9,8},{10,11... | collective-permute-start | bytes 393224 | tf_op jit(solution)/shard_map/ppermute | solution.py:214
  18.2 5.0 %collective-permute-start.2 = (bf16[8,64,128]{2,1,0:T(8,128)(2,1)S(1)}, bf16[8,64,128]{2,1,0:T(8,128)(2,1)S(1)}, u32[]{:S(2)}, u32[]{:S(2)}) collective-permute-start(bf16[8,64,128]{2,1,0:T(8,128)(2,1)S(1)} %collective-permute-done.1.refs_4_), channel_id=1, source_target_pairs={{0,2},{1,5},{2,0},{3,7},{4,6},{5,1},{6,4},{7,3},{8,10},{9,13},{10,... | collective-permute-start | bytes 393224 | tf_op jit(solution)/shard_map/ppermute | solution.py:214
  18.8 4.4 %collective-permute-start.12 = (bf16[8,64,128]{2,1,0:T(8,128)(2,1)S(1)}, bf16[8,64,128]{2,1,0:T(8,128)(2,1)S(1)}, u32[]{:S(2)}, u32[]{:S(2)}) collective-permute-start(bf16[8,64,128]{2,1,0:T(8,128)(2,1)S(1)} %collective-permute-done.refs_3_), channel_id=1, source_target_pairs={{0,1},{1,0},{2,3},{3,2},{4,5},{5,4},{6,7},{7,6},{8,9},{9,8},{10,11... | collective-permute-start | bytes 393224 | tf_op jit(solution)/shard_map/ppermute | solution.py:214
  18.9 4.4 %collective-permute-start.11 = (bf16[8,64,128]{2,1,0:T(8,128)(2,1)S(1)}, bf16[8,64,128]{2,1,0:T(8,128)(2,1)S(1)}, u32[]{:S(2)}, u32[]{:S(2)}) collective-permute-start(bf16[8,64,128]{2,1,0:T(8,128)(2,1)S(1)} %collective-permute-done.10.refs_0_), channel_id=1, source_target_pairs={{0,1},{1,0},{2,3},{3,2},{4,5},{5,4},{6,7},{7,6},{8,9},{9,8},{10,11... | collective-permute-start | bytes 393224 | tf_op jit(solution)/shard_map/ppermute | solution.py:214
  21.0 2.2 %collective-permute-start.13 = (bf16[8,64,128]{2,1,0:T(8,128)(2,1)S(1)}, bf16[8,64,128]{2,1,0:T(8,128)(2,1)S(1)}, u32[]{:S(2)}, u32[]{:S(2)}) collective-permute-start(bf16[8,64,128]{2,1,0:T(8,128)(2,1)S(1)} %collective-permute-done.8.refs_1_), channel_id=1, source_target_pairs={{0,1},{1,0},{2,3},{3,2},{4,5},{5,4},{6,7},{7,6},{8,9},{9,8},{10,11... | collective-permute-start | bytes 393224 | tf_op jit(solution)/shard_map/ppermute | solution.py:214
  23.2 1.6 %collective-permute-start.14 = (bf16[8,64,128]{2,1,0:T(8,128)(2,1)S(1)}, bf16[8,64,128]{2,1,0:T(8,128)(2,1)S(1)}, u32[]{:S(2)}, u32[]{:S(2)}) collective-permute-start(bf16[8,64,128]{2,1,0:T(8,128)(2,1)S(1)} %collective-permute-done.2.refs_6_), channel_id=1, source_target_pairs={{0,1},{1,0},{2,3},{3,2},{4,5},{5,4},{6,7},{7,6},{8,9},{9,8},{10,11... | collective-permute-start | bytes 393224 | tf_op jit(solution)/shard_map/ppermute | solution.py:214

commit v28 on v26

--- a/solution.py
+++ b/solution.py
@@ -36,19 +36,31 @@
 
 def pack_kernel(dims_hbm, right_hbm, pairs_ref, dims_ref, right_ref, sems):
     count, tile, width = pairs_ref.shape
-    copies = load_all((dims_hbm, dims_ref, sems.at[0]), (right_hbm, right_ref, sems.at[1]))
+    parts = sems.shape[0] - 1
+    step = count // parts
+    copies = load_all(
+        (dims_hbm, dims_ref, sems.at[parts, 0]),
+        *[
+            (right_hbm.at[pl.ds(half * count + part * step, step)],
+             right_ref.at[pl.ds(half * count + part * step, step)], sems.at[part, half])
+            for part in range(parts)
+            for half in range(2)
+        ],
+    )
     rows = lax.broadcasted_iota(jnp.int32, (tile, tile), 0)
     cols = lax.broadcasted_iota(jnp.int32, (tile, tile), 1)
     most = jnp.maximum(rows, cols)
-    for copy in copies:
-        copy.wait()
 
     def kept(b):
         return jnp.where(most < dims_ref[b], right_ref[b].astype(jnp.float32), 0.0)
 
-    for p in range(count):
-        both = jnp.concatenate([kept(p), kept(p + count)], axis=0)
-        pairs_ref[p] = both.T.astype(jnp.bfloat16)
+    copies[0].wait()
+    for part in range(parts):
+        for copy in copies[1 + 2 * part:3 + 2 * part]:
+            copy.wait()
+        for p in range(part * step, (part + 1) * step):
+            both = jnp.concatenate([kept(p), kept(p + count)], axis=0)
+            pairs_ref[p] = both.T.astype(jnp.bfloat16)
 
 
 def left_kernel(
@@ -241,7 +253,7 @@
         scratch_shapes=[
             pltpu.SMEM(dims_right.shape, jnp.int32),
             pltpu.VMEM(right_ops.shape, jnp.bfloat16),
-            pltpu.SemaphoreType.DMA((2,)),
+            pltpu.SemaphoreType.DMA((5, 2)),
         ],
         compiler_params=params,
         cost_estimate=pl.CostEstimate(flops=0, bytes_accessed=2 * right_ops.size, transcendentals=0),

time: 24.9 us -> 25 us (level)
  no operation moved by 1% of the time
where the time goes in v28:
time: 25 us; the launch traced here: 24.9 us
  starting transfers between devices  13.1 us (52%)
  Pallas kernels  8.31 us (33%)
  waiting for transfers between devices  3.38 us (14%)
    ppermute x15, starting transfers between devices, swap(): lax.ppermute(piece, 'sec', [(i, i ^ (odd_bit if i & CORE else even_bit))...  13.1 us
    ppermute x15, waiting for transfers between devices, swap(): lax.ppermute(piece, 'sec', [(i, i ^ (odd_bit if i & CORE else even_bit))...  3.38 us
    pallas_call x1, Pallas kernels, per_device(): pl.pallas_call(functools.partial(left_kernel, pair_count, len(EARLY if by...  2.85 us
    pallas_call x1, Pallas kernels, per_device(): pl.pallas_call(early_kernel, out_shape=jax.ShapeDtypeStruct(psi.shape, jn...  1.59 us
    pallas_call x1, Pallas kernels, per_device(): pl.pallas_call(last_kernel, out_shape=jax.ShapeDtypeStruct(psi.shape, jnp...  1.59 us
    pallas_call x1, Pallas kernels, per_device(): pl.pallas_call(pack_kernel, out_shape=jax.ShapeDtypeStruct((pair_count, t...  1.23 us
    pallas_call x1, Pallas kernels, per_device(): pl.pallas_call(middle_kernel, out_shape=jax.ShapeDtypeStruct(psi.shape, j...  1.05 us
  transfers between devices with their start and end apart: 15, of which 4 were waited for; matrix products, arithmetic and copies ran while one was open for 0% of the time, Pallas kernels for 22%

profile of v28, /device:TPU:0, one launch (start us, length us, event | category | flops | bytes accessed | tf_op | source)
XLA Modules:
  0.0 24.9 jit_solution(13650235560216665114)
XLA Ops:
  0.0 1.2 %shard_map.83.refs_0_ = bf16[8,64,128]{2,1,0:T(8,128)(2,1)S(1)} custom-call(s32[16]{0:T(128)} %dims_hbm.3, bf16[16,64,64]{2,1,0:T(8,128)(2,1)} %right_hbm.1), custom_call_target="tpu_custom_call" | custom-call | bytes 131072 | tf_op jit(solution)/shard_map/pallas_call | solution.py:248
  1.2 4.1 %collective-permute-start = (bf16[8,64,128]{2,1,0:T(8,128)(2,1)S(1)}, bf16[8,64,128]{2,1,0:T(8,128)(2,1)S(1)}, u32[]{:S(2)}, u32[]{:S(2)}) collective-permute-start(bf16[8,64,128]{2,1,0:T(8,128)(2,1)S(1)} %shard_map.83.refs_0_), channel_id=1, source_target_pairs={{0,8},{1,9},{2,10},{3,11},{4,12},{5,13},{6,14},{7,15},{8,0},{9,1},... | collective-permute-start | bytes 393224 | tf_op jit(solution)/shard_map/ppermute | solution.py:228
  5.3 0.0 collective-permute-start.6
  5.3 1.6 %collective-permute-start.5 = (bf16[8,64,128]{2,1,0:T(8,128)(2,1)S(1)}, bf16[8,64,128]{2,1,0:T(8,128)(2,1)S(1)}, u32[]{:S(2)}, u32[]{:S(2)}) collective-permute-start(bf16[8,64,128]{2,1,0:T(8,128)(2,1)S(1)} %shard_map.83.refs_0_), channel_id=1, source_target_pairs={{0,4},{1,5},{2,6},{3,7},{4,0},{5,1},{6,2},{7,3},{8,12},{9,13},{10,... | collective-permute-start | bytes 393224 | tf_op jit(solution)/shard_map/ppermute | solution.py:228
  6.9 1.5 %collective-permute-start.4 = (bf16[8,64,128]{2,1,0:T(8,128)(2,1)S(1)}, bf16[8,64,128]{2,1,0:T(8,128)(2,1)S(1)}, u32[]{:S(2)}, u32[]{:S(2)}) collective-permute-start(bf16[8,64,128]{2,1,0:T(8,128)(2,1)S(1)} %shard_map.83.refs_0_), channel_id=1, source_target_pairs={{0,2},{1,3},{2,0},{3,1},{4,6},{5,7},{6,4},{7,5},{8,10},{9,11},{10,... | collective-permute-start | bytes 393224 | tf_op jit(solution)/shard_map/ppermute | solution.py:228
  8.4 2.9 %shard_map.82 = (bf16[8,8,64,128]{3,2,1,0:T(8,128)(2,1)S(1)}, s32[202]{0:T(256)S(4)}) custom-call(s32[8]{0:T(128)} %dims_hbm.2, s32[8,8]{1,0:T(8,128)} %bitcast.1, s32[8,8]{1,0:T(8,128)} %owner_hbm.1, s32[8,8]{1,0:T(8,128)} %slot_hbm.1, bf16[8,64,64]{2,1,0:T(8,128)(2,1)} %left_hbm.1, bf16[8,8,64,128]{3,2,1,0:T(8,128)(2,1)} %psi_hbm.1), custom_call_target="tpu_custom_call" | custom-call | flops 67108864 | bytes 1048576 | tf_op jit(solution)/shard_map/pallas_call | solution.py:263
  11.3 0.5 %collective-permute-done.refs_3_ = bf16[8,64,128]{2,1,0:T(8,128)(2,1)S(1)} collective-permute-done((bf16[8,64,128]{2,1,0:T(8,128)(2,1)S(1)}, bf16[8,64,128]{2,1,0:T(8,128)(2,1)S(1)}, u32[]{:S(2)}, u32[]{:S(2)}) %collective-permute-start) | collective-permute-done | bytes 131104 | tf_op jit(solution)/shard_map/ppermute | solution.py:228
  11.8 0.7 %collective-permute-start.1 = (bf16[8,64,128]{2,1,0:T(8,128)(2,1)S(1)}, bf16[8,64,128]{2,1,0:T(8,128)(2,1)S(1)}, u32[]{:S(2)}, u32[]{:S(2)}) collective-permute-start(bf16[8,64,128]{2,1,0:T(8,128)(2,1)S(1)} %collective-permute-done.refs_3_), channel_id=1, source_target_pairs={{0,4},{1,3},{2,6},{3,1},{4,0},{5,7},{6,2},{7,5},{8,12},{9,11},{10,... | collective-permute-start | bytes 393224 | tf_op jit(solution)/shard_map/ppermute | solution.py:228
  12.4 0.5 %collective-permute-done.5.refs_2_ = bf16[8,64,128]{2,1,0:T(8,128)(2,1)S(1)} collective-permute-done((bf16[8,64,128]{2,1,0:T(8,128)(2,1)S(1)}, bf16[8,64,128]{2,1,0:T(8,128)(2,1)S(1)}, u32[]{:S(2)}, u32[]{:S(2)}) %collective-permute-start.5) | collective-permute-done | bytes 131104 | tf_op jit(solution)/shard_map/ppermute | solution.py:228
  12.9 1.5 %collective-permute-start.9 = (bf16[8,64,128]{2,1,0:T(8,128)(2,1)S(1)}, bf16[8,64,128]{2,1,0:T(8,128)(2,1)S(1)}, u32[]{:S(2)}, u32[]{:S(2)}) collective-permute-start(bf16[8,64,128]{2,1,0:T(8,128)(2,1)S(1)} %collective-permute-done.5.refs_2_), channel_id=1, source_target_pairs={{0,2},{1,3},{2,0},{3,1},{4,6},{5,7},{6,4},{7,5},{8,10},{9,11},{10,... | collective-permute-start | bytes 393224 | tf_op jit(solution)/shard_map/ppermute | solution.py:228
  14.4 0.0 collective-permute-start.8
  14.4 0.0 collective-permute-done.4.refs_1_
  14.4 0.5 %collective-permute-start.7 = (bf16[8,64,128]{2,1,0:T(8,128)(2,1)S(1)}, bf16[8,64,128]{2,1,0:T(8,128)(2,1)S(1)}, u32[]{:S(2)}, u32[]{:S(2)}) collective-permute-start(bf16[8,64,128]{2,1,0:T(8,128)(2,1)S(1)} %collective-permute-done.4.refs_1_), channel_id=1, source_target_pairs={{0,1},{1,0},{2,3},{3,2},{4,5},{5,4},{6,7},{7,6},{8,9},{9,8},{10,11... | collective-permute-start | bytes 393224 | tf_op jit(solution)/shard_map/ppermute | solution.py:228
  15.0 0.0 collective-permute-done.6.refs_5_
  15.0 0.5 %collective-permute-start.3 = (bf16[8,64,128]{2,1,0:T(8,128)(2,1)S(1)}, bf16[8,64,128]{2,1,0:T(8,128)(2,1)S(1)}, u32[]{:S(2)}, u32[]{:S(2)}) collective-permute-start(bf16[8,64,128]{2,1,0:T(8,128)(2,1)S(1)} %collective-permute-done.refs_3_), channel_id=1, source_target_pairs={{0,2},{1,5},{2,0},{3,7},{4,6},{5,1},{6,4},{7,3},{8,10},{9,13},{10,... | collective-permute-start | bytes 393224 | tf_op jit(solution)/shard_map/ppermute | solution.py:228
  15.4 1.3 %collective-permute-done.1.refs_4_ = bf16[8,64,128]{2,1,0:T(8,128)(2,1)S(1)} collective-permute-done((bf16[8,64,128]{2,1,0:T(8,128)(2,1)S(1)}, bf16[8,64,128]{2,1,0:T(8,128)(2,1)S(1)}, u32[]{:S(2)}, u32[]{:S(2)}) %collective-permute-start.1) | collective-permute-done | bytes 131104 | tf_op jit(solution)/shard_map/ppermute | solution.py:228
  16.7 1.7 %collective-permute-start.2 = (bf16[8,64,128]{2,1,0:T(8,128)(2,1)S(1)}, bf16[8,64,128]{2,1,0:T(8,128)(2,1)S(1)}, u32[]{:S(2)}, u32[]{:S(2)}) collective-permute-start(bf16[8,64,128]{2,1,0:T(8,128)(2,1)S(1)} %collective-permute-done.1.refs_4_), channel_id=1, source_target_pairs={{0,2},{1,5},{2,0},{3,7},{4,6},{5,1},{6,4},{7,3},{8,10},{9,13},{10,... | collective-permute-start | bytes 393224 | tf_op jit(solution)/shard_map/ppermute | solution.py:228
  18.4 0.0 collective-permute-done.9.refs_0_
  18.4 0.0 collective-permute-start.11
  18.4 0.0 collective-permute-done.8.refs_7_
  18.4 0.5 %collective-permute-start.12 = (bf16[8,64,128]{2,1,0:T(8,128)(2,1)S(1)}, bf16[8,64,128]{2,1,0:T(8,128)(2,1)S(1)}, u32[]{:S(2)}, u32[]{:S(2)}) collective-permute-start(bf16[8,64,128]{2,1,0:T(8,128)(2,1)S(1)} %collective-permute-done.1.refs_4_), channel_id=1, source_target_pairs={{0,1},{1,0},{2,3},{3,2},{4,5},{5,4},{6,7},{7,6},{8,9},{9,8},{10,11... | collective-permute-start | bytes 393224 | tf_op jit(solution)/shard_map/ppermute | solution.py:228
  18.9 0.0 collective-permute-done.7.refs_6_
  18.9 0.1 collective-permute-start.10
  19.0 1.6 %shard_map.84.early_ref = bf16[8,8,64,128]{3,2,1,0:T(8,128)(2,1)S(1)} custom-call(s32[202]{0:T(256)S(4)} %get-tuple-element.12.list_ref, bf16[8,8,64,128]{3,2,1,0:T(8,128)(2,1)S(1)} %get-tuple-element.15.half_ref, bf16[8,64,128]{2,1,0:T(8,128)(2,1)S(1)} %shard_map.83.refs_0_, bf16[8,64,128]{2,1,0:T(8,128)(2,1)S(1)} %collective-permute-done.4.refs_1_, ...), custom_call_target="tpu_custom_call" | custom-call | flops 67108864 | bytes 1048576 | tf_op jit(solution)/shard_map/pallas_call | solution.py:308
  20.6 0.0 collective-permute-done.3.refs_1_
  20.6 1.1 %collective-permute-done.2.refs_5_ = bf16[8,64,128]{2,1,0:T(8,128)(2,1)S(1)} collective-permute-done((bf16[8,64,128]{2,1,0:T(8,128)(2,1)S(1)}, bf16[8,64,128]{2,1,0:T(8,128)(2,1)S(1)}, u32[]{:S(2)}, u32[]{:S(2)}) %collective-permute-start.2) | collective-permute-done | bytes 131104 | tf_op jit(solution)/shard_map/ppermute | solution.py:228
  21.7 0.0 collective-permute-start.13
  21.7 0.5 %collective-permute-start.14 = (bf16[8,64,128]{2,1,0:T(8,128)(2,1)S(1)}, bf16[8,64,128]{2,1,0:T(8,128)(2,1)S(1)}, u32[]{:S(2)}, u32[]{:S(2)}) collective-permute-start(bf16[8,64,128]{2,1,0:T(8,128)(2,1)S(1)} %collective-permute-done.2.refs_5_), channel_id=1, source_target_pairs={{0,1},{1,0},{2,3},{3,2},{4,5},{5,4},{6,7},{7,6},{8,9},{9,8},{10,11... | collective-permute-start | bytes 393224 | tf_op jit(solution)/shard_map/ppermute | solution.py:228
  22.2 0.0 collective-permute-done.11.refs_3_
  22.2 0.0 collective-permute-done.10.refs_2_
  22.2 0.0 collective-permute-done.12.refs_4_
  22.2 1.1 %shard_map.85.middle_ref = bf16[8,8,64,128]{3,2,1,0:T(8,128)(2,1)S(1)} custom-call(s32[202]{0:T(256)S(4)} %get-tuple-element.12.list_ref, bf16[8,8,64,128]{3,2,1,0:T(8,128)(2,1)S(1)} %shard_map.84.early_ref, bf16[8,8,64,128]{3,2,1,0:T(8,128)(2,1)S(1)} %get-tuple-element.15.half_ref, bf16[8,64,128]{2,1,0:T(8,128)(2,1)S(1)} %collective-permute-done.9.refs_0_, ...), custom_call_target="tpu_custom_call" | custom-call | flops 16777216 | bytes 262144 | tf_op jit(solution)/shard_map/pallas_call | solution.py:320
  23.3 0.0 collective-permute-done.13.refs_0_
  23.3 0.0 collective-permute-done.14.refs_1_
  23.3 1.6 %shard_map.86 = bf16[8,8,64,128]{3,2,1,0:T(8,128)(2,1)} custom-call(s32[202]{0:T(256)S(4)} %get-tuple-element.12.list_ref, bf16[8,8,64,128]{3,2,1,0:T(8,128)(2,1)S(1)} %shard_map.85.middle_ref, bf16[8,8,64,128]{3,2,1,0:T(8,128)(2,1)S(1)} %get-tuple-element.15.half_ref, bf16[8,64,128]{2,1,0:T(8,128)(2,1)S(1)} %collective-permute-done.13.refs_0_, ...), custom_call_target="tpu_custom_call" | custom-call | flops 4194304 | bytes 1048576 | tf_op jit(solution)/shard_map/pallas_call | solution.py:329
Async XLA Ops:
  1.2 10.5 %collective-permute-start = (bf16[8,64,128]{2,1,0:T(8,128)(2,1)S(1)}, bf16[8,64,128]{2,1,0:T(8,128)(2,1)S(1)}, u32[]{:S(2)}, u32[]{:S(2)}) collective-permute-start(bf16[8,64,128]{2,1,0:T(8,128)(2,1)S(1)} %shard_map.83.refs_0_), channel_id=1, source_target_pairs={{0,8},{1,9},{2,10},{3,11},{4,12},{5,13},{6,14},{7,15},{8,0},{9,1},... | collective-permute-start | bytes 393224 | tf_op jit(solution)/shard_map/ppermute | solution.py:228
  5.3 9.6 %collective-permute-start.6 = (bf16[8,64,128]{2,1,0:T(8,128)(2,1)S(1)}, bf16[8,64,128]{2,1,0:T(8,128)(2,1)S(1)}, u32[]{:S(2)}, u32[]{:S(2)}) collective-permute-start(bf16[8,64,128]{2,1,0:T(8,128)(2,1)S(1)} %shard_map.83.refs_0_), channel_id=1, source_target_pairs={{0,1},{1,0},{2,3},{3,2},{4,5},{5,4},{6,7},{7,6},{8,9},{9,8},{10,11... | collective-permute-start | bytes 393224 | tf_op jit(solution)/shard_map/ppermute | solution.py:228
  5.3 7.6 %collective-permute-start.5 = (bf16[8,64,128]{2,1,0:T(8,128)(2,1)S(1)}, bf16[8,64,128]{2,1,0:T(8,128)(2,1)S(1)}, u32[]{:S(2)}, u32[]{:S(2)}) collective-permute-start(bf16[8,64,128]{2,1,0:T(8,128)(2,1)S(1)} %shard_map.83.refs_0_), channel_id=1, source_target_pairs={{0,4},{1,5},{2,6},{3,7},{4,0},{5,1},{6,2},{7,3},{8,12},{9,13},{10,... | collective-permute-start | bytes 393224 | tf_op jit(solution)/shard_map/ppermute | solution.py:228
  6.9 7.5 %collective-permute-start.4 = (bf16[8,64,128]{2,1,0:T(8,128)(2,1)S(1)}, bf16[8,64,128]{2,1,0:T(8,128)(2,1)S(1)}, u32[]{:S(2)}, u32[]{:S(2)}) collective-permute-start(bf16[8,64,128]{2,1,0:T(8,128)(2,1)S(1)} %shard_map.83.refs_0_), channel_id=1, source_target_pairs={{0,2},{1,3},{2,0},{3,1},{4,6},{5,7},{6,4},{7,5},{8,10},{9,11},{10,... | collective-permute-start | bytes 393224 | tf_op jit(solution)/shard_map/ppermute | solution.py:228
  11.8 5.0 %collective-permute-start.1 = (bf16[8,64,128]{2,1,0:T(8,128)(2,1)S(1)}, bf16[8,64,128]{2,1,0:T(8,128)(2,1)S(1)}, u32[]{:S(2)}, u32[]{:S(2)}) collective-permute-start(bf16[8,64,128]{2,1,0:T(8,128)(2,1)S(1)} %collective-permute-done.refs_3_), channel_id=1, source_target_pairs={{0,4},{1,3},{2,6},{3,1},{4,0},{5,7},{6,2},{7,5},{8,12},{9,11},{10,... | collective-permute-start | bytes 393224 | tf_op jit(solution)/shard_map/ppermute | solution.py:228
  12.9 5.5 %collective-permute-start.9 = (bf16[8,64,128]{2,1,0:T(8,128)(2,1)S(1)}, bf16[8,64,128]{2,1,0:T(8,128)(2,1)S(1)}, u32[]{:S(2)}, u32[]{:S(2)}) collective-permute-start(bf16[8,64,128]{2,1,0:T(8,128)(2,1)S(1)} %collective-permute-done.5.refs_2_), channel_id=1, source_target_pairs={{0,2},{1,3},{2,0},{3,1},{4,6},{5,7},{6,4},{7,5},{8,10},{9,11},{10,... | collective-permute-start | bytes 393224 | tf_op jit(solution)/shard_map/ppermute | solution.py:228
  14.4 4.0 %collective-permute-start.8 = (bf16[8,64,128]{2,1,0:T(8,128)(2,1)S(1)}, bf16[8,64,128]{2,1,0:T(8,128)(2,1)S(1)}, u32[]{:S(2)}, u32[]{:S(2)}) collective-permute-start(bf16[8,64,128]{2,1,0:T(8,128)(2,1)S(1)} %collective-permute-done.5.refs_2_), channel_id=1, source_target_pairs={{0,1},{1,0},{2,3},{3,2},{4,5},{5,4},{6,7},{7,6},{8,9},{9,8},{10,11... | collective-permute-start | bytes 393224 | tf_op jit(solution)/shard_map/ppermute | solution.py:228
  14.4 4.5 %collective-permute-start.7 = (bf16[8,64,128]{2,1,0:T(8,128)(2,1)S(1)}, bf16[8,64,128]{2,1,0:T(8,128)(2,1)S(1)}, u32[]{:S(2)}, u32[]{:S(2)}) collective-permute-start(bf16[8,64,128]{2,1,0:T(8,128)(2,1)S(1)} %collective-permute-done.4.refs_1_), channel_id=1, source_target_pairs={{0,1},{1,0},{2,3},{3,2},{4,5},{5,4},{6,7},{7,6},{8,9},{9,8},{10,11... | collective-permute-start | bytes 393224 | tf_op jit(solution)/shard_map/ppermute | solution.py:228
  15.0 5.6 %collective-permute-start.3 = (bf16[8,64,128]{2,1,0:T(8,128)(2,1)S(1)}, bf16[8,64,128]{2,1,0:T(8,128)(2,1)S(1)}, u32[]{:S(2)}, u32[]{:S(2)}) collective-permute-start(bf16[8,64,128]{2,1,0:T(8,128)(2,1)S(1)} %collective-permute-done.refs_3_), channel_id=1, source_target_pairs={{0,2},{1,5},{2,0},{3,7},{4,6},{5,1},{6,4},{7,3},{8,10},{9,13},{10,... | collective-permute-start | bytes 393224 | tf_op jit(solution)/shard_map/ppermute | solution.py:228
  16.7 5.0 %collective-permute-start.2 = (bf16[8,64,128]{2,1,0:T(8,128)(2,1)S(1)}, bf16[8,64,128]{2,1,0:T(8,128)(2,1)S(1)}, u32[]{:S(2)}, u32[]{:S(2)}) collective-permute-start(bf16[8,64,128]{2,1,0:T(8,128)(2,1)S(1)} %collective-permute-done.1.refs_4_), channel_id=1, source_target_pairs={{0,2},{1,5},{2,0},{3,7},{4,6},{5,1},{6,4},{7,3},{8,10},{9,13},{10,... | collective-permute-start | bytes 393224 | tf_op jit(solution)/shard_map/ppermute | solution.py:228
  18.4 3.8 %collective-permute-start.11 = (bf16[8,64,128]{2,1,0:T(8,128)(2,1)S(1)}, bf16[8,64,128]{2,1,0:T(8,128)(2,1)S(1)}, u32[]{:S(2)}, u32[]{:S(2)}) collective-permute-start(bf16[8,64,128]{2,1,0:T(8,128)(2,1)S(1)} %collective-permute-done.refs_3_), channel_id=1, source_target_pairs={{0,1},{1,0},{2,3},{3,2},{4,5},{5,4},{6,7},{7,6},{8,9},{9,8},{10,11... | collective-permute-start | bytes 393224 | tf_op jit(solution)/shard_map/ppermute | solution.py:228
  18.4 3.8 %collective-permute-start.12 = (bf16[8,64,128]{2,1,0:T(8,128)(2,1)S(1)}, bf16[8,64,128]{2,1,0:T(8,128)(2,1)S(1)}, u32[]{:S(2)}, u32[]{:S(2)}) collective-permute-start(bf16[8,64,128]{2,1,0:T(8,128)(2,1)S(1)} %collective-permute-done.1.refs_4_), channel_id=1, source_target_pairs={{0,1},{1,0},{2,3},{3,2},{4,5},{5,4},{6,7},{7,6},{8,9},{9,8},{10,11... | collective-permute-start | bytes 393224 | tf_op jit(solution)/shard_map/ppermute | solution.py:228
  18.9 3.3 %collective-permute-start.10 = (bf16[8,64,128]{2,1,0:T(8,128)(2,1)S(1)}, bf16[8,64,128]{2,1,0:T(8,128)(2,1)S(1)}, u32[]{:S(2)}, u32[]{:S(2)}) collective-permute-start(bf16[8,64,128]{2,1,0:T(8,128)(2,1)S(1)} %collective-permute-done.9.refs_0_), channel_id=1, source_target_pairs={{0,1},{1,0},{2,3},{3,2},{4,5},{5,4},{6,7},{7,6},{8,9},{9,8},{10,11... | collective-permute-start | bytes 393224 | tf_op jit(solution)/shard_map/ppermute | solution.py:228
  21.7 1.6 %collective-permute-start.13 = (bf16[8,64,128]{2,1,0:T(8,128)(2,1)S(1)}, bf16[8,64,128]{2,1,0:T(8,128)(2,1)S(1)}, u32[]{:S(2)}, u32[]{:S(2)}) collective-permute-start(bf16[8,64,128]{2,1,0:T(8,128)(2,1)S(1)} %collective-permute-done.3.refs_1_), channel_id=1, source_target_pairs={{0,1},{1,0},{2,3},{3,2},{4,5},{5,4},{6,7},{7,6},{8,9},{9,8},{10,11... | collective-permute-start | bytes 393224 | tf_op jit(solution)/shard_map/ppermute | solution.py:228
  21.7 1.6 %collective-permute-start.14 = (bf16[8,64,128]{2,1,0:T(8,128)(2,1)S(1)}, bf16[8,64,128]{2,1,0:T(8,128)(2,1)S(1)}, u32[]{:S(2)}, u32[]{:S(2)}) collective-permute-start(bf16[8,64,128]{2,1,0:T(8,128)(2,1)S(1)} %collective-permute-done.2.refs_5_), channel_id=1, source_target_pairs={{0,1},{1,0},{2,3},{3,2},{4,5},{5,4},{6,7},{7,6},{8,9},{9,8},{10,11... | collective-permute-start | bytes 393224 | tf_op jit(solution)/shard_map/ppermute | solution.py:228

commit v29 on v26

--- a/solution.py
+++ b/solution.py
@@ -10,7 +10,7 @@
 VMEM_LIMIT = 48 * 1024 * 1024
 FAR, NEAR, CROSS, CORE = 8, 4, 2, 1
 OWN, SIDE, BESIDE, BEYOND, CORNER = (0, 0), (CROSS, CROSS), (NEAR, NEAR), (FAR, FAR), (NEAR | CROSS, NEAR | CROSS)
-FIRST, SECOND = (FAR | NEAR, FAR | CROSS), (FAR | CROSS, FAR | NEAR)
+FIRST, SECOND = (FAR | CROSS, FAR | NEAR), (FAR | NEAR, FAR | CROSS)
 END = (FAR | NEAR | CROSS, FAR | NEAR | CROSS)
 
 

time: 24.9 us -> 26.5 us (1.064)
  waiting for transfers between devices: 3.38 us -> 5.53 us
  starting transfers between devices: 13.1 us -> 12.7 us
    ppermute x15, waiting for transfers between devices: 3.38 us -> 5.53 us  [swap(): lax.ppermute(piece, 'sec', [(i, i ^ (odd_bit if i & CORE else even_bit))...]
    ppermute x15, starting transfers between devices: 13.1 us -> 12.7 us  [swap(): lax.ppermute(piece, 'sec', [(i, i ^ (odd_bit if i & CORE else even_bit))...]
  transfers between devices with their start and end apart: 15 -> 15, of which waited for: 4 -> 4; matrix products, arithmetic and copies ran while one was open for 0% -> 0% of each run, Pallas kernels for 22% -> 21%
where the time goes in v29:
time: 26.5 us; the launch traced here: 26.3 us
  starting transfers between devices  12.7 us (48%)
  Pallas kernels  8.05 us (30%)
  waiting for transfers between devices  5.53 us (21%)
    ppermute x15, starting transfers between devices, swap(): lax.ppermute(piece, 'sec', [(i, i ^ (odd_bit if i & CORE else even_bit))...  12.7 us
    ppermute x15, waiting for transfers between devices, swap(): lax.ppermute(piece, 'sec', [(i, i ^ (odd_bit if i & CORE else even_bit))...  5.53 us
    pallas_call x1, Pallas kernels, per_device(): pl.pallas_call(functools.partial(left_kernel, pair_count, len(EARLY if by...  2.85 us
    pallas_call x1, Pallas kernels, per_device(): pl.pallas_call(early_kernel, out_shape=jax.ShapeDtypeStruct(psi.shape, jn...  1.59 us
    pallas_call x1, Pallas kernels, per_device(): pl.pallas_call(last_kernel, out_shape=jax.ShapeDtypeStruct(psi.shape, jnp...  1.47 us
    pallas_call x1, Pallas kernels, per_device(): pl.pallas_call(pack_kernel, out_shape=jax.ShapeDtypeStruct((pair_count, t...  1.09 us
    pallas_call x1, Pallas kernels, per_device(): pl.pallas_call(middle_kernel, out_shape=jax.ShapeDtypeStruct(psi.shape, j...  1.05 us
  transfers between devices with their start and end apart: 15, of which 4 were waited for; matrix products, arithmetic and copies ran while one was open for 0% of the time, Pallas kernels for 21%

profile of v29, /device:TPU:0, one launch (start us, length us, event | category | flops | bytes accessed | tf_op | source)
XLA Modules:
  0.0 26.3 jit_solution(10228624234310375973)
XLA Ops:
  0.0 1.1 %shard_map.83.refs_0_ = bf16[8,64,128]{2,1,0:T(8,128)(2,1)S(1)} custom-call(s32[16]{0:T(128)} %dims_hbm.3, bf16[16,64,64]{2,1,0:T(8,128)(2,1)} %right_hbm.1), custom_call_target="tpu_custom_call" | custom-call | bytes 131072 | tf_op jit(solution)/shard_map/pallas_call | solution.py:236
  1.1 4.1 %collective-permute-start = (bf16[8,64,128]{2,1,0:T(8,128)(2,1)S(1)}, bf16[8,64,128]{2,1,0:T(8,128)(2,1)S(1)}, u32[]{:S(2)}, u32[]{:S(2)}) collective-permute-start(bf16[8,64,128]{2,1,0:T(8,128)(2,1)S(1)} %shard_map.83.refs_0_), channel_id=1, source_target_pairs={{0,8},{1,9},{2,10},{3,11},{4,12},{5,13},{6,14},{7,15},{8,0},{9,1},... | collective-permute-start | bytes 393224 | tf_op jit(solution)/shard_map/ppermute | solution.py:216
  5.2 0.0 collective-permute-start.6
  5.2 1.6 %collective-permute-start.5 = (bf16[8,64,128]{2,1,0:T(8,128)(2,1)S(1)}, bf16[8,64,128]{2,1,0:T(8,128)(2,1)S(1)}, u32[]{:S(2)}, u32[]{:S(2)}) collective-permute-start(bf16[8,64,128]{2,1,0:T(8,128)(2,1)S(1)} %shard_map.83.refs_0_), channel_id=1, source_target_pairs={{0,4},{1,5},{2,6},{3,7},{4,0},{5,1},{6,2},{7,3},{8,12},{9,13},{10,... | collective-permute-start | bytes 393224 | tf_op jit(solution)/shard_map/ppermute | solution.py:216
  6.8 1.5 %collective-permute-start.4 = (bf16[8,64,128]{2,1,0:T(8,128)(2,1)S(1)}, bf16[8,64,128]{2,1,0:T(8,128)(2,1)S(1)}, u32[]{:S(2)}, u32[]{:S(2)}) collective-permute-start(bf16[8,64,128]{2,1,0:T(8,128)(2,1)S(1)} %shard_map.83.refs_0_), channel_id=1, source_target_pairs={{0,2},{1,3},{2,0},{3,1},{4,6},{5,7},{6,4},{7,5},{8,10},{9,11},{10,... | collective-permute-start | bytes 393224 | tf_op jit(solution)/shard_map/ppermute | solution.py:216
  8.3 2.9 %shard_map.82 = (bf16[8,8,64,128]{3,2,1,0:T(8,128)(2,1)S(1)}, s32[202]{0:T(256)S(4)}) custom-call(s32[8]{0:T(128)} %dims_hbm.2, s32[8,8]{1,0:T(8,128)} %bitcast.1, s32[8,8]{1,0:T(8,128)} %owner_hbm.1, s32[8,8]{1,0:T(8,128)} %slot_hbm.1, bf16[8,64,64]{2,1,0:T(8,128)(2,1)} %left_hbm.1, bf16[8,8,64,128]{3,2,1,0:T(8,128)(2,1)} %psi_hbm.1), custom_call_target="tpu_custom_call" | custom-call | flops 67108864 | bytes 1048576 | tf_op jit(solution)/shard_map/pallas_call | solution.py:251
  11.1 0.5 %collective-permute-done.refs_3_ = bf16[8,64,128]{2,1,0:T(8,128)(2,1)S(1)} collective-permute-done((bf16[8,64,128]{2,1,0:T(8,128)(2,1)S(1)}, bf16[8,64,128]{2,1,0:T(8,128)(2,1)S(1)}, u32[]{:S(2)}, u32[]{:S(2)}) %collective-permute-start) | collective-permute-done | bytes 131104 | tf_op jit(solution)/shard_map/ppermute | solution.py:216
  11.6 1.5 %collective-permute-start.1 = (bf16[8,64,128]{2,1,0:T(8,128)(2,1)S(1)}, bf16[8,64,128]{2,1,0:T(8,128)(2,1)S(1)}, u32[]{:S(2)}, u32[]{:S(2)}) collective-permute-start(bf16[8,64,128]{2,1,0:T(8,128)(2,1)S(1)} %collective-permute-done.refs_3_), channel_id=1, source_target_pairs={{0,2},{1,5},{2,0},{3,7},{4,6},{5,1},{6,4},{7,3},{8,10},{9,13},{10,... | collective-permute-start | bytes 393224 | tf_op jit(solution)/shard_map/ppermute | solution.py:216
  13.2 0.0 collective-permute-done.5.refs_2_
  13.2 1.1 %collective-permute-start.9 = (bf16[8,64,128]{2,1,0:T(8,128)(2,1)S(1)}, bf16[8,64,128]{2,1,0:T(8,128)(2,1)S(1)}, u32[]{:S(2)}, u32[]{:S(2)}) collective-permute-start(bf16[8,64,128]{2,1,0:T(8,128)(2,1)S(1)} %collective-permute-done.5.refs_2_), channel_id=1, source_target_pairs={{0,2},{1,3},{2,0},{3,1},{4,6},{5,7},{6,4},{7,5},{8,10},{9,11},{10,... | collective-permute-start | bytes 393224 | tf_op jit(solution)/shard_map/ppermute | solution.py:216
  14.3 0.0 collective-permute-start.8
  14.3 0.0 collective-permute-done.4.refs_1_
  14.3 0.5 %collective-permute-start.7 = (bf16[8,64,128]{2,1,0:T(8,128)(2,1)S(1)}, bf16[8,64,128]{2,1,0:T(8,128)(2,1)S(1)}, u32[]{:S(2)}, u32[]{:S(2)}) collective-permute-start(bf16[8,64,128]{2,1,0:T(8,128)(2,1)S(1)} %collective-permute-done.4.refs_1_), channel_id=1, source_target_pairs={{0,1},{1,0},{2,3},{3,2},{4,5},{5,4},{6,7},{7,6},{8,9},{9,8},{10,11... | collective-permute-start | bytes 393224 | tf_op jit(solution)/shard_map/ppermute | solution.py:216
  14.8 0.0 collective-permute-done.6.refs_5_
  14.8 0.5 %collective-permute-start.3 = (bf16[8,64,128]{2,1,0:T(8,128)(2,1)S(1)}, bf16[8,64,128]{2,1,0:T(8,128)(2,1)S(1)}, u32[]{:S(2)}, u32[]{:S(2)}) collective-permute-start(bf16[8,64,128]{2,1,0:T(8,128)(2,1)S(1)} %collective-permute-done.refs_3_), channel_id=1, source_target_pairs={{0,4},{1,3},{2,6},{3,1},{4,0},{5,7},{6,2},{7,5},{8,12},{9,11},{10,... | collective-permute-start | bytes 393224 | tf_op jit(solution)/shard_map/ppermute | solution.py:216
  15.3 2.7 %collective-permute-done.1.refs_4_ = bf16[8,64,128]{2,1,0:T(8,128)(2,1)S(1)} collective-permute-done((bf16[8,64,128]{2,1,0:T(8,128)(2,1)S(1)}, bf16[8,64,128]{2,1,0:T(8,128)(2,1)S(1)}, u32[]{:S(2)}, u32[]{:S(2)}) %collective-permute-start.1) | collective-permute-done | bytes 131104 | tf_op jit(solution)/shard_map/ppermute | solution.py:216
  18.0 0.7 %collective-permute-start.2 = (bf16[8,64,128]{2,1,0:T(8,128)(2,1)S(1)}, bf16[8,64,128]{2,1,0:T(8,128)(2,1)S(1)}, u32[]{:S(2)}, u32[]{:S(2)}) collective-permute-start(bf16[8,64,128]{2,1,0:T(8,128)(2,1)S(1)} %collective-permute-done.1.refs_4_), channel_id=1, source_target_pairs={{0,4},{1,3},{2,6},{3,1},{4,0},{5,7},{6,2},{7,5},{8,12},{9,11},{10,... | collective-permute-start | bytes 393224 | tf_op jit(solution)/shard_map/ppermute | solution.py:216
  18.6 2.1 %collective-permute-done.9.refs_0_ = bf16[8,64,128]{2,1,0:T(8,128)(2,1)S(1)} collective-permute-done((bf16[8,64,128]{2,1,0:T(8,128)(2,1)S(1)}, bf16[8,64,128]{2,1,0:T(8,128)(2,1)S(1)}, u32[]{:S(2)}, u32[]{:S(2)}) %collective-permute-start.9) | collective-permute-done | bytes 131104 | tf_op jit(solution)/shard_map/ppermute | solution.py:216
  20.8 0.0 collective-permute-start.11
  20.8 0.0 collective-permute-done.8.refs_7_
  20.8 0.5 %collective-permute-start.12 = (bf16[8,64,128]{2,1,0:T(8,128)(2,1)S(1)}, bf16[8,64,128]{2,1,0:T(8,128)(2,1)S(1)}, u32[]{:S(2)}, u32[]{:S(2)}) collective-permute-start(bf16[8,64,128]{2,1,0:T(8,128)(2,1)S(1)} %collective-permute-done.1.refs_4_), channel_id=1, source_target_pairs={{0,1},{1,0},{2,3},{3,2},{4,5},{5,4},{6,7},{7,6},{8,9},{9,8},{10,11... | collective-permute-start | bytes 393224 | tf_op jit(solution)/shard_map/ppermute | solution.py:216
  21.3 0.0 collective-permute-done.7.refs_6_
  21.3 0.1 collective-permute-start.10
  21.4 1.6 %shard_map.84.early_ref = bf16[8,8,64,128]{3,2,1,0:T(8,128)(2,1)S(1)} custom-call(s32[202]{0:T(256)S(4)} %get-tuple-element.12.list_ref, bf16[8,8,64,128]{3,2,1,0:T(8,128)(2,1)S(1)} %get-tuple-element.15.half_ref, bf16[8,64,128]{2,1,0:T(8,128)(2,1)S(1)} %shard_map.83.refs_0_, bf16[8,64,128]{2,1,0:T(8,128)(2,1)S(1)} %collective-permute-done.4.refs_1_, ...), custom_call_target="tpu_custom_call" | custom-call | flops 67108864 | bytes 1048576 | tf_op jit(solution)/shard_map/pallas_call | solution.py:296
  23.0 0.0 collective-permute-done.3.refs_1_
  23.0 0.0 collective-permute-done.2.refs_5_
  23.0 0.5 %collective-permute-start.13 = (bf16[8,64,128]{2,1,0:T(8,128)(2,1)S(1)}, bf16[8,64,128]{2,1,0:T(8,128)(2,1)S(1)}, u32[]{:S(2)}, u32[]{:S(2)}) collective-permute-start(bf16[8,64,128]{2,1,0:T(8,128)(2,1)S(1)} %collective-permute-done.3.refs_1_), channel_id=1, source_target_pairs={{0,1},{1,0},{2,3},{3,2},{4,5},{5,4},{6,7},{7,6},{8,9},{9,8},{10,11... | collective-permute-start | bytes 393224 | tf_op jit(solution)/shard_map/ppermute | solution.py:216
  23.5 0.1 collective-permute-start.14
  23.6 0.0 collective-permute-done.11.refs_3_
  23.6 0.0 collective-permute-done.10.refs_2_
  23.6 0.0 collective-permute-done.12.refs_4_
  23.6 1.1 %shard_map.85.middle_ref = bf16[8,8,64,128]{3,2,1,0:T(8,128)(2,1)S(1)} custom-call(s32[202]{0:T(256)S(4)} %get-tuple-element.12.list_ref, bf16[8,8,64,128]{3,2,1,0:T(8,128)(2,1)S(1)} %shard_map.84.early_ref, bf16[8,8,64,128]{3,2,1,0:T(8,128)(2,1)S(1)} %get-tuple-element.15.half_ref, bf16[8,64,128]{2,1,0:T(8,128)(2,1)S(1)} %collective-permute-done.9.refs_0_, ...), custom_call_target="tpu_custom_call" | custom-call | flops 16777216 | bytes 262144 | tf_op jit(solution)/shard_map/pallas_call | solution.py:308
  24.7 0.0 collective-permute-done.13.refs_0_
  24.7 0.2 collective-permute-done.14.refs_1_
  24.9 1.5 %shard_map.86 = bf16[8,8,64,128]{3,2,1,0:T(8,128)(2,1)} custom-call(s32[202]{0:T(256)S(4)} %get-tuple-element.12.list_ref, bf16[8,8,64,128]{3,2,1,0:T(8,128)(2,1)S(1)} %shard_map.85.middle_ref, bf16[8,8,64,128]{3,2,1,0:T(8,128)(2,1)S(1)} %get-tuple-element.15.half_ref, bf16[8,64,128]{2,1,0:T(8,128)(2,1)S(1)} %collective-permute-done.13.refs_0_, ...), custom_call_target="tpu_custom_call" | custom-call | flops 4194304 | bytes 1048576 | tf_op jit(solution)/shard_map/pallas_call | solution.py:317
Async XLA Ops:
  1.1 10.5 %collective-permute-start = (bf16[8,64,128]{2,1,0:T(8,128)(2,1)S(1)}, bf16[8,64,128]{2,1,0:T(8,128)(2,1)S(1)}, u32[]{:S(2)}, u32[]{:S(2)}) collective-permute-start(bf16[8,64,128]{2,1,0:T(8,128)(2,1)S(1)} %shard_map.83.refs_0_), channel_id=1, source_target_pairs={{0,8},{1,9},{2,10},{3,11},{4,12},{5,13},{6,14},{7,15},{8,0},{9,1},... | collective-permute-start | bytes 393224 | tf_op jit(solution)/shard_map/ppermute | solution.py:216
  5.2 9.6 %collective-permute-start.6 = (bf16[8,64,128]{2,1,0:T(8,128)(2,1)S(1)}, bf16[8,64,128]{2,1,0:T(8,128)(2,1)S(1)}, u32[]{:S(2)}, u32[]{:S(2)}) collective-permute-start(bf16[8,64,128]{2,1,0:T(8,128)(2,1)S(1)} %shard_map.83.refs_0_), channel_id=1, source_target_pairs={{0,1},{1,0},{2,3},{3,2},{4,5},{5,4},{6,7},{7,6},{8,9},{9,8},{10,11... | collective-permute-start | bytes 393224 | tf_op jit(solution)/shard_map/ppermute | solution.py:216
  5.2 8.0 %collective-permute-start.5 = (bf16[8,64,128]{2,1,0:T(8,128)(2,1)S(1)}, bf16[8,64,128]{2,1,0:T(8,128)(2,1)S(1)}, u32[]{:S(2)}, u32[]{:S(2)}) collective-permute-start(bf16[8,64,128]{2,1,0:T(8,128)(2,1)S(1)} %shard_map.83.refs_0_), channel_id=1, source_target_pairs={{0,4},{1,5},{2,6},{3,7},{4,0},{5,1},{6,2},{7,3},{8,12},{9,13},{10,... | collective-permute-start | bytes 393224 | tf_op jit(solution)/shard_map/ppermute | solution.py:216
  6.8 7.5 %collective-permute-start.4 = (bf16[8,64,128]{2,1,0:T(8,128)(2,1)S(1)}, bf16[8,64,128]{2,1,0:T(8,128)(2,1)S(1)}, u32[]{:S(2)}, u32[]{:S(2)}) collective-permute-start(bf16[8,64,128]{2,1,0:T(8,128)(2,1)S(1)} %shard_map.83.refs_0_), channel_id=1, source_target_pairs={{0,2},{1,3},{2,0},{3,1},{4,6},{5,7},{6,4},{7,5},{8,10},{9,11},{10,... | collective-permute-start | bytes 393224 | tf_op jit(solution)/shard_map/ppermute | solution.py:216
  11.6 6.4 %collective-permute-start.1 = (bf16[8,64,128]{2,1,0:T(8,128)(2,1)S(1)}, bf16[8,64,128]{2,1,0:T(8,128)(2,1)S(1)}, u32[]{:S(2)}, u32[]{:S(2)}) collective-permute-start(bf16[8,64,128]{2,1,0:T(8,128)(2,1)S(1)} %collective-permute-done.refs_3_), channel_id=1, source_target_pairs={{0,2},{1,5},{2,0},{3,7},{4,6},{5,1},{6,4},{7,3},{8,10},{9,13},{10,... | collective-permute-start | bytes 393224 | tf_op jit(solution)/shard_map/ppermute | solution.py:216
  13.2 7.6 %collective-permute-start.9 = (bf16[8,64,128]{2,1,0:T(8,128)(2,1)S(1)}, bf16[8,64,128]{2,1,0:T(8,128)(2,1)S(1)}, u32[]{:S(2)}, u32[]{:S(2)}) collective-permute-start(bf16[8,64,128]{2,1,0:T(8,128)(2,1)S(1)} %collective-permute-done.5.refs_2_), channel_id=1, source_target_pairs={{0,2},{1,3},{2,0},{3,1},{4,6},{5,7},{6,4},{7,5},{8,10},{9,11},{10,... | collective-permute-start | bytes 393224 | tf_op jit(solution)/shard_map/ppermute | solution.py:216
  14.3 6.5 %collective-permute-start.8 = (bf16[8,64,128]{2,1,0:T(8,128)(2,1)S(1)}, bf16[8,64,128]{2,1,0:T(8,128)(2,1)S(1)}, u32[]{:S(2)}, u32[]{:S(2)}) collective-permute-start(bf16[8,64,128]{2,1,0:T(8,128)(2,1)S(1)} %collective-permute-done.5.refs_2_), channel_id=1, source_target_pairs={{0,1},{1,0},{2,3},{3,2},{4,5},{5,4},{6,7},{7,6},{8,9},{9,8},{10,11... | collective-permute-start | bytes 393224 | tf_op jit(solution)/shard_map/ppermute | solution.py:216
  14.3 7.0 %collective-permute-start.7 = (bf16[8,64,128]{2,1,0:T(8,128)(2,1)S(1)}, bf16[8,64,128]{2,1,0:T(8,128)(2,1)S(1)}, u32[]{:S(2)}, u32[]{:S(2)}) collective-permute-start(bf16[8,64,128]{2,1,0:T(8,128)(2,1)S(1)} %collective-permute-done.4.refs_1_), channel_id=1, source_target_pairs={{0,1},{1,0},{2,3},{3,2},{4,5},{5,4},{6,7},{7,6},{8,9},{9,8},{10,11... | collective-permute-start | bytes 393224 | tf_op jit(solution)/shard_map/ppermute | solution.py:216
  14.8 8.2 %collective-permute-start.3 = (bf16[8,64,128]{2,1,0:T(8,128)(2,1)S(1)}, bf16[8,64,128]{2,1,0:T(8,128)(2,1)S(1)}, u32[]{:S(2)}, u32[]{:S(2)}) collective-permute-start(bf16[8,64,128]{2,1,0:T(8,128)(2,1)S(1)} %collective-permute-done.refs_3_), channel_id=1, source_target_pairs={{0,4},{1,3},{2,6},{3,1},{4,0},{5,7},{6,2},{7,5},{8,12},{9,11},{10,... | collective-permute-start | bytes 393224 | tf_op jit(solution)/shard_map/ppermute | solution.py:216
  18.0 5.0 %collective-permute-start.2 = (bf16[8,64,128]{2,1,0:T(8,128)(2,1)S(1)}, bf16[8,64,128]{2,1,0:T(8,128)(2,1)S(1)}, u32[]{:S(2)}, u32[]{:S(2)}) collective-permute-start(bf16[8,64,128]{2,1,0:T(8,128)(2,1)S(1)} %collective-permute-done.1.refs_4_), channel_id=1, source_target_pairs={{0,4},{1,3},{2,6},{3,1},{4,0},{5,7},{6,2},{7,5},{8,12},{9,11},{10,... | collective-permute-start | bytes 393224 | tf_op jit(solution)/shard_map/ppermute | solution.py:216
  20.8 2.8 %collective-permute-start.11 = (bf16[8,64,128]{2,1,0:T(8,128)(2,1)S(1)}, bf16[8,64,128]{2,1,0:T(8,128)(2,1)S(1)}, u32[]{:S(2)}, u32[]{:S(2)}) collective-permute-start(bf16[8,64,128]{2,1,0:T(8,128)(2,1)S(1)} %collective-permute-done.refs_3_), channel_id=1, source_target_pairs={{0,1},{1,0},{2,3},{3,2},{4,5},{5,4},{6,7},{7,6},{8,9},{9,8},{10,11... | collective-permute-start | bytes 393224 | tf_op jit(solution)/shard_map/ppermute | solution.py:216
  20.8 2.8 %collective-permute-start.12 = (bf16[8,64,128]{2,1,0:T(8,128)(2,1)S(1)}, bf16[8,64,128]{2,1,0:T(8,128)(2,1)S(1)}, u32[]{:S(2)}, u32[]{:S(2)}) collective-permute-start(bf16[8,64,128]{2,1,0:T(8,128)(2,1)S(1)} %collective-permute-done.1.refs_4_), channel_id=1, source_target_pairs={{0,1},{1,0},{2,3},{3,2},{4,5},{5,4},{6,7},{7,6},{8,9},{9,8},{10,11... | collective-permute-start | bytes 393224 | tf_op jit(solution)/shard_map/ppermute | solution.py:216
  21.3 2.3 %collective-permute-start.10 = (bf16[8,64,128]{2,1,0:T(8,128)(2,1)S(1)}, bf16[8,64,128]{2,1,0:T(8,128)(2,1)S(1)}, u32[]{:S(2)}, u32[]{:S(2)}) collective-permute-start(bf16[8,64,128]{2,1,0:T(8,128)(2,1)S(1)} %collective-permute-done.9.refs_0_), channel_id=1, source_target_pairs={{0,1},{1,0},{2,3},{3,2},{4,5},{5,4},{6,7},{7,6},{8,9},{9,8},{10,11... | collective-permute-start | bytes 393224 | tf_op jit(solution)/shard_map/ppermute | solution.py:216
  23.0 1.7 %collective-permute-start.13 = (bf16[8,64,128]{2,1,0:T(8,128)(2,1)S(1)}, bf16[8,64,128]{2,1,0:T(8,128)(2,1)S(1)}, u32[]{:S(2)}, u32[]{:S(2)}) collective-permute-start(bf16[8,64,128]{2,1,0:T(8,128)(2,1)S(1)} %collective-permute-done.3.refs_1_), channel_id=1, source_target_pairs={{0,1},{1,0},{2,3},{3,2},{4,5},{5,4},{6,7},{7,6},{8,9},{9,8},{10,11... | collective-permute-start | bytes 393224 | tf_op jit(solution)/shard_map/ppermute | solution.py:216
  23.5 1.3 %collective-permute-start.14 = (bf16[8,64,128]{2,1,0:T(8,128)(2,1)S(1)}, bf16[8,64,128]{2,1,0:T(8,128)(2,1)S(1)}, u32[]{:S(2)}, u32[]{:S(2)}) collective-permute-start(bf16[8,64,128]{2,1,0:T(8,128)(2,1)S(1)} %collective-permute-done.2.refs_5_), channel_id=1, source_target_pairs={{0,1},{1,0},{2,3},{3,2},{4,5},{5,4},{6,7},{7,6},{8,9},{9,8},{10,11... | collective-permute-start | bytes 393224 | tf_op jit(solution)/shard_map/ppermute | solution.py:216

commit v30 on v26

--- a/solution.py
+++ b/solution.py
@@ -9,7 +9,7 @@
 
 VMEM_LIMIT = 48 * 1024 * 1024
 FAR, NEAR, CROSS, CORE = 8, 4, 2, 1
-OWN, SIDE, BESIDE, BEYOND, CORNER = (0, 0), (CROSS, CROSS), (NEAR, NEAR), (FAR, FAR), (NEAR | CROSS, NEAR | CROSS)
+OWN, SIDE, BESIDE, BEYOND, CORNER = (0, 0), (CROSS, NEAR), (NEAR, CROSS), (FAR, FAR), (NEAR | CROSS, NEAR | CROSS)
 FIRST, SECOND = (FAR | NEAR, FAR | CROSS), (FAR | CROSS, FAR | NEAR)
 END = (FAR | NEAR | CROSS, FAR | NEAR | CROSS)
 

time: 24.9 us -> 25.3 us (1.016)
  waiting for transfers between devices: 3.38 us -> 3.77 us
    ppermute x15, waiting for transfers between devices: 3.38 us -> 3.77 us  [swap(): lax.ppermute(piece, 'sec', [(i, i ^ (odd_bit if i & CORE else even_bit))...]
where the time goes in v30:
time: 25.3 us; the launch traced here: 25.2 us
  starting transfers between devices  13.3 us (53%)
  Pallas kernels  8.09 us (32%)
  waiting for transfers between devices  3.77 us (15%)
    ppermute x15, starting transfers between devices, swap(): lax.ppermute(piece, 'sec', [(i, i ^ (odd_bit if i & CORE else even_bit))...  13.3 us
    ppermute x15, waiting for transfers between devices, swap(): lax.ppermute(piece, 'sec', [(i, i ^ (odd_bit if i & CORE else even_bit))...  3.77 us
    pallas_call x1, Pallas kernels, per_device(): pl.pallas_call(functools.partial(left_kernel, pair_count, len(EARLY if by...  2.91 us
    pallas_call x1, Pallas kernels, per_device(): pl.pallas_call(early_kernel, out_shape=jax.ShapeDtypeStruct(psi.shape, jn...  1.59 us
    pallas_call x1, Pallas kernels, per_device(): pl.pallas_call(last_kernel, out_shape=jax.ShapeDtypeStruct(psi.shape, jnp...  1.45 us
    pallas_call x1, Pallas kernels, per_device(): pl.pallas_call(pack_kernel, out_shape=jax.ShapeDtypeStruct((pair_count, t...  1.09 us
    pallas_call x1, Pallas kernels, per_device(): pl.pallas_call(middle_kernel, out_shape=jax.ShapeDtypeStruct(psi.shape, j...  1.05 us
  transfers between devices with their start and end apart: 15, of which 4 were waited for; matrix products, arithmetic and copies ran while one was open for 0% of the time, Pallas kernels for 22%

profile of v30, /device:TPU:0, one launch (start us, length us, event | category | flops | bytes accessed | tf_op | source)
XLA Modules:
  0.0 25.2 jit_solution(3610757906787837700)
XLA Ops:
  0.0 1.1 %shard_map.83.refs_0_ = bf16[8,64,128]{2,1,0:T(8,128)(2,1)S(1)} custom-call(s32[16]{0:T(128)} %dims_hbm.3, bf16[16,64,64]{2,1,0:T(8,128)(2,1)} %right_hbm.1), custom_call_target="tpu_custom_call" | custom-call | bytes 131072 | tf_op jit(solution)/shard_map/pallas_call | solution.py:236
  1.1 4.1 %collective-permute-start = (bf16[8,64,128]{2,1,0:T(8,128)(2,1)S(1)}, bf16[8,64,128]{2,1,0:T(8,128)(2,1)S(1)}, u32[]{:S(2)}, u32[]{:S(2)}) collective-permute-start(bf16[8,64,128]{2,1,0:T(8,128)(2,1)S(1)} %shard_map.83.refs_0_), channel_id=1, source_target_pairs={{0,8},{1,9},{2,10},{3,11},{4,12},{5,13},{6,14},{7,15},{8,0},{9,1},... | collective-permute-start | bytes 393224 | tf_op jit(solution)/shard_map/ppermute | solution.py:216
  5.2 0.0 collective-permute-start.6
  5.2 1.6 %collective-permute-start.5 = (bf16[8,64,128]{2,1,0:T(8,128)(2,1)S(1)}, bf16[8,64,128]{2,1,0:T(8,128)(2,1)S(1)}, u32[]{:S(2)}, u32[]{:S(2)}) collective-permute-start(bf16[8,64,128]{2,1,0:T(8,128)(2,1)S(1)} %shard_map.83.refs_0_), channel_id=1, source_target_pairs={{0,4},{1,3},{2,6},{3,1},{4,0},{5,7},{6,2},{7,5},{8,12},{9,11},{10,... | collective-permute-start | bytes 393224 | tf_op jit(solution)/shard_map/ppermute | solution.py:216
  6.8 1.5 %collective-permute-start.4 = (bf16[8,64,128]{2,1,0:T(8,128)(2,1)S(1)}, bf16[8,64,128]{2,1,0:T(8,128)(2,1)S(1)}, u32[]{:S(2)}, u32[]{:S(2)}) collective-permute-start(bf16[8,64,128]{2,1,0:T(8,128)(2,1)S(1)} %shard_map.83.refs_0_), channel_id=1, source_target_pairs={{0,2},{1,5},{2,0},{3,7},{4,6},{5,1},{6,4},{7,3},{8,10},{9,13},{10,... | collective-permute-start | bytes 393224 | tf_op jit(solution)/shard_map/ppermute | solution.py:216
  8.3 2.9 %shard_map.82 = (bf16[8,8,64,128]{3,2,1,0:T(8,128)(2,1)S(1)}, s32[202]{0:T(256)S(4)}) custom-call(s32[8]{0:T(128)} %dims_hbm.2, s32[8,8]{1,0:T(8,128)} %bitcast.1, s32[8,8]{1,0:T(8,128)} %owner_hbm.1, s32[8,8]{1,0:T(8,128)} %slot_hbm.1, bf16[8,64,64]{2,1,0:T(8,128)(2,1)} %left_hbm.1, bf16[8,8,64,128]{3,2,1,0:T(8,128)(2,1)} %psi_hbm.1), custom_call_target="tpu_custom_call" | custom-call | flops 67108864 | bytes 1048576 | tf_op jit(solution)/shard_map/pallas_call | solution.py:251
  11.2 0.4 %collective-permute-done.refs_3_ = bf16[8,64,128]{2,1,0:T(8,128)(2,1)S(1)} collective-permute-done((bf16[8,64,128]{2,1,0:T(8,128)(2,1)S(1)}, bf16[8,64,128]{2,1,0:T(8,128)(2,1)S(1)}, u32[]{:S(2)}, u32[]{:S(2)}) %collective-permute-start) | collective-permute-done | bytes 131104 | tf_op jit(solution)/shard_map/ppermute | solution.py:216
  11.6 0.7 %collective-permute-start.1 = (bf16[8,64,128]{2,1,0:T(8,128)(2,1)S(1)}, bf16[8,64,128]{2,1,0:T(8,128)(2,1)S(1)}, u32[]{:S(2)}, u32[]{:S(2)}) collective-permute-start(bf16[8,64,128]{2,1,0:T(8,128)(2,1)S(1)} %collective-permute-done.refs_3_), channel_id=1, source_target_pairs={{0,4},{1,3},{2,6},{3,1},{4,0},{5,7},{6,2},{7,5},{8,12},{9,11},{10,... | collective-permute-start | bytes 393224 | tf_op jit(solution)/shard_map/ppermute | solution.py:216
  12.3 0.3 %collective-permute-done.5.refs_2_ = bf16[8,64,128]{2,1,0:T(8,128)(2,1)S(1)} collective-permute-done((bf16[8,64,128]{2,1,0:T(8,128)(2,1)S(1)}, bf16[8,64,128]{2,1,0:T(8,128)(2,1)S(1)}, u32[]{:S(2)}, u32[]{:S(2)}) %collective-permute-start.5) | collective-permute-done | bytes 131104 | tf_op jit(solution)/shard_map/ppermute | solution.py:216
  12.6 2.0 %collective-permute-start.9 = (bf16[8,64,128]{2,1,0:T(8,128)(2,1)S(1)}, bf16[8,64,128]{2,1,0:T(8,128)(2,1)S(1)}, u32[]{:S(2)}, u32[]{:S(2)}) collective-permute-start(bf16[8,64,128]{2,1,0:T(8,128)(2,1)S(1)} %collective-permute-done.5.refs_2_), channel_id=1, source_target_pairs={{0,2},{1,5},{2,0},{3,7},{4,6},{5,1},{6,4},{7,3},{8,10},{9,13},{10,... | collective-permute-start | bytes 393224 | tf_op jit(solution)/shard_map/ppermute | solution.py:216
  14.6 0.0 collective-permute-start.8
  14.6 0.0 collective-permute-done.4.refs_1_
  14.6 0.5 %collective-permute-start.7 = (bf16[8,64,128]{2,1,0:T(8,128)(2,1)S(1)}, bf16[8,64,128]{2,1,0:T(8,128)(2,1)S(1)}, u32[]{:S(2)}, u32[]{:S(2)}) collective-permute-start(bf16[8,64,128]{2,1,0:T(8,128)(2,1)S(1)} %collective-permute-done.4.refs_1_), channel_id=1, source_target_pairs={{0,1},{1,0},{2,3},{3,2},{4,5},{5,4},{6,7},{7,6},{8,9},{9,8},{10,11... | collective-permute-start | bytes 393224 | tf_op jit(solution)/shard_map/ppermute | solution.py:216
  15.1 0.0 collective-permute-done.6.refs_5_
  15.1 0.0 collective-permute-start.3
  15.1 2.1 %collective-permute-done.1.refs_4_ = bf16[8,64,128]{2,1,0:T(8,128)(2,1)S(1)} collective-permute-done((bf16[8,64,128]{2,1,0:T(8,128)(2,1)S(1)}, bf16[8,64,128]{2,1,0:T(8,128)(2,1)S(1)}, u32[]{:S(2)}, u32[]{:S(2)}) %collective-permute-start.1) | collective-permute-done | bytes 131104 | tf_op jit(solution)/shard_map/ppermute | solution.py:216
  17.2 1.8 %collective-permute-start.2 = (bf16[8,64,128]{2,1,0:T(8,128)(2,1)S(1)}, bf16[8,64,128]{2,1,0:T(8,128)(2,1)S(1)}, u32[]{:S(2)}, u32[]{:S(2)}) collective-permute-start(bf16[8,64,128]{2,1,0:T(8,128)(2,1)S(1)} %collective-permute-done.1.refs_4_), channel_id=1, source_target_pairs={{0,2},{1,5},{2,0},{3,7},{4,6},{5,1},{6,4},{7,3},{8,10},{9,13},{10,... | collective-permute-start | bytes 393224 | tf_op jit(solution)/shard_map/ppermute | solution.py:216
  19.0 0.0 collective-permute-done.9.refs_0_
  19.0 0.0 collective-permute-start.11
  19.0 0.0 collective-permute-done.8.refs_7_
  19.0 0.5 %collective-permute-start.12 = (bf16[8,64,128]{2,1,0:T(8,128)(2,1)S(1)}, bf16[8,64,128]{2,1,0:T(8,128)(2,1)S(1)}, u32[]{:S(2)}, u32[]{:S(2)}) collective-permute-start(bf16[8,64,128]{2,1,0:T(8,128)(2,1)S(1)} %collective-permute-done.1.refs_4_), channel_id=1, source_target_pairs={{0,1},{1,0},{2,3},{3,2},{4,5},{5,4},{6,7},{7,6},{8,9},{9,8},{10,11... | collective-permute-start | bytes 393224 | tf_op jit(solution)/shard_map/ppermute | solution.py:216
  19.5 0.0 collective-permute-done.7.refs_6_
  19.5 0.1 collective-permute-start.10
  19.6 1.6 %shard_map.84.early_ref = bf16[8,8,64,128]{3,2,1,0:T(8,128)(2,1)S(1)} custom-call(s32[202]{0:T(256)S(4)} %get-tuple-element.12.list_ref, bf16[8,8,64,128]{3,2,1,0:T(8,128)(2,1)S(1)} %get-tuple-element.15.half_ref, bf16[8,64,128]{2,1,0:T(8,128)(2,1)S(1)} %shard_map.83.refs_0_, bf16[8,64,128]{2,1,0:T(8,128)(2,1)S(1)} %collective-permute-done.4.refs_1_, ...), custom_call_target="tpu_custom_call" | custom-call | flops 67108864 | bytes 1048576 | tf_op jit(solution)/shard_map/pallas_call | solution.py:296
  21.2 0.0 collective-permute-done.3.refs_1_
  21.2 1.0 %collective-permute-done.2.refs_5_ = bf16[8,64,128]{2,1,0:T(8,128)(2,1)S(1)} collective-permute-done((bf16[8,64,128]{2,1,0:T(8,128)(2,1)S(1)}, bf16[8,64,128]{2,1,0:T(8,128)(2,1)S(1)}, u32[]{:S(2)}, u32[]{:S(2)}) %collective-permute-start.2) | collective-permute-done | bytes 131104 | tf_op jit(solution)/shard_map/ppermute | solution.py:216
  22.1 0.0 collective-permute-start.13
  22.1 0.5 %collective-permute-start.14 = (bf16[8,64,128]{2,1,0:T(8,128)(2,1)S(1)}, bf16[8,64,128]{2,1,0:T(8,128)(2,1)S(1)}, u32[]{:S(2)}, u32[]{:S(2)}) collective-permute-start(bf16[8,64,128]{2,1,0:T(8,128)(2,1)S(1)} %collective-permute-done.2.refs_5_), channel_id=1, source_target_pairs={{0,1},{1,0},{2,3},{3,2},{4,5},{5,4},{6,7},{7,6},{8,9},{9,8},{10,11... | collective-permute-start | bytes 393224 | tf_op jit(solution)/shard_map/ppermute | solution.py:216
  22.7 0.0 collective-permute-done.11.refs_3_
  22.7 0.0 collective-permute-done.10.refs_2_
  22.7 0.0 collective-permute-done.12.refs_4_
  22.7 1.1 %shard_map.85.middle_ref = bf16[8,8,64,128]{3,2,1,0:T(8,128)(2,1)S(1)} custom-call(s32[202]{0:T(256)S(4)} %get-tuple-element.12.list_ref, bf16[8,8,64,128]{3,2,1,0:T(8,128)(2,1)S(1)} %shard_map.84.early_ref, bf16[8,8,64,128]{3,2,1,0:T(8,128)(2,1)S(1)} %get-tuple-element.15.half_ref, bf16[8,64,128]{2,1,0:T(8,128)(2,1)S(1)} %collective-permute-done.9.refs_0_, ...), custom_call_target="tpu_custom_call" | custom-call | flops 16777216 | bytes 262144 | tf_op jit(solution)/shard_map/pallas_call | solution.py:308
  23.7 0.0 collective-permute-done.13.refs_0_
  23.7 0.0 collective-permute-done.14.refs_1_
  23.7 1.4 %shard_map.86 = bf16[8,8,64,128]{3,2,1,0:T(8,128)(2,1)} custom-call(s32[202]{0:T(256)S(4)} %get-tuple-element.12.list_ref, bf16[8,8,64,128]{3,2,1,0:T(8,128)(2,1)S(1)} %shard_map.85.middle_ref, bf16[8,8,64,128]{3,2,1,0:T(8,128)(2,1)S(1)} %get-tuple-element.15.half_ref, bf16[8,64,128]{2,1,0:T(8,128)(2,1)S(1)} %collective-permute-done.13.refs_0_, ...), custom_call_target="tpu_custom_call" | custom-call | flops 4194304 | bytes 1048576 | tf_op jit(solution)/shard_map/pallas_call | solution.py:317
Async XLA Ops:
  1.1 10.5 %collective-permute-start = (bf16[8,64,128]{2,1,0:T(8,128)(2,1)S(1)}, bf16[8,64,128]{2,1,0:T(8,128)(2,1)S(1)}, u32[]{:S(2)}, u32[]{:S(2)}) collective-permute-start(bf16[8,64,128]{2,1,0:T(8,128)(2,1)S(1)} %shard_map.83.refs_0_), channel_id=1, source_target_pairs={{0,8},{1,9},{2,10},{3,11},{4,12},{5,13},{6,14},{7,15},{8,0},{9,1},... | collective-permute-start | bytes 393224 | tf_op jit(solution)/shard_map/ppermute | solution.py:216
  5.2 9.9 %collective-permute-start.6 = (bf16[8,64,128]{2,1,0:T(8,128)(2,1)S(1)}, bf16[8,64,128]{2,1,0:T(8,128)(2,1)S(1)}, u32[]{:S(2)}, u32[]{:S(2)}) collective-permute-start(bf16[8,64,128]{2,1,0:T(8,128)(2,1)S(1)} %shard_map.83.refs_0_), channel_id=1, source_target_pairs={{0,1},{1,0},{2,3},{3,2},{4,5},{5,4},{6,7},{7,6},{8,9},{9,8},{10,11... | collective-permute-start | bytes 393224 | tf_op jit(solution)/shard_map/ppermute | solution.py:216
  5.2 7.3 %collective-permute-start.5 = (bf16[8,64,128]{2,1,0:T(8,128)(2,1)S(1)}, bf16[8,64,128]{2,1,0:T(8,128)(2,1)S(1)}, u32[]{:S(2)}, u32[]{:S(2)}) collective-permute-start(bf16[8,64,128]{2,1,0:T(8,128)(2,1)S(1)} %shard_map.83.refs_0_), channel_id=1, source_target_pairs={{0,4},{1,3},{2,6},{3,1},{4,0},{5,7},{6,2},{7,5},{8,12},{9,11},{10,... | collective-permute-start | bytes 393224 | tf_op jit(solution)/shard_map/ppermute | solution.py:216
  6.8 7.8 %collective-permute-start.4 = (bf16[8,64,128]{2,1,0:T(8,128)(2,1)S(1)}, bf16[8,64,128]{2,1,0:T(8,128)(2,1)S(1)}, u32[]{:S(2)}, u32[]{:S(2)}) collective-permute-start(bf16[8,64,128]{2,1,0:T(8,128)(2,1)S(1)} %shard_map.83.refs_0_), channel_id=1, source_target_pairs={{0,2},{1,5},{2,0},{3,7},{4,6},{5,1},{6,4},{7,3},{8,10},{9,13},{10,... | collective-permute-start | bytes 393224 | tf_op jit(solution)/shard_map/ppermute | solution.py:216
  11.6 5.6 %collective-permute-start.1 = (bf16[8,64,128]{2,1,0:T(8,128)(2,1)S(1)}, bf16[8,64,128]{2,1,0:T(8,128)(2,1)S(1)}, u32[]{:S(2)}, u32[]{:S(2)}) collective-permute-start(bf16[8,64,128]{2,1,0:T(8,128)(2,1)S(1)} %collective-permute-done.refs_3_), channel_id=1, source_target_pairs={{0,4},{1,3},{2,6},{3,1},{4,0},{5,7},{6,2},{7,5},{8,12},{9,11},{10,... | collective-permute-start | bytes 393224 | tf_op jit(solution)/shard_map/ppermute | solution.py:216
  12.6 6.4 %collective-permute-start.9 = (bf16[8,64,128]{2,1,0:T(8,128)(2,1)S(1)}, bf16[8,64,128]{2,1,0:T(8,128)(2,1)S(1)}, u32[]{:S(2)}, u32[]{:S(2)}) collective-permute-start(bf16[8,64,128]{2,1,0:T(8,128)(2,1)S(1)} %collective-permute-done.5.refs_2_), channel_id=1, source_target_pairs={{0,2},{1,5},{2,0},{3,7},{4,6},{5,1},{6,4},{7,3},{8,10},{9,13},{10,... | collective-permute-start | bytes 393224 | tf_op jit(solution)/shard_map/ppermute | solution.py:216
  14.6 4.4 %collective-permute-start.8 = (bf16[8,64,128]{2,1,0:T(8,128)(2,1)S(1)}, bf16[8,64,128]{2,1,0:T(8,128)(2,1)S(1)}, u32[]{:S(2)}, u32[]{:S(2)}) collective-permute-start(bf16[8,64,128]{2,1,0:T(8,128)(2,1)S(1)} %collective-permute-done.5.refs_2_), channel_id=1, source_target_pairs={{0,1},{1,0},{2,3},{3,2},{4,5},{5,4},{6,7},{7,6},{8,9},{9,8},{10,11... | collective-permute-start | bytes 393224 | tf_op jit(solution)/shard_map/ppermute | solution.py:216
  14.6 4.9 %collective-permute-start.7 = (bf16[8,64,128]{2,1,0:T(8,128)(2,1)S(1)}, bf16[8,64,128]{2,1,0:T(8,128)(2,1)S(1)}, u32[]{:S(2)}, u32[]{:S(2)}) collective-permute-start(bf16[8,64,128]{2,1,0:T(8,128)(2,1)S(1)} %collective-permute-done.4.refs_1_), channel_id=1, source_target_pairs={{0,1},{1,0},{2,3},{3,2},{4,5},{5,4},{6,7},{7,6},{8,9},{9,8},{10,11... | collective-permute-start | bytes 393224 | tf_op jit(solution)/shard_map/ppermute | solution.py:216
  15.1 6.1 %collective-permute-start.3 = (bf16[8,64,128]{2,1,0:T(8,128)(2,1)S(1)}, bf16[8,64,128]{2,1,0:T(8,128)(2,1)S(1)}, u32[]{:S(2)}, u32[]{:S(2)}) collective-permute-start(bf16[8,64,128]{2,1,0:T(8,128)(2,1)S(1)} %collective-permute-done.refs_3_), channel_id=1, source_target_pairs={{0,2},{1,5},{2,0},{3,7},{4,6},{5,1},{6,4},{7,3},{8,10},{9,13},{10,... | collective-permute-start | bytes 393224 | tf_op jit(solution)/shard_map/ppermute | solution.py:216
  17.2 5.0 %collective-permute-start.2 = (bf16[8,64,128]{2,1,0:T(8,128)(2,1)S(1)}, bf16[8,64,128]{2,1,0:T(8,128)(2,1)S(1)}, u32[]{:S(2)}, u32[]{:S(2)}) collective-permute-start(bf16[8,64,128]{2,1,0:T(8,128)(2,1)S(1)} %collective-permute-done.1.refs_4_), channel_id=1, source_target_pairs={{0,2},{1,5},{2,0},{3,7},{4,6},{5,1},{6,4},{7,3},{8,10},{9,13},{10,... | collective-permute-start | bytes 393224 | tf_op jit(solution)/shard_map/ppermute | solution.py:216
  19.0 3.7 %collective-permute-start.11 = (bf16[8,64,128]{2,1,0:T(8,128)(2,1)S(1)}, bf16[8,64,128]{2,1,0:T(8,128)(2,1)S(1)}, u32[]{:S(2)}, u32[]{:S(2)}) collective-permute-start(bf16[8,64,128]{2,1,0:T(8,128)(2,1)S(1)} %collective-permute-done.refs_3_), channel_id=1, source_target_pairs={{0,1},{1,0},{2,3},{3,2},{4,5},{5,4},{6,7},{7,6},{8,9},{9,8},{10,11... | collective-permute-start | bytes 393224 | tf_op jit(solution)/shard_map/ppermute | solution.py:216
  19.0 3.7 %collective-permute-start.12 = (bf16[8,64,128]{2,1,0:T(8,128)(2,1)S(1)}, bf16[8,64,128]{2,1,0:T(8,128)(2,1)S(1)}, u32[]{:S(2)}, u32[]{:S(2)}) collective-permute-start(bf16[8,64,128]{2,1,0:T(8,128)(2,1)S(1)} %collective-permute-done.1.refs_4_), channel_id=1, source_target_pairs={{0,1},{1,0},{2,3},{3,2},{4,5},{5,4},{6,7},{7,6},{8,9},{9,8},{10,11... | collective-permute-start | bytes 393224 | tf_op jit(solution)/shard_map/ppermute | solution.py:216
  19.5 3.2 %collective-permute-start.10 = (bf16[8,64,128]{2,1,0:T(8,128)(2,1)S(1)}, bf16[8,64,128]{2,1,0:T(8,128)(2,1)S(1)}, u32[]{:S(2)}, u32[]{:S(2)}) collective-permute-start(bf16[8,64,128]{2,1,0:T(8,128)(2,1)S(1)} %collective-permute-done.9.refs_0_), channel_id=1, source_target_pairs={{0,1},{1,0},{2,3},{3,2},{4,5},{5,4},{6,7},{7,6},{8,9},{9,8},{10,11... | collective-permute-start | bytes 393224 | tf_op jit(solution)/shard_map/ppermute | solution.py:216
  22.1 1.6 %collective-permute-start.13 = (bf16[8,64,128]{2,1,0:T(8,128)(2,1)S(1)}, bf16[8,64,128]{2,1,0:T(8,128)(2,1)S(1)}, u32[]{:S(2)}, u32[]{:S(2)}) collective-permute-start(bf16[8,64,128]{2,1,0:T(8,128)(2,1)S(1)} %collective-permute-done.3.refs_1_), channel_id=1, source_target_pairs={{0,1},{1,0},{2,3},{3,2},{4,5},{5,4},{6,7},{7,6},{8,9},{9,8},{10,11... | collective-permute-start | bytes 393224 | tf_op jit(solution)/shard_map/ppermute | solution.py:216
  22.1 1.6 %collective-permute-start.14 = (bf16[8,64,128]{2,1,0:T(8,128)(2,1)S(1)}, bf16[8,64,128]{2,1,0:T(8,128)(2,1)S(1)}, u32[]{:S(2)}, u32[]{:S(2)}) collective-permute-start(bf16[8,64,128]{2,1,0:T(8,128)(2,1)S(1)} %collective-permute-done.2.refs_5_), channel_id=1, source_target_pairs={{0,1},{1,0},{2,3},{3,2},{4,5},{5,4},{6,7},{7,6},{8,9},{9,8},{10,11... | collective-permute-start | bytes 393224 | tf_op jit(solution)/shard_map/ppermute | solution.py:216

commit v31 on v26

--- a/solution.py
+++ b/solution.py
@@ -200,7 +200,7 @@
             store(a, middle_ref).start()
 
     merge(piece_refs, pairs_ref)
-    listed_products(16, items + 1, list_ref, half_ref, pairs_ref, out_ref)
+    listed_products(8, items + 1, list_ref, half_ref, pairs_ref, out_ref)
     for a in range(sectors):
 
         @pl.when(list_ref[2 * items + 2 + a] > 0)

time: 24.9 us -> 24.7 us (level)
  no operation moved by 1% of the time
where the time goes in v31:
time: 24.7 us; the launch traced here: 24.5 us
  starting transfers between devices  13.1 us (53%)
  Pallas kernels  7.93 us (32%)
  waiting for transfers between devices  3.38 us (14%)
    ppermute x15, starting transfers between devices, swap(): lax.ppermute(piece, 'sec', [(i, i ^ (odd_bit if i & CORE else even_bit))...  13.1 us
    ppermute x15, waiting for transfers between devices, swap(): lax.ppermute(piece, 'sec', [(i, i ^ (odd_bit if i & CORE else even_bit))...  3.38 us
    pallas_call x1, Pallas kernels, per_device(): pl.pallas_call(functools.partial(left_kernel, pair_count, len(EARLY if by...  2.85 us
    pallas_call x1, Pallas kernels, per_device(): pl.pallas_call(early_kernel, out_shape=jax.ShapeDtypeStruct(psi.shape, jn...  1.59 us
    pallas_call x1, Pallas kernels, per_device(): pl.pallas_call(last_kernel, out_shape=jax.ShapeDtypeStruct(psi.shape, jnp...  1.35 us
    pallas_call x1, Pallas kernels, per_device(): pl.pallas_call(pack_kernel, out_shape=jax.ShapeDtypeStruct((pair_count, t...  1.09 us
    pallas_call x1, Pallas kernels, per_device(): pl.pallas_call(middle_kernel, out_shape=jax.ShapeDtypeStruct(psi.shape, j...  1.05 us
  transfers between devices with their start and end apart: 15, of which 4 were waited for; matrix products, arithmetic and copies ran while one was open for 0% of the time, Pallas kernels for 22%

profile of v31, /device:TPU:0, one launch (start us, length us, event | category | flops | bytes accessed | tf_op | source)
XLA Modules:
  0.0 24.5 jit_solution(15864605939657248059)
XLA Ops:
  0.0 1.1 %shard_map.83.refs_0_ = bf16[8,64,128]{2,1,0:T(8,128)(2,1)S(1)} custom-call(s32[16]{0:T(128)} %dims_hbm.3, bf16[16,64,64]{2,1,0:T(8,128)(2,1)} %right_hbm.1), custom_call_target="tpu_custom_call" | custom-call | bytes 131072 | tf_op jit(solution)/shard_map/pallas_call | solution.py:236
  1.1 4.1 %collective-permute-start = (bf16[8,64,128]{2,1,0:T(8,128)(2,1)S(1)}, bf16[8,64,128]{2,1,0:T(8,128)(2,1)S(1)}, u32[]{:S(2)}, u32[]{:S(2)}) collective-permute-start(bf16[8,64,128]{2,1,0:T(8,128)(2,1)S(1)} %shard_map.83.refs_0_), channel_id=1, source_target_pairs={{0,8},{1,9},{2,10},{3,11},{4,12},{5,13},{6,14},{7,15},{8,0},{9,1},... | collective-permute-start | bytes 393224 | tf_op jit(solution)/shard_map/ppermute | solution.py:216
  5.2 0.0 collective-permute-start.6
  5.2 1.6 %collective-permute-start.5 = (bf16[8,64,128]{2,1,0:T(8,128)(2,1)S(1)}, bf16[8,64,128]{2,1,0:T(8,128)(2,1)S(1)}, u32[]{:S(2)}, u32[]{:S(2)}) collective-permute-start(bf16[8,64,128]{2,1,0:T(8,128)(2,1)S(1)} %shard_map.83.refs_0_), channel_id=1, source_target_pairs={{0,4},{1,5},{2,6},{3,7},{4,0},{5,1},{6,2},{7,3},{8,12},{9,13},{10,... | collective-permute-start | bytes 393224 | tf_op jit(solution)/shard_map/ppermute | solution.py:216
  6.8 1.5 %collective-permute-start.4 = (bf16[8,64,128]{2,1,0:T(8,128)(2,1)S(1)}, bf16[8,64,128]{2,1,0:T(8,128)(2,1)S(1)}, u32[]{:S(2)}, u32[]{:S(2)}) collective-permute-start(bf16[8,64,128]{2,1,0:T(8,128)(2,1)S(1)} %shard_map.83.refs_0_), channel_id=1, source_target_pairs={{0,2},{1,3},{2,0},{3,1},{4,6},{5,7},{6,4},{7,5},{8,10},{9,11},{10,... | collective-permute-start | bytes 393224 | tf_op jit(solution)/shard_map/ppermute | solution.py:216
  8.3 2.9 %shard_map.82 = (bf16[8,8,64,128]{3,2,1,0:T(8,128)(2,1)S(1)}, s32[202]{0:T(256)S(4)}) custom-call(s32[8]{0:T(128)} %dims_hbm.2, s32[8,8]{1,0:T(8,128)} %bitcast.1, s32[8,8]{1,0:T(8,128)} %owner_hbm.1, s32[8,8]{1,0:T(8,128)} %slot_hbm.1, bf16[8,64,64]{2,1,0:T(8,128)(2,1)} %left_hbm.1, bf16[8,8,64,128]{3,2,1,0:T(8,128)(2,1)} %psi_hbm.1), custom_call_target="tpu_custom_call" | custom-call | flops 67108864 | bytes 1048576 | tf_op jit(solution)/shard_map/pallas_call | solution.py:251
  11.1 0.5 %collective-permute-done.refs_3_ = bf16[8,64,128]{2,1,0:T(8,128)(2,1)S(1)} collective-permute-done((bf16[8,64,128]{2,1,0:T(8,128)(2,1)S(1)}, bf16[8,64,128]{2,1,0:T(8,128)(2,1)S(1)}, u32[]{:S(2)}, u32[]{:S(2)}) %collective-permute-start) | collective-permute-done | bytes 131104 | tf_op jit(solution)/shard_map/ppermute | solution.py:216
  11.6 0.7 %collective-permute-start.1 = (bf16[8,64,128]{2,1,0:T(8,128)(2,1)S(1)}, bf16[8,64,128]{2,1,0:T(8,128)(2,1)S(1)}, u32[]{:S(2)}, u32[]{:S(2)}) collective-permute-start(bf16[8,64,128]{2,1,0:T(8,128)(2,1)S(1)} %collective-permute-done.refs_3_), channel_id=1, source_target_pairs={{0,4},{1,3},{2,6},{3,1},{4,0},{5,7},{6,2},{7,5},{8,12},{9,11},{10,... | collective-permute-start | bytes 393224 | tf_op jit(solution)/shard_map/ppermute | solution.py:216
  12.3 0.5 %collective-permute-done.5.refs_2_ = bf16[8,64,128]{2,1,0:T(8,128)(2,1)S(1)} collective-permute-done((bf16[8,64,128]{2,1,0:T(8,128)(2,1)S(1)}, bf16[8,64,128]{2,1,0:T(8,128)(2,1)S(1)}, u32[]{:S(2)}, u32[]{:S(2)}) %collective-permute-start.5) | collective-permute-done | bytes 131104 | tf_op jit(solution)/shard_map/ppermute | solution.py:216
  12.8 1.5 %collective-permute-start.9 = (bf16[8,64,128]{2,1,0:T(8,128)(2,1)S(1)}, bf16[8,64,128]{2,1,0:T(8,128)(2,1)S(1)}, u32[]{:S(2)}, u32[]{:S(2)}) collective-permute-start(bf16[8,64,128]{2,1,0:T(8,128)(2,1)S(1)} %collective-permute-done.5.refs_2_), channel_id=1, source_target_pairs={{0,2},{1,3},{2,0},{3,1},{4,6},{5,7},{6,4},{7,5},{8,10},{9,11},{10,... | collective-permute-start | bytes 393224 | tf_op jit(solution)/shard_map/ppermute | solution.py:216
  14.3 0.0 collective-permute-start.8
  14.3 0.0 collective-permute-done.4.refs_1_
  14.3 0.5 %collective-permute-start.7 = (bf16[8,64,128]{2,1,0:T(8,128)(2,1)S(1)}, bf16[8,64,128]{2,1,0:T(8,128)(2,1)S(1)}, u32[]{:S(2)}, u32[]{:S(2)}) collective-permute-start(bf16[8,64,128]{2,1,0:T(8,128)(2,1)S(1)} %collective-permute-done.4.refs_1_), channel_id=1, source_target_pairs={{0,1},{1,0},{2,3},{3,2},{4,5},{5,4},{6,7},{7,6},{8,9},{9,8},{10,11... | collective-permute-start | bytes 393224 | tf_op jit(solution)/shard_map/ppermute | solution.py:216
  14.8 0.0 collective-permute-done.6.refs_5_
  14.8 0.5 %collective-permute-start.3 = (bf16[8,64,128]{2,1,0:T(8,128)(2,1)S(1)}, bf16[8,64,128]{2,1,0:T(8,128)(2,1)S(1)}, u32[]{:S(2)}, u32[]{:S(2)}) collective-permute-start(bf16[8,64,128]{2,1,0:T(8,128)(2,1)S(1)} %collective-permute-done.refs_3_), channel_id=1, source_target_pairs={{0,2},{1,5},{2,0},{3,7},{4,6},{5,1},{6,4},{7,3},{8,10},{9,13},{10,... | collective-permute-start | bytes 393224 | tf_op jit(solution)/shard_map/ppermute | solution.py:216
  15.3 1.3 %collective-permute-done.1.refs_4_ = bf16[8,64,128]{2,1,0:T(8,128)(2,1)S(1)} collective-permute-done((bf16[8,64,128]{2,1,0:T(8,128)(2,1)S(1)}, bf16[8,64,128]{2,1,0:T(8,128)(2,1)S(1)}, u32[]{:S(2)}, u32[]{:S(2)}) %collective-permute-start.1) | collective-permute-done | bytes 131104 | tf_op jit(solution)/shard_map/ppermute | solution.py:216
  16.6 1.7 %collective-permute-start.2 = (bf16[8,64,128]{2,1,0:T(8,128)(2,1)S(1)}, bf16[8,64,128]{2,1,0:T(8,128)(2,1)S(1)}, u32[]{:S(2)}, u32[]{:S(2)}) collective-permute-start(bf16[8,64,128]{2,1,0:T(8,128)(2,1)S(1)} %collective-permute-done.1.refs_4_), channel_id=1, source_target_pairs={{0,2},{1,5},{2,0},{3,7},{4,6},{5,1},{6,4},{7,3},{8,10},{9,13},{10,... | collective-permute-start | bytes 393224 | tf_op jit(solution)/shard_map/ppermute | solution.py:216
  18.2 0.0 collective-permute-done.9.refs_0_
  18.2 0.0 collective-permute-start.11
  18.3 0.0 collective-permute-done.8.refs_7_
  18.3 0.5 %collective-permute-start.12 = (bf16[8,64,128]{2,1,0:T(8,128)(2,1)S(1)}, bf16[8,64,128]{2,1,0:T(8,128)(2,1)S(1)}, u32[]{:S(2)}, u32[]{:S(2)}) collective-permute-start(bf16[8,64,128]{2,1,0:T(8,128)(2,1)S(1)} %collective-permute-done.1.refs_4_), channel_id=1, source_target_pairs={{0,1},{1,0},{2,3},{3,2},{4,5},{5,4},{6,7},{7,6},{8,9},{9,8},{10,11... | collective-permute-start | bytes 393224 | tf_op jit(solution)/shard_map/ppermute | solution.py:216
  18.8 0.0 collective-permute-done.7.refs_6_
  18.8 0.1 collective-permute-start.10
  18.8 1.6 %shard_map.84.early_ref = bf16[8,8,64,128]{3,2,1,0:T(8,128)(2,1)S(1)} custom-call(s32[202]{0:T(256)S(4)} %get-tuple-element.12.list_ref, bf16[8,8,64,128]{3,2,1,0:T(8,128)(2,1)S(1)} %get-tuple-element.15.half_ref, bf16[8,64,128]{2,1,0:T(8,128)(2,1)S(1)} %shard_map.83.refs_0_, bf16[8,64,128]{2,1,0:T(8,128)(2,1)S(1)} %collective-permute-done.4.refs_1_, ...), custom_call_target="tpu_custom_call" | custom-call | flops 67108864 | bytes 1048576 | tf_op jit(solution)/shard_map/pallas_call | solution.py:296
  20.4 0.0 collective-permute-done.3.refs_1_
  20.4 1.1 %collective-permute-done.2.refs_5_ = bf16[8,64,128]{2,1,0:T(8,128)(2,1)S(1)} collective-permute-done((bf16[8,64,128]{2,1,0:T(8,128)(2,1)S(1)}, bf16[8,64,128]{2,1,0:T(8,128)(2,1)S(1)}, u32[]{:S(2)}, u32[]{:S(2)}) %collective-permute-start.2) | collective-permute-done | bytes 131104 | tf_op jit(solution)/shard_map/ppermute | solution.py:216
  21.6 0.0 collective-permute-start.13
  21.6 0.5 %collective-permute-start.14 = (bf16[8,64,128]{2,1,0:T(8,128)(2,1)S(1)}, bf16[8,64,128]{2,1,0:T(8,128)(2,1)S(1)}, u32[]{:S(2)}, u32[]{:S(2)}) collective-permute-start(bf16[8,64,128]{2,1,0:T(8,128)(2,1)S(1)} %collective-permute-done.2.refs_5_), channel_id=1, source_target_pairs={{0,1},{1,0},{2,3},{3,2},{4,5},{5,4},{6,7},{7,6},{8,9},{9,8},{10,11... | collective-permute-start | bytes 393224 | tf_op jit(solution)/shard_map/ppermute | solution.py:216
  22.1 0.0 collective-permute-done.11.refs_3_
  22.1 0.0 collective-permute-done.10.refs_2_
  22.1 0.0 collective-permute-done.12.refs_4_
  22.1 1.1 %shard_map.85.middle_ref = bf16[8,8,64,128]{3,2,1,0:T(8,128)(2,1)S(1)} custom-call(s32[202]{0:T(256)S(4)} %get-tuple-element.12.list_ref, bf16[8,8,64,128]{3,2,1,0:T(8,128)(2,1)S(1)} %shard_map.84.early_ref, bf16[8,8,64,128]{3,2,1,0:T(8,128)(2,1)S(1)} %get-tuple-element.15.half_ref, bf16[8,64,128]{2,1,0:T(8,128)(2,1)S(1)} %collective-permute-done.9.refs_0_, ...), custom_call_target="tpu_custom_call" | custom-call | flops 16777216 | bytes 262144 | tf_op jit(solution)/shard_map/pallas_call | solution.py:308
  23.1 0.0 collective-permute-done.13.refs_0_
  23.1 0.0 collective-permute-done.14.refs_1_
  23.2 1.3 %shard_map.86 = bf16[8,8,64,128]{3,2,1,0:T(8,128)(2,1)} custom-call(s32[202]{0:T(256)S(4)} %get-tuple-element.12.list_ref, bf16[8,8,64,128]{3,2,1,0:T(8,128)(2,1)S(1)} %shard_map.85.middle_ref, bf16[8,8,64,128]{3,2,1,0:T(8,128)(2,1)S(1)} %get-tuple-element.15.half_ref, bf16[8,64,128]{2,1,0:T(8,128)(2,1)S(1)} %collective-permute-done.13.refs_0_, ...), custom_call_target="tpu_custom_call" | custom-call | flops 4194304 | bytes 1048576 | tf_op jit(solution)/shard_map/pallas_call | solution.py:317
Async XLA Ops:
  1.1 10.5 %collective-permute-start = (bf16[8,64,128]{2,1,0:T(8,128)(2,1)S(1)}, bf16[8,64,128]{2,1,0:T(8,128)(2,1)S(1)}, u32[]{:S(2)}, u32[]{:S(2)}) collective-permute-start(bf16[8,64,128]{2,1,0:T(8,128)(2,1)S(1)} %shard_map.83.refs_0_), channel_id=1, source_target_pairs={{0,8},{1,9},{2,10},{3,11},{4,12},{5,13},{6,14},{7,15},{8,0},{9,1},... | collective-permute-start | bytes 393224 | tf_op jit(solution)/shard_map/ppermute | solution.py:216
  5.2 9.6 %collective-permute-start.6 = (bf16[8,64,128]{2,1,0:T(8,128)(2,1)S(1)}, bf16[8,64,128]{2,1,0:T(8,128)(2,1)S(1)}, u32[]{:S(2)}, u32[]{:S(2)}) collective-permute-start(bf16[8,64,128]{2,1,0:T(8,128)(2,1)S(1)} %shard_map.83.refs_0_), channel_id=1, source_target_pairs={{0,1},{1,0},{2,3},{3,2},{4,5},{5,4},{6,7},{7,6},{8,9},{9,8},{10,11... | collective-permute-start | bytes 393224 | tf_op jit(solution)/shard_map/ppermute | solution.py:216
  5.2 7.6 %collective-permute-start.5 = (bf16[8,64,128]{2,1,0:T(8,128)(2,1)S(1)}, bf16[8,64,128]{2,1,0:T(8,128)(2,1)S(1)}, u32[]{:S(2)}, u32[]{:S(2)}) collective-permute-start(bf16[8,64,128]{2,1,0:T(8,128)(2,1)S(1)} %shard_map.83.refs_0_), channel_id=1, source_target_pairs={{0,4},{1,5},{2,6},{3,7},{4,0},{5,1},{6,2},{7,3},{8,12},{9,13},{10,... | collective-permute-start | bytes 393224 | tf_op jit(solution)/shard_map/ppermute | solution.py:216
  6.8 7.5 %collective-permute-start.4 = (bf16[8,64,128]{2,1,0:T(8,128)(2,1)S(1)}, bf16[8,64,128]{2,1,0:T(8,128)(2,1)S(1)}, u32[]{:S(2)}, u32[]{:S(2)}) collective-permute-start(bf16[8,64,128]{2,1,0:T(8,128)(2,1)S(1)} %shard_map.83.refs_0_), channel_id=1, source_target_pairs={{0,2},{1,3},{2,0},{3,1},{4,6},{5,7},{6,4},{7,5},{8,10},{9,11},{10,... | collective-permute-start | bytes 393224 | tf_op jit(solution)/shard_map/ppermute | solution.py:216
  11.6 5.0 %collective-permute-start.1 = (bf16[8,64,128]{2,1,0:T(8,128)(2,1)S(1)}, bf16[8,64,128]{2,1,0:T(8,128)(2,1)S(1)}, u32[]{:S(2)}, u32[]{:S(2)}) collective-permute-start(bf16[8,64,128]{2,1,0:T(8,128)(2,1)S(1)} %collective-permute-done.refs_3_), channel_id=1, source_target_pairs={{0,4},{1,3},{2,6},{3,1},{4,0},{5,7},{6,2},{7,5},{8,12},{9,11},{10,... | collective-permute-start | bytes 393224 | tf_op jit(solution)/shard_map/ppermute | solution.py:216
  12.8 5.5 %collective-permute-start.9 = (bf16[8,64,128]{2,1,0:T(8,128)(2,1)S(1)}, bf16[8,64,128]{2,1,0:T(8,128)(2,1)S(1)}, u32[]{:S(2)}, u32[]{:S(2)}) collective-permute-start(bf16[8,64,128]{2,1,0:T(8,128)(2,1)S(1)} %collective-permute-done.5.refs_2_), channel_id=1, source_target_pairs={{0,2},{1,3},{2,0},{3,1},{4,6},{5,7},{6,4},{7,5},{8,10},{9,11},{10,... | collective-permute-start | bytes 393224 | tf_op jit(solution)/shard_map/ppermute | solution.py:216
  14.3 4.0 %collective-permute-start.8 = (bf16[8,64,128]{2,1,0:T(8,128)(2,1)S(1)}, bf16[8,64,128]{2,1,0:T(8,128)(2,1)S(1)}, u32[]{:S(2)}, u32[]{:S(2)}) collective-permute-start(bf16[8,64,128]{2,1,0:T(8,128)(2,1)S(1)} %collective-permute-done.5.refs_2_), channel_id=1, source_target_pairs={{0,1},{1,0},{2,3},{3,2},{4,5},{5,4},{6,7},{7,6},{8,9},{9,8},{10,11... | collective-permute-start | bytes 393224 | tf_op jit(solution)/shard_map/ppermute | solution.py:216
  14.3 4.5 %collective-permute-start.7 = (bf16[8,64,128]{2,1,0:T(8,128)(2,1)S(1)}, bf16[8,64,128]{2,1,0:T(8,128)(2,1)S(1)}, u32[]{:S(2)}, u32[]{:S(2)}) collective-permute-start(bf16[8,64,128]{2,1,0:T(8,128)(2,1)S(1)} %collective-permute-done.4.refs_1_), channel_id=1, source_target_pairs={{0,1},{1,0},{2,3},{3,2},{4,5},{5,4},{6,7},{7,6},{8,9},{9,8},{10,11... | collective-permute-start | bytes 393224 | tf_op jit(solution)/shard_map/ppermute | solution.py:216
  14.8 5.6 %collective-permute-start.3 = (bf16[8,64,128]{2,1,0:T(8,128)(2,1)S(1)}, bf16[8,64,128]{2,1,0:T(8,128)(2,1)S(1)}, u32[]{:S(2)}, u32[]{:S(2)}) collective-permute-start(bf16[8,64,128]{2,1,0:T(8,128)(2,1)S(1)} %collective-permute-done.refs_3_), channel_id=1, source_target_pairs={{0,2},{1,5},{2,0},{3,7},{4,6},{5,1},{6,4},{7,3},{8,10},{9,13},{10,... | collective-permute-start | bytes 393224 | tf_op jit(solution)/shard_map/ppermute | solution.py:216
  16.6 5.0 %collective-permute-start.2 = (bf16[8,64,128]{2,1,0:T(8,128)(2,1)S(1)}, bf16[8,64,128]{2,1,0:T(8,128)(2,1)S(1)}, u32[]{:S(2)}, u32[]{:S(2)}) collective-permute-start(bf16[8,64,128]{2,1,0:T(8,128)(2,1)S(1)} %collective-permute-done.1.refs_4_), channel_id=1, source_target_pairs={{0,2},{1,5},{2,0},{3,7},{4,6},{5,1},{6,4},{7,3},{8,10},{9,13},{10,... | collective-permute-start | bytes 393224 | tf_op jit(solution)/shard_map/ppermute | solution.py:216
  18.2 3.8 %collective-permute-start.11 = (bf16[8,64,128]{2,1,0:T(8,128)(2,1)S(1)}, bf16[8,64,128]{2,1,0:T(8,128)(2,1)S(1)}, u32[]{:S(2)}, u32[]{:S(2)}) collective-permute-start(bf16[8,64,128]{2,1,0:T(8,128)(2,1)S(1)} %collective-permute-done.refs_3_), channel_id=1, source_target_pairs={{0,1},{1,0},{2,3},{3,2},{4,5},{5,4},{6,7},{7,6},{8,9},{9,8},{10,11... | collective-permute-start | bytes 393224 | tf_op jit(solution)/shard_map/ppermute | solution.py:216
  18.3 3.8 %collective-permute-start.12 = (bf16[8,64,128]{2,1,0:T(8,128)(2,1)S(1)}, bf16[8,64,128]{2,1,0:T(8,128)(2,1)S(1)}, u32[]{:S(2)}, u32[]{:S(2)}) collective-permute-start(bf16[8,64,128]{2,1,0:T(8,128)(2,1)S(1)} %collective-permute-done.1.refs_4_), channel_id=1, source_target_pairs={{0,1},{1,0},{2,3},{3,2},{4,5},{5,4},{6,7},{7,6},{8,9},{9,8},{10,11... | collective-permute-start | bytes 393224 | tf_op jit(solution)/shard_map/ppermute | solution.py:216
  18.8 3.3 %collective-permute-start.10 = (bf16[8,64,128]{2,1,0:T(8,128)(2,1)S(1)}, bf16[8,64,128]{2,1,0:T(8,128)(2,1)S(1)}, u32[]{:S(2)}, u32[]{:S(2)}) collective-permute-start(bf16[8,64,128]{2,1,0:T(8,128)(2,1)S(1)} %collective-permute-done.9.refs_0_), channel_id=1, source_target_pairs={{0,1},{1,0},{2,3},{3,2},{4,5},{5,4},{6,7},{7,6},{8,9},{9,8},{10,11... | collective-permute-start | bytes 393224 | tf_op jit(solution)/shard_map/ppermute | solution.py:216
  21.6 1.6 %collective-permute-start.13 = (bf16[8,64,128]{2,1,0:T(8,128)(2,1)S(1)}, bf16[8,64,128]{2,1,0:T(8,128)(2,1)S(1)}, u32[]{:S(2)}, u32[]{:S(2)}) collective-permute-start(bf16[8,64,128]{2,1,0:T(8,128)(2,1)S(1)} %collective-permute-done.3.refs_1_), channel_id=1, source_target_pairs={{0,1},{1,0},{2,3},{3,2},{4,5},{5,4},{6,7},{7,6},{8,9},{9,8},{10,11... | collective-permute-start | bytes 393224 | tf_op jit(solution)/shard_map/ppermute | solution.py:216
  21.6 1.6 %collective-permute-start.14 = (bf16[8,64,128]{2,1,0:T(8,128)(2,1)S(1)}, bf16[8,64,128]{2,1,0:T(8,128)(2,1)S(1)}, u32[]{:S(2)}, u32[]{:S(2)}) collective-permute-start(bf16[8,64,128]{2,1,0:T(8,128)(2,1)S(1)} %collective-permute-done.2.refs_5_), channel_id=1, source_target_pairs={{0,1},{1,0},{2,3},{3,2},{4,5},{5,4},{6,7},{7,6},{8,9},{9,8},{10,11... | collective-permute-start | bytes 393224 | tf_op jit(solution)/shard_map/ppermute | solution.py:216

commit v32 on v31

--- a/solution.py
+++ b/solution.py
@@ -18,7 +18,7 @@
     return name[1] | CORE, name[0] | CORE
 
 
-MIDDLE = (CORNER, SECOND, partner(CORNER), partner(BEYOND), partner(FIRST), END)
+MIDDLE = (SECOND, partner(CORNER), partner(BEYOND), partner(FIRST), END)
 LAST = (partner(SECOND), partner(END))
 EARLY = tuple(name for name in (
     OWN, SIDE, BESIDE, BEYOND, CORNER, FIRST, SECOND,

time: 24.7 us -> 24.6 us (level)
  waiting for transfers between devices: 3.38 us -> 4.06 us
  Pallas kernels: 7.93 us -> 7.51 us
  starting transfers between devices: 13.1 us -> 12.8 us
    ppermute x15, waiting for transfers between devices: 3.38 us -> 4.06 us  [swap(): lax.ppermute(piece, 'sec', [(i, i ^ (odd_bit if i & CORE else even_bit))...]
    pallas_call x1, Pallas kernels: 1.05 us -> 0.58 us  [per_device(): pl.pallas_call(middle_kernel, out_shape=jax.ShapeDtypeStruct(psi.shape, j...]
    ppermute x15, starting transfers between devices: 13.1 us -> 12.8 us  [swap(): lax.ppermute(piece, 'sec', [(i, i ^ (odd_bit if i & CORE else even_bit))...]
  transfers between devices with their start and end apart: 15 -> 15, of which waited for: 4 -> 7; matrix products, arithmetic and copies ran while one was open for 0% -> 0% of each run, Pallas kernels for 22% -> 21%
where the time goes in v32:
time: 24.6 us; the launch traced here: 24.5 us
  starting transfers between devices  12.8 us (52%)
  Pallas kernels  7.51 us (31%)
  waiting for transfers between devices  4.06 us (17%)
    ppermute x15, starting transfers between devices, swap(): lax.ppermute(piece, 'sec', [(i, i ^ (odd_bit if i & CORE else even_bit))...  12.8 us
    ppermute x15, waiting for transfers between devices, swap(): lax.ppermute(piece, 'sec', [(i, i ^ (odd_bit if i & CORE else even_bit))...  4.06 us
    pallas_call x1, Pallas kernels, per_device(): pl.pallas_call(functools.partial(left_kernel, pair_count, len(EARLY if by...  2.85 us
    pallas_call x1, Pallas kernels, per_device(): pl.pallas_call(early_kernel, out_shape=jax.ShapeDtypeStruct(psi.shape, jn...  1.6 us
    pallas_call x1, Pallas kernels, per_device(): pl.pallas_call(last_kernel, out_shape=jax.ShapeDtypeStruct(psi.shape, jnp...  1.38 us
    pallas_call x1, Pallas kernels, per_device(): pl.pallas_call(pack_kernel, out_shape=jax.ShapeDtypeStruct((pair_count, t...  1.09 us
    pallas_call x1, Pallas kernels, per_device(): pl.pallas_call(middle_kernel, out_shape=jax.ShapeDtypeStruct(psi.shape, j...  0.58 us
  transfers between devices with their start and end apart: 15, of which 7 were waited for; matrix products, arithmetic and copies ran while one was open for 0% of the time, Pallas kernels for 21%

profile of v32, /device:TPU:0, one launch (start us, length us, event | category | flops | bytes accessed | tf_op | source)
XLA Modules:
  0.0 24.5 jit_solution(16716436204302300201)
XLA Ops:
  0.0 1.1 %shard_map.83.refs_0_ = bf16[8,64,128]{2,1,0:T(8,128)(2,1)S(1)} custom-call(s32[16]{0:T(128)} %dims_hbm.3, bf16[16,64,64]{2,1,0:T(8,128)(2,1)} %right_hbm.1), custom_call_target="tpu_custom_call" | custom-call | bytes 131072 | tf_op jit(solution)/shard_map/pallas_call | solution.py:236
  1.1 4.1 %collective-permute-start = (bf16[8,64,128]{2,1,0:T(8,128)(2,1)S(1)}, bf16[8,64,128]{2,1,0:T(8,128)(2,1)S(1)}, u32[]{:S(2)}, u32[]{:S(2)}) collective-permute-start(bf16[8,64,128]{2,1,0:T(8,128)(2,1)S(1)} %shard_map.83.refs_0_), channel_id=1, source_target_pairs={{0,8},{1,9},{2,10},{3,11},{4,12},{5,13},{6,14},{7,15},{8,0},{9,1},... | collective-permute-start | bytes 393224 | tf_op jit(solution)/shard_map/ppermute | solution.py:216
  5.2 0.0 collective-permute-start.7
  5.2 1.6 %collective-permute-start.5 = (bf16[8,64,128]{2,1,0:T(8,128)(2,1)S(1)}, bf16[8,64,128]{2,1,0:T(8,128)(2,1)S(1)}, u32[]{:S(2)}, u32[]{:S(2)}) collective-permute-start(bf16[8,64,128]{2,1,0:T(8,128)(2,1)S(1)} %shard_map.83.refs_0_), channel_id=1, source_target_pairs={{0,4},{1,5},{2,6},{3,7},{4,0},{5,1},{6,2},{7,3},{8,12},{9,13},{10,... | collective-permute-start | bytes 393224 | tf_op jit(solution)/shard_map/ppermute | solution.py:216
  6.8 1.5 %collective-permute-start.4 = (bf16[8,64,128]{2,1,0:T(8,128)(2,1)S(1)}, bf16[8,64,128]{2,1,0:T(8,128)(2,1)S(1)}, u32[]{:S(2)}, u32[]{:S(2)}) collective-permute-start(bf16[8,64,128]{2,1,0:T(8,128)(2,1)S(1)} %shard_map.83.refs_0_), channel_id=1, source_target_pairs={{0,2},{1,3},{2,0},{3,1},{4,6},{5,7},{6,4},{7,5},{8,10},{9,11},{10,... | collective-permute-start | bytes 393224 | tf_op jit(solution)/shard_map/ppermute | solution.py:216
  8.3 2.9 %shard_map.82 = (bf16[8,8,64,128]{3,2,1,0:T(8,128)(2,1)S(1)}, s32[202]{0:T(256)S(4)}) custom-call(s32[8]{0:T(128)} %dims_hbm.2, s32[8,8]{1,0:T(8,128)} %bitcast.1, s32[8,8]{1,0:T(8,128)} %owner_hbm.1, s32[8,8]{1,0:T(8,128)} %slot_hbm.1, bf16[8,64,64]{2,1,0:T(8,128)(2,1)} %left_hbm.1, bf16[8,8,64,128]{3,2,1,0:T(8,128)(2,1)} %psi_hbm.1), custom_call_target="tpu_custom_call" | custom-call | flops 67108864 | bytes 1048576 | tf_op jit(solution)/shard_map/pallas_call | solution.py:251
  11.1 0.5 %collective-permute-done.refs_3_ = bf16[8,64,128]{2,1,0:T(8,128)(2,1)S(1)} collective-permute-done((bf16[8,64,128]{2,1,0:T(8,128)(2,1)S(1)}, bf16[8,64,128]{2,1,0:T(8,128)(2,1)S(1)}, u32[]{:S(2)}, u32[]{:S(2)}) %collective-permute-start) | collective-permute-done | bytes 131104 | tf_op jit(solution)/shard_map/ppermute | solution.py:216
  11.6 0.7 %collective-permute-start.1 = (bf16[8,64,128]{2,1,0:T(8,128)(2,1)S(1)}, bf16[8,64,128]{2,1,0:T(8,128)(2,1)S(1)}, u32[]{:S(2)}, u32[]{:S(2)}) collective-permute-start(bf16[8,64,128]{2,1,0:T(8,128)(2,1)S(1)} %collective-permute-done.refs_3_), channel_id=1, source_target_pairs={{0,4},{1,3},{2,6},{3,1},{4,0},{5,7},{6,2},{7,5},{8,12},{9,11},{10,... | collective-permute-start | bytes 393224 | tf_op jit(solution)/shard_map/ppermute | solution.py:216
  12.3 0.5 %collective-permute-done.5.refs_2_ = bf16[8,64,128]{2,1,0:T(8,128)(2,1)S(1)} collective-permute-done((bf16[8,64,128]{2,1,0:T(8,128)(2,1)S(1)}, bf16[8,64,128]{2,1,0:T(8,128)(2,1)S(1)}, u32[]{:S(2)}, u32[]{:S(2)}) %collective-permute-start.5) | collective-permute-done | bytes 131104 | tf_op jit(solution)/shard_map/ppermute | solution.py:216
  12.8 0.0 collective-permute-start.9
  12.8 1.5 %collective-permute-start.6 = (bf16[8,64,128]{2,1,0:T(8,128)(2,1)S(1)}, bf16[8,64,128]{2,1,0:T(8,128)(2,1)S(1)}, u32[]{:S(2)}, u32[]{:S(2)}) collective-permute-start(bf16[8,64,128]{2,1,0:T(8,128)(2,1)S(1)} %collective-permute-done.5.refs_2_), channel_id=1, source_target_pairs={{0,2},{1,3},{2,0},{3,1},{4,6},{5,7},{6,4},{7,5},{8,10},{9,11},{10,... | collective-permute-start | bytes 393224 | tf_op jit(solution)/shard_map/ppermute | solution.py:216
  14.3 0.0 collective-permute-done.4.refs_1_
  14.3 0.2 collective-permute-start.8
  14.5 0.0 collective-permute-done.7.refs_6_
  14.5 0.5 %collective-permute-start.3 = (bf16[8,64,128]{2,1,0:T(8,128)(2,1)S(1)}, bf16[8,64,128]{2,1,0:T(8,128)(2,1)S(1)}, u32[]{:S(2)}, u32[]{:S(2)}) collective-permute-start(bf16[8,64,128]{2,1,0:T(8,128)(2,1)S(1)} %collective-permute-done.refs_3_), channel_id=1, source_target_pairs={{0,2},{1,5},{2,0},{3,7},{4,6},{5,1},{6,4},{7,3},{8,10},{9,13},{10,... | collective-permute-start | bytes 393224 | tf_op jit(solution)/shard_map/ppermute | solution.py:216
  15.0 1.6 %collective-permute-done.1.refs_5_ = bf16[8,64,128]{2,1,0:T(8,128)(2,1)S(1)} collective-permute-done((bf16[8,64,128]{2,1,0:T(8,128)(2,1)S(1)}, bf16[8,64,128]{2,1,0:T(8,128)(2,1)S(1)}, u32[]{:S(2)}, u32[]{:S(2)}) %collective-permute-start.1) | collective-permute-done | bytes 131104 | tf_op jit(solution)/shard_map/ppermute | solution.py:216
  16.6 1.7 %collective-permute-start.2 = (bf16[8,64,128]{2,1,0:T(8,128)(2,1)S(1)}, bf16[8,64,128]{2,1,0:T(8,128)(2,1)S(1)}, u32[]{:S(2)}, u32[]{:S(2)}) collective-permute-start(bf16[8,64,128]{2,1,0:T(8,128)(2,1)S(1)} %collective-permute-done.1.refs_5_), channel_id=1, source_target_pairs={{0,2},{1,5},{2,0},{3,7},{4,6},{5,1},{6,4},{7,3},{8,10},{9,13},{10,... | collective-permute-start | bytes 393224 | tf_op jit(solution)/shard_map/ppermute | solution.py:216
  18.3 0.0 collective-permute-done.9.refs_8_
  18.3 0.0 collective-permute-start.11
  18.3 0.3 %collective-permute-done.6.refs_4_ = bf16[8,64,128]{2,1,0:T(8,128)(2,1)S(1)} collective-permute-done((bf16[8,64,128]{2,1,0:T(8,128)(2,1)S(1)}, bf16[8,64,128]{2,1,0:T(8,128)(2,1)S(1)}, u32[]{:S(2)}, u32[]{:S(2)}) %collective-permute-start.6) | collective-permute-done | bytes 131104 | tf_op jit(solution)/shard_map/ppermute | solution.py:216
  18.7 0.2 collective-permute-start.12
  18.8 0.0 collective-permute-done.8.refs_7_
  18.8 0.3 %collective-permute-start.10 = (bf16[8,64,128]{2,1,0:T(8,128)(2,1)S(1)}, bf16[8,64,128]{2,1,0:T(8,128)(2,1)S(1)}, u32[]{:S(2)}, u32[]{:S(2)}) collective-permute-start(bf16[8,64,128]{2,1,0:T(8,128)(2,1)S(1)} %collective-permute-done.6.refs_4_), channel_id=1, source_target_pairs={{0,1},{1,0},{2,3},{3,2},{4,5},{5,4},{6,7},{7,6},{8,9},{9,8},{10,11... | collective-permute-start | bytes 393224 | tf_op jit(solution)/shard_map/ppermute | solution.py:216
  19.2 1.6 %shard_map.84.early_ref = bf16[8,8,64,128]{3,2,1,0:T(8,128)(2,1)S(1)} custom-call(s32[202]{0:T(256)S(4)} %get-tuple-element.12.list_ref, bf16[8,8,64,128]{3,2,1,0:T(8,128)(2,1)S(1)} %get-tuple-element.15.half_ref, bf16[8,64,128]{2,1,0:T(8,128)(2,1)S(1)} %shard_map.83.refs_0_, bf16[8,64,128]{2,1,0:T(8,128)(2,1)S(1)} %collective-permute-done.4.refs_1_, ...), custom_call_target="tpu_custom_call" | custom-call | flops 67108864 | bytes 1048576 | tf_op jit(solution)/shard_map/pallas_call | solution.py:296
  20.8 0.0 collective-permute-done.3.refs_0_
  20.8 0.7 %collective-permute-done.2.refs_4_ = bf16[8,64,128]{2,1,0:T(8,128)(2,1)S(1)} collective-permute-done((bf16[8,64,128]{2,1,0:T(8,128)(2,1)S(1)}, bf16[8,64,128]{2,1,0:T(8,128)(2,1)S(1)}, u32[]{:S(2)}, u32[]{:S(2)}) %collective-permute-start.2) | collective-permute-done | bytes 131104 | tf_op jit(solution)/shard_map/ppermute | solution.py:216
  21.6 0.0 collective-permute-start.13
  21.6 0.5 %collective-permute-start.14 = (bf16[8,64,128]{2,1,0:T(8,128)(2,1)S(1)}, bf16[8,64,128]{2,1,0:T(8,128)(2,1)S(1)}, u32[]{:S(2)}, u32[]{:S(2)}) collective-permute-start(bf16[8,64,128]{2,1,0:T(8,128)(2,1)S(1)} %collective-permute-done.2.refs_4_), channel_id=1, source_target_pairs={{0,1},{1,0},{2,3},{3,2},{4,5},{5,4},{6,7},{7,6},{8,9},{9,8},{10,11... | collective-permute-start | bytes 393224 | tf_op jit(solution)/shard_map/ppermute | solution.py:216
  22.1 0.0 collective-permute-done.11.refs_2_
  22.1 0.0 collective-permute-done.10.refs_1_
  22.1 0.0 collective-permute-done.12.refs_3_
  22.1 0.6 %shard_map.85.middle_ref = bf16[8,8,64,128]{3,2,1,0:T(8,128)(2,1)S(1)} custom-call(s32[202]{0:T(256)S(4)} %get-tuple-element.12.list_ref, bf16[8,8,64,128]{3,2,1,0:T(8,128)(2,1)S(1)} %shard_map.84.early_ref, bf16[8,8,64,128]{3,2,1,0:T(8,128)(2,1)S(1)} %get-tuple-element.15.half_ref, bf16[8,64,128]{2,1,0:T(8,128)(2,1)S(1)} %collective-permute-done.3.refs_0_, ...), custom_call_target="tpu_custom_call" | custom-call | flops 16777216 | bytes 262144 | tf_op jit(solution)/shard_map/pallas_call | solution.py:308
  22.7 0.2 collective-permute-done.13.refs_0_
  22.9 0.2 collective-permute-done.14.refs_1_
  23.1 1.4 %shard_map.86 = bf16[8,8,64,128]{3,2,1,0:T(8,128)(2,1)} custom-call(s32[202]{0:T(256)S(4)} %get-tuple-element.12.list_ref, bf16[8,8,64,128]{3,2,1,0:T(8,128)(2,1)S(1)} %shard_map.85.middle_ref, bf16[8,8,64,128]{3,2,1,0:T(8,128)(2,1)S(1)} %get-tuple-element.15.half_ref, bf16[8,64,128]{2,1,0:T(8,128)(2,1)S(1)} %collective-permute-done.13.refs_0_, ...), custom_call_target="tpu_custom_call" | custom-call | flops 4194304 | bytes 1048576 | tf_op jit(solution)/shard_map/pallas_call | solution.py:317
Async XLA Ops:
  1.1 10.5 %collective-permute-start = (bf16[8,64,128]{2,1,0:T(8,128)(2,1)S(1)}, bf16[8,64,128]{2,1,0:T(8,128)(2,1)S(1)}, u32[]{:S(2)}, u32[]{:S(2)}) collective-permute-start(bf16[8,64,128]{2,1,0:T(8,128)(2,1)S(1)} %shard_map.83.refs_0_), channel_id=1, source_target_pairs={{0,8},{1,9},{2,10},{3,11},{4,12},{5,13},{6,14},{7,15},{8,0},{9,1},... | collective-permute-start | bytes 393224 | tf_op jit(solution)/shard_map/ppermute | solution.py:216
  5.2 9.3 %collective-permute-start.7 = (bf16[8,64,128]{2,1,0:T(8,128)(2,1)S(1)}, bf16[8,64,128]{2,1,0:T(8,128)(2,1)S(1)}, u32[]{:S(2)}, u32[]{:S(2)}) collective-permute-start(bf16[8,64,128]{2,1,0:T(8,128)(2,1)S(1)} %shard_map.83.refs_0_), channel_id=1, source_target_pairs={{0,1},{1,0},{2,3},{3,2},{4,5},{5,4},{6,7},{7,6},{8,9},{9,8},{10,11... | collective-permute-start | bytes 393224 | tf_op jit(solution)/shard_map/ppermute | solution.py:216
  5.2 7.6 %collective-permute-start.5 = (bf16[8,64,128]{2,1,0:T(8,128)(2,1)S(1)}, bf16[8,64,128]{2,1,0:T(8,128)(2,1)S(1)}, u32[]{:S(2)}, u32[]{:S(2)}) collective-permute-start(bf16[8,64,128]{2,1,0:T(8,128)(2,1)S(1)} %shard_map.83.refs_0_), channel_id=1, source_target_pairs={{0,4},{1,5},{2,6},{3,7},{4,0},{5,1},{6,2},{7,3},{8,12},{9,13},{10,... | collective-permute-start | bytes 393224 | tf_op jit(solution)/shard_map/ppermute | solution.py:216
  6.8 7.5 %collective-permute-start.4 = (bf16[8,64,128]{2,1,0:T(8,128)(2,1)S(1)}, bf16[8,64,128]{2,1,0:T(8,128)(2,1)S(1)}, u32[]{:S(2)}, u32[]{:S(2)}) collective-permute-start(bf16[8,64,128]{2,1,0:T(8,128)(2,1)S(1)} %shard_map.83.refs_0_), channel_id=1, source_target_pairs={{0,2},{1,3},{2,0},{3,1},{4,6},{5,7},{6,4},{7,5},{8,10},{9,11},{10,... | collective-permute-start | bytes 393224 | tf_op jit(solution)/shard_map/ppermute | solution.py:216
  11.6 5.0 %collective-permute-start.1 = (bf16[8,64,128]{2,1,0:T(8,128)(2,1)S(1)}, bf16[8,64,128]{2,1,0:T(8,128)(2,1)S(1)}, u32[]{:S(2)}, u32[]{:S(2)}) collective-permute-start(bf16[8,64,128]{2,1,0:T(8,128)(2,1)S(1)} %collective-permute-done.refs_3_), channel_id=1, source_target_pairs={{0,4},{1,3},{2,6},{3,1},{4,0},{5,7},{6,2},{7,5},{8,12},{9,11},{10,... | collective-permute-start | bytes 393224 | tf_op jit(solution)/shard_map/ppermute | solution.py:216
  12.8 5.6 %collective-permute-start.9 = (bf16[8,64,128]{2,1,0:T(8,128)(2,1)S(1)}, bf16[8,64,128]{2,1,0:T(8,128)(2,1)S(1)}, u32[]{:S(2)}, u32[]{:S(2)}) collective-permute-start(bf16[8,64,128]{2,1,0:T(8,128)(2,1)S(1)} %collective-permute-done.5.refs_2_), channel_id=1, source_target_pairs={{0,1},{1,0},{2,3},{3,2},{4,5},{5,4},{6,7},{7,6},{8,9},{9,8},{10,11... | collective-permute-start | bytes 393224 | tf_op jit(solution)/shard_map/ppermute | solution.py:216
  12.8 5.9 %collective-permute-start.6 = (bf16[8,64,128]{2,1,0:T(8,128)(2,1)S(1)}, bf16[8,64,128]{2,1,0:T(8,128)(2,1)S(1)}, u32[]{:S(2)}, u32[]{:S(2)}) collective-permute-start(bf16[8,64,128]{2,1,0:T(8,128)(2,1)S(1)} %collective-permute-done.5.refs_2_), channel_id=1, source_target_pairs={{0,2},{1,3},{2,0},{3,1},{4,6},{5,7},{6,4},{7,5},{8,10},{9,11},{10,... | collective-permute-start | bytes 393224 | tf_op jit(solution)/shard_map/ppermute | solution.py:216
  14.3 4.5 %collective-permute-start.8 = (bf16[8,64,128]{2,1,0:T(8,128)(2,1)S(1)}, bf16[8,64,128]{2,1,0:T(8,128)(2,1)S(1)}, u32[]{:S(2)}, u32[]{:S(2)}) collective-permute-start(bf16[8,64,128]{2,1,0:T(8,128)(2,1)S(1)} %collective-permute-done.4.refs_1_), channel_id=1, source_target_pairs={{0,1},{1,0},{2,3},{3,2},{4,5},{5,4},{6,7},{7,6},{8,9},{9,8},{10,11... | collective-permute-start | bytes 393224 | tf_op jit(solution)/shard_map/ppermute | solution.py:216
  14.5 6.3 %collective-permute-start.3 = (bf16[8,64,128]{2,1,0:T(8,128)(2,1)S(1)}, bf16[8,64,128]{2,1,0:T(8,128)(2,1)S(1)}, u32[]{:S(2)}, u32[]{:S(2)}) collective-permute-start(bf16[8,64,128]{2,1,0:T(8,128)(2,1)S(1)} %collective-permute-done.refs_3_), channel_id=1, source_target_pairs={{0,2},{1,5},{2,0},{3,7},{4,6},{5,1},{6,4},{7,3},{8,10},{9,13},{10,... | collective-permute-start | bytes 393224 | tf_op jit(solution)/shard_map/ppermute | solution.py:216
  16.6 5.0 %collective-permute-start.2 = (bf16[8,64,128]{2,1,0:T(8,128)(2,1)S(1)}, bf16[8,64,128]{2,1,0:T(8,128)(2,1)S(1)}, u32[]{:S(2)}, u32[]{:S(2)}) collective-permute-start(bf16[8,64,128]{2,1,0:T(8,128)(2,1)S(1)} %collective-permute-done.1.refs_5_), channel_id=1, source_target_pairs={{0,2},{1,5},{2,0},{3,7},{4,6},{5,1},{6,4},{7,3},{8,10},{9,13},{10,... | collective-permute-start | bytes 393224 | tf_op jit(solution)/shard_map/ppermute | solution.py:216
  18.3 3.7 %collective-permute-start.11 = (bf16[8,64,128]{2,1,0:T(8,128)(2,1)S(1)}, bf16[8,64,128]{2,1,0:T(8,128)(2,1)S(1)}, u32[]{:S(2)}, u32[]{:S(2)}) collective-permute-start(bf16[8,64,128]{2,1,0:T(8,128)(2,1)S(1)} %collective-permute-done.refs_3_), channel_id=1, source_target_pairs={{0,1},{1,0},{2,3},{3,2},{4,5},{5,4},{6,7},{7,6},{8,9},{9,8},{10,11... | collective-permute-start | bytes 393224 | tf_op jit(solution)/shard_map/ppermute | solution.py:216
  18.7 3.4 %collective-permute-start.12 = (bf16[8,64,128]{2,1,0:T(8,128)(2,1)S(1)}, bf16[8,64,128]{2,1,0:T(8,128)(2,1)S(1)}, u32[]{:S(2)}, u32[]{:S(2)}) collective-permute-start(bf16[8,64,128]{2,1,0:T(8,128)(2,1)S(1)} %collective-permute-done.1.refs_5_), channel_id=1, source_target_pairs={{0,1},{1,0},{2,3},{3,2},{4,5},{5,4},{6,7},{7,6},{8,9},{9,8},{10,11... | collective-permute-start | bytes 393224 | tf_op jit(solution)/shard_map/ppermute | solution.py:216
  18.8 3.2 %collective-permute-start.10 = (bf16[8,64,128]{2,1,0:T(8,128)(2,1)S(1)}, bf16[8,64,128]{2,1,0:T(8,128)(2,1)S(1)}, u32[]{:S(2)}, u32[]{:S(2)}) collective-permute-start(bf16[8,64,128]{2,1,0:T(8,128)(2,1)S(1)} %collective-permute-done.6.refs_4_), channel_id=1, source_target_pairs={{0,1},{1,0},{2,3},{3,2},{4,5},{5,4},{6,7},{7,6},{8,9},{9,8},{10,11... | collective-permute-start | bytes 393224 | tf_op jit(solution)/shard_map/ppermute | solution.py:216
  21.6 1.3 %collective-permute-start.13 = (bf16[8,64,128]{2,1,0:T(8,128)(2,1)S(1)}, bf16[8,64,128]{2,1,0:T(8,128)(2,1)S(1)}, u32[]{:S(2)}, u32[]{:S(2)}) collective-permute-start(bf16[8,64,128]{2,1,0:T(8,128)(2,1)S(1)} %collective-permute-done.3.refs_0_), channel_id=1, source_target_pairs={{0,1},{1,0},{2,3},{3,2},{4,5},{5,4},{6,7},{7,6},{8,9},{9,8},{10,11... | collective-permute-start | bytes 393224 | tf_op jit(solution)/shard_map/ppermute | solution.py:216
  21.6 1.5 %collective-permute-start.14 = (bf16[8,64,128]{2,1,0:T(8,128)(2,1)S(1)}, bf16[8,64,128]{2,1,0:T(8,128)(2,1)S(1)}, u32[]{:S(2)}, u32[]{:S(2)}) collective-permute-start(bf16[8,64,128]{2,1,0:T(8,128)(2,1)S(1)} %collective-permute-done.2.refs_4_), channel_id=1, source_target_pairs={{0,1},{1,0},{2,3},{3,2},{4,5},{5,4},{6,7},{7,6},{8,9},{9,8},{10,11... | collective-permute-start | bytes 393224 | tf_op jit(solution)/shard_map/ppermute | solution.py:216
